TPU v7x, 32 devices: a whole 2x2x4 slice. The times are simulated.
32 devices in a mesh: batch: 4 (over z), col: 8 (over y, x, core).
Axes of the slice: x: 2, y: 2, z: 4, core: 2. Of those that a mesh axis runs over, the one named last changes fastest.
Arguments:
- views: bfloat16 [2, 512, 4096], P(None, 'batch', 'col'), may hold values from -132 to 132
- norm_scale_gain: float32 [4096], P('col'), may hold values from 0.5 to 1.5
- norm_shift_bias: float32 [4096], P('col'), may hold values from -3 to 3
- weight: bfloat16 [4096, 8192], P(None, 'col'), may hold values from -0.09375 to 0.09375
Outputs:
- loss: float32 [], replicated
- grad_weight: float32 [4096, 8192], P('batch', 'col')
- grad_gain: float32 [4096], P('col')
- grad_bias: float32 [4096], P('col')
- views_gradient: float32 [2, 512, 4096], P(None, 'batch', 'col')
All inputs are finite; a program needn't handle non-finite values.
Results may differ from a plain program's by a relative error of at most 0.0027.
Values may be sent and summed in bfloat16 or wider, within the bound.
No kernel may reach another device: no remote copies, remote signals or barrier semaphores. Data moves between devices by JAX's collectives and lax.ppermute only.
A program may use at most 64 MiB of HBM per device.

v0:
```python
import jax
import jax.numpy as jnp
from jax import lax
from jax.sharding import PartitionSpec as P

E = 8192


eps_norm = 1e-05
eps_std = 0.0001


def gelu_slope(preactivation):
    value, pullback = jax.vjp(lambda t: jax.nn.gelu(t, approximate=True), preactivation)
    return pullback(jnp.ones_like(value))[0]


def shards(views, norm_scale_gain, norm_shift_bias, weight):
    n_batch = lax.axis_size("batch")
    n_col = lax.axis_size("col")
    local_rows = views.shape[1]
    sample_count = local_rows * n_batch
    scale = sample_count * E / 128.0
    hidden_float = views.astype(jnp.float32)
    total = lax.psum(jnp.sum(hidden_float, axis=1), "batch")
    batch_average = total[:, None, :] / sample_count
    centred = hidden_float - batch_average
    spread = lax.psum(jnp.sum(centred * centred, axis=1), "batch")
    var = spread[:, None, :] / sample_count
    inverse_deviation = 1.0 / jnp.sqrt(var + eps_norm)
    normalised_input = (hidden_float - batch_average) * inverse_deviation
    preactivation = norm_scale_gain * normalised_input + norm_shift_bias
    act = jax.nn.gelu(preactivation, approximate=True).astype(jnp.bfloat16)
    act_full = lax.all_gather(act, "col", axis=2, tiled=True)
    z_local = jnp.einsum(
        "vrk,kj->vrj", act_full, weight, preferred_element_type=jnp.float32
    ).astype(jnp.bfloat16)
    z_all = lax.all_gather(z_local, "batch", axis=1, tiled=True)
    zf_all = z_all.astype(jnp.float32)
    zmean = jnp.mean(zf_all, axis=1, keepdims=True)
    zc_all = zf_all - zmean
    zvar = jnp.sum(zc_all * zc_all, axis=1, keepdims=True) / (sample_count - 1)
    std = jnp.sqrt(zvar + eps_std)
    zcb_all = zc_all.astype(jnp.bfloat16)
    offset = lax.axis_index("batch") * local_rows
    zc_loc = lax.dynamic_slice_in_dim(zc_all, offset, local_rows, 1)
    zcb_loc = zc_loc.astype(jnp.bfloat16)
    diag = jnp.sum(jnp.square(zcb_all.astype(jnp.float32)), axis=1, keepdims=True)
    kernel_part = jnp.einsum("vrj,vmj->vrm", zcb_loc, zcb_all, preferred_element_type=jnp.float32)
    kernel = lax.psum(kernel_part, "col")
    kernel_b = kernel.astype(jnp.bfloat16)
    denom = float((sample_count - 1) ** 2 * E)
    coef = 4.0 * scale / denom
    hinge_coef = 25.0 * scale / (2.0 * E * (sample_count - 1))
    mask = jnp.where(std < 1.0, 1.0, 0.0)
    moved = jnp.einsum("vrm,vmj->vrj", kernel_b, zcb_all, preferred_element_type=jnp.float32)
    g_cov = coef * (moved - zcb_loc.astype(jnp.float32) * diag)
    g_var = -hinge_coef * mask * zc_loc / std
    summed = g_cov + g_var
    col_total = lax.psum(jnp.sum(summed, axis=1), "batch")
    zf_loc = z_local.astype(jnp.float32)
    diff = zf_loc[0] - zf_loc[1]
    g_inv = 50.0 * scale / (sample_count * E) * diff
    dz = summed - col_total[:, None, :] / sample_count + jnp.stack([g_inv, -g_inv])
    dzb = dz.astype(jnp.bfloat16)
    inv_share = jnp.sum(diff * diff) / (sample_count * E)
    hinge_share = jnp.sum(jnp.maximum(1.0 - std, 0.0)) / (2 * E)
    block_share = jnp.sum(kernel * kernel) / denom
    diag_share = jnp.sum(diag * diag) / denom
    share = 25.0 * inv_share + (25.0 * hinge_share - diag_share) / n_batch + block_share / n_col
    loss = lax.psum(share, ("batch", "col"))
    d_act_t = lax.psum_scatter(
        jnp.einsum("kj,vrj->kvr", weight, dzb, preferred_element_type=jnp.float32),
        "col",
        scatter_dimension=0,
        tiled=True,
    )
    d_act = jnp.transpose(d_act_t, (1, 2, 0))
    act_block = lax.all_to_all(act_full, "batch", split_axis=2, concat_axis=1, tiled=True)
    dz_all = lax.all_gather(dzb, "batch", axis=1, tiled=True)
    grad_weight = jnp.einsum("vnk,vnj->kj", act_block, dz_all, preferred_element_type=jnp.float32)
    preactivation_gradient = d_act * gelu_slope(preactivation)
    bias_gradient_sum, gain_gradient_sum = lax.psum(
        (
            jnp.sum(preactivation_gradient, axis=1),
            jnp.sum(preactivation_gradient * normalised_input, axis=1),
        ),
        "batch",
    )
    grad_bias = jnp.sum(bias_gradient_sum, axis=0)
    grad_gain = jnp.sum(gain_gradient_sum, axis=0)
    views_gradient = (
        norm_scale_gain
        * (
            preactivation_gradient
            - bias_gradient_sum[:, None, :] / sample_count
            - normalised_input * gain_gradient_sum[:, None, :] / sample_count
        )
        * inverse_deviation
    )
    return (loss, grad_weight, grad_gain, grad_bias, views_gradient)


def solution(mesh):
    placed = (P(None, "batch", "col"), P("col"), P("col"), P(None, "col"))
    return jax.shard_map(
        shards,
        mesh=mesh,
        in_specs=placed,
        out_specs=(P(), P("batch", "col"), P("col"), P("col"), P(None, "batch", "col")),
        check_vma=False,
    )
```

profile of v0, /device:TPU:0, one launch (start us, length us, event | category | flops | bytes accessed | tf_op | source)
XLA Modules:
  0.0 357.7 jit_solution(475246103151398990)
XLA Ops:
  7.2 0.0 all-gather.4.cloned.1.call-start
  7.2 1.0 convert_reduce_fusion.1
  8.2 13.5 %psum.49 = f32[2,512]{1,0:T(2,128)S(1)} all-reduce(f32[2,512]{1,0:T(2,128)S(1)} %convert_reduce_fusion.1), channel_id=1, replica_groups=mesh['batch'=4,'col'=8] {'batch'}, use_global_device_ids=true, to_apply=%region_1.0 | all-reduce | flops 1024 | bytes 8192 | tf_op jit(solution)/shard_map/psum | solution.py:25
  21.7 1.0 fusion.43
  22.7 8.4 %psum.50 = f32[2,512]{1,0:T(2,128)S(1)} all-reduce(f32[2,512]{1,0:T(2,128)S(1)} %fusion.43), channel_id=1, replica_groups=mesh['batch'=4,'col'=8] {'batch'}, use_global_device_ids=true, to_apply=%region_3.0 | all-reduce | flops 1024 | bytes 8192 | tf_op jit(solution)/shard_map/psum | solution.py:28
  31.1 1.9 fusion.36
  33.0 0.0 all-gather.4.cloned.1.call-update
  33.1 0.0 all-gather.6.cloned.1.call-start
  33.1 28.0 %all-gather.4.cloned.1.call-done = bf16[2,128,4096]{2,1,0:T(8,128)(2,1)} async-done(((bf16[2,128,512]{2,1,0:T(8,128)(2,1)}), bf16[2,128,4096]{2,1,0:T(8,128)(2,1)}) %all-gather.4.cloned.1.call-update) | async-done | bytes 2097168 | tf_op jit(solution)/shard_map/all_gather | solution.py:34
  61.1 7.5 %fusion.54 = (f32[2,128,1024]{2,1,0:T(8,128)}, bf16[2,128,1024]{2,1,0:T(8,128)(2,1)}) fusion(bf16[2,128,4096]{2,1,0:T(8,128)(2,1)} %all-gather.4.cloned.1.call-done, bf16[4096,1024]{1,0:T(8,128)(2,1)} %param.7), kind=kOutput, calls=%fused_computation.66 | convolution fusion | flops 2148007936 | bytes 12058624 | tf_op jit(solution)/shard_map/vrk,kj->vrj/dot_general | solution.py:35
  68.6 0.0 all-gather.6.cloned.1.call-update
  68.6 0.0 all-reduce.3.cloned.1.call-start
  68.6 46.0 %all-gather.6.cloned.1.call-done = bf16[2,512,1024]{2,1,0:T(8,128)(2,1)} async-done(((bf16[2,128,1024]{2,1,0:T(8,128)(2,1)}), bf16[2,512,1024]{2,1,0:T(8,128)(2,1)}) %all-gather.6.cloned.1.call-update) | async-done | bytes 2097168 | tf_op jit(solution)/shard_map/all_gather | solution.py:38
  114.7 2.1 convert_reduce_fusion
  116.8 2.3 multiply_reduce_fusion
  119.0 0.0 copy-start.3
  119.1 2.0 copy-done.3
  121.1 1.6 fusion.10
  122.7 0.0 all-reduce.3.cloned.1.call-update
  122.7 0.0 all-gather.8.cloned.1.call-start
  122.8 2.0 fusion.53
  124.8 51.4 %all-reduce.3.cloned.1.call-done = f32[2,128,512]{2,1,0:T(8,128)} async-done(((f32[2,128,512]{2,1,0:T(8,128)}), f32[2,128,512]{2,1,0:T(8,128)}) %all-reduce.3.cloned.1.call-update) | async-done | bytes 524304 | tf_op jit(solution)/shard_map/psum | solution.py:50
  176.1 3.1 fusion.55
  179.2 11.7 %psum.53 = f32[2,1024]{1,0:T(2,128)S(1)} all-reduce(f32[2,1024]{1,0:T(2,128)S(1)} %get-tuple-element.22), channel_id=1, replica_groups=mesh['batch'=4,'col'=8] {'batch'}, use_global_device_ids=true, to_apply=%region_14.15 | all-reduce | flops 2048 | bytes 16384 | tf_op jit(solution)/shard_map/psum | solution.py:60
  191.0 2.2 fusion.24
  193.2 0.0 all-gather.8.cloned.1.call-update
  193.2 0.0 reduce-scatter.2.cloned.1.call-start
  193.3 8.0 %fusion.4 = f32[4096,2,128]{0,2,1:T(8,128)} fusion(bf16[2,128,1024]{2,1,0:T(8,128)(2,1)} %fusion.24, bf16[4096,1024]{1,0:T(8,128)(2,1)} %param.7), kind=kOutput, calls=%fused_computation.4 | convolution fusion | flops 2147483648 | bytes 13107200 | tf_op jit(solution)/shard_map/kj,vrj->kvr/dot_general | solution.py:73
  201.2 0.0 reduce-scatter.2.cloned.1.call-update
  201.2 1.6 copy-done.4
  202.8 3.8 %copy.10 = bf16[2,128,4096]{1,0,2:T(2,128)(2,1)} copy(bf16[2,128,4096]{2,1,0:T(8,128)(2,1)S(1)} %copy-done.4) | data formatting | bytes 4194304 | tf_op jit(solution)/shard_map/all_gather | solution.py:34
  206.6 3.7 %all-to-all-start = ((bf16[2,128,4096]{1,0,2:T(2,128)(2,1)}), bf16[2,128,4096]{1,0,2:T(2,128)(2,1)S(1)}, u32[]{:S(2)}, u32[]{:S(2)}) async-start(bf16[2,128,4096]{1,0,2:T(2,128)(2,1)} %copy.10), calls=%async_computation | async-start | bytes 4194304 | tf_op jit(solution)/shard_map/all_to_all | solution.py:79
  211.0 69.3 %all-to-all-done = bf16[2,128,4096]{1,0,2:T(2,128)(2,1)S(1)} async-done(((bf16[2,128,4096]{1,0,2:T(2,128)(2,1)}), bf16[2,128,4096]{1,0,2:T(2,128)(2,1)S(1)}, u32[]{:S(2)}, u32[]{:S(2)}) %all-to-all-start) | async-done | bytes 2097184 | tf_op jit(solution)/shard_map/all_to_all | solution.py:79
  280.3 1.3 copy-done.1
  281.6 3.4 copy.13
  285.0 0.6 maximum_reduce_fusion
  286.3 0.6 multiply_reduce_fusion.4
  287.6 0.7 multiply_reduce_fusion.2
  289.0 2.3 all_to_all.16
  291.2 38.2 %psum.52 = f32[]{:T(128)} all-reduce(f32[]{:T(128)S(6)} %add.81), channel_id=1, replica_groups=mesh['batch'=4,'col'=8] {'batch','col'}, use_global_device_ids=true, to_apply=%region_12.13 | all-reduce | flops 1 | bytes 8 | tf_op jit(solution)/shard_map/psum | solution.py:71
  329.4 0.0 all-gather.8.cloned.1.call-done
  329.4 6.6 %convolution_bitcast_fusion = f32[1024,1024]{1,0:T(8,128)} fusion(bf16[2,512,1024]{1,2,0:T(8,128)(2,1)} %all_to_all.16, bf16[2,512,1024]{2,1,0:T(8,128)(2,1)} %all-gather.8.cloned.1.call-done), kind=kOutput, calls=%fused_computation.9 | convolution fusion | flops 2147483648 | bytes 8388608 | tf_op jit(solution)/shard_map/vnk,vnj->kj/dot_general | solution.py:81
  336.0 0.0 copy-done.7
  336.0 1.5 fusion.51
  337.6 11.4 %all-reduce = (f32[2,512]{1,0:T(2,128)S(1)}, f32[2,512]{1,0:T(2,128)S(1)}) all-reduce(f32[2,512]{1,0:T(2,128)S(1)} %get-tuple-element.8, f32[2,512]{1,0:T(2,128)S(1)} %get-tuple-element.7), channel_id=1, replica_groups=mesh['batch'=4,'col'=8] {'batch'}, use_global_device_ids=true, to_apply=%region_17.18 | all-reduce | flops 2048 | bytes 16384 | tf_op jit(solution)/shard_map/psum | solution.py:83
  349.0 0.6 broadcast_multiply_fusion.3
  349.6 0.6 reduce_sum.137
  350.2 1.0 fusion.42
  (17 shorter events, 0.1 us)
Async XLA Ops:
  7.2 53.9 %all-gather.4.cloned.1.call-start = ((), (), s32[]{:S(2)}) async-start(), calls=%async_computation.2 | async-start | bytes 2359296 | tf_op jit(solution)/shard_map/all_gather | solution.py:34
  33.1 81.6 %all-gather.6.cloned.1.call-start = ((), (), s32[]{:S(2)}) async-start(), calls=%async_computation.3 | async-start | bytes 2621440 | tf_op jit(solution)/shard_map/all_gather | solution.py:38
  68.6 107.5 %all-reduce.3.cloned.1.call-start = ((), (), s32[]{:S(2)}) async-start(), calls=%async_computation.4 | async-start | bytes 1048576 | tf_op jit(solution)/shard_map/psum | solution.py:50
  114.7 6.4 %copy-start = (bf16[2,512,1024]{2,1,0:T(8,128)(2,1)S(1)}, bf16[2,512,1024]{2,1,0:T(8,128)(2,1)}, u32[]{:S(2)}) copy-start(bf16[2,512,1024]{2,1,0:T(8,128)(2,1)} %all-gather.6.cloned.1.call-done) | copy-start | bytes 6291460
  119.0 2.0 copy-start.3
  122.7 206.7 %all-gather.8.cloned.1.call-start = ((), (), s32[]{:S(2)}) async-start(), calls=%async_computation.5 | async-start | bytes 2621440 | tf_op jit(solution)/shard_map/all_gather | solution.py:80
  193.2 142.8 %reduce-scatter.2.cloned.1.call-start = ((), (), s32[]{:S(2)}) async-start(), calls=%async_computation.6 | async-start | bytes 4718592 | tf_op jit(solution)/shard_map/reduce_scatter | solution.py:72
  201.2 1.6 copy-start.4
  206.6 81.0 %copy-start.5 = (f32[2,128,512]{2,1,0:T(8,128)S(1)}, f32[2,128,512]{2,1,0:T(8,128)}, u32[]{:S(2)}) copy-start(f32[2,128,512]{2,1,0:T(8,128)} %all-reduce.3.cloned.1.call-done) | copy-start | bytes 1572868
  206.6 73.7 %all-to-all-start = ((bf16[2,128,4096]{1,0,2:T(2,128)(2,1)}), bf16[2,128,4096]{1,0,2:T(2,128)(2,1)S(1)}, u32[]{:S(2)}, u32[]{:S(2)}) async-start(bf16[2,128,4096]{1,0,2:T(2,128)(2,1)} %copy.10), calls=%async_computation | async-start | bytes 4194304 | tf_op jit(solution)/shard_map/all_to_all | solution.py:79
  280.3 1.3 copy-start.1
  329.4 6.6 %copy-start.2 = (bf16[2,128,512]{2,1,0:T(8,128)(2,1)S(1)}, bf16[2,128,512]{2,1,0:T(8,128)(2,1)}, u32[]{:S(2)}) copy-start(bf16[2,128,512]{2,1,0:T(8,128)(2,1)} %param.4) | copy-start | bytes 786436
  329.4 6.6 %copy-start.6 = (f32[512]{0:T(512)S(1)}, f32[512]{0:T(512)}, u32[]{:S(2)}) copy-start(f32[512]{0:T(512)} %param.5) | copy-start | bytes 6148
  329.4 6.6 %copy-start.7 = (f32[512]{0:T(512)S(1)}, f32[512]{0:T(512)}, u32[]{:S(2)}) copy-start(f32[512]{0:T(512)} %param.6) | copy-start | bytes 6148
Sparse Core Ops, SparseCore 0:
  33.2 27.8 all-gather.3
  68.7 45.9 all-gather.5
  122.8 53.2 all-reduce.2
  193.3 66.6 all-gather.7
  263.6 60.9 reduce-scatter.1
where the time goes:
time: 358 us
  waiting for transfers between devices  195 us (54%)
  blocking collectives  83.2 us (23%)
  matrix products  26.8 us (7%)
  other arithmetic  18.2 us (5%)
  between operations  16.5 us (5%)
  local copies, waits for them, and re-layouts  14.3 us (4%)
  starting transfers between devices  3.95 us (1%)
    all_to_all x1, waiting for transfers between devices, shards(): lax.all_to_all(act_full, 'batch', split_axis=2, concat_axis=1, tiled=True)  69.3 us
    psum x1, waiting for transfers between devices, shards(): kernel = lax.psum(kernel_part, 'col')  51.4 us
    all_gather x1, waiting for transfers between devices, shards(): z_all = lax.all_gather(z_local, 'batch', axis=1, tiled=True)  46 us
    psum x1, blocking collectives, shards(): loss = lax.psum(share, ('batch', 'col'))  38.2 us
    all_gather x1, waiting for transfers between devices, shards(): act_full = lax.all_gather(act, 'col', axis=2, tiled=True)  28 us
    psum x1, blocking collectives, shards(): total = lax.psum(jnp.sum(hidden_float, axis=1), 'batch')  13.5 us
    psum x1, blocking collectives, shards(): col_total = lax.psum(jnp.sum(summed, axis=1), 'batch')  11.7 us
    psum x1, blocking collectives, shards(): lax.psum((jnp.sum(preactivation_gradient, axis=1), jnp.sum(preactivation_...  11.4 us
  transfers between devices with their start and end apart: 6, of which 4 were waited for; matrix products, arithmetic and copies ran while one was open for 7% of the time, Pallas kernels for 0%

commit v1 on v0

v1 whole, which is shorter than its diff:
```python
import jax
import jax.numpy as jnp
from jax import lax
from jax.sharding import PartitionSpec as P

eps_norm = 1e-05
eps_std = 0.0001
f32 = jnp.float32
bf16 = jnp.bfloat16


def gelu_slope(preactivation):
    value, pullback = jax.vjp(lambda t: jax.nn.gelu(t, approximate=True), preactivation)
    return pullback(jnp.ones_like(value))[0]


def xor_send(x, axis, k):
    n = lax.axis_size(axis)
    return lax.ppermute(x, axis, [(i, i ^ k) for i in range(n)])


def low_bit(k):
    return k & -k


def high_bit(k):
    return 1 << (k.bit_length() - 1)


def ring_order(n):
    return list(range(0, n, 2)) + list(range(1, n, 2))[::-1]


def ring_send(x, axis):
    order = ring_order(lax.axis_size(axis))
    n = len(order)
    return lax.ppermute(x, axis, [(order[i], order[(i + 1) % n]) for i in range(n)])


def exchange(x, axis):
    n = lax.axis_size(axis)
    me = lax.axis_index(axis)
    slots = [x]
    for d in range(1, n):
        slots.append(lax.ppermute(x, axis, [(i, (i + d) % n) for i in range(n)]))
    ordered = []
    for a in range(n):
        value = slots[0]
        for d in range(1, n):
            value = jnp.where((me - a) % n == d, slots[d], value)
        ordered.append(value)
    return ordered


def gather_pieces(x, axis):
    n = lax.axis_size(axis)
    pieces = {0: x}
    half = x.shape[0] // 2
    for k in sorted(range(2, n, 2), key=lambda k: (bin(k).count("1"), k)):
        lo, hi = low_bit(k), high_bit(k)
        if lo == hi:
            pieces[k] = xor_send(x, axis, k)
        else:
            first = xor_send(pieces[k ^ lo][:half], axis, lo)
            second = xor_send(pieces[k ^ hi][half:], axis, hi)
            pieces[k] = jnp.concatenate([first, second])
    for k in range(0, n, 2):
        pieces[k + 1] = xor_send(pieces[k], axis, 1)
    return [pieces[k] for k in range(n)]


def scatter_pieces(parts, axis, wire):
    n = lax.axis_size(axis)
    total = []
    for k in range(0, n, 2):
        got = xor_send(parts[k + 1].astype(wire), axis, 1)
        total.append(parts[k] + got.astype(f32))
    result = total[0]
    for k in range(2, n, 2):
        result = result + xor_send(total[k // 2].astype(wire), axis, k).astype(f32)
    return result


def shards(views, norm_scale_gain, norm_shift_bias, weight):
    n_batch = lax.axis_size("batch")
    n_col = lax.axis_size("col")
    b = lax.axis_index("batch")
    c = lax.axis_index("col")
    n_view, local_rows, width = views.shape
    columns = weight.shape[1]
    E = columns * n_col
    rows = local_rows * n_batch
    scale = rows * E / 128.0
    with jax.named_scope("norm_stats"):
        hidden = views.astype(f32)
        local_mean = jnp.mean(hidden, axis=1)
        local_centred = hidden - local_mean[:, None, :]
        local_spread = jnp.sum(local_centred * local_centred, axis=1)
        stats = exchange(jnp.concatenate([local_mean, local_spread]), "batch")
        mean = sum(s[:n_view] for s in stats) / n_batch
        spread = sum(s[n_view:] + local_rows * jnp.square(s[:n_view] - mean) for s in stats)
        var = spread / rows
        inverse_deviation = (1.0 / jnp.sqrt(var + eps_norm))[:, None, :]
        normalised = (hidden - mean[:, None, :]) * inverse_deviation
        preactivation = norm_scale_gain * normalised + norm_shift_bias
        act = jax.nn.gelu(preactivation, approximate=True).astype(bf16)
    with jax.named_scope("weight_order"):
        blocks = weight.reshape(n_col, width, columns)
        weight_xor = jnp.concatenate(
            [lax.dynamic_index_in_dim(blocks, c ^ k, 0, keepdims=True) for k in range(n_col)]
        ).reshape(n_col * width, columns)
    with jax.named_scope("act_gather"):
        slots = [act]
        for _ in range(1, n_batch):
            slots.append(ring_send(slots[-1], "batch"))
        pieces = [gather_pieces(s, "col") for s in slots]
    with jax.named_scope("z"):
        acts = [jnp.concatenate(p, axis=2) for p in pieces]
        z = jnp.concatenate(
            [
                jnp.einsum("vrk,kj->vrj", a, weight_xor, preferred_element_type=f32).astype(bf16)
                for a in acts
            ],
            axis=1,
        )
    with jax.named_scope("z_stats"):
        zf = z.astype(f32)
        zc = zf - jnp.mean(zf, axis=1, keepdims=True)
        zvar = jnp.sum(zc * zc, axis=1, keepdims=True) / (rows - 1)
        std = jnp.sqrt(zvar + eps_std)
        zcb = zc.astype(bf16)
        diag = jnp.sum(jnp.square(zcb.astype(f32)), axis=1, keepdims=True)
    with jax.named_scope("kernel"):
        kernel_part = jnp.einsum("vrj,vmj->vrm", zcb, zcb, preferred_element_type=f32)
        strip = rows // n_col
        parts = [
            lax.dynamic_slice_in_dim(kernel_part, (c ^ k) * strip, strip, 1) for k in range(n_col)
        ]
        kernel = scatter_pieces(parts, "col", f32)
        kernel_b = jnp.zeros((n_view, rows, rows), bf16)
        for k, piece in enumerate(gather_pieces(kernel.astype(bf16), "col")):
            kernel_b = lax.dynamic_update_slice_in_dim(kernel_b, piece, (c ^ k) * strip, 1)
    denom = float((rows - 1) ** 2 * E)
    coef = 4.0 * scale / denom
    hinge_coef = 25.0 * scale / (2.0 * E * (rows - 1))
    with jax.named_scope("dz"):
        mask = jnp.where(std < 1.0, 1.0, 0.0)
        moved = jnp.einsum("vrm,vmj->vrj", kernel_b, zcb, preferred_element_type=f32)
        summed = coef * (moved - zcb.astype(f32) * diag) - hinge_coef * mask * zc / std
        diff = zf[0] - zf[1]
        g_inv = 50.0 * scale / (rows * E) * diff
        dz = summed - jnp.mean(summed, axis=1, keepdims=True) + jnp.stack([g_inv, -g_inv])
        dzb = dz.astype(bf16)
    with jax.named_scope("loss"):
        inv_share = jnp.sum(diff * diff) / (rows * E)
        hinge_share = jnp.sum(jnp.maximum(1.0 - std, 0.0)) / (2 * E)
        block_share = jnp.sum(kernel * kernel) / denom
        diag_share = jnp.sum(diag * diag) / denom
        share = 25.0 * inv_share + 25.0 * hinge_share - diag_share + block_share
        share = jnp.broadcast_to(share, (8, 128))
        for axis, n in (("col", n_col), ("batch", n_batch)):
            k = 1
            while k < n:
                share = share + xor_send(share, axis, k)
                k *= 2
        loss = share[0, 0] / n_batch
    with jax.named_scope("d_act"):
        d_parts = [
            jnp.einsum(
                "vrj,kj->vrk",
                dzb[:, :local_rows],
                weight_xor[k * width : (k + 1) * width],
                preferred_element_type=f32,
            )
            for k in range(n_col)
        ]
        d_act = scatter_pieces(d_parts, "col", bf16)
    with jax.named_scope("grad_weight"):
        share_pieces = n_col // n_batch
        wanted = jnp.concatenate(
            [
                jnp.concatenate(
                    [
                        lax.dynamic_slice_in_dim(
                            a, (c ^ (b * share_pieces + i)) * width, width, 2
                        )
                        for i in range(share_pieces)
                    ],
                    axis=2,
                )
                for a in acts
            ],
            axis=1,
        )
        grad_weight = jnp.einsum("vnk,vnj->kj", wanted, dzb, preferred_element_type=f32)
    with jax.named_scope("norm_backward"):
        d_pre = d_act * gelu_slope(preactivation)
        sums = jnp.concatenate(
            [
                jnp.sum(d_pre, axis=1),
                jnp.sum(d_pre * normalised, axis=1),
            ]
        )
        everyone = exchange(sums, "batch")
        both = sum(everyone)
        sum_b, sum_g = both[:n_view], both[n_view : 2 * n_view]
        grad_bias = jnp.sum(sum_b, axis=0)
        grad_gain = jnp.sum(sum_g, axis=0)
        views_gradient = (
            norm_scale_gain
            * (d_pre - sum_b[:, None, :] / rows - normalised * sum_g[:, None, :] / rows)
            * inverse_deviation
        )
    return (loss, grad_weight, grad_gain, grad_bias, views_gradient)


def solution(mesh):
    placed = (P(None, "batch", "col"), P("col"), P("col"), P(None, "col"))
    return jax.shard_map(
        shards,
        mesh=mesh,
        in_specs=placed,
        out_specs=(P(), P("batch", "col"), P("col"), P("col"), P(None, "batch", "col")),
        check_vma=False,
    )
```

time: 358 us -> 183 us (0.51)
  waiting for transfers between devices: 195 us -> 39.3 us
  blocking collectives: 83.2 us -> 0 us
  starting transfers between devices: 3.95 us -> 57.6 us
  local copies, waits for them, and re-layouts: 14.3 us -> 32.2 us
  between operations: 16.5 us -> 6.18 us
  matrix products: 26.8 us -> 30.4 us
    psum x5 -> x0, blocking collectives: 83.2 us -> none  [the longest x1 38.2 us: shards(): loss = lax.psum(share, ('batch', 'col'))]
    all_gather x3 -> x0, waiting for transfers between devices: 74 us -> none  [the longest x1 46 us: shards(): z_all = lax.all_gather(z_local, 'batch', axis=1, tiled=True)]
    all_to_all x1 -> x0, waiting for transfers between devices: 69.3 us -> none  [shards(): lax.all_to_all(act_full, 'batch', split_axis=2, concat_axis=1, tiled=True)]
    ppermute x0 -> x68, starting transfers between devices: none -> 57.6 us  [the longest x59 43.4 us: xor_send(): return lax.ppermute(x, axis, [(i, i ^ k) for i in range(n)])]
    psum x1 -> x0, waiting for transfers between devices: 51.4 us -> none  [shards(): kernel = lax.psum(kernel_part, 'col')]
    ppermute x0 -> x68, waiting for transfers between devices: none -> 39.3 us  [the longest x59 34.9 us: xor_send(): return lax.ppermute(x, axis, [(i, i ^ k) for i in range(n)])]
    unnamed x16 -> x87, local copies, waits for them, and re-layouts: 4.91 us -> 17.8 us
    all_to_all x2 -> x0, local copies, waits for them, and re-layouts: 5.65 us -> none  [shards(): lax.all_to_all(act_full, 'batch', split_axis=2, concat_axis=1, tiled=True)]
  transfers between devices with their start and end apart: 6 -> 68, of which waited for: 4 -> 18; matrix products, arithmetic and copies ran while one was open for 7% -> 35% of each run, Pallas kernels for 0% -> 0%
where the time goes in v1:
time: 183 us; the launch traced here: 182 us
  starting transfers between devices  57.6 us (31%)
  waiting for transfers between devices  39.3 us (21%)
  local copies, waits for them, and re-layouts  32.2 us (18%)
  matrix products  30.4 us (17%)
  other arithmetic  16.6 us (9%)
  between operations  6.18 us (3%)
    ppermute x59, starting transfers between devices, xor_send(): return lax.ppermute(x, axis, [(i, i ^ k) for i in range(n)])  43.4 us
    ppermute x59, waiting for transfers between devices, xor_send(): return lax.ppermute(x, axis, [(i, i ^ k) for i in range(n)])  34.9 us
    unnamed x87, local copies, waits for them, and re-layouts  17.8 us
    dot_general x4, matrix products, shards(): jnp.einsum('vrk,kj->vrj', a, weight_xor, preferred_element_type=f32)  13.7 us
    ppermute x6, starting transfers between devices, exchange(): slots.append(lax.ppermute(x, axis, [(i, (i + d) % n) for i in range(n)]))  8.58 us
    dot_general x1, matrix products, shards(): jnp.einsum('vnk,vnj->kj', wanted, dzb, preferred_element_type=f32)  7.8 us
    ppermute x3, starting transfers between devices, ring_send(): lax.ppermute(x, axis, [(order[i], order[(i + 1) % n]) for i in range(n)])  5.57 us
    dynamic_update_slice x7, local copies, waits for them, and re-layouts, shards(): lax.dynamic_update_slice_in_dim(kernel_b, piece, (c ^ k) * strip, 1)  4.68 us
  transfers between devices with their start and end apart: 68, of which 18 were waited for; matrix products, arithmetic and copies ran while one was open for 35% of the time, Pallas kernels for 0%

profile of v1, /device:TPU:0, one launch (start us, length us, event | category | flops | bytes accessed | tf_op | source)
XLA Modules:
  0.0 182.3 jit_solution(12125638104582130402)
XLA Ops:
  2.7 5.1 %collective-permute-start = (f32[4,512]{1,0:T(4,128)S(1)}, f32[4,512]{1,0:T(4,128)S(1)}, u32[]{:S(2)}, u32[]{:S(2)}) collective-permute-start(f32[4,512]{1,0:T(4,128)S(1)} %pad_maximum_fusion.5), channel_id=1, source_target_pairs={{0,24},{8,0},{16,8},{24,16},{1,25},{9,1},{17,9},{25,17},{2,26},{10... | collective-permute-start | bytes 24584 | tf_op jit(solution)/shard_map/norm_stats/ppermute | solution.py:45
  8.8 2.3 %dynamic-slice_dynamic-update-slice_fusion.7 = bf16[8,512,1024]{2,1,0:T(8,128)(2,1)} fusion(bf16[8,512,1024]{2,1,0:T(8,128)(2,1)} %bitcast.55, s32[]{:T(128)S(6)} %select_n.287), kind=kLoop, calls=%fused_computation.70 | loop fusion | bytes 2097156
  11.1 2.3 %dynamic-slice_dynamic-update-slice_fusion.6 = bf16[8,512,1024]{2,1,0:T(8,128)(2,1)} fusion(bf16[8,512,1024]{2,1,0:T(8,128)(2,1)} %dynamic-slice_dynamic-update-slice_fusion.7, bf16[8,512,1024]{2,1,0:T(8,128)(2,1)} %bitcast.56, s32[]{:T(128)S(6)} %select_n.288), kind=kLoop, calls=%fused_computation.68 | loop fusion | bytes 2097156
  13.4 2.3 %dynamic-slice_dynamic-update-slice_fusion.5 = bf16[8,512,1024]{2,1,0:T(8,128)(2,1)} fusion(bf16[8,512,1024]{2,1,0:T(8,128)(2,1)} %dynamic-slice_dynamic-update-slice_fusion.6, bf16[8,512,1024]{2,1,0:T(8,128)(2,1)} %bitcast.57, s32[]{:T(128)S(6)} %select_n.289), kind=kLoop, calls=%fused_computation.66 | loop fusion | bytes 2097156
  15.7 2.3 %dynamic-slice_dynamic-update-slice_fusion.4 = bf16[8,512,1024]{2,1,0:T(8,128)(2,1)} fusion(bf16[8,512,1024]{2,1,0:T(8,128)(2,1)} %dynamic-slice_dynamic-update-slice_fusion.5, bf16[8,512,1024]{2,1,0:T(8,128)(2,1)} %bitcast.58, s32[]{:T(128)S(6)} %select_n.290), kind=kLoop, calls=%fused_computation.64 | loop fusion | bytes 2097156
  18.0 2.3 %dynamic-slice_dynamic-update-slice_fusion.3 = bf16[8,512,1024]{2,1,0:T(8,128)(2,1)} fusion(bf16[8,512,1024]{2,1,0:T(8,128)(2,1)} %dynamic-slice_dynamic-update-slice_fusion.4, bf16[8,512,1024]{2,1,0:T(8,128)(2,1)} %bitcast.59, s32[]{:T(128)S(6)} %select_n.291), kind=kLoop, calls=%fused_computation.62 | loop fusion | bytes 2097156
  20.3 2.3 %dynamic-slice_dynamic-update-slice_fusion.2 = bf16[8,512,1024]{2,1,0:T(8,128)(2,1)} fusion(bf16[8,512,1024]{2,1,0:T(8,128)(2,1)} %dynamic-slice_dynamic-update-slice_fusion.3, bf16[8,512,1024]{2,1,0:T(8,128)(2,1)} %bitcast.60, s32[]{:T(128)S(6)} %select_n.292), kind=kLoop, calls=%fused_computation.60 | loop fusion | bytes 2097156
  23.0 2.0 %collective-permute-start.11 = (bf16[2,128,512]{2,1,0:T(8,128)(2,1)S(1)}, bf16[2,128,512]{2,1,0:T(8,128)(2,1)S(1)}, u32[]{:S(2)}, u32[]{:S(2)}) collective-permute-start(bf16[2,128,512]{2,1,0:T(8,128)(2,1)S(1)} %get-tuple-element.20), channel_id=1, source_target_pairs={{0,16},{16,24},{24,8},{8,0},{1,17},{17,25},{25,9},{9,1},{2,18},{18... | collective-permute-start | bytes 786440 | tf_op jit(solution)/shard_map/act_gather/ppermute | solution.py:37
  25.0 1.5 collective-permute-start.4
  26.5 1.5 collective-permute-start.6
  28.0 2.3 %dynamic-slice_dynamic-update-slice_fusion.1 = bf16[8,512,1024]{2,1,0:T(8,128)(2,1)} fusion(bf16[8,512,1024]{2,1,0:T(8,128)(2,1)} %dynamic-slice_dynamic-update-slice_fusion.2, bf16[8,512,1024]{2,1,0:T(8,128)(2,1)} %bitcast.61, s32[]{:T(128)S(6)} %select_n.293), kind=kLoop, calls=%fused_computation.58 | loop fusion | bytes 2097156
  30.3 2.3 %dynamic-slice_dynamic-update-slice_fusion = bf16[8,512,1024]{2,1,0:T(8,128)(2,1)} fusion(bf16[8,512,1024]{2,1,0:T(8,128)(2,1)} %dynamic-slice_dynamic-update-slice_fusion.1, bf16[8,512,1024]{2,1,0:T(8,128)(2,1)} %bitcast.62, s32[]{:T(128)S(6)} %select_n.294), kind=kLoop, calls=%fused_computation.56 | loop fusion | bytes 2097156 | tf_op jit(solution)/shard_map/weight_order/concatenate | solution.py:109
  32.6 2.3 %collective-permute-done.6 = bf16[2,128,512]{2,1,0:T(8,128)(2,1)S(1)} collective-permute-done((bf16[2,128,512]{2,1,0:T(8,128)(2,1)S(1)}, bf16[2,128,512]{2,1,0:T(8,128)(2,1)S(1)}, u32[]{:S(2)}, u32[]{:S(2)}) %collective-permute-start.6) | collective-permute-done | bytes 262176 | tf_op jit(solution)/shard_map/act_gather/ppermute | solution.py:19
  35.5 1.6 collective-permute-start.9
  37.1 1.5 collective-permute-start.13
  40.0 2.3 %collective-permute-start.15 = (bf16[2,128,512]{2,1,0:T(8,128)(2,1)S(1)}, bf16[2,128,512]{2,1,0:T(8,128)(2,1)S(1)}, u32[]{:S(2)}, u32[]{:S(2)}) collective-permute-start(bf16[2,128,512]{2,1,0:T(8,128)(2,1)S(1)} %collective-permute-done.11), channel_id=1, source_target_pairs={{0,4},{1,5},{2,6},{3,7},{4,0},{5,1},{6,2},{7,3},{8,12},{9,13},{10,... | collective-permute-start | bytes 786440 | tf_op jit(solution)/shard_map/act_gather/ppermute | solution.py:19
  42.3 1.5 collective-permute-start.20
  43.9 4.7 %collective-permute-done.15 = bf16[2,128,512]{2,1,0:T(8,128)(2,1)S(1)} collective-permute-done((bf16[2,128,512]{2,1,0:T(8,128)(2,1)S(1)}, bf16[2,128,512]{2,1,0:T(8,128)(2,1)S(1)}, u32[]{:S(2)}, u32[]{:S(2)}) %collective-permute-start.15) | collective-permute-done | bytes 262176 | tf_op jit(solution)/shard_map/act_gather/ppermute | solution.py:19
  51.6 1.6 collective-permute-start.24
  53.2 6.5 %convolution_convert_fusion.3 = bf16[2,128,1024]{2,1,0:T(8,128)(2,1)S(1)} fusion(bf16[2,128,4096]{2,1,0:T(8,128)(2,1)S(1)} %constant_dynamic-update-slice_fusion, bf16[4096,1024,1]{1,0,2:T(8,128)(2,1)} %bitcast.73), kind=kOutput, calls=%fused_computation.37 | convolution fusion | flops 2147745792 | bytes 11010048 | tf_op jit(solution)/shard_map/z/vrk,kj->vrj/dot_general | solution.py:121
  60.4 2.1 %collective-permute-start.29 = (bf16[2,128,512]{2,1,0:T(8,128)(2,1)S(1)}, bf16[2,128,512]{2,1,0:T(8,128)(2,1)S(1)}, u32[]{:S(2)}, u32[]{:S(2)}) collective-permute-start(bf16[2,128,512]{2,1,0:T(8,128)(2,1)S(1)} %collective-permute-done.20), channel_id=1, source_target_pairs={{0,16},{16,24},{24,8},{8,0},{1,17},{17,25},{25,9},{9,1},{2,18},{18... | collective-permute-start | bytes 786440 | tf_op jit(solution)/shard_map/act_gather/ppermute | solution.py:37
  63.5 2.1 %collective-permute-start.27 = (bf16[1,128,512]{2,1,0:T(8,128)(2,1)S(1)}, bf16[1,128,512]{2,1,0:T(8,128)(2,1)S(1)}, u32[]{:S(2)}, u32[]{:S(2)}) collective-permute-start(bf16[1,128,512]{2,1,0:T(8,128)(2,1)S(1)} %slice.160), channel_id=1, source_target_pairs={{0,4},{1,5},{2,6},{3,7},{4,0},{5,1},{6,2},{7,3},{8,12},{9,13},{10,... | collective-permute-start | bytes 393224 | tf_op jit(solution)/shard_map/act_gather/ppermute | solution.py:19
  65.8 3.2 %collective-permute-done.29 = bf16[2,128,512]{2,1,0:T(8,128)(2,1)S(1)} collective-permute-done((bf16[2,128,512]{2,1,0:T(8,128)(2,1)S(1)}, bf16[2,128,512]{2,1,0:T(8,128)(2,1)S(1)}, u32[]{:S(2)}, u32[]{:S(2)}) %collective-permute-start.29) | collective-permute-done | bytes 262176 | tf_op jit(solution)/shard_map/act_gather/ppermute | solution.py:37
  70.5 1.4 collective-permute-start.33
  71.9 2.4 %convolution_convert_fusion.2 = bf16[2,128,1024]{2,1,0:T(8,128)(2,1)S(1)} fusion(bf16[2,128,4096]{2,1,0:T(8,128)(2,1)S(1)} %constant_dynamic-update-slice_fusion.9, bf16[4096,1024,1]{1,0,2:T(8,128)(2,1)S(1)} %bitcast.76), kind=kOutput, calls=%fused_computation.36 | convolution fusion | flops 2147745792 | bytes 11010048 | tf_op jit(solution)/shard_map/z/vrk,kj->vrj/dot_general | solution.py:121
  74.4 3.8 %collective-permute-done.33 = bf16[2,128,512]{2,1,0:T(8,128)(2,1)S(1)} collective-permute-done((bf16[2,128,512]{2,1,0:T(8,128)(2,1)S(1)}, bf16[2,128,512]{2,1,0:T(8,128)(2,1)S(1)}, u32[]{:S(2)}, u32[]{:S(2)}) %collective-permute-start.33) | collective-permute-done | bytes 262176 | tf_op jit(solution)/shard_map/act_gather/ppermute | solution.py:19
  78.2 1.6 collective-permute-start.35
  81.7 2.4 %convolution_convert_fusion.1 = bf16[2,128,1024]{2,1,0:T(8,128)(2,1)S(1)} fusion(bf16[2,128,4096]{2,1,0:T(8,128)(2,1)S(1)} %constant_dynamic-update-slice_fusion.18, bf16[4096,1024,1]{1,0,2:T(8,128)(2,1)S(1)} %bitcast.77), kind=kOutput, calls=%fused_computation.35 | convolution fusion | flops 2147745792 | bytes 11010048 | tf_op jit(solution)/shard_map/z/vrk,kj->vrj/dot_general | solution.py:121
  87.2 2.4 %convolution_convert_fusion = bf16[2,128,1024]{2,1,0:T(8,128)(2,1)S(1)} fusion(bf16[2,128,4096]{2,1,0:T(8,128)(2,1)S(1)} %constant_dynamic-update-slice_fusion.27, bf16[4096,1024,1]{1,0,2:T(8,128)(2,1)S(1)} %bitcast.78), kind=kOutput, calls=%fused_computation.34 | convolution fusion | flops 2147745792 | bytes 11010048 | tf_op jit(solution)/shard_map/z/vrk,kj->vrj/dot_general | solution.py:121
  89.9 1.8 fusion.6
  94.7 2.5 %fusion.106 = (f32[1,512,1024]{2,1,0:T(8,128)S(1)}, f32[1,512,1024]{2,1,0:T(8,128)}, f32[]{:T(128)}) fusion(f32[2,512,1024]{2,1,0:T(8,128)S(1)} %fusion.103), kind=kLoop, calls=%fused_computation.218 | loop fusion | flops 2621439 | bytes 8388612 | tf_op jit(solution)/shard_map/dz/neg | solution.py:152
  98.7 1.7 collective-permute-start.42
  105.5 2.2 %collective-permute-done.40 = f32[2,64,512]{2,1,0:T(8,128)} collective-permute-done((f32[2,64,512]{2,1,0:T(8,128)}, f32[2,64,512]{2,1,0:T(8,128)}, u32[]{:S(2)}, u32[]{:S(2)}) %collective-permute-start.40) | collective-permute-done | bytes 262176 | tf_op jit(solution)/shard_map/kernel/ppermute | solution.py:19
  107.6 4.3 %collective-permute-done.42 = f32[2,64,512]{2,1,0:T(8,128)} collective-permute-done((f32[2,64,512]{2,1,0:T(8,128)}, f32[2,64,512]{2,1,0:T(8,128)}, u32[]{:S(2)}, u32[]{:S(2)}) %collective-permute-start.42) | collective-permute-done | bytes 262176 | tf_op jit(solution)/shard_map/kernel/ppermute | solution.py:19
  113.9 2.0 %constant_dynamic-update-slice_fusion.45 = (bf16[2,512,512]{2,1,0:T(8,128)(2,1)}, bf16[2,64,512]{2,1,0:T(8,128)(2,1)S(1)}, f32[2,64,512]{2,1,0:T(8,128)S(1)}) fusion(bf16[2,512,512]{2,1,0:T(8,128)(2,1)} %broadcast_in_dim.7, s32[]{:T(128)S(6)} %select_n.295, f32[2,64,512]{2,1,0:T(8,128)} %collective-permute-done.44, ...), kind=kLoop, calls=%fused_computation.184 | loop fusion | flops 327680 | bytes 1835012 | tf_op jit(solution)/shard_map/kernel/dynamic_update_slice | solution.py:142
  117.9 1.5 collective-permute-done.45
  120.0 1.4 collective-permute-start.46
  127.1 2.1 %collective-permute-done.47 = f32[8,128]{1,0:T(8,128)S(1)} collective-permute-done((f32[8,128]{1,0:T(8,128)S(1)}, f32[8,128]{1,0:T(8,128)S(1)}, u32[]{:S(2)}, u32[]{:S(2)}) %collective-permute-start.47) | collective-permute-done | bytes 4128 | tf_op jit(solution)/shard_map/loss/ppermute | solution.py:19
  129.2 2.6 %collective-permute-start.48 = (f32[8,128]{1,0:T(8,128)S(1)}, f32[8,128]{1,0:T(8,128)S(1)}, u32[]{:S(2)}, u32[]{:S(2)}) collective-permute-start(f32[8,128]{1,0:T(8,128)S(1)} %add.304), channel_id=1, source_target_pairs={{0,8},{8,0},{16,24},{24,16},{1,9},{9,1},{17,25},{25,17},{2,10},{10... | collective-permute-start | bytes 12296 | tf_op jit(solution)/shard_map/loss/ppermute | solution.py:19
  133.4 2.6 %collective-permute-start.49 = (f32[8,128]{1,0:T(8,128)S(1)}, f32[8,128]{1,0:T(8,128)S(1)}, u32[]{:S(2)}, u32[]{:S(2)}) collective-permute-start(f32[8,128]{1,0:T(8,128)S(1)} %add.305), channel_id=1, source_target_pairs={{0,16},{8,24},{16,0},{24,8},{1,17},{9,25},{17,1},{25,9},{2,18},{10... | collective-permute-start | bytes 12296 | tf_op jit(solution)/shard_map/loss/ppermute | solution.py:19
  136.4 1.5 collective-permute-start.56
  144.2 3.3 %fusion.108 = (f32[2,1024]{1,0:T(2,128)S(1)}, f32[2,512,1024]{2,1,0:T(8,128)S(1)}) fusion(f32[2,1024]{1,0:T(2,128)S(1)} %copy-done.14, f32[2,1024]{1,0:T(2,128)S(1)} %copy-done.19, f32[2,1024]{1,0:T(2,128)S(1)} %copy-done.12, f32[2,1024]{1,0:T(2,128)S(1)} %broadcast_multiply_fusion.2, bf16[2,128,1024]{2,1,0:T(8,128)(2,1)S(1)} %copy-done.5, ...), kind=kOutput, calls=%fused_computation.219 | convolution fusion | flops 1103099904 | bytes 7380992 | tf_op jit(solution)/shard_map/dz/vrm,vmj->vrj/dot_general | solution.py:148
  152.4 1.8 collective-permute-start.60
  155.6 1.5 collective-permute-start.64
  159.8 1.7 collective-permute-done.60
  161.6 7.1 %collective-permute-done.62 = bf16[2,128,512]{2,1,0:T(8,128)(2,1)S(1)} collective-permute-done((bf16[2,128,512]{2,1,0:T(8,128)(2,1)S(1)}, bf16[2,128,512]{2,1,0:T(8,128)(2,1)S(1)}, u32[]{:S(2)}, u32[]{:S(2)}) %collective-permute-start.62) | collective-permute-done | bytes 262176 | tf_op jit(solution)/shard_map/d_act/ppermute | solution.py:19
  169.4 1.8 collective-permute-start.65
  171.8 7.8 %convolution_bitcast_fusion = f32[1024,1024]{1,0:T(8,128)} fusion(bf16[2,512,1024]{2,1,0:T(8,128)(2,1)S(1)} %fusion.4, bf16[2,128,512]{2,1,0:T(8,128)(2,1)S(1)} %get-tuple-element.31, bf16[2,128,512]{2,1,0:T(8,128)(2,1)S(1)} %get-tuple-element.30, bf16[2,128,512]{2,1,0:T(8,128)(2,1)S(1)} %get-tuple-element.29, ...), kind=kOutput, calls=%fused_computation.13 | convolution fusion | flops 2164260864 | bytes 8388608 | tf_op jit(solution)/shard_map/grad_weight/vnk,vnj->kj/dot_general | solution.py:195
  (258 shorter events, 53.2 us)
Async XLA Ops:
  2.7 19.9 %collective-permute-start = (f32[4,512]{1,0:T(4,128)S(1)}, f32[4,512]{1,0:T(4,128)S(1)}, u32[]{:S(2)}, u32[]{:S(2)}) collective-permute-start(f32[4,512]{1,0:T(4,128)S(1)} %pad_maximum_fusion.5), channel_id=1, source_target_pairs={{0,24},{8,0},{16,8},{24,16},{1,25},{9,1},{17,9},{25,17},{2,26},{10... | collective-permute-start | bytes 24584 | tf_op jit(solution)/shard_map/norm_stats/ppermute | solution.py:45
  7.8 14.8 %collective-permute-start.1 = (f32[4,512]{1,0:T(4,128)S(1)}, f32[4,512]{1,0:T(4,128)S(1)}, u32[]{:S(2)}, u32[]{:S(2)}) collective-permute-start(f32[4,512]{1,0:T(4,128)S(1)} %pad_maximum_fusion.5), channel_id=1, source_target_pairs={{0,16},{8,24},{16,0},{24,8},{1,17},{9,25},{17,1},{25,9},{2,18},{10... | collective-permute-start | bytes 24584 | tf_op jit(solution)/shard_map/norm_stats/ppermute | solution.py:45
  7.8 14.8 %collective-permute-start.2 = (f32[4,512]{1,0:T(4,128)S(1)}, f32[4,512]{1,0:T(4,128)S(1)}, u32[]{:S(2)}, u32[]{:S(2)}) collective-permute-start(f32[4,512]{1,0:T(4,128)S(1)} %pad_maximum_fusion.5), channel_id=1, source_target_pairs={{0,8},{8,16},{16,24},{24,0},{1,9},{9,17},{17,25},{25,1},{2,10},{10... | collective-permute-start | bytes 24584 | tf_op jit(solution)/shard_map/norm_stats/ppermute | solution.py:45
  23.0 14.1 %collective-permute-start.11 = (bf16[2,128,512]{2,1,0:T(8,128)(2,1)S(1)}, bf16[2,128,512]{2,1,0:T(8,128)(2,1)S(1)}, u32[]{:S(2)}, u32[]{:S(2)}) collective-permute-start(bf16[2,128,512]{2,1,0:T(8,128)(2,1)S(1)} %get-tuple-element.20), channel_id=1, source_target_pairs={{0,16},{16,24},{24,8},{8,0},{1,17},{17,25},{25,9},{9,1},{2,18},{18... | collective-permute-start | bytes 786440 | tf_op jit(solution)/shard_map/act_gather/ppermute | solution.py:37
  25.0 13.7 %collective-permute-start.3 = (bf16[2,128,512]{2,1,0:T(8,128)(2,1)S(1)}, bf16[2,128,512]{2,1,0:T(8,128)(2,1)}, u32[]{:S(2)}, u32[]{:S(2)}) collective-permute-start(bf16[2,128,512]{2,1,0:T(8,128)(2,1)S(1)} %get-tuple-element.20), channel_id=1, source_target_pairs={{0,1},{1,0},{2,3},{3,2},{4,5},{5,4},{6,7},{7,6},{8,9},{9,8},{10,11... | collective-permute-start | bytes 786440 | tf_op jit(solution)/shard_map/act_gather/ppermute | solution.py:19
  25.0 10.5 %collective-permute-start.4 = (bf16[2,128,512]{2,1,0:T(8,128)(2,1)S(1)}, bf16[2,128,512]{2,1,0:T(8,128)(2,1)S(1)}, u32[]{:S(2)}, u32[]{:S(2)}) collective-permute-start(bf16[2,128,512]{2,1,0:T(8,128)(2,1)S(1)} %get-tuple-element.20), channel_id=1, source_target_pairs={{0,2},{1,3},{2,0},{3,1},{4,6},{5,7},{6,4},{7,5},{8,10},{9,11},{10,... | collective-permute-start | bytes 786440 | tf_op jit(solution)/shard_map/act_gather/ppermute | solution.py:19
  26.5 8.4 %collective-permute-start.6 = (bf16[2,128,512]{2,1,0:T(8,128)(2,1)S(1)}, bf16[2,128,512]{2,1,0:T(8,128)(2,1)S(1)}, u32[]{:S(2)}, u32[]{:S(2)}) collective-permute-start(bf16[2,128,512]{2,1,0:T(8,128)(2,1)S(1)} %get-tuple-element.20), channel_id=1, source_target_pairs={{0,4},{1,5},{2,6},{3,7},{4,0},{5,1},{6,2},{7,3},{8,12},{9,13},{10,... | collective-permute-start | bytes 786440 | tf_op jit(solution)/shard_map/act_gather/ppermute | solution.py:19
  34.9 5.0 %collective-permute-start.8 = (bf16[1,128,512]{2,1,0:T(8,128)(2,1)S(1)}, bf16[1,128,512]{2,1,0:T(8,128)(2,1)S(1)}, u32[]{:S(2)}, u32[]{:S(2)}) collective-permute-start(bf16[1,128,512]{2,1,0:T(8,128)(2,1)S(1)} %slice.155), channel_id=1, source_target_pairs={{0,2},{1,3},{2,0},{3,1},{4,6},{5,7},{6,4},{7,5},{8,10},{9,11},{10,... | collective-permute-start | bytes 393224 | tf_op jit(solution)/shard_map/act_gather/ppermute | solution.py:19
  35.5 6.7 %collective-permute-start.9 = (bf16[1,128,512]{2,1,0:T(8,128)(2,1)S(1)}, bf16[1,128,512]{2,1,0:T(8,128)(2,1)S(1)}, u32[]{:S(2)}, u32[]{:S(2)}) collective-permute-start(bf16[1,128,512]{2,1,0:T(8,128)(2,1)S(1)} %slice.156), channel_id=1, source_target_pairs={{0,4},{1,5},{2,6},{3,7},{4,0},{5,1},{6,2},{7,3},{8,12},{9,13},{10,... | collective-permute-start | bytes 393224 | tf_op jit(solution)/shard_map/act_gather/ppermute | solution.py:19
  37.1 14.0 %collective-permute-start.12 = (bf16[2,128,512]{2,1,0:T(8,128)(2,1)S(1)}, bf16[2,128,512]{2,1,0:T(8,128)(2,1)S(1)}, u32[]{:S(2)}, u32[]{:S(2)}) collective-permute-start(bf16[2,128,512]{2,1,0:T(8,128)(2,1)S(1)} %collective-permute-done.11), channel_id=1, source_target_pairs={{0,1},{1,0},{2,3},{3,2},{4,5},{5,4},{6,7},{7,6},{8,9},{9,8},{10,11... | collective-permute-start | bytes 786440 | tf_op jit(solution)/shard_map/act_gather/ppermute | solution.py:19
  37.1 11.4 %collective-permute-start.13 = (bf16[2,128,512]{2,1,0:T(8,128)(2,1)S(1)}, bf16[2,128,512]{2,1,0:T(8,128)(2,1)S(1)}, u32[]{:S(2)}, u32[]{:S(2)}) collective-permute-start(bf16[2,128,512]{2,1,0:T(8,128)(2,1)S(1)} %collective-permute-done.11), channel_id=1, source_target_pairs={{0,2},{1,3},{2,0},{3,1},{4,6},{5,7},{6,4},{7,5},{8,10},{9,11},{10,... | collective-permute-start | bytes 786440 | tf_op jit(solution)/shard_map/act_gather/ppermute | solution.py:19
  40.0 8.6 %collective-permute-start.15 = (bf16[2,128,512]{2,1,0:T(8,128)(2,1)S(1)}, bf16[2,128,512]{2,1,0:T(8,128)(2,1)S(1)}, u32[]{:S(2)}, u32[]{:S(2)}) collective-permute-start(bf16[2,128,512]{2,1,0:T(8,128)(2,1)S(1)} %collective-permute-done.11), channel_id=1, source_target_pairs={{0,4},{1,5},{2,6},{3,7},{4,0},{5,1},{6,2},{7,3},{8,12},{9,13},{10,... | collective-permute-start | bytes 786440 | tf_op jit(solution)/shard_map/act_gather/ppermute | solution.py:19
  42.3 6.9 %collective-permute-start.7 = (bf16[2,128,512]{2,1,0:T(8,128)(2,1)S(1)}, bf16[2,128,512]{2,1,0:T(8,128)(2,1)S(1)}, u32[]{:S(2)}, u32[]{:S(2)}) collective-permute-start(bf16[2,128,512]{2,1,0:T(8,128)(2,1)S(1)} %collective-permute-done.6), channel_id=1, source_target_pairs={{0,1},{1,0},{2,3},{3,2},{4,5},{5,4},{6,7},{7,6},{8,9},{9,8},{10,11... | collective-permute-start | bytes 786440 | tf_op jit(solution)/shard_map/act_gather/ppermute | solution.py:19
  42.3 8.8 %collective-permute-start.20 = (bf16[2,128,512]{2,1,0:T(8,128)(2,1)S(1)}, bf16[2,128,512]{2,1,0:T(8,128)(2,1)S(1)}, u32[]{:S(2)}, u32[]{:S(2)}) collective-permute-start(bf16[2,128,512]{2,1,0:T(8,128)(2,1)S(1)} %collective-permute-done.11), channel_id=1, source_target_pairs={{0,16},{16,24},{24,8},{8,0},{1,17},{17,25},{25,9},{9,1},{2,18},{18... | collective-permute-start | bytes 786440 | tf_op jit(solution)/shard_map/act_gather/ppermute | solution.py:37
  48.6 11.2 %collective-permute-start.17 = (bf16[1,128,512]{2,1,0:T(8,128)(2,1)S(1)}, bf16[1,128,512]{2,1,0:T(8,128)(2,1)S(1)}, u32[]{:S(2)}, u32[]{:S(2)}) collective-permute-start(bf16[1,128,512]{2,1,0:T(8,128)(2,1)S(1)} %slice.157), channel_id=1, source_target_pairs={{0,2},{1,3},{2,0},{3,1},{4,6},{5,7},{6,4},{7,5},{8,10},{9,11},{10,... | collective-permute-start | bytes 393224 | tf_op jit(solution)/shard_map/act_gather/ppermute | solution.py:19
  49.2 10.7 %collective-permute-start.18 = (bf16[1,128,512]{2,1,0:T(8,128)(2,1)S(1)}, bf16[1,128,512]{2,1,0:T(8,128)(2,1)S(1)}, u32[]{:S(2)}, u32[]{:S(2)}) collective-permute-start(bf16[1,128,512]{2,1,0:T(8,128)(2,1)S(1)} %slice.158), channel_id=1, source_target_pairs={{0,4},{1,5},{2,6},{3,7},{4,0},{5,1},{6,2},{7,3},{8,12},{9,13},{10,... | collective-permute-start | bytes 393224 | tf_op jit(solution)/shard_map/act_gather/ppermute | solution.py:19
  51.1 9.3 %collective-permute-start.14 = (bf16[2,128,512]{2,1,0:T(8,128)(2,1)S(1)}, bf16[2,128,512]{2,1,0:T(8,128)(2,1)S(1)}, u32[]{:S(2)}, u32[]{:S(2)}) collective-permute-start(bf16[2,128,512]{2,1,0:T(8,128)(2,1)S(1)} %collective-permute-done.13), channel_id=1, source_target_pairs={{0,1},{1,0},{2,3},{3,2},{4,5},{5,4},{6,7},{7,6},{8,9},{9,8},{10,11... | collective-permute-start | bytes 786440 | tf_op jit(solution)/shard_map/act_gather/ppermute | solution.py:19
  51.1 11.5 %collective-permute-start.22 = (bf16[2,128,512]{2,1,0:T(8,128)(2,1)S(1)}, bf16[2,128,512]{2,1,0:T(8,128)(2,1)S(1)}, u32[]{:S(2)}, u32[]{:S(2)}) collective-permute-start(bf16[2,128,512]{2,1,0:T(8,128)(2,1)S(1)} %collective-permute-done.20), channel_id=1, source_target_pairs={{0,2},{1,3},{2,0},{3,1},{4,6},{5,7},{6,4},{7,5},{8,10},{9,11},{10,... | collective-permute-start | bytes 786440 | tf_op jit(solution)/shard_map/act_gather/ppermute | solution.py:19
  51.6 10.9 %collective-permute-start.24 = (bf16[2,128,512]{2,1,0:T(8,128)(2,1)S(1)}, bf16[2,128,512]{2,1,0:T(8,128)(2,1)S(1)}, u32[]{:S(2)}, u32[]{:S(2)}) collective-permute-start(bf16[2,128,512]{2,1,0:T(8,128)(2,1)S(1)} %collective-permute-done.20), channel_id=1, source_target_pairs={{0,4},{1,5},{2,6},{3,7},{4,0},{5,1},{6,2},{7,3},{8,12},{9,13},{10,... | collective-permute-start | bytes 786440 | tf_op jit(solution)/shard_map/act_gather/ppermute | solution.py:19
  59.9 5.7 %collective-permute-start.21 = (bf16[2,128,512]{2,1,0:T(8,128)(2,1)S(1)}, bf16[2,128,512]{2,1,0:T(8,128)(2,1)S(1)}, u32[]{:S(2)}, u32[]{:S(2)}) collective-permute-start(bf16[2,128,512]{2,1,0:T(8,128)(2,1)S(1)} %collective-permute-done.20), channel_id=1, source_target_pairs={{0,1},{1,0},{2,3},{3,2},{4,5},{5,4},{6,7},{7,6},{8,9},{9,8},{10,11... | collective-permute-start | bytes 786440 | tf_op jit(solution)/shard_map/act_gather/ppermute | solution.py:19
  60.4 8.5 %collective-permute-start.29 = (bf16[2,128,512]{2,1,0:T(8,128)(2,1)S(1)}, bf16[2,128,512]{2,1,0:T(8,128)(2,1)S(1)}, u32[]{:S(2)}, u32[]{:S(2)}) collective-permute-start(bf16[2,128,512]{2,1,0:T(8,128)(2,1)S(1)} %collective-permute-done.20), channel_id=1, source_target_pairs={{0,16},{16,24},{24,8},{8,0},{1,17},{17,25},{25,9},{9,1},{2,18},{18... | collective-permute-start | bytes 786440 | tf_op jit(solution)/shard_map/act_gather/ppermute | solution.py:37
  62.5 8.0 %collective-permute-start.19 = (bf16[2,128,512]{2,1,0:T(8,128)(2,1)S(1)}, bf16[2,128,512]{2,1,0:T(8,128)(2,1)S(1)}, u32[]{:S(2)}, u32[]{:S(2)}) collective-permute-start(bf16[2,128,512]{2,1,0:T(8,128)(2,1)S(1)} %pad_maximum_fusion.2), channel_id=1, source_target_pairs={{0,1},{1,0},{2,3},{3,2},{4,5},{5,4},{6,7},{7,6},{8,9},{9,8},{10,11... | collective-permute-start | bytes 786440 | tf_op jit(solution)/shard_map/act_gather/ppermute | solution.py:19
  62.6 6.3 %collective-permute-start.26 = (bf16[1,128,512]{2,1,0:T(8,128)(2,1)S(1)}, bf16[1,128,512]{2,1,0:T(8,128)(2,1)S(1)}, u32[]{:S(2)}, u32[]{:S(2)}) collective-permute-start(bf16[1,128,512]{2,1,0:T(8,128)(2,1)S(1)} %slice.159), channel_id=1, source_target_pairs={{0,2},{1,3},{2,0},{3,1},{4,6},{5,7},{6,4},{7,5},{8,10},{9,11},{10,... | collective-permute-start | bytes 393224 | tf_op jit(solution)/shard_map/act_gather/ppermute | solution.py:19
  63.5 6.1 %collective-permute-start.27 = (bf16[1,128,512]{2,1,0:T(8,128)(2,1)S(1)}, bf16[1,128,512]{2,1,0:T(8,128)(2,1)S(1)}, u32[]{:S(2)}, u32[]{:S(2)}) collective-permute-start(bf16[1,128,512]{2,1,0:T(8,128)(2,1)S(1)} %slice.160), channel_id=1, source_target_pairs={{0,4},{1,5},{2,6},{3,7},{4,0},{5,1},{6,2},{7,3},{8,12},{9,13},{10,... | collective-permute-start | bytes 393224 | tf_op jit(solution)/shard_map/act_gather/ppermute | solution.py:19
  65.6 14.2 %collective-permute-start.23 = (bf16[2,128,512]{2,1,0:T(8,128)(2,1)S(1)}, bf16[2,128,512]{2,1,0:T(8,128)(2,1)S(1)}, u32[]{:S(2)}, u32[]{:S(2)}) collective-permute-start(bf16[2,128,512]{2,1,0:T(8,128)(2,1)S(1)} %collective-permute-done.22), channel_id=1, source_target_pairs={{0,1},{1,0},{2,3},{3,2},{4,5},{5,4},{6,7},{7,6},{8,9},{9,8},{10,11... | collective-permute-start | bytes 786440 | tf_op jit(solution)/shard_map/act_gather/ppermute | solution.py:19
  68.9 11.9 %collective-permute-start.25 = (bf16[2,128,512]{2,1,0:T(8,128)(2,1)S(1)}, bf16[2,128,512]{2,1,0:T(8,128)(2,1)S(1)}, u32[]{:S(2)}, u32[]{:S(2)}) collective-permute-start(bf16[2,128,512]{2,1,0:T(8,128)(2,1)S(1)} %collective-permute-done.24), channel_id=1, source_target_pairs={{0,1},{1,0},{2,3},{3,2},{4,5},{5,4},{6,7},{7,6},{8,9},{9,8},{10,11... | collective-permute-start | bytes 786440 | tf_op jit(solution)/shard_map/act_gather/ppermute | solution.py:19
  69.0 12.0 %collective-permute-start.30 = (bf16[2,128,512]{2,1,0:T(8,128)(2,1)S(1)}, bf16[2,128,512]{2,1,0:T(8,128)(2,1)S(1)}, u32[]{:S(2)}, u32[]{:S(2)}) collective-permute-start(bf16[2,128,512]{2,1,0:T(8,128)(2,1)S(1)} %collective-permute-done.29), channel_id=1, source_target_pairs={{0,1},{1,0},{2,3},{3,2},{4,5},{5,4},{6,7},{7,6},{8,9},{9,8},{10,11... | collective-permute-start | bytes 786440 | tf_op jit(solution)/shard_map/act_gather/ppermute | solution.py:19
  69.5 8.7 %collective-permute-start.31 = (bf16[2,128,512]{2,1,0:T(8,128)(2,1)S(1)}, bf16[2,128,512]{2,1,0:T(8,128)(2,1)S(1)}, u32[]{:S(2)}, u32[]{:S(2)}) collective-permute-start(bf16[2,128,512]{2,1,0:T(8,128)(2,1)S(1)} %collective-permute-done.29), channel_id=1, source_target_pairs={{0,2},{1,3},{2,0},{3,1},{4,6},{5,7},{6,4},{7,5},{8,10},{9,11},{10,... | collective-permute-start | bytes 786440 | tf_op jit(solution)/shard_map/act_gather/ppermute | solution.py:19
  70.5 7.7 %collective-permute-start.33 = (bf16[2,128,512]{2,1,0:T(8,128)(2,1)S(1)}, bf16[2,128,512]{2,1,0:T(8,128)(2,1)S(1)}, u32[]{:S(2)}, u32[]{:S(2)}) collective-permute-start(bf16[2,128,512]{2,1,0:T(8,128)(2,1)S(1)} %collective-permute-done.29), channel_id=1, source_target_pairs={{0,4},{1,5},{2,6},{3,7},{4,0},{5,1},{6,2},{7,3},{8,12},{9,13},{10,... | collective-permute-start | bytes 786440 | tf_op jit(solution)/shard_map/act_gather/ppermute | solution.py:19
  78.2 6.0 %collective-permute-start.35 = (bf16[1,128,512]{2,1,0:T(8,128)(2,1)S(1)}, bf16[1,128,512]{2,1,0:T(8,128)(2,1)S(1)}, u32[]{:S(2)}, u32[]{:S(2)}) collective-permute-start(bf16[1,128,512]{2,1,0:T(8,128)(2,1)S(1)} %slice.161), channel_id=1, source_target_pairs={{0,2},{1,3},{2,0},{3,1},{4,6},{5,7},{6,4},{7,5},{8,10},{9,11},{10,... | collective-permute-start | bytes 393224 | tf_op jit(solution)/shard_map/act_gather/ppermute | solution.py:19
  79.8 5.7 %collective-permute-start.36 = (bf16[1,128,512]{2,1,0:T(8,128)(2,1)S(1)}, bf16[1,128,512]{2,1,0:T(8,128)(2,1)S(1)}, u32[]{:S(2)}, u32[]{:S(2)}) collective-permute-start(bf16[1,128,512]{2,1,0:T(8,128)(2,1)S(1)} %slice.162), channel_id=1, source_target_pairs={{0,4},{1,5},{2,6},{3,7},{4,0},{5,1},{6,2},{7,3},{8,12},{9,13},{10,... | collective-permute-start | bytes 393224 | tf_op jit(solution)/shard_map/act_gather/ppermute | solution.py:19
  80.9 4.7 %collective-permute-start.32 = (bf16[2,128,512]{2,1,0:T(8,128)(2,1)S(1)}, bf16[2,128,512]{2,1,0:T(8,128)(2,1)S(1)}, u32[]{:S(2)}, u32[]{:S(2)}) collective-permute-start(bf16[2,128,512]{2,1,0:T(8,128)(2,1)S(1)} %collective-permute-done.31), channel_id=1, source_target_pairs={{0,1},{1,0},{2,3},{3,2},{4,5},{5,4},{6,7},{7,6},{8,9},{9,8},{10,11... | collective-permute-start | bytes 786440 | tf_op jit(solution)/shard_map/act_gather/ppermute | solution.py:19
  94.3 11.1 %collective-permute-start.38 = (f32[2,64,512]{2,1,0:T(8,128)}, f32[2,64,512]{2,1,0:T(8,128)}, u32[]{:S(2)}, u32[]{:S(2)}) collective-permute-start(f32[2,64,512]{2,1,0:T(8,128)} %get-tuple-element.32), channel_id=1, source_target_pairs={{0,1},{1,0},{2,3},{3,2},{4,5},{5,4},{6,7},{7,6},{8,9},{9,8},{10,11... | collective-permute-start | bytes 786440 | tf_op jit(solution)/shard_map/kernel/ppermute | solution.py:19
  98.2 9.5 %collective-permute-start.40 = (f32[2,64,512]{2,1,0:T(8,128)}, f32[2,64,512]{2,1,0:T(8,128)}, u32[]{:S(2)}, u32[]{:S(2)}) collective-permute-start(f32[2,64,512]{2,1,0:T(8,128)} %get-tuple-element.36), channel_id=1, source_target_pairs={{0,2},{1,3},{2,0},{3,1},{4,6},{5,7},{6,4},{7,5},{8,10},{9,11},{10,... | collective-permute-start | bytes 786440 | tf_op jit(solution)/shard_map/kernel/ppermute | solution.py:19
  98.7 13.3 %collective-permute-start.42 = (f32[2,64,512]{2,1,0:T(8,128)}, f32[2,64,512]{2,1,0:T(8,128)}, u32[]{:S(2)}, u32[]{:S(2)}) collective-permute-start(f32[2,64,512]{2,1,0:T(8,128)} %get-tuple-element.38), channel_id=1, source_target_pairs={{0,4},{1,5},{2,6},{3,7},{4,0},{5,1},{6,2},{7,3},{8,12},{9,13},{10,... | collective-permute-start | bytes 786440 | tf_op jit(solution)/shard_map/kernel/ppermute | solution.py:19
  100.4 12.4 %collective-permute-start.44 = (f32[2,64,512]{2,1,0:T(8,128)}, f32[2,64,512]{2,1,0:T(8,128)}, u32[]{:S(2)}, u32[]{:S(2)}) collective-permute-start(f32[2,64,512]{2,1,0:T(8,128)} %get-tuple-element.37), channel_id=1, source_target_pairs={{0,6},{1,7},{2,4},{3,5},{4,2},{5,3},{6,0},{7,1},{8,14},{9,15},{10,... | collective-permute-start | bytes 786440 | tf_op jit(solution)/shard_map/kernel/ppermute | solution.py:19
  120.0 4.8 %collective-permute-start.46 = (f32[8,128]{1,0:T(8,128)S(1)}, f32[8,128]{1,0:T(8,128)S(1)}, u32[]{:S(2)}, u32[]{:S(2)}) collective-permute-start(f32[8,128]{1,0:T(8,128)S(1)} %broadcast_add_fusion), channel_id=1, source_target_pairs={{0,2},{1,3},{2,0},{3,1},{4,6},{5,7},{6,4},{7,5},{8,10},{9,11},{10,... | collective-permute-start | bytes 12296 | tf_op jit(solution)/shard_map/loss/ppermute | solution.py:19
  122.5 13.6 %collective-permute-start.53 = (bf16[2,64,512]{2,1,0:T(8,128)(2,1)S(1)}, bf16[2,64,512]{2,1,0:T(8,128)(2,1)S(1)}, u32[]{:S(2)}, u32[]{:S(2)}) collective-permute-start(bf16[2,64,512]{2,1,0:T(8,128)(2,1)S(1)} %get-tuple-element.15), channel_id=1, source_target_pairs={{0,4},{1,5},{2,6},{3,7},{4,0},{5,1},{6,2},{7,3},{8,12},{9,13},{10,... | collective-permute-start | bytes 393224 | tf_op jit(solution)/shard_map/kernel/ppermute | solution.py:19
  123.5 12.9 %collective-permute-start.51 = (bf16[2,64,512]{2,1,0:T(8,128)(2,1)S(1)}, bf16[2,64,512]{2,1,0:T(8,128)(2,1)S(1)}, u32[]{:S(2)}, u32[]{:S(2)}) collective-permute-start(bf16[2,64,512]{2,1,0:T(8,128)(2,1)S(1)} %get-tuple-element.15), channel_id=1, source_target_pairs={{0,2},{1,3},{2,0},{3,1},{4,6},{5,7},{6,4},{7,5},{8,10},{9,11},{10,... | collective-permute-start | bytes 393224 | tf_op jit(solution)/shard_map/kernel/ppermute | solution.py:19
  124.8 13.1 %collective-permute-start.50 = (bf16[2,64,512]{2,1,0:T(8,128)(2,1)S(1)}, bf16[2,64,512]{2,1,0:T(8,128)(2,1)S(1)}, u32[]{:S(2)}, u32[]{:S(2)}) collective-permute-start(bf16[2,64,512]{2,1,0:T(8,128)(2,1)S(1)} %get-tuple-element.15), channel_id=1, source_target_pairs={{0,1},{1,0},{2,3},{3,2},{4,5},{5,4},{6,7},{7,6},{8,9},{9,8},{10,11... | collective-permute-start | bytes 393224 | tf_op jit(solution)/shard_map/kernel/ppermute | solution.py:19
  133.4 24.7 %collective-permute-start.49 = (f32[8,128]{1,0:T(8,128)S(1)}, f32[8,128]{1,0:T(8,128)S(1)}, u32[]{:S(2)}, u32[]{:S(2)}) collective-permute-start(f32[8,128]{1,0:T(8,128)S(1)} %add.305), channel_id=1, source_target_pairs={{0,16},{8,24},{16,0},{24,8},{1,17},{9,25},{17,1},{25,9},{2,18},{10... | collective-permute-start | bytes 12296 | tf_op jit(solution)/shard_map/loss/ppermute | solution.py:19
  151.8 8.0 %collective-permute-start.58 = (bf16[2,128,512]{2,1,0:T(8,128)(2,1)S(1)}, bf16[2,128,512]{2,1,0:T(8,128)(2,1)S(1)}, u32[]{:S(2)}, u32[]{:S(2)}) collective-permute-start(bf16[2,128,512]{2,1,0:T(8,128)(2,1)S(1)} %convolution_convert_fusion.7), channel_id=1, source_target_pairs={{0,1},{1,0},{2,3},{3,2},{4,5},{5,4},{6,7},{7,6},{8,9},{9,8},{10,11... | collective-permute-start | bytes 786440 | tf_op jit(solution)/shard_map/d_act/ppermute | solution.py:19
  152.4 9.2 %collective-permute-start.60 = (bf16[2,128,512]{2,1,0:T(8,128)(2,1)S(1)}, bf16[2,128,512]{2,1,0:T(8,128)(2,1)S(1)}, u32[]{:S(2)}, u32[]{:S(2)}) collective-permute-start(bf16[2,128,512]{2,1,0:T(8,128)(2,1)S(1)} %add_convert_fusion.2), channel_id=1, source_target_pairs={{0,2},{1,3},{2,0},{3,1},{4,6},{5,7},{6,4},{7,5},{8,10},{9,11},{10,... | collective-permute-start | bytes 786440 | tf_op jit(solution)/shard_map/d_act/ppermute | solution.py:19
  154.7 14.1 %collective-permute-start.62 = (bf16[2,128,512]{2,1,0:T(8,128)(2,1)S(1)}, bf16[2,128,512]{2,1,0:T(8,128)(2,1)S(1)}, u32[]{:S(2)}, u32[]{:S(2)}) collective-permute-start(bf16[2,128,512]{2,1,0:T(8,128)(2,1)S(1)} %add_convert_fusion.1), channel_id=1, source_target_pairs={{0,4},{1,5},{2,6},{3,7},{4,0},{5,1},{6,2},{7,3},{8,12},{9,13},{10,... | collective-permute-start | bytes 786440 | tf_op jit(solution)/shard_map/d_act/ppermute | solution.py:19
  155.6 13.1 %collective-permute-start.64 = (bf16[2,128,512]{2,1,0:T(8,128)(2,1)S(1)}, bf16[2,128,512]{2,1,0:T(8,128)(2,1)S(1)}, u32[]{:S(2)}, u32[]{:S(2)}) collective-permute-start(bf16[2,128,512]{2,1,0:T(8,128)(2,1)S(1)} %add_convert_fusion), channel_id=1, source_target_pairs={{0,6},{1,7},{2,4},{3,5},{4,2},{5,3},{6,0},{7,1},{8,14},{9,15},{10,... | collective-permute-start | bytes 786440 | tf_op jit(solution)/shard_map/d_act/ppermute | solution.py:19
  169.4 10.3 %collective-permute-start.65 = (f32[4,512]{1,0:T(4,128)S(1)}, f32[4,512]{1,0:T(4,128)S(1)}, u32[]{:S(2)}, u32[]{:S(2)}) collective-permute-start(f32[4,512]{1,0:T(4,128)S(1)} %pad_maximum_fusion.6), channel_id=1, source_target_pairs={{0,24},{8,0},{16,8},{24,16},{1,25},{9,1},{17,9},{25,17},{2,26},{10... | collective-permute-start | bytes 24584 | tf_op jit(solution)/shard_map/norm_backward/ppermute | solution.py:45
  171.2 8.4 %collective-permute-start.66 = (f32[4,512]{1,0:T(4,128)S(1)}, f32[4,512]{1,0:T(4,128)S(1)}, u32[]{:S(2)}, u32[]{:S(2)}) collective-permute-start(f32[4,512]{1,0:T(4,128)S(1)} %pad_maximum_fusion.6), channel_id=1, source_target_pairs={{0,16},{8,24},{16,0},{24,8},{1,17},{9,25},{17,1},{25,9},{2,18},{10... | collective-permute-start | bytes 24584 | tf_op jit(solution)/shard_map/norm_backward/ppermute | solution.py:45
  171.2 8.4 %collective-permute-start.67 = (f32[4,512]{1,0:T(4,128)S(1)}, f32[4,512]{1,0:T(4,128)S(1)}, u32[]{:S(2)}, u32[]{:S(2)}) collective-permute-start(f32[4,512]{1,0:T(4,128)S(1)} %pad_maximum_fusion.6), channel_id=1, source_target_pairs={{0,8},{8,16},{16,24},{24,0},{1,9},{9,17},{17,25},{25,1},{2,10},{10... | collective-permute-start | bytes 24584 | tf_op jit(solution)/shard_map/norm_backward/ppermute | solution.py:45
  (44 other events, 309.3 us)

commit v2 on v1

v2 whole, which is shorter than its diff:
```python
import functools

import jax
import jax.numpy as jnp
from jax import lax
from jax.experimental import pallas as pl
from jax.experimental.pallas import tpu as pltpu
from jax.sharding import PartitionSpec as P

eps_norm = 1e-05
eps_std = 0.0001
f32 = jnp.float32
bf16 = jnp.bfloat16
VMEM_LIMIT = 40 * 1024 * 1024


def gelu_slope(preactivation):
    value, pullback = jax.vjp(lambda t: jax.nn.gelu(t, approximate=True), preactivation)
    return pullback(jnp.ones_like(value))[0]


def xor_send(x, axis, k):
    n = lax.axis_size(axis)
    return lax.ppermute(x, axis, [(i, i ^ k) for i in range(n)])


def ring_order(n):
    return list(range(0, n, 2)) + list(range(1, n, 2))[::-1]


def ring_send(x, axis, d):
    order = ring_order(lax.axis_size(axis))
    n = len(order)
    return lax.ppermute(x, axis, [(order[i], order[(i + d) % n]) for i in range(n)])


def exchange(x, axis):
    n = lax.axis_size(axis)
    me = lax.axis_index(axis)
    slots = [x]
    for d in range(1, n):
        slots.append(lax.ppermute(x, axis, [(i, (i + d) % n) for i in range(n)]))
    ordered = []
    for a in range(n):
        value = slots[0]
        for d in range(1, n):
            value = jnp.where((me - a) % n == d, slots[d], value)
        ordered.append(value)
    return ordered


def params():
    return pltpu.CompilerParams(vmem_limit_bytes=VMEM_LIMIT)


def cost(flops, moved):
    return pl.CostEstimate(flops=flops, bytes_accessed=moved, transcendentals=0)


def whole(shape):
    return pl.BlockSpec(shape, lambda i, index: (0,) * len(shape))


def z_kernel(count, first, last, index_ref, *refs):
    pieces, rest = refs[:count], list(refs[count:])
    w_ref = rest.pop(0)
    before = None if first else rest.pop(0)
    i = pl.program_id(0)
    if last:
        z_ref, sum_ref, total = rest
    else:
        (total,) = rest

    for j in range(count):

        @pl.when(i == j)
        def _():
            part = jnp.dot(pieces[j][...], w_ref[0], preferred_element_type=f32)
            if j > 0:
                total[...] += part
            elif first:
                total[...] = part
            else:
                total[...] = before[...] + part

    if last:

        @pl.when(i == count - 1)
        def _():
            z = total[...].astype(bf16)
            z_ref[...] = z
            zf = z.astype(f32)
            half = zf.shape[0] // 2
            sum_ref[0:1, :] = jnp.sum(zf[:half], axis=0, keepdims=True)
            sum_ref[1:2, :] = jnp.sum(zf[half:], axis=0, keepdims=True)


def z_call(index, pieces, blocks, before, last):
    count = len(pieces)
    rows, width = pieces[0].shape
    columns = blocks.shape[2]
    in_specs = [whole((rows, width)) for _ in pieces]
    in_specs.append(pl.BlockSpec((1, width, columns), lambda i, index: (index[i], 0, 0)))
    operands = list(pieces) + [blocks]
    if before is not None:
        in_specs.append(whole((rows, columns)))
        operands.append(before)
    scratch = []
    if last:
        out_shape = (
            jax.ShapeDtypeStruct((rows, columns), bf16),
            jax.ShapeDtypeStruct((2, columns), f32),
        )
        out_specs = (whole((rows, columns)), whole((2, columns)))
        scratch = [pltpu.VMEM((rows, columns), f32)]
    else:
        out_shape = jax.ShapeDtypeStruct((rows, columns), f32)
        out_specs = whole((rows, columns))
    return pl.pallas_call(
        functools.partial(z_kernel, count, before is None, last),
        out_shape=out_shape,
        grid_spec=pltpu.PrefetchScalarGridSpec(
            num_scalar_prefetch=1,
            grid=(count,),
            in_specs=in_specs,
            out_specs=out_specs,
            scratch_shapes=scratch,
        ),
        compiler_params=params(),
        cost_estimate=cost(
            2 * rows * width * columns * count, 2 * count * width * (columns + rows)
        ),
        name="z_matmul",
    )(index, *operands)


def strip_kernel(n_slots, n_sums, rows, n_col, index_ref, *refs):
    z_refs, sum_refs = refs[:n_slots], refs[n_slots : n_slots + n_sums]
    even_ref, odd_ref, strip = refs[n_slots + n_sums :]
    local_rows = z_refs[0].shape[0] // 2
    mean = sum(s[...] for s in sum_refs) / rows
    for v in range(2):
        here = pl.ds(v * local_rows, local_rows)
        rounded = [(z[here, :].astype(f32) - mean[v : v + 1]).astype(bf16) for z in z_refs]
        for u in range(n_slots):
            strip[here, pl.ds(u * local_rows, local_rows)] = lax.dot_general(
                rounded[0], rounded[u], (((1,), (1,)), ((), ())), preferred_element_type=f32
            )
    part = 2 * local_rows // n_col
    for k in range(n_col):
        start = pl.multiple_of(index_ref[k] * part, part)
        (odd_ref if k % 2 else even_ref)[k // 2] = strip[pl.ds(start, part), :]


def strip_call(index, z_slots, sums, rows, n_col):
    tall, columns = z_slots[0].shape
    wide = len(z_slots) * tall // 2
    part = jax.ShapeDtypeStruct((n_col // 2, tall // n_col, wide), f32)
    specs = [whole((tall, columns)) for _ in z_slots] + [whole((2, columns)) for _ in sums]
    return pl.pallas_call(
        functools.partial(strip_kernel, len(z_slots), len(sums), rows, n_col),
        out_shape=(part, part),
        grid_spec=pltpu.PrefetchScalarGridSpec(
            num_scalar_prefetch=1,
            grid=(1,),
            in_specs=specs,
            out_specs=(whole(part.shape), whole(part.shape)),
            scratch_shapes=[pltpu.VMEM((tall, wide), f32)],
        ),
        compiler_params=params(),
        cost_estimate=cost(2 * tall * wide * columns, 2 * tall * columns * len(z_slots)),
        name="kernel_strip",
    )(index, *z_slots, *sums)


def dz_kernel(n_batch, n_col, coef, hinge_coef, inv_coef, inv_share, hinge_share, diag_share, index_ref, *refs):
    strip_refs = refs[:n_col]
    z_refs = refs[n_col : n_col + n_batch]
    dz_ref, share_ref, strips, full, centred = refs[n_col + n_batch :]
    local_rows = z_refs[0].shape[0] // 2
    rows = local_rows * n_batch
    reach = n_batch // 2

    @pl.when(pl.program_id(0) == 0)
    def _():
        share_ref[...] = jnp.zeros_like(share_ref)
        part = 2 * local_rows // n_col
        for k in range(n_col):
            start = pl.multiple_of(index_ref[k] * part, part)
            for s in range(n_batch):
                strips[s, pl.ds(start, part), :] = strip_refs[k][s].astype(f32)
        for v in range(2):
            for s in range(n_batch):
                for u in range(reach + 1):
                    t = (s + u) % n_batch
                    block = strips[s, pl.ds(v * local_rows, local_rows), pl.ds(u * local_rows, local_rows)]
                    full[v, pl.ds(s * local_rows, local_rows), pl.ds(t * local_rows, local_rows)] = block.astype(bf16)
                    if 0 < u < n_batch - reach:
                        full[v, pl.ds(t * local_rows, local_rows), pl.ds(s * local_rows, local_rows)] = jnp.transpose(block).astype(bf16)

    share = jnp.zeros((1, 1), f32)
    grads = []
    z_views = []
    for v in range(2):
        zf = jnp.concatenate(
            [z[pl.ds(v * local_rows, local_rows), :].astype(f32) for z in z_refs], axis=0
        )
        z_views.append(zf)
        zc = zf - jnp.sum(zf, axis=0, keepdims=True) / rows
        std = jnp.sqrt(jnp.sum(zc * zc, axis=0, keepdims=True) / (rows - 1) + eps_std)
        zcb = zc.astype(bf16)
        centred[...] = zcb
        rounded = zcb.astype(f32)
        diag = jnp.sum(rounded * rounded, axis=0, keepdims=True)
        moved = jnp.dot(full[v], centred[...], preferred_element_type=f32)
        pull = jnp.where(std < 1.0, hinge_coef, 0.0) / std
        summed = coef * (moved - rounded * diag) - zc * pull
        grads.append(summed - jnp.sum(summed, axis=0, keepdims=True) / rows)
        share += hinge_share * jnp.sum(jnp.maximum(1.0 - std, 0.0), axis=1, keepdims=True)
        share -= diag_share * jnp.sum(diag * diag, axis=1, keepdims=True)
    diff = z_views[0] - z_views[1]
    share += inv_share * jnp.sum(jnp.sum(diff * diff, axis=0, keepdims=True), axis=1, keepdims=True)
    share_ref[...] += jnp.broadcast_to(share, share_ref.shape)
    dz_ref[0] = (grads[0] + inv_coef * diff).astype(bf16)
    dz_ref[1] = (grads[1] - inv_coef * diff).astype(bf16)


def dz_call(index, strips, z_slots, constants):
    n_col, n_batch = len(strips), len(z_slots)
    tall, columns = z_slots[0].shape
    rows = tall // 2 * n_batch
    tile = min(256, columns)
    part = strips[0].shape
    return pl.pallas_call(
        functools.partial(dz_kernel, n_batch, n_col, *constants),
        out_shape=(
            jax.ShapeDtypeStruct((2, rows, columns), bf16),
            jax.ShapeDtypeStruct((8, 128), f32),
        ),
        grid_spec=pltpu.PrefetchScalarGridSpec(
            num_scalar_prefetch=1,
            grid=(columns // tile,),
            in_specs=[whole(part) for _ in strips]
            + [pl.BlockSpec((tall, tile), lambda j, index: (0, j)) for _ in z_slots],
            out_specs=(
                pl.BlockSpec((2, rows, tile), lambda j, index: (0, 0, j)),
                whole((8, 128)),
            ),
            scratch_shapes=[
                pltpu.VMEM((n_batch, tall, part[2]), f32),
                pltpu.VMEM((2, rows, rows), bf16),
                pltpu.VMEM((rows, tile), bf16),
            ],
        ),
        compiler_params=params(),
        cost_estimate=cost(4 * rows * rows * columns, 8 * rows * columns),
        name="embedding_gradient",
    )(index, *strips, *z_slots)


def d_act_kernel(count, adds, index_ref, dz_ref, w_ref, *refs):
    i = pl.program_id(0)
    outs = refs[1:] if adds else refs
    two, local_rows, columns = dz_ref.shape
    dz = dz_ref[...].reshape(two * local_rows, columns)
    part = lax.dot_general(dz, w_ref[0], (((1,), (1,)), ((), ())), preferred_element_type=f32)
    if adds:
        part = part + refs[0][0].astype(f32)
    for j in range(count):

        @pl.when(i == j)
        def _():
            outs[j][...] = part.astype(outs[j].dtype)


def d_act_call(index, dz, blocks, local_rows, ks, got, kind):
    count = len(ks)
    _, width, columns = blocks.shape
    tall = 2 * local_rows
    in_specs = [
        pl.BlockSpec((2, local_rows, columns), lambda i, index: (0, 0, 0)),
        pl.BlockSpec((1, width, columns), lambda i, index: (index[i], 0, 0)),
    ]
    operands = [dz, blocks]
    if got is not None:
        first = ks[0] // 2
        in_specs.append(pl.BlockSpec((1, tall, width), lambda i, index: (first + i, 0, 0)))
        operands.append(got)
    if got is None:
        out_shape = (jax.ShapeDtypeStruct((count, tall, width), kind),)
        out_specs = (pl.BlockSpec((1, tall, width), lambda i, index: (i, 0, 0)),)
    else:
        out_shape = tuple(jax.ShapeDtypeStruct((tall, width), kind) for _ in ks)
        out_specs = tuple(whole((tall, width)) for _ in ks)

    def body(index_ref, dz_ref, w_ref, *refs):
        if got is None:
            d_act_kernel(1, False, index_ref, dz_ref, w_ref, *refs)
        else:
            d_act_kernel(count, True, index_ref, dz_ref, w_ref, *refs)

    def body_stacked(index_ref, dz_ref, w_ref, out_ref):
        two, r, n = dz_ref.shape
        part = lax.dot_general(
            dz_ref[...].reshape(two * r, n), w_ref[0], (((1,), (1,)), ((), ())), preferred_element_type=f32
        )
        out_ref[0] = part.astype(out_ref.dtype)

    return pl.pallas_call(
        body_stacked if got is None else body,
        out_shape=out_shape,
        grid_spec=pltpu.PrefetchScalarGridSpec(
            num_scalar_prefetch=1, grid=(count,), in_specs=in_specs, out_specs=out_specs
        ),
        compiler_params=params(),
        cost_estimate=cost(2 * tall * width * columns * count, 2 * count * width * (columns + tall)),
        name="d_act_matmul",
    )(index, *operands)


def weight_grad_kernel(act_ref, dz_ref, out_ref):
    out_ref[...] = lax.dot_general(
        act_ref[...], dz_ref[...], (((0,), (0,)), ((), ())), preferred_element_type=f32
    )


def weight_grad_call(act, dz):
    rows, features = act.shape
    columns = dz.shape[1]
    tile = min(256, features)
    return pl.pallas_call(
        weight_grad_kernel,
        out_shape=jax.ShapeDtypeStruct((features, columns), f32),
        grid=(features // tile,),
        in_specs=[
            pl.BlockSpec((rows, tile), lambda i: (0, i)),
            pl.BlockSpec((rows, columns), lambda i: (0, 0)),
        ],
        out_specs=pl.BlockSpec((tile, columns), lambda i: (i, 0)),
        compiler_params=params(),
        cost_estimate=cost(2 * rows * features * columns, 4 * features * columns),
        name="weight_gradient",
    )(act, dz)


def shards(views, norm_scale_gain, norm_shift_bias, weight):
    n_batch = lax.axis_size("batch")
    n_col = lax.axis_size("col")
    b = lax.axis_index("batch")
    c = lax.axis_index("col")
    n_view, local_rows, width = views.shape
    columns = weight.shape[1]
    E = columns * n_col
    rows = local_rows * n_batch
    tall = n_view * local_rows
    scale = rows * E / 128.0
    denom = float((rows - 1) ** 2 * E)
    evens = list(range(0, n_col, 2))
    far = evens[1:]
    blocks = weight.reshape(n_col, width, columns)

    def places(ks):
        return jnp.stack([c ^ k for k in ks]).astype(jnp.int32)

    with jax.named_scope("norm_stats"):
        hidden = views.astype(f32)
        local_mean = jnp.mean(hidden, axis=1)
        local_centred = hidden - local_mean[:, None, :]
        local_spread = jnp.sum(local_centred * local_centred, axis=1)
        stats = exchange(jnp.concatenate([local_mean, local_spread]), "batch")
        mean = sum(s[:n_view] for s in stats) / n_batch
        spread = sum(s[n_view:] + local_rows * jnp.square(s[:n_view] - mean) for s in stats)
        var = spread / rows
        inverse_deviation = (1.0 / jnp.sqrt(var + eps_norm))[:, None, :]
        normalised = (hidden - mean[:, None, :]) * inverse_deviation
        preactivation = norm_scale_gain * normalised + norm_shift_bias
        act = jax.nn.gelu(preactivation, approximate=True).astype(bf16)
    with jax.named_scope("act_gather"):
        pieces = {0: act.reshape(tall, width)}
        for k in far:
            pieces[k] = xor_send(pieces[0], "col", k)
        for k in evens:
            pieces[k + 1] = xor_send(pieces[k], "col", 1)
    with jax.named_scope("z"):
        z = z_call(places([0, 1]), [pieces[0], pieces[1]], blocks, None, False)
        z = z_call(places(far), [pieces[k] for k in far], blocks, z, False)
        odd = [k + 1 for k in far]
        z, z_sum = z_call(places(odd), [pieces[k] for k in odd], blocks, z, True)
    with jax.named_scope("z_ring"):
        sums = [z_sum] + [ring_send(z_sum, "batch", d) for d in range(1, n_batch)]
        slots = [z]
        for _ in range(1, n_batch):
            slots.append(ring_send(slots[-1], "batch", 1))
    with jax.named_scope("kernel"):
        reach = n_batch // 2
        everyone = places(range(n_col))
        even_part, odd_part = strip_call(everyone, slots[: reach + 1], sums, rows, n_col)
        even_part = even_part + xor_send(odd_part, "col", 1)
        strip = even_part[0]
        for k in far:
            strip = strip + xor_send(even_part[k // 2], "col", k)
        block = lax.broadcasted_iota(jnp.int32, (1, strip.shape[1]), 1) // local_rows
        twice = jnp.where((block > 0) & (block < n_batch - reach), 2.0, 1.0)
        block_share = jnp.sum(strip * strip * twice) / denom
        mine = strip.astype(bf16)
        mine = jnp.stack([mine] + [ring_send(mine, "batch", d) for d in range(1, n_batch)])
        strips = {0: mine}
        for k in far:
            strips[k] = xor_send(mine, "col", k)
        for k in evens:
            strips[k + 1] = xor_send(strips[k], "col", 1)
    with jax.named_scope("dz"):
        constants = (
            4.0 * scale / denom,
            25.0 * scale / (2.0 * E * (rows - 1)),
            50.0 * scale / (rows * E),
            25.0 / (rows * E) / n_batch,
            25.0 / (2 * E) / n_batch,
            1.0 / denom / n_batch,
        )
        dz, share = dz_call(everyone, [strips[k] for k in range(n_col)], slots, constants)
    with jax.named_scope("d_act"):
        odds = [k + 1 for k in evens]
        (away,) = d_act_call(places(odds), dz, blocks, local_rows, odds, None, bf16)
        got = xor_send(away, "col", 1)
        sends = d_act_call(places(far), dz, blocks, local_rows, far, got, bf16)
        arrived = [xor_send(part, "col", k) for k, part in zip(far, sends)]
        (d_act,) = d_act_call(places([0]), dz, blocks, local_rows, [0], got, f32)
    with jax.named_scope("grad_weight"):
        per_plane = n_col // n_batch
        order = jnp.array(ring_order(n_batch), jnp.int32)
        position = jnp.where(b % 2 == 0, b // 2, n_batch - 1 - b // 2)
        stacked = jnp.stack([pieces[k] for k in evens])

        def held(plane, i):
            k = (per_plane * plane + 2 * i) ^ (c - c % 2)
            return lax.dynamic_index_in_dim(stacked, k // 2, 0, keepdims=False)

        halves = []
        for i in range(per_plane // 2):
            own = [held(b, i)]
            for d in range(1, n_batch):
                ahead = (position + d) % n_batch
                plane = jnp.where(ahead < (n_batch + 1) // 2, 2 * ahead, 2 * (n_batch - ahead) - 1)
                own.append(ring_send(held(plane, i), "batch", d))
            own = jnp.concatenate([o.reshape(n_view, local_rows, width) for o in own], axis=1)
            other = xor_send(own, "col", 1)
            halves.append(jnp.where(c % 2 == 0, own, other))
            halves.append(jnp.where(c % 2 == 0, other, own))
        wanted = jnp.concatenate(halves, axis=2).reshape(n_view * rows, per_plane * width)
        grad_weight = weight_grad_call(wanted, dz.reshape(n_view * rows, columns))
    with jax.named_scope("loss"):
        share = share + block_share
        k = 1
        while k < n_col:
            share = share + xor_send(share, "col", k)
            k *= 2
    with jax.named_scope("norm_backward"):
        arrived, d_act, grad_weight = lax.optimization_barrier((arrived, d_act, grad_weight))
        for part in arrived:
            d_act = d_act + part.astype(f32)
        d_pre = d_act.reshape(n_view, local_rows, width) * gelu_slope(preactivation)
        sums = jnp.concatenate([jnp.sum(d_pre, axis=1), jnp.sum(d_pre * normalised, axis=1)])
        last = exchange(sums, "batch")
        loss = sum(exchange(share, "batch"))[0, 0]
        both = sum(last)
        sum_b, sum_g = both[:n_view], both[n_view:]
        grad_bias = jnp.sum(sum_b, axis=0)
        grad_gain = jnp.sum(sum_g, axis=0)
        views_gradient = (
            norm_scale_gain
            * (d_pre - sum_b[:, None, :] / rows - normalised * sum_g[:, None, :] / rows)
            * inverse_deviation
        )
    return (loss, grad_weight, grad_gain, grad_bias, views_gradient)


def solution(mesh):
    placed = (P(None, "batch", "col"), P("col"), P("col"), P(None, "col"))
    return jax.shard_map(
        shards,
        mesh=mesh,
        in_specs=placed,
        out_specs=(P(), P("batch", "col"), P("col"), P("col"), P(None, "batch", "col")),
        check_vma=False,
    )
```

time: 183 us -> 174 us (0.951)
  waiting for transfers between devices: 39.3 us -> 73.1 us
  matrix products: 30.4 us -> 0 us
  Pallas kernels: 0 us -> 22.2 us
  local copies, waits for them, and re-layouts: 32.2 us -> 12.7 us
  other arithmetic: 16.6 us -> 9.78 us
  between operations: 6.18 us -> 1.83 us
  starting transfers between devices: 57.6 us -> 53.8 us
    ppermute x3 -> x12, waiting for transfers between devices: 4.43 us -> 40.7 us  [ring_send(): lax.ppermute(x, axis, [(order[i], order[(i + d) % n]) for i in range(n)])]
    dot_general x15 -> x0, matrix products: 30.4 us -> none  [the longest x4 13.7 us: shards(): jnp.einsum('vrk,kj->vrj', a, weight_xor, preferred_element_type=f32)]
    ppermute x59 -> x26, starting transfers between devices: 43.4 us -> 18.7 us  [xor_send(): return lax.ppermute(x, axis, [(i, i ^ k) for i in range(n)])]
    pallas_call x0 -> x9, Pallas kernels: none -> 22.2 us  [the longest x3 6.05 us: d_act_call(): pl.pallas_call(body_stacked if got is None else body, out_shape=out_shape...]
    ppermute x3 -> x12, starting transfers between devices: 5.57 us -> 21.4 us  [ring_send(): lax.ppermute(x, axis, [(order[i], order[(i + d) % n]) for i in range(n)])]
    ppermute x59 -> x26, waiting for transfers between devices: 34.9 us -> 23.1 us  [xor_send(): return lax.ppermute(x, axis, [(i, i ^ k) for i in range(n)])]
    ppermute x6 -> x9, waiting for transfers between devices: 0.02 us -> 9.33 us  [exchange(): slots.append(lax.ppermute(x, axis, [(i, (i + d) % n) for i in range(n)]))]
    unnamed x87 -> x28, local copies, waits for them, and re-layouts: 17.8 us -> 12 us
  transfers between devices with their start and end apart: 68 -> 47, of which waited for: 18 -> 20; matrix products, arithmetic and copies ran while one was open for 35% -> 3% of each run, Pallas kernels for 0% -> 11%
where the time goes in v2:
time: 174 us
  waiting for transfers between devices  73.1 us (42%)
  starting transfers between devices  53.8 us (31%)
  Pallas kernels  22.2 us (13%)
  local copies, waits for them, and re-layouts  12.7 us (7%)
  other arithmetic  9.78 us (6%)
  between operations  1.83 us (1%)
    ppermute x12, waiting for transfers between devices, ring_send(): lax.ppermute(x, axis, [(order[i], order[(i + d) % n]) for i in range(n)])  40.7 us
    ppermute x26, waiting for transfers between devices, xor_send(): return lax.ppermute(x, axis, [(i, i ^ k) for i in range(n)])  23.1 us
    ppermute x12, starting transfers between devices, ring_send(): lax.ppermute(x, axis, [(order[i], order[(i + d) % n]) for i in range(n)])  21.4 us
    ppermute x26, starting transfers between devices, xor_send(): return lax.ppermute(x, axis, [(i, i ^ k) for i in range(n)])  18.7 us
    ppermute x9, starting transfers between devices, exchange(): slots.append(lax.ppermute(x, axis, [(i, (i + d) % n) for i in range(n)]))  13.7 us
    unnamed x28, local copies, waits for them, and re-layouts  12 us
    ppermute x9, waiting for transfers between devices, exchange(): slots.append(lax.ppermute(x, axis, [(i, (i + d) % n) for i in range(n)]))  9.33 us
    pallas_call x3, Pallas kernels, d_act_call(): pl.pallas_call(body_stacked if got is None else body, out_shape=out_shape...  6.05 us
  transfers between devices with their start and end apart: 47, of which 20 were waited for; matrix products, arithmetic and copies ran while one was open for 3% of the time, Pallas kernels for 11%

profile of v2, /device:TPU:0, one launch (start us, length us, event | category | flops | bytes accessed | tf_op | source)
XLA Modules:
  0.0 173.5 jit_solution(3721172537699562967)
XLA Ops:
  2.7 5.1 %collective-permute-start = (f32[4,512]{1,0:T(4,128)S(1)}, f32[4,512]{1,0:T(4,128)S(1)}, u32[]{:S(2)}, u32[]{:S(2)}) collective-permute-start(f32[4,512]{1,0:T(4,128)S(1)} %pad_maximum_fusion.4), channel_id=1, source_target_pairs={{0,24},{8,0},{16,8},{24,16},{1,25},{9,1},{17,9},{25,17},{2,26},{10... | collective-permute-start | bytes 24584 | tf_op jit(solution)/shard_map/norm_stats/ppermute | solution.py:42
  9.2 3.2 %collective-permute-done.1 = f32[4,512]{1,0:T(4,128)S(1)} collective-permute-done((f32[4,512]{1,0:T(4,128)S(1)}, f32[4,512]{1,0:T(4,128)S(1)}, u32[]{:S(2)}, u32[]{:S(2)}) %collective-permute-start.1) | collective-permute-done | bytes 8224 | tf_op jit(solution)/shard_map/norm_stats/ppermute | solution.py:42
  13.3 1.2 fusion.17
  14.6 1.6 collective-permute-start.3
  16.1 1.5 collective-permute-start.5
  18.1 5.8 %collective-permute-done.3.refs_0_ = bf16[256,512]{1,0:T(8,128)(2,1)S(1)} collective-permute-done((bf16[256,512]{1,0:T(8,128)(2,1)S(1)}, bf16[256,512]{1,0:T(8,128)(2,1)S(1)}, u32[]{:S(2)}, u32[]{:S(2)}) %collective-permute-start.3) | collective-permute-done | bytes 262176 | tf_op jit(solution)/shard_map/act_gather/ppermute | solution.py:24
  23.9 4.2 %collective-permute-done.5.refs_1_ = bf16[256,512]{1,0:T(8,128)(2,1)S(1)} collective-permute-done((bf16[256,512]{1,0:T(8,128)(2,1)S(1)}, bf16[256,512]{1,0:T(8,128)(2,1)S(1)}, u32[]{:S(2)}, u32[]{:S(2)}) %collective-permute-start.5) | collective-permute-done | bytes 262176 | tf_op jit(solution)/shard_map/act_gather/ppermute | solution.py:24
  28.7 3.4 %copy-done = bf16[4096,1024]{1,0:T(8,128)(2,1)S(1)} copy-done((bf16[4096,1024]{1,0:T(8,128)(2,1)S(1)}, bf16[4096,1024]{1,0:T(8,128)(2,1)}, u32[]{:S(2)}) %copy-start) | copy-done | bytes 8388632
  32.1 1.5 z_matmul.3.refs_4_
  33.6 1.9 %copy-done.1 = bf16[4096,1024]{1,0:T(8,128)(2,1)S(1)} copy-done((bf16[4096,1024]{1,0:T(8,128)(2,1)S(1)}, bf16[4096,1024]{1,0:T(8,128)(2,1)}, u32[]{:S(2)}) %copy-start.1) | copy-done | bytes 8388632
  35.5 2.0 %z_matmul.4.refs_4_ = f32[256,1024]{1,0:T(8,128)S(1)} custom-call(s32[3]{0:T(128)S(1)} %get-tuple-element.57.index_ref, bf16[256,512]{1,0:T(8,128)(2,1)S(1)} %collective-permute-done.3.refs_0_, bf16[256,512]{1,0:T(8,128)(2,1)S(1)} %collective-permute-done.5.refs_1_, bf16[256,512]{1,0:T(8,128)(2,1)S(1)} %collective-permute-done.7.refs_2_, ...), custom_call_target="tpu_custom_call" | custom-call | flops 805306368 | bytes 3932160 | tf_op jit(solution)/shard_map/z/z_matmul/pallas_call | solution.py:119
  37.5 2.0 %z_matmul.5 = (bf16[256,1024]{1,0:T(8,128)(2,1)S(1)}, f32[2,1024]{1,0:T(2,128)S(1)}) custom-call(s32[3]{0:T(128)S(1)} %get-tuple-element.56.index_ref, bf16[256,512]{1,0:T(8,128)(2,1)S(1)} %collective-permute-done.4.refs_0_, bf16[256,512]{1,0:T(8,128)(2,1)S(1)} %collective-permute-done.6.refs_1_, bf16[256,512]{1,0:T(8,128)(2,1)S(1)} %collective-permute-done.8.refs_2_, ...), custom_call_target="tpu_custom_call" | custom-call | flops 805306368 | bytes 3932160 | tf_op jit(solution)/shard_map/z/z_matmul/pallas_call | solution.py:119
  40.5 12.9 %collective-permute-done.10.refs_1_.refs_9_ = bf16[256,1024]{1,0:T(8,128)(2,1)S(1)} collective-permute-done((bf16[256,1024]{1,0:T(8,128)(2,1)S(1)}, bf16[256,1024]{1,0:T(8,128)(2,1)S(1)}, u32[]{:S(2)}, u32[]{:S(2)}) %collective-permute-start.10) | collective-permute-done | bytes 524320 | tf_op jit(solution)/shard_map/z_ring/ppermute | solution.py:34
  53.4 1.8 %collective-permute-start.11 = (bf16[256,1024]{1,0:T(8,128)(2,1)S(1)}, bf16[256,1024]{1,0:T(8,128)(2,1)S(1)}, u32[]{:S(2)}, u32[]{:S(2)}) collective-permute-start(bf16[256,1024]{1,0:T(8,128)(2,1)S(1)} %collective-permute-done.10.refs_1_.refs_9_), channel_id=1, source_target_pairs={{0,16},{16,24},{24,8},{8,0},{1,17},{17,25},{25,9},{9,1},{2,18},{18... | collective-permute-start | bytes 1572872 | tf_op jit(solution)/shard_map/z_ring/ppermute | solution.py:34
  55.2 2.6 %collective-permute-start.13 = (f32[2,1024]{1,0:T(2,128)S(1)}, f32[2,1024]{1,0:T(2,128)S(1)}, u32[]{:S(2)}, u32[]{:S(2)}) collective-permute-start(f32[2,1024]{1,0:T(2,128)S(1)} %get-tuple-element.20.refs_3_), channel_id=1, source_target_pairs={{0,24},{16,8},{24,0},{8,16},{1,25},{17,9},{25,1},{9,17},{2,26},{18... | collective-permute-start | bytes 24584 | tf_op jit(solution)/shard_map/z_ring/ppermute | solution.py:34
  57.9 8.8 %collective-permute-done.12.refs_4_ = f32[2,1024]{1,0:T(2,128)S(1)} collective-permute-done((f32[2,1024]{1,0:T(2,128)S(1)}, f32[2,1024]{1,0:T(2,128)S(1)}, u32[]{:S(2)}, u32[]{:S(2)}) %collective-permute-start.12) | collective-permute-done | bytes 8224 | tf_op jit(solution)/shard_map/z_ring/ppermute | solution.py:34
  67.7 1.2 kernel_strip.1
  70.5 1.9 %collective-permute-start.16 = (f32[32,384]{1,0:T(8,128)S(1)}, f32[32,384]{1,0:T(8,128)S(1)}, u32[]{:S(2)}, u32[]{:S(2)}) collective-permute-start(f32[32,384]{1,0:T(8,128)S(1)} %get-tuple-element.48), channel_id=1, source_target_pairs={{0,2},{1,3},{2,0},{3,1},{4,6},{5,7},{6,4},{7,5},{8,10},{9,11},{10,... | collective-permute-start | bytes 147464 | tf_op jit(solution)/shard_map/kernel/ppermute | solution.py:24
  72.4 2.0 %collective-permute-start.40 = (bf16[256,512]{1,0:T(8,128)(2,1)S(1)}, bf16[256,512]{1,0:T(8,128)(2,1)S(1)}, u32[]{:S(2)}, u32[]{:S(2)}) collective-permute-start(bf16[256,512]{1,0:T(8,128)(2,1)S(1)} %get-tuple-element.47), channel_id=1, source_target_pairs={{0,16},{16,24},{24,8},{8,0},{1,17},{17,25},{25,9},{9,1},{2,18},{18... | collective-permute-start | bytes 786440 | tf_op jit(solution)/shard_map/grad_weight/ppermute | solution.py:34
  74.4 1.4 collective-permute-start.41
  76.8 1.4 collective-permute-start.18
  78.2 2.4 %collective-permute-done.17 = f32[32,384]{1,0:T(8,128)S(1)} collective-permute-done((f32[32,384]{1,0:T(8,128)S(1)}, f32[32,384]{1,0:T(8,128)S(1)}, u32[]{:S(2)}, u32[]{:S(2)}) %collective-permute-start.17) | collective-permute-done | bytes 49184 | tf_op jit(solution)/shard_map/kernel/ppermute | solution.py:24
  80.6 2.2 %collective-permute-start.29 = (bf16[256,1024]{1,0:T(8,128)(2,1)S(1)}, bf16[256,1024]{1,0:T(8,128)(2,1)S(1)}, u32[]{:S(2)}, u32[]{:S(2)}) collective-permute-start(bf16[256,1024]{1,0:T(8,128)(2,1)S(1)} %collective-permute-done.11.refs_2_.refs_10_), channel_id=1, source_target_pairs={{0,16},{16,24},{24,8},{8,0},{1,17},{17,25},{25,9},{9,1},{2,18},{18... | collective-permute-start | bytes 1572872 | tf_op jit(solution)/shard_map/z_ring/ppermute | solution.py:34
  83.5 1.2 collective-permute-start.19
  84.6 2.4 %collective-permute-start.20 = (bf16[32,384]{1,0:T(8,128)(2,1)S(1)}, bf16[32,384]{1,0:T(8,128)(2,1)S(1)}, u32[]{:S(2)}, u32[]{:S(2)}) collective-permute-start(bf16[32,384]{1,0:T(8,128)(2,1)S(1)} %get-tuple-element.39), channel_id=1, source_target_pairs={{0,24},{16,8},{24,0},{8,16},{1,25},{17,9},{25,1},{9,17},{2,26},{18... | collective-permute-start | bytes 73736 | tf_op jit(solution)/shard_map/kernel/ppermute | solution.py:34
  87.0 1.7 collective-permute-done.41
  88.7 6.2 %collective-permute-start.21 = (bf16[32,384]{1,0:T(8,128)(2,1)S(1)}, bf16[32,384]{1,0:T(8,128)(2,1)S(1)}, u32[]{:S(2)}, u32[]{:S(2)}) collective-permute-start(bf16[32,384]{1,0:T(8,128)(2,1)S(1)} %get-tuple-element.39), channel_id=1, source_target_pairs={{0,8},{16,0},{24,16},{8,24},{1,9},{17,1},{25,17},{9,25},{2,10},{18... | collective-permute-start | bytes 73736 | tf_op jit(solution)/shard_map/kernel/ppermute | solution.py:34
  94.9 16.2 %collective-permute-done.42 = bf16[256,512]{1,0:T(8,128)(2,1)S(1)} collective-permute-done((bf16[256,512]{1,0:T(8,128)(2,1)S(1)}, bf16[256,512]{1,0:T(8,128)(2,1)S(1)}, u32[]{:S(2)}, u32[]{:S(2)}) %collective-permute-start.42) | collective-permute-done | bytes 262176 | tf_op jit(solution)/shard_map/grad_weight/ppermute | solution.py:34
  112.6 1.4 collective-permute-start.25
  114.0 1.7 %collective-permute-start.27 = (bf16[4,32,384]{2,1,0:T(8,128)(2,1)S(1)}, bf16[4,32,384]{2,1,0:T(8,128)(2,1)S(1)}, u32[]{:S(2)}, u32[]{:S(2)}) collective-permute-start(bf16[4,32,384]{2,1,0:T(8,128)(2,1)S(1)} %pad_maximum_fusion.3.refs_0_), channel_id=1, source_target_pairs={{0,6},{1,7},{2,4},{3,5},{4,2},{5,3},{6,0},{7,1},{8,14},{9,15},{10,... | collective-permute-start | bytes 294920 | tf_op jit(solution)/shard_map/kernel/ppermute | solution.py:24
  115.8 2.1 %collective-permute-done.23.refs_2_ = bf16[4,32,384]{2,1,0:T(8,128)(2,1)S(1)} collective-permute-done((bf16[4,32,384]{2,1,0:T(8,128)(2,1)S(1)}, bf16[4,32,384]{2,1,0:T(8,128)(2,1)S(1)}, u32[]{:S(2)}, u32[]{:S(2)}) %collective-permute-start.23) | collective-permute-done | bytes 98336 | tf_op jit(solution)/shard_map/kernel/ppermute | solution.py:24
  118.4 1.3 collective-permute-done.27.refs_6_
  121.1 5.2 %embedding_gradient.1 = (bf16[2,512,1024]{2,1,0:T(8,128)(2,1)S(1)}, f32[8,128]{1,0:T(8,128)S(1)}) custom-call(s32[8]{0:T(128)S(1)} %stack.91.index_ref, bf16[4,32,384]{2,1,0:T(8,128)(2,1)S(1)} %pad_maximum_fusion.3.refs_0_, bf16[4,32,384]{2,1,0:T(8,128)(2,1)S(1)} %collective-permute-done.22.refs_1_, bf16[4,32,384]{2,1,0:T(8,128)(2,1)S(1)} %collective-permute-done.23.refs_2_, ...), custom_call_target="tpu_custom_call" | custom-call | flops 1073741824 | bytes 4194304 | tf_op jit(solution)/shard_map/dz/embedding_gradient/pallas_call | solution.py:234
  126.3 3.4 %copy-done.2 = bf16[4096,1024]{1,0:T(8,128)(2,1)S(1)} copy-done((bf16[4096,1024]{1,0:T(8,128)(2,1)S(1)}, bf16[4096,1024]{1,0:T(8,128)(2,1)}, u32[]{:S(2)}) %copy-start.2) | copy-done | bytes 8388632
  129.7 3.4 %d_act_matmul.3 = bf16[4,256,512]{2,1,0:T(8,128)(2,1)} custom-call(s32[4]{0:T(128)S(1)} %pad_add_fusion.3.index_ref, bf16[2,512,1024]{2,1,0:T(8,128)(2,1)S(1)} %get-tuple-element.24.dz_ref, bf16[8,512,1024]{2,1,0:T(8,128)(2,1)S(1)} %bitcast.51), custom_call_target="tpu_custom_call" | custom-call | flops 1073741824 | bytes 5242880 | tf_op jit(solution)/shard_map/d_act/d_act_matmul/pallas_call | solution.py:309
  134.4 1.8 %broadcast_select_fusion.1 = (bf16[2,512,512]{2,1,0:T(8,128)(2,1)S(1)}, bf16[2,512,512]{2,1,0:T(8,128)(2,1)S(1)}) fusion(bf16[2,512,512]{2,1,0:T(8,128)(2,1)} %collective-permute-done.43, pred[]{:T(512)S(6)} %eq.126, bf16[2,128,512]{2,1,0:T(8,128)(2,1)} %bitcast.74, bf16[2,128,512]{2,1,0:T(8,128)(2,1)} %bitcast.72, bf16[2,128,512]{2,1,0:T(8,128)(2,1)} %bitcast.70, ...), kind=kLoop, calls=%fused_computation.4 | loop fusion | flops 5242880 | bytes 4194305 | tf_op jit(solution)/shard_map/grad_weight/jit(_where)/select_n | solution.py:448
  136.2 2.1 %collective-permute-start.31 = (f32[8,128]{1,0:T(8,128)S(1)}, f32[8,128]{1,0:T(8,128)S(1)}, u32[]{:S(2)}, u32[]{:S(2)}) collective-permute-start(f32[8,128]{1,0:T(8,128)S(1)} %fusion.42), channel_id=1, source_target_pairs={{0,2},{1,3},{2,0},{3,1},{4,6},{5,7},{6,4},{7,5},{8,10},{9,11},{10,... | collective-permute-start | bytes 12296 | tf_op jit(solution)/shard_map/loss/ppermute | solution.py:24
  138.4 3.4 %copy-done.3 = bf16[4096,1024]{1,0:T(8,128)(2,1)S(1)} copy-done((bf16[4096,1024]{1,0:T(8,128)(2,1)S(1)}, bf16[4096,1024]{1,0:T(8,128)(2,1)}, u32[]{:S(2)}) %copy-start.3) | copy-done | bytes 8388632
  141.7 2.1 %d_act_matmul.4 = (bf16[256,512]{1,0:T(8,128)(2,1)S(1)}, bf16[256,512]{1,0:T(8,128)(2,1)S(1)}, bf16[256,512]{1,0:T(8,128)(2,1)S(1)}) custom-call(s32[3]{0:T(128)S(1)} %get-tuple-element.57.index_ref, bf16[2,512,1024]{2,1,0:T(8,128)(2,1)S(1)} %get-tuple-element.24.dz_ref, bf16[8,512,1024]{2,1,0:T(8,128)(2,1)S(1)} %bitcast.52, ...), custom_call_target="tpu_custom_call" | custom-call | flops 805306368 | bytes 3932160 | tf_op jit(solution)/shard_map/d_act/d_act_matmul/pallas_call | solution.py:309
  144.0 1.4 collective-permute-start.38
  145.3 2.1 %collective-permute-start.39 = (bf16[256,512]{1,0:T(8,128)(2,1)S(1)}, bf16[256,512]{1,0:T(8,128)(2,1)S(1)}, u32[]{:S(2)}, u32[]{:S(2)}) collective-permute-start(bf16[256,512]{1,0:T(8,128)(2,1)S(1)} %get-tuple-element.27), channel_id=1, source_target_pairs={{0,6},{1,7},{2,4},{3,5},{4,2},{5,3},{6,0},{7,1},{8,14},{9,15},{10,... | collective-permute-start | bytes 786440 | tf_op jit(solution)/shard_map/d_act/ppermute | solution.py:24
  148.0 4.4 %weight_gradient.1 = f32[1024,1024]{1,0:T(8,128)} custom-call(bf16[1024,1024]{1,0:T(8,128)(2,1)S(1)} %bitcast.57, bf16[1024,1024]{1,0:T(8,128)(2,1)S(1)} %bitcast.56), custom_call_target="tpu_custom_call" | custom-call | flops 2147483648 | bytes 4194304 | tf_op jit(solution)/shard_map/grad_weight/weight_gradient/pallas_call | solution.py:331
  152.4 5.4 %collective-permute-done.32 = f32[8,128]{1,0:T(8,128)S(1)} collective-permute-done((f32[8,128]{1,0:T(8,128)S(1)}, f32[8,128]{1,0:T(8,128)S(1)}, u32[]{:S(2)}, u32[]{:S(2)}) %collective-permute-start.32) | collective-permute-done | bytes 4128 | tf_op jit(solution)/shard_map/loss/ppermute | solution.py:24
  157.8 2.5 %collective-permute-start.33 = (f32[8,128]{1,0:T(8,128)S(1)}, f32[8,128]{1,0:T(8,128)S(1)}, u32[]{:S(2)}, u32[]{:S(2)}) collective-permute-start(f32[8,128]{1,0:T(8,128)S(1)} %add.239), channel_id=1, source_target_pairs={{0,24},{8,0},{16,8},{24,16},{1,25},{9,1},{17,9},{25,17},{2,26},{10... | collective-permute-start | bytes 12296 | tf_op jit(solution)/shard_map/norm_backward/ppermute | solution.py:42
  162.1 3.3 %collective-permute-start.44 = (f32[4,512]{1,0:T(4,128)S(1)}, f32[4,512]{1,0:T(4,128)S(1)}, u32[]{:S(2)}, u32[]{:S(2)}) collective-permute-start(f32[4,512]{1,0:T(4,128)S(1)} %pad_maximum_fusion.5), channel_id=1, source_target_pairs={{0,24},{8,0},{16,8},{24,16},{1,25},{9,1},{17,9},{25,17},{2,26},{10... | collective-permute-start | bytes 24584 | tf_op jit(solution)/shard_map/norm_backward/ppermute | solution.py:42
  165.4 1.1 collective-permute-start.45
  167.1 2.9 %collective-permute-done.45 = f32[4,512]{1,0:T(4,128)S(1)} collective-permute-done((f32[4,512]{1,0:T(4,128)S(1)}, f32[4,512]{1,0:T(4,128)S(1)}, u32[]{:S(2)}, u32[]{:S(2)}) %collective-permute-start.45) | collective-permute-done | bytes 8224 | tf_op jit(solution)/shard_map/norm_backward/ppermute | solution.py:42
  169.9 2.0 %collective-permute-done.46 = f32[4,512]{1,0:T(4,128)S(1)} collective-permute-done((f32[4,512]{1,0:T(4,128)S(1)}, f32[4,512]{1,0:T(4,128)S(1)}, u32[]{:S(2)}, u32[]{:S(2)}) %collective-permute-start.46) | collective-permute-done | bytes 8224 | tf_op jit(solution)/shard_map/norm_backward/ppermute | solution.py:42
  (117 shorter events, 19.3 us)
Async XLA Ops:
  2.7 6.5 %collective-permute-start = (f32[4,512]{1,0:T(4,128)S(1)}, f32[4,512]{1,0:T(4,128)S(1)}, u32[]{:S(2)}, u32[]{:S(2)}) collective-permute-start(f32[4,512]{1,0:T(4,128)S(1)} %pad_maximum_fusion.4), channel_id=1, source_target_pairs={{0,24},{8,0},{16,8},{24,16},{1,25},{9,1},{17,9},{25,17},{2,26},{10... | collective-permute-start | bytes 24584 | tf_op jit(solution)/shard_map/norm_stats/ppermute | solution.py:42
  7.8 4.5 %collective-permute-start.1 = (f32[4,512]{1,0:T(4,128)S(1)}, f32[4,512]{1,0:T(4,128)S(1)}, u32[]{:S(2)}, u32[]{:S(2)}) collective-permute-start(f32[4,512]{1,0:T(4,128)S(1)} %pad_maximum_fusion.4), channel_id=1, source_target_pairs={{0,16},{8,24},{16,0},{24,8},{1,17},{9,25},{17,1},{25,9},{2,18},{10... | collective-permute-start | bytes 24584 | tf_op jit(solution)/shard_map/norm_stats/ppermute | solution.py:42
  7.8 5.4 %collective-permute-start.2 = (f32[4,512]{1,0:T(4,128)S(1)}, f32[4,512]{1,0:T(4,128)S(1)}, u32[]{:S(2)}, u32[]{:S(2)}) collective-permute-start(f32[4,512]{1,0:T(4,128)S(1)} %pad_maximum_fusion.4), channel_id=1, source_target_pairs={{0,8},{8,16},{16,24},{24,0},{1,9},{9,17},{17,25},{25,1},{2,10},{10... | collective-permute-start | bytes 24584 | tf_op jit(solution)/shard_map/norm_stats/ppermute | solution.py:42
  14.6 9.3 %collective-permute-start.3 = (bf16[256,512]{1,0:T(8,128)(2,1)S(1)}, bf16[256,512]{1,0:T(8,128)(2,1)S(1)}, u32[]{:S(2)}, u32[]{:S(2)}) collective-permute-start(bf16[256,512]{1,0:T(8,128)(2,1)S(1)} %bitcast.58), channel_id=1, source_target_pairs={{0,2},{1,3},{2,0},{3,1},{4,6},{5,7},{6,4},{7,5},{8,10},{9,11},{10,... | collective-permute-start | bytes 786440 | tf_op jit(solution)/shard_map/act_gather/ppermute | solution.py:24
  16.1 12.0 %collective-permute-start.5 = (bf16[256,512]{1,0:T(8,128)(2,1)S(1)}, bf16[256,512]{1,0:T(8,128)(2,1)S(1)}, u32[]{:S(2)}, u32[]{:S(2)}) collective-permute-start(bf16[256,512]{1,0:T(8,128)(2,1)S(1)} %bitcast.59), channel_id=1, source_target_pairs={{0,4},{1,5},{2,6},{3,7},{4,0},{5,1},{6,2},{7,3},{8,12},{9,13},{10,... | collective-permute-start | bytes 786440 | tf_op jit(solution)/shard_map/act_gather/ppermute | solution.py:24
  17.6 10.4 %collective-permute-start.7 = (bf16[256,512]{1,0:T(8,128)(2,1)S(1)}, bf16[256,512]{1,0:T(8,128)(2,1)S(1)}, u32[]{:S(2)}, u32[]{:S(2)}) collective-permute-start(bf16[256,512]{1,0:T(8,128)(2,1)S(1)} %bitcast.60), channel_id=1, source_target_pairs={{0,6},{1,7},{2,4},{3,5},{4,2},{5,3},{6,0},{7,1},{8,14},{9,15},{10,... | collective-permute-start | bytes 786440 | tf_op jit(solution)/shard_map/act_gather/ppermute | solution.py:24
  18.1 10.6 %collective-permute-start.9 = (bf16[256,512]{1,0:T(8,128)(2,1)S(1)}, bf16[256,512]{1,0:T(8,128)(2,1)S(1)}, u32[]{:S(2)}, u32[]{:S(2)}) collective-permute-start(bf16[256,512]{1,0:T(8,128)(2,1)S(1)} %bitcast.61), channel_id=1, source_target_pairs={{0,1},{1,0},{2,3},{3,2},{4,5},{5,4},{6,7},{7,6},{8,9},{9,8},{10,11... | collective-permute-start | bytes 786440 | tf_op jit(solution)/shard_map/act_gather/ppermute | solution.py:24
  23.9 13.6 %collective-permute-start.4 = (bf16[256,512]{1,0:T(8,128)(2,1)S(1)}, bf16[256,512]{1,0:T(8,128)(2,1)S(1)}, u32[]{:S(2)}, u32[]{:S(2)}) collective-permute-start(bf16[256,512]{1,0:T(8,128)(2,1)S(1)} %collective-permute-done.3.refs_0_), channel_id=1, source_target_pairs={{0,1},{1,0},{2,3},{3,2},{4,5},{5,4},{6,7},{7,6},{8,9},{9,8},{10,11... | collective-permute-start | bytes 786440 | tf_op jit(solution)/shard_map/act_gather/ppermute | solution.py:24
  28.1 9.4 %collective-permute-start.6 = (bf16[256,512]{1,0:T(8,128)(2,1)S(1)}, bf16[256,512]{1,0:T(8,128)(2,1)S(1)}, u32[]{:S(2)}, u32[]{:S(2)}) collective-permute-start(bf16[256,512]{1,0:T(8,128)(2,1)S(1)} %collective-permute-done.5.refs_1_), channel_id=1, source_target_pairs={{0,1},{1,0},{2,3},{3,2},{4,5},{5,4},{6,7},{7,6},{8,9},{9,8},{10,11... | collective-permute-start | bytes 786440 | tf_op jit(solution)/shard_map/act_gather/ppermute | solution.py:24
  28.1 9.4 %collective-permute-start.8 = (bf16[256,512]{1,0:T(8,128)(2,1)S(1)}, bf16[256,512]{1,0:T(8,128)(2,1)S(1)}, u32[]{:S(2)}, u32[]{:S(2)}) collective-permute-start(bf16[256,512]{1,0:T(8,128)(2,1)S(1)} %collective-permute-done.7.refs_2_), channel_id=1, source_target_pairs={{0,1},{1,0},{2,3},{3,2},{4,5},{5,4},{6,7},{7,6},{8,9},{9,8},{10,11... | collective-permute-start | bytes 786440 | tf_op jit(solution)/shard_map/act_gather/ppermute | solution.py:24
  39.5 13.9 %collective-permute-start.10 = (bf16[256,1024]{1,0:T(8,128)(2,1)S(1)}, bf16[256,1024]{1,0:T(8,128)(2,1)S(1)}, u32[]{:S(2)}, u32[]{:S(2)}) collective-permute-start(bf16[256,1024]{1,0:T(8,128)(2,1)S(1)} %get-tuple-element.19.refs_0_.refs_8_), channel_id=1, source_target_pairs={{0,16},{16,24},{24,8},{8,0},{1,17},{17,25},{25,9},{9,1},{2,18},{18... | collective-permute-start | bytes 1572872 | tf_op jit(solution)/shard_map/z_ring/ppermute | solution.py:34
  53.4 14.3 %collective-permute-start.11 = (bf16[256,1024]{1,0:T(8,128)(2,1)S(1)}, bf16[256,1024]{1,0:T(8,128)(2,1)S(1)}, u32[]{:S(2)}, u32[]{:S(2)}) collective-permute-start(bf16[256,1024]{1,0:T(8,128)(2,1)S(1)} %collective-permute-done.10.refs_1_.refs_9_), channel_id=1, source_target_pairs={{0,16},{16,24},{24,8},{8,0},{1,17},{17,25},{25,9},{9,1},{2,18},{18... | collective-permute-start | bytes 1572872 | tf_op jit(solution)/shard_map/z_ring/ppermute | solution.py:34
  55.2 11.5 %collective-permute-start.12 = (f32[2,1024]{1,0:T(2,128)S(1)}, f32[2,1024]{1,0:T(2,128)S(1)}, u32[]{:S(2)}, u32[]{:S(2)}) collective-permute-start(f32[2,1024]{1,0:T(2,128)S(1)} %get-tuple-element.20.refs_3_), channel_id=1, source_target_pairs={{0,16},{16,24},{24,8},{8,0},{1,17},{17,25},{25,9},{9,1},{2,18},{18... | collective-permute-start | bytes 24584 | tf_op jit(solution)/shard_map/z_ring/ppermute | solution.py:34
  55.2 12.3 %collective-permute-start.13 = (f32[2,1024]{1,0:T(2,128)S(1)}, f32[2,1024]{1,0:T(2,128)S(1)}, u32[]{:S(2)}, u32[]{:S(2)}) collective-permute-start(f32[2,1024]{1,0:T(2,128)S(1)} %get-tuple-element.20.refs_3_), channel_id=1, source_target_pairs={{0,24},{16,8},{24,0},{8,16},{1,25},{17,9},{25,1},{9,17},{2,26},{18... | collective-permute-start | bytes 24584 | tf_op jit(solution)/shard_map/z_ring/ppermute | solution.py:34
  57.8 9.9 %collective-permute-start.14 = (f32[2,1024]{1,0:T(2,128)S(1)}, f32[2,1024]{1,0:T(2,128)S(1)}, u32[]{:S(2)}, u32[]{:S(2)}) collective-permute-start(f32[2,1024]{1,0:T(2,128)S(1)} %get-tuple-element.20.refs_3_), channel_id=1, source_target_pairs={{0,8},{16,0},{24,16},{8,24},{1,9},{17,1},{25,17},{9,25},{2,10},{18... | collective-permute-start | bytes 24584 | tf_op jit(solution)/shard_map/z_ring/ppermute | solution.py:34
  68.9 1.5 collective-permute-start.15
  70.5 6.3 %collective-permute-start.16 = (f32[32,384]{1,0:T(8,128)S(1)}, f32[32,384]{1,0:T(8,128)S(1)}, u32[]{:S(2)}, u32[]{:S(2)}) collective-permute-start(f32[32,384]{1,0:T(8,128)S(1)} %get-tuple-element.48), channel_id=1, source_target_pairs={{0,2},{1,3},{2,0},{3,1},{4,6},{5,7},{6,4},{7,5},{8,10},{9,11},{10,... | collective-permute-start | bytes 147464 | tf_op jit(solution)/shard_map/kernel/ppermute | solution.py:24
  72.4 12.2 %collective-permute-start.40 = (bf16[256,512]{1,0:T(8,128)(2,1)S(1)}, bf16[256,512]{1,0:T(8,128)(2,1)S(1)}, u32[]{:S(2)}, u32[]{:S(2)}) collective-permute-start(bf16[256,512]{1,0:T(8,128)(2,1)S(1)} %get-tuple-element.47), channel_id=1, source_target_pairs={{0,16},{16,24},{24,8},{8,0},{1,17},{17,25},{25,9},{9,1},{2,18},{18... | collective-permute-start | bytes 786440 | tf_op jit(solution)/shard_map/grad_weight/ppermute | solution.py:34
  74.4 14.3 %collective-permute-start.41 = (bf16[256,512]{1,0:T(8,128)(2,1)S(1)}, bf16[256,512]{1,0:T(8,128)(2,1)S(1)}, u32[]{:S(2)}, u32[]{:S(2)}) collective-permute-start(bf16[256,512]{1,0:T(8,128)(2,1)S(1)} %get-tuple-element.46), channel_id=1, source_target_pairs={{0,24},{16,8},{24,0},{8,16},{1,25},{17,9},{25,1},{9,17},{2,26},{18... | collective-permute-start | bytes 786440 | tf_op jit(solution)/shard_map/grad_weight/ppermute | solution.py:34
  75.8 35.3 %collective-permute-start.42 = (bf16[256,512]{1,0:T(8,128)(2,1)S(1)}, bf16[256,512]{1,0:T(8,128)(2,1)S(1)}, u32[]{:S(2)}, u32[]{:S(2)}) collective-permute-start(bf16[256,512]{1,0:T(8,128)(2,1)S(1)} %get-tuple-element.45), channel_id=1, source_target_pairs={{0,8},{16,0},{24,16},{8,24},{1,9},{17,1},{25,17},{9,25},{2,10},{18... | collective-permute-start | bytes 786440 | tf_op jit(solution)/shard_map/grad_weight/ppermute | solution.py:34
  76.5 4.1 %collective-permute-start.17 = (f32[32,384]{1,0:T(8,128)S(1)}, f32[32,384]{1,0:T(8,128)S(1)}, u32[]{:S(2)}, u32[]{:S(2)}) collective-permute-start(f32[32,384]{1,0:T(8,128)S(1)} %get-tuple-element.50), channel_id=1, source_target_pairs={{0,4},{1,5},{2,6},{3,7},{4,0},{5,1},{6,2},{7,3},{8,12},{9,13},{10,... | collective-permute-start | bytes 147464 | tf_op jit(solution)/shard_map/kernel/ppermute | solution.py:24
  76.8 6.1 %collective-permute-start.18 = (f32[32,384]{1,0:T(8,128)S(1)}, f32[32,384]{1,0:T(8,128)S(1)}, u32[]{:S(2)}, u32[]{:S(2)}) collective-permute-start(f32[32,384]{1,0:T(8,128)S(1)} %get-tuple-element.49), channel_id=1, source_target_pairs={{0,6},{1,7},{2,4},{3,5},{4,2},{5,3},{6,0},{7,1},{8,14},{9,15},{10,... | collective-permute-start | bytes 147464 | tf_op jit(solution)/shard_map/kernel/ppermute | solution.py:24
  80.6 40.5 %collective-permute-start.29 = (bf16[256,1024]{1,0:T(8,128)(2,1)S(1)}, bf16[256,1024]{1,0:T(8,128)(2,1)S(1)}, u32[]{:S(2)}, u32[]{:S(2)}) collective-permute-start(bf16[256,1024]{1,0:T(8,128)(2,1)S(1)} %collective-permute-done.11.refs_2_.refs_10_), channel_id=1, source_target_pairs={{0,16},{16,24},{24,8},{8,0},{1,17},{17,25},{25,9},{9,1},{2,18},{18... | collective-permute-start | bytes 1572872 | tf_op jit(solution)/shard_map/z_ring/ppermute | solution.py:34
  82.8 38.3 %copy-start.5 = (bf16[256,1024]{1,0:T(8,128)(2,1)S(1)}, bf16[256,1024]{1,0:T(8,128)(2,1)}, u32[]{:S(2)}) copy-start(bf16[256,1024]{1,0:T(8,128)(2,1)} %copy-done.4) | copy-start | bytes 1572868
  83.5 28.7 %collective-permute-start.19 = (bf16[32,384]{1,0:T(8,128)(2,1)S(1)}, bf16[32,384]{1,0:T(8,128)(2,1)S(1)}, u32[]{:S(2)}, u32[]{:S(2)}) collective-permute-start(bf16[32,384]{1,0:T(8,128)(2,1)S(1)} %get-tuple-element.39), channel_id=1, source_target_pairs={{0,16},{16,24},{24,8},{8,0},{1,17},{17,25},{25,9},{9,1},{2,18},{18... | collective-permute-start | bytes 73736 | tf_op jit(solution)/shard_map/kernel/ppermute | solution.py:34
  84.6 27.5 %collective-permute-start.20 = (bf16[32,384]{1,0:T(8,128)(2,1)S(1)}, bf16[32,384]{1,0:T(8,128)(2,1)S(1)}, u32[]{:S(2)}, u32[]{:S(2)}) collective-permute-start(bf16[32,384]{1,0:T(8,128)(2,1)S(1)} %get-tuple-element.39), channel_id=1, source_target_pairs={{0,24},{16,8},{24,0},{8,16},{1,25},{17,9},{25,1},{9,17},{2,26},{18... | collective-permute-start | bytes 73736 | tf_op jit(solution)/shard_map/kernel/ppermute | solution.py:34
  88.7 23.5 %collective-permute-start.21 = (bf16[32,384]{1,0:T(8,128)(2,1)S(1)}, bf16[32,384]{1,0:T(8,128)(2,1)S(1)}, u32[]{:S(2)}, u32[]{:S(2)}) collective-permute-start(bf16[32,384]{1,0:T(8,128)(2,1)S(1)} %get-tuple-element.39), channel_id=1, source_target_pairs={{0,8},{16,0},{24,16},{8,24},{1,9},{17,1},{25,17},{9,25},{2,10},{18... | collective-permute-start | bytes 73736 | tf_op jit(solution)/shard_map/kernel/ppermute | solution.py:34
  112.2 22.2 %collective-permute-start.43 = (bf16[2,512,512]{2,1,0:T(8,128)(2,1)}, bf16[2,512,512]{2,1,0:T(8,128)(2,1)}, u32[]{:S(2)}, u32[]{:S(2)}) collective-permute-start(bf16[2,512,512]{2,1,0:T(8,128)(2,1)} %pad_maximum_fusion.2), channel_id=1, source_target_pairs={{0,1},{1,0},{2,3},{3,2},{4,5},{5,4},{6,7},{7,6},{8,9},{9,8},{10,11... | collective-permute-start | bytes 3145736 | tf_op jit(solution)/shard_map/grad_weight/ppermute | solution.py:24
  112.2 5.7 %collective-permute-start.23 = (bf16[4,32,384]{2,1,0:T(8,128)(2,1)S(1)}, bf16[4,32,384]{2,1,0:T(8,128)(2,1)S(1)}, u32[]{:S(2)}, u32[]{:S(2)}) collective-permute-start(bf16[4,32,384]{2,1,0:T(8,128)(2,1)S(1)} %pad_maximum_fusion.3.refs_0_), channel_id=1, source_target_pairs={{0,2},{1,3},{2,0},{3,1},{4,6},{5,7},{6,4},{7,5},{8,10},{9,11},{10,... | collective-permute-start | bytes 294920 | tf_op jit(solution)/shard_map/kernel/ppermute | solution.py:24
  112.6 5.3 %collective-permute-start.25 = (bf16[4,32,384]{2,1,0:T(8,128)(2,1)S(1)}, bf16[4,32,384]{2,1,0:T(8,128)(2,1)S(1)}, u32[]{:S(2)}, u32[]{:S(2)}) collective-permute-start(bf16[4,32,384]{2,1,0:T(8,128)(2,1)S(1)} %pad_maximum_fusion.3.refs_0_), channel_id=1, source_target_pairs={{0,4},{1,5},{2,6},{3,7},{4,0},{5,1},{6,2},{7,3},{8,12},{9,13},{10,... | collective-permute-start | bytes 294920 | tf_op jit(solution)/shard_map/kernel/ppermute | solution.py:24
  114.0 5.6 %collective-permute-start.27 = (bf16[4,32,384]{2,1,0:T(8,128)(2,1)S(1)}, bf16[4,32,384]{2,1,0:T(8,128)(2,1)S(1)}, u32[]{:S(2)}, u32[]{:S(2)}) collective-permute-start(bf16[4,32,384]{2,1,0:T(8,128)(2,1)S(1)} %pad_maximum_fusion.3.refs_0_), channel_id=1, source_target_pairs={{0,6},{1,7},{2,4},{3,5},{4,2},{5,3},{6,0},{7,1},{8,14},{9,15},{10,... | collective-permute-start | bytes 294920 | tf_op jit(solution)/shard_map/kernel/ppermute | solution.py:24
  117.9 1.8 %collective-permute-start.22 = (bf16[4,32,384]{2,1,0:T(8,128)(2,1)S(1)}, bf16[4,32,384]{2,1,0:T(8,128)(2,1)S(1)}, u32[]{:S(2)}, u32[]{:S(2)}) collective-permute-start(bf16[4,32,384]{2,1,0:T(8,128)(2,1)S(1)} %pad_maximum_fusion.3.refs_0_), channel_id=1, source_target_pairs={{0,1},{1,0},{2,3},{3,2},{4,5},{5,4},{6,7},{7,6},{8,9},{9,8},{10,11... | collective-permute-start | bytes 294920 | tf_op jit(solution)/shard_map/kernel/ppermute | solution.py:24
  117.9 2.4 %collective-permute-start.24 = (bf16[4,32,384]{2,1,0:T(8,128)(2,1)S(1)}, bf16[4,32,384]{2,1,0:T(8,128)(2,1)S(1)}, u32[]{:S(2)}, u32[]{:S(2)}) collective-permute-start(bf16[4,32,384]{2,1,0:T(8,128)(2,1)S(1)} %collective-permute-done.23.refs_2_), channel_id=1, source_target_pairs={{0,1},{1,0},{2,3},{3,2},{4,5},{5,4},{6,7},{7,6},{8,9},{9,8},{10,11... | collective-permute-start | bytes 294920 | tf_op jit(solution)/shard_map/kernel/ppermute | solution.py:24
  119.7 1.3 collective-permute-start.26
  119.7 1.5 collective-permute-start.28
  133.1 5.2 %collective-permute-start.36 = (bf16[4,256,512]{2,1,0:T(8,128)(2,1)}, bf16[4,256,512]{2,1,0:T(8,128)(2,1)S(1)}, u32[]{:S(2)}, u32[]{:S(2)}) collective-permute-start(bf16[4,256,512]{2,1,0:T(8,128)(2,1)} %d_act_matmul.3), channel_id=1, source_target_pairs={{0,1},{1,0},{2,3},{3,2},{4,5},{5,4},{6,7},{7,6},{8,9},{9,8},{10,11... | collective-permute-start | bytes 3145736 | tf_op jit(solution)/shard_map/d_act/ppermute | solution.py:24
  134.2 2.1 %collective-permute-start.30 = (f32[8,128]{1,0:T(8,128)S(1)}, f32[8,128]{1,0:T(8,128)S(1)}, u32[]{:S(2)}, u32[]{:S(2)}) collective-permute-start(f32[8,128]{1,0:T(8,128)S(1)} %broadcast_add_fusion), channel_id=1, source_target_pairs={{0,1},{1,0},{2,3},{3,2},{4,5},{5,4},{6,7},{7,6},{8,9},{9,8},{10,11... | collective-permute-start | bytes 12296 | tf_op jit(solution)/shard_map/loss/ppermute | solution.py:24
  136.2 11.5 %collective-permute-start.31 = (f32[8,128]{1,0:T(8,128)S(1)}, f32[8,128]{1,0:T(8,128)S(1)}, u32[]{:S(2)}, u32[]{:S(2)}) collective-permute-start(f32[8,128]{1,0:T(8,128)S(1)} %fusion.42), channel_id=1, source_target_pairs={{0,2},{1,3},{2,0},{3,1},{4,6},{5,7},{6,4},{7,5},{8,10},{9,11},{10,... | collective-permute-start | bytes 12296 | tf_op jit(solution)/shard_map/loss/ppermute | solution.py:24
  143.9 16.9 %collective-permute-start.37 = (bf16[256,512]{1,0:T(8,128)(2,1)S(1)}, bf16[256,512]{1,0:T(8,128)(2,1)S(1)}, u32[]{:S(2)}, u32[]{:S(2)}) collective-permute-start(bf16[256,512]{1,0:T(8,128)(2,1)S(1)} %get-tuple-element.25), channel_id=1, source_target_pairs={{0,2},{1,3},{2,0},{3,1},{4,6},{5,7},{6,4},{7,5},{8,10},{9,11},{10,... | collective-permute-start | bytes 786440 | tf_op jit(solution)/shard_map/d_act/ppermute | solution.py:24
  144.0 17.5 %collective-permute-start.38 = (bf16[256,512]{1,0:T(8,128)(2,1)S(1)}, bf16[256,512]{1,0:T(8,128)(2,1)S(1)}, u32[]{:S(2)}, u32[]{:S(2)}) collective-permute-start(bf16[256,512]{1,0:T(8,128)(2,1)S(1)} %get-tuple-element.26), channel_id=1, source_target_pairs={{0,4},{1,5},{2,6},{3,7},{4,0},{5,1},{6,2},{7,3},{8,12},{9,13},{10,... | collective-permute-start | bytes 786440 | tf_op jit(solution)/shard_map/d_act/ppermute | solution.py:24
  145.3 16.1 %collective-permute-start.39 = (bf16[256,512]{1,0:T(8,128)(2,1)S(1)}, bf16[256,512]{1,0:T(8,128)(2,1)S(1)}, u32[]{:S(2)}, u32[]{:S(2)}) collective-permute-start(bf16[256,512]{1,0:T(8,128)(2,1)S(1)} %get-tuple-element.27), channel_id=1, source_target_pairs={{0,6},{1,7},{2,4},{3,5},{4,2},{5,3},{6,0},{7,1},{8,14},{9,15},{10,... | collective-permute-start | bytes 786440 | tf_op jit(solution)/shard_map/d_act/ppermute | solution.py:24
  147.8 10.0 %collective-permute-start.32 = (f32[8,128]{1,0:T(8,128)S(1)}, f32[8,128]{1,0:T(8,128)S(1)}, u32[]{:S(2)}, u32[]{:S(2)}) collective-permute-start(f32[8,128]{1,0:T(8,128)S(1)} %add.238), channel_id=1, source_target_pairs={{0,4},{1,5},{2,6},{3,7},{4,0},{5,1},{6,2},{7,3},{8,12},{9,13},{10,... | collective-permute-start | bytes 12296 | tf_op jit(solution)/shard_map/loss/ppermute | solution.py:24
  157.8 8.7 %collective-permute-start.33 = (f32[8,128]{1,0:T(8,128)S(1)}, f32[8,128]{1,0:T(8,128)S(1)}, u32[]{:S(2)}, u32[]{:S(2)}) collective-permute-start(f32[8,128]{1,0:T(8,128)S(1)} %add.239), channel_id=1, source_target_pairs={{0,24},{8,0},{16,8},{24,16},{1,25},{9,1},{17,9},{25,17},{2,26},{10... | collective-permute-start | bytes 12296 | tf_op jit(solution)/shard_map/norm_backward/ppermute | solution.py:42
  160.3 6.2 %collective-permute-start.34 = (f32[8,128]{1,0:T(8,128)S(1)}, f32[8,128]{1,0:T(8,128)S(1)}, u32[]{:S(2)}, u32[]{:S(2)}) collective-permute-start(f32[8,128]{1,0:T(8,128)S(1)} %add.239), channel_id=1, source_target_pairs={{0,16},{8,24},{16,0},{24,8},{1,17},{9,25},{17,1},{25,9},{2,18},{10... | collective-permute-start | bytes 12296 | tf_op jit(solution)/shard_map/norm_backward/ppermute | solution.py:42
  160.8 5.7 %collective-permute-start.35 = (f32[8,128]{1,0:T(8,128)S(1)}, f32[8,128]{1,0:T(8,128)S(1)}, u32[]{:S(2)}, u32[]{:S(2)}) collective-permute-start(f32[8,128]{1,0:T(8,128)S(1)} %add.239), channel_id=1, source_target_pairs={{0,8},{8,16},{16,24},{24,0},{1,9},{9,17},{17,25},{25,1},{2,10},{10... | collective-permute-start | bytes 12296 | tf_op jit(solution)/shard_map/norm_backward/ppermute | solution.py:42
  162.1 4.9 %collective-permute-start.44 = (f32[4,512]{1,0:T(4,128)S(1)}, f32[4,512]{1,0:T(4,128)S(1)}, u32[]{:S(2)}, u32[]{:S(2)}) collective-permute-start(f32[4,512]{1,0:T(4,128)S(1)} %pad_maximum_fusion.5), channel_id=1, source_target_pairs={{0,24},{8,0},{16,8},{24,16},{1,25},{9,1},{17,9},{25,17},{2,26},{10... | collective-permute-start | bytes 24584 | tf_op jit(solution)/shard_map/norm_backward/ppermute | solution.py:42
  165.4 4.5 %collective-permute-start.45 = (f32[4,512]{1,0:T(4,128)S(1)}, f32[4,512]{1,0:T(4,128)S(1)}, u32[]{:S(2)}, u32[]{:S(2)}) collective-permute-start(f32[4,512]{1,0:T(4,128)S(1)} %pad_maximum_fusion.5), channel_id=1, source_target_pairs={{0,16},{8,24},{16,0},{24,8},{1,17},{9,25},{17,1},{25,9},{2,18},{10... | collective-permute-start | bytes 24584 | tf_op jit(solution)/shard_map/norm_backward/ppermute | solution.py:42
  166.5 5.4 %collective-permute-start.46 = (f32[4,512]{1,0:T(4,128)S(1)}, f32[4,512]{1,0:T(4,128)S(1)}, u32[]{:S(2)}, u32[]{:S(2)}) collective-permute-start(f32[4,512]{1,0:T(4,128)S(1)} %pad_maximum_fusion.5), channel_id=1, source_target_pairs={{0,8},{8,16},{16,24},{24,0},{1,9},{9,17},{17,25},{25,1},{2,10},{10... | collective-permute-start | bytes 24584 | tf_op jit(solution)/shard_map/norm_backward/ppermute | solution.py:42
  (13 other events, 138.9 us)

commit v3 on v2

--- a/solution.py
+++ b/solution.py
@@ -67,7 +67,7 @@
     before = None if first else rest.pop(0)
     i = pl.program_id(0)
     if last:
-        z_ref, sum_ref, total = rest
+        z0_ref, z1_ref, sum_ref, total = rest
     else:
         (total,) = rest
 
@@ -75,7 +75,7 @@
 
         @pl.when(i == j)
         def _():
-            part = jnp.dot(pieces[j][...], w_ref[0], preferred_element_type=f32)
+            part = jnp.dot(pieces[j][...], w_ref[...], preferred_element_type=f32)
             if j > 0:
                 total[...] += part
             elif first:
@@ -88,30 +88,31 @@
         @pl.when(i == count - 1)
         def _():
             z = total[...].astype(bf16)
-            z_ref[...] = z
-            zf = z.astype(f32)
-            half = zf.shape[0] // 2
-            sum_ref[0:1, :] = jnp.sum(zf[:half], axis=0, keepdims=True)
-            sum_ref[1:2, :] = jnp.sum(zf[half:], axis=0, keepdims=True)
-
-
-def z_call(index, pieces, blocks, before, last):
+            half = z.shape[0] // 2
+            for v, ref in enumerate((z0_ref, z1_ref)):
+                mine = z[v * half : (v + 1) * half]
+                ref[...] = mine
+                sum_ref[v : v + 1, :] = jnp.sum(mine.astype(f32), axis=0, keepdims=True)
+
+
+def z_call(index, pieces, weight, before, last):
     count = len(pieces)
     rows, width = pieces[0].shape
-    columns = blocks.shape[2]
+    columns = weight.shape[1]
     in_specs = [whole((rows, width)) for _ in pieces]
-    in_specs.append(pl.BlockSpec((1, width, columns), lambda i, index: (index[i], 0, 0)))
-    operands = list(pieces) + [blocks]
+    in_specs.append(pl.BlockSpec((width, columns), lambda i, index: (index[i], 0)))
+    operands = list(pieces) + [weight]
     if before is not None:
         in_specs.append(whole((rows, columns)))
         operands.append(before)
     scratch = []
     if last:
         out_shape = (
-            jax.ShapeDtypeStruct((rows, columns), bf16),
+            jax.ShapeDtypeStruct((rows // 2, columns), bf16),
+            jax.ShapeDtypeStruct((rows // 2, columns), bf16),
             jax.ShapeDtypeStruct((2, columns), f32),
         )
-        out_specs = (whole((rows, columns)), whole((2, columns)))
+        out_specs = (whole((rows // 2, columns)), whole((rows // 2, columns)), whole((2, columns)))
         scratch = [pltpu.VMEM((rows, columns), f32)]
     else:
         out_shape = jax.ShapeDtypeStruct((rows, columns), f32)
@@ -135,13 +136,13 @@
 
 
 def strip_kernel(n_slots, n_sums, rows, n_col, index_ref, *refs):
-    z_refs, sum_refs = refs[:n_slots], refs[n_slots : n_slots + n_sums]
-    even_ref, odd_ref, strip = refs[n_slots + n_sums :]
-    local_rows = z_refs[0].shape[0] // 2
+    z_refs, sum_refs = refs[: 2 * n_slots], refs[2 * n_slots : 2 * n_slots + n_sums]
+    even_ref, odd_ref, strip = refs[2 * n_slots + n_sums :]
+    local_rows = z_refs[0].shape[0]
     mean = sum(s[...] for s in sum_refs) / rows
     for v in range(2):
         here = pl.ds(v * local_rows, local_rows)
-        rounded = [(z[here, :].astype(f32) - mean[v : v + 1]).astype(bf16) for z in z_refs]
+        rounded = [(z[...].astype(f32) - mean[v : v + 1]).astype(bf16) for z in z_refs[v::2]]
         for u in range(n_slots):
             strip[here, pl.ds(u * local_rows, local_rows)] = lax.dot_general(
                 rounded[0], rounded[u], (((1,), (1,)), ((), ())), preferred_element_type=f32
@@ -153,10 +154,12 @@
 
 
 def strip_call(index, z_slots, sums, rows, n_col):
-    tall, columns = z_slots[0].shape
-    wide = len(z_slots) * tall // 2
+    local_rows, columns = z_slots[0][0].shape
+    tall = 2 * local_rows
+    wide = len(z_slots) * local_rows
     part = jax.ShapeDtypeStruct((n_col // 2, tall // n_col, wide), f32)
-    specs = [whole((tall, columns)) for _ in z_slots] + [whole((2, columns)) for _ in sums]
+    operands = [z for slot in z_slots for z in slot] + list(sums)
+    specs = [whole(x.shape) for x in operands]
     return pl.pallas_call(
         functools.partial(strip_kernel, len(z_slots), len(sums), rows, n_col),
         out_shape=(part, part),
@@ -170,14 +173,14 @@
         compiler_params=params(),
         cost_estimate=cost(2 * tall * wide * columns, 2 * tall * columns * len(z_slots)),
         name="kernel_strip",
-    )(index, *z_slots, *sums)
+    )(index, *operands)
 
 
 def dz_kernel(n_batch, n_col, coef, hinge_coef, inv_coef, inv_share, hinge_share, diag_share, index_ref, *refs):
     strip_refs = refs[:n_col]
-    z_refs = refs[n_col : n_col + n_batch]
-    dz_ref, share_ref, strips, full, centred = refs[n_col + n_batch :]
-    local_rows = z_refs[0].shape[0] // 2
+    z_refs = refs[n_col : n_col + 2 * n_batch]
+    dz_ref, share_ref, strips, full, centred = refs[n_col + 2 * n_batch :]
+    local_rows = z_refs[0].shape[0]
     rows = local_rows * n_batch
     reach = n_batch // 2
 
@@ -202,9 +205,7 @@
     grads = []
     z_views = []
     for v in range(2):
-        zf = jnp.concatenate(
-            [z[pl.ds(v * local_rows, local_rows), :].astype(f32) for z in z_refs], axis=0
-        )
+        zf = jnp.concatenate([z[...].astype(f32) for z in z_refs[v::2]], axis=0)
         z_views.append(zf)
         zc = zf - jnp.sum(zf, axis=0, keepdims=True) / rows
         std = jnp.sqrt(jnp.sum(zc * zc, axis=0, keepdims=True) / (rows - 1) + eps_std)
@@ -227,8 +228,9 @@
 
 def dz_call(index, strips, z_slots, constants):
     n_col, n_batch = len(strips), len(z_slots)
-    tall, columns = z_slots[0].shape
-    rows = tall // 2 * n_batch
+    local_rows, columns = z_slots[0][0].shape
+    tall = 2 * local_rows
+    rows = local_rows * n_batch
     tile = min(256, columns)
     part = strips[0].shape
     return pl.pallas_call(
@@ -241,7 +243,7 @@
             num_scalar_prefetch=1,
             grid=(columns // tile,),
             in_specs=[whole(part) for _ in strips]
-            + [pl.BlockSpec((tall, tile), lambda j, index: (0, j)) for _ in z_slots],
+            + [pl.BlockSpec((local_rows, tile), lambda j, index: (0, j)) for _ in range(2 * n_batch)],
             out_specs=(
                 pl.BlockSpec((2, rows, tile), lambda j, index: (0, 0, j)),
                 whole((8, 128)),
@@ -255,59 +257,47 @@
         compiler_params=params(),
         cost_estimate=cost(4 * rows * rows * columns, 8 * rows * columns),
         name="embedding_gradient",
-    )(index, *strips, *z_slots)
+    )(index, *strips, *[z for slot in z_slots for z in slot])
 
 
 def d_act_kernel(count, adds, index_ref, dz_ref, w_ref, *refs):
     i = pl.program_id(0)
-    outs = refs[1:] if adds else refs
     two, local_rows, columns = dz_ref.shape
-    dz = dz_ref[...].reshape(two * local_rows, columns)
-    part = lax.dot_general(dz, w_ref[0], (((1,), (1,)), ((), ())), preferred_element_type=f32)
-    if adds:
-        part = part + refs[0][0].astype(f32)
+    part = lax.dot_general(
+        dz_ref[...].reshape(two * local_rows, columns),
+        w_ref[...],
+        (((1,), (1,)), ((), ())),
+        preferred_element_type=f32,
+    )
+    if not adds:
+        refs[0][0] = part.astype(refs[0].dtype)
+        return
+    part = part + refs[0][0].astype(f32)
     for j in range(count):
 
         @pl.when(i == j)
         def _():
-            outs[j][...] = part.astype(outs[j].dtype)
-
-
-def d_act_call(index, dz, blocks, local_rows, ks, got, kind):
-    count = len(ks)
-    _, width, columns = blocks.shape
+            refs[j + 1][...] = part.astype(refs[j + 1].dtype)
+
+
+def d_act_call(index, dz, weight, local_rows, width, got, first, count, kind):
+    columns = weight.shape[1]
     tall = 2 * local_rows
     in_specs = [
         pl.BlockSpec((2, local_rows, columns), lambda i, index: (0, 0, 0)),
-        pl.BlockSpec((1, width, columns), lambda i, index: (index[i], 0, 0)),
+        pl.BlockSpec((width, columns), lambda i, index: (index[i], 0)),
     ]
-    operands = [dz, blocks]
-    if got is not None:
-        first = ks[0] // 2
-        in_specs.append(pl.BlockSpec((1, tall, width), lambda i, index: (first + i, 0, 0)))
-        operands.append(got)
+    operands = [dz, weight]
     if got is None:
         out_shape = (jax.ShapeDtypeStruct((count, tall, width), kind),)
         out_specs = (pl.BlockSpec((1, tall, width), lambda i, index: (i, 0, 0)),)
     else:
-        out_shape = tuple(jax.ShapeDtypeStruct((tall, width), kind) for _ in ks)
-        out_specs = tuple(whole((tall, width)) for _ in ks)
-
-    def body(index_ref, dz_ref, w_ref, *refs):
-        if got is None:
-            d_act_kernel(1, False, index_ref, dz_ref, w_ref, *refs)
-        else:
-            d_act_kernel(count, True, index_ref, dz_ref, w_ref, *refs)
-
-    def body_stacked(index_ref, dz_ref, w_ref, out_ref):
-        two, r, n = dz_ref.shape
-        part = lax.dot_general(
-            dz_ref[...].reshape(two * r, n), w_ref[0], (((1,), (1,)), ((), ())), preferred_element_type=f32
-        )
-        out_ref[0] = part.astype(out_ref.dtype)
-
+        in_specs.append(pl.BlockSpec((1, tall, width), lambda i, index: (first + i, 0, 0)))
+        operands.append(got)
+        out_shape = (jax.ShapeDtypeStruct((tall, width), kind),) * count
+        out_specs = (whole((tall, width)),) * count
     return pl.pallas_call(
-        body_stacked if got is None else body,
+        functools.partial(d_act_kernel, count, got is not None),
         out_shape=out_shape,
         grid_spec=pltpu.PrefetchScalarGridSpec(
             num_scalar_prefetch=1, grid=(count,), in_specs=in_specs, out_specs=out_specs
@@ -357,7 +347,7 @@
     denom = float((rows - 1) ** 2 * E)
     evens = list(range(0, n_col, 2))
     far = evens[1:]
-    blocks = weight.reshape(n_col, width, columns)
+    blocks = pltpu.with_memory_space_constraint(weight, pltpu.HBM)
 
     def places(ks):
         return jnp.stack([c ^ k for k in ks]).astype(jnp.int32)
@@ -385,12 +375,12 @@
         z = z_call(places([0, 1]), [pieces[0], pieces[1]], blocks, None, False)
         z = z_call(places(far), [pieces[k] for k in far], blocks, z, False)
         odd = [k + 1 for k in far]
-        z, z_sum = z_call(places(odd), [pieces[k] for k in odd], blocks, z, True)
+        *z, z_sum = z_call(places(odd), [pieces[k] for k in odd], blocks, z, True)
     with jax.named_scope("z_ring"):
         sums = [z_sum] + [ring_send(z_sum, "batch", d) for d in range(1, n_batch)]
         slots = [z]
         for _ in range(1, n_batch):
-            slots.append(ring_send(slots[-1], "batch", 1))
+            slots.append([ring_send(x, "batch", 1) for x in slots[-1]])
     with jax.named_scope("kernel"):
         reach = n_batch // 2
         everyone = places(range(n_col))
@@ -404,6 +394,7 @@
         block_share = jnp.sum(strip * strip * twice) / denom
         mine = strip.astype(bf16)
         mine = jnp.stack([mine] + [ring_send(mine, "batch", d) for d in range(1, n_batch)])
+        mine, held_back = lax.optimization_barrier((mine, [pieces[k] for k in evens]))
         strips = {0: mine}
         for k in far:
             strips[k] = xor_send(mine, "col", k)
@@ -420,17 +411,19 @@
         )
         dz, share = dz_call(everyone, [strips[k] for k in range(n_col)], slots, constants)
     with jax.named_scope("d_act"):
-        odds = [k + 1 for k in evens]
-        (away,) = d_act_call(places(odds), dz, blocks, local_rows, odds, None, bf16)
+        half = len(evens)
+        (away,) = d_act_call(
+            places([k + 1 for k in evens]), dz, blocks, local_rows, width, None, 0, half, bf16
+        )
         got = xor_send(away, "col", 1)
-        sends = d_act_call(places(far), dz, blocks, local_rows, far, got, bf16)
+        sends = d_act_call(places(far), dz, blocks, local_rows, width, got, 1, half - 1, bf16)
         arrived = [xor_send(part, "col", k) for k, part in zip(far, sends)]
-        (d_act,) = d_act_call(places([0]), dz, blocks, local_rows, [0], got, f32)
+        (d_act,) = d_act_call(places([0]), dz, blocks, local_rows, width, got, 0, 1, f32)
     with jax.named_scope("grad_weight"):
         per_plane = n_col // n_batch
         order = jnp.array(ring_order(n_batch), jnp.int32)
         position = jnp.where(b % 2 == 0, b // 2, n_batch - 1 - b // 2)
-        stacked = jnp.stack([pieces[k] for k in evens])
+        stacked = jnp.stack(held_back)
 
         def held(plane, i):
             k = (per_plane * plane + 2 * i) ^ (c - c % 2)
@@ -460,11 +453,16 @@
         for part in arrived:
             d_act = d_act + part.astype(f32)
         d_pre = d_act.reshape(n_view, local_rows, width) * gelu_slope(preactivation)
-        sums = jnp.concatenate([jnp.sum(d_pre, axis=1), jnp.sum(d_pre * normalised, axis=1)])
-        last = exchange(sums, "batch")
-        loss = sum(exchange(share, "batch"))[0, 0]
-        both = sum(last)
-        sum_b, sum_g = both[:n_view], both[n_view:]
+        sums = jnp.concatenate(
+            [
+                jnp.sum(d_pre, axis=1),
+                jnp.sum(d_pre * normalised, axis=1),
+                jnp.broadcast_to(share[:1, :1], (2 * n_view, width)),
+            ]
+        )
+        both = sum(exchange(sums, "batch"))
+        sum_b, sum_g = both[:n_view], both[n_view : 2 * n_view]
+        loss = jnp.max(both[2 * n_view :])
         grad_bias = jnp.sum(sum_b, axis=0)
         grad_gain = jnp.sum(sum_g, axis=0)
         views_gradient = (

time: 174 us -> 163 us (0.937)
  Pallas kernels: 22.2 us -> 32.6 us
  local copies, waits for them, and re-layouts: 12.7 us -> 2.41 us
  waiting for transfers between devices: 73.1 us -> 64.9 us
  starting transfers between devices: 53.8 us -> 51 us
    unnamed x28 -> x30, local copies, waits for them, and re-layouts: 12 us -> 1.01 us
    ppermute x12 -> x15, waiting for transfers between devices: 40.7 us -> 33.2 us  [ring_send(): lax.ppermute(x, axis, [(order[i], order[(i + d) % n]) for i in range(n)])]
    ppermute x9 -> x6, starting transfers between devices: 13.7 us -> 8.13 us  [exchange(): slots.append(lax.ppermute(x, axis, [(i, (i + d) % n) for i in range(n)]))]
    pallas_call x3, Pallas kernels: 6.05 us -> 11.2 us  [d_act_call(): pl.pallas_call(functools.partial(d_act_kernel, count, got is not None), o...]
    pallas_call x3, Pallas kernels: 5.47 us -> 10.6 us  [z_call(): pl.pallas_call(functools.partial(z_kernel, count, before is None, last),...]
    ppermute x12 -> x15, starting transfers between devices: 21.4 us -> 23.5 us  [ring_send(): lax.ppermute(x, axis, [(order[i], order[(i + d) % n]) for i in range(n)])]
    ppermute x9 -> x6, waiting for transfers between devices: 9.33 us -> 8.68 us  [exchange(): slots.append(lax.ppermute(x, axis, [(i, (i + d) % n) for i in range(n)]))]
  transfers between devices with their start and end apart: 47 -> 47, of which waited for: 20 -> 26; matrix products, arithmetic and copies ran while one was open for 3% -> 3% of each run, Pallas kernels for 11% -> 17%
where the time goes in v3:
time: 163 us
  waiting for transfers between devices  64.9 us (40%)
  starting transfers between devices  51 us (31%)
  Pallas kernels  32.6 us (20%)
  other arithmetic  10.3 us (6%)
  local copies, waits for them, and re-layouts  2.41 us (1%)
  between operations  1.67 us (1%)
    ppermute x15, waiting for transfers between devices, ring_send(): lax.ppermute(x, axis, [(order[i], order[(i + d) % n]) for i in range(n)])  33.2 us
    ppermute x15, starting transfers between devices, ring_send(): lax.ppermute(x, axis, [(order[i], order[(i + d) % n]) for i in range(n)])  23.5 us
    ppermute x26, waiting for transfers between devices, xor_send(): return lax.ppermute(x, axis, [(i, i ^ k) for i in range(n)])  23.1 us
    ppermute x26, starting transfers between devices, xor_send(): return lax.ppermute(x, axis, [(i, i ^ k) for i in range(n)])  19.4 us
    pallas_call x3, Pallas kernels, d_act_call(): pl.pallas_call(functools.partial(d_act_kernel, count, got is not None), o...  11.2 us
    pallas_call x3, Pallas kernels, z_call(): pl.pallas_call(functools.partial(z_kernel, count, before is None, last),...  10.6 us
    ppermute x6, waiting for transfers between devices, exchange(): slots.append(lax.ppermute(x, axis, [(i, (i + d) % n) for i in range(n)]))  8.68 us
    ppermute x6, starting transfers between devices, exchange(): slots.append(lax.ppermute(x, axis, [(i, (i + d) % n) for i in range(n)]))  8.13 us
  transfers between devices with their start and end apart: 47, of which 26 were waited for; matrix products, arithmetic and copies ran while one was open for 3% of the time, Pallas kernels for 17%

profile of v3, /device:TPU:0, one launch (start us, length us, event | category | flops | bytes accessed | tf_op | source)
XLA Modules:
  0.0 162.9 jit_solution(6002228298094580980)
XLA Ops:
  2.7 5.1 %collective-permute-start = (f32[4,512]{1,0:T(4,128)S(1)}, f32[4,512]{1,0:T(4,128)S(1)}, u32[]{:S(2)}, u32[]{:S(2)}) collective-permute-start(f32[4,512]{1,0:T(4,128)S(1)} %pad_maximum_fusion.4), channel_id=1, source_target_pairs={{0,24},{8,0},{16,8},{24,16},{1,25},{9,1},{17,9},{25,17},{2,26},{10... | collective-permute-start | bytes 24584 | tf_op jit(solution)/shard_map/norm_stats/ppermute | solution.py:42
  9.2 3.2 %collective-permute-done.1 = f32[4,512]{1,0:T(4,128)S(1)} collective-permute-done((f32[4,512]{1,0:T(4,128)S(1)}, f32[4,512]{1,0:T(4,128)S(1)}, u32[]{:S(2)}, u32[]{:S(2)}) %collective-permute-start.1) | collective-permute-done | bytes 8224 | tf_op jit(solution)/shard_map/norm_stats/ppermute | solution.py:42
  13.3 1.2 fusion.17
  14.6 1.6 collective-permute-start.3
  16.1 1.5 collective-permute-start.5
  18.1 5.8 %collective-permute-done.3.refs_0_ = bf16[256,512]{1,0:T(8,128)(2,1)S(1)} collective-permute-done((bf16[256,512]{1,0:T(8,128)(2,1)S(1)}, bf16[256,512]{1,0:T(8,128)(2,1)S(1)}, u32[]{:S(2)}, u32[]{:S(2)}) %collective-permute-start.3) | collective-permute-done | bytes 262176 | tf_op jit(solution)/shard_map/act_gather/ppermute | solution.py:24
  23.9 4.2 %collective-permute-done.5.refs_1_ = bf16[256,512]{1,0:T(8,128)(2,1)S(1)} collective-permute-done((bf16[256,512]{1,0:T(8,128)(2,1)S(1)}, bf16[256,512]{1,0:T(8,128)(2,1)S(1)}, u32[]{:S(2)}, u32[]{:S(2)}) %collective-permute-start.5) | collective-permute-done | bytes 262176 | tf_op jit(solution)/shard_map/act_gather/ppermute | solution.py:24
  28.7 2.7 %z_matmul.3.refs_4_ = f32[256,1024]{1,0:T(8,128)S(1)} custom-call(s32[2]{0:T(128)S(1)} %pad_add_fusion.2.index_ref, bf16[256,512]{1,0:T(8,128)(2,1)S(1)} %bitcast.53, bf16[256,512]{1,0:T(8,128)(2,1)S(1)} %collective-permute-done.9.refs_1_, bf16[4096,1024]{1,0:T(8,128)(2,1)} %w_ref.5), custom_call_target="tpu_custom_call" | custom-call | flops 536870912 | bytes 2621440 | tf_op jit(solution)/shard_map/z/z_matmul/pallas_call | solution.py:120
  31.5 3.9 %z_matmul.4.refs_4_ = f32[256,1024]{1,0:T(8,128)S(1)} custom-call(s32[3]{0:T(128)S(1)} %get-tuple-element.68.index_ref, bf16[256,512]{1,0:T(8,128)(2,1)S(1)} %collective-permute-done.3.refs_0_, bf16[256,512]{1,0:T(8,128)(2,1)S(1)} %collective-permute-done.5.refs_1_, bf16[256,512]{1,0:T(8,128)(2,1)S(1)} %collective-permute-done.7.refs_2_, ...), custom_call_target="tpu_custom_call" | custom-call | flops 805306368 | bytes 3932160 | tf_op jit(solution)/shard_map/z/z_matmul/pallas_call | solution.py:120
  35.4 4.0 %z_matmul.5 = (bf16[128,1024]{1,0:T(8,128)(2,1)S(1)}, bf16[128,1024]{1,0:T(8,128)(2,1)S(1)}, f32[2,1024]{1,0:T(2,128)S(1)}) custom-call(s32[3]{0:T(128)S(1)} %get-tuple-element.69.index_ref, bf16[256,512]{1,0:T(8,128)(2,1)S(1)} %collective-permute-done.4.refs_0_, bf16[256,512]{1,0:T(8,128)(2,1)S(1)} %collective-permute-done.6.refs_1_, ...), custom_call_target="tpu_custom_call" | custom-call | flops 805306368 | bytes 3932160 | tf_op jit(solution)/shard_map/z/z_matmul/pallas_call | solution.py:120
  40.9 7.7 %collective-permute-done.10.refs_2_.refs_10_ = bf16[128,1024]{1,0:T(8,128)(2,1)S(1)} collective-permute-done((bf16[128,1024]{1,0:T(8,128)(2,1)S(1)}, bf16[128,1024]{1,0:T(8,128)(2,1)S(1)}, u32[]{:S(2)}, u32[]{:S(2)}) %collective-permute-start.10) | collective-permute-done | bytes 262176 | tf_op jit(solution)/shard_map/z_ring/ppermute | solution.py:34
  48.6 1.8 %collective-permute-start.12 = (bf16[128,1024]{1,0:T(8,128)(2,1)S(1)}, bf16[128,1024]{1,0:T(8,128)(2,1)S(1)}, u32[]{:S(2)}, u32[]{:S(2)}) collective-permute-start(bf16[128,1024]{1,0:T(8,128)(2,1)S(1)} %collective-permute-done.10.refs_2_.refs_10_), channel_id=1, source_target_pairs={{0,16},{16,24},{24,8},{8,0},{1,17},{17,25},{25,9},{9,1},{2,18},{18... | collective-permute-start | bytes 786440 | tf_op jit(solution)/shard_map/z_ring/ppermute | solution.py:34
  50.4 3.8 %collective-permute-done.11.refs_3_.refs_11_ = bf16[128,1024]{1,0:T(8,128)(2,1)S(1)} collective-permute-done((bf16[128,1024]{1,0:T(8,128)(2,1)S(1)}, bf16[128,1024]{1,0:T(8,128)(2,1)S(1)}, u32[]{:S(2)}, u32[]{:S(2)}) %collective-permute-start.11) | collective-permute-done | bytes 262176 | tf_op jit(solution)/shard_map/z_ring/ppermute | solution.py:34
  54.2 1.8 %collective-permute-start.13 = (bf16[128,1024]{1,0:T(8,128)(2,1)S(1)}, bf16[128,1024]{1,0:T(8,128)(2,1)S(1)}, u32[]{:S(2)}, u32[]{:S(2)}) collective-permute-start(bf16[128,1024]{1,0:T(8,128)(2,1)S(1)} %collective-permute-done.11.refs_3_.refs_11_), channel_id=1, source_target_pairs={{0,16},{16,24},{24,8},{8,0},{1,17},{17,25},{25,9},{9,1},{2,18},{18... | collective-permute-start | bytes 786440 | tf_op jit(solution)/shard_map/z_ring/ppermute | solution.py:34
  56.1 2.6 %collective-permute-start.15 = (f32[2,1024]{1,0:T(2,128)S(1)}, f32[2,1024]{1,0:T(2,128)S(1)}, u32[]{:S(2)}, u32[]{:S(2)}) collective-permute-start(f32[2,1024]{1,0:T(2,128)S(1)} %get-tuple-element.27.refs_6_), channel_id=1, source_target_pairs={{0,24},{16,8},{24,0},{8,16},{1,25},{17,9},{25,1},{9,17},{2,26},{18... | collective-permute-start | bytes 24584 | tf_op jit(solution)/shard_map/z_ring/ppermute | solution.py:34
  58.7 6.3 %collective-permute-done.14.refs_7_ = f32[2,1024]{1,0:T(2,128)S(1)} collective-permute-done((f32[2,1024]{1,0:T(2,128)S(1)}, f32[2,1024]{1,0:T(2,128)S(1)}, u32[]{:S(2)}, u32[]{:S(2)}) %collective-permute-start.14) | collective-permute-done | bytes 8224 | tf_op jit(solution)/shard_map/z_ring/ppermute | solution.py:34
  65.1 1.2 kernel_strip.1
  66.3 1.4 collective-permute-done.17
  67.8 1.3 collective-permute-start.18
  69.9 1.4 collective-permute-start.20
  72.0 1.8 %collective-permute-done.19 = f32[32,384]{1,0:T(8,128)S(1)} collective-permute-done((f32[32,384]{1,0:T(8,128)S(1)}, f32[32,384]{1,0:T(8,128)S(1)}, u32[]{:S(2)}, u32[]{:S(2)}) %collective-permute-start.19) | collective-permute-done | bytes 49184 | tf_op jit(solution)/shard_map/kernel/ppermute | solution.py:24
  73.7 1.2 collective-permute-done.20
  75.5 1.9 %collective-permute-start.21 = (bf16[32,384]{1,0:T(8,128)(2,1)S(1)}, bf16[32,384]{1,0:T(8,128)(2,1)S(1)}, u32[]{:S(2)}, u32[]{:S(2)}) collective-permute-start(bf16[32,384]{1,0:T(8,128)(2,1)S(1)} %get-tuple-element.50), channel_id=1, source_target_pairs={{0,16},{16,24},{24,8},{8,0},{1,17},{17,25},{25,9},{9,1},{2,18},{18... | collective-permute-start | bytes 73736 | tf_op jit(solution)/shard_map/kernel/ppermute | solution.py:34
  77.4 1.4 collective-permute-start.22
  79.5 2.2 %collective-permute-start.31 = (bf16[128,1024]{1,0:T(8,128)(2,1)S(1)}, bf16[128,1024]{1,0:T(8,128)(2,1)S(1)}, u32[]{:S(2)}, u32[]{:S(2)}) collective-permute-start(bf16[128,1024]{1,0:T(8,128)(2,1)S(1)} %collective-permute-done.12.refs_4_.refs_12_), channel_id=1, source_target_pairs={{0,16},{16,24},{24,8},{8,0},{1,17},{17,25},{25,9},{9,1},{2,18},{18... | collective-permute-start | bytes 786440 | tf_op jit(solution)/shard_map/z_ring/ppermute | solution.py:34
  81.8 1.4 collective-permute-done.22
  83.8 1.6 collective-permute-start.25
  85.9 1.5 collective-permute-start.29
  87.5 1.7 %collective-permute-done.31.refs_14_ = bf16[128,1024]{1,0:T(8,128)(2,1)S(1)} collective-permute-done((bf16[128,1024]{1,0:T(8,128)(2,1)S(1)}, bf16[128,1024]{1,0:T(8,128)(2,1)S(1)}, u32[]{:S(2)}, u32[]{:S(2)}) %collective-permute-start.31) | collective-permute-done | bytes 262176 | tf_op jit(solution)/shard_map/z_ring/ppermute | solution.py:34
  89.8 2.5 %collective-permute-done.32.refs_15_ = bf16[128,1024]{1,0:T(8,128)(2,1)S(1)} collective-permute-done((bf16[128,1024]{1,0:T(8,128)(2,1)S(1)}, bf16[128,1024]{1,0:T(8,128)(2,1)S(1)}, u32[]{:S(2)}, u32[]{:S(2)}) %collective-permute-start.32) | collective-permute-done | bytes 262176 | tf_op jit(solution)/shard_map/z_ring/ppermute | solution.py:34
  92.3 2.4 %collective-permute-start.37 = (bf16[256,512]{1,0:T(8,128)(2,1)S(1)}, bf16[256,512]{1,0:T(8,128)(2,1)S(1)}, u32[]{:S(2)}, u32[]{:S(2)}) collective-permute-start(bf16[256,512]{1,0:T(8,128)(2,1)S(1)} %get-tuple-element.59), channel_id=1, source_target_pairs={{0,16},{16,24},{24,8},{8,0},{1,17},{17,25},{25,9},{9,1},{2,18},{18... | collective-permute-start | bytes 786440 | tf_op jit(solution)/shard_map/grad_weight/ppermute | solution.py:34
  94.8 7.2 %collective-permute-start.38 = (bf16[256,512]{1,0:T(8,128)(2,1)S(1)}, bf16[256,512]{1,0:T(8,128)(2,1)S(1)}, u32[]{:S(2)}, u32[]{:S(2)}) collective-permute-start(bf16[256,512]{1,0:T(8,128)(2,1)S(1)} %get-tuple-element.58), channel_id=1, source_target_pairs={{0,24},{16,8},{24,0},{8,16},{1,25},{17,9},{25,1},{9,17},{2,26},{18... | collective-permute-start | bytes 786440 | tf_op jit(solution)/shard_map/grad_weight/ppermute | solution.py:34
  104.4 5.2 %embedding_gradient.1 = (bf16[2,512,1024]{2,1,0:T(8,128)(2,1)S(1)}, f32[8,128]{1,0:T(8,128)S(1)}) custom-call(s32[8]{0:T(128)S(1)} %stack.95.index_ref, bf16[4,32,384]{2,1,0:T(8,128)(2,1)S(1)} %pad_maximum_fusion.3.refs_0_, bf16[4,32,384]{2,1,0:T(8,128)(2,1)S(1)} %collective-permute-done.24.refs_1_, bf16[4,32,384]{2,1,0:T(8,128)(2,1)S(1)} %collective-permute-done.25.refs_2_, ...), custom_call_target="tpu_custom_call" | custom-call | flops 1073741824 | bytes 4194304 | tf_op jit(solution)/shard_map/dz/embedding_gradient/pallas_call | solution.py:236
  109.7 5.4 %d_act_matmul.3 = bf16[4,256,512]{2,1,0:T(8,128)(2,1)} custom-call(s32[4]{0:T(128)S(1)} %pad_add_fusion.3.index_ref, bf16[2,512,1024]{2,1,0:T(8,128)(2,1)S(1)} %get-tuple-element.31.dz_ref, bf16[4096,1024]{1,0:T(8,128)(2,1)} %w_ref.5), custom_call_target="tpu_custom_call" | custom-call | flops 1073741824 | bytes 5242880 | tf_op jit(solution)/shard_map/d_act/d_act_matmul/pallas_call | solution.py:299
  115.5 9.0 %collective-permute-done.39 = bf16[256,512]{1,0:T(8,128)(2,1)S(1)} collective-permute-done((bf16[256,512]{1,0:T(8,128)(2,1)S(1)}, bf16[256,512]{1,0:T(8,128)(2,1)S(1)}, u32[]{:S(2)}, u32[]{:S(2)}) %collective-permute-start.39) | collective-permute-done | bytes 262176 | tf_op jit(solution)/shard_map/grad_weight/ppermute | solution.py:34
  126.8 1.4 collective-permute-done.41
  128.3 1.4 collective-permute-start.42
  129.7 2.2 %collective-permute-done.42 = f32[8,128]{1,0:T(8,128)S(1)} collective-permute-done((f32[8,128]{1,0:T(8,128)S(1)}, f32[8,128]{1,0:T(8,128)S(1)}, u32[]{:S(2)}, u32[]{:S(2)}) %collective-permute-start.42) | collective-permute-done | bytes 4128 | tf_op jit(solution)/shard_map/loss/ppermute | solution.py:24
  133.0 2.5 %collective-permute-done.43 = f32[8,128]{1,0:T(8,128)S(1)} collective-permute-done((f32[8,128]{1,0:T(8,128)S(1)}, f32[8,128]{1,0:T(8,128)S(1)}, u32[]{:S(2)}, u32[]{:S(2)}) %collective-permute-start.43) | collective-permute-done | bytes 4128 | tf_op jit(solution)/shard_map/loss/ppermute | solution.py:24
  136.7 4.0 %d_act_matmul.4 = (bf16[256,512]{1,0:T(8,128)(2,1)S(1)}, bf16[256,512]{1,0:T(8,128)(2,1)S(1)}, bf16[256,512]{1,0:T(8,128)(2,1)S(1)}) custom-call(s32[3]{0:T(128)S(1)} %get-tuple-element.68.index_ref, bf16[2,512,1024]{2,1,0:T(8,128)(2,1)S(1)} %get-tuple-element.31.dz_ref, bf16[4096,1024]{1,0:T(8,128)(2,1)} %w_ref.5, ...), custom_call_target="tpu_custom_call" | custom-call | flops 805306368 | bytes 3932160 | tf_op jit(solution)/shard_map/d_act/d_act_matmul/pallas_call | solution.py:299
  140.8 1.5 collective-permute-start.34
  142.9 1.6 collective-permute-start.36
  144.4 1.7 %d_act_matmul.5 = f32[256,512]{1,0:T(8,128)S(1)} custom-call(s32[1]{0:T(128)} %bitcast.3.index_ref, bf16[2,512,1024]{2,1,0:T(8,128)(2,1)S(1)} %get-tuple-element.31.dz_ref, bf16[4096,1024]{1,0:T(8,128)(2,1)} %w_ref.5, bf16[4,256,512]{2,1,0:T(8,128)(2,1)S(1)} %collective-permute-done.33.refs_0_), custom_call_target="tpu_custom_call" | custom-call | flops 268435456 | bytes 1310720 | tf_op jit(solution)/shard_map/d_act/d_act_matmul/pallas_call | solution.py:299
  146.2 1.6 broadcast_select_fusion.1
  148.1 4.4 %weight_gradient.1 = f32[1024,1024]{1,0:T(8,128)} custom-call(bf16[1024,1024]{1,0:T(8,128)(2,1)S(1)} %bitcast.48, bf16[1024,1024]{1,0:T(8,128)(2,1)S(1)} %bitcast.47), custom_call_target="tpu_custom_call" | custom-call | flops 2147483648 | bytes 4194304 | tf_op jit(solution)/shard_map/grad_weight/weight_gradient/pallas_call | solution.py:321
  154.4 1.9 %collective-permute-start.46 = (f32[8,512]{1,0:T(8,128)S(1)}, f32[8,512]{1,0:T(8,128)S(1)}, u32[]{:S(2)}, u32[]{:S(2)}) collective-permute-start(f32[8,512]{1,0:T(8,128)S(1)} %maximum_maximum_fusion), channel_id=1, source_target_pairs={{0,8},{8,16},{16,24},{24,0},{1,9},{9,17},{17,25},{25,1},{2,10},{10... | collective-permute-start | bytes 49160 | tf_op jit(solution)/shard_map/norm_backward/ppermute | solution.py:42
  156.4 1.7 %collective-permute-done.44 = f32[8,512]{1,0:T(8,128)S(1)} collective-permute-done((f32[8,512]{1,0:T(8,128)S(1)}, f32[8,512]{1,0:T(8,128)S(1)}, u32[]{:S(2)}, u32[]{:S(2)}) %collective-permute-start.44) | collective-permute-done | bytes 16416 | tf_op jit(solution)/shard_map/norm_backward/ppermute | solution.py:42
  159.0 1.6 collective-permute-done.46
  (120 shorter events, 24.7 us)
Async XLA Ops:
  2.7 6.5 %collective-permute-start = (f32[4,512]{1,0:T(4,128)S(1)}, f32[4,512]{1,0:T(4,128)S(1)}, u32[]{:S(2)}, u32[]{:S(2)}) collective-permute-start(f32[4,512]{1,0:T(4,128)S(1)} %pad_maximum_fusion.4), channel_id=1, source_target_pairs={{0,24},{8,0},{16,8},{24,16},{1,25},{9,1},{17,9},{25,17},{2,26},{10... | collective-permute-start | bytes 24584 | tf_op jit(solution)/shard_map/norm_stats/ppermute | solution.py:42
  7.8 4.5 %collective-permute-start.1 = (f32[4,512]{1,0:T(4,128)S(1)}, f32[4,512]{1,0:T(4,128)S(1)}, u32[]{:S(2)}, u32[]{:S(2)}) collective-permute-start(f32[4,512]{1,0:T(4,128)S(1)} %pad_maximum_fusion.4), channel_id=1, source_target_pairs={{0,16},{8,24},{16,0},{24,8},{1,17},{9,25},{17,1},{25,9},{2,18},{10... | collective-permute-start | bytes 24584 | tf_op jit(solution)/shard_map/norm_stats/ppermute | solution.py:42
  7.8 5.4 %collective-permute-start.2 = (f32[4,512]{1,0:T(4,128)S(1)}, f32[4,512]{1,0:T(4,128)S(1)}, u32[]{:S(2)}, u32[]{:S(2)}) collective-permute-start(f32[4,512]{1,0:T(4,128)S(1)} %pad_maximum_fusion.4), channel_id=1, source_target_pairs={{0,8},{8,16},{16,24},{24,0},{1,9},{9,17},{17,25},{25,1},{2,10},{10... | collective-permute-start | bytes 24584 | tf_op jit(solution)/shard_map/norm_stats/ppermute | solution.py:42
  14.6 9.3 %collective-permute-start.3 = (bf16[256,512]{1,0:T(8,128)(2,1)S(1)}, bf16[256,512]{1,0:T(8,128)(2,1)S(1)}, u32[]{:S(2)}, u32[]{:S(2)}) collective-permute-start(bf16[256,512]{1,0:T(8,128)(2,1)S(1)} %bitcast.49), channel_id=1, source_target_pairs={{0,2},{1,3},{2,0},{3,1},{4,6},{5,7},{6,4},{7,5},{8,10},{9,11},{10,... | collective-permute-start | bytes 786440 | tf_op jit(solution)/shard_map/act_gather/ppermute | solution.py:24
  16.1 12.0 %collective-permute-start.5 = (bf16[256,512]{1,0:T(8,128)(2,1)S(1)}, bf16[256,512]{1,0:T(8,128)(2,1)S(1)}, u32[]{:S(2)}, u32[]{:S(2)}) collective-permute-start(bf16[256,512]{1,0:T(8,128)(2,1)S(1)} %bitcast.50), channel_id=1, source_target_pairs={{0,4},{1,5},{2,6},{3,7},{4,0},{5,1},{6,2},{7,3},{8,12},{9,13},{10,... | collective-permute-start | bytes 786440 | tf_op jit(solution)/shard_map/act_gather/ppermute | solution.py:24
  17.6 10.4 %collective-permute-start.7 = (bf16[256,512]{1,0:T(8,128)(2,1)S(1)}, bf16[256,512]{1,0:T(8,128)(2,1)S(1)}, u32[]{:S(2)}, u32[]{:S(2)}) collective-permute-start(bf16[256,512]{1,0:T(8,128)(2,1)S(1)} %bitcast.51), channel_id=1, source_target_pairs={{0,6},{1,7},{2,4},{3,5},{4,2},{5,3},{6,0},{7,1},{8,14},{9,15},{10,... | collective-permute-start | bytes 786440 | tf_op jit(solution)/shard_map/act_gather/ppermute | solution.py:24
  18.1 10.6 %collective-permute-start.9 = (bf16[256,512]{1,0:T(8,128)(2,1)S(1)}, bf16[256,512]{1,0:T(8,128)(2,1)S(1)}, u32[]{:S(2)}, u32[]{:S(2)}) collective-permute-start(bf16[256,512]{1,0:T(8,128)(2,1)S(1)} %bitcast.52), channel_id=1, source_target_pairs={{0,1},{1,0},{2,3},{3,2},{4,5},{5,4},{6,7},{7,6},{8,9},{9,8},{10,11... | collective-permute-start | bytes 786440 | tf_op jit(solution)/shard_map/act_gather/ppermute | solution.py:24
  23.9 11.5 %collective-permute-start.4 = (bf16[256,512]{1,0:T(8,128)(2,1)S(1)}, bf16[256,512]{1,0:T(8,128)(2,1)S(1)}, u32[]{:S(2)}, u32[]{:S(2)}) collective-permute-start(bf16[256,512]{1,0:T(8,128)(2,1)S(1)} %collective-permute-done.3.refs_0_), channel_id=1, source_target_pairs={{0,1},{1,0},{2,3},{3,2},{4,5},{5,4},{6,7},{7,6},{8,9},{9,8},{10,11... | collective-permute-start | bytes 786440 | tf_op jit(solution)/shard_map/act_gather/ppermute | solution.py:24
  28.1 7.3 %collective-permute-start.6 = (bf16[256,512]{1,0:T(8,128)(2,1)S(1)}, bf16[256,512]{1,0:T(8,128)(2,1)S(1)}, u32[]{:S(2)}, u32[]{:S(2)}) collective-permute-start(bf16[256,512]{1,0:T(8,128)(2,1)S(1)} %collective-permute-done.5.refs_1_), channel_id=1, source_target_pairs={{0,1},{1,0},{2,3},{3,2},{4,5},{5,4},{6,7},{7,6},{8,9},{9,8},{10,11... | collective-permute-start | bytes 786440 | tf_op jit(solution)/shard_map/act_gather/ppermute | solution.py:24
  28.1 7.3 %collective-permute-start.8 = (bf16[256,512]{1,0:T(8,128)(2,1)S(1)}, bf16[256,512]{1,0:T(8,128)(2,1)S(1)}, u32[]{:S(2)}, u32[]{:S(2)}) collective-permute-start(bf16[256,512]{1,0:T(8,128)(2,1)S(1)} %collective-permute-done.7.refs_2_), channel_id=1, source_target_pairs={{0,1},{1,0},{2,3},{3,2},{4,5},{5,4},{6,7},{7,6},{8,9},{9,8},{10,11... | collective-permute-start | bytes 786440 | tf_op jit(solution)/shard_map/act_gather/ppermute | solution.py:24
  39.4 9.2 %collective-permute-start.10 = (bf16[128,1024]{1,0:T(8,128)(2,1)S(1)}, bf16[128,1024]{1,0:T(8,128)(2,1)S(1)}, u32[]{:S(2)}, u32[]{:S(2)}) collective-permute-start(bf16[128,1024]{1,0:T(8,128)(2,1)S(1)} %get-tuple-element.25.refs_0_.refs_8_), channel_id=1, source_target_pairs={{0,16},{16,24},{24,8},{8,0},{1,17},{17,25},{25,9},{9,1},{2,18},{18... | collective-permute-start | bytes 786440 | tf_op jit(solution)/shard_map/z_ring/ppermute | solution.py:34
  40.3 13.9 %collective-permute-start.11 = (bf16[128,1024]{1,0:T(8,128)(2,1)S(1)}, bf16[128,1024]{1,0:T(8,128)(2,1)S(1)}, u32[]{:S(2)}, u32[]{:S(2)}) collective-permute-start(bf16[128,1024]{1,0:T(8,128)(2,1)S(1)} %get-tuple-element.26.refs_1_.refs_9_), channel_id=1, source_target_pairs={{0,16},{16,24},{24,8},{8,0},{1,17},{17,25},{25,9},{9,1},{2,18},{18... | collective-permute-start | bytes 786440 | tf_op jit(solution)/shard_map/z_ring/ppermute | solution.py:34
  48.6 16.4 %collective-permute-start.12 = (bf16[128,1024]{1,0:T(8,128)(2,1)S(1)}, bf16[128,1024]{1,0:T(8,128)(2,1)S(1)}, u32[]{:S(2)}, u32[]{:S(2)}) collective-permute-start(bf16[128,1024]{1,0:T(8,128)(2,1)S(1)} %collective-permute-done.10.refs_2_.refs_10_), channel_id=1, source_target_pairs={{0,16},{16,24},{24,8},{8,0},{1,17},{17,25},{25,9},{9,1},{2,18},{18... | collective-permute-start | bytes 786440 | tf_op jit(solution)/shard_map/z_ring/ppermute | solution.py:34
  54.2 10.8 %collective-permute-start.13 = (bf16[128,1024]{1,0:T(8,128)(2,1)S(1)}, bf16[128,1024]{1,0:T(8,128)(2,1)S(1)}, u32[]{:S(2)}, u32[]{:S(2)}) collective-permute-start(bf16[128,1024]{1,0:T(8,128)(2,1)S(1)} %collective-permute-done.11.refs_3_.refs_11_), channel_id=1, source_target_pairs={{0,16},{16,24},{24,8},{8,0},{1,17},{17,25},{25,9},{9,1},{2,18},{18... | collective-permute-start | bytes 786440 | tf_op jit(solution)/shard_map/z_ring/ppermute | solution.py:34
  56.0 9.0 %collective-permute-start.14 = (f32[2,1024]{1,0:T(2,128)S(1)}, f32[2,1024]{1,0:T(2,128)S(1)}, u32[]{:S(2)}, u32[]{:S(2)}) collective-permute-start(f32[2,1024]{1,0:T(2,128)S(1)} %get-tuple-element.27.refs_6_), channel_id=1, source_target_pairs={{0,16},{16,24},{24,8},{8,0},{1,17},{17,25},{25,9},{9,1},{2,18},{18... | collective-permute-start | bytes 24584 | tf_op jit(solution)/shard_map/z_ring/ppermute | solution.py:34
  56.1 9.0 %collective-permute-start.15 = (f32[2,1024]{1,0:T(2,128)S(1)}, f32[2,1024]{1,0:T(2,128)S(1)}, u32[]{:S(2)}, u32[]{:S(2)}) collective-permute-start(f32[2,1024]{1,0:T(2,128)S(1)} %get-tuple-element.27.refs_6_), channel_id=1, source_target_pairs={{0,24},{16,8},{24,0},{8,16},{1,25},{17,9},{25,1},{9,17},{2,26},{18... | collective-permute-start | bytes 24584 | tf_op jit(solution)/shard_map/z_ring/ppermute | solution.py:34
  58.6 6.4 %collective-permute-start.16 = (f32[2,1024]{1,0:T(2,128)S(1)}, f32[2,1024]{1,0:T(2,128)S(1)}, u32[]{:S(2)}, u32[]{:S(2)}) collective-permute-start(f32[2,1024]{1,0:T(2,128)S(1)} %get-tuple-element.27.refs_6_), channel_id=1, source_target_pairs={{0,8},{16,0},{24,16},{8,24},{1,9},{17,1},{25,17},{9,25},{2,10},{18... | collective-permute-start | bytes 24584 | tf_op jit(solution)/shard_map/z_ring/ppermute | solution.py:34
  66.2 1.5 collective-permute-start.17
  67.8 4.2 %collective-permute-start.18 = (f32[32,384]{1,0:T(8,128)S(1)}, f32[32,384]{1,0:T(8,128)S(1)}, u32[]{:S(2)}, u32[]{:S(2)}) collective-permute-start(f32[32,384]{1,0:T(8,128)S(1)} %get-tuple-element.60), channel_id=1, source_target_pairs={{0,2},{1,3},{2,0},{3,1},{4,6},{5,7},{6,4},{7,5},{8,10},{9,11},{10,... | collective-permute-start | bytes 147464 | tf_op jit(solution)/shard_map/kernel/ppermute | solution.py:24
  69.1 4.6 %collective-permute-start.19 = (f32[32,384]{1,0:T(8,128)S(1)}, f32[32,384]{1,0:T(8,128)S(1)}, u32[]{:S(2)}, u32[]{:S(2)}) collective-permute-start(f32[32,384]{1,0:T(8,128)S(1)} %get-tuple-element.62), channel_id=1, source_target_pairs={{0,4},{1,5},{2,6},{3,7},{4,0},{5,1},{6,2},{7,3},{8,12},{9,13},{10,... | collective-permute-start | bytes 147464 | tf_op jit(solution)/shard_map/kernel/ppermute | solution.py:24
  69.9 5.0 %collective-permute-start.20 = (f32[32,384]{1,0:T(8,128)S(1)}, f32[32,384]{1,0:T(8,128)S(1)}, u32[]{:S(2)}, u32[]{:S(2)}) collective-permute-start(f32[32,384]{1,0:T(8,128)S(1)} %get-tuple-element.61), channel_id=1, source_target_pairs={{0,6},{1,7},{2,4},{3,5},{4,2},{5,3},{6,0},{7,1},{8,14},{9,15},{10,... | collective-permute-start | bytes 147464 | tf_op jit(solution)/shard_map/kernel/ppermute | solution.py:24
  75.5 6.3 %collective-permute-start.21 = (bf16[32,384]{1,0:T(8,128)(2,1)S(1)}, bf16[32,384]{1,0:T(8,128)(2,1)S(1)}, u32[]{:S(2)}, u32[]{:S(2)}) collective-permute-start(bf16[32,384]{1,0:T(8,128)(2,1)S(1)} %get-tuple-element.50), channel_id=1, source_target_pairs={{0,16},{16,24},{24,8},{8,0},{1,17},{17,25},{25,9},{9,1},{2,18},{18... | collective-permute-start | bytes 73736 | tf_op jit(solution)/shard_map/kernel/ppermute | solution.py:34
  77.4 5.8 %collective-permute-start.22 = (bf16[32,384]{1,0:T(8,128)(2,1)S(1)}, bf16[32,384]{1,0:T(8,128)(2,1)S(1)}, u32[]{:S(2)}, u32[]{:S(2)}) collective-permute-start(bf16[32,384]{1,0:T(8,128)(2,1)S(1)} %get-tuple-element.50), channel_id=1, source_target_pairs={{0,24},{16,8},{24,0},{8,16},{1,25},{17,9},{25,1},{9,17},{2,26},{18... | collective-permute-start | bytes 73736 | tf_op jit(solution)/shard_map/kernel/ppermute | solution.py:34
  78.8 5.0 %collective-permute-start.23 = (bf16[32,384]{1,0:T(8,128)(2,1)S(1)}, bf16[32,384]{1,0:T(8,128)(2,1)S(1)}, u32[]{:S(2)}, u32[]{:S(2)}) collective-permute-start(bf16[32,384]{1,0:T(8,128)(2,1)S(1)} %get-tuple-element.50), channel_id=1, source_target_pairs={{0,8},{16,0},{24,16},{8,24},{1,9},{17,1},{25,17},{9,25},{2,10},{18... | collective-permute-start | bytes 73736 | tf_op jit(solution)/shard_map/kernel/ppermute | solution.py:34
  79.5 9.7 %collective-permute-start.31 = (bf16[128,1024]{1,0:T(8,128)(2,1)S(1)}, bf16[128,1024]{1,0:T(8,128)(2,1)S(1)}, u32[]{:S(2)}, u32[]{:S(2)}) collective-permute-start(bf16[128,1024]{1,0:T(8,128)(2,1)S(1)} %collective-permute-done.12.refs_4_.refs_12_), channel_id=1, source_target_pairs={{0,16},{16,24},{24,8},{8,0},{1,17},{17,25},{25,9},{9,1},{2,18},{18... | collective-permute-start | bytes 786440 | tf_op jit(solution)/shard_map/z_ring/ppermute | solution.py:34
  81.7 10.6 %collective-permute-start.32 = (bf16[128,1024]{1,0:T(8,128)(2,1)S(1)}, bf16[128,1024]{1,0:T(8,128)(2,1)S(1)}, u32[]{:S(2)}, u32[]{:S(2)}) collective-permute-start(bf16[128,1024]{1,0:T(8,128)(2,1)S(1)} %collective-permute-done.13.refs_5_.refs_13_), channel_id=1, source_target_pairs={{0,16},{16,24},{24,8},{8,0},{1,17},{17,25},{25,9},{9,1},{2,18},{18... | collective-permute-start | bytes 786440 | tf_op jit(solution)/shard_map/z_ring/ppermute | solution.py:34
  83.8 5.5 %collective-permute-start.25 = (bf16[4,32,384]{2,1,0:T(8,128)(2,1)S(1)}, bf16[4,32,384]{2,1,0:T(8,128)(2,1)S(1)}, u32[]{:S(2)}, u32[]{:S(2)}) collective-permute-start(bf16[4,32,384]{2,1,0:T(8,128)(2,1)S(1)} %pad_maximum_fusion.3.refs_0_), channel_id=1, source_target_pairs={{0,2},{1,3},{2,0},{3,1},{4,6},{5,7},{6,4},{7,5},{8,10},{9,11},{10,... | collective-permute-start | bytes 294920 | tf_op jit(solution)/shard_map/kernel/ppermute | solution.py:24
  85.4 9.4 %collective-permute-start.27 = (bf16[4,32,384]{2,1,0:T(8,128)(2,1)S(1)}, bf16[4,32,384]{2,1,0:T(8,128)(2,1)S(1)}, u32[]{:S(2)}, u32[]{:S(2)}) collective-permute-start(bf16[4,32,384]{2,1,0:T(8,128)(2,1)S(1)} %pad_maximum_fusion.3.refs_0_), channel_id=1, source_target_pairs={{0,4},{1,5},{2,6},{3,7},{4,0},{5,1},{6,2},{7,3},{8,12},{9,13},{10,... | collective-permute-start | bytes 294920 | tf_op jit(solution)/shard_map/kernel/ppermute | solution.py:24
  85.9 16.1 %collective-permute-start.29 = (bf16[4,32,384]{2,1,0:T(8,128)(2,1)S(1)}, bf16[4,32,384]{2,1,0:T(8,128)(2,1)S(1)}, u32[]{:S(2)}, u32[]{:S(2)}) collective-permute-start(bf16[4,32,384]{2,1,0:T(8,128)(2,1)S(1)} %pad_maximum_fusion.3.refs_0_), channel_id=1, source_target_pairs={{0,6},{1,7},{2,4},{3,5},{4,2},{5,3},{6,0},{7,1},{8,14},{9,15},{10,... | collective-permute-start | bytes 294920 | tf_op jit(solution)/shard_map/kernel/ppermute | solution.py:24
  89.2 12.7 %collective-permute-start.24 = (bf16[4,32,384]{2,1,0:T(8,128)(2,1)S(1)}, bf16[4,32,384]{2,1,0:T(8,128)(2,1)S(1)}, u32[]{:S(2)}, u32[]{:S(2)}) collective-permute-start(bf16[4,32,384]{2,1,0:T(8,128)(2,1)S(1)} %pad_maximum_fusion.3.refs_0_), channel_id=1, source_target_pairs={{0,1},{1,0},{2,3},{3,2},{4,5},{5,4},{6,7},{7,6},{8,9},{9,8},{10,11... | collective-permute-start | bytes 294920 | tf_op jit(solution)/shard_map/kernel/ppermute | solution.py:24
  89.3 12.8 %collective-permute-start.26 = (bf16[4,32,384]{2,1,0:T(8,128)(2,1)S(1)}, bf16[4,32,384]{2,1,0:T(8,128)(2,1)S(1)}, u32[]{:S(2)}, u32[]{:S(2)}) collective-permute-start(bf16[4,32,384]{2,1,0:T(8,128)(2,1)S(1)} %collective-permute-done.25.refs_2_), channel_id=1, source_target_pairs={{0,1},{1,0},{2,3},{3,2},{4,5},{5,4},{6,7},{7,6},{8,9},{9,8},{10,11... | collective-permute-start | bytes 294920 | tf_op jit(solution)/shard_map/kernel/ppermute | solution.py:24
  89.8 34.7 %copy-start.5 = (bf16[1,256,512]{2,1,0:T(8,128)(2,1)}, bf16[1,256,512]{2,1,0:T(8,128)(2,1)S(1)}, u32[]{:S(2)}) copy-start(bf16[1,256,512]{2,1,0:T(8,128)(2,1)S(1)} %get-tuple-element.56) | copy-start | bytes 786436
  92.3 23.1 %collective-permute-start.37 = (bf16[256,512]{1,0:T(8,128)(2,1)S(1)}, bf16[256,512]{1,0:T(8,128)(2,1)S(1)}, u32[]{:S(2)}, u32[]{:S(2)}) collective-permute-start(bf16[256,512]{1,0:T(8,128)(2,1)S(1)} %get-tuple-element.59), channel_id=1, source_target_pairs={{0,16},{16,24},{24,8},{8,0},{1,17},{17,25},{25,9},{9,1},{2,18},{18... | collective-permute-start | bytes 786440 | tf_op jit(solution)/shard_map/grad_weight/ppermute | solution.py:34
  94.8 20.7 %collective-permute-start.38 = (bf16[256,512]{1,0:T(8,128)(2,1)S(1)}, bf16[256,512]{1,0:T(8,128)(2,1)S(1)}, u32[]{:S(2)}, u32[]{:S(2)}) collective-permute-start(bf16[256,512]{1,0:T(8,128)(2,1)S(1)} %get-tuple-element.58), channel_id=1, source_target_pairs={{0,24},{16,8},{24,0},{8,16},{1,25},{17,9},{25,1},{9,17},{2,26},{18... | collective-permute-start | bytes 786440 | tf_op jit(solution)/shard_map/grad_weight/ppermute | solution.py:34
  101.9 22.6 %collective-permute-start.39 = (bf16[256,512]{1,0:T(8,128)(2,1)S(1)}, bf16[256,512]{1,0:T(8,128)(2,1)S(1)}, u32[]{:S(2)}, u32[]{:S(2)}) collective-permute-start(bf16[256,512]{1,0:T(8,128)(2,1)S(1)} %get-tuple-element.57), channel_id=1, source_target_pairs={{0,8},{16,0},{24,16},{8,24},{1,9},{17,1},{25,17},{9,25},{2,10},{18... | collective-permute-start | bytes 786440 | tf_op jit(solution)/shard_map/grad_weight/ppermute | solution.py:34
  101.9 1.4 collective-permute-start.28
  102.0 1.4 collective-permute-start.30
  115.1 21.6 %collective-permute-start.33 = (bf16[4,256,512]{2,1,0:T(8,128)(2,1)}, bf16[4,256,512]{2,1,0:T(8,128)(2,1)S(1)}, u32[]{:S(2)}, u32[]{:S(2)}) collective-permute-start(bf16[4,256,512]{2,1,0:T(8,128)(2,1)} %d_act_matmul.3), channel_id=1, source_target_pairs={{0,1},{1,0},{2,3},{3,2},{4,5},{5,4},{6,7},{7,6},{8,9},{9,8},{10,11... | collective-permute-start | bytes 3145736 | tf_op jit(solution)/shard_map/d_act/ppermute | solution.py:24
  125.6 20.5 %collective-permute-start.40 = (bf16[2,512,512]{2,1,0:T(8,128)(2,1)}, bf16[2,512,512]{2,1,0:T(8,128)(2,1)}, u32[]{:S(2)}, u32[]{:S(2)}) collective-permute-start(bf16[2,512,512]{2,1,0:T(8,128)(2,1)} %pad_maximum_fusion.2), channel_id=1, source_target_pairs={{0,1},{1,0},{2,3},{3,2},{4,5},{5,4},{6,7},{7,6},{8,9},{9,8},{10,11... | collective-permute-start | bytes 3145736 | tf_op jit(solution)/shard_map/grad_weight/ppermute | solution.py:24
  126.3 1.9 %collective-permute-start.41 = (f32[8,128]{1,0:T(8,128)S(1)}, f32[8,128]{1,0:T(8,128)S(1)}, u32[]{:S(2)}, u32[]{:S(2)}) collective-permute-start(f32[8,128]{1,0:T(8,128)S(1)} %broadcast_add_fusion), channel_id=1, source_target_pairs={{0,1},{1,0},{2,3},{3,2},{4,5},{5,4},{6,7},{7,6},{8,9},{9,8},{10,11... | collective-permute-start | bytes 12296 | tf_op jit(solution)/shard_map/loss/ppermute | solution.py:24
  128.3 3.6 %collective-permute-start.42 = (f32[8,128]{1,0:T(8,128)S(1)}, f32[8,128]{1,0:T(8,128)S(1)}, u32[]{:S(2)}, u32[]{:S(2)}) collective-permute-start(f32[8,128]{1,0:T(8,128)S(1)} %fusion.42), channel_id=1, source_target_pairs={{0,2},{1,3},{2,0},{3,1},{4,6},{5,7},{6,4},{7,5},{8,10},{9,11},{10,... | collective-permute-start | bytes 12296 | tf_op jit(solution)/shard_map/loss/ppermute | solution.py:24
  131.9 3.6 %collective-permute-start.43 = (f32[8,128]{1,0:T(8,128)S(1)}, f32[8,128]{1,0:T(8,128)S(1)}, u32[]{:S(2)}, u32[]{:S(2)}) collective-permute-start(f32[8,128]{1,0:T(8,128)S(1)} %add.232), channel_id=1, source_target_pairs={{0,4},{1,5},{2,6},{3,7},{4,0},{5,1},{6,2},{7,3},{8,12},{9,13},{10,... | collective-permute-start | bytes 12296 | tf_op jit(solution)/shard_map/loss/ppermute | solution.py:24
  140.8 11.7 %collective-permute-start.34 = (bf16[256,512]{1,0:T(8,128)(2,1)S(1)}, bf16[256,512]{1,0:T(8,128)(2,1)S(1)}, u32[]{:S(2)}, u32[]{:S(2)}) collective-permute-start(bf16[256,512]{1,0:T(8,128)(2,1)S(1)} %get-tuple-element.32), channel_id=1, source_target_pairs={{0,2},{1,3},{2,0},{3,1},{4,6},{5,7},{6,4},{7,5},{8,10},{9,11},{10,... | collective-permute-start | bytes 786440 | tf_op jit(solution)/shard_map/d_act/ppermute | solution.py:24
  142.2 11.4 %collective-permute-start.35 = (bf16[256,512]{1,0:T(8,128)(2,1)S(1)}, bf16[256,512]{1,0:T(8,128)(2,1)S(1)}, u32[]{:S(2)}, u32[]{:S(2)}) collective-permute-start(bf16[256,512]{1,0:T(8,128)(2,1)S(1)} %get-tuple-element.33), channel_id=1, source_target_pairs={{0,4},{1,5},{2,6},{3,7},{4,0},{5,1},{6,2},{7,3},{8,12},{9,13},{10,... | collective-permute-start | bytes 786440 | tf_op jit(solution)/shard_map/d_act/ppermute | solution.py:24
  142.9 10.8 %collective-permute-start.36 = (bf16[256,512]{1,0:T(8,128)(2,1)S(1)}, bf16[256,512]{1,0:T(8,128)(2,1)S(1)}, u32[]{:S(2)}, u32[]{:S(2)}) collective-permute-start(bf16[256,512]{1,0:T(8,128)(2,1)S(1)} %get-tuple-element.34), channel_id=1, source_target_pairs={{0,6},{1,7},{2,4},{3,5},{4,2},{5,3},{6,0},{7,1},{8,14},{9,15},{10,... | collective-permute-start | bytes 786440 | tf_op jit(solution)/shard_map/d_act/ppermute | solution.py:24
  154.3 3.7 %collective-permute-start.44 = (f32[8,512]{1,0:T(8,128)S(1)}, f32[8,512]{1,0:T(8,128)S(1)}, u32[]{:S(2)}, u32[]{:S(2)}) collective-permute-start(f32[8,512]{1,0:T(8,128)S(1)} %maximum_maximum_fusion), channel_id=1, source_target_pairs={{0,24},{8,0},{16,8},{24,16},{1,25},{9,1},{17,9},{25,17},{2,26},{10... | collective-permute-start | bytes 49160 | tf_op jit(solution)/shard_map/norm_backward/ppermute | solution.py:42
  154.3 4.7 %collective-permute-start.45 = (f32[8,512]{1,0:T(8,128)S(1)}, f32[8,512]{1,0:T(8,128)S(1)}, u32[]{:S(2)}, u32[]{:S(2)}) collective-permute-start(f32[8,512]{1,0:T(8,128)S(1)} %maximum_maximum_fusion), channel_id=1, source_target_pairs={{0,16},{8,24},{16,0},{24,8},{1,17},{9,25},{17,1},{25,9},{2,18},{10... | collective-permute-start | bytes 49160 | tf_op jit(solution)/shard_map/norm_backward/ppermute | solution.py:42
  154.4 6.2 %collective-permute-start.46 = (f32[8,512]{1,0:T(8,128)S(1)}, f32[8,512]{1,0:T(8,128)S(1)}, u32[]{:S(2)}, u32[]{:S(2)}) collective-permute-start(f32[8,512]{1,0:T(8,128)S(1)} %maximum_maximum_fusion), channel_id=1, source_target_pairs={{0,8},{8,16},{16,24},{24,0},{1,9},{9,17},{17,25},{25,1},{2,10},{10... | collective-permute-start | bytes 49160 | tf_op jit(solution)/shard_map/norm_backward/ppermute | solution.py:42
  (14 other events, 103.0 us)

commit v4 on v3

--- a/solution.py
+++ b/solution.py
@@ -54,45 +54,58 @@
 
 
 def cost(flops, moved):
-    return pl.CostEstimate(flops=flops, bytes_accessed=moved, transcendentals=0)
+    return pl.CostEstimate(flops=flops // 1000, bytes_accessed=moved // 1000, transcendentals=0)
 
 
 def whole(shape):
     return pl.BlockSpec(shape, lambda i, index: (0,) * len(shape))
+
+
+SPLITS = 4
+
+
+def weight_copies(index_ref, w_ref, buffer, sems, j):
+    width = buffer.shape[1]
+    step = width // SPLITS
+    start = pl.multiple_of(index_ref[j] * width, width)
+    return [
+        pltpu.make_async_copy(
+            w_ref.at[pl.ds(start + q * step, step)],
+            buffer.at[j, pl.ds(q * step, step)],
+            sems.at[j, q],
+        )
+        for q in range(SPLITS)
+    ]
+
+
+def weight_scratch(count, width, columns):
+    return [pltpu.VMEM((count, width, columns), bf16), pltpu.SemaphoreType.DMA((count, SPLITS))]
 
 
 def z_kernel(count, first, last, index_ref, *refs):
     pieces, rest = refs[:count], list(refs[count:])
     w_ref = rest.pop(0)
     before = None if first else rest.pop(0)
-    i = pl.program_id(0)
-    if last:
-        z0_ref, z1_ref, sum_ref, total = rest
-    else:
-        (total,) = rest
-
+    buffer, sems = rest[-2:]
     for j in range(count):
-
-        @pl.when(i == j)
-        def _():
-            part = jnp.dot(pieces[j][...], w_ref[...], preferred_element_type=f32)
-            if j > 0:
-                total[...] += part
-            elif first:
-                total[...] = part
-            else:
-                total[...] = before[...] + part
-
-    if last:
-
-        @pl.when(i == count - 1)
-        def _():
-            z = total[...].astype(bf16)
-            half = z.shape[0] // 2
-            for v, ref in enumerate((z0_ref, z1_ref)):
-                mine = z[v * half : (v + 1) * half]
-                ref[...] = mine
-                sum_ref[v : v + 1, :] = jnp.sum(mine.astype(f32), axis=0, keepdims=True)
+        for copy in weight_copies(index_ref, w_ref, buffer, sems, j):
+            copy.start()
+    total = None if first else before[...]
+    for j in range(count):
+        for copy in weight_copies(index_ref, w_ref, buffer, sems, j):
+            copy.wait()
+        part = jnp.dot(pieces[j][...], buffer[j], preferred_element_type=f32)
+        total = part if total is None else total + part
+    if not last:
+        rest[0][...] = total
+        return
+    z0_ref, z1_ref, sum_ref = rest[:3]
+    z = total.astype(bf16)
+    half = z.shape[0] // 2
+    for v, ref in enumerate((z0_ref, z1_ref)):
+        mine = z[v * half : (v + 1) * half]
+        ref[...] = mine
+        sum_ref[v : v + 1, :] = jnp.sum(mine.astype(f32), axis=0, keepdims=True)
 
 
 def z_call(index, pieces, weight, before, last):
@@ -100,12 +113,11 @@
     rows, width = pieces[0].shape
     columns = weight.shape[1]
     in_specs = [whole((rows, width)) for _ in pieces]
-    in_specs.append(pl.BlockSpec((width, columns), lambda i, index: (index[i], 0)))
+    in_specs.append(pl.BlockSpec(memory_space=pl.ANY))
     operands = list(pieces) + [weight]
     if before is not None:
         in_specs.append(whole((rows, columns)))
         operands.append(before)
-    scratch = []
     if last:
         out_shape = (
             jax.ShapeDtypeStruct((rows // 2, columns), bf16),
@@ -113,7 +125,6 @@
             jax.ShapeDtypeStruct((2, columns), f32),
         )
         out_specs = (whole((rows // 2, columns)), whole((rows // 2, columns)), whole((2, columns)))
-        scratch = [pltpu.VMEM((rows, columns), f32)]
     else:
         out_shape = jax.ShapeDtypeStruct((rows, columns), f32)
         out_specs = whole((rows, columns))
@@ -122,10 +133,10 @@
         out_shape=out_shape,
         grid_spec=pltpu.PrefetchScalarGridSpec(
             num_scalar_prefetch=1,
-            grid=(count,),
+            grid=(1,),
             in_specs=in_specs,
             out_specs=out_specs,
-            scratch_shapes=scratch,
+            scratch_shapes=weight_scratch(count, width, columns),
         ),
         compiler_params=params(),
         cost_estimate=cost(
@@ -260,47 +271,74 @@
     )(index, *strips, *[z for slot in z_slots for z in slot])
 
 
-def d_act_kernel(count, adds, index_ref, dz_ref, w_ref, *refs):
-    i = pl.program_id(0)
+EXTRA = 16
+
+
+def share_rows(share, width, kind):
+    high = share.astype(bf16).astype(f32)
+    middle = (share - high).astype(bf16).astype(f32)
+    low = share - high - middle
+    row = lax.broadcasted_iota(jnp.int32, (EXTRA, width), 0)
+    rows = jnp.where(row == 0, high, jnp.where(row == 1, middle, jnp.where(row == 2, low, 0.0)))
+    return rows.astype(kind)
+
+
+def share_of(rows):
+    return rows[0:1].astype(f32) + rows[1:2].astype(f32) + rows[2:3].astype(f32)
+
+
+def d_act_kernel(count, first, index_ref, dz_ref, share_ref, w_ref, *refs):
+    buffer, sems = refs[-2:]
+    for j in range(count):
+        for copy in weight_copies(index_ref, w_ref, buffer, sems, j):
+            copy.start()
     two, local_rows, columns = dz_ref.shape
-    part = lax.dot_general(
-        dz_ref[...].reshape(two * local_rows, columns),
-        w_ref[...],
-        (((1,), (1,)), ((), ())),
-        preferred_element_type=f32,
-    )
-    if not adds:
-        refs[0][0] = part.astype(refs[0].dtype)
-        return
-    part = part + refs[0][0].astype(f32)
+    dz = dz_ref[...].reshape(two * local_rows, columns)
     for j in range(count):
-
-        @pl.when(i == j)
-        def _():
-            refs[j + 1][...] = part.astype(refs[j + 1].dtype)
-
-
-def d_act_call(index, dz, weight, local_rows, width, got, first, count, kind):
+        for copy in weight_copies(index_ref, w_ref, buffer, sems, j):
+            copy.wait()
+        part = lax.dot_general(
+            dz, buffer[j], (((1,), (1,)), ((), ())), preferred_element_type=f32
+        )
+        tall, width = part.shape
+        share = share_ref[0:1, 0:1]
+        if first is None:
+            refs[0][j, :tall] = part.astype(refs[0].dtype)
+            refs[0][j, tall:] = share_rows(share, width, refs[0].dtype)
+        else:
+            out_ref = refs[j + 1]
+            out_ref[:tall] = (part + refs[0][first + j, :tall].astype(f32)).astype(out_ref.dtype)
+            share = share + share_of(refs[0][first + j, tall:])[:, 0:1]
+            out_ref[tall:] = share_rows(share, width, out_ref.dtype)
+
+
+def d_act_call(index, dz, share, weight, local_rows, width, got, first, count, kind):
     columns = weight.shape[1]
     tall = 2 * local_rows
     in_specs = [
         pl.BlockSpec((2, local_rows, columns), lambda i, index: (0, 0, 0)),
-        pl.BlockSpec((width, columns), lambda i, index: (index[i], 0)),
+        whole(share.shape),
+        pl.BlockSpec(memory_space=pl.ANY),
     ]
-    operands = [dz, weight]
+    operands = [dz, share, weight]
+    long = tall + EXTRA
     if got is None:
-        out_shape = (jax.ShapeDtypeStruct((count, tall, width), kind),)
-        out_specs = (pl.BlockSpec((1, tall, width), lambda i, index: (i, 0, 0)),)
+        out_shape = (jax.ShapeDtypeStruct((count, long, width), kind),)
+        out_specs = (whole((count, long, width)),)
     else:
-        in_specs.append(pl.BlockSpec((1, tall, width), lambda i, index: (first + i, 0, 0)))
+        in_specs.append(whole(got.shape))
         operands.append(got)
-        out_shape = (jax.ShapeDtypeStruct((tall, width), kind),) * count
-        out_specs = (whole((tall, width)),) * count
+        out_shape = (jax.ShapeDtypeStruct((long, width), kind),) * count
+        out_specs = (whole((long, width)),) * count
     return pl.pallas_call(
-        functools.partial(d_act_kernel, count, got is not None),
+        functools.partial(d_act_kernel, count, None if got is None else first),
         out_shape=out_shape,
         grid_spec=pltpu.PrefetchScalarGridSpec(
-            num_scalar_prefetch=1, grid=(count,), in_specs=in_specs, out_specs=out_specs
+            num_scalar_prefetch=1,
+            grid=(1,),
+            in_specs=in_specs,
+            out_specs=out_specs,
+            scratch_shapes=weight_scratch(count, width, columns),
         ),
         compiler_params=params(),
         cost_estimate=cost(2 * tall * width * columns * count, 2 * count * width * (columns + tall)),
@@ -389,17 +427,18 @@
         strip = even_part[0]
         for k in far:
             strip = strip + xor_send(even_part[k // 2], "col", k)
+        strip, slots[reach + 1 :] = lax.optimization_barrier((strip, slots[reach + 1 :]))
         block = lax.broadcasted_iota(jnp.int32, (1, strip.shape[1]), 1) // local_rows
         twice = jnp.where((block > 0) & (block < n_batch - reach), 2.0, 1.0)
         block_share = jnp.sum(strip * strip * twice) / denom
         mine = strip.astype(bf16)
         mine = jnp.stack([mine] + [ring_send(mine, "batch", d) for d in range(1, n_batch)])
-        mine, held_back = lax.optimization_barrier((mine, [pieces[k] for k in evens]))
         strips = {0: mine}
         for k in far:
             strips[k] = xor_send(mine, "col", k)
         for k in evens:
             strips[k + 1] = xor_send(strips[k], "col", 1)
+        strips, held_back = lax.optimization_barrier((strips, [pieces[k] for k in evens]))
     with jax.named_scope("dz"):
         constants = (
             4.0 * scale / denom,
@@ -410,15 +449,17 @@
             1.0 / denom / n_batch,
         )
         dz, share = dz_call(everyone, [strips[k] for k in range(n_col)], slots, constants)
+        share = share + block_share
     with jax.named_scope("d_act"):
         half = len(evens)
         (away,) = d_act_call(
-            places([k + 1 for k in evens]), dz, blocks, local_rows, width, None, 0, half, bf16
+            places([k + 1 for k in evens]), dz, share, blocks, local_rows, width, None, 0, half, bf16
         )
         got = xor_send(away, "col", 1)
-        sends = d_act_call(places(far), dz, blocks, local_rows, width, got, 1, half - 1, bf16)
+        sends = d_act_call(places(far), dz, share, blocks, local_rows, width, got, 1, half - 1, bf16)
         arrived = [xor_send(part, "col", k) for k, part in zip(far, sends)]
-        (d_act,) = d_act_call(places([0]), dz, blocks, local_rows, width, got, 0, 1, f32)
+        got, _ = lax.optimization_barrier((got, sends))
+        (d_act,) = d_act_call(places([0]), dz, share, blocks, local_rows, width, got, 0, 1, f32)
     with jax.named_scope("grad_weight"):
         per_plane = n_col // n_batch
         order = jnp.array(ring_order(n_batch), jnp.int32)
@@ -436,28 +477,27 @@
                 ahead = (position + d) % n_batch
                 plane = jnp.where(ahead < (n_batch + 1) // 2, 2 * ahead, 2 * (n_batch - ahead) - 1)
                 own.append(ring_send(held(plane, i), "batch", d))
+            own, d_act = lax.optimization_barrier((own, d_act))
             own = jnp.concatenate([o.reshape(n_view, local_rows, width) for o in own], axis=1)
             other = xor_send(own, "col", 1)
             halves.append(jnp.where(c % 2 == 0, own, other))
             halves.append(jnp.where(c % 2 == 0, other, own))
         wanted = jnp.concatenate(halves, axis=2).reshape(n_view * rows, per_plane * width)
         grad_weight = weight_grad_call(wanted, dz.reshape(n_view * rows, columns))
-    with jax.named_scope("loss"):
-        share = share + block_share
-        k = 1
-        while k < n_col:
-            share = share + xor_send(share, "col", k)
-            k *= 2
     with jax.named_scope("norm_backward"):
         arrived, d_act, grad_weight = lax.optimization_barrier((arrived, d_act, grad_weight))
+        shares = [share_of(part[tall:]) for part in [d_act] + arrived]
+        while len(shares) > 1:
+            shares = [x + y for x, y in zip(shares[::2], shares[1::2])]
+        d_act = d_act[:tall]
         for part in arrived:
-            d_act = d_act + part.astype(f32)
+            d_act = d_act + part[:tall].astype(f32)
         d_pre = d_act.reshape(n_view, local_rows, width) * gelu_slope(preactivation)
         sums = jnp.concatenate(
             [
                 jnp.sum(d_pre, axis=1),
                 jnp.sum(d_pre * normalised, axis=1),
-                jnp.broadcast_to(share[:1, :1], (2 * n_view, width)),
+                jnp.broadcast_to(shares[0], (2 * n_view, width)),
             ]
         )
         both = sum(exchange(sums, "batch"))

time: 163 us -> 175 us (1.074)
  local copies, waits for them, and re-layouts: 2.41 us -> 19.4 us
  waiting for transfers between devices: 64.9 us -> 59.9 us
  Pallas kernels: 32.6 us -> 29.4 us
    unnamed x30 -> x84, local copies, waits for them, and re-layouts: 1.01 us -> 19.2 us
    ppermute x6, starting transfers between devices: 8.13 us -> 16.1 us  [exchange(): slots.append(lax.ppermute(x, axis, [(i, (i + d) % n) for i in range(n)]))]
    ppermute x6, waiting for transfers between devices: 8.68 us -> 3.74 us  [exchange(): slots.append(lax.ppermute(x, axis, [(i, (i + d) % n) for i in range(n)]))]
    ppermute x26 -> x23, starting transfers between devices: 19.4 us -> 15.4 us  [xor_send(): return lax.ppermute(x, axis, [(i, i ^ k) for i in range(n)])]
    ppermute x15, starting transfers between devices: 23.5 us -> 21 us  [ring_send(): lax.ppermute(x, axis, [(order[i], order[(i + d) % n]) for i in range(n)])]
    pallas_call x3, Pallas kernels: 10.6 us -> 8.78 us  [z_call(): pl.pallas_call(functools.partial(z_kernel, count, before is None, last),...]
    ppermute x26 -> x23, waiting for transfers between devices: 23.1 us -> 22 us  [xor_send(): return lax.ppermute(x, axis, [(i, i ^ k) for i in range(n)])]
  transfers between devices with their start and end apart: 47 -> 44, of which waited for: 26 -> 21; matrix products, arithmetic and copies ran while one was open for 3% -> 2% of each run, Pallas kernels for 17% -> 9%
where the time goes in v4:
time: 175 us; the launch traced here: 174 us
  waiting for transfers between devices  59.9 us (34%)
  starting transfers between devices  52.4 us (30%)
  Pallas kernels  29.4 us (17%)
  local copies, waits for them, and re-layouts  19.4 us (11%)
  other arithmetic  11.5 us (7%)
  between operations  1.78 us (1%)
    ppermute x15, waiting for transfers between devices, ring_send(): lax.ppermute(x, axis, [(order[i], order[(i + d) % n]) for i in range(n)])  34.2 us
    ppermute x23, waiting for transfers between devices, xor_send(): return lax.ppermute(x, axis, [(i, i ^ k) for i in range(n)])  22 us
    ppermute x15, starting transfers between devices, ring_send(): lax.ppermute(x, axis, [(order[i], order[(i + d) % n]) for i in range(n)])  21 us
    unnamed x84, local copies, waits for them, and re-layouts  19.2 us
    ppermute x6, starting transfers between devices, exchange(): slots.append(lax.ppermute(x, axis, [(i, (i + d) % n) for i in range(n)]))  16.1 us
    ppermute x23, starting transfers between devices, xor_send(): return lax.ppermute(x, axis, [(i, i ^ k) for i in range(n)])  15.4 us
    pallas_call x3, Pallas kernels, d_act_call(): pl.pallas_call(functools.partial(d_act_kernel, count, None if got is None...  9.85 us
    pallas_call x3, Pallas kernels, z_call(): pl.pallas_call(functools.partial(z_kernel, count, before is None, last),...  8.78 us
  transfers between devices with their start and end apart: 44, of which 21 were waited for; matrix products, arithmetic and copies ran while one was open for 2% of the time, Pallas kernels for 9%

profile of v4, /device:TPU:0, one launch (start us, length us, event | category | flops | bytes accessed | tf_op | source)
XLA Modules:
  0.0 174.5 jit_solution(3928115545524547174)
XLA Ops:
  2.7 3.1 %collective-permute-start.2 = (f32[4,512]{1,0:T(4,128)S(1)}, f32[4,512]{1,0:T(4,128)S(1)}, u32[]{:S(2)}, u32[]{:S(2)}) collective-permute-start(f32[4,512]{1,0:T(4,128)S(1)} %pad_maximum_fusion.5), channel_id=1, source_target_pairs={{0,8},{8,16},{16,24},{24,0},{1,9},{9,17},{17,25},{25,1},{2,10},{10... | collective-permute-start | bytes 24584 | tf_op jit(solution)/shard_map/norm_stats/ppermute | solution.py:42
  5.8 2.6 %collective-permute-start.1 = (f32[4,512]{1,0:T(4,128)S(1)}, f32[4,512]{1,0:T(4,128)S(1)}, u32[]{:S(2)}, u32[]{:S(2)}) collective-permute-start(f32[4,512]{1,0:T(4,128)S(1)} %pad_maximum_fusion.5), channel_id=1, source_target_pairs={{0,16},{8,24},{16,0},{24,8},{1,17},{9,25},{17,1},{25,9},{2,18},{10... | collective-permute-start | bytes 24584 | tf_op jit(solution)/shard_map/norm_stats/ppermute | solution.py:42
  8.4 1.3 collective-permute-start
  10.4 1.6 collective-permute-done
  12.1 1.2 fusion.17
  13.3 2.5 %collective-permute-start.7 = (bf16[256,512]{1,0:T(8,128)(2,1)S(1)}, bf16[256,512]{1,0:T(8,128)(2,1)S(1)}, u32[]{:S(2)}, u32[]{:S(2)}) collective-permute-start(bf16[256,512]{1,0:T(8,128)(2,1)S(1)} %bitcast.50), channel_id=1, source_target_pairs={{0,6},{1,7},{2,4},{3,5},{4,2},{5,3},{6,0},{7,1},{8,14},{9,15},{10,... | collective-permute-start | bytes 786440 | tf_op jit(solution)/shard_map/act_gather/ppermute | solution.py:24
  16.9 6.7 %collective-permute-done.7.refs_2_ = bf16[256,512]{1,0:T(8,128)(2,1)S(1)} collective-permute-done((bf16[256,512]{1,0:T(8,128)(2,1)S(1)}, bf16[256,512]{1,0:T(8,128)(2,1)S(1)}, u32[]{:S(2)}, u32[]{:S(2)}) %collective-permute-start.7) | collective-permute-done | bytes 262176 | tf_op jit(solution)/shard_map/act_gather/ppermute | solution.py:24
  23.6 3.0 %collective-permute-done.5.refs_1_ = bf16[256,512]{1,0:T(8,128)(2,1)S(1)} collective-permute-done((bf16[256,512]{1,0:T(8,128)(2,1)S(1)}, bf16[256,512]{1,0:T(8,128)(2,1)S(1)}, u32[]{:S(2)}, u32[]{:S(2)}) %collective-permute-start.5) | collective-permute-done | bytes 262176 | tf_op jit(solution)/shard_map/act_gather/ppermute | solution.py:24
  27.2 2.8 %z_matmul.3.refs_4_ = f32[256,1024]{1,0:T(8,128)S(1)} custom-call(s32[2]{0:T(128)S(1)} %pad_add_fusion.2.index_ref, bf16[256,512]{1,0:T(8,128)(2,1)S(1)} %bitcast.54, bf16[256,512]{1,0:T(8,128)(2,1)S(1)} %collective-permute-done.9.refs_1_, bf16[4096,1024]{1,0:T(8,128)(2,1)} %w_ref.5), custom_call_target="tpu_custom_call" | custom-call | flops 536870 | bytes 2621 | tf_op jit(solution)/shard_map/z/z_matmul/pallas_call | solution.py:131
  30.1 3.0 %z_matmul.4.refs_4_ = f32[256,1024]{1,0:T(8,128)S(1)} custom-call(s32[3]{0:T(128)S(1)} %get-tuple-element.100.index_ref, bf16[256,512]{1,0:T(8,128)(2,1)S(1)} %collective-permute-done.3.refs_0_, bf16[256,512]{1,0:T(8,128)(2,1)S(1)} %collective-permute-done.5.refs_1_, bf16[256,512]{1,0:T(8,128)(2,1)S(1)} %collective-permute-done.7.refs_2_, ...), custom_call_target="tpu_custom_call" | custom-call | flops 805306 | bytes 3932 | tf_op jit(solution)/shard_map/z/z_matmul/pallas_call | solution.py:131
  34.7 3.0 %z_matmul.5 = (bf16[128,1024]{1,0:T(8,128)(2,1)S(1)}, bf16[128,1024]{1,0:T(8,128)(2,1)S(1)}, f32[2,1024]{1,0:T(2,128)S(1)}) custom-call(s32[3]{0:T(128)S(1)} %get-tuple-element.101.index_ref, bf16[256,512]{1,0:T(8,128)(2,1)S(1)} %copy-done.14, bf16[256,512]{1,0:T(8,128)(2,1)S(1)} %collective-permute-done.6.refs_1_, ...), custom_call_target="tpu_custom_call" | custom-call | flops 805306 | bytes 3932 | tf_op jit(solution)/shard_map/z/z_matmul/pallas_call | solution.py:131
  38.7 2.5 %collective-permute-start.11 = (bf16[128,1024]{1,0:T(8,128)(2,1)S(1)}, bf16[128,1024]{1,0:T(8,128)(2,1)S(1)}, u32[]{:S(2)}, u32[]{:S(2)}) collective-permute-start(bf16[128,1024]{1,0:T(8,128)(2,1)S(1)} %get-tuple-element.42.refs_1_.refs_9_), channel_id=1, source_target_pairs={{0,16},{16,24},{24,8},{8,0},{1,17},{17,25},{25,9},{9,1},{2,18},{18... | collective-permute-start | bytes 786440 | tf_op jit(solution)/shard_map/z_ring/ppermute | solution.py:34
  41.2 5.7 %collective-permute-done.10.refs_2_.refs_10_ = bf16[128,1024]{1,0:T(8,128)(2,1)S(1)} collective-permute-done((bf16[128,1024]{1,0:T(8,128)(2,1)S(1)}, bf16[128,1024]{1,0:T(8,128)(2,1)S(1)}, u32[]{:S(2)}, u32[]{:S(2)}) %collective-permute-start.10) | collective-permute-done | bytes 262176 | tf_op jit(solution)/shard_map/z_ring/ppermute | solution.py:34
  46.9 1.8 %collective-permute-start.12 = (bf16[128,1024]{1,0:T(8,128)(2,1)S(1)}, bf16[128,1024]{1,0:T(8,128)(2,1)S(1)}, u32[]{:S(2)}, u32[]{:S(2)}) collective-permute-start(bf16[128,1024]{1,0:T(8,128)(2,1)S(1)} %collective-permute-done.10.refs_2_.refs_10_), channel_id=1, source_target_pairs={{0,16},{16,24},{24,8},{8,0},{1,17},{17,25},{25,9},{9,1},{2,18},{18... | collective-permute-start | bytes 786440 | tf_op jit(solution)/shard_map/z_ring/ppermute | solution.py:34
  48.7 3.8 %collective-permute-done.11.refs_3_.refs_11_ = bf16[128,1024]{1,0:T(8,128)(2,1)S(1)} collective-permute-done((bf16[128,1024]{1,0:T(8,128)(2,1)S(1)}, bf16[128,1024]{1,0:T(8,128)(2,1)S(1)}, u32[]{:S(2)}, u32[]{:S(2)}) %collective-permute-start.11) | collective-permute-done | bytes 262176 | tf_op jit(solution)/shard_map/z_ring/ppermute | solution.py:34
  52.6 1.8 %collective-permute-start.13 = (bf16[128,1024]{1,0:T(8,128)(2,1)S(1)}, bf16[128,1024]{1,0:T(8,128)(2,1)S(1)}, u32[]{:S(2)}, u32[]{:S(2)}) collective-permute-start(bf16[128,1024]{1,0:T(8,128)(2,1)S(1)} %collective-permute-done.11.refs_3_.refs_11_), channel_id=1, source_target_pairs={{0,16},{16,24},{24,8},{8,0},{1,17},{17,25},{25,9},{9,1},{2,18},{18... | collective-permute-start | bytes 786440 | tf_op jit(solution)/shard_map/z_ring/ppermute | solution.py:34
  54.6 2.8 %collective-permute-start.15 = (f32[2,1024]{1,0:T(2,128)S(1)}, f32[2,1024]{1,0:T(2,128)S(1)}, u32[]{:S(2)}, u32[]{:S(2)}) collective-permute-start(f32[2,1024]{1,0:T(2,128)S(1)} %get-tuple-element.43.refs_6_), channel_id=1, source_target_pairs={{0,24},{16,8},{24,0},{8,16},{1,25},{17,9},{25,1},{9,17},{2,26},{18... | collective-permute-start | bytes 24584 | tf_op jit(solution)/shard_map/z_ring/ppermute | solution.py:34
  58.4 6.3 %collective-permute-done.16.refs_9_ = f32[2,1024]{1,0:T(2,128)S(1)} collective-permute-done((f32[2,1024]{1,0:T(2,128)S(1)}, f32[2,1024]{1,0:T(2,128)S(1)}, u32[]{:S(2)}, u32[]{:S(2)}) %collective-permute-start.16) | collective-permute-done | bytes 8224 | tf_op jit(solution)/shard_map/z_ring/ppermute | solution.py:34
  64.7 1.2 kernel_strip.1
  66.8 1.4 collective-permute-start.22
  68.3 1.6 collective-permute-start.18
  69.8 1.5 collective-permute-start.20
  72.7 2.1 %collective-permute-done.20 = f32[32,384]{1,0:T(8,128)S(1)} collective-permute-done((f32[32,384]{1,0:T(8,128)S(1)}, f32[32,384]{1,0:T(8,128)S(1)}, u32[]{:S(2)}, u32[]{:S(2)}) %collective-permute-start.20) | collective-permute-done | bytes 49184 | tf_op jit(solution)/shard_map/kernel/ppermute | solution.py:24
  75.4 4.9 %collective-permute-done.22.refs_15_ = bf16[128,1024]{1,0:T(8,128)(2,1)S(1)} collective-permute-done((bf16[128,1024]{1,0:T(8,128)(2,1)S(1)}, bf16[128,1024]{1,0:T(8,128)(2,1)S(1)}, u32[]{:S(2)}, u32[]{:S(2)}) %collective-permute-start.22) | collective-permute-done | bytes 262176 | tf_op jit(solution)/shard_map/z_ring/ppermute | solution.py:34
  81.6 1.5 collective-permute-start.25
  83.1 1.6 collective-permute-start.24
  85.3 1.1 collective-permute-done.25
  86.3 2.5 %collective-permute-done.24 = bf16[32,384]{1,0:T(8,128)(2,1)S(1)} collective-permute-done((bf16[32,384]{1,0:T(8,128)(2,1)S(1)}, bf16[32,384]{1,0:T(8,128)(2,1)S(1)}, u32[]{:S(2)}, u32[]{:S(2)}) %collective-permute-start.24) | collective-permute-done | bytes 24608 | tf_op jit(solution)/shard_map/kernel/ppermute | solution.py:34
  88.8 1.8 %collective-permute-start.31 = (bf16[4,32,384]{2,1,0:T(8,128)(2,1)S(1)}, bf16[4,32,384]{2,1,0:T(8,128)(2,1)S(1)}, u32[]{:S(2)}, u32[]{:S(2)}) collective-permute-start(bf16[4,32,384]{2,1,0:T(8,128)(2,1)S(1)} %pad_maximum_fusion.3.refs_0_), channel_id=1, source_target_pairs={{0,6},{1,7},{2,4},{3,5},{4,2},{5,3},{6,0},{7,1},{8,14},{9,15},{10,... | collective-permute-start | bytes 294920 | tf_op jit(solution)/shard_map/kernel/ppermute | solution.py:24
  90.6 1.2 collective-permute-start.29
  92.4 2.2 %collective-permute-done.31.refs_6_ = bf16[4,32,384]{2,1,0:T(8,128)(2,1)S(1)} collective-permute-done((bf16[4,32,384]{2,1,0:T(8,128)(2,1)S(1)}, bf16[4,32,384]{2,1,0:T(8,128)(2,1)S(1)}, u32[]{:S(2)}, u32[]{:S(2)}) %collective-permute-start.31) | collective-permute-done | bytes 98336 | tf_op jit(solution)/shard_map/kernel/ppermute | solution.py:24
  110.7 5.2 %embedding_gradient.1 = (bf16[2,512,1024]{2,1,0:T(8,128)(2,1)S(1)}, f32[8,128]{1,0:T(8,128)S(1)}) custom-call(s32[8]{0:T(128)S(1)} %stack.95.index_ref, bf16[4,32,384]{2,1,0:T(8,128)(2,1)S(1)} %pad_maximum_fusion.3.refs_0_, bf16[4,32,384]{2,1,0:T(8,128)(2,1)S(1)} %copy-done.22, bf16[4,32,384]{2,1,0:T(8,128)(2,1)S(1)} %copy-done.20, ...), custom_call_target="tpu_custom_call" | custom-call | flops 1073741 | bytes 4194 | tf_op jit(solution)/shard_map/dz/embedding_gradient/pallas_call | solution.py:247
  116.0 4.8 %d_act_matmul.3 = bf16[4,272,512]{2,1,0:T(8,128)(2,1)} custom-call(s32[4]{0:T(128)S(1)} %pad_add_fusion.3.index_ref, bf16[2,512,1024]{2,1,0:T(8,128)(2,1)S(1)} %get-tuple-element.57.dz_ref, f32[8,128]{1,0:T(8,128)S(1)} %broadcast_add_fusion.share_ref, bf16[4096,1024]{1,0:T(8,128)(2,1)} %w_ref.5), custom_call_target="tpu_custom_call" | custom-call | flops 1073741 | bytes 5242 | tf_op jit(solution)/shard_map/d_act/d_act_matmul/pallas_call | solution.py:333
  121.1 1.2 pad_maximum_fusion.1
  122.4 1.1 collective-permute-start.39
  123.5 1.6 collective-permute-start.38
  125.1 1.4 collective-permute-start.37
  126.5 3.3 %d_act_matmul.4 = (bf16[272,512]{1,0:T(8,128)(2,1)S(1)}, bf16[272,512]{1,0:T(8,128)(2,1)S(1)}, bf16[272,512]{1,0:T(8,128)(2,1)S(1)}) custom-call(s32[3]{0:T(128)S(1)} %get-tuple-element.100.index_ref, bf16[2,512,1024]{2,1,0:T(8,128)(2,1)S(1)} %get-tuple-element.57.dz_ref, f32[8,128]{1,0:T(8,128)S(1)} %broadcast_add_fusion.share_ref, ...), custom_call_target="tpu_custom_call" | custom-call | flops 805306 | bytes 3932 | tf_op jit(solution)/shard_map/d_act/d_act_matmul/pallas_call | solution.py:333
  131.2 1.8 %d_act_matmul.5 = f32[272,512]{1,0:T(8,128)S(1)} custom-call(s32[1]{0:T(128)} %bitcast.3.index_ref, bf16[2,512,1024]{2,1,0:T(8,128)(2,1)S(1)} %get-tuple-element.57.dz_ref, f32[8,128]{1,0:T(8,128)S(1)} %broadcast_add_fusion.share_ref, bf16[4096,1024]{1,0:T(8,128)(2,1)} %w_ref.5, bf16[4,272,512]{2,1,0:T(8,128)(2,1)S(1)} %collective-permute-done.33.refs_0_), custom_call_target="tpu_custom_call" | custom-call | flops 268435 | bytes 1310 | tf_op jit(solution)/shard_map/d_act/d_act_matmul/pallas_call | solution.py:333
  133.9 9.9 %collective-permute-done.39 = bf16[256,512]{1,0:T(8,128)(2,1)S(1)} collective-permute-done((bf16[256,512]{1,0:T(8,128)(2,1)S(1)}, bf16[256,512]{1,0:T(8,128)(2,1)S(1)}, u32[]{:S(2)}, u32[]{:S(2)}) %collective-permute-start.39) | collective-permute-done | bytes 262176 | tf_op jit(solution)/shard_map/grad_weight/ppermute | solution.py:34
  145.0 1.4 collective-permute-start.34
  147.2 1.4 collective-permute-start.36
  148.5 1.9 %broadcast_select_fusion.1 = (bf16[2,512,512]{2,1,0:T(8,128)(2,1)S(1)}, bf16[2,512,512]{2,1,0:T(8,128)(2,1)S(1)}) fusion(bf16[2,512,512]{2,1,0:T(8,128)(2,1)} %collective-permute-done.40, pred[]{:T(512)S(6)} %eq.103, bf16[2,128,512]{2,1,0:T(8,128)(2,1)} %bitcast.62, bf16[2,128,512]{2,1,0:T(8,128)(2,1)} %bitcast.64, bf16[2,128,512]{2,1,0:T(8,128)(2,1)} %bitcast.66, ...), kind=kLoop, calls=%fused_computation.4 | loop fusion | flops 5242880 | bytes 4194305 | tf_op jit(solution)/shard_map/grad_weight/jit(_where)/select_n | solution.py:483
  150.7 4.4 %weight_gradient.1 = f32[1024,1024]{1,0:T(8,128)} custom-call(bf16[1024,1024]{1,0:T(8,128)(2,1)S(1)} %bitcast.49, bf16[1024,1024]{1,0:T(8,128)(2,1)S(1)} %bitcast.48), custom_call_target="tpu_custom_call" | custom-call | flops 2147483 | bytes 4194 | tf_op jit(solution)/shard_map/grad_weight/weight_gradient/pallas_call | solution.py:359
  155.1 6.0 %collective-permute-done.35 = bf16[272,512]{1,0:T(8,128)(2,1)S(1)} collective-permute-done((bf16[272,512]{1,0:T(8,128)(2,1)S(1)}, bf16[272,512]{1,0:T(8,128)(2,1)S(1)}, u32[]{:S(2)}, u32[]{:S(2)}) %collective-permute-start.35) | collective-permute-done | bytes 278560 | tf_op jit(solution)/shard_map/d_act/ppermute | solution.py:24
  161.8 5.6 %collective-permute-start.43 = (f32[8,512]{1,0:T(8,128)S(1)}, f32[8,512]{1,0:T(8,128)S(1)}, u32[]{:S(2)}, u32[]{:S(2)}) collective-permute-start(f32[8,512]{1,0:T(8,128)S(1)} %pad_maximum_fusion.4), channel_id=1, source_target_pairs={{0,8},{8,16},{16,24},{24,0},{1,9},{9,17},{17,25},{25,1},{2,10},{10... | collective-permute-start | bytes 49160 | tf_op jit(solution)/shard_map/norm_backward/ppermute | solution.py:42
  168.0 2.8 %collective-permute-start.41 = (f32[8,512]{1,0:T(8,128)S(1)}, f32[8,512]{1,0:T(8,128)S(1)}, u32[]{:S(2)}, u32[]{:S(2)}) collective-permute-start(f32[8,512]{1,0:T(8,128)S(1)} %pad_maximum_fusion.4), channel_id=1, source_target_pairs={{0,24},{8,0},{16,8},{24,16},{1,25},{9,1},{17,9},{25,17},{2,26},{10... | collective-permute-start | bytes 49160 | tf_op jit(solution)/shard_map/norm_backward/ppermute | solution.py:42
  170.8 1.2 collective-permute-done.42
  (165 shorter events, 37.7 us)
Async XLA Ops:
  2.7 7.0 %collective-permute-start.2 = (f32[4,512]{1,0:T(4,128)S(1)}, f32[4,512]{1,0:T(4,128)S(1)}, u32[]{:S(2)}, u32[]{:S(2)}) collective-permute-start(f32[4,512]{1,0:T(4,128)S(1)} %pad_maximum_fusion.5), channel_id=1, source_target_pairs={{0,8},{8,16},{16,24},{24,0},{1,9},{9,17},{17,25},{25,1},{2,10},{10... | collective-permute-start | bytes 24584 | tf_op jit(solution)/shard_map/norm_stats/ppermute | solution.py:42
  5.8 4.6 %collective-permute-start.1 = (f32[4,512]{1,0:T(4,128)S(1)}, f32[4,512]{1,0:T(4,128)S(1)}, u32[]{:S(2)}, u32[]{:S(2)}) collective-permute-start(f32[4,512]{1,0:T(4,128)S(1)} %pad_maximum_fusion.5), channel_id=1, source_target_pairs={{0,16},{8,24},{16,0},{24,8},{1,17},{9,25},{17,1},{25,9},{2,18},{10... | collective-permute-start | bytes 24584 | tf_op jit(solution)/shard_map/norm_stats/ppermute | solution.py:42
  8.4 3.7 %collective-permute-start = (f32[4,512]{1,0:T(4,128)S(1)}, f32[4,512]{1,0:T(4,128)S(1)}, u32[]{:S(2)}, u32[]{:S(2)}) collective-permute-start(f32[4,512]{1,0:T(4,128)S(1)} %pad_maximum_fusion.5), channel_id=1, source_target_pairs={{0,24},{8,0},{16,8},{24,16},{1,25},{9,1},{17,9},{25,17},{2,26},{10... | collective-permute-start | bytes 24584 | tf_op jit(solution)/shard_map/norm_stats/ppermute | solution.py:42
  13.3 10.2 %collective-permute-start.7 = (bf16[256,512]{1,0:T(8,128)(2,1)S(1)}, bf16[256,512]{1,0:T(8,128)(2,1)S(1)}, u32[]{:S(2)}, u32[]{:S(2)}) collective-permute-start(bf16[256,512]{1,0:T(8,128)(2,1)S(1)} %bitcast.50), channel_id=1, source_target_pairs={{0,6},{1,7},{2,4},{3,5},{4,2},{5,3},{6,0},{7,1},{8,14},{9,15},{10,... | collective-permute-start | bytes 786440 | tf_op jit(solution)/shard_map/act_gather/ppermute | solution.py:24
  15.8 10.7 %collective-permute-start.5 = (bf16[256,512]{1,0:T(8,128)(2,1)S(1)}, bf16[256,512]{1,0:T(8,128)(2,1)S(1)}, u32[]{:S(2)}, u32[]{:S(2)}) collective-permute-start(bf16[256,512]{1,0:T(8,128)(2,1)S(1)} %bitcast.51), channel_id=1, source_target_pairs={{0,4},{1,5},{2,6},{3,7},{4,0},{5,1},{6,2},{7,3},{8,12},{9,13},{10,... | collective-permute-start | bytes 786440 | tf_op jit(solution)/shard_map/act_gather/ppermute | solution.py:24
  16.3 10.3 %collective-permute-start.3 = (bf16[256,512]{1,0:T(8,128)(2,1)S(1)}, bf16[256,512]{1,0:T(8,128)(2,1)S(1)}, u32[]{:S(2)}, u32[]{:S(2)}) collective-permute-start(bf16[256,512]{1,0:T(8,128)(2,1)S(1)} %bitcast.52), channel_id=1, source_target_pairs={{0,2},{1,3},{2,0},{3,1},{4,6},{5,7},{6,4},{7,5},{8,10},{9,11},{10,... | collective-permute-start | bytes 786440 | tf_op jit(solution)/shard_map/act_gather/ppermute | solution.py:24
  16.9 10.3 %collective-permute-start.9 = (bf16[256,512]{1,0:T(8,128)(2,1)S(1)}, bf16[256,512]{1,0:T(8,128)(2,1)S(1)}, u32[]{:S(2)}, u32[]{:S(2)}) collective-permute-start(bf16[256,512]{1,0:T(8,128)(2,1)S(1)} %bitcast.53), channel_id=1, source_target_pairs={{0,1},{1,0},{2,3},{3,2},{4,5},{5,4},{6,7},{7,6},{8,9},{9,8},{10,11... | collective-permute-start | bytes 786440 | tf_op jit(solution)/shard_map/act_gather/ppermute | solution.py:24
  23.6 9.5 %collective-permute-start.8 = (bf16[256,512]{1,0:T(8,128)(2,1)S(1)}, bf16[256,512]{1,0:T(8,128)(2,1)S(1)}, u32[]{:S(2)}, u32[]{:S(2)}) collective-permute-start(bf16[256,512]{1,0:T(8,128)(2,1)S(1)} %collective-permute-done.7.refs_2_), channel_id=1, source_target_pairs={{0,1},{1,0},{2,3},{3,2},{4,5},{5,4},{6,7},{7,6},{8,9},{9,8},{10,11... | collective-permute-start | bytes 786440 | tf_op jit(solution)/shard_map/act_gather/ppermute | solution.py:24
  26.5 6.5 %collective-permute-start.6 = (bf16[256,512]{1,0:T(8,128)(2,1)S(1)}, bf16[256,512]{1,0:T(8,128)(2,1)S(1)}, u32[]{:S(2)}, u32[]{:S(2)}) collective-permute-start(bf16[256,512]{1,0:T(8,128)(2,1)S(1)} %collective-permute-done.5.refs_1_), channel_id=1, source_target_pairs={{0,1},{1,0},{2,3},{3,2},{4,5},{5,4},{6,7},{7,6},{8,9},{9,8},{10,11... | collective-permute-start | bytes 786440 | tf_op jit(solution)/shard_map/act_gather/ppermute | solution.py:24
  26.6 6.4 %collective-permute-start.4 = (bf16[256,512]{1,0:T(8,128)(2,1)S(1)}, bf16[256,512]{1,0:T(8,128)(2,1)S(1)}, u32[]{:S(2)}, u32[]{:S(2)}) collective-permute-start(bf16[256,512]{1,0:T(8,128)(2,1)S(1)} %collective-permute-done.3.refs_0_), channel_id=1, source_target_pairs={{0,1},{1,0},{2,3},{3,2},{4,5},{5,4},{6,7},{7,6},{8,9},{9,8},{10,11... | collective-permute-start | bytes 786440 | tf_op jit(solution)/shard_map/act_gather/ppermute | solution.py:24
  37.7 9.2 %collective-permute-start.10 = (bf16[128,1024]{1,0:T(8,128)(2,1)S(1)}, bf16[128,1024]{1,0:T(8,128)(2,1)S(1)}, u32[]{:S(2)}, u32[]{:S(2)}) collective-permute-start(bf16[128,1024]{1,0:T(8,128)(2,1)S(1)} %get-tuple-element.41.refs_0_.refs_8_), channel_id=1, source_target_pairs={{0,16},{16,24},{24,8},{8,0},{1,17},{17,25},{25,9},{9,1},{2,18},{18... | collective-permute-start | bytes 786440 | tf_op jit(solution)/shard_map/z_ring/ppermute | solution.py:34
  38.7 13.9 %collective-permute-start.11 = (bf16[128,1024]{1,0:T(8,128)(2,1)S(1)}, bf16[128,1024]{1,0:T(8,128)(2,1)S(1)}, u32[]{:S(2)}, u32[]{:S(2)}) collective-permute-start(bf16[128,1024]{1,0:T(8,128)(2,1)S(1)} %get-tuple-element.42.refs_1_.refs_9_), channel_id=1, source_target_pairs={{0,16},{16,24},{24,8},{8,0},{1,17},{17,25},{25,9},{9,1},{2,18},{18... | collective-permute-start | bytes 786440 | tf_op jit(solution)/shard_map/z_ring/ppermute | solution.py:34
  46.9 17.7 %collective-permute-start.12 = (bf16[128,1024]{1,0:T(8,128)(2,1)S(1)}, bf16[128,1024]{1,0:T(8,128)(2,1)S(1)}, u32[]{:S(2)}, u32[]{:S(2)}) collective-permute-start(bf16[128,1024]{1,0:T(8,128)(2,1)S(1)} %collective-permute-done.10.refs_2_.refs_10_), channel_id=1, source_target_pairs={{0,16},{16,24},{24,8},{8,0},{1,17},{17,25},{25,9},{9,1},{2,18},{18... | collective-permute-start | bytes 786440 | tf_op jit(solution)/shard_map/z_ring/ppermute | solution.py:34
  52.6 12.1 %collective-permute-start.13 = (bf16[128,1024]{1,0:T(8,128)(2,1)S(1)}, bf16[128,1024]{1,0:T(8,128)(2,1)S(1)}, u32[]{:S(2)}, u32[]{:S(2)}) collective-permute-start(bf16[128,1024]{1,0:T(8,128)(2,1)S(1)} %collective-permute-done.11.refs_3_.refs_11_), channel_id=1, source_target_pairs={{0,16},{16,24},{24,8},{8,0},{1,17},{17,25},{25,9},{9,1},{2,18},{18... | collective-permute-start | bytes 786440 | tf_op jit(solution)/shard_map/z_ring/ppermute | solution.py:34
  54.3 10.3 %collective-permute-start.16 = (f32[2,1024]{1,0:T(2,128)S(1)}, f32[2,1024]{1,0:T(2,128)S(1)}, u32[]{:S(2)}, u32[]{:S(2)}) collective-permute-start(f32[2,1024]{1,0:T(2,128)S(1)} %get-tuple-element.43.refs_6_), channel_id=1, source_target_pairs={{0,8},{16,0},{24,16},{8,24},{1,9},{17,1},{25,17},{9,25},{2,10},{18... | collective-permute-start | bytes 24584 | tf_op jit(solution)/shard_map/z_ring/ppermute | solution.py:34
  54.6 10.1 %collective-permute-start.15 = (f32[2,1024]{1,0:T(2,128)S(1)}, f32[2,1024]{1,0:T(2,128)S(1)}, u32[]{:S(2)}, u32[]{:S(2)}) collective-permute-start(f32[2,1024]{1,0:T(2,128)S(1)} %get-tuple-element.43.refs_6_), channel_id=1, source_target_pairs={{0,24},{16,8},{24,0},{8,16},{1,25},{17,9},{25,1},{9,17},{2,26},{18... | collective-permute-start | bytes 24584 | tf_op jit(solution)/shard_map/z_ring/ppermute | solution.py:34
  57.4 7.2 %collective-permute-start.14 = (f32[2,1024]{1,0:T(2,128)S(1)}, f32[2,1024]{1,0:T(2,128)S(1)}, u32[]{:S(2)}, u32[]{:S(2)}) collective-permute-start(f32[2,1024]{1,0:T(2,128)S(1)} %get-tuple-element.43.refs_6_), channel_id=1, source_target_pairs={{0,16},{16,24},{24,8},{8,0},{1,17},{17,25},{25,9},{9,1},{2,18},{18... | collective-permute-start | bytes 24584 | tf_op jit(solution)/shard_map/z_ring/ppermute | solution.py:34
  64.7 34.7 %copy-start.2 = (bf16[128,1024]{1,0:T(8,128)(2,1)}, bf16[128,1024]{1,0:T(8,128)(2,1)S(1)}, u32[]{:S(2)}) copy-start(bf16[128,1024]{1,0:T(8,128)(2,1)S(1)} %collective-permute-done.12.refs_4_.refs_12_) | copy-start | bytes 786436
  64.7 34.7 %copy-start.4 = (bf16[128,1024]{1,0:T(8,128)(2,1)}, bf16[128,1024]{1,0:T(8,128)(2,1)S(1)}, u32[]{:S(2)}) copy-start(bf16[128,1024]{1,0:T(8,128)(2,1)S(1)} %collective-permute-done.13.refs_5_.refs_13_) | copy-start | bytes 786436
  65.9 2.3 %collective-permute-start.17 = (f32[4,32,384]{2,1,0:T(8,128)S(1)}, f32[4,32,384]{2,1,0:T(8,128)S(1)}, u32[]{:S(2)}, u32[]{:S(2)}) collective-permute-start(f32[4,32,384]{2,1,0:T(8,128)S(1)} %get-tuple-element.45), channel_id=1, source_target_pairs={{0,1},{1,0},{2,3},{3,2},{4,5},{5,4},{6,7},{7,6},{8,9},{9,8},{10,11... | collective-permute-start | bytes 589832 | tf_op jit(solution)/shard_map/kernel/ppermute | solution.py:24
  66.0 9.4 %collective-permute-start.21 = (bf16[128,1024]{1,0:T(8,128)(2,1)S(1)}, bf16[128,1024]{1,0:T(8,128)(2,1)S(1)}, u32[]{:S(2)}, u32[]{:S(2)}) collective-permute-start(bf16[128,1024]{1,0:T(8,128)(2,1)S(1)} %collective-permute-done.12.refs_4_.refs_12_), channel_id=1, source_target_pairs={{0,16},{16,24},{24,8},{8,0},{1,17},{17,25},{25,9},{9,1},{2,18},{18... | collective-permute-start | bytes 786440 | tf_op jit(solution)/shard_map/z_ring/ppermute | solution.py:34
  66.8 13.5 %collective-permute-start.22 = (bf16[128,1024]{1,0:T(8,128)(2,1)S(1)}, bf16[128,1024]{1,0:T(8,128)(2,1)S(1)}, u32[]{:S(2)}, u32[]{:S(2)}) collective-permute-start(bf16[128,1024]{1,0:T(8,128)(2,1)S(1)} %collective-permute-done.13.refs_5_.refs_13_), channel_id=1, source_target_pairs={{0,16},{16,24},{24,8},{8,0},{1,17},{17,25},{25,9},{9,1},{2,18},{18... | collective-permute-start | bytes 786440 | tf_op jit(solution)/shard_map/z_ring/ppermute | solution.py:34
  68.3 4.4 %collective-permute-start.18 = (f32[32,384]{1,0:T(8,128)S(1)}, f32[32,384]{1,0:T(8,128)S(1)}, u32[]{:S(2)}, u32[]{:S(2)}) collective-permute-start(f32[32,384]{1,0:T(8,128)S(1)} %get-tuple-element.90), channel_id=1, source_target_pairs={{0,2},{1,3},{2,0},{3,1},{4,6},{5,7},{6,4},{7,5},{8,10},{9,11},{10,... | collective-permute-start | bytes 147464 | tf_op jit(solution)/shard_map/kernel/ppermute | solution.py:24
  69.8 5.0 %collective-permute-start.20 = (f32[32,384]{1,0:T(8,128)S(1)}, f32[32,384]{1,0:T(8,128)S(1)}, u32[]{:S(2)}, u32[]{:S(2)}) collective-permute-start(f32[32,384]{1,0:T(8,128)S(1)} %get-tuple-element.91), channel_id=1, source_target_pairs={{0,6},{1,7},{2,4},{3,5},{4,2},{5,3},{6,0},{7,1},{8,14},{9,15},{10,... | collective-permute-start | bytes 147464 | tf_op jit(solution)/shard_map/kernel/ppermute | solution.py:24
  71.3 4.1 %collective-permute-start.19 = (f32[32,384]{1,0:T(8,128)S(1)}, f32[32,384]{1,0:T(8,128)S(1)}, u32[]{:S(2)}, u32[]{:S(2)}) collective-permute-start(f32[32,384]{1,0:T(8,128)S(1)} %get-tuple-element.92), channel_id=1, source_target_pairs={{0,4},{1,5},{2,6},{3,7},{4,0},{5,1},{6,2},{7,3},{8,12},{9,13},{10,... | collective-permute-start | bytes 147464 | tf_op jit(solution)/shard_map/kernel/ppermute | solution.py:24
  75.4 24.0 %copy-start.9 = (bf16[128,1024]{1,0:T(8,128)(2,1)}, bf16[128,1024]{1,0:T(8,128)(2,1)S(1)}, u32[]{:S(2)}) copy-start(bf16[128,1024]{1,0:T(8,128)(2,1)S(1)} %collective-permute-done.21.refs_14_) | copy-start | bytes 786436
  81.6 4.7 %collective-permute-start.25 = (bf16[32,384]{1,0:T(8,128)(2,1)S(1)}, bf16[32,384]{1,0:T(8,128)(2,1)S(1)}, u32[]{:S(2)}, u32[]{:S(2)}) collective-permute-start(bf16[32,384]{1,0:T(8,128)(2,1)S(1)} %get-tuple-element.94), channel_id=1, source_target_pairs={{0,8},{16,0},{24,16},{8,24},{1,9},{17,1},{25,17},{9,25},{2,10},{18... | collective-permute-start | bytes 73736 | tf_op jit(solution)/shard_map/kernel/ppermute | solution.py:34
  83.1 5.7 %collective-permute-start.24 = (bf16[32,384]{1,0:T(8,128)(2,1)S(1)}, bf16[32,384]{1,0:T(8,128)(2,1)S(1)}, u32[]{:S(2)}, u32[]{:S(2)}) collective-permute-start(bf16[32,384]{1,0:T(8,128)(2,1)S(1)} %get-tuple-element.94), channel_id=1, source_target_pairs={{0,24},{16,8},{24,0},{8,16},{1,25},{17,9},{25,1},{9,17},{2,26},{18... | collective-permute-start | bytes 73736 | tf_op jit(solution)/shard_map/kernel/ppermute | solution.py:34
  84.7 4.1 %collective-permute-start.23 = (bf16[32,384]{1,0:T(8,128)(2,1)S(1)}, bf16[32,384]{1,0:T(8,128)(2,1)S(1)}, u32[]{:S(2)}, u32[]{:S(2)}) collective-permute-start(bf16[32,384]{1,0:T(8,128)(2,1)S(1)} %get-tuple-element.94), channel_id=1, source_target_pairs={{0,16},{16,24},{24,8},{8,0},{1,17},{17,25},{25,9},{9,1},{2,18},{18... | collective-permute-start | bytes 73736 | tf_op jit(solution)/shard_map/kernel/ppermute | solution.py:34
  88.8 5.7 %collective-permute-start.31 = (bf16[4,32,384]{2,1,0:T(8,128)(2,1)S(1)}, bf16[4,32,384]{2,1,0:T(8,128)(2,1)S(1)}, u32[]{:S(2)}, u32[]{:S(2)}) collective-permute-start(bf16[4,32,384]{2,1,0:T(8,128)(2,1)S(1)} %pad_maximum_fusion.3.refs_0_), channel_id=1, source_target_pairs={{0,6},{1,7},{2,4},{3,5},{4,2},{5,3},{6,0},{7,1},{8,14},{9,15},{10,... | collective-permute-start | bytes 294920 | tf_op jit(solution)/shard_map/kernel/ppermute | solution.py:24
  90.6 5.0 %collective-permute-start.29 = (bf16[4,32,384]{2,1,0:T(8,128)(2,1)S(1)}, bf16[4,32,384]{2,1,0:T(8,128)(2,1)S(1)}, u32[]{:S(2)}, u32[]{:S(2)}) collective-permute-start(bf16[4,32,384]{2,1,0:T(8,128)(2,1)S(1)} %pad_maximum_fusion.3.refs_0_), channel_id=1, source_target_pairs={{0,4},{1,5},{2,6},{3,7},{4,0},{5,1},{6,2},{7,3},{8,12},{9,13},{10,... | collective-permute-start | bytes 294920 | tf_op jit(solution)/shard_map/kernel/ppermute | solution.py:24
  91.8 4.6 %collective-permute-start.27 = (bf16[4,32,384]{2,1,0:T(8,128)(2,1)S(1)}, bf16[4,32,384]{2,1,0:T(8,128)(2,1)S(1)}, u32[]{:S(2)}, u32[]{:S(2)}) collective-permute-start(bf16[4,32,384]{2,1,0:T(8,128)(2,1)S(1)} %pad_maximum_fusion.3.refs_0_), channel_id=1, source_target_pairs={{0,2},{1,3},{2,0},{3,1},{4,6},{5,7},{6,4},{7,5},{8,10},{9,11},{10,... | collective-permute-start | bytes 294920 | tf_op jit(solution)/shard_map/kernel/ppermute | solution.py:24
  92.4 5.7 %collective-permute-start.26 = (bf16[4,32,384]{2,1,0:T(8,128)(2,1)S(1)}, bf16[4,32,384]{2,1,0:T(8,128)(2,1)S(1)}, u32[]{:S(2)}, u32[]{:S(2)}) collective-permute-start(bf16[4,32,384]{2,1,0:T(8,128)(2,1)S(1)} %pad_maximum_fusion.3.refs_0_), channel_id=1, source_target_pairs={{0,1},{1,0},{2,3},{3,2},{4,5},{5,4},{6,7},{7,6},{8,9},{9,8},{10,11... | collective-permute-start | bytes 294920 | tf_op jit(solution)/shard_map/kernel/ppermute | solution.py:24
  94.6 4.2 %collective-permute-start.32 = (bf16[4,32,384]{2,1,0:T(8,128)(2,1)S(1)}, bf16[4,32,384]{2,1,0:T(8,128)(2,1)S(1)}, u32[]{:S(2)}, u32[]{:S(2)}) collective-permute-start(bf16[4,32,384]{2,1,0:T(8,128)(2,1)S(1)} %collective-permute-done.31.refs_6_), channel_id=1, source_target_pairs={{0,1},{1,0},{2,3},{3,2},{4,5},{5,4},{6,7},{7,6},{8,9},{9,8},{10,11... | collective-permute-start | bytes 294920 | tf_op jit(solution)/shard_map/kernel/ppermute | solution.py:24
  95.6 3.8 %collective-permute-start.30 = (bf16[4,32,384]{2,1,0:T(8,128)(2,1)S(1)}, bf16[4,32,384]{2,1,0:T(8,128)(2,1)S(1)}, u32[]{:S(2)}, u32[]{:S(2)}) collective-permute-start(bf16[4,32,384]{2,1,0:T(8,128)(2,1)S(1)} %collective-permute-done.29.refs_4_), channel_id=1, source_target_pairs={{0,1},{1,0},{2,3},{3,2},{4,5},{5,4},{6,7},{7,6},{8,9},{9,8},{10,11... | collective-permute-start | bytes 294920 | tf_op jit(solution)/shard_map/kernel/ppermute | solution.py:24
  96.5 3.5 %collective-permute-start.28 = (bf16[4,32,384]{2,1,0:T(8,128)(2,1)S(1)}, bf16[4,32,384]{2,1,0:T(8,128)(2,1)S(1)}, u32[]{:S(2)}, u32[]{:S(2)}) collective-permute-start(bf16[4,32,384]{2,1,0:T(8,128)(2,1)S(1)} %collective-permute-done.27.refs_2_), channel_id=1, source_target_pairs={{0,1},{1,0},{2,3},{3,2},{4,5},{5,4},{6,7},{7,6},{8,9},{9,8},{10,11... | collective-permute-start | bytes 294920 | tf_op jit(solution)/shard_map/kernel/ppermute | solution.py:24
  120.8 5.7 %collective-permute-start.33 = (bf16[4,272,512]{2,1,0:T(8,128)(2,1)}, bf16[4,272,512]{2,1,0:T(8,128)(2,1)S(1)}, u32[]{:S(2)}, u32[]{:S(2)}) collective-permute-start(bf16[4,272,512]{2,1,0:T(8,128)(2,1)} %d_act_matmul.3), channel_id=1, source_target_pairs={{0,1},{1,0},{2,3},{3,2},{4,5},{5,4},{6,7},{7,6},{8,9},{9,8},{10,11... | collective-permute-start | bytes 3342344 | tf_op jit(solution)/shard_map/d_act/ppermute | solution.py:24
  122.4 21.4 %copy-start.36 = (bf16[256,512]{1,0:T(8,128)(2,1)}, bf16[256,512]{1,0:T(8,128)(2,1)S(1)}, u32[]{:S(2)}) copy-start(bf16[256,512]{1,0:T(8,128)(2,1)S(1)} %get-tuple-element.68) | copy-start | bytes 786436
  122.4 21.4 %collective-permute-start.39 = (bf16[256,512]{1,0:T(8,128)(2,1)S(1)}, bf16[256,512]{1,0:T(8,128)(2,1)S(1)}, u32[]{:S(2)}, u32[]{:S(2)}) collective-permute-start(bf16[256,512]{1,0:T(8,128)(2,1)S(1)} %get-tuple-element.86), channel_id=1, source_target_pairs={{0,8},{16,0},{24,16},{8,24},{1,9},{17,1},{25,17},{9,25},{2,10},{18... | collective-permute-start | bytes 786440 | tf_op jit(solution)/shard_map/grad_weight/ppermute | solution.py:34
  123.5 20.3 %collective-permute-start.38 = (bf16[256,512]{1,0:T(8,128)(2,1)S(1)}, bf16[256,512]{1,0:T(8,128)(2,1)S(1)}, u32[]{:S(2)}, u32[]{:S(2)}) collective-permute-start(bf16[256,512]{1,0:T(8,128)(2,1)S(1)} %get-tuple-element.87), channel_id=1, source_target_pairs={{0,24},{16,8},{24,0},{8,16},{1,25},{17,9},{25,1},{9,17},{2,26},{18... | collective-permute-start | bytes 786440 | tf_op jit(solution)/shard_map/grad_weight/ppermute | solution.py:34
  125.1 18.7 %collective-permute-start.37 = (bf16[256,512]{1,0:T(8,128)(2,1)S(1)}, bf16[256,512]{1,0:T(8,128)(2,1)S(1)}, u32[]{:S(2)}, u32[]{:S(2)}) collective-permute-start(bf16[256,512]{1,0:T(8,128)(2,1)S(1)} %get-tuple-element.88), channel_id=1, source_target_pairs={{0,16},{16,24},{24,8},{8,0},{1,17},{17,25},{25,9},{9,1},{2,18},{18... | collective-permute-start | bytes 786440 | tf_op jit(solution)/shard_map/grad_weight/ppermute | solution.py:34
  145.0 3.5 %collective-permute-start.40 = (bf16[2,512,512]{2,1,0:T(8,128)(2,1)}, bf16[2,512,512]{2,1,0:T(8,128)(2,1)}, u32[]{:S(2)}, u32[]{:S(2)}) collective-permute-start(bf16[2,512,512]{2,1,0:T(8,128)(2,1)} %pad_maximum_fusion.2), channel_id=1, source_target_pairs={{0,1},{1,0},{2,3},{3,2},{4,5},{5,4},{6,7},{7,6},{8,9},{9,8},{10,11... | collective-permute-start | bytes 3145736 | tf_op jit(solution)/shard_map/grad_weight/ppermute | solution.py:24
  145.0 10.1 %collective-permute-start.34 = (bf16[272,512]{1,0:T(8,128)(2,1)S(1)}, bf16[272,512]{1,0:T(8,128)(2,1)S(1)}, u32[]{:S(2)}, u32[]{:S(2)}) collective-permute-start(bf16[272,512]{1,0:T(8,128)(2,1)S(1)} %copy-done.34), channel_id=1, source_target_pairs={{0,2},{1,3},{2,0},{3,1},{4,6},{5,7},{6,4},{7,5},{8,10},{9,11},{10,... | collective-permute-start | bytes 835592 | tf_op jit(solution)/shard_map/d_act/ppermute | solution.py:24
  146.4 14.7 %collective-permute-start.35 = (bf16[272,512]{1,0:T(8,128)(2,1)S(1)}, bf16[272,512]{1,0:T(8,128)(2,1)S(1)}, u32[]{:S(2)}, u32[]{:S(2)}) collective-permute-start(bf16[272,512]{1,0:T(8,128)(2,1)S(1)} %copy-done.32), channel_id=1, source_target_pairs={{0,4},{1,5},{2,6},{3,7},{4,0},{5,1},{6,2},{7,3},{8,12},{9,13},{10,... | collective-permute-start | bytes 835592 | tf_op jit(solution)/shard_map/d_act/ppermute | solution.py:24
  147.2 13.9 %collective-permute-start.36 = (bf16[272,512]{1,0:T(8,128)(2,1)S(1)}, bf16[272,512]{1,0:T(8,128)(2,1)S(1)}, u32[]{:S(2)}, u32[]{:S(2)}) collective-permute-start(bf16[272,512]{1,0:T(8,128)(2,1)S(1)} %copy-done.30), channel_id=1, source_target_pairs={{0,6},{1,7},{2,4},{3,5},{4,2},{5,3},{6,0},{7,1},{8,14},{9,15},{10,... | collective-permute-start | bytes 835592 | tf_op jit(solution)/shard_map/d_act/ppermute | solution.py:24
  161.8 9.1 %collective-permute-start.43 = (f32[8,512]{1,0:T(8,128)S(1)}, f32[8,512]{1,0:T(8,128)S(1)}, u32[]{:S(2)}, u32[]{:S(2)}) collective-permute-start(f32[8,512]{1,0:T(8,128)S(1)} %pad_maximum_fusion.4), channel_id=1, source_target_pairs={{0,8},{8,16},{16,24},{24,0},{1,9},{9,17},{17,25},{25,1},{2,10},{10... | collective-permute-start | bytes 49160 | tf_op jit(solution)/shard_map/norm_backward/ppermute | solution.py:42
  167.4 4.6 %collective-permute-start.42 = (f32[8,512]{1,0:T(8,128)S(1)}, f32[8,512]{1,0:T(8,128)S(1)}, u32[]{:S(2)}, u32[]{:S(2)}) collective-permute-start(f32[8,512]{1,0:T(8,128)S(1)} %pad_maximum_fusion.4), channel_id=1, source_target_pairs={{0,16},{8,24},{16,0},{24,8},{1,17},{9,25},{17,1},{25,9},{2,18},{10... | collective-permute-start | bytes 49160 | tf_op jit(solution)/shard_map/norm_backward/ppermute | solution.py:42
  168.0 4.3 %collective-permute-start.41 = (f32[8,512]{1,0:T(8,128)S(1)}, f32[8,512]{1,0:T(8,128)S(1)}, u32[]{:S(2)}, u32[]{:S(2)}) collective-permute-start(f32[8,512]{1,0:T(8,128)S(1)} %pad_maximum_fusion.4), channel_id=1, source_target_pairs={{0,24},{8,0},{16,8},{24,16},{1,25},{9,1},{17,9},{25,17},{2,26},{10... | collective-permute-start | bytes 49160 | tf_op jit(solution)/shard_map/norm_backward/ppermute | solution.py:42
  (38 other events, 106.5 us)

commit v5 on v4

v5 whole, which is shorter than its diff:
```python
import functools

import jax
import jax.numpy as jnp
from jax import lax
from jax.experimental import pallas as pl
from jax.experimental.pallas import tpu as pltpu
from jax.sharding import PartitionSpec as P

eps_norm = 1e-05
eps_std = 0.0001
f32 = jnp.float32
bf16 = jnp.bfloat16
MIB = 1024 * 1024


def gelu_slope(preactivation):
    value, pullback = jax.vjp(lambda t: jax.nn.gelu(t, approximate=True), preactivation)
    return pullback(jnp.ones_like(value))[0]


def xor_send(x, axis, k):
    n = lax.axis_size(axis)
    return lax.ppermute(x, axis, [(i, i ^ k) for i in range(n)])


def ring_order(n):
    return list(range(0, n, 2)) + list(range(1, n, 2))[::-1]


def ring_send(x, axis, d):
    order = ring_order(lax.axis_size(axis))
    n = len(order)
    return lax.ppermute(x, axis, [(order[i], order[(i + d) % n]) for i in range(n)])


def exchange(x, axis):
    n = lax.axis_size(axis)
    me = lax.axis_index(axis)
    slots = [x]
    for d in range(1, n):
        slots.append(lax.ppermute(x, axis, [(i, (i + d) % n) for i in range(n)]))
    ordered = []
    for a in range(n):
        value = slots[0]
        for d in range(1, n):
            value = jnp.where((me - a) % n == d, slots[d], value)
        ordered.append(value)
    return ordered


def params(limit):
    return pltpu.CompilerParams(vmem_limit_bytes=limit * MIB)


def cost(flops, moved):
    return pl.CostEstimate(flops=flops, bytes_accessed=moved, transcendentals=0)


IN_SMEM = pl.BlockSpec(memory_space=pltpu.SMEM)
IN_VMEM = pl.BlockSpec(memory_space=pltpu.VMEM)
ANYWHERE = pl.BlockSpec(memory_space=pl.ANY)
LOADS = 8


def load_kernel(w_ref, out_ref, sems):
    step = w_ref.shape[0] // LOADS
    copies = [
        pltpu.make_async_copy(
            w_ref.at[pl.ds(i * step, step)], out_ref.at[pl.ds(i * step, step)], sems.at[i]
        )
        for i in range(LOADS)
    ]
    for copy in copies:
        copy.start()
    for copy in copies:
        copy.wait()


def load_call(weight):
    return pl.pallas_call(
        load_kernel,
        out_shape=pltpu.VMEM(weight.shape, weight.dtype),
        in_specs=[ANYWHERE],
        out_specs=IN_VMEM,
        scratch_shapes=[pltpu.SemaphoreType.DMA((LOADS,))],
        compiler_params=params(4),
        cost_estimate=cost(0, 4 * weight.size),
        name="weight_load",
    )(pltpu.with_memory_space_constraint(weight, pltpu.HBM))


def weight_rows(index_ref, w_ref, j, width):
    return w_ref[pl.ds(pl.multiple_of(index_ref[j] * width, width), width), :]


def z_kernel(count, first, last, local_rows, index_ref, *refs):
    pieces, rest = refs[:count], list(refs[count:])
    w_ref = rest.pop(0)
    total = None if first else rest.pop(0)[...]
    width = pieces[0].shape[1]
    for j in range(count):
        part = jnp.dot(
            pieces[j][...], weight_rows(index_ref, w_ref, j, width), preferred_element_type=f32
        )
        total = part if total is None else total + part
    if not last:
        rest[0][...] = total
        return
    z = total.astype(bf16)
    *z_refs, sum_ref = rest
    for v, ref in enumerate(z_refs):
        mine = z[v * local_rows : (v + 1) * local_rows]
        ref[...] = mine
        sum_ref[v : v + 1, :] = jnp.sum(mine.astype(f32), axis=0, keepdims=True)


def z_call(index, pieces, weight, before, last, local_rows):
    count = len(pieces)
    tall, width = pieces[0].shape
    columns = weight.shape[1]
    operands = [index] + list(pieces) + [weight] + ([] if before is None else [before])
    if last:
        groups = tall // local_rows
        out_shape = (jax.ShapeDtypeStruct((local_rows, columns), bf16),) * groups
        out_shape += (jax.ShapeDtypeStruct((groups, columns), f32),)
    else:
        out_shape = jax.ShapeDtypeStruct((tall, columns), f32)
    return pl.pallas_call(
        functools.partial(z_kernel, count, before is None, last, local_rows),
        out_shape=out_shape,
        in_specs=[IN_SMEM] + [IN_VMEM] * (len(operands) - 1),
        out_specs=jax.tree.map(lambda _: IN_VMEM, out_shape),
        compiler_params=params(8),
        cost_estimate=cost(2 * tall * width * columns * count, 2 * tall * columns),
        name="z_matmul",
    )(*operands)


def strip_kernel(n_slots, n_sums, rows, n_col, index_ref, *refs):
    z_refs, sum_refs = refs[: 2 * n_slots], refs[2 * n_slots : 2 * n_slots + n_sums]
    even_ref, odd_ref, strip = refs[2 * n_slots + n_sums :]
    local_rows = z_refs[0].shape[0]
    mean = sum(s[...] for s in sum_refs) / rows
    for v in range(2):
        here = pl.ds(v * local_rows, local_rows)
        rounded = [(z[...].astype(f32) - mean[v : v + 1]).astype(bf16) for z in z_refs[v::2]]
        for u in range(n_slots):
            strip[here, pl.ds(u * local_rows, local_rows)] = lax.dot_general(
                rounded[0], rounded[u], (((1,), (1,)), ((), ())), preferred_element_type=f32
            )
    part = 2 * local_rows // n_col
    for k in range(n_col):
        start = pl.multiple_of(index_ref[k] * part, part)
        (odd_ref if k % 2 else even_ref)[k // 2] = strip[pl.ds(start, part), :]


def strip_call(index, z_slots, sums, rows, n_col):
    local_rows, columns = z_slots[0][0].shape
    tall = 2 * local_rows
    wide = len(z_slots) * local_rows
    part = jax.ShapeDtypeStruct((n_col // 2, tall // n_col, wide), f32)
    operands = [index] + [z for slot in z_slots for z in slot] + list(sums)
    return pl.pallas_call(
        functools.partial(strip_kernel, len(z_slots), len(sums), rows, n_col),
        out_shape=(part, part),
        in_specs=[IN_SMEM] + [IN_VMEM] * (len(operands) - 1),
        out_specs=(IN_VMEM, IN_VMEM),
        scratch_shapes=[pltpu.VMEM((tall, wide), f32)],
        compiler_params=params(10),
        cost_estimate=cost(2 * tall * wide * columns, 2 * tall * columns * len(z_slots)),
        name="kernel_strip",
    )(*operands)


def dz_kernel(n_batch, n_col, tile, constants, index_ref, *refs):
    coef, hinge_coef, inv_coef, inv_share, hinge_share, diag_share = constants
    strip_refs = refs[:n_col]
    z_refs = refs[n_col : n_col + 2 * n_batch]
    dz_ref, share_ref, strips, full, centred = refs[n_col + 2 * n_batch :]
    local_rows, columns = z_refs[0].shape
    rows = local_rows * n_batch
    reach = n_batch // 2
    share_ref[...] = jnp.zeros_like(share_ref)
    part = 2 * local_rows // n_col
    for k in range(n_col):
        start = pl.multiple_of(index_ref[k] * part, part)
        for s in range(n_batch):
            strips[s, pl.ds(start, part), :] = strip_refs[k][s].astype(f32)
    for v in range(2):
        for s in range(n_batch):
            here = pl.ds(s * local_rows, local_rows)
            for u in range(reach + 1):
                t = (s + u) % n_batch
                there = pl.ds(t * local_rows, local_rows)
                block = strips[
                    s, pl.ds(v * local_rows, local_rows), pl.ds(u * local_rows, local_rows)
                ]
                full[v, here, there] = block.astype(bf16)
                if 0 < u < n_batch - reach:
                    full[v, there, here] = jnp.transpose(block).astype(bf16)

    def one_tile(j, carry):
        here = pl.ds(pl.multiple_of(j * tile, tile), tile)
        share = jnp.zeros((1, 1), f32)
        grads = []
        z_views = []
        for v in range(2):
            zf = jnp.concatenate([z[:, here].astype(f32) for z in z_refs[v::2]], axis=0)
            z_views.append(zf)
            zc = zf - jnp.sum(zf, axis=0, keepdims=True) / rows
            std = jnp.sqrt(jnp.sum(zc * zc, axis=0, keepdims=True) / (rows - 1) + eps_std)
            zcb = zc.astype(bf16)
            centred[...] = zcb
            rounded = zcb.astype(f32)
            diag = jnp.sum(rounded * rounded, axis=0, keepdims=True)
            moved = jnp.dot(full[v], centred[...], preferred_element_type=f32)
            pull = jnp.where(std < 1.0, hinge_coef, 0.0) / std
            summed = coef * (moved - rounded * diag) - zc * pull
            grads.append(summed - jnp.sum(summed, axis=0, keepdims=True) / rows)
            share += hinge_share * jnp.sum(jnp.maximum(1.0 - std, 0.0), axis=1, keepdims=True)
            share -= diag_share * jnp.sum(diag * diag, axis=1, keepdims=True)
        diff = z_views[0] - z_views[1]
        share += inv_share * jnp.sum(
            jnp.sum(diff * diff, axis=0, keepdims=True), axis=1, keepdims=True
        )
        share_ref[...] += jnp.broadcast_to(share, share_ref.shape)
        dz_ref[0, :, here] = (grads[0] + inv_coef * diff).astype(bf16)
        dz_ref[1, :, here] = (grads[1] - inv_coef * diff).astype(bf16)
        return carry

    lax.fori_loop(0, columns // tile, one_tile, 0)


def dz_call(index, strips, z_slots, constants):
    n_col, n_batch = len(strips), len(z_slots)
    local_rows, columns = z_slots[0][0].shape
    tall = 2 * local_rows
    rows = local_rows * n_batch
    tile = min(256, columns)
    operands = [index] + list(strips) + [z for slot in z_slots for z in slot]
    return pl.pallas_call(
        functools.partial(dz_kernel, n_batch, n_col, tile, constants),
        out_shape=(
            jax.ShapeDtypeStruct((2, rows, columns), bf16),
            jax.ShapeDtypeStruct((8, 128), f32),
        ),
        in_specs=[IN_SMEM] + [IN_VMEM] * (len(operands) - 1),
        out_specs=(IN_VMEM, IN_VMEM),
        scratch_shapes=[
            pltpu.VMEM((n_batch, tall, strips[0].shape[2]), f32),
            pltpu.VMEM((2, rows, rows), bf16),
            pltpu.VMEM((rows, tile), bf16),
        ],
        compiler_params=params(24),
        cost_estimate=cost(4 * rows * rows * columns, 8 * rows * columns),
        name="embedding_gradient",
    )(*operands)


EXTRA = 16


def share_rows(share, width, kind):
    high = share.astype(bf16).astype(f32)
    middle = (share - high).astype(bf16).astype(f32)
    low = share - high - middle
    row = lax.broadcasted_iota(jnp.int32, (EXTRA, width), 0)
    rows = jnp.where(row == 0, high, jnp.where(row == 1, middle, jnp.where(row == 2, low, 0.0)))
    return rows.astype(kind)


def share_of(rows):
    return rows[0:1].astype(f32) + rows[1:2].astype(f32) + rows[2:3].astype(f32)


def d_act_kernel(count, adds, index_ref, dz_ref, share_ref, w_ref, *refs):
    local_rows, columns = dz_ref.shape[1] // adds[1], dz_ref.shape[2]
    tall = 2 * local_rows
    dz = jnp.concatenate([dz_ref[0, :local_rows], dz_ref[1, :local_rows]], axis=0)
    width = w_ref.shape[0] // adds[2]
    share = share_ref[0:1, 0:1]
    for j in range(count):
        part = lax.dot_general(
            dz,
            weight_rows(index_ref, w_ref, j, width),
            (((1,), (1,)), ((), ())),
            preferred_element_type=f32,
        )
        if not adds[0]:
            refs[0][j, :tall] = part.astype(refs[0].dtype)
            refs[0][j, tall:] = share_rows(share, width, refs[0].dtype)
        else:
            got = refs[0]
            out_ref = refs[j + 1]
            slot = (j + 1) % count
            out_ref[:tall] = (part + got[slot, :tall].astype(f32)).astype(out_ref.dtype)
            whole_share = share + share_of(got[slot, tall:])[:, 0:1]
            out_ref[tall:] = share_rows(whole_share, width, out_ref.dtype)


def d_act_call(index, dz, share, weight, n_batch, n_col, got):
    columns = weight.shape[1]
    width = weight.shape[0] // n_col
    tall = 2 * dz.shape[1] // n_batch
    count = n_col // 2
    operands = [index, dz, share, weight] + ([] if got is None else [got])
    if got is None:
        out_shape = (jax.ShapeDtypeStruct((count, tall + EXTRA, width), bf16),)
    else:
        out_shape = (jax.ShapeDtypeStruct((tall + EXTRA, width), bf16),) * (count - 1)
        out_shape += (jax.ShapeDtypeStruct((tall + EXTRA, width), f32),)
    return pl.pallas_call(
        functools.partial(d_act_kernel, count, (got is not None, n_batch, n_col)),
        out_shape=out_shape,
        in_specs=[IN_SMEM] + [IN_VMEM] * (len(operands) - 1),
        out_specs=(IN_VMEM,) * len(out_shape),
        compiler_params=params(8),
        cost_estimate=cost(2 * tall * width * columns * count, 2 * count * width * tall),
        name="d_act_matmul",
    )(*operands)


def weight_grad_kernel(groups, half, tile, place_ref, *refs):
    n_far, aliased = groups[-2:]
    near = [refs[g * half : (g + 1) * half] for g in range(3)]
    arrived = refs[3 * half : 3 * half + n_far]
    dz_ref = refs[3 * half + n_far]
    out_ref, act, product, sems = refs[3 * half + n_far + 1 + aliased :]
    local_rows = near[0][0].shape[0] // 2
    rows = dz_ref.shape[1]
    for e in range(half):

        @pl.when(place_ref[0] == e)
        def _():
            act[pl.ds(0, local_rows)] = near[0][e][:local_rows]
            act[pl.ds(rows, local_rows)] = near[0][e][local_rows:]
            at = local_rows
            for group in near[1:]:
                size = group[e].shape[0]
                act[pl.ds(at, size)] = group[e][...]
                at += size

    for s in range(n_far):
        act[pl.ds(rows + (s + 1) * local_rows, local_rows)] = arrived[s][...]
    width = act.shape[1]
    copies = []
    for i in range(width // tile):
        total = None
        for v in range(2):
            part = lax.dot_general(
                act[pl.ds(v * rows, rows), pl.ds(i * tile, tile)],
                dz_ref[v],
                (((0,), (0,)), ((), ())),
                preferred_element_type=f32,
            )
            total = part if total is None else total + part
        product[pl.ds(i * tile, tile)] = total
        start = pl.multiple_of(place_ref[1] * width + i * tile, tile)
        copies.append(
            pltpu.make_async_copy(
                product.at[pl.ds(i * tile, tile)], out_ref.at[pl.ds(start, tile)], sems.at[i]
            )
        )
        copies[-1].start()
    for copy in copies:
        copy.wait()


def weight_grad_call(place, near, arrived, dz, features, before):
    half = len(near[0])
    width = near[0][0].shape[1]
    _, rows, columns = dz.shape
    tile = min(256, width)
    operands = [place] + [x for group in near for x in group] + list(arrived) + [dz]
    specs = [IN_SMEM] + [IN_VMEM] * (len(operands) - 1)
    aliases = {}
    if before is not None:
        aliases = {len(operands): 0}
        operands.append(before)
        specs.append(ANYWHERE)
    return pl.pallas_call(
        functools.partial(
            weight_grad_kernel, (len(arrived), int(before is not None)), half, tile
        ),
        out_shape=jax.ShapeDtypeStruct((features, columns), f32),
        in_specs=specs,
        out_specs=ANYWHERE,
        scratch_shapes=[
            pltpu.VMEM((2 * rows, width), bf16),
            pltpu.VMEM((width, columns), f32),
            pltpu.SemaphoreType.DMA((width // tile,)),
        ],
        input_output_aliases=aliases,
        compiler_params=params(12),
        cost_estimate=cost(4 * rows * width * columns, 4 * width * columns),
        name="weight_gradient",
    )(*operands)


def gather_pieces(x, n_col):
    pieces = {0: x}
    for k in range(2, n_col, 2):
        pieces[k] = xor_send(x, "col", k)
    for k in range(0, n_col, 2):
        pieces[k + 1] = xor_send(pieces[k], "col", 1)
    return pieces


def shards(views, norm_scale_gain, norm_shift_bias, weight):
    n_batch = lax.axis_size("batch")
    n_col = lax.axis_size("col")
    b = lax.axis_index("batch")
    c = lax.axis_index("col")
    n_view, local_rows, width = views.shape
    features, columns = weight.shape
    E = columns * n_col
    rows = local_rows * n_batch
    tall = n_view * local_rows
    reach = n_batch // 2
    scale = rows * E / 128.0
    denom = float((rows - 1) ** 2 * E)
    evens = list(range(0, n_col, 2))
    odds = [k + 1 for k in evens]
    far = evens[1:]

    def places(ks):
        return jnp.stack([c ^ k for k in ks]).astype(jnp.int32)

    with jax.named_scope("weight_load"):
        held_weight = load_call(weight)
    with jax.named_scope("norm_stats"):
        hidden = views.astype(f32)
        local_mean = jnp.mean(hidden, axis=1)
        local_centred = hidden - local_mean[:, None, :]
        local_spread = jnp.sum(local_centred * local_centred, axis=1)
        stats = exchange(jnp.concatenate([local_mean, local_spread]), "batch")
        mean = sum(s[:n_view] for s in stats) / n_batch
        spread = sum(s[n_view:] + local_rows * jnp.square(s[:n_view] - mean) for s in stats)
        var = spread / rows
        inverse_deviation = (1.0 / jnp.sqrt(var + eps_norm))[:, None, :]
        normalised = (hidden - mean[:, None, :]) * inverse_deviation
        preactivation = norm_scale_gain * normalised + norm_shift_bias
        act = jax.nn.gelu(preactivation, approximate=True).astype(bf16)
    with jax.named_scope("act_gather"):
        pieces = gather_pieces(act.reshape(tall, width), n_col)
        ring = [act[0]]
        for _ in range(1, n_batch):
            ring.append(ring_send(ring[-1], "batch", 1))
        ring = lax.optimization_barrier(ring)
        near_pieces = gather_pieces(jnp.concatenate(ring[1 : reach + 1]), n_col)
        last_pieces = gather_pieces(jnp.concatenate(ring[reach + 1 :]), n_col)
    with jax.named_scope("z"):

        def z_of(source, groups):
            total = None
            for i, ks in enumerate(groups):
                total = z_call(
                    places(ks),
                    [source[k] for k in ks],
                    held_weight,
                    total,
                    i == len(groups) - 1,
                    local_rows,
                )
            return total

        z_own0, z_own1, z_sum = z_of(pieces, [[0, 1], far, [k + 1 for k in far]])
        *z_near, _ = z_of(near_pieces, [evens, odds])
        *z_last, _ = z_of(last_pieces, [evens, odds])
    with jax.named_scope("z_ring"):
        z_ring = [z_own1]
        for _ in range(1, n_batch):
            z_ring.append(ring_send(z_ring[-1], "batch", 1))
        sums = [z_sum] + [ring_send(z_sum, "batch", d) for d in range(1, n_batch)]
        slots = [list(pair) for pair in zip([z_own0] + z_near + z_last, z_ring)]
    with jax.named_scope("kernel"):
        everyone = places(range(n_col))
        even_part, odd_part = strip_call(everyone, slots[: reach + 1], sums, rows, n_col)
        even_part = even_part + xor_send(odd_part, "col", 1)
        strip = even_part[0]
        for k in far:
            strip = strip + xor_send(even_part[k // 2], "col", k)
        strip, slots[reach + 1 :] = lax.optimization_barrier((strip, slots[reach + 1 :]))
        block = lax.broadcasted_iota(jnp.int32, (1, strip.shape[1]), 1) // local_rows
        twice = jnp.where((block > 0) & (block < n_batch - reach), 2.0, 1.0)
        block_share = jnp.sum(strip * strip * twice) / denom
        mine = strip.astype(bf16)
        mine = jnp.stack([mine] + [ring_send(mine, "batch", d) for d in range(1, n_batch)])
        strips = gather_pieces(mine, n_col)
        strips, held_back = lax.optimization_barrier((strips, [pieces[k] for k in evens]))
    with jax.named_scope("dz"):
        constants = (
            4.0 * scale / denom,
            25.0 * scale / (2.0 * E * (rows - 1)),
            50.0 * scale / (rows * E),
            25.0 / (rows * E) / n_batch,
            25.0 / (2 * E) / n_batch,
            1.0 / denom / n_batch,
        )
        dz, share = dz_call(everyone, [strips[k] for k in range(n_col)], slots, constants)
        share = share + block_share
    with jax.named_scope("d_act"):
        (away,) = d_act_call(places(odds), dz, share, held_weight, n_batch, n_col, None)
        got = xor_send(away, "col", 1)
        *sends, d_act = d_act_call(
            places(far + [0]), dz, share, held_weight, n_batch, n_col, got
        )
        arrived = [xor_send(part, "col", k) for k, part in zip(far, sends)]
    with jax.named_scope("grad_weight"):
        per_plane = n_col // n_batch
        position = jnp.where(b % 2 == 0, b // 2, n_batch - 1 - b // 2)

        def held_place(plane, i):
            return ((per_plane * plane + 2 * i) ^ (c - c % 2)) // 2

        grad_weight = None
        for i in range(per_plane // 2):
            mine = []
            for d in range(1, n_batch):
                ahead = (position + d) % n_batch
                plane = jnp.where(ahead < (n_batch + 1) // 2, 2 * ahead, 2 * (n_batch - ahead) - 1)
                place = held_place(plane, i)
                block = held_back[0][local_rows:]
                for e in range(1, n_col // 2):
                    block = jnp.where(place == e, held_back[e][local_rows:], block)
                mine.append(ring_send(block, "batch", d))
            mine, d_act = lax.optimization_barrier((mine, d_act))
            other = [xor_send(x, "col", 1) for x in mine]
            for parity, ks, blocks in ((0, evens, mine), (1, odds, other)):
                row = 2 * i + (c % 2 if parity == 0 else 1 - c % 2)
                grad_weight = weight_grad_call(
                    jnp.stack([held_place(b, i), row]).astype(jnp.int32),
                    [[group[k] for k in ks] for group in (pieces, near_pieces, last_pieces)],
                    blocks,
                    dz,
                    features // n_batch,
                    grad_weight,
                )
    with jax.named_scope("norm_backward"):
        arrived, d_act, grad_weight = lax.optimization_barrier((arrived, d_act, grad_weight))
        shares = [share_of(part[tall:]) for part in [d_act] + arrived]
        while len(shares) > 1:
            shares = [x + y for x, y in zip(shares[::2], shares[1::2])]
        d_act = d_act[:tall]
        for part in arrived:
            d_act = d_act + part[:tall].astype(f32)
        d_pre = d_act.reshape(n_view, local_rows, width) * gelu_slope(preactivation)
        sums = jnp.concatenate(
            [
                jnp.sum(d_pre, axis=1),
                jnp.sum(d_pre * normalised, axis=1),
                jnp.broadcast_to(shares[0], (2 * n_view, width)),
            ]
        )
        both = sum(exchange(sums, "batch"))
        sum_b, sum_g = both[:n_view], both[n_view : 2 * n_view]
        loss = jnp.max(both[2 * n_view :])
        grad_bias = jnp.sum(sum_b, axis=0)
        grad_gain = jnp.sum(sum_g, axis=0)
        views_gradient = (
            norm_scale_gain
            * (d_pre - sum_b[:, None, :] / rows - normalised * sum_g[:, None, :] / rows)
            * inverse_deviation
        )
    return (loss, grad_weight, grad_gain, grad_bias, views_gradient)


def solution(mesh):
    placed = (P(None, "batch", "col"), P("col"), P("col"), P(None, "col"))
    return jax.shard_map(
        shards,
        mesh=mesh,
        in_specs=placed,
        out_specs=(P(), P("batch", "col"), P("col"), P("col"), P(None, "batch", "col")),
        check_vma=False,
    )
```

time: 175 us -> 170 us (0.971)
  waiting for transfers between devices: 59.9 us -> 32.8 us
  local copies, waits for them, and re-layouts: 19.4 us -> 36.3 us
  Pallas kernels: 29.4 us -> 35 us
  other arithmetic: 11.5 us -> 7.49 us
  starting transfers between devices: 52.4 us -> 55.4 us
    ppermute x15, waiting for transfers between devices: 34.2 us -> 9.24 us  [ring_send(): lax.ppermute(x, axis, [(order[i], order[(i + d) % n]) for i in range(n)])]
    unnamed x84 -> x165, local copies, waits for them, and re-layouts: 19.2 us -> 36.2 us
    ppermute x23 -> x39, starting transfers between devices: 15.4 us -> 24.2 us  [xor_send(): return lax.ppermute(x, axis, [(i, i ^ k) for i in range(n)])]
    ppermute x23 -> x39, waiting for transfers between devices: 22 us -> 14.2 us  [xor_send(): return lax.ppermute(x, axis, [(i, i ^ k) for i in range(n)])]
    ppermute x6, starting transfers between devices: 16.1 us -> 8.68 us  [exchange(): slots.append(lax.ppermute(x, axis, [(i, (i + d) % n) for i in range(n)]))]
    ppermute x6, waiting for transfers between devices: 3.74 us -> 9.33 us  [exchange(): slots.append(lax.ppermute(x, axis, [(i, (i + d) % n) for i in range(n)]))]
    pallas_call x8 -> x13, Pallas kernels: 28.3 us -> 33.3 us  [the longest x7 12.4 us: z_call(): pl.pallas_call(functools.partial(z_kernel, count, before is None, last, l...]
    select_n x1 -> x2, other arithmetic: 1.88 us -> 0.06 us  [shards(): block = jnp.where(place == e, held_back[e][local_rows:], block)]
  transfers between devices with their start and end apart: 44 -> 60, of which waited for: 21 -> 24; matrix products, arithmetic and copies ran while one was open for 2% -> 0% of each run, Pallas kernels for 9% -> 15%
where the time goes in v5:
time: 170 us; the launch traced here: 169 us
  starting transfers between devices  55.4 us (33%)
  local copies, waits for them, and re-layouts  36.3 us (21%)
  Pallas kernels  35 us (21%)
  waiting for transfers between devices  32.8 us (19%)
  other arithmetic  7.49 us (4%)
  between operations  2.18 us (1%)
    unnamed x165, local copies, waits for them, and re-layouts  36.2 us
    ppermute x39, starting transfers between devices, xor_send(): return lax.ppermute(x, axis, [(i, i ^ k) for i in range(n)])  24.2 us
    ppermute x15, starting transfers between devices, ring_send(): lax.ppermute(x, axis, [(order[i], order[(i + d) % n]) for i in range(n)])  22.5 us
    ppermute x39, waiting for transfers between devices, xor_send(): return lax.ppermute(x, axis, [(i, i ^ k) for i in range(n)])  14.2 us
    pallas_call x7, Pallas kernels, z_call(): pl.pallas_call(functools.partial(z_kernel, count, before is None, last, l...  12.4 us
    ppermute x6, waiting for transfers between devices, exchange(): slots.append(lax.ppermute(x, axis, [(i, (i + d) % n) for i in range(n)]))  9.33 us
    ppermute x15, waiting for transfers between devices, ring_send(): lax.ppermute(x, axis, [(order[i], order[(i + d) % n]) for i in range(n)])  9.24 us
    ppermute x6, starting transfers between devices, exchange(): slots.append(lax.ppermute(x, axis, [(i, (i + d) % n) for i in range(n)]))  8.68 us
  transfers between devices with their start and end apart: 60, of which 24 were waited for; matrix products, arithmetic and copies ran while one was open for 0% of the time, Pallas kernels for 15%

profile of v5, /device:TPU:0, one launch (start us, length us, event | category | flops | bytes accessed | tf_op | source)
XLA Modules:
  0.0 169.1 jit_solution(14828394222850234283)
XLA Ops:
  2.7 5.1 %collective-permute-start = (f32[4,512]{1,0:T(4,128)S(1)}, f32[4,512]{1,0:T(4,128)S(1)}, u32[]{:S(2)}, u32[]{:S(2)}) collective-permute-start(f32[4,512]{1,0:T(4,128)S(1)} %pad_maximum_fusion.2), channel_id=1, source_target_pairs={{0,24},{8,0},{16,8},{24,16},{1,25},{9,1},{17,9},{25,17},{2,26},{10... | collective-permute-start | bytes 24584 | tf_op jit(solution)/shard_map/norm_stats/ppermute | solution.py:42
  9.2 3.2 %collective-permute-done.1 = f32[4,512]{1,0:T(4,128)S(1)} collective-permute-done((f32[4,512]{1,0:T(4,128)S(1)}, f32[4,512]{1,0:T(4,128)S(1)}, u32[]{:S(2)}, u32[]{:S(2)}) %collective-permute-start.1) | collective-permute-done | bytes 8224 | tf_op jit(solution)/shard_map/norm_stats/ppermute | solution.py:42
  13.4 1.2 fusion.17
  15.8 1.5 collective-permute-start.3
  17.3 1.5 collective-permute-start.5
  19.6 2.0 %collective-permute-start.11 = (bf16[128,512]{1,0:T(8,128)(2,1)S(1)}, bf16[128,512]{1,0:T(8,128)(2,1)S(1)}, u32[]{:S(2)}, u32[]{:S(2)}) collective-permute-start(bf16[128,512]{1,0:T(8,128)(2,1)S(1)} %collective-permute-done.10), channel_id=1, source_target_pairs={{0,16},{16,24},{24,8},{8,0},{1,17},{17,25},{25,9},{9,1},{2,18},{18... | collective-permute-start | bytes 393224 | tf_op jit(solution)/shard_map/act_gather/ppermute | solution.py:34
  21.7 3.5 %weight_load.1.refs_2_.refs_3_.refs_4_.w_ref = bf16[4096,1024]{1,0:T(8,128)(2,1)S(1)} custom-call(bf16[4096,1024]{1,0:T(8,128)(2,1)} %w_ref.1), custom_call_target="tpu_custom_call" | custom-call | bytes 16777216 | tf_op jit(solution)/shard_map/weight_load/weight_load/pallas_call | solution.py:81
  25.3 2.2 %collective-permute-start.12 = (bf16[128,512]{1,0:T(8,128)(2,1)S(1)}, bf16[128,512]{1,0:T(8,128)(2,1)S(1)}, u32[]{:S(2)}, u32[]{:S(2)}) collective-permute-start(bf16[128,512]{1,0:T(8,128)(2,1)S(1)} %collective-permute-done.11), channel_id=1, source_target_pairs={{0,16},{16,24},{24,8},{8,0},{1,17},{17,25},{25,9},{9,1},{2,18},{18... | collective-permute-start | bytes 393224 | tf_op jit(solution)/shard_map/act_gather/ppermute | solution.py:34
  29.3 1.3 z_matmul.7.refs_4_
  30.6 1.4 collective-permute-start.14
  32.0 1.5 collective-permute-start.16
  34.2 1.6 z_matmul.8.refs_4_
  35.8 2.2 %z_matmul.9 = (bf16[128,1024]{1,0:T(8,128)(2,1)S(1)}, bf16[128,1024]{1,0:T(8,128)(2,1)}, f32[2,1024]{1,0:T(2,128)S(1)}) custom-call(s32[3]{0:T(128)S(1)} %pad_add_fusion.1.index_ref, bf16[256,512]{1,0:T(8,128)(2,1)S(1)} %collective-permute-done.4.refs_0_.refs_1_, bf16[256,512]{1,0:T(8,128)(2,1)S(1)} %collective-permute-done.6.refs_1_.refs_2_, ...), custom_call_target="tpu_custom_call" | custom-call | flops 805306368 | bytes 524288 | tf_op jit(solution)/shard_map/z/z_matmul/pallas_call | solution.py:129
  38.0 2.9 %collective-permute-start.20 = (bf16[128,1024]{1,0:T(8,128)(2,1)}, bf16[128,1024]{1,0:T(8,128)(2,1)}, u32[]{:S(2)}, u32[]{:S(2)}) collective-permute-start(bf16[128,1024]{1,0:T(8,128)(2,1)} %get-tuple-element.47.refs_1_.refs_9_), channel_id=1, source_target_pairs={{0,16},{16,24},{24,8},{8,0},{1,17},{17,25},{25,9},{9,1},{2,18},{18... | collective-permute-start | bytes 786440 | tf_op jit(solution)/shard_map/z_ring/ppermute | solution.py:34
  41.5 2.7 %collective-permute-done.16.refs_2_.refs_6_ = bf16[256,512]{1,0:T(8,128)(2,1)S(1)} collective-permute-done((bf16[256,512]{1,0:T(8,128)(2,1)S(1)}, bf16[256,512]{1,0:T(8,128)(2,1)S(1)}, u32[]{:S(2)}, u32[]{:S(2)}) %collective-permute-start.16) | collective-permute-done | bytes 262176 | tf_op jit(solution)/shard_map/act_gather/ppermute | solution.py:24
  44.2 1.3 collective-permute-done.18.refs_3_.refs_7_
  45.8 2.7 %collective-permute-start.21 = (bf16[128,1024]{1,0:T(8,128)(2,1)}, bf16[128,1024]{1,0:T(8,128)(2,1)S(1)}, u32[]{:S(2)}, u32[]{:S(2)}) collective-permute-start(bf16[128,1024]{1,0:T(8,128)(2,1)} %collective-permute-done.20.refs_3_.refs_11_), channel_id=1, source_target_pairs={{0,16},{16,24},{24,8},{8,0},{1,17},{17,25},{25,9},{9,1},{2,18},{18... | collective-permute-start | bytes 786440 | tf_op jit(solution)/shard_map/z_ring/ppermute | solution.py:34
  48.6 3.4 %copy-done.1 = bf16[4096,1024]{1,0:T(8,128)(2,1)S(1)} copy-done((bf16[4096,1024]{1,0:T(8,128)(2,1)S(1)}, bf16[4096,1024]{1,0:T(8,128)(2,1)}, u32[]{:S(2)}) %copy-start.1) | copy-done | bytes 8388632
  52.0 1.8 %z_matmul.10.refs_5_ = f32[256,1024]{1,0:T(8,128)S(1)} custom-call(s32[4]{0:T(128)S(1)} %pad_add_fusion.5.index_ref, bf16[256,512]{1,0:T(8,128)(2,1)S(1)} %constant_dynamic-update-slice_fusion.refs_0_.refs_4_, bf16[256,512]{1,0:T(8,128)(2,1)S(1)} %collective-permute-done.14.refs_1_.refs_5_, bf16[256,512]{1,0:T(8,128)(2,1)S(1)} %collective-permute-done.16.refs_2_.refs_6_, ...), custom_call_target="tpu_custom_call" | custom-call | flops 1073741824 | bytes 524288 | tf_op jit(solution)/shard_map/z/z_matmul/pallas_call | solution.py:129
  53.9 2.1 %collective-permute-start.23 = (f32[2,1024]{1,0:T(2,128)S(1)}, f32[2,1024]{1,0:T(2,128)S(1)}, u32[]{:S(2)}, u32[]{:S(2)}) collective-permute-start(f32[2,1024]{1,0:T(2,128)S(1)} %get-tuple-element.52.refs_6_), channel_id=1, source_target_pairs={{0,24},{16,8},{24,0},{8,16},{1,25},{17,9},{25,1},{9,17},{2,26},{18... | collective-permute-start | bytes 24584 | tf_op jit(solution)/shard_map/z_ring/ppermute | solution.py:34
  57.0 2.4 %z_matmul.11 = (bf16[128,1024]{1,0:T(8,128)(2,1)S(1)}, bf16[128,1024]{1,0:T(8,128)(2,1)S(1)}, f32[2,1024]{1,0:T(2,128)}) custom-call(s32[4]{0:T(128)S(1)} %pad_add_fusion.4.index_ref, bf16[256,512]{1,0:T(8,128)(2,1)S(1)} %collective-permute-done.13.refs_0_.refs_4_, bf16[256,512]{1,0:T(8,128)(2,1)S(1)} %collective-permute-done.15.refs_1_.refs_5_, ...), custom_call_target="tpu_custom_call" | custom-call | flops 1073741824 | bytes 524288 | tf_op jit(solution)/shard_map/z/z_matmul/pallas_call | solution.py:129
  60.5 1.7 %kernel_strip.1 = (f32[4,32,384]{2,1,0:T(8,128)S(1)}, f32[4,32,384]{2,1,0:T(8,128)S(1)}) custom-call(s32[8]{0:T(128)S(1)} %stack.59.index_ref, bf16[128,1024]{1,0:T(8,128)(2,1)S(1)} %get-tuple-element.46.refs_0_.refs_8_, bf16[128,1024]{1,0:T(8,128)(2,1)} %get-tuple-element.47.refs_1_.refs_9_, bf16[128,1024]{1,0:T(8,128)(2,1)S(1)} %get-tuple-element.50.refs_2_.refs_10_, ...), custom_call_target="tpu_custom_call" | custom-call | flops 201326592 | bytes 1572864 | tf_op jit(solution)/shard_map/kernel/kernel_strip/pallas_call | solution.py:164
  62.4 1.6 collective-permute-start.30
  64.0 1.5 collective-permute-start.32
  66.0 2.7 %collective-permute-done.30.refs_1_.refs_9_ = bf16[128,512]{1,0:T(8,128)(2,1)S(1)} collective-permute-done((bf16[128,512]{1,0:T(8,128)(2,1)S(1)}, bf16[128,512]{1,0:T(8,128)(2,1)S(1)}, u32[]{:S(2)}, u32[]{:S(2)}) %collective-permute-start.30) | collective-permute-done | bytes 131104 | tf_op jit(solution)/shard_map/act_gather/ppermute | solution.py:24
  68.6 3.7 %collective-permute-done.32.refs_2_.refs_10_ = bf16[128,512]{1,0:T(8,128)(2,1)S(1)} collective-permute-done((bf16[128,512]{1,0:T(8,128)(2,1)S(1)}, bf16[128,512]{1,0:T(8,128)(2,1)S(1)}, u32[]{:S(2)}, u32[]{:S(2)}) %collective-permute-start.32) | collective-permute-done | bytes 131104 | tf_op jit(solution)/shard_map/act_gather/ppermute | solution.py:24
  72.9 1.3 z_matmul.12.refs_5_
  75.3 1.6 collective-permute-start.28
  77.6 1.3 collective-permute-start.26
  78.9 1.9 %z_matmul.13 = (bf16[128,1024]{1,0:T(8,128)(2,1)S(1)}, f32[1,1024]{1,0:T(1,128)}) custom-call(s32[4]{0:T(128)S(1)} %pad_add_fusion.4.index_ref, bf16[128,512]{1,0:T(8,128)(2,1)S(1)} %collective-permute-done.29.refs_0_.refs_8_, bf16[128,512]{1,0:T(8,128)(2,1)S(1)} %collective-permute-done.31.refs_1_.refs_9_, ...), custom_call_target="tpu_custom_call" | custom-call | flops 536870912 | bytes 262144 | tf_op jit(solution)/shard_map/z/z_matmul/pallas_call | solution.py:129
  83.1 1.4 collective-permute-start.39
  84.5 2.0 %collective-permute-start.38 = (bf16[32,384]{1,0:T(8,128)(2,1)S(1)}, bf16[32,384]{1,0:T(8,128)(2,1)S(1)}, u32[]{:S(2)}, u32[]{:S(2)}) collective-permute-start(bf16[32,384]{1,0:T(8,128)(2,1)S(1)} %get-tuple-element.100), channel_id=1, source_target_pairs={{0,24},{16,8},{24,0},{8,16},{1,25},{17,9},{25,1},{9,17},{2,26},{18... | collective-permute-start | bytes 73736 | tf_op jit(solution)/shard_map/kernel/ppermute | solution.py:34
  87.8 2.3 %collective-permute-done.38 = bf16[32,384]{1,0:T(8,128)(2,1)S(1)} collective-permute-done((bf16[32,384]{1,0:T(8,128)(2,1)S(1)}, bf16[32,384]{1,0:T(8,128)(2,1)S(1)}, u32[]{:S(2)}, u32[]{:S(2)}) %collective-permute-start.38) | collective-permute-done | bytes 24608 | tf_op jit(solution)/shard_map/kernel/ppermute | solution.py:34
  92.5 1.4 collective-permute-start.45
  114.6 5.1 %embedding_gradient.1 = (bf16[2,512,1024]{2,1,0:T(8,128)(2,1)S(1)}, f32[8,128]{1,0:T(8,128)S(1)}) custom-call(s32[8]{0:T(128)S(1)} %stack.59.index_ref, bf16[4,32,384]{2,1,0:T(8,128)(2,1)S(1)} %copy-done.51, bf16[4,32,384]{2,1,0:T(8,128)(2,1)S(1)} %copy-done.66, bf16[4,32,384]{2,1,0:T(8,128)(2,1)S(1)} %copy-done.60, bf16[4,32,384]{2,1,0:T(8,128)(2,1)S(1)} %copy-done.68, ...), custom_call_target="tpu_custom_call" | custom-call | flops 1073741824 | bytes 4194304 | tf_op jit(solution)/shard_map/dz/embedding_gradient/pallas_call | solution.py:242
  119.8 3.4 %copy-done.2 = bf16[4096,1024]{1,0:T(8,128)(2,1)S(1)} copy-done((bf16[4096,1024]{1,0:T(8,128)(2,1)S(1)}, bf16[4096,1024]{1,0:T(8,128)(2,1)}, u32[]{:S(2)}) %copy-start.2) | copy-done | bytes 8388632
  123.2 2.8 %d_act_matmul.2 = bf16[4,272,512]{2,1,0:T(8,128)(2,1)} custom-call(s32[4]{0:T(128)S(1)} %pad_add_fusion.4.index_ref, bf16[2,512,1024]{2,1,0:T(8,128)(2,1)S(1)} %get-tuple-element.68.dz_ref.refs_15_, f32[8,128]{1,0:T(8,128)S(1)} %broadcast_add_fusion.share_ref, bf16[4096,1024]{1,0:T(8,128)(2,1)S(1)} %copy-done.2), custom_call_target="tpu_custom_call" | custom-call | flops 1073741824 | bytes 1048576 | tf_op jit(solution)/shard_map/d_act/d_act_matmul/pallas_call | solution.py:313
  126.5 1.4 collective-permute-start.51
  128.0 2.0 %collective-permute-start.52 = (bf16[128,512]{1,0:T(8,128)(2,1)S(1)}, bf16[128,512]{1,0:T(8,128)(2,1)}, u32[]{:S(2)}, u32[]{:S(2)}) collective-permute-start(bf16[128,512]{1,0:T(8,128)(2,1)S(1)} %get-tuple-element.95), channel_id=1, source_target_pairs={{0,24},{16,8},{24,0},{8,16},{1,25},{17,9},{25,1},{9,17},{2,26},{18... | collective-permute-start | bytes 393224 | tf_op jit(solution)/shard_map/grad_weight/ppermute | solution.py:34
  130.1 3.4 %copy-done.3 = bf16[4096,1024]{1,0:T(8,128)(2,1)S(1)} copy-done((bf16[4096,1024]{1,0:T(8,128)(2,1)S(1)}, bf16[4096,1024]{1,0:T(8,128)(2,1)}, u32[]{:S(2)}) %copy-start.3) | copy-done | bytes 8388632
  133.5 2.5 %d_act_matmul.3 = (bf16[272,512]{1,0:T(8,128)(2,1)S(1)}, bf16[272,512]{1,0:T(8,128)(2,1)S(1)}, bf16[272,512]{1,0:T(8,128)(2,1)S(1)}, f32[272,512]{1,0:T(8,128)S(1)}) custom-call(s32[4]{0:T(128)S(1)} %pad_add_fusion.index_ref, bf16[2,512,1024]{2,1,0:T(8,128)(2,1)S(1)} %get-tuple-element.68.dz_ref.refs_15_, f32[8,128]{1,0:T(8,128)S(1)} %broadcast_add_fusion.share_ref, ...), custom_call_target="tpu_custom_call" | custom-call | flops 1073741824 | bytes 1048576 | tf_op jit(solution)/shard_map/d_act/d_act_matmul/pallas_call | solution.py:313
  138.4 3.4 %collective-permute-done.53.refs_14_ = bf16[128,512]{1,0:T(8,128)(2,1)} collective-permute-done((bf16[128,512]{1,0:T(8,128)(2,1)S(1)}, bf16[128,512]{1,0:T(8,128)(2,1)}, u32[]{:S(2)}, u32[]{:S(2)}) %collective-permute-start.53) | collective-permute-done | bytes 131104 | tf_op jit(solution)/shard_map/grad_weight/ppermute | solution.py:34
  141.9 1.5 collective-permute-start.48
  143.9 1.5 collective-permute-start.50
  151.6 3.5 %weight_gradient.2.refs_16_ = f32[1024,1024]{1,0:T(8,128)} custom-call(s32[2]{0:T(128)S(1)} %pad_add_fusion.7.place_ref, bf16[256,512]{1,0:T(8,128)(2,1)S(1)} %bitcast.44, bf16[256,512]{1,0:T(8,128)(2,1)S(1)} %collective-permute-done.3.refs_0_.refs_1_, bf16[256,512]{1,0:T(8,128)(2,1)S(1)} %collective-permute-done.5.refs_1_.refs_2_, ...), custom_call_target="tpu_custom_call" | custom-call | flops 1073741824 | bytes 2097152 | tf_op jit(solution)/shard_map/grad_weight/weight_gradient/pallas_call | solution.py:382
  155.4 3.3 %weight_gradient.3 = f32[1024,1024]{1,0:T(8,128)} custom-call(s32[2]{0:T(128)S(1)} %pad_add_fusion.6.place_ref, bf16[256,512]{1,0:T(8,128)(2,1)S(1)} %copy-done.5, bf16[256,512]{1,0:T(8,128)(2,1)S(1)} %copy-done.7, bf16[256,512]{1,0:T(8,128)(2,1)S(1)} %copy-done.9, bf16[256,512]{1,0:T(8,128)(2,1)S(1)} %copy-done.11, ...), custom_call_target="tpu_custom_call", output_to_operand_aliasing={{}: (17, {})} | custom-call | flops 1073741824 | bytes 2097152 | tf_op jit(solution)/shard_map/grad_weight/weight_gradient/pallas_call | solution.py:382
  159.5 1.9 %collective-permute-start.57 = (f32[8,512]{1,0:T(8,128)S(1)}, f32[8,512]{1,0:T(8,128)S(1)}, u32[]{:S(2)}, u32[]{:S(2)}) collective-permute-start(f32[8,512]{1,0:T(8,128)S(1)} %pad_maximum_fusion.1), channel_id=1, source_target_pairs={{0,24},{8,0},{16,8},{24,16},{1,25},{9,1},{17,9},{25,17},{2,26},{10... | collective-permute-start | bytes 49160 | tf_op jit(solution)/shard_map/norm_backward/ppermute | solution.py:42
  163.3 2.8 %collective-permute-done.58 = f32[8,512]{1,0:T(8,128)S(1)} collective-permute-done((f32[8,512]{1,0:T(8,128)S(1)}, f32[8,512]{1,0:T(8,128)S(1)}, u32[]{:S(2)}, u32[]{:S(2)}) %collective-permute-start.58) | collective-permute-done | bytes 16416 | tf_op jit(solution)/shard_map/norm_backward/ppermute | solution.py:42
  (288 shorter events, 56.6 us)
Async XLA Ops:
  2.7 6.5 %collective-permute-start = (f32[4,512]{1,0:T(4,128)S(1)}, f32[4,512]{1,0:T(4,128)S(1)}, u32[]{:S(2)}, u32[]{:S(2)}) collective-permute-start(f32[4,512]{1,0:T(4,128)S(1)} %pad_maximum_fusion.2), channel_id=1, source_target_pairs={{0,24},{8,0},{16,8},{24,16},{1,25},{9,1},{17,9},{25,17},{2,26},{10... | collective-permute-start | bytes 24584 | tf_op jit(solution)/shard_map/norm_stats/ppermute | solution.py:42
  7.8 5.4 %collective-permute-start.2 = (f32[4,512]{1,0:T(4,128)S(1)}, f32[4,512]{1,0:T(4,128)S(1)}, u32[]{:S(2)}, u32[]{:S(2)}) collective-permute-start(f32[4,512]{1,0:T(4,128)S(1)} %pad_maximum_fusion.2), channel_id=1, source_target_pairs={{0,8},{8,16},{16,24},{24,0},{1,9},{9,17},{17,25},{25,1},{2,10},{10... | collective-permute-start | bytes 24584 | tf_op jit(solution)/shard_map/norm_stats/ppermute | solution.py:42
  14.6 5.0 %collective-permute-start.10 = (bf16[128,512]{1,0:T(8,128)(2,1)S(1)}, bf16[128,512]{1,0:T(8,128)(2,1)S(1)}, u32[]{:S(2)}, u32[]{:S(2)}) collective-permute-start(bf16[128,512]{1,0:T(8,128)(2,1)S(1)} %slice_bitcast_fusion), channel_id=1, source_target_pairs={{0,16},{16,24},{24,8},{8,0},{1,17},{17,25},{25,9},{9,1},{2,18},{18... | collective-permute-start | bytes 393224 | tf_op jit(solution)/shard_map/act_gather/ppermute | solution.py:34
  15.8 11.8 %collective-permute-start.3 = (bf16[256,512]{1,0:T(8,128)(2,1)S(1)}, bf16[256,512]{1,0:T(8,128)(2,1)S(1)}, u32[]{:S(2)}, u32[]{:S(2)}) collective-permute-start(bf16[256,512]{1,0:T(8,128)(2,1)S(1)} %bitcast.37), channel_id=1, source_target_pairs={{0,2},{1,3},{2,0},{3,1},{4,6},{5,7},{6,4},{7,5},{8,10},{9,11},{10,... | collective-permute-start | bytes 786440 | tf_op jit(solution)/shard_map/act_gather/ppermute | solution.py:24
  17.3 11.4 %collective-permute-start.5 = (bf16[256,512]{1,0:T(8,128)(2,1)S(1)}, bf16[256,512]{1,0:T(8,128)(2,1)S(1)}, u32[]{:S(2)}, u32[]{:S(2)}) collective-permute-start(bf16[256,512]{1,0:T(8,128)(2,1)S(1)} %bitcast.38), channel_id=1, source_target_pairs={{0,4},{1,5},{2,6},{3,7},{4,0},{5,1},{6,2},{7,3},{8,12},{9,13},{10,... | collective-permute-start | bytes 786440 | tf_op jit(solution)/shard_map/act_gather/ppermute | solution.py:24
  18.8 9.9 %collective-permute-start.7 = (bf16[256,512]{1,0:T(8,128)(2,1)S(1)}, bf16[256,512]{1,0:T(8,128)(2,1)S(1)}, u32[]{:S(2)}, u32[]{:S(2)}) collective-permute-start(bf16[256,512]{1,0:T(8,128)(2,1)S(1)} %bitcast.39), channel_id=1, source_target_pairs={{0,6},{1,7},{2,4},{3,5},{4,2},{5,3},{6,0},{7,1},{8,14},{9,15},{10,... | collective-permute-start | bytes 786440 | tf_op jit(solution)/shard_map/act_gather/ppermute | solution.py:24
  19.3 10.0 %collective-permute-start.9 = (bf16[256,512]{1,0:T(8,128)(2,1)S(1)}, bf16[256,512]{1,0:T(8,128)(2,1)S(1)}, u32[]{:S(2)}, u32[]{:S(2)}) collective-permute-start(bf16[256,512]{1,0:T(8,128)(2,1)S(1)} %bitcast.40), channel_id=1, source_target_pairs={{0,1},{1,0},{2,3},{3,2},{4,5},{5,4},{6,7},{7,6},{8,9},{9,8},{10,11... | collective-permute-start | bytes 786440 | tf_op jit(solution)/shard_map/act_gather/ppermute | solution.py:24
  19.6 5.7 %collective-permute-start.11 = (bf16[128,512]{1,0:T(8,128)(2,1)S(1)}, bf16[128,512]{1,0:T(8,128)(2,1)S(1)}, u32[]{:S(2)}, u32[]{:S(2)}) collective-permute-start(bf16[128,512]{1,0:T(8,128)(2,1)S(1)} %collective-permute-done.10), channel_id=1, source_target_pairs={{0,16},{16,24},{24,8},{8,0},{1,17},{17,25},{25,9},{9,1},{2,18},{18... | collective-permute-start | bytes 393224 | tf_op jit(solution)/shard_map/act_gather/ppermute | solution.py:34
  25.3 5.2 %collective-permute-start.12 = (bf16[128,512]{1,0:T(8,128)(2,1)S(1)}, bf16[128,512]{1,0:T(8,128)(2,1)S(1)}, u32[]{:S(2)}, u32[]{:S(2)}) collective-permute-start(bf16[128,512]{1,0:T(8,128)(2,1)S(1)} %collective-permute-done.11), channel_id=1, source_target_pairs={{0,16},{16,24},{24,8},{8,0},{1,17},{17,25},{25,9},{9,1},{2,18},{18... | collective-permute-start | bytes 393224 | tf_op jit(solution)/shard_map/act_gather/ppermute | solution.py:34
  27.6 5.9 %collective-permute-start.4 = (bf16[256,512]{1,0:T(8,128)(2,1)S(1)}, bf16[256,512]{1,0:T(8,128)(2,1)S(1)}, u32[]{:S(2)}, u32[]{:S(2)}) collective-permute-start(bf16[256,512]{1,0:T(8,128)(2,1)S(1)} %collective-permute-done.3.refs_0_.refs_1_), channel_id=1, source_target_pairs={{0,1},{1,0},{2,3},{3,2},{4,5},{5,4},{6,7},{7,6},{8,9},{9,8},{10,11... | collective-permute-start | bytes 786440 | tf_op jit(solution)/shard_map/act_gather/ppermute | solution.py:24
  28.7 7.0 %collective-permute-start.6 = (bf16[256,512]{1,0:T(8,128)(2,1)S(1)}, bf16[256,512]{1,0:T(8,128)(2,1)S(1)}, u32[]{:S(2)}, u32[]{:S(2)}) collective-permute-start(bf16[256,512]{1,0:T(8,128)(2,1)S(1)} %collective-permute-done.5.refs_1_.refs_2_), channel_id=1, source_target_pairs={{0,1},{1,0},{2,3},{3,2},{4,5},{5,4},{6,7},{7,6},{8,9},{9,8},{10,11... | collective-permute-start | bytes 786440 | tf_op jit(solution)/shard_map/act_gather/ppermute | solution.py:24
  28.7 7.0 %collective-permute-start.8 = (bf16[256,512]{1,0:T(8,128)(2,1)S(1)}, bf16[256,512]{1,0:T(8,128)(2,1)S(1)}, u32[]{:S(2)}, u32[]{:S(2)}) collective-permute-start(bf16[256,512]{1,0:T(8,128)(2,1)S(1)} %collective-permute-done.7.refs_2_.refs_3_), channel_id=1, source_target_pairs={{0,1},{1,0},{2,3},{3,2},{4,5},{5,4},{6,7},{7,6},{8,9},{9,8},{10,11... | collective-permute-start | bytes 786440 | tf_op jit(solution)/shard_map/act_gather/ppermute | solution.py:24
  30.6 10.3 %collective-permute-start.14 = (bf16[256,512]{1,0:T(8,128)(2,1)S(1)}, bf16[256,512]{1,0:T(8,128)(2,1)S(1)}, u32[]{:S(2)}, u32[]{:S(2)}) collective-permute-start(bf16[256,512]{1,0:T(8,128)(2,1)S(1)} %constant_dynamic-update-slice_fusion.refs_0_.refs_4_), channel_id=1, source_target_pairs={{0,2},{1,3},{2,0},{3,1},{4,6},{5,7},{6,4},{7,5},{8,10},{9,11},{10,... | collective-permute-start | bytes 786440 | tf_op jit(solution)/shard_map/act_gather/ppermute | solution.py:24
  32.0 12.2 %collective-permute-start.16 = (bf16[256,512]{1,0:T(8,128)(2,1)S(1)}, bf16[256,512]{1,0:T(8,128)(2,1)S(1)}, u32[]{:S(2)}, u32[]{:S(2)}) collective-permute-start(bf16[256,512]{1,0:T(8,128)(2,1)S(1)} %constant_dynamic-update-slice_fusion.refs_0_.refs_4_), channel_id=1, source_target_pairs={{0,4},{1,5},{2,6},{3,7},{4,0},{5,1},{6,2},{7,3},{8,12},{9,13},{10,... | collective-permute-start | bytes 786440 | tf_op jit(solution)/shard_map/act_gather/ppermute | solution.py:24
  33.5 12.0 %collective-permute-start.18 = (bf16[256,512]{1,0:T(8,128)(2,1)S(1)}, bf16[256,512]{1,0:T(8,128)(2,1)S(1)}, u32[]{:S(2)}, u32[]{:S(2)}) collective-permute-start(bf16[256,512]{1,0:T(8,128)(2,1)S(1)} %constant_dynamic-update-slice_fusion.refs_0_.refs_4_), channel_id=1, source_target_pairs={{0,6},{1,7},{2,4},{3,5},{4,2},{5,3},{6,0},{7,1},{8,14},{9,15},{10,... | collective-permute-start | bytes 786440 | tf_op jit(solution)/shard_map/act_gather/ppermute | solution.py:24
  38.0 7.8 %collective-permute-start.20 = (bf16[128,1024]{1,0:T(8,128)(2,1)}, bf16[128,1024]{1,0:T(8,128)(2,1)}, u32[]{:S(2)}, u32[]{:S(2)}) collective-permute-start(bf16[128,1024]{1,0:T(8,128)(2,1)} %get-tuple-element.47.refs_1_.refs_9_), channel_id=1, source_target_pairs={{0,16},{16,24},{24,8},{8,0},{1,17},{17,25},{25,9},{9,1},{2,18},{18... | collective-permute-start | bytes 786440 | tf_op jit(solution)/shard_map/z_ring/ppermute | solution.py:34
  40.9 12.9 %collective-permute-start.13 = (bf16[256,512]{1,0:T(8,128)(2,1)S(1)}, bf16[256,512]{1,0:T(8,128)(2,1)S(1)}, u32[]{:S(2)}, u32[]{:S(2)}) collective-permute-start(bf16[256,512]{1,0:T(8,128)(2,1)S(1)} %constant_dynamic-update-slice_fusion.refs_0_.refs_4_), channel_id=1, source_target_pairs={{0,1},{1,0},{2,3},{3,2},{4,5},{5,4},{6,7},{7,6},{8,9},{9,8},{10,11... | collective-permute-start | bytes 786440 | tf_op jit(solution)/shard_map/act_gather/ppermute | solution.py:24
  40.9 13.0 %collective-permute-start.15 = (bf16[256,512]{1,0:T(8,128)(2,1)S(1)}, bf16[256,512]{1,0:T(8,128)(2,1)S(1)}, u32[]{:S(2)}, u32[]{:S(2)}) collective-permute-start(bf16[256,512]{1,0:T(8,128)(2,1)S(1)} %collective-permute-done.14.refs_1_.refs_5_), channel_id=1, source_target_pairs={{0,1},{1,0},{2,3},{3,2},{4,5},{5,4},{6,7},{7,6},{8,9},{9,8},{10,11... | collective-permute-start | bytes 786440 | tf_op jit(solution)/shard_map/act_gather/ppermute | solution.py:24
  44.2 11.8 %collective-permute-start.17 = (bf16[256,512]{1,0:T(8,128)(2,1)S(1)}, bf16[256,512]{1,0:T(8,128)(2,1)S(1)}, u32[]{:S(2)}, u32[]{:S(2)}) collective-permute-start(bf16[256,512]{1,0:T(8,128)(2,1)S(1)} %collective-permute-done.16.refs_2_.refs_6_), channel_id=1, source_target_pairs={{0,1},{1,0},{2,3},{3,2},{4,5},{5,4},{6,7},{7,6},{8,9},{9,8},{10,11... | collective-permute-start | bytes 786440 | tf_op jit(solution)/shard_map/act_gather/ppermute | solution.py:24
  45.5 11.6 %collective-permute-start.19 = (bf16[256,512]{1,0:T(8,128)(2,1)S(1)}, bf16[256,512]{1,0:T(8,128)(2,1)S(1)}, u32[]{:S(2)}, u32[]{:S(2)}) collective-permute-start(bf16[256,512]{1,0:T(8,128)(2,1)S(1)} %collective-permute-done.18.refs_3_.refs_7_), channel_id=1, source_target_pairs={{0,1},{1,0},{2,3},{3,2},{4,5},{5,4},{6,7},{7,6},{8,9},{9,8},{10,11... | collective-permute-start | bytes 786440 | tf_op jit(solution)/shard_map/act_gather/ppermute | solution.py:24
  45.8 14.7 %collective-permute-start.21 = (bf16[128,1024]{1,0:T(8,128)(2,1)}, bf16[128,1024]{1,0:T(8,128)(2,1)S(1)}, u32[]{:S(2)}, u32[]{:S(2)}) collective-permute-start(bf16[128,1024]{1,0:T(8,128)(2,1)} %collective-permute-done.20.refs_3_.refs_11_), channel_id=1, source_target_pairs={{0,16},{16,24},{24,8},{8,0},{1,17},{17,25},{25,9},{9,1},{2,18},{18... | collective-permute-start | bytes 786440 | tf_op jit(solution)/shard_map/z_ring/ppermute | solution.py:34
  53.8 5.6 %collective-permute-start.22 = (f32[2,1024]{1,0:T(2,128)S(1)}, f32[2,1024]{1,0:T(2,128)S(1)}, u32[]{:S(2)}, u32[]{:S(2)}) collective-permute-start(f32[2,1024]{1,0:T(2,128)S(1)} %get-tuple-element.52.refs_6_), channel_id=1, source_target_pairs={{0,16},{16,24},{24,8},{8,0},{1,17},{17,25},{25,9},{9,1},{2,18},{18... | collective-permute-start | bytes 24584 | tf_op jit(solution)/shard_map/z_ring/ppermute | solution.py:34
  53.9 5.6 %collective-permute-start.23 = (f32[2,1024]{1,0:T(2,128)S(1)}, f32[2,1024]{1,0:T(2,128)S(1)}, u32[]{:S(2)}, u32[]{:S(2)}) collective-permute-start(f32[2,1024]{1,0:T(2,128)S(1)} %get-tuple-element.52.refs_6_), channel_id=1, source_target_pairs={{0,24},{16,8},{24,0},{8,16},{1,25},{17,9},{25,1},{9,17},{2,26},{18... | collective-permute-start | bytes 24584 | tf_op jit(solution)/shard_map/z_ring/ppermute | solution.py:34
  62.3 11.9 %collective-permute-start.25 = (f32[4,32,384]{2,1,0:T(8,128)S(1)}, f32[4,32,384]{2,1,0:T(8,128)S(1)}, u32[]{:S(2)}, u32[]{:S(2)}) collective-permute-start(f32[4,32,384]{2,1,0:T(8,128)S(1)} %get-tuple-element.54), channel_id=1, source_target_pairs={{0,1},{1,0},{2,3},{3,2},{4,5},{5,4},{6,7},{7,6},{8,9},{9,8},{10,11... | collective-permute-start | bytes 589832 | tf_op jit(solution)/shard_map/kernel/ppermute | solution.py:24
  62.4 6.2 %collective-permute-start.30 = (bf16[128,512]{1,0:T(8,128)(2,1)S(1)}, bf16[128,512]{1,0:T(8,128)(2,1)S(1)}, u32[]{:S(2)}, u32[]{:S(2)}) collective-permute-start(bf16[128,512]{1,0:T(8,128)(2,1)S(1)} %collective-permute-done.12.refs_0_.refs_8_), channel_id=1, source_target_pairs={{0,2},{1,3},{2,0},{3,1},{4,6},{5,7},{6,4},{7,5},{8,10},{9,11},{10,... | collective-permute-start | bytes 393224 | tf_op jit(solution)/shard_map/act_gather/ppermute | solution.py:24
  64.0 8.4 %collective-permute-start.32 = (bf16[128,512]{1,0:T(8,128)(2,1)S(1)}, bf16[128,512]{1,0:T(8,128)(2,1)S(1)}, u32[]{:S(2)}, u32[]{:S(2)}) collective-permute-start(bf16[128,512]{1,0:T(8,128)(2,1)S(1)} %collective-permute-done.12.refs_0_.refs_8_), channel_id=1, source_target_pairs={{0,4},{1,5},{2,6},{3,7},{4,0},{5,1},{6,2},{7,3},{8,12},{9,13},{10,... | collective-permute-start | bytes 393224 | tf_op jit(solution)/shard_map/act_gather/ppermute | solution.py:24
  65.5 6.9 %collective-permute-start.34 = (bf16[128,512]{1,0:T(8,128)(2,1)S(1)}, bf16[128,512]{1,0:T(8,128)(2,1)S(1)}, u32[]{:S(2)}, u32[]{:S(2)}) collective-permute-start(bf16[128,512]{1,0:T(8,128)(2,1)S(1)} %collective-permute-done.12.refs_0_.refs_8_), channel_id=1, source_target_pairs={{0,6},{1,7},{2,4},{3,5},{4,2},{5,3},{6,0},{7,1},{8,14},{9,15},{10,... | collective-permute-start | bytes 393224 | tf_op jit(solution)/shard_map/act_gather/ppermute | solution.py:24
  66.0 9.3 %collective-permute-start.29 = (bf16[128,512]{1,0:T(8,128)(2,1)S(1)}, bf16[128,512]{1,0:T(8,128)(2,1)S(1)}, u32[]{:S(2)}, u32[]{:S(2)}) collective-permute-start(bf16[128,512]{1,0:T(8,128)(2,1)S(1)} %collective-permute-done.12.refs_0_.refs_8_), channel_id=1, source_target_pairs={{0,1},{1,0},{2,3},{3,2},{4,5},{5,4},{6,7},{7,6},{8,9},{9,8},{10,11... | collective-permute-start | bytes 393224 | tf_op jit(solution)/shard_map/act_gather/ppermute | solution.py:24
  68.6 8.2 %collective-permute-start.31 = (bf16[128,512]{1,0:T(8,128)(2,1)S(1)}, bf16[128,512]{1,0:T(8,128)(2,1)S(1)}, u32[]{:S(2)}, u32[]{:S(2)}) collective-permute-start(bf16[128,512]{1,0:T(8,128)(2,1)S(1)} %collective-permute-done.30.refs_1_.refs_9_), channel_id=1, source_target_pairs={{0,1},{1,0},{2,3},{3,2},{4,5},{5,4},{6,7},{7,6},{8,9},{9,8},{10,11... | collective-permute-start | bytes 393224 | tf_op jit(solution)/shard_map/act_gather/ppermute | solution.py:24
  72.3 5.2 %collective-permute-start.33 = (bf16[128,512]{1,0:T(8,128)(2,1)S(1)}, bf16[128,512]{1,0:T(8,128)(2,1)S(1)}, u32[]{:S(2)}, u32[]{:S(2)}) collective-permute-start(bf16[128,512]{1,0:T(8,128)(2,1)S(1)} %collective-permute-done.32.refs_2_.refs_10_), channel_id=1, source_target_pairs={{0,1},{1,0},{2,3},{3,2},{4,5},{5,4},{6,7},{7,6},{8,9},{9,8},{10,11... | collective-permute-start | bytes 393224 | tf_op jit(solution)/shard_map/act_gather/ppermute | solution.py:24
  72.3 6.5 %collective-permute-start.35 = (bf16[128,512]{1,0:T(8,128)(2,1)S(1)}, bf16[128,512]{1,0:T(8,128)(2,1)S(1)}, u32[]{:S(2)}, u32[]{:S(2)}) collective-permute-start(bf16[128,512]{1,0:T(8,128)(2,1)S(1)} %collective-permute-done.34.refs_3_.refs_11_), channel_id=1, source_target_pairs={{0,1},{1,0},{2,3},{3,2},{4,5},{5,4},{6,7},{7,6},{8,9},{9,8},{10,11... | collective-permute-start | bytes 393224 | tf_op jit(solution)/shard_map/act_gather/ppermute | solution.py:24
  74.2 8.3 %collective-permute-start.36 = (bf16[128,1024]{1,0:T(8,128)(2,1)S(1)}, bf16[128,1024]{1,0:T(8,128)(2,1)S(1)}, u32[]{:S(2)}, u32[]{:S(2)}) collective-permute-start(bf16[128,1024]{1,0:T(8,128)(2,1)S(1)} %collective-permute-done.21.refs_5_.refs_13_), channel_id=1, source_target_pairs={{0,16},{16,24},{24,8},{8,0},{1,17},{17,25},{25,9},{9,1},{2,18},{18... | collective-permute-start | bytes 786440 | tf_op jit(solution)/shard_map/z_ring/ppermute | solution.py:34
  75.3 5.5 %collective-permute-start.28 = (f32[32,384]{1,0:T(8,128)S(1)}, f32[32,384]{1,0:T(8,128)S(1)}, u32[]{:S(2)}, u32[]{:S(2)}) collective-permute-start(f32[32,384]{1,0:T(8,128)S(1)} %get-tuple-element.97), channel_id=1, source_target_pairs={{0,6},{1,7},{2,4},{3,5},{4,2},{5,3},{6,0},{7,1},{8,14},{9,15},{10,... | collective-permute-start | bytes 147464 | tf_op jit(solution)/shard_map/kernel/ppermute | solution.py:24
  83.1 4.7 %collective-permute-start.39 = (bf16[32,384]{1,0:T(8,128)(2,1)S(1)}, bf16[32,384]{1,0:T(8,128)(2,1)S(1)}, u32[]{:S(2)}, u32[]{:S(2)}) collective-permute-start(bf16[32,384]{1,0:T(8,128)(2,1)S(1)} %get-tuple-element.100), channel_id=1, source_target_pairs={{0,8},{16,0},{24,16},{8,24},{1,9},{17,1},{25,17},{9,25},{2,10},{18... | collective-permute-start | bytes 73736 | tf_op jit(solution)/shard_map/kernel/ppermute | solution.py:34
  84.5 5.6 %collective-permute-start.38 = (bf16[32,384]{1,0:T(8,128)(2,1)S(1)}, bf16[32,384]{1,0:T(8,128)(2,1)S(1)}, u32[]{:S(2)}, u32[]{:S(2)}) collective-permute-start(bf16[32,384]{1,0:T(8,128)(2,1)S(1)} %get-tuple-element.100), channel_id=1, source_target_pairs={{0,24},{16,8},{24,0},{8,16},{1,25},{17,9},{25,1},{9,17},{2,26},{18... | collective-permute-start | bytes 73736 | tf_op jit(solution)/shard_map/kernel/ppermute | solution.py:34
  90.4 5.0 %collective-permute-start.41 = (bf16[4,32,384]{2,1,0:T(8,128)(2,1)S(1)}, bf16[4,32,384]{2,1,0:T(8,128)(2,1)S(1)}, u32[]{:S(2)}, u32[]{:S(2)}) collective-permute-start(bf16[4,32,384]{2,1,0:T(8,128)(2,1)S(1)} %pad_maximum_fusion.refs_0_), channel_id=1, source_target_pairs={{0,2},{1,3},{2,0},{3,1},{4,6},{5,7},{6,4},{7,5},{8,10},{9,11},{10,... | collective-permute-start | bytes 294920 | tf_op jit(solution)/shard_map/kernel/ppermute | solution.py:24
  92.5 5.5 %collective-permute-start.45 = (bf16[4,32,384]{2,1,0:T(8,128)(2,1)S(1)}, bf16[4,32,384]{2,1,0:T(8,128)(2,1)S(1)}, u32[]{:S(2)}, u32[]{:S(2)}) collective-permute-start(bf16[4,32,384]{2,1,0:T(8,128)(2,1)S(1)} %pad_maximum_fusion.refs_0_), channel_id=1, source_target_pairs={{0,6},{1,7},{2,4},{3,5},{4,2},{5,3},{6,0},{7,1},{8,14},{9,15},{10,... | collective-permute-start | bytes 294920 | tf_op jit(solution)/shard_map/kernel/ppermute | solution.py:24
  93.9 5.3 %collective-permute-start.40 = (bf16[4,32,384]{2,1,0:T(8,128)(2,1)S(1)}, bf16[4,32,384]{2,1,0:T(8,128)(2,1)S(1)}, u32[]{:S(2)}, u32[]{:S(2)}) collective-permute-start(bf16[4,32,384]{2,1,0:T(8,128)(2,1)S(1)} %pad_maximum_fusion.refs_0_), channel_id=1, source_target_pairs={{0,1},{1,0},{2,3},{3,2},{4,5},{5,4},{6,7},{7,6},{8,9},{9,8},{10,11... | collective-permute-start | bytes 294920 | tf_op jit(solution)/shard_map/kernel/ppermute | solution.py:24
  126.5 11.0 %collective-permute-start.51 = (bf16[128,512]{1,0:T(8,128)(2,1)S(1)}, bf16[128,512]{1,0:T(8,128)(2,1)}, u32[]{:S(2)}, u32[]{:S(2)}) collective-permute-start(bf16[128,512]{1,0:T(8,128)(2,1)S(1)} %select_select_fusion.2), channel_id=1, source_target_pairs={{0,16},{16,24},{24,8},{8,0},{1,17},{17,25},{25,9},{9,1},{2,18},{18... | collective-permute-start | bytes 393224 | tf_op jit(solution)/shard_map/grad_weight/ppermute | solution.py:34
  128.0 10.3 %collective-permute-start.52 = (bf16[128,512]{1,0:T(8,128)(2,1)S(1)}, bf16[128,512]{1,0:T(8,128)(2,1)}, u32[]{:S(2)}, u32[]{:S(2)}) collective-permute-start(bf16[128,512]{1,0:T(8,128)(2,1)S(1)} %get-tuple-element.95), channel_id=1, source_target_pairs={{0,24},{16,8},{24,0},{8,16},{1,25},{17,9},{25,1},{9,17},{2,26},{18... | collective-permute-start | bytes 393224 | tf_op jit(solution)/shard_map/grad_weight/ppermute | solution.py:34
  130.0 11.8 %collective-permute-start.53 = (bf16[128,512]{1,0:T(8,128)(2,1)S(1)}, bf16[128,512]{1,0:T(8,128)(2,1)}, u32[]{:S(2)}, u32[]{:S(2)}) collective-permute-start(bf16[128,512]{1,0:T(8,128)(2,1)S(1)} %get-tuple-element.94), channel_id=1, source_target_pairs={{0,8},{16,0},{24,16},{8,24},{1,9},{17,1},{25,17},{9,25},{2,10},{18... | collective-permute-start | bytes 393224 | tf_op jit(solution)/shard_map/grad_weight/ppermute | solution.py:34
  141.9 16.8 %collective-permute-start.48 = (bf16[272,512]{1,0:T(8,128)(2,1)}, bf16[272,512]{1,0:T(8,128)(2,1)S(1)}, u32[]{:S(2)}, u32[]{:S(2)}) collective-permute-start(bf16[272,512]{1,0:T(8,128)(2,1)} %copy-done.54), channel_id=1, source_target_pairs={{0,2},{1,3},{2,0},{3,1},{4,6},{5,7},{6,4},{7,5},{8,10},{9,11},{10,... | collective-permute-start | bytes 835592 | tf_op jit(solution)/shard_map/d_act/ppermute | solution.py:24
  143.4 15.3 %collective-permute-start.49 = (bf16[272,512]{1,0:T(8,128)(2,1)}, bf16[272,512]{1,0:T(8,128)(2,1)S(1)}, u32[]{:S(2)}, u32[]{:S(2)}) collective-permute-start(bf16[272,512]{1,0:T(8,128)(2,1)} %copy-done.53), channel_id=1, source_target_pairs={{0,4},{1,5},{2,6},{3,7},{4,0},{5,1},{6,2},{7,3},{8,12},{9,13},{10,... | collective-permute-start | bytes 835592 | tf_op jit(solution)/shard_map/d_act/ppermute | solution.py:24
  143.9 14.8 %collective-permute-start.50 = (bf16[272,512]{1,0:T(8,128)(2,1)}, bf16[272,512]{1,0:T(8,128)(2,1)S(1)}, u32[]{:S(2)}, u32[]{:S(2)}) collective-permute-start(bf16[272,512]{1,0:T(8,128)(2,1)} %copy-done.52), channel_id=1, source_target_pairs={{0,6},{1,7},{2,4},{3,5},{4,2},{5,3},{6,0},{7,1},{8,14},{9,15},{10,... | collective-permute-start | bytes 835592 | tf_op jit(solution)/shard_map/d_act/ppermute | solution.py:24
  145.4 9.9 %collective-permute-start.55 = (bf16[128,512]{1,0:T(8,128)(2,1)}, bf16[128,512]{1,0:T(8,128)(2,1)S(1)}, u32[]{:S(2)}, u32[]{:S(2)}) collective-permute-start(bf16[128,512]{1,0:T(8,128)(2,1)} %collective-permute-done.52.refs_13_), channel_id=1, source_target_pairs={{0,1},{1,0},{2,3},{3,2},{4,5},{5,4},{6,7},{7,6},{8,9},{9,8},{10,11... | collective-permute-start | bytes 393224 | tf_op jit(solution)/shard_map/grad_weight/ppermute | solution.py:24
  145.4 9.9 %collective-permute-start.56 = (bf16[128,512]{1,0:T(8,128)(2,1)}, bf16[128,512]{1,0:T(8,128)(2,1)S(1)}, u32[]{:S(2)}, u32[]{:S(2)}) collective-permute-start(bf16[128,512]{1,0:T(8,128)(2,1)} %collective-permute-done.53.refs_14_), channel_id=1, source_target_pairs={{0,1},{1,0},{2,3},{3,2},{4,5},{5,4},{6,7},{7,6},{8,9},{9,8},{10,11... | collective-permute-start | bytes 393224 | tf_op jit(solution)/shard_map/grad_weight/ppermute | solution.py:24
  161.4 4.6 %collective-permute-start.58 = (f32[8,512]{1,0:T(8,128)S(1)}, f32[8,512]{1,0:T(8,128)S(1)}, u32[]{:S(2)}, u32[]{:S(2)}) collective-permute-start(f32[8,512]{1,0:T(8,128)S(1)} %pad_maximum_fusion.1), channel_id=1, source_target_pairs={{0,16},{8,24},{16,0},{24,8},{1,17},{9,25},{17,1},{25,9},{2,18},{10... | collective-permute-start | bytes 49160 | tf_op jit(solution)/shard_map/norm_backward/ppermute | solution.py:42
  161.4 5.5 %collective-permute-start.59 = (f32[8,512]{1,0:T(8,128)S(1)}, f32[8,512]{1,0:T(8,128)S(1)}, u32[]{:S(2)}, u32[]{:S(2)}) collective-permute-start(f32[8,512]{1,0:T(8,128)S(1)} %pad_maximum_fusion.1), channel_id=1, source_target_pairs={{0,8},{8,16},{16,24},{24,0},{1,9},{9,17},{17,25},{25,1},{2,10},{10... | collective-permute-start | bytes 49160 | tf_op jit(solution)/shard_map/norm_backward/ppermute | solution.py:42
  (94 other events, 359.6 us)

commit v6 on v5

--- a/solution.py
+++ b/solution.py
@@ -34,19 +34,15 @@
     return lax.ppermute(x, axis, [(order[i], order[(i + d) % n]) for i in range(n)])
 
 
+def exchange_sum(parts):
+    parts = list(parts)
+    while len(parts) > 1:
+        parts = [x + y for x, y in zip(parts[::2], parts[1::2])]
+    return parts[0]
+
+
 def exchange(x, axis):
-    n = lax.axis_size(axis)
-    me = lax.axis_index(axis)
-    slots = [x]
-    for d in range(1, n):
-        slots.append(lax.ppermute(x, axis, [(i, (i + d) % n) for i in range(n)]))
-    ordered = []
-    for a in range(n):
-        value = slots[0]
-        for d in range(1, n):
-            value = jnp.where((me - a) % n == d, slots[d], value)
-        ordered.append(value)
-    return ordered
+    return [x] + [xor_send(x, axis, k) for k in range(1, lax.axis_size(axis))]
 
 
 def params(limit):
@@ -90,18 +86,19 @@
     )(pltpu.with_memory_space_constraint(weight, pltpu.HBM))
 
 
-def weight_rows(index_ref, w_ref, j, width):
-    return w_ref[pl.ds(pl.multiple_of(index_ref[j] * width, width), width), :]
-
-
-def z_kernel(count, first, last, local_rows, index_ref, *refs):
+def weight_rows(place_ref, w_ref, k, width):
+    return w_ref[pl.ds(pl.multiple_of((place_ref[1] ^ k) * width, width), width), :]
+
+
+def z_kernel(ks, first, last, local_rows, place_ref, *refs):
+    count = len(ks)
     pieces, rest = refs[:count], list(refs[count:])
     w_ref = rest.pop(0)
     total = None if first else rest.pop(0)[...]
     width = pieces[0].shape[1]
     for j in range(count):
         part = jnp.dot(
-            pieces[j][...], weight_rows(index_ref, w_ref, j, width), preferred_element_type=f32
+            pieces[j][...], weight_rows(place_ref, w_ref, ks[j], width), preferred_element_type=f32
         )
         total = part if total is None else total + part
     if not last:
@@ -115,11 +112,11 @@
         sum_ref[v : v + 1, :] = jnp.sum(mine.astype(f32), axis=0, keepdims=True)
 
 
-def z_call(index, pieces, weight, before, last, local_rows):
-    count = len(pieces)
+def z_call(place, ks, pieces, weight, before, last, local_rows):
+    count = len(ks)
     tall, width = pieces[0].shape
     columns = weight.shape[1]
-    operands = [index] + list(pieces) + [weight] + ([] if before is None else [before])
+    operands = [place] + list(pieces) + [weight] + ([] if before is None else [before])
     if last:
         groups = tall // local_rows
         out_shape = (jax.ShapeDtypeStruct((local_rows, columns), bf16),) * groups
@@ -127,7 +124,7 @@
     else:
         out_shape = jax.ShapeDtypeStruct((tall, columns), f32)
     return pl.pallas_call(
-        functools.partial(z_kernel, count, before is None, last, local_rows),
+        functools.partial(z_kernel, tuple(ks), before is None, last, local_rows),
         out_shape=out_shape,
         in_specs=[IN_SMEM] + [IN_VMEM] * (len(operands) - 1),
         out_specs=jax.tree.map(lambda _: IN_VMEM, out_shape),
@@ -137,7 +134,7 @@
     )(*operands)
 
 
-def strip_kernel(n_slots, n_sums, rows, n_col, index_ref, *refs):
+def strip_kernel(n_slots, n_sums, rows, n_col, place_ref, *refs):
     z_refs, sum_refs = refs[: 2 * n_slots], refs[2 * n_slots : 2 * n_slots + n_sums]
     even_ref, odd_ref, strip = refs[2 * n_slots + n_sums :]
     local_rows = z_refs[0].shape[0]
@@ -151,16 +148,16 @@
             )
     part = 2 * local_rows // n_col
     for k in range(n_col):
-        start = pl.multiple_of(index_ref[k] * part, part)
+        start = pl.multiple_of((place_ref[1] ^ k) * part, part)
         (odd_ref if k % 2 else even_ref)[k // 2] = strip[pl.ds(start, part), :]
 
 
-def strip_call(index, z_slots, sums, rows, n_col):
+def strip_call(place, z_slots, sums, rows, n_col):
     local_rows, columns = z_slots[0][0].shape
     tall = 2 * local_rows
     wide = len(z_slots) * local_rows
     part = jax.ShapeDtypeStruct((n_col // 2, tall // n_col, wide), f32)
-    operands = [index] + [z for slot in z_slots for z in slot] + list(sums)
+    operands = [place] + [z for slot in z_slots for z in slot] + list(sums)
     return pl.pallas_call(
         functools.partial(strip_kernel, len(z_slots), len(sums), rows, n_col),
         out_shape=(part, part),
@@ -173,18 +170,22 @@
     )(*operands)
 
 
-def dz_kernel(n_batch, n_col, tile, constants, index_ref, *refs):
-    coef, hinge_coef, inv_coef, inv_share, hinge_share, diag_share = constants
+def dz_kernel(n_batch, n_col, tile, constants, place_ref, own_ref, *refs):
+    coef, hinge_coef, inv_coef, inv_share, hinge_share, diag_share, block_share = constants
     strip_refs = refs[:n_col]
     z_refs = refs[n_col : n_col + 2 * n_batch]
     dz_ref, share_ref, strips, full, centred = refs[n_col + 2 * n_batch :]
     local_rows, columns = z_refs[0].shape
     rows = local_rows * n_batch
     reach = n_batch // 2
-    share_ref[...] = jnp.zeros_like(share_ref)
+    own = own_ref[...]
+    block = lax.broadcasted_iota(jnp.int32, own.shape, 1) // local_rows
+    own = own * own * jnp.where((block > 0) & (block < n_batch - reach), 2.0, 1.0)
+    own = jnp.sum(jnp.sum(own, axis=0, keepdims=True), axis=1, keepdims=True)
+    share_ref[...] = jnp.broadcast_to(block_share * own, share_ref.shape)
     part = 2 * local_rows // n_col
     for k in range(n_col):
-        start = pl.multiple_of(index_ref[k] * part, part)
+        start = pl.multiple_of((place_ref[1] ^ k) * part, part)
         for s in range(n_batch):
             strips[s, pl.ds(start, part), :] = strip_refs[k][s].astype(f32)
     for v in range(2):
@@ -232,13 +233,13 @@
     lax.fori_loop(0, columns // tile, one_tile, 0)
 
 
-def dz_call(index, strips, z_slots, constants):
+def dz_call(place, own, strips, z_slots, constants):
     n_col, n_batch = len(strips), len(z_slots)
     local_rows, columns = z_slots[0][0].shape
     tall = 2 * local_rows
     rows = local_rows * n_batch
     tile = min(256, columns)
-    operands = [index] + list(strips) + [z for slot in z_slots for z in slot]
+    operands = [place, own] + list(strips) + [z for slot in z_slots for z in slot]
     return pl.pallas_call(
         functools.partial(dz_kernel, n_batch, n_col, tile, constants),
         out_shape=(
@@ -274,16 +275,17 @@
     return rows[0:1].astype(f32) + rows[1:2].astype(f32) + rows[2:3].astype(f32)
 
 
-def d_act_kernel(count, adds, index_ref, dz_ref, share_ref, w_ref, *refs):
+def d_act_kernel(count, adds, place_ref, dz_ref, share_ref, w_ref, *refs):
     local_rows, columns = dz_ref.shape[1] // adds[1], dz_ref.shape[2]
     tall = 2 * local_rows
     dz = jnp.concatenate([dz_ref[0, :local_rows], dz_ref[1, :local_rows]], axis=0)
     width = w_ref.shape[0] // adds[2]
     share = share_ref[0:1, 0:1]
     for j in range(count):
+        k = 2 * ((j + 1) % count) if adds[0] else 2 * j + 1
         part = lax.dot_general(
             dz,
-            weight_rows(index_ref, w_ref, j, width),
+            weight_rows(place_ref, w_ref, k, width),
             (((1,), (1,)), ((), ())),
             preferred_element_type=f32,
         )
@@ -299,12 +301,12 @@
             out_ref[tall:] = share_rows(whole_share, width, out_ref.dtype)
 
 
-def d_act_call(index, dz, share, weight, n_batch, n_col, got):
+def d_act_call(place, dz, share, weight, n_batch, n_col, got):
     columns = weight.shape[1]
     width = weight.shape[0] // n_col
     tall = 2 * dz.shape[1] // n_batch
     count = n_col // 2
-    operands = [index, dz, share, weight] + ([] if got is None else [got])
+    operands = [place, dz, share, weight] + ([] if got is None else [got])
     if got is None:
         out_shape = (jax.ShapeDtypeStruct((count, tall + EXTRA, width), bf16),)
     else:
@@ -321,25 +323,63 @@
     )(*operands)
 
 
-def weight_grad_kernel(groups, half, tile, place_ref, *refs):
-    n_far, aliased = groups[-2:]
-    near = [refs[g * half : (g + 1) * half] for g in range(3)]
-    arrived = refs[3 * half : 3 * half + n_far]
-    dz_ref = refs[3 * half + n_far]
-    out_ref, act, product, sems = refs[3 * half + n_far + 1 + aliased :]
+def held_place(plane, c, block, n_col, n_batch):
+    return (((n_col // n_batch) * plane + 2 * block) ^ (c - (c & 1))) >> 1
+
+
+def pick_kernel(n_batch, n_col, local_rows, place_ref, *refs):
+    half = n_col // 2
+    pieces, outs = refs[:half], refs[half:]
+    b, c = place_ref[0], place_ref[1]
+    position = jnp.where((b & 1) == 0, b >> 1, n_batch - 1 - (b >> 1))
+    i = 0
+    for block in range(n_col // n_batch // 2):
+        for d in range(1, n_batch):
+            ahead = position + d
+            ahead = jnp.where(ahead >= n_batch, ahead - n_batch, ahead)
+            plane = jnp.where(2 * ahead < n_batch, 2 * ahead, 2 * (n_batch - ahead) - 1)
+            chosen = held_place(plane, c, block, n_col, n_batch)
+            for e in range(half):
+
+                @pl.when(chosen == e)
+                def _():
+                    outs[i][...] = pieces[e][local_rows:]
+
+            i += 1
+
+
+def pick_call(place, pieces, n_batch, n_col):
+    tall, width = pieces[0].shape
+    count = n_col // n_batch // 2 * (n_batch - 1)
+    out_shape = (jax.ShapeDtypeStruct((tall // 2, width), bf16),) * count
+    return pl.pallas_call(
+        functools.partial(pick_kernel, n_batch, n_col, tall // 2),
+        out_shape=out_shape,
+        in_specs=[IN_SMEM] + [IN_VMEM] * len(pieces),
+        out_specs=(IN_VMEM,) * count,
+        compiler_params=params(4),
+        cost_estimate=cost(0, tall * width * count),
+        name="pick_blocks",
+    )(place, *pieces)
+
+
+def weight_grad_kernel(n_far, aliased, half, tile, which, place_ref, *refs):
+    near = [refs[:half], refs[half : 2 * half]]
+    arrived = refs[2 * half : 2 * half + n_far]
+    dz_ref = refs[2 * half + n_far]
+    out_ref, act, product, sems = refs[2 * half + n_far + 1 + aliased :]
+    block, parity = which
+    chosen = held_place(place_ref[0], place_ref[1], block, 2 * half, n_far + 1)
+    out_row = 2 * block + ((place_ref[1] & 1) ^ parity)
     local_rows = near[0][0].shape[0] // 2
     rows = dz_ref.shape[1]
     for e in range(half):
 
-        @pl.when(place_ref[0] == e)
+        @pl.when(chosen == e)
         def _():
             act[pl.ds(0, local_rows)] = near[0][e][:local_rows]
             act[pl.ds(rows, local_rows)] = near[0][e][local_rows:]
-            at = local_rows
-            for group in near[1:]:
-                size = group[e].shape[0]
-                act[pl.ds(at, size)] = group[e][...]
-                at += size
+            act[pl.ds(local_rows, rows - local_rows)] = near[1][e][...]
 
     for s in range(n_far):
         act[pl.ds(rows + (s + 1) * local_rows, local_rows)] = arrived[s][...]
@@ -356,7 +396,7 @@
             )
             total = part if total is None else total + part
         product[pl.ds(i * tile, tile)] = total
-        start = pl.multiple_of(place_ref[1] * width + i * tile, tile)
+        start = pl.multiple_of(out_row * width + i * tile, tile)
         copies.append(
             pltpu.make_async_copy(
                 product.at[pl.ds(i * tile, tile)], out_ref.at[pl.ds(start, tile)], sems.at[i]
@@ -367,7 +407,7 @@
         copy.wait()
 
 
-def weight_grad_call(place, near, arrived, dz, features, before):
+def weight_grad_call(place, which, near, arrived, dz, features, before):
     half = len(near[0])
     width = near[0][0].shape[1]
     _, rows, columns = dz.shape
@@ -381,7 +421,7 @@
         specs.append(ANYWHERE)
     return pl.pallas_call(
         functools.partial(
-            weight_grad_kernel, (len(arrived), int(before is not None)), half, tile
+            weight_grad_kernel, len(arrived), int(before is not None), half, tile, which
         ),
         out_shape=jax.ShapeDtypeStruct((features, columns), f32),
         in_specs=specs,
@@ -410,8 +450,10 @@
 def shards(views, norm_scale_gain, norm_shift_bias, weight):
     n_batch = lax.axis_size("batch")
     n_col = lax.axis_size("col")
-    b = lax.axis_index("batch")
-    c = lax.axis_index("col")
+    place = jnp.stack([lax.axis_index("batch"), lax.axis_index("col")]).astype(jnp.int32)
+    views, norm_scale_gain, norm_shift_bias, weight, place = lax.optimization_barrier(
+        (views, norm_scale_gain, norm_shift_bias, weight, place)
+    )
     n_view, local_rows, width = views.shape
     features, columns = weight.shape
     E = columns * n_col
@@ -424,9 +466,6 @@
     odds = [k + 1 for k in evens]
     far = evens[1:]
 
-    def places(ks):
-        return jnp.stack([c ^ k for k in ks]).astype(jnp.int32)
-
     with jax.named_scope("weight_load"):
         held_weight = load_call(weight)
     with jax.named_scope("norm_stats"):
@@ -435,8 +474,10 @@
         local_centred = hidden - local_mean[:, None, :]
         local_spread = jnp.sum(local_centred * local_centred, axis=1)
         stats = exchange(jnp.concatenate([local_mean, local_spread]), "batch")
-        mean = sum(s[:n_view] for s in stats) / n_batch
-        spread = sum(s[n_view:] + local_rows * jnp.square(s[:n_view] - mean) for s in stats)
+        mean = exchange_sum(s[:n_view] for s in stats) / n_batch
+        spread = exchange_sum(
+            s[n_view:] + local_rows * jnp.square(s[:n_view] - mean) for s in stats
+        )
         var = spread / rows
         inverse_deviation = (1.0 / jnp.sqrt(var + eps_norm))[:, None, :]
         normalised = (hidden - mean[:, None, :]) * inverse_deviation
@@ -447,16 +488,15 @@
         ring = [act[0]]
         for _ in range(1, n_batch):
             ring.append(ring_send(ring[-1], "batch", 1))
-        ring = lax.optimization_barrier(ring)
-        near_pieces = gather_pieces(jnp.concatenate(ring[1 : reach + 1]), n_col)
-        last_pieces = gather_pieces(jnp.concatenate(ring[reach + 1 :]), n_col)
+        far_pieces = gather_pieces(jnp.concatenate(ring[1:]), n_col)
     with jax.named_scope("z"):
 
         def z_of(source, groups):
             total = None
             for i, ks in enumerate(groups):
                 total = z_call(
-                    places(ks),
+                    place,
+                    ks,
                     [source[k] for k in ks],
                     held_weight,
                     total,
@@ -466,29 +506,30 @@
             return total
 
         z_own0, z_own1, z_sum = z_of(pieces, [[0, 1], far, [k + 1 for k in far]])
-        *z_near, _ = z_of(near_pieces, [evens, odds])
-        *z_last, _ = z_of(last_pieces, [evens, odds])
+        *z_far, _ = z_of(far_pieces, [evens, odds])
     with jax.named_scope("z_ring"):
         z_ring = [z_own1]
         for _ in range(1, n_batch):
             z_ring.append(ring_send(z_ring[-1], "batch", 1))
-        sums = [z_sum] + [ring_send(z_sum, "batch", d) for d in range(1, n_batch)]
-        slots = [list(pair) for pair in zip([z_own0] + z_near + z_last, z_ring)]
+        sums = exchange(z_sum, "batch")
+        slots = [list(pair) for pair in zip([z_own0] + z_far, z_ring)]
     with jax.named_scope("kernel"):
-        everyone = places(range(n_col))
-        even_part, odd_part = strip_call(everyone, slots[: reach + 1], sums, rows, n_col)
+        even_part, odd_part = strip_call(place, slots[: reach + 1], sums, rows, n_col)
         even_part = even_part + xor_send(odd_part, "col", 1)
         strip = even_part[0]
         for k in far:
             strip = strip + xor_send(even_part[k // 2], "col", k)
-        strip, slots[reach + 1 :] = lax.optimization_barrier((strip, slots[reach + 1 :]))
-        block = lax.broadcasted_iota(jnp.int32, (1, strip.shape[1]), 1) // local_rows
-        twice = jnp.where((block > 0) & (block < n_batch - reach), 2.0, 1.0)
-        block_share = jnp.sum(strip * strip * twice) / denom
+        strip, z_ring[reach + 1 :] = lax.optimization_barrier((strip, z_ring[reach + 1 :]))
+        slots = [list(pair) for pair in zip([z_own0] + z_far, z_ring)]
         mine = strip.astype(bf16)
         mine = jnp.stack([mine] + [ring_send(mine, "batch", d) for d in range(1, n_batch)])
+        mine, held_back = lax.optimization_barrier((mine, [pieces[k] for k in evens]))
         strips = gather_pieces(mine, n_col)
-        strips, held_back = lax.optimization_barrier((strips, [pieces[k] for k in evens]))
+        picked = pick_call(place, held_back, n_batch, n_col)
+        blocks = [
+            ring_send(x, "batch", 1 + i % (n_batch - 1)) for i, x in enumerate(picked)
+        ]
+        strips, blocks = lax.optimization_barrier((strips, blocks))
     with jax.named_scope("dz"):
         constants = (
             4.0 * scale / denom,
@@ -497,51 +538,32 @@
             25.0 / (rows * E) / n_batch,
             25.0 / (2 * E) / n_batch,
             1.0 / denom / n_batch,
-        )
-        dz, share = dz_call(everyone, [strips[k] for k in range(n_col)], slots, constants)
-        share = share + block_share
+            1.0 / denom,
+        )
+        dz, share = dz_call(place, strip, [strips[k] for k in range(n_col)], slots, constants)
     with jax.named_scope("d_act"):
-        (away,) = d_act_call(places(odds), dz, share, held_weight, n_batch, n_col, None)
+        (away,) = d_act_call(place, dz, share, held_weight, n_batch, n_col, None)
         got = xor_send(away, "col", 1)
-        *sends, d_act = d_act_call(
-            places(far + [0]), dz, share, held_weight, n_batch, n_col, got
-        )
+        *sends, d_act = d_act_call(place, dz, share, held_weight, n_batch, n_col, got)
         arrived = [xor_send(part, "col", k) for k, part in zip(far, sends)]
     with jax.named_scope("grad_weight"):
-        per_plane = n_col // n_batch
-        position = jnp.where(b % 2 == 0, b // 2, n_batch - 1 - b // 2)
-
-        def held_place(plane, i):
-            return ((per_plane * plane + 2 * i) ^ (c - c % 2)) // 2
-
         grad_weight = None
-        for i in range(per_plane // 2):
-            mine = []
-            for d in range(1, n_batch):
-                ahead = (position + d) % n_batch
-                plane = jnp.where(ahead < (n_batch + 1) // 2, 2 * ahead, 2 * (n_batch - ahead) - 1)
-                place = held_place(plane, i)
-                block = held_back[0][local_rows:]
-                for e in range(1, n_col // 2):
-                    block = jnp.where(place == e, held_back[e][local_rows:], block)
-                mine.append(ring_send(block, "batch", d))
-            mine, d_act = lax.optimization_barrier((mine, d_act))
+        for block in range(n_col // n_batch // 2):
+            mine = blocks[block * (n_batch - 1) : (block + 1) * (n_batch - 1)]
             other = [xor_send(x, "col", 1) for x in mine]
-            for parity, ks, blocks in ((0, evens, mine), (1, odds, other)):
-                row = 2 * i + (c % 2 if parity == 0 else 1 - c % 2)
+            for parity, ks, far_rows in ((0, evens, mine), (1, odds, other)):
                 grad_weight = weight_grad_call(
-                    jnp.stack([held_place(b, i), row]).astype(jnp.int32),
-                    [[group[k] for k in ks] for group in (pieces, near_pieces, last_pieces)],
-                    blocks,
+                    place,
+                    (block, parity),
+                    [[group[k] for k in ks] for group in (pieces, far_pieces)],
+                    far_rows,
                     dz,
                     features // n_batch,
                     grad_weight,
                 )
     with jax.named_scope("norm_backward"):
         arrived, d_act, grad_weight = lax.optimization_barrier((arrived, d_act, grad_weight))
-        shares = [share_of(part[tall:]) for part in [d_act] + arrived]
-        while len(shares) > 1:
-            shares = [x + y for x, y in zip(shares[::2], shares[1::2])]
+        share = exchange_sum(share_of(part[tall:]) for part in [d_act] + arrived)
         d_act = d_act[:tall]
         for part in arrived:
             d_act = d_act + part[:tall].astype(f32)
@@ -550,10 +572,10 @@
             [
                 jnp.sum(d_pre, axis=1),
                 jnp.sum(d_pre * normalised, axis=1),
-                jnp.broadcast_to(shares[0], (2 * n_view, width)),
+                jnp.broadcast_to(share, (2 * n_view, width)),
             ]
         )
-        both = sum(exchange(sums, "batch"))
+        both = exchange_sum(exchange(sums, "batch"))
         sum_b, sum_g = both[:n_view], both[n_view : 2 * n_view]
         loss = jnp.max(both[2 * n_view :])
         grad_bias = jnp.sum(sum_b, axis=0)

time: 170 us -> 140 us (0.82)
  local copies, waits for them, and re-layouts: 36.3 us -> 0.07 us
  waiting for transfers between devices: 32.8 us -> 46.4 us
  Pallas kernels: 35 us -> 29 us
    unnamed x165 -> x8, local copies, waits for them, and re-layouts: 36.2 us -> 0.04 us
    ppermute x39 -> x41, starting transfers between devices: 24.2 us -> 37 us  [xor_send(): return lax.ppermute(x, axis, [(i, i ^ k) for i in range(n)])]
    ppermute x15 -> x12, waiting for transfers between devices: 9.24 us -> 21 us  [ring_send(): lax.ppermute(x, axis, [(order[i], order[(i + d) % n]) for i in range(n)])]
    ppermute x39 -> x41, waiting for transfers between devices: 14.2 us -> 25.4 us  [xor_send(): return lax.ppermute(x, axis, [(i, i ^ k) for i in range(n)])]
    ppermute x6 -> x0, waiting for transfers between devices: 9.33 us -> none  [exchange(): slots.append(lax.ppermute(x, axis, [(i, (i + d) % n) for i in range(n)]))]
    ppermute x6 -> x0, starting transfers between devices: 8.68 us -> none  [exchange(): slots.append(lax.ppermute(x, axis, [(i, (i + d) % n) for i in range(n)]))]
    pallas_call x9 -> x8, Pallas kernels: 19.3 us -> 16 us  [the longest x5 9.62 us: z_call(): pl.pallas_call(functools.partial(z_kernel, tuple(ks), before is None, las...]
    ppermute x15 -> x12, starting transfers between devices: 22.5 us -> 19.8 us  [ring_send(): lax.ppermute(x, axis, [(order[i], order[(i + d) % n]) for i in range(n)])]
  transfers between devices with their start and end apart: 60 -> 53, of which waited for: 24 -> 22; matrix products, arithmetic and copies ran while one was open for 0% -> 0% of each run, Pallas kernels for 15% -> 15%
where the time goes in v6:
time: 140 us
  starting transfers between devices  56.8 us (41%)
  waiting for transfers between devices  46.4 us (33%)
  Pallas kernels  29 us (21%)
  other arithmetic  6.27 us (4%)
    ppermute x41, starting transfers between devices, xor_send(): return lax.ppermute(x, axis, [(i, i ^ k) for i in range(n)])  37 us
    ppermute x41, waiting for transfers between devices, xor_send(): return lax.ppermute(x, axis, [(i, i ^ k) for i in range(n)])  25.4 us
    ppermute x12, waiting for transfers between devices, ring_send(): lax.ppermute(x, axis, [(order[i], order[(i + d) % n]) for i in range(n)])  21 us
    ppermute x12, starting transfers between devices, ring_send(): lax.ppermute(x, axis, [(order[i], order[(i + d) % n]) for i in range(n)])  19.8 us
    pallas_call x5, Pallas kernels, z_call(): pl.pallas_call(functools.partial(z_kernel, tuple(ks), before is None, las...  9.62 us
    pallas_call x2, Pallas kernels, weight_grad_call(): pl.pallas_call(functools.partial(weight_grad_kernel, len(arrived), int(be...  5.79 us
    pallas_call x1, Pallas kernels, dz_call(): pl.pallas_call(functools.partial(dz_kernel, n_batch, n_col, tile, constan...  4.66 us
    pallas_call x2, Pallas kernels, d_act_call(): pl.pallas_call(functools.partial(d_act_kernel, count, (got is not None, n...  3.69 us
  transfers between devices with their start and end apart: 53, of which 22 were waited for; matrix products, arithmetic and copies ran while one was open for 0% of the time, Pallas kernels for 15%

profile of v6, /device:TPU:0, one launch (start us, length us, event | category | flops | bytes accessed | tf_op | source)
XLA Modules:
  0.0 139.6 jit_solution(3119563048620781826)
XLA Ops:
  2.8 5.1 %collective-permute-start.2 = (f32[4,512]{1,0:T(4,128)S(1)}, f32[4,512]{1,0:T(4,128)S(1)}, u32[]{:S(2)}, u32[]{:S(2)}) collective-permute-start(f32[4,512]{1,0:T(4,128)S(1)} %pad_maximum_fusion.2), channel_id=1, source_target_pairs={{0,24},{8,16},{16,8},{24,0},{1,25},{9,17},{17,9},{25,1},{2,26},{10... | collective-permute-start | bytes 24584 | tf_op jit(solution)/shard_map/norm_stats/ppermute | solution.py:24
  9.5 2.9 %collective-permute-done.1 = f32[4,512]{1,0:T(4,128)S(1)} collective-permute-done((f32[4,512]{1,0:T(4,128)S(1)}, f32[4,512]{1,0:T(4,128)S(1)}, u32[]{:S(2)}, u32[]{:S(2)}) %collective-permute-start.1) | collective-permute-done | bytes 8224 | tf_op jit(solution)/shard_map/norm_stats/ppermute | solution.py:24
  12.5 1.2 fusion.17
  13.7 2.1 %collective-permute-start.10 = (bf16[128,512]{1,0:T(8,128)(2,1)S(1)}, bf16[128,512]{1,0:T(8,128)(2,1)S(1)}, u32[]{:S(2)}, u32[]{:S(2)}) collective-permute-start(bf16[128,512]{1,0:T(8,128)(2,1)S(1)} %slice_bitcast_fusion), channel_id=1, source_target_pairs={{0,16},{16,24},{24,8},{8,0},{1,17},{17,25},{25,9},{9,1},{2,18},{18... | collective-permute-start | bytes 393224 | tf_op jit(solution)/shard_map/act_gather/ppermute | solution.py:34
  15.8 2.4 %collective-permute-start.7 = (bf16[256,512]{1,0:T(8,128)(2,1)S(1)}, bf16[256,512]{1,0:T(8,128)(2,1)S(1)}, u32[]{:S(2)}, u32[]{:S(2)}) collective-permute-start(bf16[256,512]{1,0:T(8,128)(2,1)S(1)} %bitcast.27), channel_id=1, source_target_pairs={{0,6},{1,7},{2,4},{3,5},{4,2},{5,3},{6,0},{7,1},{8,14},{9,15},{10,... | collective-permute-start | bytes 786440 | tf_op jit(solution)/shard_map/act_gather/ppermute | solution.py:24
  18.9 2.8 %collective-permute-start.11 = (bf16[128,512]{1,0:T(8,128)(2,1)S(1)}, bf16[128,512]{1,0:T(8,128)(2,1)S(1)}, u32[]{:S(2)}, u32[]{:S(2)}) collective-permute-start(bf16[128,512]{1,0:T(8,128)(2,1)S(1)} %collective-permute-done.10), channel_id=1, source_target_pairs={{0,16},{16,24},{24,8},{8,0},{1,17},{17,25},{25,9},{9,1},{2,18},{18... | collective-permute-start | bytes 393224 | tf_op jit(solution)/shard_map/act_gather/ppermute | solution.py:34
  21.7 1.5 %collective-permute-start.5 = (bf16[256,512]{1,0:T(8,128)(2,1)S(1)}, bf16[256,512]{1,0:T(8,128)(2,1)S(1)}, u32[]{:S(2)}, u32[]{:S(2)}) collective-permute-start(bf16[256,512]{1,0:T(8,128)(2,1)S(1)} %bitcast.29), channel_id=1, source_target_pairs={{0,4},{1,5},{2,6},{3,7},{4,0},{5,1},{6,2},{7,3},{8,12},{9,13},{10,... | collective-permute-start | bytes 786440 | tf_op jit(solution)/shard_map/act_gather/ppermute | solution.py:24
  23.2 1.5 %collective-permute-start.3 = (bf16[256,512]{1,0:T(8,128)(2,1)S(1)}, bf16[256,512]{1,0:T(8,128)(2,1)S(1)}, u32[]{:S(2)}, u32[]{:S(2)}) collective-permute-start(bf16[256,512]{1,0:T(8,128)(2,1)S(1)} %bitcast.30), channel_id=1, source_target_pairs={{0,2},{1,3},{2,0},{3,1},{4,6},{5,7},{6,4},{7,5},{8,10},{9,11},{10,... | collective-permute-start | bytes 786440 | tf_op jit(solution)/shard_map/act_gather/ppermute | solution.py:24
  24.7 2.8 %collective-permute-start.12 = (bf16[128,512]{1,0:T(8,128)(2,1)S(1)}, bf16[128,512]{1,0:T(8,128)(2,1)S(1)}, u32[]{:S(2)}, u32[]{:S(2)}) collective-permute-start(bf16[128,512]{1,0:T(8,128)(2,1)S(1)} %collective-permute-done.11), channel_id=1, source_target_pairs={{0,16},{16,24},{24,8},{8,0},{1,17},{17,25},{25,9},{9,1},{2,18},{18... | collective-permute-start | bytes 393224 | tf_op jit(solution)/shard_map/act_gather/ppermute | solution.py:34
  27.7 2.4 %collective-permute-done.12 = bf16[128,512]{1,0:T(8,128)(2,1)S(1)} collective-permute-done((bf16[128,512]{1,0:T(8,128)(2,1)S(1)}, bf16[128,512]{1,0:T(8,128)(2,1)S(1)}, u32[]{:S(2)}, u32[]{:S(2)}) %collective-permute-start.12) | collective-permute-done | bytes 131104 | tf_op jit(solution)/shard_map/act_gather/ppermute | solution.py:34
  30.1 3.1 %collective-permute-start.18 = (bf16[384,512]{1,0:T(8,128)(2,1)S(1)}, bf16[384,512]{1,0:T(8,128)(2,1)S(1)}, u32[]{:S(2)}, u32[]{:S(2)}) collective-permute-start(bf16[384,512]{1,0:T(8,128)(2,1)S(1)} %constant_dynamic-update-slice_fusion.refs_0_.refs_4_), channel_id=1, source_target_pairs={{0,6},{1,7},{2,4},{3,5},{4,2},{5,3},{6,0},{7,1},{8,14},{9,15},{10,... | collective-permute-start | bytes 1179656 | tf_op jit(solution)/shard_map/act_gather/ppermute | solution.py:24
  34.4 3.5 %weight_load.1.refs_2_.refs_3_.refs_4_.w_ref = bf16[4096,1024]{1,0:T(8,128)(2,1)S(1)} custom-call(bf16[4096,1024]{1,0:T(8,128)(2,1)} %w_ref), custom_call_target="tpu_custom_call" | custom-call | bytes 16777216 | tf_op jit(solution)/shard_map/weight_load/weight_load/pallas_call | solution.py:77
  37.9 1.2 z_matmul.5.refs_4_
  39.1 1.5 %z_matmul.6.refs_4_ = f32[256,1024]{1,0:T(8,128)S(1)} custom-call(s32[2]{0:T(128)S(1)} %pad_add_fusion.place_ref, bf16[256,512]{1,0:T(8,128)(2,1)S(1)} %collective-permute-done.3.refs_0_.refs_1_, bf16[256,512]{1,0:T(8,128)(2,1)S(1)} %collective-permute-done.5.refs_1_.refs_2_, bf16[256,512]{1,0:T(8,128)(2,1)S(1)} %collective-permute-done.7.refs_2_.refs_3_, ...), custom_call_target="tpu_custom_call" | custom-call | flops 805306368 | bytes 524288 | tf_op jit(solution)/shard_map/z/z_matmul/pallas_call | solution.py:126
  40.7 1.5 %z_matmul.7 = (bf16[128,1024]{1,0:T(8,128)(2,1)S(1)}, bf16[128,1024]{1,0:T(8,128)(2,1)S(1)}, f32[2,1024]{1,0:T(2,128)S(1)}) custom-call(s32[2]{0:T(128)S(1)} %pad_add_fusion.place_ref, bf16[256,512]{1,0:T(8,128)(2,1)S(1)} %collective-permute-done.4.refs_0_.refs_1_, bf16[256,512]{1,0:T(8,128)(2,1)S(1)} %collective-permute-done.6.refs_1_.refs_2_, ...), custom_call_target="tpu_custom_call" | custom-call | flops 805306368 | bytes 524288 | tf_op jit(solution)/shard_map/z/z_matmul/pallas_call | solution.py:126
  42.2 3.4 %collective-permute-start.20 = (bf16[128,1024]{1,0:T(8,128)(2,1)S(1)}, bf16[128,1024]{1,0:T(8,128)(2,1)S(1)}, u32[]{:S(2)}, u32[]{:S(2)}) collective-permute-start(bf16[128,1024]{1,0:T(8,128)(2,1)S(1)} %get-tuple-element.56.refs_1_.refs_9_), channel_id=1, source_target_pairs={{0,16},{16,24},{24,8},{8,0},{1,17},{17,25},{25,9},{9,1},{2,18},{18... | collective-permute-start | bytes 786440 | tf_op jit(solution)/shard_map/z_ring/ppermute | solution.py:34
  46.1 3.4 %collective-permute-done.16.refs_2_.refs_6_ = bf16[384,512]{1,0:T(8,128)(2,1)S(1)} collective-permute-done((bf16[384,512]{1,0:T(8,128)(2,1)S(1)}, bf16[384,512]{1,0:T(8,128)(2,1)S(1)}, u32[]{:S(2)}, u32[]{:S(2)}) %collective-permute-start.16) | collective-permute-done | bytes 393248 | tf_op jit(solution)/shard_map/act_gather/ppermute | solution.py:24
  50.1 1.3 collective-permute-done.20.refs_3_.refs_11_
  51.4 3.4 %collective-permute-start.21 = (bf16[128,1024]{1,0:T(8,128)(2,1)S(1)}, bf16[128,1024]{1,0:T(8,128)(2,1)S(1)}, u32[]{:S(2)}, u32[]{:S(2)}) collective-permute-start(bf16[128,1024]{1,0:T(8,128)(2,1)S(1)} %collective-permute-done.20.refs_3_.refs_11_), channel_id=1, source_target_pairs={{0,16},{16,24},{24,8},{8,0},{1,17},{17,25},{25,9},{9,1},{2,18},{18... | collective-permute-start | bytes 786440 | tf_op jit(solution)/shard_map/z_ring/ppermute | solution.py:34
  54.8 2.3 %z_matmul.8.refs_5_ = f32[384,1024]{1,0:T(8,128)S(1)} custom-call(s32[2]{0:T(128)S(1)} %pad_add_fusion.place_ref, bf16[384,512]{1,0:T(8,128)(2,1)S(1)} %constant_dynamic-update-slice_fusion.refs_0_.refs_4_, bf16[384,512]{1,0:T(8,128)(2,1)S(1)} %collective-permute-done.14.refs_1_.refs_5_, bf16[384,512]{1,0:T(8,128)(2,1)S(1)} %collective-permute-done.16.refs_2_.refs_6_, ...), custom_call_target="tpu_custom_call" | custom-call | flops 1610612736 | bytes 786432 | tf_op jit(solution)/shard_map/z/z_matmul/pallas_call | solution.py:126
  57.3 4.3 %collective-permute-start.22 = (f32[2,1024]{1,0:T(2,128)S(1)}, f32[2,1024]{1,0:T(2,128)S(1)}, u32[]{:S(2)}, u32[]{:S(2)}) collective-permute-start(f32[2,1024]{1,0:T(2,128)S(1)} %get-tuple-element.59.refs_6_), channel_id=1, source_target_pairs={{0,8},{8,0},{16,24},{24,16},{1,9},{9,1},{17,25},{25,17},{2,10},{10... | collective-permute-start | bytes 24584 | tf_op jit(solution)/shard_map/z_ring/ppermute | solution.py:24
  61.6 3.0 %z_matmul.9 = (bf16[128,1024]{1,0:T(8,128)(2,1)S(1)}, bf16[128,1024]{1,0:T(8,128)(2,1)S(1)}, bf16[128,1024]{1,0:T(8,128)(2,1)S(1)}, f32[3,1024]{1,0:T(4,128)}) custom-call(s32[2]{0:T(128)S(1)} %pad_add_fusion.place_ref, bf16[384,512]{1,0:T(8,128)(2,1)S(1)} %collective-permute-done.13.refs_0_.refs_4_, ...), custom_call_target="tpu_custom_call" | custom-call | flops 1610612736 | bytes 786432 | tf_op jit(solution)/shard_map/z/z_matmul/pallas_call | solution.py:126
  64.6 1.2 kernel_strip.1
  65.8 1.4 %collective-permute-done.25 = f32[4,32,384]{2,1,0:T(8,128)S(1)} collective-permute-done((f32[4,32,384]{2,1,0:T(8,128)S(1)}, f32[4,32,384]{2,1,0:T(8,128)S(1)}, u32[]{:S(2)}, u32[]{:S(2)}) %collective-permute-start.25) | collective-permute-done | bytes 196640 | tf_op jit(solution)/shard_map/kernel/ppermute | solution.py:24
  67.3 1.5 %collective-permute-start.26 = (f32[32,384]{1,0:T(8,128)S(1)}, f32[32,384]{1,0:T(8,128)S(1)}, u32[]{:S(2)}, u32[]{:S(2)}) collective-permute-start(f32[32,384]{1,0:T(8,128)S(1)} %get-tuple-element.102), channel_id=1, source_target_pairs={{0,2},{1,3},{2,0},{3,1},{4,6},{5,7},{6,4},{7,5},{8,10},{9,11},{10,... | collective-permute-start | bytes 147464 | tf_op jit(solution)/shard_map/kernel/ppermute | solution.py:24
  68.8 1.5 %collective-permute-start.28 = (f32[32,384]{1,0:T(8,128)S(1)}, f32[32,384]{1,0:T(8,128)S(1)}, u32[]{:S(2)}, u32[]{:S(2)}) collective-permute-start(f32[32,384]{1,0:T(8,128)S(1)} %get-tuple-element.103), channel_id=1, source_target_pairs={{0,6},{1,7},{2,4},{3,5},{4,2},{5,3},{6,0},{7,1},{8,14},{9,15},{10,... | collective-permute-start | bytes 147464 | tf_op jit(solution)/shard_map/kernel/ppermute | solution.py:24
  71.5 2.4 %collective-permute-done.28 = f32[32,384]{1,0:T(8,128)S(1)} collective-permute-done((f32[32,384]{1,0:T(8,128)S(1)}, f32[32,384]{1,0:T(8,128)S(1)}, u32[]{:S(2)}, u32[]{:S(2)}) %collective-permute-start.28) | collective-permute-done | bytes 49184 | tf_op jit(solution)/shard_map/kernel/ppermute | solution.py:24
  74.5 4.1 %collective-permute-done.29.refs_15_ = bf16[128,1024]{1,0:T(8,128)(2,1)S(1)} collective-permute-done((bf16[128,1024]{1,0:T(8,128)(2,1)S(1)}, bf16[128,1024]{1,0:T(8,128)(2,1)S(1)}, u32[]{:S(2)}, u32[]{:S(2)}) %collective-permute-start.29) | collective-permute-done | bytes 262176 | tf_op jit(solution)/shard_map/z_ring/ppermute | solution.py:34
  79.6 2.0 %collective-permute-start.30 = (bf16[32,384]{1,0:T(8,128)(2,1)S(1)}, bf16[32,384]{1,0:T(8,128)(2,1)S(1)}, u32[]{:S(2)}, u32[]{:S(2)}) collective-permute-start(bf16[32,384]{1,0:T(8,128)(2,1)S(1)} %convert_element_type.47), channel_id=1, source_target_pairs={{0,16},{16,24},{24,8},{8,0},{1,17},{17,25},{25,9},{9,1},{2,18},{18... | collective-permute-start | bytes 73736 | tf_op jit(solution)/shard_map/kernel/ppermute | solution.py:34
  81.6 2.6 %collective-permute-done.31 = bf16[32,384]{1,0:T(8,128)(2,1)S(1)} collective-permute-done((bf16[32,384]{1,0:T(8,128)(2,1)S(1)}, bf16[32,384]{1,0:T(8,128)(2,1)S(1)}, u32[]{:S(2)}, u32[]{:S(2)}) %collective-permute-start.31) | collective-permute-done | bytes 24608 | tf_op jit(solution)/shard_map/kernel/ppermute | solution.py:34
  84.2 2.1 %collective-permute-done.32 = bf16[32,384]{1,0:T(8,128)(2,1)S(1)} collective-permute-done((bf16[32,384]{1,0:T(8,128)(2,1)S(1)}, bf16[32,384]{1,0:T(8,128)(2,1)S(1)}, u32[]{:S(2)}, u32[]{:S(2)}) %collective-permute-start.32) | collective-permute-done | bytes 24608 | tf_op jit(solution)/shard_map/kernel/ppermute | solution.py:34
  86.3 2.7 %collective-permute-start.38 = (bf16[4,32,384]{2,1,0:T(8,128)(2,1)S(1)}, bf16[4,32,384]{2,1,0:T(8,128)(2,1)S(1)}, u32[]{:S(2)}, u32[]{:S(2)}) collective-permute-start(bf16[4,32,384]{2,1,0:T(8,128)(2,1)S(1)} %pad_maximum_fusion.refs_0_), channel_id=1, source_target_pairs={{0,6},{1,7},{2,4},{3,5},{4,2},{5,3},{6,0},{7,1},{8,14},{9,15},{10,... | collective-permute-start | bytes 294920 | tf_op jit(solution)/shard_map/kernel/ppermute | solution.py:24
  91.1 1.4 %collective-permute-done.38.refs_6_ = bf16[4,32,384]{2,1,0:T(8,128)(2,1)S(1)} collective-permute-done((bf16[4,32,384]{2,1,0:T(8,128)(2,1)S(1)}, bf16[4,32,384]{2,1,0:T(8,128)(2,1)S(1)}, u32[]{:S(2)}, u32[]{:S(2)}) %collective-permute-start.38) | collective-permute-done | bytes 98336 | tf_op jit(solution)/shard_map/kernel/ppermute | solution.py:24
  92.5 1.7 %collective-permute-start.41 = (bf16[128,512]{1,0:T(8,128)(2,1)S(1)}, bf16[128,512]{1,0:T(8,128)(2,1)S(1)}, u32[]{:S(2)}, u32[]{:S(2)}) collective-permute-start(bf16[128,512]{1,0:T(8,128)(2,1)S(1)} %get-tuple-element.69), channel_id=1, source_target_pairs={{0,24},{16,8},{24,0},{8,16},{1,25},{17,9},{25,1},{9,17},{2,26},{18... | collective-permute-start | bytes 393224 | tf_op jit(solution)/shard_map/kernel/ppermute | solution.py:34
  95.7 4.6 %collective-permute-done.41.refs_9_ = bf16[128,512]{1,0:T(8,128)(2,1)S(1)} collective-permute-done((bf16[128,512]{1,0:T(8,128)(2,1)S(1)}, bf16[128,512]{1,0:T(8,128)(2,1)S(1)}, u32[]{:S(2)}, u32[]{:S(2)}) %collective-permute-start.41) | collective-permute-done | bytes 131104 | tf_op jit(solution)/shard_map/kernel/ppermute | solution.py:34
  100.3 3.2 %collective-permute-done.42.refs_10_ = bf16[128,512]{1,0:T(8,128)(2,1)S(1)} collective-permute-done((bf16[128,512]{1,0:T(8,128)(2,1)S(1)}, bf16[128,512]{1,0:T(8,128)(2,1)S(1)}, u32[]{:S(2)}, u32[]{:S(2)}) %collective-permute-start.42) | collective-permute-done | bytes 131104 | tf_op jit(solution)/shard_map/kernel/ppermute | solution.py:34
  103.6 4.7 %embedding_gradient.1 = (bf16[2,512,1024]{2,1,0:T(8,128)(2,1)S(1)}, f32[8,128]{1,0:T(8,128)S(1)}) custom-call(s32[2]{0:T(128)S(1)} %pad_add_fusion.place_ref, f32[32,384]{1,0:T(8,128)S(1)} %fusion.25.own_ref, bf16[4,32,384]{2,1,0:T(8,128)(2,1)S(1)} %pad_maximum_fusion.refs_0_, bf16[4,32,384]{2,1,0:T(8,128)(2,1)S(1)} %collective-permute-done.33.refs_1_, ...), custom_call_target="tpu_custom_call" | custom-call | flops 1073741824 | bytes 4194304 | tf_op jit(solution)/shard_map/dz/embedding_gradient/pallas_call | solution.py:243
  108.3 1.8 %d_act_matmul.2 = bf16[4,272,512]{2,1,0:T(8,128)(2,1)S(1)} custom-call(s32[2]{0:T(128)S(1)} %pad_add_fusion.place_ref, bf16[2,512,1024]{2,1,0:T(8,128)(2,1)S(1)} %get-tuple-element.81.dz_ref.refs_11_, f32[8,128]{1,0:T(8,128)S(1)} %get-tuple-element.82.share_ref, bf16[4096,1024]{1,0:T(8,128)(2,1)S(1)} %weight_load.1.refs_2_.refs_3_.refs_4_.w_ref), custom_call_target="tpu_custom_call" | custom-call | flops 1073741824 | bytes 1048576 | tf_op jit(solution)/shard_map/d_act/d_act_matmul/pallas_call | solution.py:315
  110.7 2.2 %collective-permute-done.43.refs_0_ = bf16[4,272,512]{2,1,0:T(8,128)(2,1)S(1)} collective-permute-done((bf16[4,272,512]{2,1,0:T(8,128)(2,1)S(1)}, bf16[4,272,512]{2,1,0:T(8,128)(2,1)S(1)}, u32[]{:S(2)}, u32[]{:S(2)}) %collective-permute-start.43) | collective-permute-done | bytes 1114144 | tf_op jit(solution)/shard_map/d_act/ppermute | solution.py:24
  112.9 1.8 %d_act_matmul.3 = (bf16[272,512]{1,0:T(8,128)(2,1)S(1)}, bf16[272,512]{1,0:T(8,128)(2,1)S(1)}, bf16[272,512]{1,0:T(8,128)(2,1)S(1)}, f32[272,512]{1,0:T(8,128)S(1)}) custom-call(s32[2]{0:T(128)S(1)} %pad_add_fusion.place_ref, bf16[2,512,1024]{2,1,0:T(8,128)(2,1)S(1)} %get-tuple-element.81.dz_ref.refs_11_, f32[8,128]{1,0:T(8,128)S(1)} %get-tuple-element.82.share_ref, ...), custom_call_target="tpu_custom_call" | custom-call | flops 1073741824 | bytes 1048576 | tf_op jit(solution)/shard_map/d_act/d_act_matmul/pallas_call | solution.py:315
  114.8 1.5 %collective-permute-start.44 = (bf16[272,512]{1,0:T(8,128)(2,1)S(1)}, bf16[272,512]{1,0:T(8,128)(2,1)S(1)}, u32[]{:S(2)}, u32[]{:S(2)}) collective-permute-start(bf16[272,512]{1,0:T(8,128)(2,1)S(1)} %get-tuple-element.83), channel_id=1, source_target_pairs={{0,2},{1,3},{2,0},{3,1},{4,6},{5,7},{6,4},{7,5},{8,10},{9,11},{10,... | collective-permute-start | bytes 835592 | tf_op jit(solution)/shard_map/d_act/ppermute | solution.py:24
  116.3 1.7 %collective-permute-start.45 = (bf16[272,512]{1,0:T(8,128)(2,1)S(1)}, bf16[272,512]{1,0:T(8,128)(2,1)S(1)}, u32[]{:S(2)}, u32[]{:S(2)}) collective-permute-start(bf16[272,512]{1,0:T(8,128)(2,1)S(1)} %get-tuple-element.84), channel_id=1, source_target_pairs={{0,4},{1,5},{2,6},{3,7},{4,0},{5,1},{6,2},{7,3},{8,12},{9,13},{10,... | collective-permute-start | bytes 835592 | tf_op jit(solution)/shard_map/d_act/ppermute | solution.py:24
  118.9 2.9 %weight_gradient.2.refs_12_ = f32[1024,1024]{1,0:T(8,128)} custom-call(s32[2]{0:T(128)S(1)} %pad_add_fusion.place_ref, bf16[256,512]{1,0:T(8,128)(2,1)S(1)} %bitcast.33, bf16[256,512]{1,0:T(8,128)(2,1)S(1)} %collective-permute-done.3.refs_0_.refs_1_, bf16[256,512]{1,0:T(8,128)(2,1)S(1)} %collective-permute-done.5.refs_1_.refs_2_, ...), custom_call_target="tpu_custom_call" | custom-call | flops 1073741824 | bytes 2097152 | tf_op jit(solution)/shard_map/grad_weight/weight_gradient/pallas_call | solution.py:422
  121.8 2.9 %weight_gradient.3 = f32[1024,1024]{1,0:T(8,128)} custom-call(s32[2]{0:T(128)S(1)} %pad_add_fusion.place_ref, bf16[256,512]{1,0:T(8,128)(2,1)S(1)} %collective-permute-done.9.refs_1_.refs_0_, bf16[256,512]{1,0:T(8,128)(2,1)S(1)} %collective-permute-done.4.refs_0_.refs_1_, ...), custom_call_target="tpu_custom_call", output_to_operand_aliasing={{}: (13, {})} | custom-call | flops 1073741824 | bytes 2097152 | tf_op jit(solution)/shard_map/grad_weight/weight_gradient/pallas_call | solution.py:422
  124.7 6.0 %collective-permute-done.45 = bf16[272,512]{1,0:T(8,128)(2,1)S(1)} collective-permute-done((bf16[272,512]{1,0:T(8,128)(2,1)S(1)}, bf16[272,512]{1,0:T(8,128)(2,1)S(1)}, u32[]{:S(2)}, u32[]{:S(2)}) %collective-permute-start.45) | collective-permute-done | bytes 278560 | tf_op jit(solution)/shard_map/d_act/ppermute | solution.py:24
  131.5 2.2 %collective-permute-start.52 = (f32[8,512]{1,0:T(8,128)S(1)}, f32[8,512]{1,0:T(8,128)S(1)}, u32[]{:S(2)}, u32[]{:S(2)}) collective-permute-start(f32[8,512]{1,0:T(8,128)S(1)} %pad_maximum_fusion.1), channel_id=1, source_target_pairs={{0,24},{8,16},{16,8},{24,0},{1,25},{9,17},{17,9},{25,1},{2,26},{10... | collective-permute-start | bytes 49160 | tf_op jit(solution)/shard_map/norm_backward/ppermute | solution.py:24
  133.6 1.3 collective-permute-start.50
  135.0 1.1 collective-permute-done.51
  (102 shorter events, 18.9 us)
Async XLA Ops:
  2.8 6.7 %collective-permute-start.2 = (f32[4,512]{1,0:T(4,128)S(1)}, f32[4,512]{1,0:T(4,128)S(1)}, u32[]{:S(2)}, u32[]{:S(2)}) collective-permute-start(f32[4,512]{1,0:T(4,128)S(1)} %pad_maximum_fusion.2), channel_id=1, source_target_pairs={{0,24},{8,16},{16,8},{24,0},{1,25},{9,17},{17,9},{25,1},{2,26},{10... | collective-permute-start | bytes 24584 | tf_op jit(solution)/shard_map/norm_stats/ppermute | solution.py:24
  7.9 4.5 %collective-permute-start.1 = (f32[4,512]{1,0:T(4,128)S(1)}, f32[4,512]{1,0:T(4,128)S(1)}, u32[]{:S(2)}, u32[]{:S(2)}) collective-permute-start(f32[4,512]{1,0:T(4,128)S(1)} %pad_maximum_fusion.2), channel_id=1, source_target_pairs={{0,16},{8,24},{16,0},{24,8},{1,17},{9,25},{17,1},{25,9},{2,18},{10... | collective-permute-start | bytes 24584 | tf_op jit(solution)/shard_map/norm_stats/ppermute | solution.py:24
  7.9 4.5 %collective-permute-start = (f32[4,512]{1,0:T(4,128)S(1)}, f32[4,512]{1,0:T(4,128)S(1)}, u32[]{:S(2)}, u32[]{:S(2)}) collective-permute-start(f32[4,512]{1,0:T(4,128)S(1)} %pad_maximum_fusion.2), channel_id=1, source_target_pairs={{0,8},{8,0},{16,24},{24,16},{1,9},{9,1},{17,25},{25,17},{2,10},{10... | collective-permute-start | bytes 24584 | tf_op jit(solution)/shard_map/norm_stats/ppermute | solution.py:24
  13.7 5.1 %collective-permute-start.10 = (bf16[128,512]{1,0:T(8,128)(2,1)S(1)}, bf16[128,512]{1,0:T(8,128)(2,1)S(1)}, u32[]{:S(2)}, u32[]{:S(2)}) collective-permute-start(bf16[128,512]{1,0:T(8,128)(2,1)S(1)} %slice_bitcast_fusion), channel_id=1, source_target_pairs={{0,16},{16,24},{24,8},{8,0},{1,17},{17,25},{25,9},{9,1},{2,18},{18... | collective-permute-start | bytes 393224 | tf_op jit(solution)/shard_map/act_gather/ppermute | solution.py:34
  15.8 11.8 %collective-permute-start.7 = (bf16[256,512]{1,0:T(8,128)(2,1)S(1)}, bf16[256,512]{1,0:T(8,128)(2,1)S(1)}, u32[]{:S(2)}, u32[]{:S(2)}) collective-permute-start(bf16[256,512]{1,0:T(8,128)(2,1)S(1)} %bitcast.27), channel_id=1, source_target_pairs={{0,6},{1,7},{2,4},{3,5},{4,2},{5,3},{6,0},{7,1},{8,14},{9,15},{10,... | collective-permute-start | bytes 786440 | tf_op jit(solution)/shard_map/act_gather/ppermute | solution.py:24
  18.9 5.8 %collective-permute-start.11 = (bf16[128,512]{1,0:T(8,128)(2,1)S(1)}, bf16[128,512]{1,0:T(8,128)(2,1)S(1)}, u32[]{:S(2)}, u32[]{:S(2)}) collective-permute-start(bf16[128,512]{1,0:T(8,128)(2,1)S(1)} %collective-permute-done.10), channel_id=1, source_target_pairs={{0,16},{16,24},{24,8},{8,0},{1,17},{17,25},{25,9},{9,1},{2,18},{18... | collective-permute-start | bytes 393224 | tf_op jit(solution)/shard_map/act_gather/ppermute | solution.py:34
  21.7 11.5 %collective-permute-start.9 = (bf16[256,512]{1,0:T(8,128)(2,1)S(1)}, bf16[256,512]{1,0:T(8,128)(2,1)S(1)}, u32[]{:S(2)}, u32[]{:S(2)}) collective-permute-start(bf16[256,512]{1,0:T(8,128)(2,1)S(1)} %bitcast.28), channel_id=1, source_target_pairs={{0,1},{1,0},{2,3},{3,2},{4,5},{5,4},{6,7},{7,6},{8,9},{9,8},{10,11... | collective-permute-start | bytes 786440 | tf_op jit(solution)/shard_map/act_gather/ppermute | solution.py:24
  21.7 11.5 %collective-permute-start.5 = (bf16[256,512]{1,0:T(8,128)(2,1)S(1)}, bf16[256,512]{1,0:T(8,128)(2,1)S(1)}, u32[]{:S(2)}, u32[]{:S(2)}) collective-permute-start(bf16[256,512]{1,0:T(8,128)(2,1)S(1)} %bitcast.29), channel_id=1, source_target_pairs={{0,4},{1,5},{2,6},{3,7},{4,0},{5,1},{6,2},{7,3},{8,12},{9,13},{10,... | collective-permute-start | bytes 786440 | tf_op jit(solution)/shard_map/act_gather/ppermute | solution.py:24
  23.2 10.7 %collective-permute-start.3 = (bf16[256,512]{1,0:T(8,128)(2,1)S(1)}, bf16[256,512]{1,0:T(8,128)(2,1)S(1)}, u32[]{:S(2)}, u32[]{:S(2)}) collective-permute-start(bf16[256,512]{1,0:T(8,128)(2,1)S(1)} %bitcast.30), channel_id=1, source_target_pairs={{0,2},{1,3},{2,0},{3,1},{4,6},{5,7},{6,4},{7,5},{8,10},{9,11},{10,... | collective-permute-start | bytes 786440 | tf_op jit(solution)/shard_map/act_gather/ppermute | solution.py:24
  24.7 5.4 %collective-permute-start.12 = (bf16[128,512]{1,0:T(8,128)(2,1)S(1)}, bf16[128,512]{1,0:T(8,128)(2,1)S(1)}, u32[]{:S(2)}, u32[]{:S(2)}) collective-permute-start(bf16[128,512]{1,0:T(8,128)(2,1)S(1)} %collective-permute-done.11), channel_id=1, source_target_pairs={{0,16},{16,24},{24,8},{8,0},{1,17},{17,25},{25,9},{9,1},{2,18},{18... | collective-permute-start | bytes 393224 | tf_op jit(solution)/shard_map/act_gather/ppermute | solution.py:34
  27.6 6.3 %collective-permute-start.8 = (bf16[256,512]{1,0:T(8,128)(2,1)S(1)}, bf16[256,512]{1,0:T(8,128)(2,1)S(1)}, u32[]{:S(2)}, u32[]{:S(2)}) collective-permute-start(bf16[256,512]{1,0:T(8,128)(2,1)S(1)} %collective-permute-done.7.refs_2_.refs_3_), channel_id=1, source_target_pairs={{0,1},{1,0},{2,3},{3,2},{4,5},{5,4},{6,7},{7,6},{8,9},{9,8},{10,11... | collective-permute-start | bytes 786440 | tf_op jit(solution)/shard_map/act_gather/ppermute | solution.py:24
  30.1 15.6 %collective-permute-start.18 = (bf16[384,512]{1,0:T(8,128)(2,1)S(1)}, bf16[384,512]{1,0:T(8,128)(2,1)S(1)}, u32[]{:S(2)}, u32[]{:S(2)}) collective-permute-start(bf16[384,512]{1,0:T(8,128)(2,1)S(1)} %constant_dynamic-update-slice_fusion.refs_0_.refs_4_), channel_id=1, source_target_pairs={{0,6},{1,7},{2,4},{3,5},{4,2},{5,3},{6,0},{7,1},{8,14},{9,15},{10,... | collective-permute-start | bytes 1179656 | tf_op jit(solution)/shard_map/act_gather/ppermute | solution.py:24
  33.2 16.3 %collective-permute-start.16 = (bf16[384,512]{1,0:T(8,128)(2,1)S(1)}, bf16[384,512]{1,0:T(8,128)(2,1)S(1)}, u32[]{:S(2)}, u32[]{:S(2)}) collective-permute-start(bf16[384,512]{1,0:T(8,128)(2,1)S(1)} %constant_dynamic-update-slice_fusion.refs_0_.refs_4_), channel_id=1, source_target_pairs={{0,4},{1,5},{2,6},{3,7},{4,0},{5,1},{6,2},{7,3},{8,12},{9,13},{10,... | collective-permute-start | bytes 1179656 | tf_op jit(solution)/shard_map/act_gather/ppermute | solution.py:24
  33.2 16.4 %collective-permute-start.14 = (bf16[384,512]{1,0:T(8,128)(2,1)S(1)}, bf16[384,512]{1,0:T(8,128)(2,1)S(1)}, u32[]{:S(2)}, u32[]{:S(2)}) collective-permute-start(bf16[384,512]{1,0:T(8,128)(2,1)S(1)} %constant_dynamic-update-slice_fusion.refs_0_.refs_4_), channel_id=1, source_target_pairs={{0,2},{1,3},{2,0},{3,1},{4,6},{5,7},{6,4},{7,5},{8,10},{9,11},{10,... | collective-permute-start | bytes 1179656 | tf_op jit(solution)/shard_map/act_gather/ppermute | solution.py:24
  33.9 6.8 %collective-permute-start.6 = (bf16[256,512]{1,0:T(8,128)(2,1)S(1)}, bf16[256,512]{1,0:T(8,128)(2,1)S(1)}, u32[]{:S(2)}, u32[]{:S(2)}) collective-permute-start(bf16[256,512]{1,0:T(8,128)(2,1)S(1)} %collective-permute-done.5.refs_1_.refs_2_), channel_id=1, source_target_pairs={{0,1},{1,0},{2,3},{3,2},{4,5},{5,4},{6,7},{7,6},{8,9},{9,8},{10,11... | collective-permute-start | bytes 786440 | tf_op jit(solution)/shard_map/act_gather/ppermute | solution.py:24
  33.9 6.8 %collective-permute-start.4 = (bf16[256,512]{1,0:T(8,128)(2,1)S(1)}, bf16[256,512]{1,0:T(8,128)(2,1)S(1)}, u32[]{:S(2)}, u32[]{:S(2)}) collective-permute-start(bf16[256,512]{1,0:T(8,128)(2,1)S(1)} %collective-permute-done.3.refs_0_.refs_1_), channel_id=1, source_target_pairs={{0,1},{1,0},{2,3},{3,2},{4,5},{5,4},{6,7},{7,6},{8,9},{9,8},{10,11... | collective-permute-start | bytes 786440 | tf_op jit(solution)/shard_map/act_gather/ppermute | solution.py:24
  42.2 9.2 %collective-permute-start.20 = (bf16[128,1024]{1,0:T(8,128)(2,1)S(1)}, bf16[128,1024]{1,0:T(8,128)(2,1)S(1)}, u32[]{:S(2)}, u32[]{:S(2)}) collective-permute-start(bf16[128,1024]{1,0:T(8,128)(2,1)S(1)} %get-tuple-element.56.refs_1_.refs_9_), channel_id=1, source_target_pairs={{0,16},{16,24},{24,8},{8,0},{1,17},{17,25},{25,9},{9,1},{2,18},{18... | collective-permute-start | bytes 786440 | tf_op jit(solution)/shard_map/z_ring/ppermute | solution.py:34
  45.6 11.5 %collective-permute-start.13 = (bf16[384,512]{1,0:T(8,128)(2,1)S(1)}, bf16[384,512]{1,0:T(8,128)(2,1)S(1)}, u32[]{:S(2)}, u32[]{:S(2)}) collective-permute-start(bf16[384,512]{1,0:T(8,128)(2,1)S(1)} %constant_dynamic-update-slice_fusion.refs_0_.refs_4_), channel_id=1, source_target_pairs={{0,1},{1,0},{2,3},{3,2},{4,5},{5,4},{6,7},{7,6},{8,9},{9,8},{10,11... | collective-permute-start | bytes 1179656 | tf_op jit(solution)/shard_map/act_gather/ppermute | solution.py:24
  45.6 11.6 %collective-permute-start.19 = (bf16[384,512]{1,0:T(8,128)(2,1)S(1)}, bf16[384,512]{1,0:T(8,128)(2,1)S(1)}, u32[]{:S(2)}, u32[]{:S(2)}) collective-permute-start(bf16[384,512]{1,0:T(8,128)(2,1)S(1)} %collective-permute-done.18.refs_3_.refs_7_), channel_id=1, source_target_pairs={{0,1},{1,0},{2,3},{3,2},{4,5},{5,4},{6,7},{7,6},{8,9},{9,8},{10,11... | collective-permute-start | bytes 1179656 | tf_op jit(solution)/shard_map/act_gather/ppermute | solution.py:24
  49.5 7.8 %collective-permute-start.17 = (bf16[384,512]{1,0:T(8,128)(2,1)S(1)}, bf16[384,512]{1,0:T(8,128)(2,1)S(1)}, u32[]{:S(2)}, u32[]{:S(2)}) collective-permute-start(bf16[384,512]{1,0:T(8,128)(2,1)S(1)} %collective-permute-done.16.refs_2_.refs_6_), channel_id=1, source_target_pairs={{0,1},{1,0},{2,3},{3,2},{4,5},{5,4},{6,7},{7,6},{8,9},{9,8},{10,11... | collective-permute-start | bytes 1179656 | tf_op jit(solution)/shard_map/act_gather/ppermute | solution.py:24
  49.6 12.0 %collective-permute-start.15 = (bf16[384,512]{1,0:T(8,128)(2,1)S(1)}, bf16[384,512]{1,0:T(8,128)(2,1)S(1)}, u32[]{:S(2)}, u32[]{:S(2)}) collective-permute-start(bf16[384,512]{1,0:T(8,128)(2,1)S(1)} %collective-permute-done.14.refs_1_.refs_5_), channel_id=1, source_target_pairs={{0,1},{1,0},{2,3},{3,2},{4,5},{5,4},{6,7},{7,6},{8,9},{9,8},{10,11... | collective-permute-start | bytes 1179656 | tf_op jit(solution)/shard_map/act_gather/ppermute | solution.py:24
  51.4 13.2 %collective-permute-start.21 = (bf16[128,1024]{1,0:T(8,128)(2,1)S(1)}, bf16[128,1024]{1,0:T(8,128)(2,1)S(1)}, u32[]{:S(2)}, u32[]{:S(2)}) collective-permute-start(bf16[128,1024]{1,0:T(8,128)(2,1)S(1)} %collective-permute-done.20.refs_3_.refs_11_), channel_id=1, source_target_pairs={{0,16},{16,24},{24,8},{8,0},{1,17},{17,25},{25,9},{9,1},{2,18},{18... | collective-permute-start | bytes 786440 | tf_op jit(solution)/shard_map/z_ring/ppermute | solution.py:34
  57.1 7.4 %collective-permute-start.24 = (f32[2,1024]{1,0:T(2,128)S(1)}, f32[2,1024]{1,0:T(2,128)S(1)}, u32[]{:S(2)}, u32[]{:S(2)}) collective-permute-start(f32[2,1024]{1,0:T(2,128)S(1)} %get-tuple-element.59.refs_6_), channel_id=1, source_target_pairs={{0,24},{8,16},{16,8},{24,0},{1,25},{9,17},{17,9},{25,1},{2,26},{10... | collective-permute-start | bytes 24584 | tf_op jit(solution)/shard_map/z_ring/ppermute | solution.py:24
  57.2 7.4 %collective-permute-start.23 = (f32[2,1024]{1,0:T(2,128)S(1)}, f32[2,1024]{1,0:T(2,128)S(1)}, u32[]{:S(2)}, u32[]{:S(2)}) collective-permute-start(f32[2,1024]{1,0:T(2,128)S(1)} %get-tuple-element.59.refs_6_), channel_id=1, source_target_pairs={{0,16},{8,24},{16,0},{24,8},{1,17},{9,25},{17,1},{25,9},{2,18},{10... | collective-permute-start | bytes 24584 | tf_op jit(solution)/shard_map/z_ring/ppermute | solution.py:24
  57.3 7.3 %collective-permute-start.22 = (f32[2,1024]{1,0:T(2,128)S(1)}, f32[2,1024]{1,0:T(2,128)S(1)}, u32[]{:S(2)}, u32[]{:S(2)}) collective-permute-start(f32[2,1024]{1,0:T(2,128)S(1)} %get-tuple-element.59.refs_6_), channel_id=1, source_target_pairs={{0,8},{8,0},{16,24},{24,16},{1,9},{9,1},{17,25},{25,17},{2,10},{10... | collective-permute-start | bytes 24584 | tf_op jit(solution)/shard_map/z_ring/ppermute | solution.py:24
  67.3 4.2 %collective-permute-start.26 = (f32[32,384]{1,0:T(8,128)S(1)}, f32[32,384]{1,0:T(8,128)S(1)}, u32[]{:S(2)}, u32[]{:S(2)}) collective-permute-start(f32[32,384]{1,0:T(8,128)S(1)} %get-tuple-element.102), channel_id=1, source_target_pairs={{0,2},{1,3},{2,0},{3,1},{4,6},{5,7},{6,4},{7,5},{8,10},{9,11},{10,... | collective-permute-start | bytes 147464 | tf_op jit(solution)/shard_map/kernel/ppermute | solution.py:24
  68.8 5.0 %collective-permute-start.28 = (f32[32,384]{1,0:T(8,128)S(1)}, f32[32,384]{1,0:T(8,128)S(1)}, u32[]{:S(2)}, u32[]{:S(2)}) collective-permute-start(f32[32,384]{1,0:T(8,128)S(1)} %get-tuple-element.103), channel_id=1, source_target_pairs={{0,6},{1,7},{2,4},{3,5},{4,2},{5,3},{6,0},{7,1},{8,14},{9,15},{10,... | collective-permute-start | bytes 147464 | tf_op jit(solution)/shard_map/kernel/ppermute | solution.py:24
  70.3 4.2 %collective-permute-start.27 = (f32[32,384]{1,0:T(8,128)S(1)}, f32[32,384]{1,0:T(8,128)S(1)}, u32[]{:S(2)}, u32[]{:S(2)}) collective-permute-start(f32[32,384]{1,0:T(8,128)S(1)} %get-tuple-element.104), channel_id=1, source_target_pairs={{0,4},{1,5},{2,6},{3,7},{4,0},{5,1},{6,2},{7,3},{8,12},{9,13},{10,... | collective-permute-start | bytes 147464 | tf_op jit(solution)/shard_map/kernel/ppermute | solution.py:24
  70.9 7.7 %collective-permute-start.29 = (bf16[128,1024]{1,0:T(8,128)(2,1)S(1)}, bf16[128,1024]{1,0:T(8,128)(2,1)S(1)}, u32[]{:S(2)}, u32[]{:S(2)}) collective-permute-start(bf16[128,1024]{1,0:T(8,128)(2,1)S(1)} %collective-permute-done.21.refs_5_.refs_13_), channel_id=1, source_target_pairs={{0,16},{16,24},{24,8},{8,0},{1,17},{17,25},{25,9},{9,1},{2,18},{18... | collective-permute-start | bytes 786440 | tf_op jit(solution)/shard_map/z_ring/ppermute | solution.py:34
  78.6 5.6 %collective-permute-start.31 = (bf16[32,384]{1,0:T(8,128)(2,1)S(1)}, bf16[32,384]{1,0:T(8,128)(2,1)S(1)}, u32[]{:S(2)}, u32[]{:S(2)}) collective-permute-start(bf16[32,384]{1,0:T(8,128)(2,1)S(1)} %convert_element_type.47), channel_id=1, source_target_pairs={{0,24},{16,8},{24,0},{8,16},{1,25},{17,9},{25,1},{9,17},{2,26},{18... | collective-permute-start | bytes 73736 | tf_op jit(solution)/shard_map/kernel/ppermute | solution.py:34
  79.6 4.7 %collective-permute-start.30 = (bf16[32,384]{1,0:T(8,128)(2,1)S(1)}, bf16[32,384]{1,0:T(8,128)(2,1)S(1)}, u32[]{:S(2)}, u32[]{:S(2)}) collective-permute-start(bf16[32,384]{1,0:T(8,128)(2,1)S(1)} %convert_element_type.47), channel_id=1, source_target_pairs={{0,16},{16,24},{24,8},{8,0},{1,17},{17,25},{25,9},{9,1},{2,18},{18... | collective-permute-start | bytes 73736 | tf_op jit(solution)/shard_map/kernel/ppermute | solution.py:34
  81.6 4.7 %collective-permute-start.32 = (bf16[32,384]{1,0:T(8,128)(2,1)S(1)}, bf16[32,384]{1,0:T(8,128)(2,1)S(1)}, u32[]{:S(2)}, u32[]{:S(2)}) collective-permute-start(bf16[32,384]{1,0:T(8,128)(2,1)S(1)} %convert_element_type.47), channel_id=1, source_target_pairs={{0,8},{16,0},{24,16},{8,24},{1,9},{17,1},{25,17},{9,25},{2,10},{18... | collective-permute-start | bytes 73736 | tf_op jit(solution)/shard_map/kernel/ppermute | solution.py:34
  86.3 6.2 %collective-permute-start.38 = (bf16[4,32,384]{2,1,0:T(8,128)(2,1)S(1)}, bf16[4,32,384]{2,1,0:T(8,128)(2,1)S(1)}, u32[]{:S(2)}, u32[]{:S(2)}) collective-permute-start(bf16[4,32,384]{2,1,0:T(8,128)(2,1)S(1)} %pad_maximum_fusion.refs_0_), channel_id=1, source_target_pairs={{0,6},{1,7},{2,4},{3,5},{4,2},{5,3},{6,0},{7,1},{8,14},{9,15},{10,... | collective-permute-start | bytes 294920 | tf_op jit(solution)/shard_map/kernel/ppermute | solution.py:24
  89.1 5.1 %collective-permute-start.36 = (bf16[4,32,384]{2,1,0:T(8,128)(2,1)S(1)}, bf16[4,32,384]{2,1,0:T(8,128)(2,1)S(1)}, u32[]{:S(2)}, u32[]{:S(2)}) collective-permute-start(bf16[4,32,384]{2,1,0:T(8,128)(2,1)S(1)} %pad_maximum_fusion.refs_0_), channel_id=1, source_target_pairs={{0,4},{1,5},{2,6},{3,7},{4,0},{5,1},{6,2},{7,3},{8,12},{9,13},{10,... | collective-permute-start | bytes 294920 | tf_op jit(solution)/shard_map/kernel/ppermute | solution.py:24
  90.0 5.7 %collective-permute-start.40 = (bf16[128,512]{1,0:T(8,128)(2,1)S(1)}, bf16[128,512]{1,0:T(8,128)(2,1)S(1)}, u32[]{:S(2)}, u32[]{:S(2)}) collective-permute-start(bf16[128,512]{1,0:T(8,128)(2,1)S(1)} %get-tuple-element.68), channel_id=1, source_target_pairs={{0,16},{16,24},{24,8},{8,0},{1,17},{17,25},{25,9},{9,1},{2,18},{18... | collective-permute-start | bytes 393224 | tf_op jit(solution)/shard_map/kernel/ppermute | solution.py:34
  90.5 4.6 %collective-permute-start.34 = (bf16[4,32,384]{2,1,0:T(8,128)(2,1)S(1)}, bf16[4,32,384]{2,1,0:T(8,128)(2,1)S(1)}, u32[]{:S(2)}, u32[]{:S(2)}) collective-permute-start(bf16[4,32,384]{2,1,0:T(8,128)(2,1)S(1)} %pad_maximum_fusion.refs_0_), channel_id=1, source_target_pairs={{0,2},{1,3},{2,0},{3,1},{4,6},{5,7},{6,4},{7,5},{8,10},{9,11},{10,... | collective-permute-start | bytes 294920 | tf_op jit(solution)/shard_map/kernel/ppermute | solution.py:24
  91.1 4.1 %collective-permute-start.33 = (bf16[4,32,384]{2,1,0:T(8,128)(2,1)S(1)}, bf16[4,32,384]{2,1,0:T(8,128)(2,1)S(1)}, u32[]{:S(2)}, u32[]{:S(2)}) collective-permute-start(bf16[4,32,384]{2,1,0:T(8,128)(2,1)S(1)} %pad_maximum_fusion.refs_0_), channel_id=1, source_target_pairs={{0,1},{1,0},{2,3},{3,2},{4,5},{5,4},{6,7},{7,6},{8,9},{9,8},{10,11... | collective-permute-start | bytes 294920 | tf_op jit(solution)/shard_map/kernel/ppermute | solution.py:24
  92.5 7.8 %collective-permute-start.41 = (bf16[128,512]{1,0:T(8,128)(2,1)S(1)}, bf16[128,512]{1,0:T(8,128)(2,1)S(1)}, u32[]{:S(2)}, u32[]{:S(2)}) collective-permute-start(bf16[128,512]{1,0:T(8,128)(2,1)S(1)} %get-tuple-element.69), channel_id=1, source_target_pairs={{0,24},{16,8},{24,0},{8,16},{1,25},{17,9},{25,1},{9,17},{2,26},{18... | collective-permute-start | bytes 393224 | tf_op jit(solution)/shard_map/kernel/ppermute | solution.py:34
  94.2 9.4 %collective-permute-start.42 = (bf16[128,512]{1,0:T(8,128)(2,1)S(1)}, bf16[128,512]{1,0:T(8,128)(2,1)S(1)}, u32[]{:S(2)}, u32[]{:S(2)}) collective-permute-start(bf16[128,512]{1,0:T(8,128)(2,1)S(1)} %get-tuple-element.70), channel_id=1, source_target_pairs={{0,8},{16,0},{24,16},{8,24},{1,9},{17,1},{25,17},{9,25},{2,10},{18... | collective-permute-start | bytes 393224 | tf_op jit(solution)/shard_map/kernel/ppermute | solution.py:34
  95.1 8.5 %collective-permute-start.39 = (bf16[4,32,384]{2,1,0:T(8,128)(2,1)S(1)}, bf16[4,32,384]{2,1,0:T(8,128)(2,1)S(1)}, u32[]{:S(2)}, u32[]{:S(2)}) collective-permute-start(bf16[4,32,384]{2,1,0:T(8,128)(2,1)S(1)} %collective-permute-done.38.refs_6_), channel_id=1, source_target_pairs={{0,1},{1,0},{2,3},{3,2},{4,5},{5,4},{6,7},{7,6},{8,9},{9,8},{10,11... | collective-permute-start | bytes 294920 | tf_op jit(solution)/shard_map/kernel/ppermute | solution.py:24
  95.1 8.5 %collective-permute-start.37 = (bf16[4,32,384]{2,1,0:T(8,128)(2,1)S(1)}, bf16[4,32,384]{2,1,0:T(8,128)(2,1)S(1)}, u32[]{:S(2)}, u32[]{:S(2)}) collective-permute-start(bf16[4,32,384]{2,1,0:T(8,128)(2,1)S(1)} %collective-permute-done.36.refs_4_), channel_id=1, source_target_pairs={{0,1},{1,0},{2,3},{3,2},{4,5},{5,4},{6,7},{7,6},{8,9},{9,8},{10,11... | collective-permute-start | bytes 294920 | tf_op jit(solution)/shard_map/kernel/ppermute | solution.py:24
  95.6 8.0 %collective-permute-start.35 = (bf16[4,32,384]{2,1,0:T(8,128)(2,1)S(1)}, bf16[4,32,384]{2,1,0:T(8,128)(2,1)S(1)}, u32[]{:S(2)}, u32[]{:S(2)}) collective-permute-start(bf16[4,32,384]{2,1,0:T(8,128)(2,1)S(1)} %collective-permute-done.34.refs_2_), channel_id=1, source_target_pairs={{0,1},{1,0},{2,3},{3,2},{4,5},{5,4},{6,7},{7,6},{8,9},{9,8},{10,11... | collective-permute-start | bytes 294920 | tf_op jit(solution)/shard_map/kernel/ppermute | solution.py:24
  110.2 8.2 %collective-permute-start.47 = (bf16[128,512]{1,0:T(8,128)(2,1)S(1)}, bf16[128,512]{1,0:T(8,128)(2,1)S(1)}, u32[]{:S(2)}, u32[]{:S(2)}) collective-permute-start(bf16[128,512]{1,0:T(8,128)(2,1)S(1)} %collective-permute-done.40.refs_8_), channel_id=1, source_target_pairs={{0,1},{1,0},{2,3},{3,2},{4,5},{5,4},{6,7},{7,6},{8,9},{9,8},{10,11... | collective-permute-start | bytes 393224 | tf_op jit(solution)/shard_map/grad_weight/ppermute | solution.py:24
  114.8 9.9 %collective-permute-start.44 = (bf16[272,512]{1,0:T(8,128)(2,1)S(1)}, bf16[272,512]{1,0:T(8,128)(2,1)S(1)}, u32[]{:S(2)}, u32[]{:S(2)}) collective-permute-start(bf16[272,512]{1,0:T(8,128)(2,1)S(1)} %get-tuple-element.83), channel_id=1, source_target_pairs={{0,2},{1,3},{2,0},{3,1},{4,6},{5,7},{6,4},{7,5},{8,10},{9,11},{10,... | collective-permute-start | bytes 835592 | tf_op jit(solution)/shard_map/d_act/ppermute | solution.py:24
  116.3 14.4 %collective-permute-start.45 = (bf16[272,512]{1,0:T(8,128)(2,1)S(1)}, bf16[272,512]{1,0:T(8,128)(2,1)S(1)}, u32[]{:S(2)}, u32[]{:S(2)}) collective-permute-start(bf16[272,512]{1,0:T(8,128)(2,1)S(1)} %get-tuple-element.84), channel_id=1, source_target_pairs={{0,4},{1,5},{2,6},{3,7},{4,0},{5,1},{6,2},{7,3},{8,12},{9,13},{10,... | collective-permute-start | bytes 835592 | tf_op jit(solution)/shard_map/d_act/ppermute | solution.py:24
  118.1 12.6 %collective-permute-start.46 = (bf16[272,512]{1,0:T(8,128)(2,1)S(1)}, bf16[272,512]{1,0:T(8,128)(2,1)S(1)}, u32[]{:S(2)}, u32[]{:S(2)}) collective-permute-start(bf16[272,512]{1,0:T(8,128)(2,1)S(1)} %get-tuple-element.85), channel_id=1, source_target_pairs={{0,6},{1,7},{2,4},{3,5},{4,2},{5,3},{6,0},{7,1},{8,14},{9,15},{10,... | collective-permute-start | bytes 835592 | tf_op jit(solution)/shard_map/d_act/ppermute | solution.py:24
  131.4 4.7 %collective-permute-start.51 = (f32[8,512]{1,0:T(8,128)S(1)}, f32[8,512]{1,0:T(8,128)S(1)}, u32[]{:S(2)}, u32[]{:S(2)}) collective-permute-start(f32[8,512]{1,0:T(8,128)S(1)} %pad_maximum_fusion.1), channel_id=1, source_target_pairs={{0,16},{8,24},{16,0},{24,8},{1,17},{9,25},{17,1},{25,9},{2,18},{10... | collective-permute-start | bytes 49160 | tf_op jit(solution)/shard_map/norm_backward/ppermute | solution.py:24
  131.5 5.6 %collective-permute-start.52 = (f32[8,512]{1,0:T(8,128)S(1)}, f32[8,512]{1,0:T(8,128)S(1)}, u32[]{:S(2)}, u32[]{:S(2)}) collective-permute-start(f32[8,512]{1,0:T(8,128)S(1)} %pad_maximum_fusion.1), channel_id=1, source_target_pairs={{0,24},{8,16},{16,8},{24,0},{1,25},{9,17},{17,9},{25,1},{2,26},{10... | collective-permute-start | bytes 49160 | tf_op jit(solution)/shard_map/norm_backward/ppermute | solution.py:24
  (8 other events, 41.9 us)

commit v7 on v6

--- a/solution.py
+++ b/solution.py
@@ -59,7 +59,8 @@
 LOADS = 8
 
 
-def load_kernel(w_ref, out_ref, sems):
+def load_kernel(w_ref, out_ref, flag_ref, sems):
+    flag_ref[...] = jnp.zeros_like(flag_ref)
     step = w_ref.shape[0] // LOADS
     copies = [
         pltpu.make_async_copy(
@@ -73,12 +74,15 @@
         copy.wait()
 
 
-def load_call(weight):
+def load_call(weight, flag_shape):
     return pl.pallas_call(
         load_kernel,
-        out_shape=pltpu.VMEM(weight.shape, weight.dtype),
+        out_shape=(
+            pltpu.VMEM(weight.shape, weight.dtype),
+            jax.ShapeDtypeStruct(flag_shape, f32),
+        ),
         in_specs=[ANYWHERE],
-        out_specs=IN_VMEM,
+        out_specs=(IN_VMEM, IN_VMEM),
         scratch_shapes=[pltpu.SemaphoreType.DMA((LOADS,))],
         compiler_params=params(4),
         cost_estimate=cost(0, 4 * weight.size),
@@ -134,14 +138,19 @@
     )(*operands)
 
 
-def strip_kernel(n_slots, n_sums, rows, n_col, place_ref, *refs):
-    z_refs, sum_refs = refs[: 2 * n_slots], refs[2 * n_slots : 2 * n_slots + n_sums]
-    even_ref, odd_ref, strip = refs[2 * n_slots + n_sums :]
-    local_rows = z_refs[0].shape[0]
-    mean = sum(s[...] for s in sum_refs) / rows
+def strip_kernel(n_batch, n_slots, rows, n_col, place_ref, *refs):
+    z_refs = [refs[:n_batch], refs[n_batch : n_batch + n_slots]]
+    sum_refs = refs[n_batch + n_slots : 2 * n_batch]
+    even_ref, odd_ref, strip = refs[2 * n_batch :]
+    local_rows = z_refs[0][0].shape[0]
     for v in range(2):
         here = pl.ds(v * local_rows, local_rows)
-        rounded = [(z[...].astype(f32) - mean[v : v + 1]).astype(bf16) for z in z_refs[v::2]]
+        zf = [z[...].astype(f32) for z in z_refs[v]]
+        total = sum(jnp.sum(z, axis=0, keepdims=True) for z in zf)
+        if v == 1:
+            total = total + sum(s[1:2] for s in sum_refs)
+        mean = total / rows
+        rounded = [(z - mean).astype(bf16) for z in zf[:n_slots]]
         for u in range(n_slots):
             strip[here, pl.ds(u * local_rows, local_rows)] = lax.dot_general(
                 rounded[0], rounded[u], (((1,), (1,)), ((), ())), preferred_element_type=f32
@@ -152,20 +161,20 @@
         (odd_ref if k % 2 else even_ref)[k // 2] = strip[pl.ds(start, part), :]
 
 
-def strip_call(place, z_slots, sums, rows, n_col):
-    local_rows, columns = z_slots[0][0].shape
+def strip_call(place, z0, z1, sums, rows, n_col):
+    local_rows, columns = z0[0].shape
     tall = 2 * local_rows
-    wide = len(z_slots) * local_rows
+    wide = len(z1) * local_rows
     part = jax.ShapeDtypeStruct((n_col // 2, tall // n_col, wide), f32)
-    operands = [place] + [z for slot in z_slots for z in slot] + list(sums)
+    operands = [place] + list(z0) + list(z1) + list(sums)
     return pl.pallas_call(
-        functools.partial(strip_kernel, len(z_slots), len(sums), rows, n_col),
+        functools.partial(strip_kernel, len(z0), len(z1), rows, n_col),
         out_shape=(part, part),
         in_specs=[IN_SMEM] + [IN_VMEM] * (len(operands) - 1),
         out_specs=(IN_VMEM, IN_VMEM),
         scratch_shapes=[pltpu.VMEM((tall, wide), f32)],
-        compiler_params=params(10),
-        cost_estimate=cost(2 * tall * wide * columns, 2 * tall * columns * len(z_slots)),
+        compiler_params=params(12),
+        cost_estimate=cost(2 * tall * wide * columns, 2 * tall * columns * len(z0)),
         name="kernel_strip",
     )(*operands)
 
@@ -439,11 +448,20 @@
 
 
 def gather_pieces(x, n_col):
+    return sibling_pieces(link_pieces(x, n_col), n_col)
+
+
+def link_pieces(x, n_col):
     pieces = {0: x}
     for k in range(2, n_col, 2):
         pieces[k] = xor_send(x, "col", k)
+    return pieces
+
+
+def sibling_pieces(pieces, n_col):
     for k in range(0, n_col, 2):
-        pieces[k + 1] = xor_send(pieces[k], "col", 1)
+        if k + 1 not in pieces:
+            pieces[k + 1] = xor_send(pieces[k], "col", 1)
     return pieces
 
 
@@ -467,13 +485,14 @@
     far = evens[1:]
 
     with jax.named_scope("weight_load"):
-        held_weight = load_call(weight)
+        held_weight, loaded = load_call(weight, (2 * n_view, width))
     with jax.named_scope("norm_stats"):
         hidden = views.astype(f32)
         local_mean = jnp.mean(hidden, axis=1)
         local_centred = hidden - local_mean[:, None, :]
         local_spread = jnp.sum(local_centred * local_centred, axis=1)
         stats = exchange(jnp.concatenate([local_mean, local_spread]), "batch")
+        stats[-1] = stats[-1] + loaded
         mean = exchange_sum(s[:n_view] for s in stats) / n_batch
         spread = exchange_sum(
             s[n_view:] + local_rows * jnp.square(s[:n_view] - mean) for s in stats
@@ -484,11 +503,12 @@
         preactivation = norm_scale_gain * normalised + norm_shift_bias
         act = jax.nn.gelu(preactivation, approximate=True).astype(bf16)
     with jax.named_scope("act_gather"):
-        pieces = gather_pieces(act.reshape(tall, width), n_col)
-        ring = [act[0]]
-        for _ in range(1, n_batch):
-            ring.append(ring_send(ring[-1], "batch", 1))
-        far_pieces = gather_pieces(jnp.concatenate(ring[1:]), n_col)
+        pieces = link_pieces(act.reshape(tall, width), n_col)
+        pieces[1] = xor_send(pieces[0], "col", 1)
+        first, pieces[1] = lax.optimization_barrier((act[0], pieces[1]))
+        others = [ring_send(first, "batch", d) for d in range(1, n_batch)]
+        pieces = sibling_pieces(pieces, n_col)
+        far_pieces = gather_pieces(jnp.concatenate(others), n_col)
     with jax.named_scope("z"):
 
         def z_of(source, groups):
@@ -511,16 +531,16 @@
         z_ring = [z_own1]
         for _ in range(1, n_batch):
             z_ring.append(ring_send(z_ring[-1], "batch", 1))
-        sums = exchange(z_sum, "batch")
-        slots = [list(pair) for pair in zip([z_own0] + z_far, z_ring)]
+        sums = [ring_send(z_sum, "batch", d) for d in range(reach + 1, n_batch)]
+        z_flat = [z_own0] + z_far
     with jax.named_scope("kernel"):
-        even_part, odd_part = strip_call(place, slots[: reach + 1], sums, rows, n_col)
+        even_part, odd_part = strip_call(place, z_flat, z_ring[: reach + 1], sums, rows, n_col)
         even_part = even_part + xor_send(odd_part, "col", 1)
+        even_part, z_ring[reach + 1 :] = lax.optimization_barrier((even_part, z_ring[reach + 1 :]))
         strip = even_part[0]
         for k in far:
             strip = strip + xor_send(even_part[k // 2], "col", k)
-        strip, z_ring[reach + 1 :] = lax.optimization_barrier((strip, z_ring[reach + 1 :]))
-        slots = [list(pair) for pair in zip([z_own0] + z_far, z_ring)]
+        slots = list(zip(z_flat, z_ring))
         mine = strip.astype(bf16)
         mine = jnp.stack([mine] + [ring_send(mine, "batch", d) for d in range(1, n_batch)])
         mine, held_back = lax.optimization_barrier((mine, [pieces[k] for k in evens]))
@@ -529,7 +549,7 @@
         blocks = [
             ring_send(x, "batch", 1 + i % (n_batch - 1)) for i, x in enumerate(picked)
         ]
-        strips, blocks = lax.optimization_barrier((strips, blocks))
+        strips, blocks[0] = lax.optimization_barrier((strips, blocks[0]))
     with jax.named_scope("dz"):
         constants = (
             4.0 * scale / denom,
@@ -541,6 +561,7 @@
             1.0 / denom,
         )
         dz, share = dz_call(place, strip, [strips[k] for k in range(n_col)], slots, constants)
+        dz, blocks[1:] = lax.optimization_barrier((dz, blocks[1:]))
     with jax.named_scope("d_act"):
         (away,) = d_act_call(place, dz, share, held_weight, n_batch, n_col, None)
         got = xor_send(away, "col", 1)

time: 140 us -> 133 us (0.950)
  starting transfers between devices: 56.8 us -> 46.6 us
  waiting for transfers between devices: 46.4 us -> 50.6 us
    ppermute x41 -> x38, waiting for transfers between devices: 25.4 us -> 36.7 us  [xor_send(): return lax.ppermute(x, axis, [(i, i ^ k) for i in range(n)])]
    ppermute x41 -> x38, starting transfers between devices: 37 us -> 29.8 us  [xor_send(): return lax.ppermute(x, axis, [(i, i ^ k) for i in range(n)])]
    ppermute x12 -> x13, waiting for transfers between devices: 21 us -> 13.9 us  [ring_send(): lax.ppermute(x, axis, [(order[i], order[(i + d) % n]) for i in range(n)])]
    ppermute x12 -> x13, starting transfers between devices: 19.8 us -> 16.8 us  [ring_send(): lax.ppermute(x, axis, [(order[i], order[(i + d) % n]) for i in range(n)])]
  transfers between devices with their start and end apart: 53 -> 51, of which waited for: 22 -> 25; matrix products, arithmetic and copies ran while one was open for 0% -> 0% of each run, Pallas kernels for 15% -> 21%
where the time goes in v7:
time: 133 us
  waiting for transfers between devices  50.6 us (38%)
  starting transfers between devices  46.6 us (35%)
  Pallas kernels  29.4 us (22%)
  other arithmetic  5.3 us (4%)
    ppermute x38, waiting for transfers between devices, xor_send(): return lax.ppermute(x, axis, [(i, i ^ k) for i in range(n)])  36.7 us
    ppermute x38, starting transfers between devices, xor_send(): return lax.ppermute(x, axis, [(i, i ^ k) for i in range(n)])  29.8 us
    ppermute x13, starting transfers between devices, ring_send(): lax.ppermute(x, axis, [(order[i], order[(i + d) % n]) for i in range(n)])  16.8 us
    ppermute x13, waiting for transfers between devices, ring_send(): lax.ppermute(x, axis, [(order[i], order[(i + d) % n]) for i in range(n)])  13.9 us
    pallas_call x5, Pallas kernels, z_call(): pl.pallas_call(functools.partial(z_kernel, tuple(ks), before is None, las...  9.62 us
    pallas_call x2, Pallas kernels, weight_grad_call(): pl.pallas_call(functools.partial(weight_grad_kernel, len(arrived), int(be...  5.79 us
    pallas_call x1, Pallas kernels, dz_call(): pl.pallas_call(functools.partial(dz_kernel, n_batch, n_col, tile, constan...  4.66 us
    pallas_call x2, Pallas kernels, d_act_call(): pl.pallas_call(functools.partial(d_act_kernel, count, (got is not None, n...  3.68 us
  transfers between devices with their start and end apart: 51, of which 25 were waited for; matrix products, arithmetic and copies ran while one was open for 0% of the time, Pallas kernels for 21%

profile of v7, /device:TPU:0, one launch (start us, length us, event | category | flops | bytes accessed | tf_op | source)
XLA Modules:
  0.0 133.0 jit_solution(16020905556549847277)
XLA Ops:
  1.7 1.0 fusion.8
  2.8 5.1 %collective-permute-start.2 = (f32[4,512]{1,0:T(4,128)S(1)}, f32[4,512]{1,0:T(4,128)S(1)}, u32[]{:S(2)}, u32[]{:S(2)}) collective-permute-start(f32[4,512]{1,0:T(4,128)S(1)} %pad_maximum_fusion.2), channel_id=1, source_target_pairs={{0,24},{8,16},{16,8},{24,0},{1,25},{9,17},{17,9},{25,1},{2,26},{10... | collective-permute-start | bytes 24584 | tf_op jit(solution)/shard_map/norm_stats/ppermute | solution.py:24
  8.6 3.5 %weight_load.1 = (bf16[4096,1024]{1,0:T(8,128)(2,1)S(1)}, f32[4,512]{1,0:T(4,128)S(1)}) custom-call(bf16[4096,1024]{1,0:T(8,128)(2,1)} %w_ref), custom_call_target="tpu_custom_call" | custom-call | bytes 16777216 | tf_op jit(solution)/shard_map/weight_load/weight_load/pallas_call | solution.py:78
  12.9 2.5 %collective-permute-start.7 = (bf16[256,512]{1,0:T(8,128)(2,1)S(1)}, bf16[256,512]{1,0:T(8,128)(2,1)S(1)}, u32[]{:S(2)}, u32[]{:S(2)}) collective-permute-start(bf16[256,512]{1,0:T(8,128)(2,1)S(1)} %bitcast.26), channel_id=1, source_target_pairs={{0,6},{1,7},{2,4},{3,5},{4,2},{5,3},{6,0},{7,1},{8,14},{9,15},{10,... | collective-permute-start | bytes 786440 | tf_op jit(solution)/shard_map/act_gather/ppermute | solution.py:24
  16.5 2.1 %collective-permute-start.10 = (bf16[128,512]{1,0:T(8,128)(2,1)S(1)}, bf16[128,512]{1,0:T(8,128)(2,1)S(1)}, u32[]{:S(2)}, u32[]{:S(2)}) collective-permute-start(bf16[128,512]{1,0:T(8,128)(2,1)S(1)} %slice_bitcast_fusion), channel_id=1, source_target_pairs={{0,16},{16,24},{24,8},{8,0},{1,17},{17,25},{25,9},{9,1},{2,18},{18... | collective-permute-start | bytes 393224 | tf_op jit(solution)/shard_map/act_gather/ppermute | solution.py:34
  18.5 1.4 %collective-permute-start.11 = (bf16[128,512]{1,0:T(8,128)(2,1)S(1)}, bf16[128,512]{1,0:T(8,128)(2,1)S(1)}, u32[]{:S(2)}, u32[]{:S(2)}) collective-permute-start(bf16[128,512]{1,0:T(8,128)(2,1)S(1)} %slice_bitcast_fusion), channel_id=1, source_target_pairs={{0,24},{16,8},{24,0},{8,16},{1,25},{17,9},{25,1},{9,17},{2,26},{18... | collective-permute-start | bytes 393224 | tf_op jit(solution)/shard_map/act_gather/ppermute | solution.py:34
  20.0 3.0 %collective-permute-done.7.refs_2_.refs_3_ = bf16[256,512]{1,0:T(8,128)(2,1)S(1)} collective-permute-done((bf16[256,512]{1,0:T(8,128)(2,1)S(1)}, bf16[256,512]{1,0:T(8,128)(2,1)S(1)}, u32[]{:S(2)}, u32[]{:S(2)}) %collective-permute-start.7) | collective-permute-done | bytes 262176 | tf_op jit(solution)/shard_map/act_gather/ppermute | solution.py:24
  23.0 1.0 collective-permute-start.12
  24.0 4.1 %collective-permute-done.5.refs_1_.refs_2_ = bf16[256,512]{1,0:T(8,128)(2,1)S(1)} collective-permute-done((bf16[256,512]{1,0:T(8,128)(2,1)S(1)}, bf16[256,512]{1,0:T(8,128)(2,1)S(1)}, u32[]{:S(2)}, u32[]{:S(2)}) %collective-permute-start.5) | collective-permute-done | bytes 262176 | tf_op jit(solution)/shard_map/act_gather/ppermute | solution.py:24
  28.8 2.8 %collective-permute-done.12 = bf16[128,512]{1,0:T(8,128)(2,1)S(1)} collective-permute-done((bf16[128,512]{1,0:T(8,128)(2,1)S(1)}, bf16[128,512]{1,0:T(8,128)(2,1)S(1)}, u32[]{:S(2)}, u32[]{:S(2)}) %collective-permute-start.12) | collective-permute-done | bytes 131104 | tf_op jit(solution)/shard_map/act_gather/ppermute | solution.py:34
  31.6 2.5 %collective-permute-start.18 = (bf16[384,512]{1,0:T(8,128)(2,1)S(1)}, bf16[384,512]{1,0:T(8,128)(2,1)S(1)}, u32[]{:S(2)}, u32[]{:S(2)}) collective-permute-start(bf16[384,512]{1,0:T(8,128)(2,1)S(1)} %constant_dynamic-update-slice_fusion.refs_0_.refs_4_), channel_id=1, source_target_pairs={{0,6},{1,7},{2,4},{3,5},{4,2},{5,3},{6,0},{7,1},{8,14},{9,15},{10,... | collective-permute-start | bytes 1179656 | tf_op jit(solution)/shard_map/act_gather/ppermute | solution.py:24
  35.1 1.2 z_matmul.5.refs_4_
  36.4 1.5 %z_matmul.6.refs_4_ = f32[256,1024]{1,0:T(8,128)S(1)} custom-call(s32[2]{0:T(128)S(1)} %pad_add_fusion.place_ref, bf16[256,512]{1,0:T(8,128)(2,1)S(1)} %collective-permute-done.3.refs_0_.refs_1_, bf16[256,512]{1,0:T(8,128)(2,1)S(1)} %collective-permute-done.5.refs_1_.refs_2_, bf16[256,512]{1,0:T(8,128)(2,1)S(1)} %collective-permute-done.7.refs_2_.refs_3_, ...), custom_call_target="tpu_custom_call" | custom-call | flops 805306368 | bytes 524288 | tf_op jit(solution)/shard_map/z/z_matmul/pallas_call | solution.py:130
  38.0 1.5 %z_matmul.7 = (bf16[128,1024]{1,0:T(8,128)(2,1)S(1)}, bf16[128,1024]{1,0:T(8,128)(2,1)S(1)}, f32[2,1024]{1,0:T(2,128)S(1)}) custom-call(s32[2]{0:T(128)S(1)} %pad_add_fusion.place_ref, bf16[256,512]{1,0:T(8,128)(2,1)S(1)} %collective-permute-done.4.refs_0_.refs_1_, bf16[256,512]{1,0:T(8,128)(2,1)S(1)} %collective-permute-done.6.refs_1_.refs_2_, ...), custom_call_target="tpu_custom_call" | custom-call | flops 805306368 | bytes 524288 | tf_op jit(solution)/shard_map/z/z_matmul/pallas_call | solution.py:130
  39.7 4.9 %collective-permute-done.18.refs_3_.refs_7_ = bf16[384,512]{1,0:T(8,128)(2,1)S(1)} collective-permute-done((bf16[384,512]{1,0:T(8,128)(2,1)S(1)}, bf16[384,512]{1,0:T(8,128)(2,1)S(1)}, u32[]{:S(2)}, u32[]{:S(2)}) %collective-permute-start.18) | collective-permute-done | bytes 393248 | tf_op jit(solution)/shard_map/act_gather/ppermute | solution.py:24
  44.6 7.4 %collective-permute-done.16.refs_2_.refs_6_ = bf16[384,512]{1,0:T(8,128)(2,1)S(1)} collective-permute-done((bf16[384,512]{1,0:T(8,128)(2,1)S(1)}, bf16[384,512]{1,0:T(8,128)(2,1)S(1)}, u32[]{:S(2)}, u32[]{:S(2)}) %collective-permute-start.16) | collective-permute-done | bytes 393248 | tf_op jit(solution)/shard_map/act_gather/ppermute | solution.py:24
  52.5 2.3 %z_matmul.8.refs_5_ = f32[384,1024]{1,0:T(8,128)S(1)} custom-call(s32[2]{0:T(128)S(1)} %pad_add_fusion.place_ref, bf16[384,512]{1,0:T(8,128)(2,1)S(1)} %constant_dynamic-update-slice_fusion.refs_0_.refs_4_, bf16[384,512]{1,0:T(8,128)(2,1)S(1)} %collective-permute-done.14.refs_1_.refs_5_, bf16[384,512]{1,0:T(8,128)(2,1)S(1)} %collective-permute-done.16.refs_2_.refs_6_, ...), custom_call_target="tpu_custom_call" | custom-call | flops 1610612736 | bytes 786432 | tf_op jit(solution)/shard_map/z/z_matmul/pallas_call | solution.py:130
  54.9 2.1 %collective-permute-start.22 = (f32[2,1024]{1,0:T(2,128)S(1)}, f32[2,1024]{1,0:T(2,128)S(1)}, u32[]{:S(2)}, u32[]{:S(2)}) collective-permute-start(f32[2,1024]{1,0:T(2,128)S(1)} %get-tuple-element.69), channel_id=1, source_target_pairs={{0,8},{16,0},{24,16},{8,24},{1,9},{17,1},{25,17},{9,25},{2,10},{18... | collective-permute-start | bytes 24584 | tf_op jit(solution)/shard_map/z_ring/ppermute | solution.py:34
  57.0 4.0 %collective-permute-done.21.refs_6_.refs_13_ = bf16[128,1024]{1,0:T(8,128)(2,1)S(1)} collective-permute-done((bf16[128,1024]{1,0:T(8,128)(2,1)S(1)}, bf16[128,1024]{1,0:T(8,128)(2,1)S(1)}, u32[]{:S(2)}, u32[]{:S(2)}) %collective-permute-start.21) | collective-permute-done | bytes 262176 | tf_op jit(solution)/shard_map/z_ring/ppermute | solution.py:34
  61.0 1.2 collective-permute-start.24
  62.1 3.0 %z_matmul.9 = (bf16[128,1024]{1,0:T(8,128)(2,1)S(1)}, bf16[128,1024]{1,0:T(8,128)(2,1)S(1)}, bf16[128,1024]{1,0:T(8,128)(2,1)S(1)}, f32[3,1024]{1,0:T(4,128)}) custom-call(s32[2]{0:T(128)S(1)} %pad_add_fusion.place_ref, bf16[384,512]{1,0:T(8,128)(2,1)S(1)} %collective-permute-done.13.refs_0_.refs_4_, ...), custom_call_target="tpu_custom_call" | custom-call | flops 1610612736 | bytes 786432 | tf_op jit(solution)/shard_map/z/z_matmul/pallas_call | solution.py:130
  65.1 1.6 %kernel_strip.1 = (f32[4,32,384]{2,1,0:T(8,128)S(1)}, f32[4,32,384]{2,1,0:T(8,128)S(1)}) custom-call(s32[2]{0:T(128)S(1)} %pad_add_fusion.place_ref, bf16[128,1024]{1,0:T(8,128)(2,1)S(1)} %get-tuple-element.63.refs_0_.refs_8_, bf16[128,1024]{1,0:T(8,128)(2,1)S(1)} %get-tuple-element.65.refs_1_.refs_10_, ...), custom_call_target="tpu_custom_call" | custom-call | flops 201326592 | bytes 2097152 | tf_op jit(solution)/shard_map/kernel/kernel_strip/pallas_call | solution.py:170
  66.8 1.4 %collective-permute-done.23 = f32[4,32,384]{2,1,0:T(8,128)S(1)} collective-permute-done((f32[4,32,384]{2,1,0:T(8,128)S(1)}, f32[4,32,384]{2,1,0:T(8,128)S(1)}, u32[]{:S(2)}, u32[]{:S(2)}) %collective-permute-start.23) | collective-permute-done | bytes 196640 | tf_op jit(solution)/shard_map/kernel/ppermute | solution.py:24
  68.4 1.6 %collective-permute-start.25 = (f32[32,384]{1,0:T(8,128)S(1)}, f32[32,384]{1,0:T(8,128)S(1)}, u32[]{:S(2)}, u32[]{:S(2)}) collective-permute-start(f32[32,384]{1,0:T(8,128)S(1)} %get-tuple-element.114), channel_id=1, source_target_pairs={{0,2},{1,3},{2,0},{3,1},{4,6},{5,7},{6,4},{7,5},{8,10},{9,11},{10,... | collective-permute-start | bytes 147464 | tf_op jit(solution)/shard_map/kernel/ppermute | solution.py:24
  70.0 1.4 %collective-permute-start.27 = (f32[32,384]{1,0:T(8,128)S(1)}, f32[32,384]{1,0:T(8,128)S(1)}, u32[]{:S(2)}, u32[]{:S(2)}) collective-permute-start(f32[32,384]{1,0:T(8,128)S(1)} %get-tuple-element.115), channel_id=1, source_target_pairs={{0,6},{1,7},{2,4},{3,5},{4,2},{5,3},{6,0},{7,1},{8,14},{9,15},{10,... | collective-permute-start | bytes 147464 | tf_op jit(solution)/shard_map/kernel/ppermute | solution.py:24
  72.8 2.2 %collective-permute-done.27 = f32[32,384]{1,0:T(8,128)S(1)} collective-permute-done((f32[32,384]{1,0:T(8,128)S(1)}, f32[32,384]{1,0:T(8,128)S(1)}, u32[]{:S(2)}, u32[]{:S(2)}) %collective-permute-start.27) | collective-permute-done | bytes 49184 | tf_op jit(solution)/shard_map/kernel/ppermute | solution.py:24
  75.5 2.2 %collective-permute-start.30 = (bf16[32,384]{1,0:T(8,128)(2,1)S(1)}, bf16[32,384]{1,0:T(8,128)(2,1)S(1)}, u32[]{:S(2)}, u32[]{:S(2)}) collective-permute-start(bf16[32,384]{1,0:T(8,128)(2,1)S(1)} %get-tuple-element.110), channel_id=1, source_target_pairs={{0,8},{16,0},{24,16},{8,24},{1,9},{17,1},{25,17},{9,25},{2,10},{18... | collective-permute-start | bytes 73736 | tf_op jit(solution)/shard_map/kernel/ppermute | solution.py:34
  77.8 1.6 %collective-permute-start.29 = (bf16[32,384]{1,0:T(8,128)(2,1)S(1)}, bf16[32,384]{1,0:T(8,128)(2,1)S(1)}, u32[]{:S(2)}, u32[]{:S(2)}) collective-permute-start(bf16[32,384]{1,0:T(8,128)(2,1)S(1)} %get-tuple-element.110), channel_id=1, source_target_pairs={{0,24},{16,8},{24,0},{8,16},{1,25},{17,9},{25,1},{9,17},{2,26},{18... | collective-permute-start | bytes 73736 | tf_op jit(solution)/shard_map/kernel/ppermute | solution.py:34
  80.6 2.9 %collective-permute-done.29 = bf16[32,384]{1,0:T(8,128)(2,1)S(1)} collective-permute-done((bf16[32,384]{1,0:T(8,128)(2,1)S(1)}, bf16[32,384]{1,0:T(8,128)(2,1)S(1)}, u32[]{:S(2)}, u32[]{:S(2)}) %collective-permute-start.29) | collective-permute-done | bytes 24608 | tf_op jit(solution)/shard_map/kernel/ppermute | solution.py:34
  83.5 1.6 %collective-permute-start.36 = (bf16[4,32,384]{2,1,0:T(8,128)(2,1)S(1)}, bf16[4,32,384]{2,1,0:T(8,128)(2,1)S(1)}, u32[]{:S(2)}, u32[]{:S(2)}) collective-permute-start(bf16[4,32,384]{2,1,0:T(8,128)(2,1)S(1)} %pad_maximum_fusion.refs_0_), channel_id=1, source_target_pairs={{0,6},{1,7},{2,4},{3,5},{4,2},{5,3},{6,0},{7,1},{8,14},{9,15},{10,... | collective-permute-start | bytes 294920 | tf_op jit(solution)/shard_map/kernel/ppermute | solution.py:24
  85.8 1.3 collective-permute-start.32
  87.7 1.1 collective-permute-start.38
  90.6 2.0 %collective-permute-start.39 = (bf16[128,512]{1,0:T(8,128)(2,1)S(1)}, bf16[128,512]{1,0:T(8,128)(2,1)S(1)}, u32[]{:S(2)}, u32[]{:S(2)}) collective-permute-start(bf16[128,512]{1,0:T(8,128)(2,1)S(1)} %get-tuple-element.89), channel_id=1, source_target_pairs={{0,24},{16,8},{24,0},{8,16},{1,25},{17,9},{25,1},{9,17},{2,26},{18... | collective-permute-start | bytes 393224 | tf_op jit(solution)/shard_map/kernel/ppermute | solution.py:34
  92.7 1.7 %collective-permute-start.40 = (bf16[128,512]{1,0:T(8,128)(2,1)S(1)}, bf16[128,512]{1,0:T(8,128)(2,1)S(1)}, u32[]{:S(2)}, u32[]{:S(2)}) collective-permute-start(bf16[128,512]{1,0:T(8,128)(2,1)S(1)} %get-tuple-element.90), channel_id=1, source_target_pairs={{0,8},{16,0},{24,16},{8,24},{1,9},{17,1},{25,17},{9,25},{2,10},{18... | collective-permute-start | bytes 393224 | tf_op jit(solution)/shard_map/kernel/ppermute | solution.py:34
  94.4 4.7 %embedding_gradient.1 = (bf16[2,512,1024]{2,1,0:T(8,128)(2,1)S(1)}, f32[8,128]{1,0:T(8,128)S(1)}) custom-call(s32[2]{0:T(128)S(1)} %pad_add_fusion.place_ref, f32[32,384]{1,0:T(8,128)S(1)} %get-tuple-element.111.own_ref, bf16[4,32,384]{2,1,0:T(8,128)(2,1)S(1)} %pad_maximum_fusion.refs_0_, bf16[4,32,384]{2,1,0:T(8,128)(2,1)S(1)} %collective-permute-done.31.refs_1_, ...), custom_call_target="tpu_custom_call" | custom-call | flops 1073741824 | bytes 4194304 | tf_op jit(solution)/shard_map/dz/embedding_gradient/pallas_call | solution.py:252
  99.0 3.2 %collective-permute-done.40.refs_10_ = bf16[128,512]{1,0:T(8,128)(2,1)S(1)} collective-permute-done((bf16[128,512]{1,0:T(8,128)(2,1)S(1)}, bf16[128,512]{1,0:T(8,128)(2,1)S(1)}, u32[]{:S(2)}, u32[]{:S(2)}) %collective-permute-start.40) | collective-permute-done | bytes 131104 | tf_op jit(solution)/shard_map/kernel/ppermute | solution.py:34
  102.2 1.8 %d_act_matmul.2 = bf16[4,272,512]{2,1,0:T(8,128)(2,1)S(1)} custom-call(s32[2]{0:T(128)S(1)} %pad_add_fusion.place_ref, bf16[2,512,1024]{2,1,0:T(8,128)(2,1)S(1)} %get-tuple-element.91.dz_ref.refs_11_, f32[8,128]{1,0:T(8,128)S(1)} %get-tuple-element.92.share_ref, bf16[4096,1024]{1,0:T(8,128)(2,1)S(1)} %get-tuple-element.61.refs_2_.refs_3_.refs_4_.w_ref), custom_call_target="tpu_custom_call" | custom-call | flops 1073741824 | bytes 1048576 | tf_op jit(solution)/shard_map/d_act/d_act_matmul/pallas_call | solution.py:324
  104.6 2.2 %collective-permute-done.41.refs_0_ = bf16[4,272,512]{2,1,0:T(8,128)(2,1)S(1)} collective-permute-done((bf16[4,272,512]{2,1,0:T(8,128)(2,1)S(1)}, bf16[4,272,512]{2,1,0:T(8,128)(2,1)S(1)}, u32[]{:S(2)}, u32[]{:S(2)}) %collective-permute-start.41) | collective-permute-done | bytes 1114144 | tf_op jit(solution)/shard_map/d_act/ppermute | solution.py:24
  106.9 1.8 %d_act_matmul.3 = (bf16[272,512]{1,0:T(8,128)(2,1)S(1)}, bf16[272,512]{1,0:T(8,128)(2,1)S(1)}, bf16[272,512]{1,0:T(8,128)(2,1)S(1)}, f32[272,512]{1,0:T(8,128)S(1)}) custom-call(s32[2]{0:T(128)S(1)} %pad_add_fusion.place_ref, bf16[2,512,1024]{2,1,0:T(8,128)(2,1)S(1)} %get-tuple-element.91.dz_ref.refs_11_, f32[8,128]{1,0:T(8,128)S(1)} %get-tuple-element.92.share_ref, ...), custom_call_target="tpu_custom_call" | custom-call | flops 1073741824 | bytes 1048576 | tf_op jit(solution)/shard_map/d_act/d_act_matmul/pallas_call | solution.py:324
  108.7 1.2 collective-permute-start.42
  110.8 1.4 %collective-permute-start.44 = (bf16[272,512]{1,0:T(8,128)(2,1)S(1)}, bf16[272,512]{1,0:T(8,128)(2,1)S(1)}, u32[]{:S(2)}, u32[]{:S(2)}) collective-permute-start(bf16[272,512]{1,0:T(8,128)(2,1)S(1)} %get-tuple-element.95), channel_id=1, source_target_pairs={{0,6},{1,7},{2,4},{3,5},{4,2},{5,3},{6,0},{7,1},{8,14},{9,15},{10,... | collective-permute-start | bytes 835592 | tf_op jit(solution)/shard_map/d_act/ppermute | solution.py:24
  112.8 2.9 %weight_gradient.2.refs_12_ = f32[1024,1024]{1,0:T(8,128)} custom-call(s32[2]{0:T(128)S(1)} %pad_add_fusion.place_ref, bf16[256,512]{1,0:T(8,128)(2,1)S(1)} %bitcast.31, bf16[256,512]{1,0:T(8,128)(2,1)S(1)} %collective-permute-done.3.refs_0_.refs_1_, bf16[256,512]{1,0:T(8,128)(2,1)S(1)} %collective-permute-done.5.refs_1_.refs_2_, ...), custom_call_target="tpu_custom_call" | custom-call | flops 1073741824 | bytes 2097152 | tf_op jit(solution)/shard_map/grad_weight/weight_gradient/pallas_call | solution.py:431
  115.7 2.9 %weight_gradient.3 = f32[1024,1024]{1,0:T(8,128)} custom-call(s32[2]{0:T(128)S(1)} %pad_add_fusion.place_ref, bf16[256,512]{1,0:T(8,128)(2,1)S(1)} %collective-permute-done.9.refs_1_.refs_0_, bf16[256,512]{1,0:T(8,128)(2,1)S(1)} %collective-permute-done.4.refs_0_.refs_1_, ...), custom_call_target="tpu_custom_call", output_to_operand_aliasing={{}: (13, {})} | custom-call | flops 1073741824 | bytes 2097152 | tf_op jit(solution)/shard_map/grad_weight/weight_gradient/pallas_call | solution.py:431
  118.6 5.7 %collective-permute-done.43 = bf16[272,512]{1,0:T(8,128)(2,1)S(1)} collective-permute-done((bf16[272,512]{1,0:T(8,128)(2,1)S(1)}, bf16[272,512]{1,0:T(8,128)(2,1)S(1)}, u32[]{:S(2)}, u32[]{:S(2)}) %collective-permute-start.43) | collective-permute-done | bytes 278560 | tf_op jit(solution)/shard_map/d_act/ppermute | solution.py:24
  125.1 1.8 %collective-permute-start.50 = (f32[8,512]{1,0:T(8,128)S(1)}, f32[8,512]{1,0:T(8,128)S(1)}, u32[]{:S(2)}, u32[]{:S(2)}) collective-permute-start(f32[8,512]{1,0:T(8,128)S(1)} %pad_maximum_fusion.1), channel_id=1, source_target_pairs={{0,24},{8,16},{16,8},{24,0},{1,25},{9,17},{17,9},{25,1},{2,26},{10... | collective-permute-start | bytes 49160 | tf_op jit(solution)/shard_map/norm_backward/ppermute | solution.py:24
  126.9 1.6 %collective-permute-start.48 = (f32[8,512]{1,0:T(8,128)S(1)}, f32[8,512]{1,0:T(8,128)S(1)}, u32[]{:S(2)}, u32[]{:S(2)}) collective-permute-start(f32[8,512]{1,0:T(8,128)S(1)} %pad_maximum_fusion.1), channel_id=1, source_target_pairs={{0,8},{8,0},{16,24},{24,16},{1,9},{9,1},{17,25},{25,17},{2,10},{10... | collective-permute-start | bytes 49160 | tf_op jit(solution)/shard_map/norm_backward/ppermute | solution.py:24
  128.6 1.1 collective-permute-done.49
  129.7 1.1 collective-permute-done.50
  (97 shorter events, 17.6 us)
Async XLA Ops:
  2.8 9.2 %collective-permute-start.2 = (f32[4,512]{1,0:T(4,128)S(1)}, f32[4,512]{1,0:T(4,128)S(1)}, u32[]{:S(2)}, u32[]{:S(2)}) collective-permute-start(f32[4,512]{1,0:T(4,128)S(1)} %pad_maximum_fusion.2), channel_id=1, source_target_pairs={{0,24},{8,16},{16,8},{24,0},{1,25},{9,17},{17,9},{25,1},{2,26},{10... | collective-permute-start | bytes 24584 | tf_op jit(solution)/shard_map/norm_stats/ppermute | solution.py:24
  7.9 4.5 %collective-permute-start.1 = (f32[4,512]{1,0:T(4,128)S(1)}, f32[4,512]{1,0:T(4,128)S(1)}, u32[]{:S(2)}, u32[]{:S(2)}) collective-permute-start(f32[4,512]{1,0:T(4,128)S(1)} %pad_maximum_fusion.2), channel_id=1, source_target_pairs={{0,16},{8,24},{16,0},{24,8},{1,17},{9,25},{17,1},{25,9},{2,18},{10... | collective-permute-start | bytes 24584 | tf_op jit(solution)/shard_map/norm_stats/ppermute | solution.py:24
  7.9 4.5 %collective-permute-start = (f32[4,512]{1,0:T(4,128)S(1)}, f32[4,512]{1,0:T(4,128)S(1)}, u32[]{:S(2)}, u32[]{:S(2)}) collective-permute-start(f32[4,512]{1,0:T(4,128)S(1)} %pad_maximum_fusion.2), channel_id=1, source_target_pairs={{0,8},{8,0},{16,24},{24,16},{1,9},{9,1},{17,25},{25,17},{2,10},{10... | collective-permute-start | bytes 24584 | tf_op jit(solution)/shard_map/norm_stats/ppermute | solution.py:24
  12.8 3.6 %collective-permute-start.9 = (bf16[256,512]{1,0:T(8,128)(2,1)S(1)}, bf16[256,512]{1,0:T(8,128)(2,1)S(1)}, u32[]{:S(2)}, u32[]{:S(2)}) collective-permute-start(bf16[256,512]{1,0:T(8,128)(2,1)S(1)} %bitcast.25), channel_id=1, source_target_pairs={{0,1},{1,0},{2,3},{3,2},{4,5},{5,4},{6,7},{7,6},{8,9},{9,8},{10,11... | collective-permute-start | bytes 786440 | tf_op jit(solution)/shard_map/act_gather/ppermute | solution.py:24
  12.9 10.1 %collective-permute-start.7 = (bf16[256,512]{1,0:T(8,128)(2,1)S(1)}, bf16[256,512]{1,0:T(8,128)(2,1)S(1)}, u32[]{:S(2)}, u32[]{:S(2)}) collective-permute-start(bf16[256,512]{1,0:T(8,128)(2,1)S(1)} %bitcast.26), channel_id=1, source_target_pairs={{0,6},{1,7},{2,4},{3,5},{4,2},{5,3},{6,0},{7,1},{8,14},{9,15},{10,... | collective-permute-start | bytes 786440 | tf_op jit(solution)/shard_map/act_gather/ppermute | solution.py:24
  15.4 12.7 %collective-permute-start.5 = (bf16[256,512]{1,0:T(8,128)(2,1)S(1)}, bf16[256,512]{1,0:T(8,128)(2,1)S(1)}, u32[]{:S(2)}, u32[]{:S(2)}) collective-permute-start(bf16[256,512]{1,0:T(8,128)(2,1)S(1)} %bitcast.27), channel_id=1, source_target_pairs={{0,4},{1,5},{2,6},{3,7},{4,0},{5,1},{6,2},{7,3},{8,12},{9,13},{10,... | collective-permute-start | bytes 786440 | tf_op jit(solution)/shard_map/act_gather/ppermute | solution.py:24
  15.9 12.3 %collective-permute-start.3 = (bf16[256,512]{1,0:T(8,128)(2,1)S(1)}, bf16[256,512]{1,0:T(8,128)(2,1)S(1)}, u32[]{:S(2)}, u32[]{:S(2)}) collective-permute-start(bf16[256,512]{1,0:T(8,128)(2,1)S(1)} %bitcast.28), channel_id=1, source_target_pairs={{0,2},{1,3},{2,0},{3,1},{4,6},{5,7},{6,4},{7,5},{8,10},{9,11},{10,... | collective-permute-start | bytes 786440 | tf_op jit(solution)/shard_map/act_gather/ppermute | solution.py:24
  16.5 12.2 %collective-permute-start.10 = (bf16[128,512]{1,0:T(8,128)(2,1)S(1)}, bf16[128,512]{1,0:T(8,128)(2,1)S(1)}, u32[]{:S(2)}, u32[]{:S(2)}) collective-permute-start(bf16[128,512]{1,0:T(8,128)(2,1)S(1)} %slice_bitcast_fusion), channel_id=1, source_target_pairs={{0,16},{16,24},{24,8},{8,0},{1,17},{17,25},{25,9},{9,1},{2,18},{18... | collective-permute-start | bytes 393224 | tf_op jit(solution)/shard_map/act_gather/ppermute | solution.py:34
  18.5 10.2 %collective-permute-start.11 = (bf16[128,512]{1,0:T(8,128)(2,1)S(1)}, bf16[128,512]{1,0:T(8,128)(2,1)S(1)}, u32[]{:S(2)}, u32[]{:S(2)}) collective-permute-start(bf16[128,512]{1,0:T(8,128)(2,1)S(1)} %slice_bitcast_fusion), channel_id=1, source_target_pairs={{0,24},{16,8},{24,0},{8,16},{1,25},{17,9},{25,1},{9,17},{2,26},{18... | collective-permute-start | bytes 393224 | tf_op jit(solution)/shard_map/act_gather/ppermute | solution.py:34
  23.0 8.6 %collective-permute-start.12 = (bf16[128,512]{1,0:T(8,128)(2,1)S(1)}, bf16[128,512]{1,0:T(8,128)(2,1)S(1)}, u32[]{:S(2)}, u32[]{:S(2)}) collective-permute-start(bf16[128,512]{1,0:T(8,128)(2,1)S(1)} %slice_bitcast_fusion), channel_id=1, source_target_pairs={{0,8},{16,0},{24,16},{8,24},{1,9},{17,1},{25,17},{9,25},{2,10},{18... | collective-permute-start | bytes 393224 | tf_op jit(solution)/shard_map/act_gather/ppermute | solution.py:34
  28.1 6.5 %collective-permute-start.8 = (bf16[256,512]{1,0:T(8,128)(2,1)S(1)}, bf16[256,512]{1,0:T(8,128)(2,1)S(1)}, u32[]{:S(2)}, u32[]{:S(2)}) collective-permute-start(bf16[256,512]{1,0:T(8,128)(2,1)S(1)} %collective-permute-done.7.refs_2_.refs_3_), channel_id=1, source_target_pairs={{0,1},{1,0},{2,3},{3,2},{4,5},{5,4},{6,7},{7,6},{8,9},{9,8},{10,11... | collective-permute-start | bytes 786440 | tf_op jit(solution)/shard_map/act_gather/ppermute | solution.py:24
  28.2 9.7 %collective-permute-start.6 = (bf16[256,512]{1,0:T(8,128)(2,1)S(1)}, bf16[256,512]{1,0:T(8,128)(2,1)S(1)}, u32[]{:S(2)}, u32[]{:S(2)}) collective-permute-start(bf16[256,512]{1,0:T(8,128)(2,1)S(1)} %collective-permute-done.5.refs_1_.refs_2_), channel_id=1, source_target_pairs={{0,1},{1,0},{2,3},{3,2},{4,5},{5,4},{6,7},{7,6},{8,9},{9,8},{10,11... | collective-permute-start | bytes 786440 | tf_op jit(solution)/shard_map/act_gather/ppermute | solution.py:24
  28.6 9.3 %collective-permute-start.4 = (bf16[256,512]{1,0:T(8,128)(2,1)S(1)}, bf16[256,512]{1,0:T(8,128)(2,1)S(1)}, u32[]{:S(2)}, u32[]{:S(2)}) collective-permute-start(bf16[256,512]{1,0:T(8,128)(2,1)S(1)} %collective-permute-done.3.refs_0_.refs_1_), channel_id=1, source_target_pairs={{0,1},{1,0},{2,3},{3,2},{4,5},{5,4},{6,7},{7,6},{8,9},{9,8},{10,11... | collective-permute-start | bytes 786440 | tf_op jit(solution)/shard_map/act_gather/ppermute | solution.py:24
  31.6 13.0 %collective-permute-start.18 = (bf16[384,512]{1,0:T(8,128)(2,1)S(1)}, bf16[384,512]{1,0:T(8,128)(2,1)S(1)}, u32[]{:S(2)}, u32[]{:S(2)}) collective-permute-start(bf16[384,512]{1,0:T(8,128)(2,1)S(1)} %constant_dynamic-update-slice_fusion.refs_0_.refs_4_), channel_id=1, source_target_pairs={{0,6},{1,7},{2,4},{3,5},{4,2},{5,3},{6,0},{7,1},{8,14},{9,15},{10,... | collective-permute-start | bytes 1179656 | tf_op jit(solution)/shard_map/act_gather/ppermute | solution.py:24
  34.1 17.9 %collective-permute-start.16 = (bf16[384,512]{1,0:T(8,128)(2,1)S(1)}, bf16[384,512]{1,0:T(8,128)(2,1)S(1)}, u32[]{:S(2)}, u32[]{:S(2)}) collective-permute-start(bf16[384,512]{1,0:T(8,128)(2,1)S(1)} %constant_dynamic-update-slice_fusion.refs_0_.refs_4_), channel_id=1, source_target_pairs={{0,4},{1,5},{2,6},{3,7},{4,0},{5,1},{6,2},{7,3},{8,12},{9,13},{10,... | collective-permute-start | bytes 1179656 | tf_op jit(solution)/shard_map/act_gather/ppermute | solution.py:24
  34.6 17.5 %collective-permute-start.14 = (bf16[384,512]{1,0:T(8,128)(2,1)S(1)}, bf16[384,512]{1,0:T(8,128)(2,1)S(1)}, u32[]{:S(2)}, u32[]{:S(2)}) collective-permute-start(bf16[384,512]{1,0:T(8,128)(2,1)S(1)} %constant_dynamic-update-slice_fusion.refs_0_.refs_4_), channel_id=1, source_target_pairs={{0,2},{1,3},{2,0},{3,1},{4,6},{5,7},{6,4},{7,5},{8,10},{9,11},{10,... | collective-permute-start | bytes 1179656 | tf_op jit(solution)/shard_map/act_gather/ppermute | solution.py:24
  39.5 13.0 %collective-permute-start.20 = (bf16[128,1024]{1,0:T(8,128)(2,1)S(1)}, bf16[128,1024]{1,0:T(8,128)(2,1)S(1)}, u32[]{:S(2)}, u32[]{:S(2)}) collective-permute-start(bf16[128,1024]{1,0:T(8,128)(2,1)S(1)} %get-tuple-element.68.refs_4_.refs_9_), channel_id=1, source_target_pairs={{0,16},{16,24},{24,8},{8,0},{1,17},{17,25},{25,9},{9,1},{2,18},{18... | collective-permute-start | bytes 786440 | tf_op jit(solution)/shard_map/z_ring/ppermute | solution.py:34
  39.6 15.3 %collective-permute-start.13 = (bf16[384,512]{1,0:T(8,128)(2,1)S(1)}, bf16[384,512]{1,0:T(8,128)(2,1)S(1)}, u32[]{:S(2)}, u32[]{:S(2)}) collective-permute-start(bf16[384,512]{1,0:T(8,128)(2,1)S(1)} %constant_dynamic-update-slice_fusion.refs_0_.refs_4_), channel_id=1, source_target_pairs={{0,1},{1,0},{2,3},{3,2},{4,5},{5,4},{6,7},{7,6},{8,9},{9,8},{10,11... | collective-permute-start | bytes 1179656 | tf_op jit(solution)/shard_map/act_gather/ppermute | solution.py:24
  44.6 17.6 %collective-permute-start.19 = (bf16[384,512]{1,0:T(8,128)(2,1)S(1)}, bf16[384,512]{1,0:T(8,128)(2,1)S(1)}, u32[]{:S(2)}, u32[]{:S(2)}) collective-permute-start(bf16[384,512]{1,0:T(8,128)(2,1)S(1)} %collective-permute-done.18.refs_3_.refs_7_), channel_id=1, source_target_pairs={{0,1},{1,0},{2,3},{3,2},{4,5},{5,4},{6,7},{7,6},{8,9},{9,8},{10,11... | collective-permute-start | bytes 1179656 | tf_op jit(solution)/shard_map/act_gather/ppermute | solution.py:24
  52.0 10.1 %collective-permute-start.17 = (bf16[384,512]{1,0:T(8,128)(2,1)S(1)}, bf16[384,512]{1,0:T(8,128)(2,1)S(1)}, u32[]{:S(2)}, u32[]{:S(2)}) collective-permute-start(bf16[384,512]{1,0:T(8,128)(2,1)S(1)} %collective-permute-done.16.refs_2_.refs_6_), channel_id=1, source_target_pairs={{0,1},{1,0},{2,3},{3,2},{4,5},{5,4},{6,7},{7,6},{8,9},{9,8},{10,11... | collective-permute-start | bytes 1179656 | tf_op jit(solution)/shard_map/act_gather/ppermute | solution.py:24
  52.1 10.0 %collective-permute-start.15 = (bf16[384,512]{1,0:T(8,128)(2,1)S(1)}, bf16[384,512]{1,0:T(8,128)(2,1)S(1)}, u32[]{:S(2)}, u32[]{:S(2)}) collective-permute-start(bf16[384,512]{1,0:T(8,128)(2,1)S(1)} %collective-permute-done.14.refs_1_.refs_5_), channel_id=1, source_target_pairs={{0,1},{1,0},{2,3},{3,2},{4,5},{5,4},{6,7},{7,6},{8,9},{9,8},{10,11... | collective-permute-start | bytes 1179656 | tf_op jit(solution)/shard_map/act_gather/ppermute | solution.py:24
  52.5 8.4 %collective-permute-start.21 = (bf16[128,1024]{1,0:T(8,128)(2,1)S(1)}, bf16[128,1024]{1,0:T(8,128)(2,1)S(1)}, u32[]{:S(2)}, u32[]{:S(2)}) collective-permute-start(bf16[128,1024]{1,0:T(8,128)(2,1)S(1)} %collective-permute-done.20.refs_5_.refs_11_), channel_id=1, source_target_pairs={{0,16},{16,24},{24,8},{8,0},{1,17},{17,25},{25,9},{9,1},{2,18},{18... | collective-permute-start | bytes 786440 | tf_op jit(solution)/shard_map/z_ring/ppermute | solution.py:34
  54.9 10.3 %collective-permute-start.22 = (f32[2,1024]{1,0:T(2,128)S(1)}, f32[2,1024]{1,0:T(2,128)S(1)}, u32[]{:S(2)}, u32[]{:S(2)}) collective-permute-start(f32[2,1024]{1,0:T(2,128)S(1)} %get-tuple-element.69), channel_id=1, source_target_pairs={{0,8},{16,0},{24,16},{8,24},{1,9},{17,1},{25,17},{9,25},{2,10},{18... | collective-permute-start | bytes 24584 | tf_op jit(solution)/shard_map/z_ring/ppermute | solution.py:34
  61.0 7.4 %collective-permute-start.24 = (bf16[128,1024]{1,0:T(8,128)(2,1)S(1)}, bf16[128,1024]{1,0:T(8,128)(2,1)S(1)}, u32[]{:S(2)}, u32[]{:S(2)}) collective-permute-start(bf16[128,1024]{1,0:T(8,128)(2,1)S(1)} %collective-permute-done.21.refs_6_.refs_13_), channel_id=1, source_target_pairs={{0,16},{16,24},{24,8},{8,0},{1,17},{17,25},{25,9},{9,1},{2,18},{18... | collective-permute-start | bytes 786440 | tf_op jit(solution)/shard_map/z_ring/ppermute | solution.py:34
  68.4 4.3 %collective-permute-start.25 = (f32[32,384]{1,0:T(8,128)S(1)}, f32[32,384]{1,0:T(8,128)S(1)}, u32[]{:S(2)}, u32[]{:S(2)}) collective-permute-start(f32[32,384]{1,0:T(8,128)S(1)} %get-tuple-element.114), channel_id=1, source_target_pairs={{0,2},{1,3},{2,0},{3,1},{4,6},{5,7},{6,4},{7,5},{8,10},{9,11},{10,... | collective-permute-start | bytes 147464 | tf_op jit(solution)/shard_map/kernel/ppermute | solution.py:24
  70.0 5.0 %collective-permute-start.27 = (f32[32,384]{1,0:T(8,128)S(1)}, f32[32,384]{1,0:T(8,128)S(1)}, u32[]{:S(2)}, u32[]{:S(2)}) collective-permute-start(f32[32,384]{1,0:T(8,128)S(1)} %get-tuple-element.115), channel_id=1, source_target_pairs={{0,6},{1,7},{2,4},{3,5},{4,2},{5,3},{6,0},{7,1},{8,14},{9,15},{10,... | collective-permute-start | bytes 147464 | tf_op jit(solution)/shard_map/kernel/ppermute | solution.py:24
  71.4 4.1 %collective-permute-start.26 = (f32[32,384]{1,0:T(8,128)S(1)}, f32[32,384]{1,0:T(8,128)S(1)}, u32[]{:S(2)}, u32[]{:S(2)}) collective-permute-start(f32[32,384]{1,0:T(8,128)S(1)} %get-tuple-element.116), channel_id=1, source_target_pairs={{0,4},{1,5},{2,6},{3,7},{4,0},{5,1},{6,2},{7,3},{8,12},{9,13},{10,... | collective-permute-start | bytes 147464 | tf_op jit(solution)/shard_map/kernel/ppermute | solution.py:24
  75.5 5.0 %collective-permute-start.30 = (bf16[32,384]{1,0:T(8,128)(2,1)S(1)}, bf16[32,384]{1,0:T(8,128)(2,1)S(1)}, u32[]{:S(2)}, u32[]{:S(2)}) collective-permute-start(bf16[32,384]{1,0:T(8,128)(2,1)S(1)} %get-tuple-element.110), channel_id=1, source_target_pairs={{0,8},{16,0},{24,16},{8,24},{1,9},{17,1},{25,17},{9,25},{2,10},{18... | collective-permute-start | bytes 73736 | tf_op jit(solution)/shard_map/kernel/ppermute | solution.py:34
  77.8 5.7 %collective-permute-start.29 = (bf16[32,384]{1,0:T(8,128)(2,1)S(1)}, bf16[32,384]{1,0:T(8,128)(2,1)S(1)}, u32[]{:S(2)}, u32[]{:S(2)}) collective-permute-start(bf16[32,384]{1,0:T(8,128)(2,1)S(1)} %get-tuple-element.110), channel_id=1, source_target_pairs={{0,24},{16,8},{24,0},{8,16},{1,25},{17,9},{25,1},{9,17},{2,26},{18... | collective-permute-start | bytes 73736 | tf_op jit(solution)/shard_map/kernel/ppermute | solution.py:34
  79.4 4.1 %collective-permute-start.28 = (bf16[32,384]{1,0:T(8,128)(2,1)S(1)}, bf16[32,384]{1,0:T(8,128)(2,1)S(1)}, u32[]{:S(2)}, u32[]{:S(2)}) collective-permute-start(bf16[32,384]{1,0:T(8,128)(2,1)S(1)} %get-tuple-element.110), channel_id=1, source_target_pairs={{0,16},{16,24},{24,8},{8,0},{1,17},{17,25},{25,9},{9,1},{2,18},{18... | collective-permute-start | bytes 73736 | tf_op jit(solution)/shard_map/kernel/ppermute | solution.py:34
  83.5 5.6 %collective-permute-start.36 = (bf16[4,32,384]{2,1,0:T(8,128)(2,1)S(1)}, bf16[4,32,384]{2,1,0:T(8,128)(2,1)S(1)}, u32[]{:S(2)}, u32[]{:S(2)}) collective-permute-start(bf16[4,32,384]{2,1,0:T(8,128)(2,1)S(1)} %pad_maximum_fusion.refs_0_), channel_id=1, source_target_pairs={{0,6},{1,7},{2,4},{3,5},{4,2},{5,3},{6,0},{7,1},{8,14},{9,15},{10,... | collective-permute-start | bytes 294920 | tf_op jit(solution)/shard_map/kernel/ppermute | solution.py:24
  85.0 5.1 %collective-permute-start.34 = (bf16[4,32,384]{2,1,0:T(8,128)(2,1)S(1)}, bf16[4,32,384]{2,1,0:T(8,128)(2,1)S(1)}, u32[]{:S(2)}, u32[]{:S(2)}) collective-permute-start(bf16[4,32,384]{2,1,0:T(8,128)(2,1)S(1)} %pad_maximum_fusion.refs_0_), channel_id=1, source_target_pairs={{0,4},{1,5},{2,6},{3,7},{4,0},{5,1},{6,2},{7,3},{8,12},{9,13},{10,... | collective-permute-start | bytes 294920 | tf_op jit(solution)/shard_map/kernel/ppermute | solution.py:24
  85.8 4.6 %collective-permute-start.32 = (bf16[4,32,384]{2,1,0:T(8,128)(2,1)S(1)}, bf16[4,32,384]{2,1,0:T(8,128)(2,1)S(1)}, u32[]{:S(2)}, u32[]{:S(2)}) collective-permute-start(bf16[4,32,384]{2,1,0:T(8,128)(2,1)S(1)} %pad_maximum_fusion.refs_0_), channel_id=1, source_target_pairs={{0,2},{1,3},{2,0},{3,1},{4,6},{5,7},{6,4},{7,5},{8,10},{9,11},{10,... | collective-permute-start | bytes 294920 | tf_op jit(solution)/shard_map/kernel/ppermute | solution.py:24
  87.7 5.0 %collective-permute-start.38 = (bf16[128,512]{1,0:T(8,128)(2,1)S(1)}, bf16[128,512]{1,0:T(8,128)(2,1)S(1)}, u32[]{:S(2)}, u32[]{:S(2)}) collective-permute-start(bf16[128,512]{1,0:T(8,128)(2,1)S(1)} %get-tuple-element.78), channel_id=1, source_target_pairs={{0,16},{16,24},{24,8},{8,0},{1,17},{17,25},{25,9},{9,1},{2,18},{18... | collective-permute-start | bytes 393224 | tf_op jit(solution)/shard_map/kernel/ppermute | solution.py:34
  89.1 5.3 %collective-permute-start.37 = (bf16[4,32,384]{2,1,0:T(8,128)(2,1)S(1)}, bf16[4,32,384]{2,1,0:T(8,128)(2,1)S(1)}, u32[]{:S(2)}, u32[]{:S(2)}) collective-permute-start(bf16[4,32,384]{2,1,0:T(8,128)(2,1)S(1)} %collective-permute-done.36.refs_6_), channel_id=1, source_target_pairs={{0,1},{1,0},{2,3},{3,2},{4,5},{5,4},{6,7},{7,6},{8,9},{9,8},{10,11... | collective-permute-start | bytes 294920 | tf_op jit(solution)/shard_map/kernel/ppermute | solution.py:24
  90.1 4.2 %collective-permute-start.35 = (bf16[4,32,384]{2,1,0:T(8,128)(2,1)S(1)}, bf16[4,32,384]{2,1,0:T(8,128)(2,1)S(1)}, u32[]{:S(2)}, u32[]{:S(2)}) collective-permute-start(bf16[4,32,384]{2,1,0:T(8,128)(2,1)S(1)} %collective-permute-done.34.refs_4_), channel_id=1, source_target_pairs={{0,1},{1,0},{2,3},{3,2},{4,5},{5,4},{6,7},{7,6},{8,9},{9,8},{10,11... | collective-permute-start | bytes 294920 | tf_op jit(solution)/shard_map/kernel/ppermute | solution.py:24
  90.4 4.0 %collective-permute-start.33 = (bf16[4,32,384]{2,1,0:T(8,128)(2,1)S(1)}, bf16[4,32,384]{2,1,0:T(8,128)(2,1)S(1)}, u32[]{:S(2)}, u32[]{:S(2)}) collective-permute-start(bf16[4,32,384]{2,1,0:T(8,128)(2,1)S(1)} %collective-permute-done.32.refs_2_), channel_id=1, source_target_pairs={{0,1},{1,0},{2,3},{3,2},{4,5},{5,4},{6,7},{7,6},{8,9},{9,8},{10,11... | collective-permute-start | bytes 294920 | tf_op jit(solution)/shard_map/kernel/ppermute | solution.py:24
  90.6 8.4 %collective-permute-start.39 = (bf16[128,512]{1,0:T(8,128)(2,1)S(1)}, bf16[128,512]{1,0:T(8,128)(2,1)S(1)}, u32[]{:S(2)}, u32[]{:S(2)}) collective-permute-start(bf16[128,512]{1,0:T(8,128)(2,1)S(1)} %get-tuple-element.89), channel_id=1, source_target_pairs={{0,24},{16,8},{24,0},{8,16},{1,25},{17,9},{25,1},{9,17},{2,26},{18... | collective-permute-start | bytes 393224 | tf_op jit(solution)/shard_map/kernel/ppermute | solution.py:34
  92.7 9.5 %collective-permute-start.40 = (bf16[128,512]{1,0:T(8,128)(2,1)S(1)}, bf16[128,512]{1,0:T(8,128)(2,1)S(1)}, u32[]{:S(2)}, u32[]{:S(2)}) collective-permute-start(bf16[128,512]{1,0:T(8,128)(2,1)S(1)} %get-tuple-element.90), channel_id=1, source_target_pairs={{0,8},{16,0},{24,16},{8,24},{1,9},{17,1},{25,17},{9,25},{2,10},{18... | collective-permute-start | bytes 393224 | tf_op jit(solution)/shard_map/kernel/ppermute | solution.py:34
  104.1 8.2 %collective-permute-start.45 = (bf16[128,512]{1,0:T(8,128)(2,1)S(1)}, bf16[128,512]{1,0:T(8,128)(2,1)S(1)}, u32[]{:S(2)}, u32[]{:S(2)}) collective-permute-start(bf16[128,512]{1,0:T(8,128)(2,1)S(1)} %collective-permute-done.38.refs_8_), channel_id=1, source_target_pairs={{0,1},{1,0},{2,3},{3,2},{4,5},{5,4},{6,7},{7,6},{8,9},{9,8},{10,11... | collective-permute-start | bytes 393224 | tf_op jit(solution)/shard_map/grad_weight/ppermute | solution.py:24
  108.7 9.9 %collective-permute-start.42 = (bf16[272,512]{1,0:T(8,128)(2,1)S(1)}, bf16[272,512]{1,0:T(8,128)(2,1)S(1)}, u32[]{:S(2)}, u32[]{:S(2)}) collective-permute-start(bf16[272,512]{1,0:T(8,128)(2,1)S(1)} %get-tuple-element.93), channel_id=1, source_target_pairs={{0,2},{1,3},{2,0},{3,1},{4,6},{5,7},{6,4},{7,5},{8,10},{9,11},{10,... | collective-permute-start | bytes 835592 | tf_op jit(solution)/shard_map/d_act/ppermute | solution.py:24
  110.0 14.4 %collective-permute-start.43 = (bf16[272,512]{1,0:T(8,128)(2,1)S(1)}, bf16[272,512]{1,0:T(8,128)(2,1)S(1)}, u32[]{:S(2)}, u32[]{:S(2)}) collective-permute-start(bf16[272,512]{1,0:T(8,128)(2,1)S(1)} %get-tuple-element.94), channel_id=1, source_target_pairs={{0,4},{1,5},{2,6},{3,7},{4,0},{5,1},{6,2},{7,3},{8,12},{9,13},{10,... | collective-permute-start | bytes 835592 | tf_op jit(solution)/shard_map/d_act/ppermute | solution.py:24
  110.8 13.5 %collective-permute-start.44 = (bf16[272,512]{1,0:T(8,128)(2,1)S(1)}, bf16[272,512]{1,0:T(8,128)(2,1)S(1)}, u32[]{:S(2)}, u32[]{:S(2)}) collective-permute-start(bf16[272,512]{1,0:T(8,128)(2,1)S(1)} %get-tuple-element.95), channel_id=1, source_target_pairs={{0,6},{1,7},{2,4},{3,5},{4,2},{5,3},{6,0},{7,1},{8,14},{9,15},{10,... | collective-permute-start | bytes 835592 | tf_op jit(solution)/shard_map/d_act/ppermute | solution.py:24
  112.3 3.4 %collective-permute-start.46 = (bf16[128,512]{1,0:T(8,128)(2,1)S(1)}, bf16[128,512]{1,0:T(8,128)(2,1)S(1)}, u32[]{:S(2)}, u32[]{:S(2)}) collective-permute-start(bf16[128,512]{1,0:T(8,128)(2,1)S(1)} %collective-permute-done.39.refs_9_), channel_id=1, source_target_pairs={{0,1},{1,0},{2,3},{3,2},{4,5},{5,4},{6,7},{7,6},{8,9},{9,8},{10,11... | collective-permute-start | bytes 393224 | tf_op jit(solution)/shard_map/grad_weight/ppermute | solution.py:24
  112.3 3.4 %collective-permute-start.47 = (bf16[128,512]{1,0:T(8,128)(2,1)S(1)}, bf16[128,512]{1,0:T(8,128)(2,1)S(1)}, u32[]{:S(2)}, u32[]{:S(2)}) collective-permute-start(bf16[128,512]{1,0:T(8,128)(2,1)S(1)} %collective-permute-done.40.refs_10_), channel_id=1, source_target_pairs={{0,1},{1,0},{2,3},{3,2},{4,5},{5,4},{6,7},{7,6},{8,9},{9,8},{10,11... | collective-permute-start | bytes 393224 | tf_op jit(solution)/shard_map/grad_weight/ppermute | solution.py:24
  125.0 4.7 %collective-permute-start.49 = (f32[8,512]{1,0:T(8,128)S(1)}, f32[8,512]{1,0:T(8,128)S(1)}, u32[]{:S(2)}, u32[]{:S(2)}) collective-permute-start(f32[8,512]{1,0:T(8,128)S(1)} %pad_maximum_fusion.1), channel_id=1, source_target_pairs={{0,16},{8,24},{16,0},{24,8},{1,17},{9,25},{17,1},{25,9},{2,18},{10... | collective-permute-start | bytes 49160 | tf_op jit(solution)/shard_map/norm_backward/ppermute | solution.py:24
  125.1 5.7 %collective-permute-start.50 = (f32[8,512]{1,0:T(8,128)S(1)}, f32[8,512]{1,0:T(8,128)S(1)}, u32[]{:S(2)}, u32[]{:S(2)}) collective-permute-start(f32[8,512]{1,0:T(8,128)S(1)} %pad_maximum_fusion.1), channel_id=1, source_target_pairs={{0,24},{8,16},{16,8},{24,0},{1,25},{9,17},{17,9},{25,1},{2,26},{10... | collective-permute-start | bytes 49160 | tf_op jit(solution)/shard_map/norm_backward/ppermute | solution.py:24
  126.9 3.9 %collective-permute-start.48 = (f32[8,512]{1,0:T(8,128)S(1)}, f32[8,512]{1,0:T(8,128)S(1)}, u32[]{:S(2)}, u32[]{:S(2)}) collective-permute-start(f32[8,512]{1,0:T(8,128)S(1)} %pad_maximum_fusion.1), channel_id=1, source_target_pairs={{0,8},{8,0},{16,24},{24,16},{1,9},{9,1},{17,25},{25,17},{2,10},{10... | collective-permute-start | bytes 49160 | tf_op jit(solution)/shard_map/norm_backward/ppermute | solution.py:24
  (6 other events, 35.4 us)

commit v8 on v7

--- a/solution.py
+++ b/solution.py
@@ -138,10 +138,10 @@
     )(*operands)
 
 
-def strip_kernel(n_batch, n_slots, rows, n_col, place_ref, *refs):
+def strip_kernel(n_batch, n_slots, rows, *refs):
     z_refs = [refs[:n_batch], refs[n_batch : n_batch + n_slots]]
     sum_refs = refs[n_batch + n_slots : 2 * n_batch]
-    even_ref, odd_ref, strip = refs[2 * n_batch :]
+    strip = refs[2 * n_batch]
     local_rows = z_refs[0][0].shape[0]
     for v in range(2):
         here = pl.ds(v * local_rows, local_rows)
@@ -155,28 +155,30 @@
             strip[here, pl.ds(u * local_rows, local_rows)] = lax.dot_general(
                 rounded[0], rounded[u], (((1,), (1,)), ((), ())), preferred_element_type=f32
             )
-    part = 2 * local_rows // n_col
-    for k in range(n_col):
-        start = pl.multiple_of((place_ref[1] ^ k) * part, part)
-        (odd_ref if k % 2 else even_ref)[k // 2] = strip[pl.ds(start, part), :]
-
-
-def strip_call(place, z0, z1, sums, rows, n_col):
+
+
+def strip_call(z0, z1, sums, rows):
     local_rows, columns = z0[0].shape
     tall = 2 * local_rows
     wide = len(z1) * local_rows
-    part = jax.ShapeDtypeStruct((n_col // 2, tall // n_col, wide), f32)
-    operands = [place] + list(z0) + list(z1) + list(sums)
+    operands = list(z0) + list(z1) + list(sums)
     return pl.pallas_call(
-        functools.partial(strip_kernel, len(z0), len(z1), rows, n_col),
-        out_shape=(part, part),
-        in_specs=[IN_SMEM] + [IN_VMEM] * (len(operands) - 1),
-        out_specs=(IN_VMEM, IN_VMEM),
-        scratch_shapes=[pltpu.VMEM((tall, wide), f32)],
+        functools.partial(strip_kernel, len(z0), len(z1), rows),
+        out_shape=jax.ShapeDtypeStruct((tall, wide), f32),
+        in_specs=[IN_VMEM] * len(operands),
+        out_specs=IN_VMEM,
         compiler_params=params(12),
         cost_estimate=cost(2 * tall * wide * columns, 2 * tall * columns * len(z0)),
         name="kernel_strip",
     )(*operands)
+
+
+def ring_position(plane, n):
+    return jnp.where((plane & 1) == 0, plane >> 1, n - 1 - (plane >> 1))
+
+
+def ring_plane(position, n):
+    return jnp.where(2 * position < n, 2 * position, 2 * (n - position) - 1)
 
 
 def dz_kernel(n_batch, n_col, tile, constants, place_ref, own_ref, *refs):
@@ -193,10 +195,13 @@
     own = jnp.sum(jnp.sum(own, axis=0, keepdims=True), axis=1, keepdims=True)
     share_ref[...] = jnp.broadcast_to(block_share * own, share_ref.shape)
     part = 2 * local_rows // n_col
-    for k in range(n_col):
-        start = pl.multiple_of((place_ref[1] ^ k) * part, part)
-        for s in range(n_batch):
-            strips[s, pl.ds(start, part), :] = strip_refs[k][s].astype(f32)
+    position = ring_position(place_ref[0], n_batch)
+    for s in range(n_batch):
+        behind = position - s
+        plane = ring_plane(jnp.where(behind < 0, behind + n_batch, behind), n_batch)
+        for k in range(n_col):
+            start = pl.multiple_of((place_ref[1] ^ k) * part, part)
+            strips[s, pl.ds(start, part), :] = strip_refs[k][plane].astype(f32)
     for v in range(2):
         for s in range(n_batch):
             here = pl.ds(s * local_rows, local_rows)
@@ -340,13 +345,13 @@
     half = n_col // 2
     pieces, outs = refs[:half], refs[half:]
     b, c = place_ref[0], place_ref[1]
-    position = jnp.where((b & 1) == 0, b >> 1, n_batch - 1 - (b >> 1))
+    position = ring_position(b, n_batch)
     i = 0
     for block in range(n_col // n_batch // 2):
         for d in range(1, n_batch):
             ahead = position + d
             ahead = jnp.where(ahead >= n_batch, ahead - n_batch, ahead)
-            plane = jnp.where(2 * ahead < n_batch, 2 * ahead, 2 * (n_batch - ahead) - 1)
+            plane = ring_plane(ahead, n_batch)
             chosen = held_place(plane, c, block, n_col, n_batch)
             for e in range(half):
 
@@ -508,11 +513,10 @@
         first, pieces[1] = lax.optimization_barrier((act[0], pieces[1]))
         others = [ring_send(first, "batch", d) for d in range(1, n_batch)]
         pieces = sibling_pieces(pieces, n_col)
-        far_pieces = gather_pieces(jnp.concatenate(others), n_col)
+        far_pieces = link_pieces(jnp.concatenate(others), n_col)
     with jax.named_scope("z"):
 
-        def z_of(source, groups):
-            total = None
+        def z_of(source, groups, total=None):
             for i, ks in enumerate(groups):
                 total = z_call(
                     place,
@@ -526,30 +530,40 @@
             return total
 
         z_own0, z_own1, z_sum = z_of(pieces, [[0, 1], far, [k + 1 for k in far]])
-        *z_far, _ = z_of(far_pieces, [evens, odds])
+        z_sum, held_back = lax.optimization_barrier((z_sum, [pieces[k] for k in evens]))
     with jax.named_scope("z_ring"):
-        z_ring = [z_own1]
-        for _ in range(1, n_batch):
-            z_ring.append(ring_send(z_ring[-1], "batch", 1))
+        z_ring = [z_own1, ring_send(z_own1, "batch", 1)]
+        z_ring[1], far_pieces[far[-1]] = lax.optimization_barrier((z_ring[1], far_pieces[far[-1]]))
+        z_ring.append(ring_send(z_ring[1], "batch", 1))
         sums = [ring_send(z_sum, "batch", d) for d in range(reach + 1, n_batch)]
-        z_flat = [z_own0] + z_far
-    with jax.named_scope("kernel"):
-        even_part, odd_part = strip_call(place, z_flat, z_ring[: reach + 1], sums, rows, n_col)
-        even_part = even_part + xor_send(odd_part, "col", 1)
-        even_part, z_ring[reach + 1 :] = lax.optimization_barrier((even_part, z_ring[reach + 1 :]))
-        strip = even_part[0]
-        for k in far:
-            strip = strip + xor_send(even_part[k // 2], "col", k)
-        slots = list(zip(z_flat, z_ring))
-        mine = strip.astype(bf16)
-        mine = jnp.stack([mine] + [ring_send(mine, "batch", d) for d in range(1, n_batch)])
-        mine, held_back = lax.optimization_barrier((mine, [pieces[k] for k in evens]))
-        strips = gather_pieces(mine, n_col)
         picked = pick_call(place, held_back, n_batch, n_col)
         blocks = [
             ring_send(x, "batch", 1 + i % (n_batch - 1)) for i, x in enumerate(picked)
         ]
-        strips, blocks[0] = lax.optimization_barrier((strips, blocks[0]))
+    with jax.named_scope("z_far"):
+        start = z_call(
+            place, [0, far[-1]], [far_pieces[0], far_pieces[far[-1]]], held_weight, None, False, local_rows
+        )
+        start, far_pieces[far[0]], z_ring[2] = lax.optimization_barrier(
+            (start, far_pieces[far[0]], z_ring[2])
+        )
+        far_pieces = sibling_pieces(far_pieces, n_col)
+        for _ in range(3, n_batch):
+            z_ring.append(ring_send(z_ring[-1], "batch", 1))
+        *z_far, _ = z_of(far_pieces, [far[:-1], odds], start)
+        z_flat = [z_own0] + z_far
+    with jax.named_scope("kernel"):
+        strip = strip_call(z_flat, z_ring[: reach + 1], sums, rows)
+        part = tall // n_col
+        parts = lax.all_to_all(strip.reshape(n_col, part, -1), "col", 0, 0, tiled=True)
+        parts, z_ring[reach + 1 :], blocks = lax.optimization_barrier(
+            (parts, z_ring[reach + 1 :], blocks)
+        )
+        slots = list(zip(z_flat, z_ring))
+        strip = jnp.sum(parts, axis=0)
+        mine = jnp.broadcast_to(strip.astype(bf16)[None], (n_batch,) + strip.shape)
+        mine = lax.all_to_all(mine, "batch", 0, 0, tiled=True)
+        strips = gather_pieces(mine, n_col)
     with jax.named_scope("dz"):
         constants = (
             4.0 * scale / denom,
@@ -561,7 +575,6 @@
             1.0 / denom,
         )
         dz, share = dz_call(place, strip, [strips[k] for k in range(n_col)], slots, constants)
-        dz, blocks[1:] = lax.optimization_barrier((dz, blocks[1:]))
     with jax.named_scope("d_act"):
         (away,) = d_act_call(place, dz, share, held_weight, n_batch, n_col, None)
         got = xor_send(away, "col", 1)

time: 133 us -> 156 us (1.17)
  local copies, waits for them, and re-layouts: 0.07 us -> 12.6 us
  blocking collectives: 0 us -> 8.55 us
  starting transfers between devices: 46.6 us -> 42.7 us
  waiting for transfers between devices: 50.6 us -> 53.8 us
    unnamed x8 -> x72, local copies, waits for them, and re-layouts: 0.04 us -> 12.6 us
    all_to_all x0 -> x1, blocking collectives: none -> 8.55 us  [shards(): mine = lax.all_to_all(mine, 'batch', 0, 0, tiled=True)]
    ppermute x13 -> x10, waiting for transfers between devices: 13.9 us -> 19.8 us  [ring_send(): lax.ppermute(x, axis, [(order[i], order[(i + d) % n]) for i in range(n)])]
    ppermute x13 -> x10, starting transfers between devices: 16.8 us -> 12.1 us  [ring_send(): lax.ppermute(x, axis, [(order[i], order[(i + d) % n]) for i in range(n)])]
    all_to_all x0 -> x1, starting transfers between devices: none -> 4.11 us  [shards(): lax.all_to_all(strip.reshape(n_col, part, -1), 'col', 0, 0, tiled=True)]
    ppermute x38 -> x34, starting transfers between devices: 29.8 us -> 26.5 us  [xor_send(): return lax.ppermute(x, axis, [(i, i ^ k) for i in range(n)])]
    ppermute x38 -> x34, waiting for transfers between devices: 36.7 us -> 34 us  [xor_send(): return lax.ppermute(x, axis, [(i, i ^ k) for i in range(n)])]
    pallas_call x5 -> x6, Pallas kernels: 9.62 us -> 10.5 us  [z_call(): pl.pallas_call(functools.partial(z_kernel, tuple(ks), before is None, las...]
  transfers between devices with their start and end apart: 51 -> 45, of which waited for: 25 -> 21; matrix products, arithmetic and copies ran while one was open for 0% -> 0% of each run, Pallas kernels for 21% -> 15%
where the time goes in v8:
time: 156 us; the launch traced here: 155 us
  waiting for transfers between devices  53.8 us (34%)
  starting transfers between devices  42.7 us (27%)
  Pallas kernels  30.1 us (19%)
  local copies, waits for them, and re-layouts  12.6 us (8%)
  blocking collectives  8.55 us (5%)
  other arithmetic  6.26 us (4%)
    ppermute x34, waiting for transfers between devices, xor_send(): return lax.ppermute(x, axis, [(i, i ^ k) for i in range(n)])  34 us
    ppermute x34, starting transfers between devices, xor_send(): return lax.ppermute(x, axis, [(i, i ^ k) for i in range(n)])  26.5 us
    ppermute x10, waiting for transfers between devices, ring_send(): lax.ppermute(x, axis, [(order[i], order[(i + d) % n]) for i in range(n)])  19.8 us
    unnamed x72, local copies, waits for them, and re-layouts  12.6 us
    ppermute x10, starting transfers between devices, ring_send(): lax.ppermute(x, axis, [(order[i], order[(i + d) % n]) for i in range(n)])  12.1 us
    pallas_call x6, Pallas kernels, z_call(): pl.pallas_call(functools.partial(z_kernel, tuple(ks), before is None, las...  10.5 us
    all_to_all x1, blocking collectives, shards(): mine = lax.all_to_all(mine, 'batch', 0, 0, tiled=True)  8.55 us
    pallas_call x2, Pallas kernels, weight_grad_call(): pl.pallas_call(functools.partial(weight_grad_kernel, len(arrived), int(be...  6.23 us
  transfers between devices with their start and end apart: 45, of which 21 were waited for; matrix products, arithmetic and copies ran while one was open for 0% of the time, Pallas kernels for 15%

profile of v8, /device:TPU:0, one launch (start us, length us, event | category | flops | bytes accessed | tf_op | source)
XLA Modules:
  0.0 155.3 jit_solution(16180178405021513724)
XLA Ops:
  0.7 1.0 convert_reduce_fusion
  1.7 1.0 fusion.8
  2.8 5.1 %collective-permute-start.2 = (f32[4,512]{1,0:T(4,128)S(1)}, f32[4,512]{1,0:T(4,128)S(1)}, u32[]{:S(2)}, u32[]{:S(2)}) collective-permute-start(f32[4,512]{1,0:T(4,128)S(1)} %pad_maximum_fusion.1), channel_id=1, source_target_pairs={{0,24},{8,16},{16,8},{24,0},{1,25},{9,17},{17,9},{25,1},{2,26},{10... | collective-permute-start | bytes 24584 | tf_op jit(solution)/shard_map/norm_stats/ppermute | solution.py:24
  8.6 3.5 %weight_load.1 = (bf16[4096,1024]{1,0:T(8,128)(2,1)S(1)}, f32[4,512]{1,0:T(4,128)S(1)}) custom-call(bf16[4096,1024]{1,0:T(8,128)(2,1)} %w_ref), custom_call_target="tpu_custom_call" | custom-call | bytes 16777216 | tf_op jit(solution)/shard_map/weight_load/weight_load/pallas_call | solution.py:78
  12.9 2.5 %collective-permute-start.7 = (bf16[256,512]{1,0:T(8,128)(2,1)S(1)}, bf16[256,512]{1,0:T(8,128)(2,1)S(1)}, u32[]{:S(2)}, u32[]{:S(2)}) collective-permute-start(bf16[256,512]{1,0:T(8,128)(2,1)S(1)} %bitcast.10), channel_id=1, source_target_pairs={{0,6},{1,7},{2,4},{3,5},{4,2},{5,3},{6,0},{7,1},{8,14},{9,15},{10,... | collective-permute-start | bytes 786440 | tf_op jit(solution)/shard_map/act_gather/ppermute | solution.py:24
  16.5 2.1 %collective-permute-start.10 = (bf16[128,512]{1,0:T(8,128)(2,1)S(1)}, bf16[128,512]{1,0:T(8,128)(2,1)S(1)}, u32[]{:S(2)}, u32[]{:S(2)}) collective-permute-start(bf16[128,512]{1,0:T(8,128)(2,1)S(1)} %slice_bitcast_fusion), channel_id=1, source_target_pairs={{0,16},{16,24},{24,8},{8,0},{1,17},{17,25},{25,9},{9,1},{2,18},{18... | collective-permute-start | bytes 393224 | tf_op jit(solution)/shard_map/act_gather/ppermute | solution.py:34
  18.5 1.4 collective-permute-start.11
  20.0 1.3 z_matmul.6.refs_4_
  21.3 1.7 %collective-permute-done.7.refs_2_.refs_3_ = bf16[256,512]{1,0:T(8,128)(2,1)S(1)} collective-permute-done((bf16[256,512]{1,0:T(8,128)(2,1)S(1)}, bf16[256,512]{1,0:T(8,128)(2,1)S(1)}, u32[]{:S(2)}, u32[]{:S(2)}) %collective-permute-start.7) | collective-permute-done | bytes 262176 | tf_op jit(solution)/shard_map/act_gather/ppermute | solution.py:24
  23.0 1.0 collective-permute-start.12
  24.0 4.1 %collective-permute-done.5.refs_1_.refs_2_ = bf16[256,512]{1,0:T(8,128)(2,1)S(1)} collective-permute-done((bf16[256,512]{1,0:T(8,128)(2,1)S(1)}, bf16[256,512]{1,0:T(8,128)(2,1)S(1)}, u32[]{:S(2)}, u32[]{:S(2)}) %collective-permute-start.5) | collective-permute-done | bytes 262176 | tf_op jit(solution)/shard_map/act_gather/ppermute | solution.py:24
  28.8 2.8 %collective-permute-done.12 = bf16[128,512]{1,0:T(8,128)(2,1)S(1)} collective-permute-done((bf16[128,512]{1,0:T(8,128)(2,1)S(1)}, bf16[128,512]{1,0:T(8,128)(2,1)S(1)}, u32[]{:S(2)}, u32[]{:S(2)}) %collective-permute-start.12) | collective-permute-done | bytes 131104 | tf_op jit(solution)/shard_map/act_gather/ppermute | solution.py:34
  31.6 2.5 %collective-permute-start.15 = (bf16[384,512]{1,0:T(8,128)(2,1)S(1)}, bf16[384,512]{1,0:T(8,128)(2,1)S(1)}, u32[]{:S(2)}, u32[]{:S(2)}) collective-permute-start(bf16[384,512]{1,0:T(8,128)(2,1)S(1)} %constant_dynamic-update-slice_fusion.refs_0_.refs_4_), channel_id=1, source_target_pairs={{0,6},{1,7},{2,4},{3,5},{4,2},{5,3},{6,0},{7,1},{8,14},{9,15},{10,... | collective-permute-start | bytes 1179656 | tf_op jit(solution)/shard_map/act_gather/ppermute | solution.py:24
  34.1 1.6 %z_matmul.7.refs_4_ = f32[256,1024]{1,0:T(8,128)S(1)} custom-call(s32[2]{0:T(128)S(1)} %pad_add_fusion.place_ref, bf16[256,512]{1,0:T(8,128)(2,1)S(1)} %collective-permute-done.3.refs_0_.refs_1_, bf16[256,512]{1,0:T(8,128)(2,1)S(1)} %collective-permute-done.5.refs_1_.refs_2_, bf16[256,512]{1,0:T(8,128)(2,1)S(1)} %collective-permute-done.7.refs_2_.refs_3_, ...), custom_call_target="tpu_custom_call" | custom-call | flops 805306368 | bytes 524288 | tf_op jit(solution)/shard_map/z/z_matmul/pallas_call | solution.py:130
  35.8 1.6 z_matmul.8
  38.5 6.0 %collective-permute-done.15.refs_1_.refs_7_ = bf16[384,512]{1,0:T(8,128)(2,1)S(1)} collective-permute-done((bf16[384,512]{1,0:T(8,128)(2,1)S(1)}, bf16[384,512]{1,0:T(8,128)(2,1)S(1)}, u32[]{:S(2)}, u32[]{:S(2)}) %collective-permute-start.15) | collective-permute-done | bytes 393248 | tf_op jit(solution)/shard_map/act_gather/ppermute | solution.py:24
  45.4 1.2 collective-permute-start.17
  47.1 5.0 %collective-permute-done.19.refs_1_.refs_6_ = bf16[384,512]{1,0:T(8,128)(2,1)S(1)} collective-permute-done((bf16[384,512]{1,0:T(8,128)(2,1)S(1)}, bf16[384,512]{1,0:T(8,128)(2,1)S(1)}, u32[]{:S(2)}, u32[]{:S(2)}) %collective-permute-start.19) | collective-permute-done | bytes 393248 | tf_op jit(solution)/shard_map/act_gather/ppermute | solution.py:24
  52.1 1.5 z_matmul.9.refs_3_
  54.7 1.5 z_matmul.10.refs_5_
  56.3 3.0 %z_matmul.11 = (bf16[128,1024]{1,0:T(8,128)(2,1)S(1)}, bf16[128,1024]{1,0:T(8,128)(2,1)S(1)}, bf16[128,1024]{1,0:T(8,128)(2,1)S(1)}, f32[3,1024]{1,0:T(4,128)}) custom-call(s32[2]{0:T(128)S(1)} %pad_add_fusion.place_ref, bf16[384,512]{1,0:T(8,128)(2,1)S(1)} %collective-permute-done.13.refs_0_.refs_4_, ...), custom_call_target="tpu_custom_call" | custom-call | flops 1610612736 | bytes 786432 | tf_op jit(solution)/shard_map/z_far/z_matmul/pallas_call | solution.py:130
  59.4 1.0 kernel_strip.1
  61.1 4.1 %all-to-all-start = ((f32[8,32,384]{2,1,0:T(8,128)}), f32[8,32,384]{2,1,0:T(8,128)}, u32[]{:S(2)}, u32[]{:S(2)}) async-start(f32[8,32,384]{2,1,0:T(8,128)} %bitcast.16), calls=%async_computation | async-start | bytes 786432 | tf_op jit(solution)/shard_map/kernel/all_to_all | solution.py:558
  65.3 2.5 %collective-permute-start.23 = (bf16[128,1024]{1,0:T(8,128)(2,1)}, bf16[128,1024]{1,0:T(8,128)(2,1)S(1)}, u32[]{:S(2)}, u32[]{:S(2)}) collective-permute-start(bf16[128,1024]{1,0:T(8,128)(2,1)} %copy-done.21), channel_id=1, source_target_pairs={{0,16},{16,24},{24,8},{8,0},{1,17},{17,25},{25,9},{9,1},{2,18},{18... | collective-permute-start | bytes 786440 | tf_op jit(solution)/shard_map/z_far/ppermute | solution.py:34
  68.5 2.2 %collective-permute-start.25 = (bf16[128,512]{1,0:T(8,128)(2,1)S(1)}, bf16[128,512]{1,0:T(8,128)(2,1)}, u32[]{:S(2)}, u32[]{:S(2)}) collective-permute-start(bf16[128,512]{1,0:T(8,128)(2,1)S(1)} %get-tuple-element.75), channel_id=1, source_target_pairs={{0,24},{16,8},{24,0},{8,16},{1,25},{17,9},{25,1},{9,17},{2,26},{18... | collective-permute-start | bytes 393224 | tf_op jit(solution)/shard_map/z_ring/ppermute | solution.py:34
  70.7 1.0 collective-permute-start.26
  71.8 5.7 %collective-permute-done.24.refs_8_ = bf16[128,512]{1,0:T(8,128)(2,1)} collective-permute-done((bf16[128,512]{1,0:T(8,128)(2,1)S(1)}, bf16[128,512]{1,0:T(8,128)(2,1)}, u32[]{:S(2)}, u32[]{:S(2)}) %collective-permute-start.24) | collective-permute-done | bytes 131104 | tf_op jit(solution)/shard_map/z_ring/ppermute | solution.py:34
  77.5 5.5 %collective-permute-done.25.refs_9_ = bf16[128,512]{1,0:T(8,128)(2,1)} collective-permute-done((bf16[128,512]{1,0:T(8,128)(2,1)S(1)}, bf16[128,512]{1,0:T(8,128)(2,1)}, u32[]{:S(2)}, u32[]{:S(2)}) %collective-permute-start.25) | collective-permute-done | bytes 131104 | tf_op jit(solution)/shard_map/z_ring/ppermute | solution.py:34
  83.0 5.0 %collective-permute-done.26.refs_10_ = bf16[128,512]{1,0:T(8,128)(2,1)} collective-permute-done((bf16[128,512]{1,0:T(8,128)(2,1)S(1)}, bf16[128,512]{1,0:T(8,128)(2,1)}, u32[]{:S(2)}, u32[]{:S(2)}) %collective-permute-start.26) | collective-permute-done | bytes 131104 | tf_op jit(solution)/shard_map/z_ring/ppermute | solution.py:34
  88.7 1.0 reduce_sum.65.own_ref
  89.8 8.5 %all_to_all.10.refs_0_ = bf16[4,32,384]{2,1,0:T(8,128)(2,1)S(1)} all-to-all(bf16[4,32,384]{2,1,0:T(8,128)(2,1)S(1)} %broadcast_in_dim.6), channel_id=1, replica_groups=mesh['batch'=4,'col'=8] {'batch'}, dimensions={0} | all-to-all | bytes 196608 | tf_op jit(solution)/shard_map/kernel/all_to_all | solution.py:565
  98.3 2.6 %collective-permute-start.32 = (bf16[4,32,384]{2,1,0:T(8,128)(2,1)S(1)}, bf16[4,32,384]{2,1,0:T(8,128)(2,1)S(1)}, u32[]{:S(2)}, u32[]{:S(2)}) collective-permute-start(bf16[4,32,384]{2,1,0:T(8,128)(2,1)S(1)} %all_to_all.10.refs_0_), channel_id=1, source_target_pairs={{0,6},{1,7},{2,4},{3,5},{4,2},{5,3},{6,0},{7,1},{8,14},{9,15},{10,... | collective-permute-start | bytes 294920 | tf_op jit(solution)/shard_map/kernel/ppermute | solution.py:24
  101.8 2.9 %collective-permute-done.32.refs_6_ = bf16[4,32,384]{2,1,0:T(8,128)(2,1)S(1)} collective-permute-done((bf16[4,32,384]{2,1,0:T(8,128)(2,1)S(1)}, bf16[4,32,384]{2,1,0:T(8,128)(2,1)S(1)}, u32[]{:S(2)}, u32[]{:S(2)}) %collective-permute-start.32) | collective-permute-done | bytes 98336 | tf_op jit(solution)/shard_map/kernel/ppermute | solution.py:24
  104.7 1.0 collective-permute-done.30.refs_4_
  115.0 4.7 %embedding_gradient.1 = (bf16[2,512,1024]{2,1,0:T(8,128)(2,1)S(1)}, f32[8,128]{1,0:T(8,128)S(1)}) custom-call(s32[2]{0:T(128)S(1)} %pad_add_fusion.place_ref, f32[32,384]{1,0:T(8,128)S(1)} %reduce_sum.65.own_ref, bf16[4,32,384]{2,1,0:T(8,128)(2,1)S(1)} %all_to_all.10.refs_0_, bf16[4,32,384]{2,1,0:T(8,128)(2,1)S(1)} %collective-permute-done.27.refs_1_, ...), custom_call_target="tpu_custom_call" | custom-call | flops 1073741824 | bytes 4194304 | tf_op jit(solution)/shard_map/dz/embedding_gradient/pallas_call | solution.py:257
  119.7 3.4 %copy-done.1 = bf16[4096,1024]{1,0:T(8,128)(2,1)S(1)} copy-done((bf16[4096,1024]{1,0:T(8,128)(2,1)S(1)}, bf16[4096,1024]{1,0:T(8,128)(2,1)}, u32[]{:S(2)}) %copy-start.1) | copy-done | bytes 8388632
  123.0 1.8 %d_act_matmul.2 = bf16[4,272,512]{2,1,0:T(8,128)(2,1)S(1)} custom-call(s32[2]{0:T(128)S(1)} %pad_add_fusion.place_ref, bf16[2,512,1024]{2,1,0:T(8,128)(2,1)S(1)} %get-tuple-element.79.dz_ref.refs_11_, f32[8,128]{1,0:T(8,128)S(1)} %get-tuple-element.80.share_ref, bf16[4096,1024]{1,0:T(8,128)(2,1)S(1)} %copy-done.1), custom_call_target="tpu_custom_call" | custom-call | flops 1073741824 | bytes 1048576 | tf_op jit(solution)/shard_map/d_act/d_act_matmul/pallas_call | solution.py:329
  125.5 2.3 %collective-permute-done.34.refs_0_ = bf16[4,272,512]{2,1,0:T(8,128)(2,1)S(1)} collective-permute-done((bf16[4,272,512]{2,1,0:T(8,128)(2,1)S(1)}, bf16[4,272,512]{2,1,0:T(8,128)(2,1)S(1)}, u32[]{:S(2)}, u32[]{:S(2)}) %collective-permute-start.34) | collective-permute-done | bytes 1114144 | tf_op jit(solution)/shard_map/d_act/ppermute | solution.py:24
  127.8 1.8 %d_act_matmul.3 = (bf16[272,512]{1,0:T(8,128)(2,1)S(1)}, bf16[272,512]{1,0:T(8,128)(2,1)S(1)}, bf16[272,512]{1,0:T(8,128)(2,1)S(1)}, f32[272,512]{1,0:T(8,128)S(1)}) custom-call(s32[2]{0:T(128)S(1)} %pad_add_fusion.place_ref, bf16[2,512,1024]{2,1,0:T(8,128)(2,1)S(1)} %get-tuple-element.79.dz_ref.refs_11_, f32[8,128]{1,0:T(8,128)S(1)} %get-tuple-element.80.share_ref, ...), custom_call_target="tpu_custom_call" | custom-call | flops 1073741824 | bytes 1048576 | tf_op jit(solution)/shard_map/d_act/d_act_matmul/pallas_call | solution.py:329
  130.4 1.2 collective-permute-start.36
  131.7 1.6 %collective-permute-start.37 = (bf16[272,512]{1,0:T(8,128)(2,1)S(1)}, bf16[272,512]{1,0:T(8,128)(2,1)S(1)}, u32[]{:S(2)}, u32[]{:S(2)}) collective-permute-start(bf16[272,512]{1,0:T(8,128)(2,1)S(1)} %get-tuple-element.83), channel_id=1, source_target_pairs={{0,6},{1,7},{2,4},{3,5},{4,2},{5,3},{6,0},{7,1},{8,14},{9,15},{10,... | collective-permute-start | bytes 835592 | tf_op jit(solution)/shard_map/d_act/ppermute | solution.py:24
  133.8 3.4 %weight_gradient.2.refs_12_ = f32[1024,1024]{1,0:T(8,128)} custom-call(s32[2]{0:T(128)S(1)} %pad_add_fusion.place_ref, bf16[256,512]{1,0:T(8,128)(2,1)S(1)} %bitcast.15, bf16[256,512]{1,0:T(8,128)(2,1)S(1)} %collective-permute-done.3.refs_0_.refs_1_, bf16[256,512]{1,0:T(8,128)(2,1)S(1)} %collective-permute-done.5.refs_1_.refs_2_, ...), custom_call_target="tpu_custom_call" | custom-call | flops 1073741824 | bytes 2097152 | tf_op jit(solution)/shard_map/grad_weight/weight_gradient/pallas_call | solution.py:436
  137.3 2.9 %weight_gradient.3 = f32[1024,1024]{1,0:T(8,128)} custom-call(s32[2]{0:T(128)S(1)} %pad_add_fusion.place_ref, bf16[256,512]{1,0:T(8,128)(2,1)S(1)} %copy-done.8, bf16[256,512]{1,0:T(8,128)(2,1)S(1)} %copy-done.14, bf16[256,512]{1,0:T(8,128)(2,1)S(1)} %copy-done.12, bf16[256,512]{1,0:T(8,128)(2,1)S(1)} %copy-done.10, ...), custom_call_target="tpu_custom_call", output_to_operand_aliasing={{}: (13, {})} | custom-call | flops 1073741824 | bytes 2097152 | tf_op jit(solution)/shard_map/grad_weight/weight_gradient/pallas_call | solution.py:436
  140.2 5.1 %collective-permute-done.37 = bf16[272,512]{1,0:T(8,128)(2,1)S(1)} collective-permute-done((bf16[272,512]{1,0:T(8,128)(2,1)S(1)}, bf16[272,512]{1,0:T(8,128)(2,1)S(1)}, u32[]{:S(2)}, u32[]{:S(2)}) %collective-permute-start.37) | collective-permute-done | bytes 278560 | tf_op jit(solution)/shard_map/d_act/ppermute | solution.py:24
  146.8 2.6 %collective-permute-start.43 = (f32[8,512]{1,0:T(8,128)S(1)}, f32[8,512]{1,0:T(8,128)S(1)}, u32[]{:S(2)}, u32[]{:S(2)}) collective-permute-start(f32[8,512]{1,0:T(8,128)S(1)} %pad_maximum_fusion), channel_id=1, source_target_pairs={{0,24},{8,16},{16,8},{24,0},{1,25},{9,17},{17,9},{25,1},{2,26},{10... | collective-permute-start | bytes 49160 | tf_op jit(solution)/shard_map/norm_backward/ppermute | solution.py:24
  149.5 1.1 collective-permute-done.42
  150.6 1.7 %collective-permute-done.43 = f32[8,512]{1,0:T(8,128)S(1)} collective-permute-done((f32[8,512]{1,0:T(8,128)S(1)}, f32[8,512]{1,0:T(8,128)S(1)}, u32[]{:S(2)}, u32[]{:S(2)}) %collective-permute-start.43) | collective-permute-done | bytes 16416 | tf_op jit(solution)/shard_map/norm_backward/ppermute | solution.py:24
  154.4 1.0 fusion.22
  (150 shorter events, 24.8 us)
Async XLA Ops:
  2.8 9.3 %collective-permute-start.2 = (f32[4,512]{1,0:T(4,128)S(1)}, f32[4,512]{1,0:T(4,128)S(1)}, u32[]{:S(2)}, u32[]{:S(2)}) collective-permute-start(f32[4,512]{1,0:T(4,128)S(1)} %pad_maximum_fusion.1), channel_id=1, source_target_pairs={{0,24},{8,16},{16,8},{24,0},{1,25},{9,17},{17,9},{25,1},{2,26},{10... | collective-permute-start | bytes 24584 | tf_op jit(solution)/shard_map/norm_stats/ppermute | solution.py:24
  7.9 4.5 %collective-permute-start.1 = (f32[4,512]{1,0:T(4,128)S(1)}, f32[4,512]{1,0:T(4,128)S(1)}, u32[]{:S(2)}, u32[]{:S(2)}) collective-permute-start(f32[4,512]{1,0:T(4,128)S(1)} %pad_maximum_fusion.1), channel_id=1, source_target_pairs={{0,16},{8,24},{16,0},{24,8},{1,17},{9,25},{17,1},{25,9},{2,18},{10... | collective-permute-start | bytes 24584 | tf_op jit(solution)/shard_map/norm_stats/ppermute | solution.py:24
  7.9 4.5 %collective-permute-start = (f32[4,512]{1,0:T(4,128)S(1)}, f32[4,512]{1,0:T(4,128)S(1)}, u32[]{:S(2)}, u32[]{:S(2)}) collective-permute-start(f32[4,512]{1,0:T(4,128)S(1)} %pad_maximum_fusion.1), channel_id=1, source_target_pairs={{0,8},{8,0},{16,24},{24,16},{1,9},{9,1},{17,25},{25,17},{2,10},{10... | collective-permute-start | bytes 24584 | tf_op jit(solution)/shard_map/norm_stats/ppermute | solution.py:24
  12.1 44.2 %copy-start = (bf16[4096,1024]{1,0:T(8,128)(2,1)}, bf16[4096,1024]{1,0:T(8,128)(2,1)S(1)}, u32[]{:S(2)}) copy-start(bf16[4096,1024]{1,0:T(8,128)(2,1)S(1)} %get-tuple-element.55.refs_2_.refs_3_.refs_4_.w_ref) | copy-start | bytes 25165828
  12.8 3.6 %collective-permute-start.9 = (bf16[256,512]{1,0:T(8,128)(2,1)S(1)}, bf16[256,512]{1,0:T(8,128)(2,1)S(1)}, u32[]{:S(2)}, u32[]{:S(2)}) collective-permute-start(bf16[256,512]{1,0:T(8,128)(2,1)S(1)} %bitcast.9), channel_id=1, source_target_pairs={{0,1},{1,0},{2,3},{3,2},{4,5},{5,4},{6,7},{7,6},{8,9},{9,8},{10,11... | collective-permute-start | bytes 786440 | tf_op jit(solution)/shard_map/act_gather/ppermute | solution.py:24
  12.9 10.1 %collective-permute-start.7 = (bf16[256,512]{1,0:T(8,128)(2,1)S(1)}, bf16[256,512]{1,0:T(8,128)(2,1)S(1)}, u32[]{:S(2)}, u32[]{:S(2)}) collective-permute-start(bf16[256,512]{1,0:T(8,128)(2,1)S(1)} %bitcast.10), channel_id=1, source_target_pairs={{0,6},{1,7},{2,4},{3,5},{4,2},{5,3},{6,0},{7,1},{8,14},{9,15},{10,... | collective-permute-start | bytes 786440 | tf_op jit(solution)/shard_map/act_gather/ppermute | solution.py:24
  15.4 12.7 %collective-permute-start.5 = (bf16[256,512]{1,0:T(8,128)(2,1)S(1)}, bf16[256,512]{1,0:T(8,128)(2,1)S(1)}, u32[]{:S(2)}, u32[]{:S(2)}) collective-permute-start(bf16[256,512]{1,0:T(8,128)(2,1)S(1)} %bitcast.11), channel_id=1, source_target_pairs={{0,4},{1,5},{2,6},{3,7},{4,0},{5,1},{6,2},{7,3},{8,12},{9,13},{10,... | collective-permute-start | bytes 786440 | tf_op jit(solution)/shard_map/act_gather/ppermute | solution.py:24
  15.9 12.3 %collective-permute-start.3 = (bf16[256,512]{1,0:T(8,128)(2,1)S(1)}, bf16[256,512]{1,0:T(8,128)(2,1)S(1)}, u32[]{:S(2)}, u32[]{:S(2)}) collective-permute-start(bf16[256,512]{1,0:T(8,128)(2,1)S(1)} %bitcast.12), channel_id=1, source_target_pairs={{0,2},{1,3},{2,0},{3,1},{4,6},{5,7},{6,4},{7,5},{8,10},{9,11},{10,... | collective-permute-start | bytes 786440 | tf_op jit(solution)/shard_map/act_gather/ppermute | solution.py:24
  16.5 12.2 %collective-permute-start.10 = (bf16[128,512]{1,0:T(8,128)(2,1)S(1)}, bf16[128,512]{1,0:T(8,128)(2,1)S(1)}, u32[]{:S(2)}, u32[]{:S(2)}) collective-permute-start(bf16[128,512]{1,0:T(8,128)(2,1)S(1)} %slice_bitcast_fusion), channel_id=1, source_target_pairs={{0,16},{16,24},{24,8},{8,0},{1,17},{17,25},{25,9},{9,1},{2,18},{18... | collective-permute-start | bytes 393224 | tf_op jit(solution)/shard_map/act_gather/ppermute | solution.py:34
  18.5 10.2 %collective-permute-start.11 = (bf16[128,512]{1,0:T(8,128)(2,1)S(1)}, bf16[128,512]{1,0:T(8,128)(2,1)S(1)}, u32[]{:S(2)}, u32[]{:S(2)}) collective-permute-start(bf16[128,512]{1,0:T(8,128)(2,1)S(1)} %slice_bitcast_fusion), channel_id=1, source_target_pairs={{0,24},{16,8},{24,0},{8,16},{1,25},{17,9},{25,1},{9,17},{2,26},{18... | collective-permute-start | bytes 393224 | tf_op jit(solution)/shard_map/act_gather/ppermute | solution.py:34
  23.0 8.6 %collective-permute-start.12 = (bf16[128,512]{1,0:T(8,128)(2,1)S(1)}, bf16[128,512]{1,0:T(8,128)(2,1)S(1)}, u32[]{:S(2)}, u32[]{:S(2)}) collective-permute-start(bf16[128,512]{1,0:T(8,128)(2,1)S(1)} %slice_bitcast_fusion), channel_id=1, source_target_pairs={{0,8},{16,0},{24,16},{8,24},{1,9},{17,1},{25,17},{9,25},{2,10},{18... | collective-permute-start | bytes 393224 | tf_op jit(solution)/shard_map/act_gather/ppermute | solution.py:34
  28.1 7.6 %collective-permute-start.8 = (bf16[256,512]{1,0:T(8,128)(2,1)S(1)}, bf16[256,512]{1,0:T(8,128)(2,1)S(1)}, u32[]{:S(2)}, u32[]{:S(2)}) collective-permute-start(bf16[256,512]{1,0:T(8,128)(2,1)S(1)} %collective-permute-done.7.refs_2_.refs_3_), channel_id=1, source_target_pairs={{0,1},{1,0},{2,3},{3,2},{4,5},{5,4},{6,7},{7,6},{8,9},{9,8},{10,11... | collective-permute-start | bytes 786440 | tf_op jit(solution)/shard_map/act_gather/ppermute | solution.py:24
  28.2 7.5 %collective-permute-start.6 = (bf16[256,512]{1,0:T(8,128)(2,1)S(1)}, bf16[256,512]{1,0:T(8,128)(2,1)S(1)}, u32[]{:S(2)}, u32[]{:S(2)}) collective-permute-start(bf16[256,512]{1,0:T(8,128)(2,1)S(1)} %collective-permute-done.5.refs_1_.refs_2_), channel_id=1, source_target_pairs={{0,1},{1,0},{2,3},{3,2},{4,5},{5,4},{6,7},{7,6},{8,9},{9,8},{10,11... | collective-permute-start | bytes 786440 | tf_op jit(solution)/shard_map/act_gather/ppermute | solution.py:24
  28.6 7.1 %collective-permute-start.4 = (bf16[256,512]{1,0:T(8,128)(2,1)S(1)}, bf16[256,512]{1,0:T(8,128)(2,1)S(1)}, u32[]{:S(2)}, u32[]{:S(2)}) collective-permute-start(bf16[256,512]{1,0:T(8,128)(2,1)S(1)} %collective-permute-done.3.refs_0_.refs_1_), channel_id=1, source_target_pairs={{0,1},{1,0},{2,3},{3,2},{4,5},{5,4},{6,7},{7,6},{8,9},{9,8},{10,11... | collective-permute-start | bytes 786440 | tf_op jit(solution)/shard_map/act_gather/ppermute | solution.py:24
  31.6 13.0 %collective-permute-start.15 = (bf16[384,512]{1,0:T(8,128)(2,1)S(1)}, bf16[384,512]{1,0:T(8,128)(2,1)S(1)}, u32[]{:S(2)}, u32[]{:S(2)}) collective-permute-start(bf16[384,512]{1,0:T(8,128)(2,1)S(1)} %constant_dynamic-update-slice_fusion.refs_0_.refs_4_), channel_id=1, source_target_pairs={{0,6},{1,7},{2,4},{3,5},{4,2},{5,3},{6,0},{7,1},{8,14},{9,15},{10,... | collective-permute-start | bytes 1179656 | tf_op jit(solution)/shard_map/act_gather/ppermute | solution.py:24
  37.3 22.0 %copy-start.15 = (bf16[128,1024]{1,0:T(8,128)(2,1)}, bf16[128,1024]{1,0:T(8,128)(2,1)S(1)}, u32[]{:S(2)}) copy-start(bf16[128,1024]{1,0:T(8,128)(2,1)S(1)} %get-tuple-element.57.refs_0_.refs_8_) | copy-start | bytes 786436
  37.4 22.0 %copy-start.17 = (bf16[128,1024]{1,0:T(8,128)(2,1)}, bf16[128,1024]{1,0:T(8,128)(2,1)S(1)}, u32[]{:S(2)}) copy-start(bf16[128,1024]{1,0:T(8,128)(2,1)S(1)} %get-tuple-element.59.refs_4_.refs_9_) | copy-start | bytes 786436
  37.4 8.0 %collective-permute-start.14 = (bf16[128,1024]{1,0:T(8,128)(2,1)S(1)}, bf16[128,1024]{1,0:T(8,128)(2,1)S(1)}, u32[]{:S(2)}, u32[]{:S(2)}) collective-permute-start(bf16[128,1024]{1,0:T(8,128)(2,1)S(1)} %get-tuple-element.59.refs_4_.refs_9_), channel_id=1, source_target_pairs={{0,16},{16,24},{24,8},{8,0},{1,17},{17,25},{25,9},{9,1},{2,18},{18... | collective-permute-start | bytes 786440 | tf_op jit(solution)/shard_map/z_ring/ppermute | solution.py:34
  37.4 14.6 %collective-permute-start.19 = (bf16[384,512]{1,0:T(8,128)(2,1)S(1)}, bf16[384,512]{1,0:T(8,128)(2,1)S(1)}, u32[]{:S(2)}, u32[]{:S(2)}) collective-permute-start(bf16[384,512]{1,0:T(8,128)(2,1)S(1)} %constant_dynamic-update-slice_fusion.refs_0_.refs_4_), channel_id=1, source_target_pairs={{0,4},{1,5},{2,6},{3,7},{4,0},{5,1},{6,2},{7,3},{8,12},{9,13},{10,... | collective-permute-start | bytes 1179656 | tf_op jit(solution)/shard_map/act_gather/ppermute | solution.py:24
  38.0 15.6 %collective-permute-start.16 = (bf16[384,512]{1,0:T(8,128)(2,1)S(1)}, bf16[384,512]{1,0:T(8,128)(2,1)S(1)}, u32[]{:S(2)}, u32[]{:S(2)}) collective-permute-start(bf16[384,512]{1,0:T(8,128)(2,1)S(1)} %constant_dynamic-update-slice_fusion.refs_0_.refs_4_), channel_id=1, source_target_pairs={{0,2},{1,3},{2,0},{3,1},{4,6},{5,7},{6,4},{7,5},{8,10},{9,11},{10,... | collective-permute-start | bytes 1179656 | tf_op jit(solution)/shard_map/act_gather/ppermute | solution.py:24
  45.4 8.2 %collective-permute-start.17 = (bf16[128,1024]{1,0:T(8,128)(2,1)S(1)}, bf16[128,1024]{1,0:T(8,128)(2,1)S(1)}, u32[]{:S(2)}, u32[]{:S(2)}) collective-permute-start(bf16[128,1024]{1,0:T(8,128)(2,1)S(1)} %collective-permute-done.14.refs_5_.refs_11_), channel_id=1, source_target_pairs={{0,16},{16,24},{24,8},{8,0},{1,17},{17,25},{25,9},{9,1},{2,18},{18... | collective-permute-start | bytes 786440 | tf_op jit(solution)/shard_map/z_ring/ppermute | solution.py:34
  46.6 9.7 %collective-permute-start.13 = (bf16[384,512]{1,0:T(8,128)(2,1)S(1)}, bf16[384,512]{1,0:T(8,128)(2,1)S(1)}, u32[]{:S(2)}, u32[]{:S(2)}) collective-permute-start(bf16[384,512]{1,0:T(8,128)(2,1)S(1)} %constant_dynamic-update-slice_fusion.refs_0_.refs_4_), channel_id=1, source_target_pairs={{0,1},{1,0},{2,3},{3,2},{4,5},{5,4},{6,7},{7,6},{8,9},{9,8},{10,11... | collective-permute-start | bytes 1179656 | tf_op jit(solution)/shard_map/z_far/ppermute | solution.py:24
  46.6 9.7 %collective-permute-start.21 = (bf16[384,512]{1,0:T(8,128)(2,1)S(1)}, bf16[384,512]{1,0:T(8,128)(2,1)S(1)}, u32[]{:S(2)}, u32[]{:S(2)}) collective-permute-start(bf16[384,512]{1,0:T(8,128)(2,1)S(1)} %collective-permute-done.15.refs_1_.refs_7_), channel_id=1, source_target_pairs={{0,1},{1,0},{2,3},{3,2},{4,5},{5,4},{6,7},{7,6},{8,9},{9,8},{10,11... | collective-permute-start | bytes 1179656 | tf_op jit(solution)/shard_map/z_far/ppermute | solution.py:24
  52.0 4.2 %collective-permute-start.20 = (bf16[384,512]{1,0:T(8,128)(2,1)S(1)}, bf16[384,512]{1,0:T(8,128)(2,1)S(1)}, u32[]{:S(2)}, u32[]{:S(2)}) collective-permute-start(bf16[384,512]{1,0:T(8,128)(2,1)S(1)} %collective-permute-done.19.refs_1_.refs_6_), channel_id=1, source_target_pairs={{0,1},{1,0},{2,3},{3,2},{4,5},{5,4},{6,7},{7,6},{8,9},{9,8},{10,11... | collective-permute-start | bytes 1179656 | tf_op jit(solution)/shard_map/z_far/ppermute | solution.py:24
  53.6 2.6 %collective-permute-start.18 = (bf16[384,512]{1,0:T(8,128)(2,1)S(1)}, bf16[384,512]{1,0:T(8,128)(2,1)S(1)}, u32[]{:S(2)}, u32[]{:S(2)}) collective-permute-start(bf16[384,512]{1,0:T(8,128)(2,1)S(1)} %collective-permute-done.16.refs_0_.refs_5_), channel_id=1, source_target_pairs={{0,1},{1,0},{2,3},{3,2},{4,5},{5,4},{6,7},{7,6},{8,9},{9,8},{10,11... | collective-permute-start | bytes 1179656 | tf_op jit(solution)/shard_map/z_far/ppermute | solution.py:24
  54.2 5.1 %collective-permute-start.22 = (f32[2,1024]{1,0:T(2,128)S(1)}, f32[2,1024]{1,0:T(2,128)S(1)}, u32[]{:S(2)}, u32[]{:S(2)}) collective-permute-start(f32[2,1024]{1,0:T(2,128)S(1)} %get-tuple-element.69), channel_id=1, source_target_pairs={{0,8},{16,0},{24,16},{8,24},{1,9},{17,1},{25,17},{9,25},{2,10},{18... | collective-permute-start | bytes 24584 | tf_op jit(solution)/shard_map/z_ring/ppermute | solution.py:34
  61.1 27.6 %all-to-all-start = ((f32[8,32,384]{2,1,0:T(8,128)}), f32[8,32,384]{2,1,0:T(8,128)}, u32[]{:S(2)}, u32[]{:S(2)}) async-start(f32[8,32,384]{2,1,0:T(8,128)} %bitcast.16), calls=%async_computation | async-start | bytes 786432 | tf_op jit(solution)/shard_map/kernel/all_to_all | solution.py:558
  65.3 22.7 %collective-permute-start.23 = (bf16[128,1024]{1,0:T(8,128)(2,1)}, bf16[128,1024]{1,0:T(8,128)(2,1)S(1)}, u32[]{:S(2)}, u32[]{:S(2)}) collective-permute-start(bf16[128,1024]{1,0:T(8,128)(2,1)} %copy-done.21), channel_id=1, source_target_pairs={{0,16},{16,24},{24,8},{8,0},{1,17},{17,25},{25,9},{9,1},{2,18},{18... | collective-permute-start | bytes 786440 | tf_op jit(solution)/shard_map/z_far/ppermute | solution.py:34
  68.4 9.1 %collective-permute-start.24 = (bf16[128,512]{1,0:T(8,128)(2,1)S(1)}, bf16[128,512]{1,0:T(8,128)(2,1)}, u32[]{:S(2)}, u32[]{:S(2)}) collective-permute-start(bf16[128,512]{1,0:T(8,128)(2,1)S(1)} %get-tuple-element.74), channel_id=1, source_target_pairs={{0,16},{16,24},{24,8},{8,0},{1,17},{17,25},{25,9},{9,1},{2,18},{18... | collective-permute-start | bytes 393224 | tf_op jit(solution)/shard_map/z_ring/ppermute | solution.py:34
  68.5 14.5 %collective-permute-start.25 = (bf16[128,512]{1,0:T(8,128)(2,1)S(1)}, bf16[128,512]{1,0:T(8,128)(2,1)}, u32[]{:S(2)}, u32[]{:S(2)}) collective-permute-start(bf16[128,512]{1,0:T(8,128)(2,1)S(1)} %get-tuple-element.75), channel_id=1, source_target_pairs={{0,24},{16,8},{24,0},{8,16},{1,25},{17,9},{25,1},{9,17},{2,26},{18... | collective-permute-start | bytes 393224 | tf_op jit(solution)/shard_map/z_ring/ppermute | solution.py:34
  70.7 17.3 %collective-permute-start.26 = (bf16[128,512]{1,0:T(8,128)(2,1)S(1)}, bf16[128,512]{1,0:T(8,128)(2,1)}, u32[]{:S(2)}, u32[]{:S(2)}) collective-permute-start(bf16[128,512]{1,0:T(8,128)(2,1)S(1)} %get-tuple-element.76), channel_id=1, source_target_pairs={{0,8},{16,0},{24,16},{8,24},{1,9},{17,1},{25,17},{9,25},{2,10},{18... | collective-permute-start | bytes 393224 | tf_op jit(solution)/shard_map/z_ring/ppermute | solution.py:34
  98.3 6.3 %collective-permute-start.32 = (bf16[4,32,384]{2,1,0:T(8,128)(2,1)S(1)}, bf16[4,32,384]{2,1,0:T(8,128)(2,1)S(1)}, u32[]{:S(2)}, u32[]{:S(2)}) collective-permute-start(bf16[4,32,384]{2,1,0:T(8,128)(2,1)S(1)} %all_to_all.10.refs_0_), channel_id=1, source_target_pairs={{0,6},{1,7},{2,4},{3,5},{4,2},{5,3},{6,0},{7,1},{8,14},{9,15},{10,... | collective-permute-start | bytes 294920 | tf_op jit(solution)/shard_map/kernel/ppermute | solution.py:24
  100.9 4.7 %collective-permute-start.30 = (bf16[4,32,384]{2,1,0:T(8,128)(2,1)S(1)}, bf16[4,32,384]{2,1,0:T(8,128)(2,1)S(1)}, u32[]{:S(2)}, u32[]{:S(2)}) collective-permute-start(bf16[4,32,384]{2,1,0:T(8,128)(2,1)S(1)} %all_to_all.10.refs_0_), channel_id=1, source_target_pairs={{0,4},{1,5},{2,6},{3,7},{4,0},{5,1},{6,2},{7,3},{8,12},{9,13},{10,... | collective-permute-start | bytes 294920 | tf_op jit(solution)/shard_map/kernel/ppermute | solution.py:24
  101.5 4.6 %collective-permute-start.28 = (bf16[4,32,384]{2,1,0:T(8,128)(2,1)S(1)}, bf16[4,32,384]{2,1,0:T(8,128)(2,1)S(1)}, u32[]{:S(2)}, u32[]{:S(2)}) collective-permute-start(bf16[4,32,384]{2,1,0:T(8,128)(2,1)S(1)} %all_to_all.10.refs_0_), channel_id=1, source_target_pairs={{0,2},{1,3},{2,0},{3,1},{4,6},{5,7},{6,4},{7,5},{8,10},{9,11},{10,... | collective-permute-start | bytes 294920 | tf_op jit(solution)/shard_map/kernel/ppermute | solution.py:24
  101.8 4.3 %collective-permute-start.27 = (bf16[4,32,384]{2,1,0:T(8,128)(2,1)S(1)}, bf16[4,32,384]{2,1,0:T(8,128)(2,1)S(1)}, u32[]{:S(2)}, u32[]{:S(2)}) collective-permute-start(bf16[4,32,384]{2,1,0:T(8,128)(2,1)S(1)} %all_to_all.10.refs_0_), channel_id=1, source_target_pairs={{0,1},{1,0},{2,3},{3,2},{4,5},{5,4},{6,7},{7,6},{8,9},{9,8},{10,11... | collective-permute-start | bytes 294920 | tf_op jit(solution)/shard_map/kernel/ppermute | solution.py:24
  104.7 1.5 collective-permute-start.33
  105.6 1.3 collective-permute-start.31
  106.1 1.3 collective-permute-start.29
  124.9 2.9 %collective-permute-start.34 = (bf16[4,272,512]{2,1,0:T(8,128)(2,1)S(1)}, bf16[4,272,512]{2,1,0:T(8,128)(2,1)S(1)}, u32[]{:S(2)}, u32[]{:S(2)}) collective-permute-start(bf16[4,272,512]{2,1,0:T(8,128)(2,1)S(1)} %d_act_matmul.2), channel_id=1, source_target_pairs={{0,1},{1,0},{2,3},{3,2},{4,5},{5,4},{6,7},{7,6},{8,9},{9,8},{10,11... | collective-permute-start | bytes 3342344 | tf_op jit(solution)/shard_map/d_act/ppermute | solution.py:24
  125.1 8.2 %collective-permute-start.38 = (bf16[128,512]{1,0:T(8,128)(2,1)}, bf16[128,512]{1,0:T(8,128)(2,1)S(1)}, u32[]{:S(2)}, u32[]{:S(2)}) collective-permute-start(bf16[128,512]{1,0:T(8,128)(2,1)} %collective-permute-done.24.refs_8_), channel_id=1, source_target_pairs={{0,1},{1,0},{2,3},{3,2},{4,5},{5,4},{6,7},{7,6},{8,9},{9,8},{10,11... | collective-permute-start | bytes 393224 | tf_op jit(solution)/shard_map/grad_weight/ppermute | solution.py:24
  129.6 10.5 %collective-permute-start.35 = (bf16[272,512]{1,0:T(8,128)(2,1)S(1)}, bf16[272,512]{1,0:T(8,128)(2,1)S(1)}, u32[]{:S(2)}, u32[]{:S(2)}) collective-permute-start(bf16[272,512]{1,0:T(8,128)(2,1)S(1)} %get-tuple-element.81), channel_id=1, source_target_pairs={{0,2},{1,3},{2,0},{3,1},{4,6},{5,7},{6,4},{7,5},{8,10},{9,11},{10,... | collective-permute-start | bytes 835592 | tf_op jit(solution)/shard_map/d_act/ppermute | solution.py:24
  130.4 9.7 %collective-permute-start.36 = (bf16[272,512]{1,0:T(8,128)(2,1)S(1)}, bf16[272,512]{1,0:T(8,128)(2,1)S(1)}, u32[]{:S(2)}, u32[]{:S(2)}) collective-permute-start(bf16[272,512]{1,0:T(8,128)(2,1)S(1)} %get-tuple-element.82), channel_id=1, source_target_pairs={{0,4},{1,5},{2,6},{3,7},{4,0},{5,1},{6,2},{7,3},{8,12},{9,13},{10,... | collective-permute-start | bytes 835592 | tf_op jit(solution)/shard_map/d_act/ppermute | solution.py:24
  131.7 13.6 %collective-permute-start.37 = (bf16[272,512]{1,0:T(8,128)(2,1)S(1)}, bf16[272,512]{1,0:T(8,128)(2,1)S(1)}, u32[]{:S(2)}, u32[]{:S(2)}) collective-permute-start(bf16[272,512]{1,0:T(8,128)(2,1)S(1)} %get-tuple-element.83), channel_id=1, source_target_pairs={{0,6},{1,7},{2,4},{3,5},{4,2},{5,3},{6,0},{7,1},{8,14},{9,15},{10,... | collective-permute-start | bytes 835592 | tf_op jit(solution)/shard_map/d_act/ppermute | solution.py:24
  133.3 3.9 %collective-permute-start.39 = (bf16[128,512]{1,0:T(8,128)(2,1)}, bf16[128,512]{1,0:T(8,128)(2,1)S(1)}, u32[]{:S(2)}, u32[]{:S(2)}) collective-permute-start(bf16[128,512]{1,0:T(8,128)(2,1)} %collective-permute-done.25.refs_9_), channel_id=1, source_target_pairs={{0,1},{1,0},{2,3},{3,2},{4,5},{5,4},{6,7},{7,6},{8,9},{9,8},{10,11... | collective-permute-start | bytes 393224 | tf_op jit(solution)/shard_map/grad_weight/ppermute | solution.py:24
  133.3 3.9 %collective-permute-start.40 = (bf16[128,512]{1,0:T(8,128)(2,1)}, bf16[128,512]{1,0:T(8,128)(2,1)S(1)}, u32[]{:S(2)}, u32[]{:S(2)}) collective-permute-start(bf16[128,512]{1,0:T(8,128)(2,1)} %collective-permute-done.26.refs_10_), channel_id=1, source_target_pairs={{0,1},{1,0},{2,3},{3,2},{4,5},{5,4},{6,7},{7,6},{8,9},{9,8},{10,11... | collective-permute-start | bytes 393224 | tf_op jit(solution)/shard_map/grad_weight/ppermute | solution.py:24
  145.9 4.7 %collective-permute-start.42 = (f32[8,512]{1,0:T(8,128)S(1)}, f32[8,512]{1,0:T(8,128)S(1)}, u32[]{:S(2)}, u32[]{:S(2)}) collective-permute-start(f32[8,512]{1,0:T(8,128)S(1)} %pad_maximum_fusion), channel_id=1, source_target_pairs={{0,16},{8,24},{16,0},{24,8},{1,17},{9,25},{17,1},{25,9},{2,18},{10... | collective-permute-start | bytes 49160 | tf_op jit(solution)/shard_map/norm_backward/ppermute | solution.py:24
  146.8 5.5 %collective-permute-start.43 = (f32[8,512]{1,0:T(8,128)S(1)}, f32[8,512]{1,0:T(8,128)S(1)}, u32[]{:S(2)}, u32[]{:S(2)}) collective-permute-start(f32[8,512]{1,0:T(8,128)S(1)} %pad_maximum_fusion), channel_id=1, source_target_pairs={{0,24},{8,16},{16,8},{24,0},{1,25},{9,17},{17,9},{25,1},{2,26},{10... | collective-permute-start | bytes 49160 | tf_op jit(solution)/shard_map/norm_backward/ppermute | solution.py:24
  149.4 3.7 %collective-permute-start.41 = (f32[8,512]{1,0:T(8,128)S(1)}, f32[8,512]{1,0:T(8,128)S(1)}, u32[]{:S(2)}, u32[]{:S(2)}) collective-permute-start(f32[8,512]{1,0:T(8,128)S(1)} %pad_maximum_fusion), channel_id=1, source_target_pairs={{0,8},{8,0},{16,24},{24,16},{1,9},{9,1},{17,25},{25,17},{2,10},{10... | collective-permute-start | bytes 49160 | tf_op jit(solution)/shard_map/norm_backward/ppermute | solution.py:24
  (32 other events, 121.7 us)

commit v9 on v7

--- a/solution.py
+++ b/solution.py
@@ -372,56 +372,92 @@
     )(place, *pieces)
 
 
-def weight_grad_kernel(n_far, aliased, half, tile, which, place_ref, *refs):
-    near = [refs[:half], refs[half : 2 * half]]
-    arrived = refs[2 * half : 2 * half + n_far]
-    dz_ref = refs[2 * half + n_far]
-    out_ref, act, product, sems = refs[2 * half + n_far + 1 + aliased :]
-    block, parity = which
-    chosen = held_place(place_ref[0], place_ref[1], block, 2 * half, n_far + 1)
-    out_row = 2 * block + ((place_ref[1] & 1) ^ parity)
-    local_rows = near[0][0].shape[0] // 2
-    rows = dz_ref.shape[1]
+def rows_product(act, dz, width, tile, write):
+    for i in range(width // tile):
+        write(
+            i,
+            lax.dot_general(
+                act[:, pl.ds(i * tile, tile)],
+                dz[...],
+                (((0,), (0,)), ((), ())),
+                preferred_element_type=f32,
+            ),
+        )
+
+
+def weight_grad_kernel(n_batch, half, tile, block, place_ref, *refs):
+    own, far = refs[:half], refs[half : 2 * half]
+    dz_ref, out_ref, act = refs[2 * half :]
+    local_rows = own[0].shape[0] // 2
+    chosen = held_place(place_ref[0], place_ref[1], block, 2 * half, n_batch)
     for e in range(half):
 
         @pl.when(chosen == e)
         def _():
-            act[pl.ds(0, local_rows)] = near[0][e][:local_rows]
-            act[pl.ds(rows, local_rows)] = near[0][e][local_rows:]
-            act[pl.ds(local_rows, rows - local_rows)] = near[1][e][...]
-
-    for s in range(n_far):
-        act[pl.ds(rows + (s + 1) * local_rows, local_rows)] = arrived[s][...]
+            act[:local_rows] = own[e][:local_rows]
+            act[local_rows:] = far[e][...]
+
+    def write(i, product):
+        out_ref[pl.ds(i * tile, tile)] = product
+
+    rows_product(act, dz_ref.at[0], act.shape[1], tile, write)
+
+
+def weight_grad_call(place, n_batch, block, own, far, dz):
+    width = own[0].shape[1]
+    _, rows, columns = dz.shape
+    tile = min(256, width)
+    operands = [place] + list(own) + list(far) + [dz]
+    return pl.pallas_call(
+        functools.partial(weight_grad_kernel, n_batch, len(own), tile, block),
+        out_shape=jax.ShapeDtypeStruct((width, columns), f32),
+        in_specs=[IN_SMEM] + [IN_VMEM] * (len(operands) - 1),
+        out_specs=IN_VMEM,
+        scratch_shapes=[pltpu.VMEM((rows, width), bf16)],
+        compiler_params=params(8),
+        cost_estimate=cost(2 * rows * width * columns, 2 * rows * columns),
+        name="weight_gradient_0",
+    )(*operands)
+
+
+def weight_grad_last_kernel(n_batch, half, tile, aliased, which, place_ref, *refs):
+    own, blocks = refs[:half], refs[half : half + n_batch - 1]
+    dz_ref, before_ref = refs[half + n_batch - 1 : half + n_batch + 1]
+    out_ref, act, product, sems = refs[half + n_batch + 1 + aliased :]
+    local_rows = own[0].shape[0] // 2
+    block, parity = which
+    chosen = held_place(place_ref[0], place_ref[1], block, 2 * half, n_batch)
+    out_row = 2 * block + ((place_ref[1] & 1) ^ parity)
+    for e in range(half):
+
+        @pl.when(chosen == e)
+        def _():
+            act[:local_rows] = own[e][local_rows:]
+
+    for s in range(n_batch - 1):
+        act[pl.ds((s + 1) * local_rows, local_rows)] = blocks[s][...]
     width = act.shape[1]
     copies = []
-    for i in range(width // tile):
-        total = None
-        for v in range(2):
-            part = lax.dot_general(
-                act[pl.ds(v * rows, rows), pl.ds(i * tile, tile)],
-                dz_ref[v],
-                (((0,), (0,)), ((), ())),
-                preferred_element_type=f32,
-            )
-            total = part if total is None else total + part
-        product[pl.ds(i * tile, tile)] = total
+
+    def write(i, part):
+        here = pl.ds(i * tile, tile)
+        product[here] = before_ref[here] + part
         start = pl.multiple_of(out_row * width + i * tile, tile)
         copies.append(
-            pltpu.make_async_copy(
-                product.at[pl.ds(i * tile, tile)], out_ref.at[pl.ds(start, tile)], sems.at[i]
-            )
+            pltpu.make_async_copy(product.at[here], out_ref.at[pl.ds(start, tile)], sems.at[i])
         )
         copies[-1].start()
+
+    rows_product(act, dz_ref.at[1], width, tile, write)
     for copy in copies:
         copy.wait()
 
 
-def weight_grad_call(place, which, near, arrived, dz, features, before):
-    half = len(near[0])
-    width = near[0][0].shape[1]
+def weight_grad_last_call(place, which, own, blocks, dz, product, features, before):
+    width = own[0].shape[1]
     _, rows, columns = dz.shape
     tile = min(256, width)
-    operands = [place] + [x for group in near for x in group] + list(arrived) + [dz]
+    operands = [place] + list(own) + list(blocks) + [dz, product]
     specs = [IN_SMEM] + [IN_VMEM] * (len(operands) - 1)
     aliases = {}
     if before is not None:
@@ -430,20 +466,25 @@
         specs.append(ANYWHERE)
     return pl.pallas_call(
         functools.partial(
-            weight_grad_kernel, len(arrived), int(before is not None), half, tile, which
+            weight_grad_last_kernel,
+            len(blocks) + 1,
+            len(own),
+            tile,
+            int(before is not None),
+            which,
         ),
         out_shape=jax.ShapeDtypeStruct((features, columns), f32),
         in_specs=specs,
         out_specs=ANYWHERE,
         scratch_shapes=[
-            pltpu.VMEM((2 * rows, width), bf16),
+            pltpu.VMEM((rows, width), bf16),
             pltpu.VMEM((width, columns), f32),
             pltpu.SemaphoreType.DMA((width // tile,)),
         ],
         input_output_aliases=aliases,
-        compiler_params=params(12),
-        cost_estimate=cost(4 * rows * width * columns, 4 * width * columns),
-        name="weight_gradient",
+        compiler_params=params(10),
+        cost_estimate=cost(2 * rows * width * columns, 4 * width * columns),
+        name="weight_gradient_1",
     )(*operands)
 
 
@@ -508,11 +549,10 @@
         first, pieces[1] = lax.optimization_barrier((act[0], pieces[1]))
         others = [ring_send(first, "batch", d) for d in range(1, n_batch)]
         pieces = sibling_pieces(pieces, n_col)
-        far_pieces = gather_pieces(jnp.concatenate(others), n_col)
+        far_pieces = link_pieces(jnp.concatenate(others), n_col)
     with jax.named_scope("z"):
 
-        def z_of(source, groups):
-            total = None
+        def z_of(source, groups, total=None):
             for i, ks in enumerate(groups):
                 total = z_call(
                     place,
@@ -526,30 +566,38 @@
             return total
 
         z_own0, z_own1, z_sum = z_of(pieces, [[0, 1], far, [k + 1 for k in far]])
-        *z_far, _ = z_of(far_pieces, [evens, odds])
+        z_sum, held_back = lax.optimization_barrier((z_sum, [pieces[k] for k in evens]))
     with jax.named_scope("z_ring"):
-        z_ring = [z_own1]
-        for _ in range(1, n_batch):
+        z_ring = [z_own1, ring_send(z_own1, "batch", 1)]
+        z_ring[1], far_pieces[far[-1]] = lax.optimization_barrier((z_ring[1], far_pieces[far[-1]]))
+        z_ring.append(ring_send(z_ring[1], "batch", 1))
+        sums = [ring_send(z_sum, "batch", d) for d in range(reach + 1, n_batch)]
+        picked = pick_call(place, held_back, n_batch, n_col)
+        blocks = [
+            ring_send(x, "batch", 1 + i % (n_batch - 1)) for i, x in enumerate(picked)
+        ]
+    with jax.named_scope("z_far"):
+        start = z_call(
+            place, [0, far[-1]], [far_pieces[0], far_pieces[far[-1]]], held_weight, None, False, local_rows
+        )
+        start, far_pieces[far[0]], z_ring[2] = lax.optimization_barrier(
+            (start, far_pieces[far[0]], z_ring[2])
+        )
+        far_pieces = sibling_pieces(far_pieces, n_col)
+        for _ in range(3, n_batch):
             z_ring.append(ring_send(z_ring[-1], "batch", 1))
-        sums = [ring_send(z_sum, "batch", d) for d in range(reach + 1, n_batch)]
+        *z_far, _ = z_of(far_pieces, [far[:-1], odds], start)
         z_flat = [z_own0] + z_far
     with jax.named_scope("kernel"):
         even_part, odd_part = strip_call(place, z_flat, z_ring[: reach + 1], sums, rows, n_col)
         even_part = even_part + xor_send(odd_part, "col", 1)
-        even_part, z_ring[reach + 1 :] = lax.optimization_barrier((even_part, z_ring[reach + 1 :]))
         strip = even_part[0]
         for k in far:
             strip = strip + xor_send(even_part[k // 2], "col", k)
-        slots = list(zip(z_flat, z_ring))
         mine = strip.astype(bf16)
         mine = jnp.stack([mine] + [ring_send(mine, "batch", d) for d in range(1, n_batch)])
-        mine, held_back = lax.optimization_barrier((mine, [pieces[k] for k in evens]))
         strips = gather_pieces(mine, n_col)
-        picked = pick_call(place, held_back, n_batch, n_col)
-        blocks = [
-            ring_send(x, "batch", 1 + i % (n_batch - 1)) for i, x in enumerate(picked)
-        ]
-        strips, blocks[0] = lax.optimization_barrier((strips, blocks[0]))
+        slots = list(zip(z_flat, z_ring))
     with jax.named_scope("dz"):
         constants = (
             4.0 * scale / denom,
@@ -561,29 +609,36 @@
             1.0 / denom,
         )
         dz, share = dz_call(place, strip, [strips[k] for k in range(n_col)], slots, constants)
-        dz, blocks[1:] = lax.optimization_barrier((dz, blocks[1:]))
     with jax.named_scope("d_act"):
         (away,) = d_act_call(place, dz, share, held_weight, n_batch, n_col, None)
         got = xor_send(away, "col", 1)
         *sends, d_act = d_act_call(place, dz, share, held_weight, n_batch, n_col, got)
         arrived = [xor_send(part, "col", k) for k, part in zip(far, sends)]
     with jax.named_scope("grad_weight"):
+        sides = ((0, evens), (1, odds))
+        products = {}
+        for block in range(n_col // n_batch // 2):
+            for parity, ks in sides:
+                products[block, parity] = weight_grad_call(
+                    place, n_batch, block, [pieces[k] for k in ks], [far_pieces[k] for k in ks], dz
+                )
+        arrived, blocks, products = lax.optimization_barrier((arrived, blocks, products))
         grad_weight = None
         for block in range(n_col // n_batch // 2):
             mine = blocks[block * (n_batch - 1) : (block + 1) * (n_batch - 1)]
             other = [xor_send(x, "col", 1) for x in mine]
-            for parity, ks, far_rows in ((0, evens, mine), (1, odds, other)):
-                grad_weight = weight_grad_call(
+            for (parity, ks), far_rows in zip(sides, (mine, other)):
+                grad_weight = weight_grad_last_call(
                     place,
                     (block, parity),
-                    [[group[k] for k in ks] for group in (pieces, far_pieces)],
+                    [pieces[k] for k in ks],
                     far_rows,
                     dz,
+                    products[block, parity],
                     features // n_batch,
                     grad_weight,
                 )
     with jax.named_scope("norm_backward"):
-        arrived, d_act, grad_weight = lax.optimization_barrier((arrived, d_act, grad_weight))
         share = exchange_sum(share_of(part[tall:]) for part in [d_act] + arrived)
         d_act = d_act[:tall]
         for part in arrived:

time: 133 us -> 129 us (0.970)
  waiting for transfers between devices: 50.6 us -> 40.9 us
  starting transfers between devices: 46.6 us -> 49.1 us
  Pallas kernels: 29.4 us -> 31.8 us
    ppermute x38, waiting for transfers between devices: 36.7 us -> 24.2 us  [xor_send(): return lax.ppermute(x, axis, [(i, i ^ k) for i in range(n)])]
    ppermute x13, waiting for transfers between devices: 13.9 us -> 16.7 us  [ring_send(): lax.ppermute(x, axis, [(order[i], order[(i + d) % n]) for i in range(n)])]
    ppermute x13, starting transfers between devices: 16.8 us -> 19.2 us  [ring_send(): lax.ppermute(x, axis, [(order[i], order[(i + d) % n]) for i in range(n)])]
    pallas_call x2 -> x4, Pallas kernels: 5.79 us -> 7.45 us  [the longest x2 4.78 us: weight_grad_last_call(): pl.pallas_call(functools.partial(weight_grad_last_kernel, len(blocks) + 1...]
    pallas_call x5 -> x6, Pallas kernels: 9.62 us -> 10.3 us  [z_call(): pl.pallas_call(functools.partial(z_kernel, tuple(ks), before is None, las...]
  transfers between devices with their start and end apart: 51 -> 51, of which waited for: 25 -> 18; matrix products, arithmetic and copies ran while one was open for 0% -> 2% of each run, Pallas kernels for 21% -> 15%
where the time goes in v9:
time: 129 us
  starting transfers between devices  49.1 us (38%)
  waiting for transfers between devices  40.9 us (32%)
  Pallas kernels  31.8 us (25%)
  other arithmetic  5.31 us (4%)
    ppermute x38, starting transfers between devices, xor_send(): return lax.ppermute(x, axis, [(i, i ^ k) for i in range(n)])  30 us
    ppermute x38, waiting for transfers between devices, xor_send(): return lax.ppermute(x, axis, [(i, i ^ k) for i in range(n)])  24.2 us
    ppermute x13, starting transfers between devices, ring_send(): lax.ppermute(x, axis, [(order[i], order[(i + d) % n]) for i in range(n)])  19.2 us
    ppermute x13, waiting for transfers between devices, ring_send(): lax.ppermute(x, axis, [(order[i], order[(i + d) % n]) for i in range(n)])  16.7 us
    pallas_call x6, Pallas kernels, z_call(): pl.pallas_call(functools.partial(z_kernel, tuple(ks), before is None, las...  10.3 us
    pallas_call x2, Pallas kernels, weight_grad_last_call(): pl.pallas_call(functools.partial(weight_grad_last_kernel, len(blocks) + 1...  4.78 us
    pallas_call x1, Pallas kernels, dz_call(): pl.pallas_call(functools.partial(dz_kernel, n_batch, n_col, tile, constan...  4.65 us
    pallas_call x2, Pallas kernels, d_act_call(): pl.pallas_call(functools.partial(d_act_kernel, count, (got is not None, n...  3.69 us
  transfers between devices with their start and end apart: 51, of which 18 were waited for; matrix products, arithmetic and copies ran while one was open for 2% of the time, Pallas kernels for 15%

profile of v9, /device:TPU:0, one launch (start us, length us, event | category | flops | bytes accessed | tf_op | source)
XLA Modules:
  0.0 128.5 jit_solution(13741819934233478686)
XLA Ops:
  2.8 5.1 %collective-permute-start.2 = (f32[4,512]{1,0:T(4,128)S(1)}, f32[4,512]{1,0:T(4,128)S(1)}, u32[]{:S(2)}, u32[]{:S(2)}) collective-permute-start(f32[4,512]{1,0:T(4,128)S(1)} %pad_maximum_fusion.2), channel_id=1, source_target_pairs={{0,24},{8,16},{16,8},{24,0},{1,25},{9,17},{17,9},{25,1},{2,26},{10... | collective-permute-start | bytes 24584 | tf_op jit(solution)/shard_map/norm_stats/ppermute | solution.py:24
  8.6 3.5 %weight_load.1 = (bf16[4096,1024]{1,0:T(8,128)(2,1)S(1)}, f32[4,512]{1,0:T(4,128)S(1)}) custom-call(bf16[4096,1024]{1,0:T(8,128)(2,1)} %w_ref), custom_call_target="tpu_custom_call" | custom-call | bytes 16777216 | tf_op jit(solution)/shard_map/weight_load/weight_load/pallas_call | solution.py:78
  12.9 1.6 %collective-permute-start.3 = (bf16[256,512]{1,0:T(8,128)(2,1)S(1)}, bf16[256,512]{1,0:T(8,128)(2,1)S(1)}, u32[]{:S(2)}, u32[]{:S(2)}) collective-permute-start(bf16[256,512]{1,0:T(8,128)(2,1)S(1)} %bitcast.28), channel_id=1, source_target_pairs={{0,2},{1,3},{2,0},{3,1},{4,6},{5,7},{6,4},{7,5},{8,10},{9,11},{10,... | collective-permute-start | bytes 786440 | tf_op jit(solution)/shard_map/act_gather/ppermute | solution.py:24
  14.4 1.5 %collective-permute-start.5 = (bf16[256,512]{1,0:T(8,128)(2,1)S(1)}, bf16[256,512]{1,0:T(8,128)(2,1)S(1)}, u32[]{:S(2)}, u32[]{:S(2)}) collective-permute-start(bf16[256,512]{1,0:T(8,128)(2,1)S(1)} %bitcast.29), channel_id=1, source_target_pairs={{0,4},{1,5},{2,6},{3,7},{4,0},{5,1},{6,2},{7,3},{8,12},{9,13},{10,... | collective-permute-start | bytes 786440 | tf_op jit(solution)/shard_map/act_gather/ppermute | solution.py:24
  16.5 2.1 %collective-permute-start.10 = (bf16[128,512]{1,0:T(8,128)(2,1)S(1)}, bf16[128,512]{1,0:T(8,128)(2,1)S(1)}, u32[]{:S(2)}, u32[]{:S(2)}) collective-permute-start(bf16[128,512]{1,0:T(8,128)(2,1)S(1)} %slice_bitcast_fusion), channel_id=1, source_target_pairs={{0,16},{16,24},{24,8},{8,0},{1,17},{17,25},{25,9},{9,1},{2,18},{18... | collective-permute-start | bytes 393224 | tf_op jit(solution)/shard_map/act_gather/ppermute | solution.py:34
  18.5 1.4 %collective-permute-start.11 = (bf16[128,512]{1,0:T(8,128)(2,1)S(1)}, bf16[128,512]{1,0:T(8,128)(2,1)S(1)}, u32[]{:S(2)}, u32[]{:S(2)}) collective-permute-start(bf16[128,512]{1,0:T(8,128)(2,1)S(1)} %slice_bitcast_fusion), channel_id=1, source_target_pairs={{0,24},{16,8},{24,0},{8,16},{1,25},{17,9},{25,1},{9,17},{2,26},{18... | collective-permute-start | bytes 393224 | tf_op jit(solution)/shard_map/act_gather/ppermute | solution.py:34
  20.0 1.2 z_matmul.6.refs_4_
  23.1 5.4 %collective-permute-done.5.refs_1_.refs_2_ = bf16[256,512]{1,0:T(8,128)(2,1)S(1)} collective-permute-done((bf16[256,512]{1,0:T(8,128)(2,1)S(1)}, bf16[256,512]{1,0:T(8,128)(2,1)S(1)}, u32[]{:S(2)}, u32[]{:S(2)}) %collective-permute-start.5) | collective-permute-done | bytes 262176 | tf_op jit(solution)/shard_map/act_gather/ppermute | solution.py:24
  29.1 2.5 %collective-permute-done.12 = bf16[128,512]{1,0:T(8,128)(2,1)S(1)} collective-permute-done((bf16[128,512]{1,0:T(8,128)(2,1)S(1)}, bf16[128,512]{1,0:T(8,128)(2,1)S(1)}, u32[]{:S(2)}, u32[]{:S(2)}) %collective-permute-start.12) | collective-permute-done | bytes 131104 | tf_op jit(solution)/shard_map/act_gather/ppermute | solution.py:34
  31.6 2.5 %collective-permute-start.15 = (bf16[384,512]{1,0:T(8,128)(2,1)S(1)}, bf16[384,512]{1,0:T(8,128)(2,1)S(1)}, u32[]{:S(2)}, u32[]{:S(2)}) collective-permute-start(bf16[384,512]{1,0:T(8,128)(2,1)S(1)} %constant_dynamic-update-slice_fusion.refs_0_.refs_4_), channel_id=1, source_target_pairs={{0,6},{1,7},{2,4},{3,5},{4,2},{5,3},{6,0},{7,1},{8,14},{9,15},{10,... | collective-permute-start | bytes 1179656 | tf_op jit(solution)/shard_map/act_gather/ppermute | solution.py:24
  34.1 1.5 %z_matmul.7.refs_4_ = f32[256,1024]{1,0:T(8,128)S(1)} custom-call(s32[2]{0:T(128)S(1)} %pad_add_fusion.place_ref, bf16[256,512]{1,0:T(8,128)(2,1)S(1)} %collective-permute-done.3.refs_0_.refs_1_, bf16[256,512]{1,0:T(8,128)(2,1)S(1)} %collective-permute-done.5.refs_1_.refs_2_, bf16[256,512]{1,0:T(8,128)(2,1)S(1)} %collective-permute-done.7.refs_2_.refs_3_, ...), custom_call_target="tpu_custom_call" | custom-call | flops 805306368 | bytes 524288 | tf_op jit(solution)/shard_map/z/z_matmul/pallas_call | solution.py:130
  35.7 1.5 %z_matmul.8 = (bf16[128,1024]{1,0:T(8,128)(2,1)S(1)}, bf16[128,1024]{1,0:T(8,128)(2,1)S(1)}, f32[2,1024]{1,0:T(2,128)S(1)}) custom-call(s32[2]{0:T(128)S(1)} %pad_add_fusion.place_ref, bf16[256,512]{1,0:T(8,128)(2,1)S(1)} %collective-permute-done.4.refs_0_.refs_1_, bf16[256,512]{1,0:T(8,128)(2,1)S(1)} %collective-permute-done.6.refs_1_.refs_2_, ...), custom_call_target="tpu_custom_call" | custom-call | flops 805306368 | bytes 524288 | tf_op jit(solution)/shard_map/z/z_matmul/pallas_call | solution.py:130
  38.4 6.8 %collective-permute-done.14.refs_5_.refs_11_ = bf16[128,1024]{1,0:T(8,128)(2,1)S(1)} collective-permute-done((bf16[128,1024]{1,0:T(8,128)(2,1)S(1)}, bf16[128,1024]{1,0:T(8,128)(2,1)S(1)}, u32[]{:S(2)}, u32[]{:S(2)}) %collective-permute-start.14) | collective-permute-done | bytes 262176 | tf_op jit(solution)/shard_map/z_ring/ppermute | solution.py:34
  45.2 1.2 collective-permute-start.17
  46.9 5.1 %collective-permute-done.19.refs_1_.refs_6_ = bf16[384,512]{1,0:T(8,128)(2,1)S(1)} collective-permute-done((bf16[384,512]{1,0:T(8,128)(2,1)S(1)}, bf16[384,512]{1,0:T(8,128)(2,1)S(1)}, u32[]{:S(2)}, u32[]{:S(2)}) %collective-permute-start.19) | collective-permute-done | bytes 393248 | tf_op jit(solution)/shard_map/act_gather/ppermute | solution.py:24
  52.0 1.5 %z_matmul.9.refs_3_ = f32[384,1024]{1,0:T(8,128)S(1)} custom-call(s32[2]{0:T(128)S(1)} %pad_add_fusion.place_ref, bf16[384,512]{1,0:T(8,128)(2,1)S(1)} %constant_dynamic-update-slice_fusion.refs_0_.refs_4_, bf16[384,512]{1,0:T(8,128)(2,1)S(1)} %collective-permute-done.15.refs_1_.refs_7_, bf16[4096,1024]{1,0:T(8,128)(2,1)S(1)} %get-tuple-element.55.refs_2_.refs_3_.refs_4_.w_ref), custom_call_target="tpu_custom_call" | custom-call | flops 805306368 | bytes 786432 | tf_op jit(solution)/shard_map/z_far/z_matmul/pallas_call | solution.py:130
  54.5 1.5 %z_matmul.10.refs_5_ = f32[384,1024]{1,0:T(8,128)S(1)} custom-call(s32[2]{0:T(128)S(1)} %pad_add_fusion.place_ref, bf16[384,512]{1,0:T(8,128)(2,1)S(1)} %collective-permute-done.16.refs_0_.refs_5_, bf16[384,512]{1,0:T(8,128)(2,1)S(1)} %collective-permute-done.19.refs_1_.refs_6_, bf16[4096,1024]{1,0:T(8,128)(2,1)S(1)} %get-tuple-element.55.refs_2_.refs_3_.refs_4_.w_ref, ...), custom_call_target="tpu_custom_call" | custom-call | flops 805306368 | bytes 786432 | tf_op jit(solution)/shard_map/z_far/z_matmul/pallas_call | solution.py:130
  56.1 3.0 %z_matmul.11 = (bf16[128,1024]{1,0:T(8,128)(2,1)S(1)}, bf16[128,1024]{1,0:T(8,128)(2,1)S(1)}, bf16[128,1024]{1,0:T(8,128)(2,1)S(1)}, f32[3,1024]{1,0:T(4,128)}) custom-call(s32[2]{0:T(128)S(1)} %pad_add_fusion.place_ref, bf16[384,512]{1,0:T(8,128)(2,1)S(1)} %collective-permute-done.13.refs_0_.refs_4_, ...), custom_call_target="tpu_custom_call" | custom-call | flops 1610612736 | bytes 786432 | tf_op jit(solution)/shard_map/z_far/z_matmul/pallas_call | solution.py:130
  59.1 1.6 %kernel_strip.1 = (f32[4,32,384]{2,1,0:T(8,128)S(1)}, f32[4,32,384]{2,1,0:T(8,128)S(1)}) custom-call(s32[2]{0:T(128)S(1)} %pad_add_fusion.place_ref, bf16[128,1024]{1,0:T(8,128)(2,1)S(1)} %get-tuple-element.57.refs_0_.refs_8_, bf16[128,1024]{1,0:T(8,128)(2,1)S(1)} %get-tuple-element.64.refs_1_.refs_10_, ...), custom_call_target="tpu_custom_call" | custom-call | flops 201326592 | bytes 2097152 | tf_op jit(solution)/shard_map/kernel/kernel_strip/pallas_call | solution.py:170
  60.9 1.2 collective-permute-done.23
  62.2 2.1 %collective-permute-start.26 = (f32[32,384]{1,0:T(8,128)S(1)}, f32[32,384]{1,0:T(8,128)S(1)}, u32[]{:S(2)}, u32[]{:S(2)}) collective-permute-start(f32[32,384]{1,0:T(8,128)S(1)} %get-tuple-element.103), channel_id=1, source_target_pairs={{0,6},{1,7},{2,4},{3,5},{4,2},{5,3},{6,0},{7,1},{8,14},{9,15},{10,... | collective-permute-start | bytes 147464 | tf_op jit(solution)/shard_map/kernel/ppermute | solution.py:24
  65.8 1.5 %collective-permute-done.26 = f32[32,384]{1,0:T(8,128)S(1)} collective-permute-done((f32[32,384]{1,0:T(8,128)S(1)}, f32[32,384]{1,0:T(8,128)S(1)}, u32[]{:S(2)}, u32[]{:S(2)}) %collective-permute-start.26) | collective-permute-done | bytes 49184 | tf_op jit(solution)/shard_map/kernel/ppermute | solution.py:24
  69.0 2.8 %collective-permute-start.29 = (bf16[32,384]{1,0:T(8,128)(2,1)S(1)}, bf16[32,384]{1,0:T(8,128)(2,1)S(1)}, u32[]{:S(2)}, u32[]{:S(2)}) collective-permute-start(bf16[32,384]{1,0:T(8,128)(2,1)S(1)} %get-tuple-element.98), channel_id=1, source_target_pairs={{0,8},{16,0},{24,16},{8,24},{1,9},{17,1},{25,17},{9,25},{2,10},{18... | collective-permute-start | bytes 73736 | tf_op jit(solution)/shard_map/kernel/ppermute | solution.py:34
  71.8 1.6 %collective-permute-start.28 = (bf16[32,384]{1,0:T(8,128)(2,1)S(1)}, bf16[32,384]{1,0:T(8,128)(2,1)S(1)}, u32[]{:S(2)}, u32[]{:S(2)}) collective-permute-start(bf16[32,384]{1,0:T(8,128)(2,1)S(1)} %get-tuple-element.98), channel_id=1, source_target_pairs={{0,24},{16,8},{24,0},{8,16},{1,25},{17,9},{25,1},{9,17},{2,26},{18... | collective-permute-start | bytes 73736 | tf_op jit(solution)/shard_map/kernel/ppermute | solution.py:34
  73.4 2.8 %collective-permute-start.37 = (bf16[128,1024]{1,0:T(8,128)(2,1)S(1)}, bf16[128,1024]{1,0:T(8,128)(2,1)S(1)}, u32[]{:S(2)}, u32[]{:S(2)}) collective-permute-start(bf16[128,1024]{1,0:T(8,128)(2,1)S(1)} %collective-permute-done.17.refs_6_.refs_13_), channel_id=1, source_target_pairs={{0,16},{16,24},{24,8},{8,0},{1,17},{17,25},{25,9},{9,1},{2,18},{18... | collective-permute-start | bytes 786440 | tf_op jit(solution)/shard_map/z_far/ppermute | solution.py:34
  76.2 1.5 %collective-permute-done.28 = bf16[32,384]{1,0:T(8,128)(2,1)S(1)} collective-permute-done((bf16[32,384]{1,0:T(8,128)(2,1)S(1)}, bf16[32,384]{1,0:T(8,128)(2,1)S(1)}, u32[]{:S(2)}, u32[]{:S(2)}) %collective-permute-start.28) | collective-permute-done | bytes 24608 | tf_op jit(solution)/shard_map/kernel/ppermute | solution.py:34
  78.4 1.5 %collective-permute-start.33 = (bf16[4,32,384]{2,1,0:T(8,128)(2,1)S(1)}, bf16[4,32,384]{2,1,0:T(8,128)(2,1)S(1)}, u32[]{:S(2)}, u32[]{:S(2)}) collective-permute-start(bf16[4,32,384]{2,1,0:T(8,128)(2,1)S(1)} %pad_maximum_fusion.refs_0_), channel_id=1, source_target_pairs={{0,4},{1,5},{2,6},{3,7},{4,0},{5,1},{6,2},{7,3},{8,12},{9,13},{10,... | collective-permute-start | bytes 294920 | tf_op jit(solution)/shard_map/kernel/ppermute | solution.py:24
  80.0 1.3 %collective-permute-start.35 = (bf16[4,32,384]{2,1,0:T(8,128)(2,1)S(1)}, bf16[4,32,384]{2,1,0:T(8,128)(2,1)S(1)}, u32[]{:S(2)}, u32[]{:S(2)}) collective-permute-start(bf16[4,32,384]{2,1,0:T(8,128)(2,1)S(1)} %pad_maximum_fusion.refs_0_), channel_id=1, source_target_pairs={{0,6},{1,7},{2,4},{3,5},{4,2},{5,3},{6,0},{7,1},{8,14},{9,15},{10,... | collective-permute-start | bytes 294920 | tf_op jit(solution)/shard_map/kernel/ppermute | solution.py:24
  81.3 1.1 collective-permute-done.31.refs_2_
  83.1 2.4 %collective-permute-done.35.refs_6_ = bf16[4,32,384]{2,1,0:T(8,128)(2,1)S(1)} collective-permute-done((bf16[4,32,384]{2,1,0:T(8,128)(2,1)S(1)}, bf16[4,32,384]{2,1,0:T(8,128)(2,1)S(1)}, u32[]{:S(2)}, u32[]{:S(2)}) %collective-permute-start.35) | collective-permute-done | bytes 98336 | tf_op jit(solution)/shard_map/kernel/ppermute | solution.py:24
  85.5 1.3 collective-permute-done.36.refs_7_
  86.8 4.7 %embedding_gradient.1 = (bf16[2,512,1024]{2,1,0:T(8,128)(2,1)S(1)}, f32[8,128]{1,0:T(8,128)S(1)}) custom-call(s32[2]{0:T(128)S(1)} %pad_add_fusion.place_ref, f32[32,384]{1,0:T(8,128)S(1)} %get-tuple-element.99.own_ref, bf16[4,32,384]{2,1,0:T(8,128)(2,1)S(1)} %pad_maximum_fusion.refs_0_, bf16[4,32,384]{2,1,0:T(8,128)(2,1)S(1)} %collective-permute-done.30.refs_1_, ...), custom_call_target="tpu_custom_call" | custom-call | flops 1073741824 | bytes 4194304 | tf_op jit(solution)/shard_map/dz/embedding_gradient/pallas_call | solution.py:252
  91.4 1.8 %d_act_matmul.2 = bf16[4,272,512]{2,1,0:T(8,128)(2,1)S(1)} custom-call(s32[2]{0:T(128)S(1)} %pad_add_fusion.place_ref, bf16[2,512,1024]{2,1,0:T(8,128)(2,1)S(1)} %get-tuple-element.72.dz_ref.refs_8_.refs_7_, f32[8,128]{1,0:T(8,128)S(1)} %get-tuple-element.73.share_ref, bf16[4096,1024]{1,0:T(8,128)(2,1)S(1)} %get-tuple-element.55.refs_2_.refs_3_.refs_4_.w_ref), custom_call_target="tpu_custom_call" | custom-call | flops 1073741824 | bytes 1048576 | tf_op jit(solution)/shard_map/d_act/d_act_matmul/pallas_call | solution.py:324
  93.5 2.6 %collective-permute-done.38.refs_0_ = bf16[4,272,512]{2,1,0:T(8,128)(2,1)S(1)} collective-permute-done((bf16[4,272,512]{2,1,0:T(8,128)(2,1)S(1)}, bf16[4,272,512]{2,1,0:T(8,128)(2,1)S(1)}, u32[]{:S(2)}, u32[]{:S(2)}) %collective-permute-start.38) | collective-permute-done | bytes 1114144 | tf_op jit(solution)/shard_map/d_act/ppermute | solution.py:24
  96.1 1.8 %d_act_matmul.3 = (bf16[272,512]{1,0:T(8,128)(2,1)S(1)}, bf16[272,512]{1,0:T(8,128)(2,1)S(1)}, bf16[272,512]{1,0:T(8,128)(2,1)S(1)}, f32[272,512]{1,0:T(8,128)S(1)}) custom-call(s32[2]{0:T(128)S(1)} %pad_add_fusion.place_ref, bf16[2,512,1024]{2,1,0:T(8,128)(2,1)S(1)} %get-tuple-element.72.dz_ref.refs_8_.refs_7_, f32[8,128]{1,0:T(8,128)S(1)} %get-tuple-element.73.share_ref, ...), custom_call_target="tpu_custom_call" | custom-call | flops 1073741824 | bytes 1048576 | tf_op jit(solution)/shard_map/d_act/d_act_matmul/pallas_call | solution.py:324
  97.9 1.5 %collective-permute-start.39 = (bf16[272,512]{1,0:T(8,128)(2,1)S(1)}, bf16[272,512]{1,0:T(8,128)(2,1)S(1)}, u32[]{:S(2)}, u32[]{:S(2)}) collective-permute-start(bf16[272,512]{1,0:T(8,128)(2,1)S(1)} %get-tuple-element.75), channel_id=1, source_target_pairs={{0,2},{1,3},{2,0},{3,1},{4,6},{5,7},{6,4},{7,5},{8,10},{9,11},{10,... | collective-permute-start | bytes 835592 | tf_op jit(solution)/shard_map/d_act/ppermute | solution.py:24
  99.9 1.6 %collective-permute-start.41 = (bf16[272,512]{1,0:T(8,128)(2,1)S(1)}, bf16[272,512]{1,0:T(8,128)(2,1)S(1)}, u32[]{:S(2)}, u32[]{:S(2)}) collective-permute-start(bf16[272,512]{1,0:T(8,128)(2,1)S(1)} %get-tuple-element.77), channel_id=1, source_target_pairs={{0,6},{1,7},{2,4},{3,5},{4,2},{5,3},{6,0},{7,1},{8,14},{9,15},{10,... | collective-permute-start | bytes 835592 | tf_op jit(solution)/shard_map/d_act/ppermute | solution.py:24
  102.1 1.1 collective-permute-start.42
  103.3 2.2 %collective-permute-start.43 = (bf16[128,512]{1,0:T(8,128)(2,1)S(1)}, bf16[128,512]{1,0:T(8,128)(2,1)S(1)}, u32[]{:S(2)}, u32[]{:S(2)}) collective-permute-start(bf16[128,512]{1,0:T(8,128)(2,1)S(1)} %get-tuple-element.83), channel_id=1, source_target_pairs={{0,24},{16,8},{24,0},{8,16},{1,25},{17,9},{25,1},{9,17},{2,26},{18... | collective-permute-start | bytes 393224 | tf_op jit(solution)/shard_map/z_ring/ppermute | solution.py:34
  105.5 2.3 %collective-permute-done.42.refs_4_ = bf16[128,512]{1,0:T(8,128)(2,1)S(1)} collective-permute-done((bf16[128,512]{1,0:T(8,128)(2,1)S(1)}, bf16[128,512]{1,0:T(8,128)(2,1)S(1)}, u32[]{:S(2)}, u32[]{:S(2)}) %collective-permute-start.42) | collective-permute-done | bytes 131104 | tf_op jit(solution)/shard_map/z_ring/ppermute | solution.py:34
  107.7 2.5 %collective-permute-start.44 = (bf16[128,512]{1,0:T(8,128)(2,1)S(1)}, bf16[128,512]{1,0:T(8,128)(2,1)S(1)}, u32[]{:S(2)}, u32[]{:S(2)}) collective-permute-start(bf16[128,512]{1,0:T(8,128)(2,1)S(1)} %get-tuple-element.84), channel_id=1, source_target_pairs={{0,8},{16,0},{24,16},{8,24},{1,9},{17,1},{25,17},{9,25},{2,10},{18... | collective-permute-start | bytes 393224 | tf_op jit(solution)/shard_map/z_ring/ppermute | solution.py:34
  110.3 1.3 %weight_gradient_0.2.refs_8_ = f32[512,1024]{1,0:T(8,128)S(1)} custom-call(s32[2]{0:T(128)S(1)} %pad_add_fusion.place_ref, bf16[256,512]{1,0:T(8,128)(2,1)S(1)} %bitcast.33, bf16[256,512]{1,0:T(8,128)(2,1)S(1)} %collective-permute-done.3.refs_0_.refs_1_, bf16[256,512]{1,0:T(8,128)(2,1)S(1)} %collective-permute-done.5.refs_1_.refs_2_, ...), custom_call_target="tpu_custom_call" | custom-call | flops 536870912 | bytes 1048576 | tf_op jit(solution)/shard_map/grad_weight/weight_gradient_0/pallas_call | solution.py:411
  111.6 1.3 %weight_gradient_0.3.refs_8_ = f32[512,1024]{1,0:T(8,128)S(1)} custom-call(s32[2]{0:T(128)S(1)} %pad_add_fusion.place_ref, bf16[256,512]{1,0:T(8,128)(2,1)S(1)} %collective-permute-done.9.refs_1_.refs_0_, bf16[256,512]{1,0:T(8,128)(2,1)S(1)} %collective-permute-done.4.refs_0_.refs_1_, bf16[256,512]{1,0:T(8,128)(2,1)S(1)} %collective-permute-done.6.refs_1_.refs_2_, ...), custom_call_target="tpu_custom_call" | custom-call | flops 536870912 | bytes 1048576 | tf_op jit(solution)/shard_map/grad_weight/weight_gradient_0/pallas_call | solution.py:411
  113.0 3.6 %collective-permute-done.44.refs_6_ = bf16[128,512]{1,0:T(8,128)(2,1)S(1)} collective-permute-done((bf16[128,512]{1,0:T(8,128)(2,1)S(1)}, bf16[128,512]{1,0:T(8,128)(2,1)S(1)}, u32[]{:S(2)}, u32[]{:S(2)}) %collective-permute-start.44) | collective-permute-done | bytes 131104 | tf_op jit(solution)/shard_map/z_ring/ppermute | solution.py:34
  117.3 1.8 %collective-permute-start.47 = (f32[8,512]{1,0:T(8,128)S(1)}, f32[8,512]{1,0:T(8,128)S(1)}, u32[]{:S(2)}, u32[]{:S(2)}) collective-permute-start(f32[8,512]{1,0:T(8,128)S(1)} %pad_maximum_fusion.1), channel_id=1, source_target_pairs={{0,24},{8,16},{16,8},{24,0},{1,25},{9,17},{17,9},{25,1},{2,26},{10... | collective-permute-start | bytes 49160 | tf_op jit(solution)/shard_map/norm_backward/ppermute | solution.py:24
  119.0 1.7 %collective-permute-start.45 = (f32[8,512]{1,0:T(8,128)S(1)}, f32[8,512]{1,0:T(8,128)S(1)}, u32[]{:S(2)}, u32[]{:S(2)}) collective-permute-start(f32[8,512]{1,0:T(8,128)S(1)} %pad_maximum_fusion.1), channel_id=1, source_target_pairs={{0,8},{8,0},{16,24},{24,16},{1,9},{9,1},{17,25},{25,17},{2,10},{10... | collective-permute-start | bytes 49160 | tf_op jit(solution)/shard_map/norm_backward/ppermute | solution.py:24
  121.3 2.4 %weight_gradient_1.2.refs_9_ = f32[1024,1024]{1,0:T(8,128)} custom-call(s32[2]{0:T(128)S(1)} %pad_add_fusion.place_ref, bf16[256,512]{1,0:T(8,128)(2,1)S(1)} %bitcast.34, bf16[256,512]{1,0:T(8,128)(2,1)S(1)} %collective-permute-done.3.refs_0_.refs_1_, bf16[256,512]{1,0:T(8,128)(2,1)S(1)} %collective-permute-done.5.refs_1_.refs_2_, ...), custom_call_target="tpu_custom_call" | custom-call | flops 536870912 | bytes 2097152 | tf_op jit(solution)/shard_map/grad_weight/weight_gradient_1/pallas_call | solution.py:467
  126.0 2.4 %weight_gradient_1.3 = f32[1024,1024]{1,0:T(8,128)} custom-call(s32[2]{0:T(128)S(1)} %pad_add_fusion.place_ref, bf16[256,512]{1,0:T(8,128)(2,1)S(1)} %collective-permute-done.9.refs_1_.refs_0_, bf16[256,512]{1,0:T(8,128)(2,1)S(1)} %collective-permute-done.4.refs_0_.refs_1_, ...), custom_call_target="tpu_custom_call", output_to_operand_aliasing={{}: (10, {})} | custom-call | flops 536870912 | bytes 2097152 | tf_op jit(solution)/shard_map/grad_weight/weight_gradient_1/pallas_call | solution.py:467
  (100 shorter events, 18.8 us)
Async XLA Ops:
  2.8 9.2 %collective-permute-start.2 = (f32[4,512]{1,0:T(4,128)S(1)}, f32[4,512]{1,0:T(4,128)S(1)}, u32[]{:S(2)}, u32[]{:S(2)}) collective-permute-start(f32[4,512]{1,0:T(4,128)S(1)} %pad_maximum_fusion.2), channel_id=1, source_target_pairs={{0,24},{8,16},{16,8},{24,0},{1,25},{9,17},{17,9},{25,1},{2,26},{10... | collective-permute-start | bytes 24584 | tf_op jit(solution)/shard_map/norm_stats/ppermute | solution.py:24
  7.9 4.5 %collective-permute-start.1 = (f32[4,512]{1,0:T(4,128)S(1)}, f32[4,512]{1,0:T(4,128)S(1)}, u32[]{:S(2)}, u32[]{:S(2)}) collective-permute-start(f32[4,512]{1,0:T(4,128)S(1)} %pad_maximum_fusion.2), channel_id=1, source_target_pairs={{0,16},{8,24},{16,0},{24,8},{1,17},{9,25},{17,1},{25,9},{2,18},{10... | collective-permute-start | bytes 24584 | tf_op jit(solution)/shard_map/norm_stats/ppermute | solution.py:24
  7.9 4.5 %collective-permute-start = (f32[4,512]{1,0:T(4,128)S(1)}, f32[4,512]{1,0:T(4,128)S(1)}, u32[]{:S(2)}, u32[]{:S(2)}) collective-permute-start(f32[4,512]{1,0:T(4,128)S(1)} %pad_maximum_fusion.2), channel_id=1, source_target_pairs={{0,8},{8,0},{16,24},{24,16},{1,9},{9,1},{17,25},{25,17},{2,10},{10... | collective-permute-start | bytes 24584 | tf_op jit(solution)/shard_map/norm_stats/ppermute | solution.py:24
  12.8 3.6 %collective-permute-start.9 = (bf16[256,512]{1,0:T(8,128)(2,1)S(1)}, bf16[256,512]{1,0:T(8,128)(2,1)S(1)}, u32[]{:S(2)}, u32[]{:S(2)}) collective-permute-start(bf16[256,512]{1,0:T(8,128)(2,1)S(1)} %bitcast.27), channel_id=1, source_target_pairs={{0,1},{1,0},{2,3},{3,2},{4,5},{5,4},{6,7},{7,6},{8,9},{9,8},{10,11... | collective-permute-start | bytes 786440 | tf_op jit(solution)/shard_map/act_gather/ppermute | solution.py:24
  12.9 9.2 %collective-permute-start.3 = (bf16[256,512]{1,0:T(8,128)(2,1)S(1)}, bf16[256,512]{1,0:T(8,128)(2,1)S(1)}, u32[]{:S(2)}, u32[]{:S(2)}) collective-permute-start(bf16[256,512]{1,0:T(8,128)(2,1)S(1)} %bitcast.28), channel_id=1, source_target_pairs={{0,2},{1,3},{2,0},{3,1},{4,6},{5,7},{6,4},{7,5},{8,10},{9,11},{10,... | collective-permute-start | bytes 786440 | tf_op jit(solution)/shard_map/act_gather/ppermute | solution.py:24
  14.4 14.0 %collective-permute-start.5 = (bf16[256,512]{1,0:T(8,128)(2,1)S(1)}, bf16[256,512]{1,0:T(8,128)(2,1)S(1)}, u32[]{:S(2)}, u32[]{:S(2)}) collective-permute-start(bf16[256,512]{1,0:T(8,128)(2,1)S(1)} %bitcast.29), channel_id=1, source_target_pairs={{0,4},{1,5},{2,6},{3,7},{4,0},{5,1},{6,2},{7,3},{8,12},{9,13},{10,... | collective-permute-start | bytes 786440 | tf_op jit(solution)/shard_map/act_gather/ppermute | solution.py:24
  16.0 12.5 %collective-permute-start.7 = (bf16[256,512]{1,0:T(8,128)(2,1)S(1)}, bf16[256,512]{1,0:T(8,128)(2,1)S(1)}, u32[]{:S(2)}, u32[]{:S(2)}) collective-permute-start(bf16[256,512]{1,0:T(8,128)(2,1)S(1)} %bitcast.30), channel_id=1, source_target_pairs={{0,6},{1,7},{2,4},{3,5},{4,2},{5,3},{6,0},{7,1},{8,14},{9,15},{10,... | collective-permute-start | bytes 786440 | tf_op jit(solution)/shard_map/act_gather/ppermute | solution.py:24
  16.5 12.5 %collective-permute-start.10 = (bf16[128,512]{1,0:T(8,128)(2,1)S(1)}, bf16[128,512]{1,0:T(8,128)(2,1)S(1)}, u32[]{:S(2)}, u32[]{:S(2)}) collective-permute-start(bf16[128,512]{1,0:T(8,128)(2,1)S(1)} %slice_bitcast_fusion), channel_id=1, source_target_pairs={{0,16},{16,24},{24,8},{8,0},{1,17},{17,25},{25,9},{9,1},{2,18},{18... | collective-permute-start | bytes 393224 | tf_op jit(solution)/shard_map/act_gather/ppermute | solution.py:34
  18.5 10.5 %collective-permute-start.11 = (bf16[128,512]{1,0:T(8,128)(2,1)S(1)}, bf16[128,512]{1,0:T(8,128)(2,1)S(1)}, u32[]{:S(2)}, u32[]{:S(2)}) collective-permute-start(bf16[128,512]{1,0:T(8,128)(2,1)S(1)} %slice_bitcast_fusion), channel_id=1, source_target_pairs={{0,24},{16,8},{24,0},{8,16},{1,25},{17,9},{25,1},{9,17},{2,26},{18... | collective-permute-start | bytes 393224 | tf_op jit(solution)/shard_map/act_gather/ppermute | solution.py:34
  22.1 9.5 %collective-permute-start.12 = (bf16[128,512]{1,0:T(8,128)(2,1)S(1)}, bf16[128,512]{1,0:T(8,128)(2,1)S(1)}, u32[]{:S(2)}, u32[]{:S(2)}) collective-permute-start(bf16[128,512]{1,0:T(8,128)(2,1)S(1)} %slice_bitcast_fusion), channel_id=1, source_target_pairs={{0,8},{16,0},{24,16},{8,24},{1,9},{17,1},{25,17},{9,25},{2,10},{18... | collective-permute-start | bytes 393224 | tf_op jit(solution)/shard_map/act_gather/ppermute | solution.py:34
  28.4 7.2 %collective-permute-start.4 = (bf16[256,512]{1,0:T(8,128)(2,1)S(1)}, bf16[256,512]{1,0:T(8,128)(2,1)S(1)}, u32[]{:S(2)}, u32[]{:S(2)}) collective-permute-start(bf16[256,512]{1,0:T(8,128)(2,1)S(1)} %collective-permute-done.3.refs_0_.refs_1_), channel_id=1, source_target_pairs={{0,1},{1,0},{2,3},{3,2},{4,5},{5,4},{6,7},{7,6},{8,9},{9,8},{10,11... | collective-permute-start | bytes 786440 | tf_op jit(solution)/shard_map/act_gather/ppermute | solution.py:24
  28.4 7.2 %collective-permute-start.6 = (bf16[256,512]{1,0:T(8,128)(2,1)S(1)}, bf16[256,512]{1,0:T(8,128)(2,1)S(1)}, u32[]{:S(2)}, u32[]{:S(2)}) collective-permute-start(bf16[256,512]{1,0:T(8,128)(2,1)S(1)} %collective-permute-done.5.refs_1_.refs_2_), channel_id=1, source_target_pairs={{0,1},{1,0},{2,3},{3,2},{4,5},{5,4},{6,7},{7,6},{8,9},{9,8},{10,11... | collective-permute-start | bytes 786440 | tf_op jit(solution)/shard_map/act_gather/ppermute | solution.py:24
  29.0 6.7 %collective-permute-start.8 = (bf16[256,512]{1,0:T(8,128)(2,1)S(1)}, bf16[256,512]{1,0:T(8,128)(2,1)S(1)}, u32[]{:S(2)}, u32[]{:S(2)}) collective-permute-start(bf16[256,512]{1,0:T(8,128)(2,1)S(1)} %collective-permute-done.7.refs_2_.refs_3_), channel_id=1, source_target_pairs={{0,1},{1,0},{2,3},{3,2},{4,5},{5,4},{6,7},{7,6},{8,9},{9,8},{10,11... | collective-permute-start | bytes 786440 | tf_op jit(solution)/shard_map/act_gather/ppermute | solution.py:24
  31.6 13.6 %collective-permute-start.15 = (bf16[384,512]{1,0:T(8,128)(2,1)S(1)}, bf16[384,512]{1,0:T(8,128)(2,1)S(1)}, u32[]{:S(2)}, u32[]{:S(2)}) collective-permute-start(bf16[384,512]{1,0:T(8,128)(2,1)S(1)} %constant_dynamic-update-slice_fusion.refs_0_.refs_4_), channel_id=1, source_target_pairs={{0,6},{1,7},{2,4},{3,5},{4,2},{5,3},{6,0},{7,1},{8,14},{9,15},{10,... | collective-permute-start | bytes 1179656 | tf_op jit(solution)/shard_map/act_gather/ppermute | solution.py:24
  37.2 8.0 %collective-permute-start.14 = (bf16[128,1024]{1,0:T(8,128)(2,1)S(1)}, bf16[128,1024]{1,0:T(8,128)(2,1)S(1)}, u32[]{:S(2)}, u32[]{:S(2)}) collective-permute-start(bf16[128,1024]{1,0:T(8,128)(2,1)S(1)} %get-tuple-element.59.refs_4_.refs_9_), channel_id=1, source_target_pairs={{0,16},{16,24},{24,8},{8,0},{1,17},{17,25},{25,9},{9,1},{2,18},{18... | collective-permute-start | bytes 786440 | tf_op jit(solution)/shard_map/z_ring/ppermute | solution.py:34
  37.3 14.7 %collective-permute-start.19 = (bf16[384,512]{1,0:T(8,128)(2,1)S(1)}, bf16[384,512]{1,0:T(8,128)(2,1)S(1)}, u32[]{:S(2)}, u32[]{:S(2)}) collective-permute-start(bf16[384,512]{1,0:T(8,128)(2,1)S(1)} %constant_dynamic-update-slice_fusion.refs_0_.refs_4_), channel_id=1, source_target_pairs={{0,4},{1,5},{2,6},{3,7},{4,0},{5,1},{6,2},{7,3},{8,12},{9,13},{10,... | collective-permute-start | bytes 1179656 | tf_op jit(solution)/shard_map/act_gather/ppermute | solution.py:24
  37.9 15.7 %collective-permute-start.16 = (bf16[384,512]{1,0:T(8,128)(2,1)S(1)}, bf16[384,512]{1,0:T(8,128)(2,1)S(1)}, u32[]{:S(2)}, u32[]{:S(2)}) collective-permute-start(bf16[384,512]{1,0:T(8,128)(2,1)S(1)} %constant_dynamic-update-slice_fusion.refs_0_.refs_4_), channel_id=1, source_target_pairs={{0,2},{1,3},{2,0},{3,1},{4,6},{5,7},{6,4},{7,5},{8,10},{9,11},{10,... | collective-permute-start | bytes 1179656 | tf_op jit(solution)/shard_map/act_gather/ppermute | solution.py:24
  45.2 8.3 %collective-permute-start.17 = (bf16[128,1024]{1,0:T(8,128)(2,1)S(1)}, bf16[128,1024]{1,0:T(8,128)(2,1)S(1)}, u32[]{:S(2)}, u32[]{:S(2)}) collective-permute-start(bf16[128,1024]{1,0:T(8,128)(2,1)S(1)} %collective-permute-done.14.refs_5_.refs_11_), channel_id=1, source_target_pairs={{0,16},{16,24},{24,8},{8,0},{1,17},{17,25},{25,9},{9,1},{2,18},{18... | collective-permute-start | bytes 786440 | tf_op jit(solution)/shard_map/z_ring/ppermute | solution.py:34
  46.4 9.7 %collective-permute-start.13 = (bf16[384,512]{1,0:T(8,128)(2,1)S(1)}, bf16[384,512]{1,0:T(8,128)(2,1)S(1)}, u32[]{:S(2)}, u32[]{:S(2)}) collective-permute-start(bf16[384,512]{1,0:T(8,128)(2,1)S(1)} %constant_dynamic-update-slice_fusion.refs_0_.refs_4_), channel_id=1, source_target_pairs={{0,1},{1,0},{2,3},{3,2},{4,5},{5,4},{6,7},{7,6},{8,9},{9,8},{10,11... | collective-permute-start | bytes 1179656 | tf_op jit(solution)/shard_map/z_far/ppermute | solution.py:24
  46.4 9.7 %collective-permute-start.21 = (bf16[384,512]{1,0:T(8,128)(2,1)S(1)}, bf16[384,512]{1,0:T(8,128)(2,1)S(1)}, u32[]{:S(2)}, u32[]{:S(2)}) collective-permute-start(bf16[384,512]{1,0:T(8,128)(2,1)S(1)} %collective-permute-done.15.refs_1_.refs_7_), channel_id=1, source_target_pairs={{0,1},{1,0},{2,3},{3,2},{4,5},{5,4},{6,7},{7,6},{8,9},{9,8},{10,11... | collective-permute-start | bytes 1179656 | tf_op jit(solution)/shard_map/z_far/ppermute | solution.py:24
  52.0 4.1 %collective-permute-start.20 = (bf16[384,512]{1,0:T(8,128)(2,1)S(1)}, bf16[384,512]{1,0:T(8,128)(2,1)S(1)}, u32[]{:S(2)}, u32[]{:S(2)}) collective-permute-start(bf16[384,512]{1,0:T(8,128)(2,1)S(1)} %collective-permute-done.19.refs_1_.refs_6_), channel_id=1, source_target_pairs={{0,1},{1,0},{2,3},{3,2},{4,5},{5,4},{6,7},{7,6},{8,9},{9,8},{10,11... | collective-permute-start | bytes 1179656 | tf_op jit(solution)/shard_map/z_far/ppermute | solution.py:24
  53.6 2.5 %collective-permute-start.18 = (bf16[384,512]{1,0:T(8,128)(2,1)S(1)}, bf16[384,512]{1,0:T(8,128)(2,1)S(1)}, u32[]{:S(2)}, u32[]{:S(2)}) collective-permute-start(bf16[384,512]{1,0:T(8,128)(2,1)S(1)} %collective-permute-done.16.refs_0_.refs_5_), channel_id=1, source_target_pairs={{0,1},{1,0},{2,3},{3,2},{4,5},{5,4},{6,7},{7,6},{8,9},{9,8},{10,11... | collective-permute-start | bytes 1179656 | tf_op jit(solution)/shard_map/z_far/ppermute | solution.py:24
  54.1 4.9 %collective-permute-start.22 = (f32[2,1024]{1,0:T(2,128)S(1)}, f32[2,1024]{1,0:T(2,128)S(1)}, u32[]{:S(2)}, u32[]{:S(2)}) collective-permute-start(f32[2,1024]{1,0:T(2,128)S(1)} %get-tuple-element.69), channel_id=1, source_target_pairs={{0,8},{16,0},{24,16},{8,24},{1,9},{17,1},{25,17},{9,25},{2,10},{18... | collective-permute-start | bytes 24584 | tf_op jit(solution)/shard_map/z_ring/ppermute | solution.py:34
  62.2 5.1 %collective-permute-start.26 = (f32[32,384]{1,0:T(8,128)S(1)}, f32[32,384]{1,0:T(8,128)S(1)}, u32[]{:S(2)}, u32[]{:S(2)}) collective-permute-start(f32[32,384]{1,0:T(8,128)S(1)} %get-tuple-element.103), channel_id=1, source_target_pairs={{0,6},{1,7},{2,4},{3,5},{4,2},{5,3},{6,0},{7,1},{8,14},{9,15},{10,... | collective-permute-start | bytes 147464 | tf_op jit(solution)/shard_map/kernel/ppermute | solution.py:24
  64.3 4.1 %collective-permute-start.25 = (f32[32,384]{1,0:T(8,128)S(1)}, f32[32,384]{1,0:T(8,128)S(1)}, u32[]{:S(2)}, u32[]{:S(2)}) collective-permute-start(f32[32,384]{1,0:T(8,128)S(1)} %get-tuple-element.104), channel_id=1, source_target_pairs={{0,4},{1,5},{2,6},{3,7},{4,0},{5,1},{6,2},{7,3},{8,12},{9,13},{10,... | collective-permute-start | bytes 147464 | tf_op jit(solution)/shard_map/kernel/ppermute | solution.py:24
  64.8 4.1 %collective-permute-start.24 = (f32[32,384]{1,0:T(8,128)S(1)}, f32[32,384]{1,0:T(8,128)S(1)}, u32[]{:S(2)}, u32[]{:S(2)}) collective-permute-start(f32[32,384]{1,0:T(8,128)S(1)} %get-tuple-element.102), channel_id=1, source_target_pairs={{0,2},{1,3},{2,0},{3,1},{4,6},{5,7},{6,4},{7,5},{8,10},{9,11},{10,... | collective-permute-start | bytes 147464 | tf_op jit(solution)/shard_map/kernel/ppermute | solution.py:24
  69.0 7.2 %collective-permute-start.29 = (bf16[32,384]{1,0:T(8,128)(2,1)S(1)}, bf16[32,384]{1,0:T(8,128)(2,1)S(1)}, u32[]{:S(2)}, u32[]{:S(2)}) collective-permute-start(bf16[32,384]{1,0:T(8,128)(2,1)S(1)} %get-tuple-element.98), channel_id=1, source_target_pairs={{0,8},{16,0},{24,16},{8,24},{1,9},{17,1},{25,17},{9,25},{2,10},{18... | collective-permute-start | bytes 73736 | tf_op jit(solution)/shard_map/kernel/ppermute | solution.py:34
  71.8 5.9 %collective-permute-start.28 = (bf16[32,384]{1,0:T(8,128)(2,1)S(1)}, bf16[32,384]{1,0:T(8,128)(2,1)S(1)}, u32[]{:S(2)}, u32[]{:S(2)}) collective-permute-start(bf16[32,384]{1,0:T(8,128)(2,1)S(1)} %get-tuple-element.98), channel_id=1, source_target_pairs={{0,24},{16,8},{24,0},{8,16},{1,25},{17,9},{25,1},{9,17},{2,26},{18... | collective-permute-start | bytes 73736 | tf_op jit(solution)/shard_map/kernel/ppermute | solution.py:34
  73.4 4.3 %collective-permute-start.27 = (bf16[32,384]{1,0:T(8,128)(2,1)S(1)}, bf16[32,384]{1,0:T(8,128)(2,1)S(1)}, u32[]{:S(2)}, u32[]{:S(2)}) collective-permute-start(bf16[32,384]{1,0:T(8,128)(2,1)S(1)} %get-tuple-element.98), channel_id=1, source_target_pairs={{0,16},{16,24},{24,8},{8,0},{1,17},{17,25},{25,9},{9,1},{2,18},{18... | collective-permute-start | bytes 73736 | tf_op jit(solution)/shard_map/kernel/ppermute | solution.py:34
  73.4 12.1 %collective-permute-start.37 = (bf16[128,1024]{1,0:T(8,128)(2,1)S(1)}, bf16[128,1024]{1,0:T(8,128)(2,1)S(1)}, u32[]{:S(2)}, u32[]{:S(2)}) collective-permute-start(bf16[128,1024]{1,0:T(8,128)(2,1)S(1)} %collective-permute-done.17.refs_6_.refs_13_), channel_id=1, source_target_pairs={{0,16},{16,24},{24,8},{8,0},{1,17},{17,25},{25,9},{9,1},{2,18},{18... | collective-permute-start | bytes 786440 | tf_op jit(solution)/shard_map/z_far/ppermute | solution.py:34
  77.7 4.7 %collective-permute-start.31 = (bf16[4,32,384]{2,1,0:T(8,128)(2,1)S(1)}, bf16[4,32,384]{2,1,0:T(8,128)(2,1)S(1)}, u32[]{:S(2)}, u32[]{:S(2)}) collective-permute-start(bf16[4,32,384]{2,1,0:T(8,128)(2,1)S(1)} %pad_maximum_fusion.refs_0_), channel_id=1, source_target_pairs={{0,2},{1,3},{2,0},{3,1},{4,6},{5,7},{6,4},{7,5},{8,10},{9,11},{10,... | collective-permute-start | bytes 294920 | tf_op jit(solution)/shard_map/kernel/ppermute | solution.py:24
  78.4 4.6 %collective-permute-start.33 = (bf16[4,32,384]{2,1,0:T(8,128)(2,1)S(1)}, bf16[4,32,384]{2,1,0:T(8,128)(2,1)S(1)}, u32[]{:S(2)}, u32[]{:S(2)}) collective-permute-start(bf16[4,32,384]{2,1,0:T(8,128)(2,1)S(1)} %pad_maximum_fusion.refs_0_), channel_id=1, source_target_pairs={{0,4},{1,5},{2,6},{3,7},{4,0},{5,1},{6,2},{7,3},{8,12},{9,13},{10,... | collective-permute-start | bytes 294920 | tf_op jit(solution)/shard_map/kernel/ppermute | solution.py:24
  80.0 5.5 %collective-permute-start.35 = (bf16[4,32,384]{2,1,0:T(8,128)(2,1)S(1)}, bf16[4,32,384]{2,1,0:T(8,128)(2,1)S(1)}, u32[]{:S(2)}, u32[]{:S(2)}) collective-permute-start(bf16[4,32,384]{2,1,0:T(8,128)(2,1)S(1)} %pad_maximum_fusion.refs_0_), channel_id=1, source_target_pairs={{0,6},{1,7},{2,4},{3,5},{4,2},{5,3},{6,0},{7,1},{8,14},{9,15},{10,... | collective-permute-start | bytes 294920 | tf_op jit(solution)/shard_map/kernel/ppermute | solution.py:24
  81.3 4.2 %collective-permute-start.30 = (bf16[4,32,384]{2,1,0:T(8,128)(2,1)S(1)}, bf16[4,32,384]{2,1,0:T(8,128)(2,1)S(1)}, u32[]{:S(2)}, u32[]{:S(2)}) collective-permute-start(bf16[4,32,384]{2,1,0:T(8,128)(2,1)S(1)} %pad_maximum_fusion.refs_0_), channel_id=1, source_target_pairs={{0,1},{1,0},{2,3},{3,2},{4,5},{5,4},{6,7},{7,6},{8,9},{9,8},{10,11... | collective-permute-start | bytes 294920 | tf_op jit(solution)/shard_map/kernel/ppermute | solution.py:24
  82.4 3.1 %collective-permute-start.32 = (bf16[4,32,384]{2,1,0:T(8,128)(2,1)S(1)}, bf16[4,32,384]{2,1,0:T(8,128)(2,1)S(1)}, u32[]{:S(2)}, u32[]{:S(2)}) collective-permute-start(bf16[4,32,384]{2,1,0:T(8,128)(2,1)S(1)} %collective-permute-done.31.refs_2_), channel_id=1, source_target_pairs={{0,1},{1,0},{2,3},{3,2},{4,5},{5,4},{6,7},{7,6},{8,9},{9,8},{10,11... | collective-permute-start | bytes 294920 | tf_op jit(solution)/shard_map/kernel/ppermute | solution.py:24
  83.1 2.4 %collective-permute-start.34 = (bf16[4,32,384]{2,1,0:T(8,128)(2,1)S(1)}, bf16[4,32,384]{2,1,0:T(8,128)(2,1)S(1)}, u32[]{:S(2)}, u32[]{:S(2)}) collective-permute-start(bf16[4,32,384]{2,1,0:T(8,128)(2,1)S(1)} %collective-permute-done.33.refs_4_), channel_id=1, source_target_pairs={{0,1},{1,0},{2,3},{3,2},{4,5},{5,4},{6,7},{7,6},{8,9},{9,8},{10,11... | collective-permute-start | bytes 294920 | tf_op jit(solution)/shard_map/kernel/ppermute | solution.py:24
  93.3 2.8 %collective-permute-start.38 = (bf16[4,272,512]{2,1,0:T(8,128)(2,1)S(1)}, bf16[4,272,512]{2,1,0:T(8,128)(2,1)S(1)}, u32[]{:S(2)}, u32[]{:S(2)}) collective-permute-start(bf16[4,272,512]{2,1,0:T(8,128)(2,1)S(1)} %d_act_matmul.2), channel_id=1, source_target_pairs={{0,1},{1,0},{2,3},{3,2},{4,5},{5,4},{6,7},{7,6},{8,9},{9,8},{10,11... | collective-permute-start | bytes 3342344 | tf_op jit(solution)/shard_map/d_act/ppermute | solution.py:24
  97.9 18.6 %collective-permute-start.39 = (bf16[272,512]{1,0:T(8,128)(2,1)S(1)}, bf16[272,512]{1,0:T(8,128)(2,1)S(1)}, u32[]{:S(2)}, u32[]{:S(2)}) collective-permute-start(bf16[272,512]{1,0:T(8,128)(2,1)S(1)} %get-tuple-element.75), channel_id=1, source_target_pairs={{0,2},{1,3},{2,0},{3,1},{4,6},{5,7},{6,4},{7,5},{8,10},{9,11},{10,... | collective-permute-start | bytes 835592 | tf_op jit(solution)/shard_map/d_act/ppermute | solution.py:24
  99.5 17.0 %collective-permute-start.40 = (bf16[272,512]{1,0:T(8,128)(2,1)S(1)}, bf16[272,512]{1,0:T(8,128)(2,1)S(1)}, u32[]{:S(2)}, u32[]{:S(2)}) collective-permute-start(bf16[272,512]{1,0:T(8,128)(2,1)S(1)} %get-tuple-element.76), channel_id=1, source_target_pairs={{0,4},{1,5},{2,6},{3,7},{4,0},{5,1},{6,2},{7,3},{8,12},{9,13},{10,... | collective-permute-start | bytes 835592 | tf_op jit(solution)/shard_map/d_act/ppermute | solution.py:24
  99.9 16.6 %collective-permute-start.41 = (bf16[272,512]{1,0:T(8,128)(2,1)S(1)}, bf16[272,512]{1,0:T(8,128)(2,1)S(1)}, u32[]{:S(2)}, u32[]{:S(2)}) collective-permute-start(bf16[272,512]{1,0:T(8,128)(2,1)S(1)} %get-tuple-element.77), channel_id=1, source_target_pairs={{0,6},{1,7},{2,4},{3,5},{4,2},{5,3},{6,0},{7,1},{8,14},{9,15},{10,... | collective-permute-start | bytes 835592 | tf_op jit(solution)/shard_map/d_act/ppermute | solution.py:24
  102.1 5.6 %collective-permute-start.42 = (bf16[128,512]{1,0:T(8,128)(2,1)S(1)}, bf16[128,512]{1,0:T(8,128)(2,1)S(1)}, u32[]{:S(2)}, u32[]{:S(2)}) collective-permute-start(bf16[128,512]{1,0:T(8,128)(2,1)S(1)} %get-tuple-element.82), channel_id=1, source_target_pairs={{0,16},{16,24},{24,8},{8,0},{1,17},{17,25},{25,9},{9,1},{2,18},{18... | collective-permute-start | bytes 393224 | tf_op jit(solution)/shard_map/z_ring/ppermute | solution.py:34
  103.3 9.7 %collective-permute-start.43 = (bf16[128,512]{1,0:T(8,128)(2,1)S(1)}, bf16[128,512]{1,0:T(8,128)(2,1)S(1)}, u32[]{:S(2)}, u32[]{:S(2)}) collective-permute-start(bf16[128,512]{1,0:T(8,128)(2,1)S(1)} %get-tuple-element.83), channel_id=1, source_target_pairs={{0,24},{16,8},{24,0},{8,16},{1,25},{17,9},{25,1},{9,17},{2,26},{18... | collective-permute-start | bytes 393224 | tf_op jit(solution)/shard_map/z_ring/ppermute | solution.py:34
  107.7 8.8 %collective-permute-start.44 = (bf16[128,512]{1,0:T(8,128)(2,1)S(1)}, bf16[128,512]{1,0:T(8,128)(2,1)S(1)}, u32[]{:S(2)}, u32[]{:S(2)}) collective-permute-start(bf16[128,512]{1,0:T(8,128)(2,1)S(1)} %get-tuple-element.84), channel_id=1, source_target_pairs={{0,8},{16,0},{24,16},{8,24},{1,9},{17,1},{25,17},{9,25},{2,10},{18... | collective-permute-start | bytes 393224 | tf_op jit(solution)/shard_map/z_ring/ppermute | solution.py:34
  117.2 6.5 %collective-permute-start.46 = (f32[8,512]{1,0:T(8,128)S(1)}, f32[8,512]{1,0:T(8,128)S(1)}, u32[]{:S(2)}, u32[]{:S(2)}) collective-permute-start(f32[8,512]{1,0:T(8,128)S(1)} %pad_maximum_fusion.1), channel_id=1, source_target_pairs={{0,16},{8,24},{16,0},{24,8},{1,17},{9,25},{17,1},{25,9},{2,18},{10... | collective-permute-start | bytes 49160 | tf_op jit(solution)/shard_map/norm_backward/ppermute | solution.py:24
  117.3 6.5 %collective-permute-start.47 = (f32[8,512]{1,0:T(8,128)S(1)}, f32[8,512]{1,0:T(8,128)S(1)}, u32[]{:S(2)}, u32[]{:S(2)}) collective-permute-start(f32[8,512]{1,0:T(8,128)S(1)} %pad_maximum_fusion.1), channel_id=1, source_target_pairs={{0,24},{8,16},{16,8},{24,0},{1,25},{9,17},{17,9},{25,1},{2,26},{10... | collective-permute-start | bytes 49160 | tf_op jit(solution)/shard_map/norm_backward/ppermute | solution.py:24
  119.0 4.7 %collective-permute-start.45 = (f32[8,512]{1,0:T(8,128)S(1)}, f32[8,512]{1,0:T(8,128)S(1)}, u32[]{:S(2)}, u32[]{:S(2)}) collective-permute-start(f32[8,512]{1,0:T(8,128)S(1)} %pad_maximum_fusion.1), channel_id=1, source_target_pairs={{0,8},{8,0},{16,24},{24,16},{1,9},{9,1},{17,25},{25,17},{2,10},{10... | collective-permute-start | bytes 49160 | tf_op jit(solution)/shard_map/norm_backward/ppermute | solution.py:24
  120.7 5.2 %collective-permute-start.48 = (bf16[128,512]{1,0:T(8,128)(2,1)S(1)}, bf16[128,512]{1,0:T(8,128)(2,1)S(1)}, u32[]{:S(2)}, u32[]{:S(2)}) collective-permute-start(bf16[128,512]{1,0:T(8,128)(2,1)S(1)} %collective-permute-done.42.refs_4_), channel_id=1, source_target_pairs={{0,1},{1,0},{2,3},{3,2},{4,5},{5,4},{6,7},{7,6},{8,9},{9,8},{10,11... | collective-permute-start | bytes 393224 | tf_op jit(solution)/shard_map/grad_weight/ppermute | solution.py:24
  120.8 5.2 %collective-permute-start.49 = (bf16[128,512]{1,0:T(8,128)(2,1)S(1)}, bf16[128,512]{1,0:T(8,128)(2,1)S(1)}, u32[]{:S(2)}, u32[]{:S(2)}) collective-permute-start(bf16[128,512]{1,0:T(8,128)(2,1)S(1)} %collective-permute-done.43.refs_5_), channel_id=1, source_target_pairs={{0,1},{1,0},{2,3},{3,2},{4,5},{5,4},{6,7},{7,6},{8,9},{9,8},{10,11... | collective-permute-start | bytes 393224 | tf_op jit(solution)/shard_map/grad_weight/ppermute | solution.py:24
  (6 other events, 34.3 us)

commit v10 on v7

--- a/solution.py
+++ b/solution.py
@@ -109,11 +109,8 @@
         rest[0][...] = total
         return
     z = total.astype(bf16)
-    *z_refs, sum_ref = rest
-    for v, ref in enumerate(z_refs):
-        mine = z[v * local_rows : (v + 1) * local_rows]
-        ref[...] = mine
-        sum_ref[v : v + 1, :] = jnp.sum(mine.astype(f32), axis=0, keepdims=True)
+    for v, ref in enumerate(rest):
+        ref[...] = z[v * local_rows : (v + 1) * local_rows]
 
 
 def z_call(place, ks, pieces, weight, before, last, local_rows):
@@ -124,7 +121,6 @@
     if last:
         groups = tall // local_rows
         out_shape = (jax.ShapeDtypeStruct((local_rows, columns), bf16),) * groups
-        out_shape += (jax.ShapeDtypeStruct((groups, columns), f32),)
     else:
         out_shape = jax.ShapeDtypeStruct((tall, columns), f32)
     return pl.pallas_call(
@@ -138,43 +134,49 @@
     )(*operands)
 
 
-def strip_kernel(n_batch, n_slots, rows, n_col, place_ref, *refs):
-    z_refs = [refs[:n_batch], refs[n_batch : n_batch + n_slots]]
-    sum_refs = refs[n_batch + n_slots : 2 * n_batch]
-    even_ref, odd_ref, strip = refs[2 * n_batch :]
-    local_rows = z_refs[0][0].shape[0]
+def upper_blocks(n):
+    return [(s, t) for s in range(n) for t in range(s, n)]
+
+
+def strip_kernel(n_batch, n_col, place_ref, *refs):
+    z_refs, (even_ref, odd_ref, strip) = refs[: 2 * n_batch], refs[2 * n_batch :]
+    local_rows = z_refs[0].shape[0]
+    rows = local_rows * n_batch
     for v in range(2):
-        here = pl.ds(v * local_rows, local_rows)
-        zf = [z[...].astype(f32) for z in z_refs[v]]
-        total = sum(jnp.sum(z, axis=0, keepdims=True) for z in zf)
-        if v == 1:
-            total = total + sum(s[1:2] for s in sum_refs)
-        mean = total / rows
-        rounded = [(z - mean).astype(bf16) for z in zf[:n_slots]]
-        for u in range(n_slots):
-            strip[here, pl.ds(u * local_rows, local_rows)] = lax.dot_general(
-                rounded[0], rounded[u], (((1,), (1,)), ((), ())), preferred_element_type=f32
+        zf = [z[...].astype(f32) for z in z_refs[v::2]]
+        mean = sum(jnp.sum(z, axis=0, keepdims=True) for z in zf) / rows
+        rounded = jnp.concatenate([(z - mean).astype(bf16) for z in zf], axis=0)
+        at = 0
+        for s in range(n_batch):
+            product = lax.dot_general(
+                rounded[s * local_rows : (s + 1) * local_rows],
+                rounded[s * local_rows :],
+                (((1,), (1,)), ((), ())),
+                preferred_element_type=f32,
             )
+            strip[pl.ds(v * local_rows, local_rows), pl.ds(at, product.shape[1])] = product
+            at += product.shape[1]
     part = 2 * local_rows // n_col
     for k in range(n_col):
         start = pl.multiple_of((place_ref[1] ^ k) * part, part)
         (odd_ref if k % 2 else even_ref)[k // 2] = strip[pl.ds(start, part), :]
 
 
-def strip_call(place, z0, z1, sums, rows, n_col):
-    local_rows, columns = z0[0].shape
+def strip_call(place, z_slots, n_col):
+    n_batch = len(z_slots)
+    local_rows, columns = z_slots[0][0].shape
     tall = 2 * local_rows
-    wide = len(z1) * local_rows
+    wide = len(upper_blocks(n_batch)) * local_rows
     part = jax.ShapeDtypeStruct((n_col // 2, tall // n_col, wide), f32)
-    operands = [place] + list(z0) + list(z1) + list(sums)
+    operands = [place] + [z for slot in z_slots for z in slot]
     return pl.pallas_call(
-        functools.partial(strip_kernel, len(z0), len(z1), rows, n_col),
+        functools.partial(strip_kernel, n_batch, n_col),
         out_shape=(part, part),
         in_specs=[IN_SMEM] + [IN_VMEM] * (len(operands) - 1),
         out_specs=(IN_VMEM, IN_VMEM),
         scratch_shapes=[pltpu.VMEM((tall, wide), f32)],
-        compiler_params=params(12),
-        cost_estimate=cost(2 * tall * wide * columns, 2 * tall * columns * len(z0)),
+        compiler_params=params(18),
+        cost_estimate=cost(2 * tall * wide * columns, 2 * tall * columns * n_batch),
         name="kernel_strip",
     )(*operands)
 
@@ -186,29 +188,25 @@
     dz_ref, share_ref, strips, full, centred = refs[n_col + 2 * n_batch :]
     local_rows, columns = z_refs[0].shape
     rows = local_rows * n_batch
-    reach = n_batch // 2
     own = own_ref[...]
     block = lax.broadcasted_iota(jnp.int32, own.shape, 1) // local_rows
-    own = own * own * jnp.where((block > 0) & (block < n_batch - reach), 2.0, 1.0)
+    on_diagonal = functools.reduce(
+        jnp.logical_or, [block == i for i, (s, t) in enumerate(upper_blocks(n_batch)) if s == t]
+    )
+    own = own * own * jnp.where(on_diagonal, 1.0, 2.0)
     own = jnp.sum(jnp.sum(own, axis=0, keepdims=True), axis=1, keepdims=True)
     share_ref[...] = jnp.broadcast_to(block_share * own, share_ref.shape)
     part = 2 * local_rows // n_col
     for k in range(n_col):
         start = pl.multiple_of((place_ref[1] ^ k) * part, part)
-        for s in range(n_batch):
-            strips[s, pl.ds(start, part), :] = strip_refs[k][s].astype(f32)
+        strips[pl.ds(start, part), :] = strip_refs[k][...].astype(f32)
     for v in range(2):
-        for s in range(n_batch):
-            here = pl.ds(s * local_rows, local_rows)
-            for u in range(reach + 1):
-                t = (s + u) % n_batch
-                there = pl.ds(t * local_rows, local_rows)
-                block = strips[
-                    s, pl.ds(v * local_rows, local_rows), pl.ds(u * local_rows, local_rows)
-                ]
-                full[v, here, there] = block.astype(bf16)
-                if 0 < u < n_batch - reach:
-                    full[v, there, here] = jnp.transpose(block).astype(bf16)
+        for i, (s, t) in enumerate(upper_blocks(n_batch)):
+            here, there = pl.ds(s * local_rows, local_rows), pl.ds(t * local_rows, local_rows)
+            block = strips[pl.ds(v * local_rows, local_rows), pl.ds(i * local_rows, local_rows)]
+            full[v, here, there] = block.astype(bf16)
+            if s < t:
+                full[v, there, here] = jnp.transpose(block).astype(bf16)
 
     def one_tile(j, carry):
         here = pl.ds(pl.multiple_of(j * tile, tile), tile)
@@ -258,7 +256,7 @@
         in_specs=[IN_SMEM] + [IN_VMEM] * (len(operands) - 1),
         out_specs=(IN_VMEM, IN_VMEM),
         scratch_shapes=[
-            pltpu.VMEM((n_batch, tall, strips[0].shape[2]), f32),
+            pltpu.VMEM((tall, strips[0].shape[1]), f32),
             pltpu.VMEM((2, rows, rows), bf16),
             pltpu.VMEM((rows, tile), bf16),
         ],
@@ -477,7 +475,6 @@
     E = columns * n_col
     rows = local_rows * n_batch
     tall = n_view * local_rows
-    reach = n_batch // 2
     scale = rows * E / 128.0
     denom = float((rows - 1) ** 2 * E)
     evens = list(range(0, n_col, 2))
@@ -508,11 +505,10 @@
         first, pieces[1] = lax.optimization_barrier((act[0], pieces[1]))
         others = [ring_send(first, "batch", d) for d in range(1, n_batch)]
         pieces = sibling_pieces(pieces, n_col)
-        far_pieces = gather_pieces(jnp.concatenate(others), n_col)
+        far_pieces = link_pieces(jnp.concatenate(others), n_col)
     with jax.named_scope("z"):
 
-        def z_of(source, groups):
-            total = None
+        def z_of(source, groups, total=None):
             for i, ks in enumerate(groups):
                 total = z_call(
                     place,
@@ -525,31 +521,36 @@
                 )
             return total
 
-        z_own0, z_own1, z_sum = z_of(pieces, [[0, 1], far, [k + 1 for k in far]])
-        *z_far, _ = z_of(far_pieces, [evens, odds])
+        z_own0, z_own1 = z_of(pieces, [[0, 1], far, [k + 1 for k in far]])
     with jax.named_scope("z_ring"):
-        z_ring = [z_own1]
-        for _ in range(1, n_batch):
+        z_ring = [z_own1, ring_send(z_own1, "batch", 1)]
+        z_ring[1], far_pieces[far[-1]] = lax.optimization_barrier((z_ring[1], far_pieces[far[-1]]))
+        z_ring.append(ring_send(z_ring[1], "batch", 1))
+    with jax.named_scope("z_far"):
+        start = z_call(
+            place, [0, far[-1]], [far_pieces[0], far_pieces[far[-1]]], held_weight, None, False, local_rows
+        )
+        start, far_pieces[far[0]], z_ring[2] = lax.optimization_barrier(
+            (start, far_pieces[far[0]], z_ring[2])
+        )
+        far_pieces = sibling_pieces(far_pieces, n_col)
+        for _ in range(3, n_batch):
             z_ring.append(ring_send(z_ring[-1], "batch", 1))
-        sums = [ring_send(z_sum, "batch", d) for d in range(reach + 1, n_batch)]
-        z_flat = [z_own0] + z_far
+        z_far = z_of(far_pieces, [far[:-1], odds], start)
+        slots = list(zip([z_own0] + list(z_far), z_ring))
     with jax.named_scope("kernel"):
-        even_part, odd_part = strip_call(place, z_flat, z_ring[: reach + 1], sums, rows, n_col)
+        even_part, odd_part = strip_call(place, slots, n_col)
         even_part = even_part + xor_send(odd_part, "col", 1)
-        even_part, z_ring[reach + 1 :] = lax.optimization_barrier((even_part, z_ring[reach + 1 :]))
+        even_part, held_back = lax.optimization_barrier((even_part, [pieces[k] for k in evens]))
         strip = even_part[0]
         for k in far:
             strip = strip + xor_send(even_part[k // 2], "col", k)
-        slots = list(zip(z_flat, z_ring))
-        mine = strip.astype(bf16)
-        mine = jnp.stack([mine] + [ring_send(mine, "batch", d) for d in range(1, n_batch)])
-        mine, held_back = lax.optimization_barrier((mine, [pieces[k] for k in evens]))
-        strips = gather_pieces(mine, n_col)
         picked = pick_call(place, held_back, n_batch, n_col)
         blocks = [
             ring_send(x, "batch", 1 + i % (n_batch - 1)) for i, x in enumerate(picked)
         ]
-        strips, blocks[0] = lax.optimization_barrier((strips, blocks[0]))
+        strips = gather_pieces(strip.astype(bf16), n_col)
+        strips, blocks = lax.optimization_barrier((strips, blocks))
     with jax.named_scope("dz"):
         constants = (
             4.0 * scale / denom,
@@ -558,10 +559,9 @@
             25.0 / (rows * E) / n_batch,
             25.0 / (2 * E) / n_batch,
             1.0 / denom / n_batch,
-            1.0 / denom,
+            1.0 / denom / n_batch,
         )
         dz, share = dz_call(place, strip, [strips[k] for k in range(n_col)], slots, constants)
-        dz, blocks[1:] = lax.optimization_barrier((dz, blocks[1:]))
     with jax.named_scope("d_act"):
         (away,) = d_act_call(place, dz, share, held_weight, n_batch, n_col, None)
         got = xor_send(away, "col", 1)
@@ -583,7 +583,6 @@
                     grad_weight,
                 )
     with jax.named_scope("norm_backward"):
-        arrived, d_act, grad_weight = lax.optimization_barrier((arrived, d_act, grad_weight))
         share = exchange_sum(share_of(part[tall:]) for part in [d_act] + arrived)
         d_act = d_act[:tall]
         for part in arrived:

time: 133 us -> 126 us (0.947)
  starting transfers between devices: 46.6 us -> 40.9 us
  waiting for transfers between devices: 50.6 us -> 47.5 us
    ppermute x13 -> x9, starting transfers between devices: 16.8 us -> 11.4 us  [ring_send(): lax.ppermute(x, axis, [(order[i], order[(i + d) % n]) for i in range(n)])]
    ppermute x13 -> x9, waiting for transfers between devices: 13.9 us -> 9.23 us  [ring_send(): lax.ppermute(x, axis, [(order[i], order[(i + d) % n]) for i in range(n)])]
    ppermute x38, waiting for transfers between devices: 36.7 us -> 38.3 us  [xor_send(): return lax.ppermute(x, axis, [(i, i ^ k) for i in range(n)])]
    pallas_call x5 -> x6, Pallas kernels: 9.62 us -> 9.68 us  [z_call(): pl.pallas_call(functools.partial(z_kernel, tuple(ks), before is None, las...]
  transfers between devices with their start and end apart: 51 -> 47, of which waited for: 25 -> 19; matrix products, arithmetic and copies ran while one was open for 0% -> 1% of each run, Pallas kernels for 21% -> 16%
where the time goes in v10:
time: 126 us
  waiting for transfers between devices  47.5 us (38%)
  starting transfers between devices  40.9 us (32%)
  Pallas kernels  30.6 us (24%)
  other arithmetic  5.35 us (4%)
    ppermute x38, waiting for transfers between devices, xor_send(): return lax.ppermute(x, axis, [(i, i ^ k) for i in range(n)])  38.3 us
    ppermute x38, starting transfers between devices, xor_send(): return lax.ppermute(x, axis, [(i, i ^ k) for i in range(n)])  29.5 us
    ppermute x9, starting transfers between devices, ring_send(): lax.ppermute(x, axis, [(order[i], order[(i + d) % n]) for i in range(n)])  11.4 us
    pallas_call x6, Pallas kernels, z_call(): pl.pallas_call(functools.partial(z_kernel, tuple(ks), before is None, las...  9.68 us
    ppermute x9, waiting for transfers between devices, ring_send(): lax.ppermute(x, axis, [(order[i], order[(i + d) % n]) for i in range(n)])  9.23 us
    pallas_call x2, Pallas kernels, weight_grad_call(): pl.pallas_call(functools.partial(weight_grad_kernel, len(arrived), int(be...  5.79 us
    pallas_call x1, Pallas kernels, dz_call(): pl.pallas_call(functools.partial(dz_kernel, n_batch, n_col, tile, constan...  4.67 us
    pallas_call x2, Pallas kernels, d_act_call(): pl.pallas_call(functools.partial(d_act_kernel, count, (got is not None, n...  3.69 us
  transfers between devices with their start and end apart: 47, of which 19 were waited for; matrix products, arithmetic and copies ran while one was open for 1% of the time, Pallas kernels for 16%

profile of v10, /device:TPU:0, one launch (start us, length us, event | category | flops | bytes accessed | tf_op | source)
XLA Modules:
  0.0 125.6 jit_solution(16381498431740446199)
XLA Ops:
  0.7 1.0 convert_reduce_fusion
  1.7 1.0 fusion.8
  2.8 5.1 %collective-permute-start.2 = (f32[4,512]{1,0:T(4,128)S(1)}, f32[4,512]{1,0:T(4,128)S(1)}, u32[]{:S(2)}, u32[]{:S(2)}) collective-permute-start(f32[4,512]{1,0:T(4,128)S(1)} %pad_maximum_fusion.1), channel_id=1, source_target_pairs={{0,24},{8,16},{16,8},{24,0},{1,25},{9,17},{17,9},{25,1},{2,26},{10... | collective-permute-start | bytes 24584 | tf_op jit(solution)/shard_map/norm_stats/ppermute | solution.py:24
  8.6 3.5 %weight_load.1 = (bf16[4096,1024]{1,0:T(8,128)(2,1)S(1)}, f32[4,512]{1,0:T(4,128)S(1)}) custom-call(bf16[4096,1024]{1,0:T(8,128)(2,1)} %w_ref), custom_call_target="tpu_custom_call" | custom-call | bytes 16777216 | tf_op jit(solution)/shard_map/weight_load/weight_load/pallas_call | solution.py:78
  12.9 2.5 %collective-permute-start.7 = (bf16[256,512]{1,0:T(8,128)(2,1)S(1)}, bf16[256,512]{1,0:T(8,128)(2,1)S(1)}, u32[]{:S(2)}, u32[]{:S(2)}) collective-permute-start(bf16[256,512]{1,0:T(8,128)(2,1)S(1)} %bitcast.22), channel_id=1, source_target_pairs={{0,6},{1,7},{2,4},{3,5},{4,2},{5,3},{6,0},{7,1},{8,14},{9,15},{10,... | collective-permute-start | bytes 786440 | tf_op jit(solution)/shard_map/act_gather/ppermute | solution.py:24
  16.5 2.1 %collective-permute-start.10 = (bf16[128,512]{1,0:T(8,128)(2,1)S(1)}, bf16[128,512]{1,0:T(8,128)(2,1)S(1)}, u32[]{:S(2)}, u32[]{:S(2)}) collective-permute-start(bf16[128,512]{1,0:T(8,128)(2,1)S(1)} %slice_bitcast_fusion.3), channel_id=1, source_target_pairs={{0,16},{16,24},{24,8},{8,0},{1,17},{17,25},{25,9},{9,1},{2,18},{18... | collective-permute-start | bytes 393224 | tf_op jit(solution)/shard_map/act_gather/ppermute | solution.py:34
  18.5 1.4 %collective-permute-start.11 = (bf16[128,512]{1,0:T(8,128)(2,1)S(1)}, bf16[128,512]{1,0:T(8,128)(2,1)S(1)}, u32[]{:S(2)}, u32[]{:S(2)}) collective-permute-start(bf16[128,512]{1,0:T(8,128)(2,1)S(1)} %slice_bitcast_fusion.3), channel_id=1, source_target_pairs={{0,24},{16,8},{24,0},{8,16},{1,25},{17,9},{25,1},{9,17},{2,26},{18... | collective-permute-start | bytes 393224 | tf_op jit(solution)/shard_map/act_gather/ppermute | solution.py:34
  20.0 1.2 z_matmul.6.refs_4_
  21.2 1.8 %collective-permute-done.7.refs_2_.refs_3_ = bf16[256,512]{1,0:T(8,128)(2,1)S(1)} collective-permute-done((bf16[256,512]{1,0:T(8,128)(2,1)S(1)}, bf16[256,512]{1,0:T(8,128)(2,1)S(1)}, u32[]{:S(2)}, u32[]{:S(2)}) %collective-permute-start.7) | collective-permute-done | bytes 262176 | tf_op jit(solution)/shard_map/act_gather/ppermute | solution.py:24
  23.0 1.0 collective-permute-start.12
  24.0 4.1 %collective-permute-done.5.refs_1_.refs_2_ = bf16[256,512]{1,0:T(8,128)(2,1)S(1)} collective-permute-done((bf16[256,512]{1,0:T(8,128)(2,1)S(1)}, bf16[256,512]{1,0:T(8,128)(2,1)S(1)}, u32[]{:S(2)}, u32[]{:S(2)}) %collective-permute-start.5) | collective-permute-done | bytes 262176 | tf_op jit(solution)/shard_map/act_gather/ppermute | solution.py:24
  28.8 2.8 %collective-permute-done.12 = bf16[128,512]{1,0:T(8,128)(2,1)S(1)} collective-permute-done((bf16[128,512]{1,0:T(8,128)(2,1)S(1)}, bf16[128,512]{1,0:T(8,128)(2,1)S(1)}, u32[]{:S(2)}, u32[]{:S(2)}) %collective-permute-start.12) | collective-permute-done | bytes 131104 | tf_op jit(solution)/shard_map/act_gather/ppermute | solution.py:34
  31.6 2.5 %collective-permute-start.15 = (bf16[384,512]{1,0:T(8,128)(2,1)S(1)}, bf16[384,512]{1,0:T(8,128)(2,1)S(1)}, u32[]{:S(2)}, u32[]{:S(2)}) collective-permute-start(bf16[384,512]{1,0:T(8,128)(2,1)S(1)} %constant_dynamic-update-slice_fusion.refs_0_.refs_4_), channel_id=1, source_target_pairs={{0,6},{1,7},{2,4},{3,5},{4,2},{5,3},{6,0},{7,1},{8,14},{9,15},{10,... | collective-permute-start | bytes 1179656 | tf_op jit(solution)/shard_map/act_gather/ppermute | solution.py:24
  34.1 1.5 %z_matmul.7.refs_4_ = f32[256,1024]{1,0:T(8,128)S(1)} custom-call(s32[2]{0:T(128)S(1)} %pad_add_fusion.place_ref, bf16[256,512]{1,0:T(8,128)(2,1)S(1)} %collective-permute-done.3.refs_0_.refs_1_, bf16[256,512]{1,0:T(8,128)(2,1)S(1)} %collective-permute-done.5.refs_1_.refs_2_, bf16[256,512]{1,0:T(8,128)(2,1)S(1)} %collective-permute-done.7.refs_2_.refs_3_, ...), custom_call_target="tpu_custom_call" | custom-call | flops 805306368 | bytes 524288 | tf_op jit(solution)/shard_map/z/z_matmul/pallas_call | solution.py:126
  35.7 1.5 %z_matmul.8 = (bf16[128,1024]{1,0:T(8,128)(2,1)S(1)}, bf16[128,1024]{1,0:T(8,128)(2,1)S(1)}) custom-call(s32[2]{0:T(128)S(1)} %pad_add_fusion.place_ref, bf16[256,512]{1,0:T(8,128)(2,1)S(1)} %collective-permute-done.4.refs_0_.refs_1_, bf16[256,512]{1,0:T(8,128)(2,1)S(1)} %collective-permute-done.6.refs_1_.refs_2_, ...), custom_call_target="tpu_custom_call" | custom-call | flops 805306368 | bytes 524288 | tf_op jit(solution)/shard_map/z/z_matmul/pallas_call | solution.py:126
  38.4 6.2 %collective-permute-done.15.refs_1_.refs_7_ = bf16[384,512]{1,0:T(8,128)(2,1)S(1)} collective-permute-done((bf16[384,512]{1,0:T(8,128)(2,1)S(1)}, bf16[384,512]{1,0:T(8,128)(2,1)S(1)}, u32[]{:S(2)}, u32[]{:S(2)}) %collective-permute-start.15) | collective-permute-done | bytes 393248 | tf_op jit(solution)/shard_map/act_gather/ppermute | solution.py:24
  45.2 1.2 collective-permute-start.17
  46.9 5.1 %collective-permute-done.19.refs_1_.refs_6_ = bf16[384,512]{1,0:T(8,128)(2,1)S(1)} collective-permute-done((bf16[384,512]{1,0:T(8,128)(2,1)S(1)}, bf16[384,512]{1,0:T(8,128)(2,1)S(1)}, u32[]{:S(2)}, u32[]{:S(2)}) %collective-permute-start.19) | collective-permute-done | bytes 393248 | tf_op jit(solution)/shard_map/act_gather/ppermute | solution.py:24
  52.0 1.5 %z_matmul.9.refs_3_ = f32[384,1024]{1,0:T(8,128)S(1)} custom-call(s32[2]{0:T(128)S(1)} %pad_add_fusion.place_ref, bf16[384,512]{1,0:T(8,128)(2,1)S(1)} %constant_dynamic-update-slice_fusion.refs_0_.refs_4_, bf16[384,512]{1,0:T(8,128)(2,1)S(1)} %collective-permute-done.15.refs_1_.refs_7_, bf16[4096,1024]{1,0:T(8,128)(2,1)S(1)} %get-tuple-element.57.refs_2_.refs_3_.refs_4_.w_ref), custom_call_target="tpu_custom_call" | custom-call | flops 805306368 | bytes 786432 | tf_op jit(solution)/shard_map/z_far/z_matmul/pallas_call | solution.py:126
  54.7 1.5 %z_matmul.10.refs_5_ = f32[384,1024]{1,0:T(8,128)S(1)} custom-call(s32[2]{0:T(128)S(1)} %pad_add_fusion.place_ref, bf16[384,512]{1,0:T(8,128)(2,1)S(1)} %collective-permute-done.16.refs_0_.refs_5_, bf16[384,512]{1,0:T(8,128)(2,1)S(1)} %collective-permute-done.19.refs_1_.refs_6_, bf16[4096,1024]{1,0:T(8,128)(2,1)S(1)} %get-tuple-element.57.refs_2_.refs_3_.refs_4_.w_ref, ...), custom_call_target="tpu_custom_call" | custom-call | flops 805306368 | bytes 786432 | tf_op jit(solution)/shard_map/z_far/z_matmul/pallas_call | solution.py:126
  56.2 2.3 %z_matmul.11 = (bf16[128,1024]{1,0:T(8,128)(2,1)S(1)}, bf16[128,1024]{1,0:T(8,128)(2,1)S(1)}, bf16[128,1024]{1,0:T(8,128)(2,1)S(1)}) custom-call(s32[2]{0:T(128)S(1)} %pad_add_fusion.place_ref, bf16[384,512]{1,0:T(8,128)(2,1)S(1)} %collective-permute-done.13.refs_0_.refs_4_, bf16[384,512]{1,0:T(8,128)(2,1)S(1)} %collective-permute-done.18.refs_1_.refs_5_, ...), custom_call_target="tpu_custom_call" | custom-call | flops 1610612736 | bytes 786432 | tf_op jit(solution)/shard_map/z_far/z_matmul/pallas_call | solution.py:126
  58.6 3.8 %collective-permute-done.22.refs_7_.refs_15_ = bf16[128,1024]{1,0:T(8,128)(2,1)S(1)} collective-permute-done((bf16[128,1024]{1,0:T(8,128)(2,1)S(1)}, bf16[128,1024]{1,0:T(8,128)(2,1)S(1)}, u32[]{:S(2)}, u32[]{:S(2)}) %collective-permute-start.22) | collective-permute-done | bytes 262176 | tf_op jit(solution)/shard_map/z_far/ppermute | solution.py:34
  62.4 2.7 %kernel_strip.1 = (f32[4,32,1280]{2,1,0:T(8,128)S(1)}, f32[4,32,1280]{2,1,0:T(8,128)S(1)}) custom-call(s32[2]{0:T(128)S(1)} %pad_add_fusion.place_ref, bf16[128,1024]{1,0:T(8,128)(2,1)S(1)} %get-tuple-element.59.refs_0_.refs_8_, bf16[128,1024]{1,0:T(8,128)(2,1)S(1)} %get-tuple-element.60.refs_1_.refs_9_, ...), custom_call_target="tpu_custom_call" | custom-call | flops 671088640 | bytes 2097152 | tf_op jit(solution)/shard_map/kernel/kernel_strip/pallas_call | solution.py:172
  65.2 2.1 %collective-permute-done.23 = f32[4,32,1280]{2,1,0:T(8,128)S(1)} collective-permute-done((f32[4,32,1280]{2,1,0:T(8,128)S(1)}, f32[4,32,1280]{2,1,0:T(8,128)S(1)}, u32[]{:S(2)}, u32[]{:S(2)}) %collective-permute-start.23) | collective-permute-done | bytes 655392 | tf_op jit(solution)/shard_map/kernel/ppermute | solution.py:24
  67.4 1.6 %collective-permute-start.24 = (f32[32,1280]{1,0:T(8,128)S(1)}, f32[32,1280]{1,0:T(8,128)S(1)}, u32[]{:S(2)}, u32[]{:S(2)}) collective-permute-start(f32[32,1280]{1,0:T(8,128)S(1)} %get-tuple-element.106), channel_id=1, source_target_pairs={{0,2},{1,3},{2,0},{3,1},{4,6},{5,7},{6,4},{7,5},{8,10},{9,11},{10,... | collective-permute-start | bytes 491528 | tf_op jit(solution)/shard_map/kernel/ppermute | solution.py:24
  68.9 1.5 %collective-permute-start.26 = (f32[32,1280]{1,0:T(8,128)S(1)}, f32[32,1280]{1,0:T(8,128)S(1)}, u32[]{:S(2)}, u32[]{:S(2)}) collective-permute-start(f32[32,1280]{1,0:T(8,128)S(1)} %get-tuple-element.107), channel_id=1, source_target_pairs={{0,6},{1,7},{2,4},{3,5},{4,2},{5,3},{6,0},{7,1},{8,14},{9,15},{10,... | collective-permute-start | bytes 491528 | tf_op jit(solution)/shard_map/kernel/ppermute | solution.py:24
  71.6 1.9 %collective-permute-start.34 = (bf16[128,512]{1,0:T(8,128)(2,1)S(1)}, bf16[128,512]{1,0:T(8,128)(2,1)S(1)}, u32[]{:S(2)}, u32[]{:S(2)}) collective-permute-start(bf16[128,512]{1,0:T(8,128)(2,1)S(1)} %get-tuple-element.77), channel_id=1, source_target_pairs={{0,16},{16,24},{24,8},{8,0},{1,17},{17,25},{25,9},{9,1},{2,18},{18... | collective-permute-start | bytes 393224 | tf_op jit(solution)/shard_map/kernel/ppermute | solution.py:34
  73.5 2.2 %collective-permute-start.35 = (bf16[128,512]{1,0:T(8,128)(2,1)S(1)}, bf16[128,512]{1,0:T(8,128)(2,1)S(1)}, u32[]{:S(2)}, u32[]{:S(2)}) collective-permute-start(bf16[128,512]{1,0:T(8,128)(2,1)S(1)} %get-tuple-element.78), channel_id=1, source_target_pairs={{0,24},{16,8},{24,0},{8,16},{1,25},{17,9},{25,1},{9,17},{2,26},{18... | collective-permute-start | bytes 393224 | tf_op jit(solution)/shard_map/kernel/ppermute | solution.py:34
  75.7 2.6 %collective-permute-done.26 = f32[32,1280]{1,0:T(8,128)S(1)} collective-permute-done((f32[32,1280]{1,0:T(8,128)S(1)}, f32[32,1280]{1,0:T(8,128)S(1)}, u32[]{:S(2)}, u32[]{:S(2)}) %collective-permute-start.26) | collective-permute-done | bytes 163872 | tf_op jit(solution)/shard_map/kernel/ppermute | solution.py:24
  78.3 1.4 %collective-permute-done.25 = f32[32,1280]{1,0:T(8,128)S(1)} collective-permute-done((f32[32,1280]{1,0:T(8,128)S(1)}, f32[32,1280]{1,0:T(8,128)S(1)}, u32[]{:S(2)}, u32[]{:S(2)}) %collective-permute-start.25) | collective-permute-done | bytes 163872 | tf_op jit(solution)/shard_map/kernel/ppermute | solution.py:24
  79.7 1.5 %collective-permute-start.32 = (bf16[32,1280]{1,0:T(8,128)(2,1)S(1)}, bf16[32,1280]{1,0:T(8,128)(2,1)S(1)}, u32[]{:S(2)}, u32[]{:S(2)}) collective-permute-start(bf16[32,1280]{1,0:T(8,128)(2,1)S(1)} %get-tuple-element.80.refs_0_), channel_id=1, source_target_pairs={{0,6},{1,7},{2,4},{3,5},{4,2},{5,3},{6,0},{7,1},{8,14},{9,15},{10,... | collective-permute-start | bytes 245768 | tf_op jit(solution)/shard_map/kernel/ppermute | solution.py:24
  81.1 1.5 %collective-permute-start.30 = (bf16[32,1280]{1,0:T(8,128)(2,1)S(1)}, bf16[32,1280]{1,0:T(8,128)(2,1)S(1)}, u32[]{:S(2)}, u32[]{:S(2)}) collective-permute-start(bf16[32,1280]{1,0:T(8,128)(2,1)S(1)} %get-tuple-element.80.refs_0_), channel_id=1, source_target_pairs={{0,4},{1,5},{2,6},{3,7},{4,0},{5,1},{6,2},{7,3},{8,12},{9,13},{10,... | collective-permute-start | bytes 245768 | tf_op jit(solution)/shard_map/kernel/ppermute | solution.py:24
  83.2 1.0 collective-permute-start.36
  85.9 1.2 collective-permute-done.28.refs_2_
  87.1 2.0 %collective-permute-done.36.refs_10_ = bf16[128,512]{1,0:T(8,128)(2,1)S(1)} collective-permute-done((bf16[128,512]{1,0:T(8,128)(2,1)S(1)}, bf16[128,512]{1,0:T(8,128)(2,1)S(1)}, u32[]{:S(2)}, u32[]{:S(2)}) %collective-permute-start.36) | collective-permute-done | bytes 131104 | tf_op jit(solution)/shard_map/kernel/ppermute | solution.py:34
  89.1 4.7 %embedding_gradient.1 = (bf16[2,512,1024]{2,1,0:T(8,128)(2,1)S(1)}, f32[8,128]{1,0:T(8,128)S(1)}) custom-call(s32[2]{0:T(128)S(1)} %pad_add_fusion.place_ref, f32[32,1280]{1,0:T(8,128)S(1)} %get-tuple-element.103.own_ref, bf16[32,1280]{1,0:T(8,128)(2,1)S(1)} %get-tuple-element.80.refs_0_, bf16[32,1280]{1,0:T(8,128)(2,1)S(1)} %collective-permute-done.27.refs_1_, ...), custom_call_target="tpu_custom_call" | custom-call | flops 1073741824 | bytes 4194304 | tf_op jit(solution)/shard_map/dz/embedding_gradient/pallas_call | solution.py:250
  93.8 1.8 %d_act_matmul.2 = bf16[4,272,512]{2,1,0:T(8,128)(2,1)S(1)} custom-call(s32[2]{0:T(128)S(1)} %pad_add_fusion.place_ref, bf16[2,512,1024]{2,1,0:T(8,128)(2,1)S(1)} %get-tuple-element.88.dz_ref.refs_11_, f32[8,128]{1,0:T(8,128)S(1)} %get-tuple-element.89.share_ref, bf16[4096,1024]{1,0:T(8,128)(2,1)S(1)} %get-tuple-element.57.refs_2_.refs_3_.refs_4_.w_ref), custom_call_target="tpu_custom_call" | custom-call | flops 1073741824 | bytes 1048576 | tf_op jit(solution)/shard_map/d_act/d_act_matmul/pallas_call | solution.py:322
  95.7 2.7 %collective-permute-done.37.refs_0_ = bf16[4,272,512]{2,1,0:T(8,128)(2,1)S(1)} collective-permute-done((bf16[4,272,512]{2,1,0:T(8,128)(2,1)S(1)}, bf16[4,272,512]{2,1,0:T(8,128)(2,1)S(1)}, u32[]{:S(2)}, u32[]{:S(2)}) %collective-permute-start.37) | collective-permute-done | bytes 1114144 | tf_op jit(solution)/shard_map/d_act/ppermute | solution.py:24
  98.5 1.8 %d_act_matmul.3 = (bf16[272,512]{1,0:T(8,128)(2,1)S(1)}, bf16[272,512]{1,0:T(8,128)(2,1)S(1)}, bf16[272,512]{1,0:T(8,128)(2,1)S(1)}, f32[272,512]{1,0:T(8,128)S(1)}) custom-call(s32[2]{0:T(128)S(1)} %pad_add_fusion.place_ref, bf16[2,512,1024]{2,1,0:T(8,128)(2,1)S(1)} %get-tuple-element.88.dz_ref.refs_11_, f32[8,128]{1,0:T(8,128)S(1)} %get-tuple-element.89.share_ref, ...), custom_call_target="tpu_custom_call" | custom-call | flops 1073741824 | bytes 1048576 | tf_op jit(solution)/shard_map/d_act/d_act_matmul/pallas_call | solution.py:322
  100.3 1.5 %collective-permute-start.38 = (bf16[272,512]{1,0:T(8,128)(2,1)S(1)}, bf16[272,512]{1,0:T(8,128)(2,1)S(1)}, u32[]{:S(2)}, u32[]{:S(2)}) collective-permute-start(bf16[272,512]{1,0:T(8,128)(2,1)S(1)} %get-tuple-element.91), channel_id=1, source_target_pairs={{0,2},{1,3},{2,0},{3,1},{4,6},{5,7},{6,4},{7,5},{8,10},{9,11},{10,... | collective-permute-start | bytes 835592 | tf_op jit(solution)/shard_map/d_act/ppermute | solution.py:24
  102.4 1.5 %collective-permute-start.40 = (bf16[272,512]{1,0:T(8,128)(2,1)S(1)}, bf16[272,512]{1,0:T(8,128)(2,1)S(1)}, u32[]{:S(2)}, u32[]{:S(2)}) collective-permute-start(bf16[272,512]{1,0:T(8,128)(2,1)S(1)} %get-tuple-element.93), channel_id=1, source_target_pairs={{0,6},{1,7},{2,4},{3,5},{4,2},{5,3},{6,0},{7,1},{8,14},{9,15},{10,... | collective-permute-start | bytes 835592 | tf_op jit(solution)/shard_map/d_act/ppermute | solution.py:24
  104.4 2.9 %weight_gradient.2.refs_12_ = f32[1024,1024]{1,0:T(8,128)} custom-call(s32[2]{0:T(128)S(1)} %pad_add_fusion.place_ref, bf16[256,512]{1,0:T(8,128)(2,1)S(1)} %bitcast.27, bf16[256,512]{1,0:T(8,128)(2,1)S(1)} %collective-permute-done.3.refs_0_.refs_1_, bf16[256,512]{1,0:T(8,128)(2,1)S(1)} %collective-permute-done.5.refs_1_.refs_2_, ...), custom_call_target="tpu_custom_call" | custom-call | flops 1073741824 | bytes 2097152 | tf_op jit(solution)/shard_map/grad_weight/weight_gradient/pallas_call | solution.py:429
  107.3 2.6 %collective-permute-done.38 = bf16[272,512]{1,0:T(8,128)(2,1)S(1)} collective-permute-done((bf16[272,512]{1,0:T(8,128)(2,1)S(1)}, bf16[272,512]{1,0:T(8,128)(2,1)S(1)}, u32[]{:S(2)}, u32[]{:S(2)}) %collective-permute-start.38) | collective-permute-done | bytes 278560 | tf_op jit(solution)/shard_map/d_act/ppermute | solution.py:24
  109.9 6.4 %collective-permute-done.39 = bf16[272,512]{1,0:T(8,128)(2,1)S(1)} collective-permute-done((bf16[272,512]{1,0:T(8,128)(2,1)S(1)}, bf16[272,512]{1,0:T(8,128)(2,1)S(1)}, u32[]{:S(2)}, u32[]{:S(2)}) %collective-permute-start.39) | collective-permute-done | bytes 278560 | tf_op jit(solution)/shard_map/d_act/ppermute | solution.py:24
  117.3 2.2 %collective-permute-start.43 = (f32[8,512]{1,0:T(8,128)S(1)}, f32[8,512]{1,0:T(8,128)S(1)}, u32[]{:S(2)}, u32[]{:S(2)}) collective-permute-start(f32[8,512]{1,0:T(8,128)S(1)} %pad_maximum_fusion), channel_id=1, source_target_pairs={{0,24},{8,16},{16,8},{24,0},{1,25},{9,17},{17,9},{25,1},{2,26},{10... | collective-permute-start | bytes 49160 | tf_op jit(solution)/shard_map/norm_backward/ppermute | solution.py:24
  119.5 1.0 collective-permute-start.41
  120.5 2.9 %weight_gradient.3 = f32[1024,1024]{1,0:T(8,128)} custom-call(s32[2]{0:T(128)S(1)} %pad_add_fusion.place_ref, bf16[256,512]{1,0:T(8,128)(2,1)S(1)} %collective-permute-done.9.refs_1_.refs_0_, bf16[256,512]{1,0:T(8,128)(2,1)S(1)} %collective-permute-done.4.refs_0_.refs_1_, ...), custom_call_target="tpu_custom_call", output_to_operand_aliasing={{}: (13, {})} | custom-call | flops 1073741824 | bytes 2097152 | tf_op jit(solution)/shard_map/grad_weight/weight_gradient/pallas_call | solution.py:429
  124.6 1.0 fusion.22
  (89 shorter events, 13.6 us)
Async XLA Ops:
  2.8 9.7 %copy-start = (bf16[2,128,512]{2,1,0:T(8,128)(2,1)S(1)}, bf16[2,128,512]{2,1,0:T(8,128)(2,1)}, u32[]{:S(2)}) copy-start(bf16[2,128,512]{2,1,0:T(8,128)(2,1)} %param.4) | copy-start | bytes 786436
  2.8 9.2 %collective-permute-start.2 = (f32[4,512]{1,0:T(4,128)S(1)}, f32[4,512]{1,0:T(4,128)S(1)}, u32[]{:S(2)}, u32[]{:S(2)}) collective-permute-start(f32[4,512]{1,0:T(4,128)S(1)} %pad_maximum_fusion.1), channel_id=1, source_target_pairs={{0,24},{8,16},{16,8},{24,0},{1,25},{9,17},{17,9},{25,1},{2,26},{10... | collective-permute-start | bytes 24584 | tf_op jit(solution)/shard_map/norm_stats/ppermute | solution.py:24
  7.9 4.5 %collective-permute-start.1 = (f32[4,512]{1,0:T(4,128)S(1)}, f32[4,512]{1,0:T(4,128)S(1)}, u32[]{:S(2)}, u32[]{:S(2)}) collective-permute-start(f32[4,512]{1,0:T(4,128)S(1)} %pad_maximum_fusion.1), channel_id=1, source_target_pairs={{0,16},{8,24},{16,0},{24,8},{1,17},{9,25},{17,1},{25,9},{2,18},{10... | collective-permute-start | bytes 24584 | tf_op jit(solution)/shard_map/norm_stats/ppermute | solution.py:24
  7.9 4.5 %collective-permute-start = (f32[4,512]{1,0:T(4,128)S(1)}, f32[4,512]{1,0:T(4,128)S(1)}, u32[]{:S(2)}, u32[]{:S(2)}) collective-permute-start(f32[4,512]{1,0:T(4,128)S(1)} %pad_maximum_fusion.1), channel_id=1, source_target_pairs={{0,8},{8,0},{16,24},{24,16},{1,9},{9,1},{17,25},{25,17},{2,10},{10... | collective-permute-start | bytes 24584 | tf_op jit(solution)/shard_map/norm_stats/ppermute | solution.py:24
  12.8 3.6 %collective-permute-start.9 = (bf16[256,512]{1,0:T(8,128)(2,1)S(1)}, bf16[256,512]{1,0:T(8,128)(2,1)S(1)}, u32[]{:S(2)}, u32[]{:S(2)}) collective-permute-start(bf16[256,512]{1,0:T(8,128)(2,1)S(1)} %bitcast.21), channel_id=1, source_target_pairs={{0,1},{1,0},{2,3},{3,2},{4,5},{5,4},{6,7},{7,6},{8,9},{9,8},{10,11... | collective-permute-start | bytes 786440 | tf_op jit(solution)/shard_map/act_gather/ppermute | solution.py:24
  12.9 10.1 %collective-permute-start.7 = (bf16[256,512]{1,0:T(8,128)(2,1)S(1)}, bf16[256,512]{1,0:T(8,128)(2,1)S(1)}, u32[]{:S(2)}, u32[]{:S(2)}) collective-permute-start(bf16[256,512]{1,0:T(8,128)(2,1)S(1)} %bitcast.22), channel_id=1, source_target_pairs={{0,6},{1,7},{2,4},{3,5},{4,2},{5,3},{6,0},{7,1},{8,14},{9,15},{10,... | collective-permute-start | bytes 786440 | tf_op jit(solution)/shard_map/act_gather/ppermute | solution.py:24
  15.4 12.7 %collective-permute-start.5 = (bf16[256,512]{1,0:T(8,128)(2,1)S(1)}, bf16[256,512]{1,0:T(8,128)(2,1)S(1)}, u32[]{:S(2)}, u32[]{:S(2)}) collective-permute-start(bf16[256,512]{1,0:T(8,128)(2,1)S(1)} %bitcast.23), channel_id=1, source_target_pairs={{0,4},{1,5},{2,6},{3,7},{4,0},{5,1},{6,2},{7,3},{8,12},{9,13},{10,... | collective-permute-start | bytes 786440 | tf_op jit(solution)/shard_map/act_gather/ppermute | solution.py:24
  15.9 12.3 %collective-permute-start.3 = (bf16[256,512]{1,0:T(8,128)(2,1)S(1)}, bf16[256,512]{1,0:T(8,128)(2,1)S(1)}, u32[]{:S(2)}, u32[]{:S(2)}) collective-permute-start(bf16[256,512]{1,0:T(8,128)(2,1)S(1)} %bitcast.24), channel_id=1, source_target_pairs={{0,2},{1,3},{2,0},{3,1},{4,6},{5,7},{6,4},{7,5},{8,10},{9,11},{10,... | collective-permute-start | bytes 786440 | tf_op jit(solution)/shard_map/act_gather/ppermute | solution.py:24
  16.5 12.2 %collective-permute-start.10 = (bf16[128,512]{1,0:T(8,128)(2,1)S(1)}, bf16[128,512]{1,0:T(8,128)(2,1)S(1)}, u32[]{:S(2)}, u32[]{:S(2)}) collective-permute-start(bf16[128,512]{1,0:T(8,128)(2,1)S(1)} %slice_bitcast_fusion.3), channel_id=1, source_target_pairs={{0,16},{16,24},{24,8},{8,0},{1,17},{17,25},{25,9},{9,1},{2,18},{18... | collective-permute-start | bytes 393224 | tf_op jit(solution)/shard_map/act_gather/ppermute | solution.py:34
  18.5 10.2 %collective-permute-start.11 = (bf16[128,512]{1,0:T(8,128)(2,1)S(1)}, bf16[128,512]{1,0:T(8,128)(2,1)S(1)}, u32[]{:S(2)}, u32[]{:S(2)}) collective-permute-start(bf16[128,512]{1,0:T(8,128)(2,1)S(1)} %slice_bitcast_fusion.3), channel_id=1, source_target_pairs={{0,24},{16,8},{24,0},{8,16},{1,25},{17,9},{25,1},{9,17},{2,26},{18... | collective-permute-start | bytes 393224 | tf_op jit(solution)/shard_map/act_gather/ppermute | solution.py:34
  23.0 8.6 %collective-permute-start.12 = (bf16[128,512]{1,0:T(8,128)(2,1)S(1)}, bf16[128,512]{1,0:T(8,128)(2,1)S(1)}, u32[]{:S(2)}, u32[]{:S(2)}) collective-permute-start(bf16[128,512]{1,0:T(8,128)(2,1)S(1)} %slice_bitcast_fusion.3), channel_id=1, source_target_pairs={{0,8},{16,0},{24,16},{8,24},{1,9},{17,1},{25,17},{9,25},{2,10},{18... | collective-permute-start | bytes 393224 | tf_op jit(solution)/shard_map/act_gather/ppermute | solution.py:34
  28.1 7.5 %collective-permute-start.8 = (bf16[256,512]{1,0:T(8,128)(2,1)S(1)}, bf16[256,512]{1,0:T(8,128)(2,1)S(1)}, u32[]{:S(2)}, u32[]{:S(2)}) collective-permute-start(bf16[256,512]{1,0:T(8,128)(2,1)S(1)} %collective-permute-done.7.refs_2_.refs_3_), channel_id=1, source_target_pairs={{0,1},{1,0},{2,3},{3,2},{4,5},{5,4},{6,7},{7,6},{8,9},{9,8},{10,11... | collective-permute-start | bytes 786440 | tf_op jit(solution)/shard_map/act_gather/ppermute | solution.py:24
  28.2 7.4 %collective-permute-start.6 = (bf16[256,512]{1,0:T(8,128)(2,1)S(1)}, bf16[256,512]{1,0:T(8,128)(2,1)S(1)}, u32[]{:S(2)}, u32[]{:S(2)}) collective-permute-start(bf16[256,512]{1,0:T(8,128)(2,1)S(1)} %collective-permute-done.5.refs_1_.refs_2_), channel_id=1, source_target_pairs={{0,1},{1,0},{2,3},{3,2},{4,5},{5,4},{6,7},{7,6},{8,9},{9,8},{10,11... | collective-permute-start | bytes 786440 | tf_op jit(solution)/shard_map/act_gather/ppermute | solution.py:24
  28.6 7.0 %collective-permute-start.4 = (bf16[256,512]{1,0:T(8,128)(2,1)S(1)}, bf16[256,512]{1,0:T(8,128)(2,1)S(1)}, u32[]{:S(2)}, u32[]{:S(2)}) collective-permute-start(bf16[256,512]{1,0:T(8,128)(2,1)S(1)} %collective-permute-done.3.refs_0_.refs_1_), channel_id=1, source_target_pairs={{0,1},{1,0},{2,3},{3,2},{4,5},{5,4},{6,7},{7,6},{8,9},{9,8},{10,11... | collective-permute-start | bytes 786440 | tf_op jit(solution)/shard_map/act_gather/ppermute | solution.py:24
  31.6 13.0 %collective-permute-start.15 = (bf16[384,512]{1,0:T(8,128)(2,1)S(1)}, bf16[384,512]{1,0:T(8,128)(2,1)S(1)}, u32[]{:S(2)}, u32[]{:S(2)}) collective-permute-start(bf16[384,512]{1,0:T(8,128)(2,1)S(1)} %constant_dynamic-update-slice_fusion.refs_0_.refs_4_), channel_id=1, source_target_pairs={{0,6},{1,7},{2,4},{3,5},{4,2},{5,3},{6,0},{7,1},{8,14},{9,15},{10,... | collective-permute-start | bytes 1179656 | tf_op jit(solution)/shard_map/act_gather/ppermute | solution.py:24
  37.2 8.0 %collective-permute-start.14 = (bf16[128,1024]{1,0:T(8,128)(2,1)S(1)}, bf16[128,1024]{1,0:T(8,128)(2,1)S(1)}, u32[]{:S(2)}, u32[]{:S(2)}) collective-permute-start(bf16[128,1024]{1,0:T(8,128)(2,1)S(1)} %get-tuple-element.60.refs_1_.refs_9_), channel_id=1, source_target_pairs={{0,16},{16,24},{24,8},{8,0},{1,17},{17,25},{25,9},{9,1},{2,18},{18... | collective-permute-start | bytes 786440 | tf_op jit(solution)/shard_map/z_ring/ppermute | solution.py:34
  37.3 14.7 %collective-permute-start.19 = (bf16[384,512]{1,0:T(8,128)(2,1)S(1)}, bf16[384,512]{1,0:T(8,128)(2,1)S(1)}, u32[]{:S(2)}, u32[]{:S(2)}) collective-permute-start(bf16[384,512]{1,0:T(8,128)(2,1)S(1)} %constant_dynamic-update-slice_fusion.refs_0_.refs_4_), channel_id=1, source_target_pairs={{0,4},{1,5},{2,6},{3,7},{4,0},{5,1},{6,2},{7,3},{8,12},{9,13},{10,... | collective-permute-start | bytes 1179656 | tf_op jit(solution)/shard_map/act_gather/ppermute | solution.py:24
  37.8 15.7 %collective-permute-start.16 = (bf16[384,512]{1,0:T(8,128)(2,1)S(1)}, bf16[384,512]{1,0:T(8,128)(2,1)S(1)}, u32[]{:S(2)}, u32[]{:S(2)}) collective-permute-start(bf16[384,512]{1,0:T(8,128)(2,1)S(1)} %constant_dynamic-update-slice_fusion.refs_0_.refs_4_), channel_id=1, source_target_pairs={{0,2},{1,3},{2,0},{3,1},{4,6},{5,7},{6,4},{7,5},{8,10},{9,11},{10,... | collective-permute-start | bytes 1179656 | tf_op jit(solution)/shard_map/act_gather/ppermute | solution.py:24
  45.2 8.4 %collective-permute-start.17 = (bf16[128,1024]{1,0:T(8,128)(2,1)S(1)}, bf16[128,1024]{1,0:T(8,128)(2,1)S(1)}, u32[]{:S(2)}, u32[]{:S(2)}) collective-permute-start(bf16[128,1024]{1,0:T(8,128)(2,1)S(1)} %collective-permute-done.14.refs_3_.refs_11_), channel_id=1, source_target_pairs={{0,16},{16,24},{24,8},{8,0},{1,17},{17,25},{25,9},{9,1},{2,18},{18... | collective-permute-start | bytes 786440 | tf_op jit(solution)/shard_map/z_ring/ppermute | solution.py:34
  46.4 9.8 %collective-permute-start.13 = (bf16[384,512]{1,0:T(8,128)(2,1)S(1)}, bf16[384,512]{1,0:T(8,128)(2,1)S(1)}, u32[]{:S(2)}, u32[]{:S(2)}) collective-permute-start(bf16[384,512]{1,0:T(8,128)(2,1)S(1)} %constant_dynamic-update-slice_fusion.refs_0_.refs_4_), channel_id=1, source_target_pairs={{0,1},{1,0},{2,3},{3,2},{4,5},{5,4},{6,7},{7,6},{8,9},{9,8},{10,11... | collective-permute-start | bytes 1179656 | tf_op jit(solution)/shard_map/z_far/ppermute | solution.py:24
  46.4 9.8 %collective-permute-start.21 = (bf16[384,512]{1,0:T(8,128)(2,1)S(1)}, bf16[384,512]{1,0:T(8,128)(2,1)S(1)}, u32[]{:S(2)}, u32[]{:S(2)}) collective-permute-start(bf16[384,512]{1,0:T(8,128)(2,1)S(1)} %collective-permute-done.15.refs_1_.refs_7_), channel_id=1, source_target_pairs={{0,1},{1,0},{2,3},{3,2},{4,5},{5,4},{6,7},{7,6},{8,9},{9,8},{10,11... | collective-permute-start | bytes 1179656 | tf_op jit(solution)/shard_map/z_far/ppermute | solution.py:24
  52.0 4.2 %collective-permute-start.20 = (bf16[384,512]{1,0:T(8,128)(2,1)S(1)}, bf16[384,512]{1,0:T(8,128)(2,1)S(1)}, u32[]{:S(2)}, u32[]{:S(2)}) collective-permute-start(bf16[384,512]{1,0:T(8,128)(2,1)S(1)} %collective-permute-done.19.refs_1_.refs_6_), channel_id=1, source_target_pairs={{0,1},{1,0},{2,3},{3,2},{4,5},{5,4},{6,7},{7,6},{8,9},{9,8},{10,11... | collective-permute-start | bytes 1179656 | tf_op jit(solution)/shard_map/z_far/ppermute | solution.py:24
  53.6 2.7 %collective-permute-start.18 = (bf16[384,512]{1,0:T(8,128)(2,1)S(1)}, bf16[384,512]{1,0:T(8,128)(2,1)S(1)}, u32[]{:S(2)}, u32[]{:S(2)}) collective-permute-start(bf16[384,512]{1,0:T(8,128)(2,1)S(1)} %collective-permute-done.16.refs_0_.refs_5_), channel_id=1, source_target_pairs={{0,1},{1,0},{2,3},{3,2},{4,5},{5,4},{6,7},{7,6},{8,9},{9,8},{10,11... | collective-permute-start | bytes 1179656 | tf_op jit(solution)/shard_map/z_far/ppermute | solution.py:24
  54.1 8.3 %collective-permute-start.22 = (bf16[128,1024]{1,0:T(8,128)(2,1)S(1)}, bf16[128,1024]{1,0:T(8,128)(2,1)S(1)}, u32[]{:S(2)}, u32[]{:S(2)}) collective-permute-start(bf16[128,1024]{1,0:T(8,128)(2,1)S(1)} %collective-permute-done.17.refs_5_.refs_13_), channel_id=1, source_target_pairs={{0,16},{16,24},{24,8},{8,0},{1,17},{17,25},{25,9},{9,1},{2,18},{18... | collective-permute-start | bytes 786440 | tf_op jit(solution)/shard_map/z_far/ppermute | solution.py:34
  65.1 2.2 %collective-permute-start.23 = (f32[4,32,1280]{2,1,0:T(8,128)S(1)}, f32[4,32,1280]{2,1,0:T(8,128)S(1)}, u32[]{:S(2)}, u32[]{:S(2)}) collective-permute-start(f32[4,32,1280]{2,1,0:T(8,128)S(1)} %get-tuple-element.71), channel_id=1, source_target_pairs={{0,1},{1,0},{2,3},{3,2},{4,5},{5,4},{6,7},{7,6},{8,9},{9,8},{10,11... | collective-permute-start | bytes 1966088 | tf_op jit(solution)/shard_map/kernel/ppermute | solution.py:24
  67.4 8.3 %collective-permute-start.24 = (f32[32,1280]{1,0:T(8,128)S(1)}, f32[32,1280]{1,0:T(8,128)S(1)}, u32[]{:S(2)}, u32[]{:S(2)}) collective-permute-start(f32[32,1280]{1,0:T(8,128)S(1)} %get-tuple-element.106), channel_id=1, source_target_pairs={{0,2},{1,3},{2,0},{3,1},{4,6},{5,7},{6,4},{7,5},{8,10},{9,11},{10,... | collective-permute-start | bytes 491528 | tf_op jit(solution)/shard_map/kernel/ppermute | solution.py:24
  68.9 9.3 %collective-permute-start.26 = (f32[32,1280]{1,0:T(8,128)S(1)}, f32[32,1280]{1,0:T(8,128)S(1)}, u32[]{:S(2)}, u32[]{:S(2)}) collective-permute-start(f32[32,1280]{1,0:T(8,128)S(1)} %get-tuple-element.107), channel_id=1, source_target_pairs={{0,6},{1,7},{2,4},{3,5},{4,2},{5,3},{6,0},{7,1},{8,14},{9,15},{10,... | collective-permute-start | bytes 491528 | tf_op jit(solution)/shard_map/kernel/ppermute | solution.py:24
  70.4 9.2 %collective-permute-start.25 = (f32[32,1280]{1,0:T(8,128)S(1)}, f32[32,1280]{1,0:T(8,128)S(1)}, u32[]{:S(2)}, u32[]{:S(2)}) collective-permute-start(f32[32,1280]{1,0:T(8,128)S(1)} %get-tuple-element.108), channel_id=1, source_target_pairs={{0,4},{1,5},{2,6},{3,7},{4,0},{5,1},{6,2},{7,3},{8,12},{9,13},{10,... | collective-permute-start | bytes 491528 | tf_op jit(solution)/shard_map/kernel/ppermute | solution.py:24
  71.6 11.6 %collective-permute-start.34 = (bf16[128,512]{1,0:T(8,128)(2,1)S(1)}, bf16[128,512]{1,0:T(8,128)(2,1)S(1)}, u32[]{:S(2)}, u32[]{:S(2)}) collective-permute-start(bf16[128,512]{1,0:T(8,128)(2,1)S(1)} %get-tuple-element.77), channel_id=1, source_target_pairs={{0,16},{16,24},{24,8},{8,0},{1,17},{17,25},{25,9},{9,1},{2,18},{18... | collective-permute-start | bytes 393224 | tf_op jit(solution)/shard_map/kernel/ppermute | solution.py:34
  73.5 10.7 %collective-permute-start.35 = (bf16[128,512]{1,0:T(8,128)(2,1)S(1)}, bf16[128,512]{1,0:T(8,128)(2,1)S(1)}, u32[]{:S(2)}, u32[]{:S(2)}) collective-permute-start(bf16[128,512]{1,0:T(8,128)(2,1)S(1)} %get-tuple-element.78), channel_id=1, source_target_pairs={{0,24},{16,8},{24,0},{8,16},{1,25},{17,9},{25,1},{9,17},{2,26},{18... | collective-permute-start | bytes 393224 | tf_op jit(solution)/shard_map/kernel/ppermute | solution.py:34
  79.7 5.4 %collective-permute-start.32 = (bf16[32,1280]{1,0:T(8,128)(2,1)S(1)}, bf16[32,1280]{1,0:T(8,128)(2,1)S(1)}, u32[]{:S(2)}, u32[]{:S(2)}) collective-permute-start(bf16[32,1280]{1,0:T(8,128)(2,1)S(1)} %get-tuple-element.80.refs_0_), channel_id=1, source_target_pairs={{0,6},{1,7},{2,4},{3,5},{4,2},{5,3},{6,0},{7,1},{8,14},{9,15},{10,... | collective-permute-start | bytes 245768 | tf_op jit(solution)/shard_map/kernel/ppermute | solution.py:24
  81.1 4.8 %collective-permute-start.30 = (bf16[32,1280]{1,0:T(8,128)(2,1)S(1)}, bf16[32,1280]{1,0:T(8,128)(2,1)S(1)}, u32[]{:S(2)}, u32[]{:S(2)}) collective-permute-start(bf16[32,1280]{1,0:T(8,128)(2,1)S(1)} %get-tuple-element.80.refs_0_), channel_id=1, source_target_pairs={{0,4},{1,5},{2,6},{3,7},{4,0},{5,1},{6,2},{7,3},{8,12},{9,13},{10,... | collective-permute-start | bytes 245768 | tf_op jit(solution)/shard_map/kernel/ppermute | solution.py:24
  82.7 4.4 %collective-permute-start.28 = (bf16[32,1280]{1,0:T(8,128)(2,1)S(1)}, bf16[32,1280]{1,0:T(8,128)(2,1)S(1)}, u32[]{:S(2)}, u32[]{:S(2)}) collective-permute-start(bf16[32,1280]{1,0:T(8,128)(2,1)S(1)} %get-tuple-element.80.refs_0_), channel_id=1, source_target_pairs={{0,2},{1,3},{2,0},{3,1},{4,6},{5,7},{6,4},{7,5},{8,10},{9,11},{10,... | collective-permute-start | bytes 245768 | tf_op jit(solution)/shard_map/kernel/ppermute | solution.py:24
  83.2 5.9 %collective-permute-start.36 = (bf16[128,512]{1,0:T(8,128)(2,1)S(1)}, bf16[128,512]{1,0:T(8,128)(2,1)S(1)}, u32[]{:S(2)}, u32[]{:S(2)}) collective-permute-start(bf16[128,512]{1,0:T(8,128)(2,1)S(1)} %get-tuple-element.79), channel_id=1, source_target_pairs={{0,8},{16,0},{24,16},{8,24},{1,9},{17,1},{25,17},{9,25},{2,10},{18... | collective-permute-start | bytes 393224 | tf_op jit(solution)/shard_map/kernel/ppermute | solution.py:34
  84.2 4.8 %collective-permute-start.27 = (bf16[32,1280]{1,0:T(8,128)(2,1)S(1)}, bf16[32,1280]{1,0:T(8,128)(2,1)S(1)}, u32[]{:S(2)}, u32[]{:S(2)}) collective-permute-start(bf16[32,1280]{1,0:T(8,128)(2,1)S(1)} %get-tuple-element.80.refs_0_), channel_id=1, source_target_pairs={{0,1},{1,0},{2,3},{3,2},{4,5},{5,4},{6,7},{7,6},{8,9},{9,8},{10,11... | collective-permute-start | bytes 245768 | tf_op jit(solution)/shard_map/kernel/ppermute | solution.py:24
  85.1 4.0 %collective-permute-start.33 = (bf16[32,1280]{1,0:T(8,128)(2,1)S(1)}, bf16[32,1280]{1,0:T(8,128)(2,1)S(1)}, u32[]{:S(2)}, u32[]{:S(2)}) collective-permute-start(bf16[32,1280]{1,0:T(8,128)(2,1)S(1)} %collective-permute-done.32.refs_6_), channel_id=1, source_target_pairs={{0,1},{1,0},{2,3},{3,2},{4,5},{5,4},{6,7},{7,6},{8,9},{9,8},{10,11... | collective-permute-start | bytes 245768 | tf_op jit(solution)/shard_map/kernel/ppermute | solution.py:24
  85.9 3.2 %collective-permute-start.31 = (bf16[32,1280]{1,0:T(8,128)(2,1)S(1)}, bf16[32,1280]{1,0:T(8,128)(2,1)S(1)}, u32[]{:S(2)}, u32[]{:S(2)}) collective-permute-start(bf16[32,1280]{1,0:T(8,128)(2,1)S(1)} %collective-permute-done.30.refs_4_), channel_id=1, source_target_pairs={{0,1},{1,0},{2,3},{3,2},{4,5},{5,4},{6,7},{7,6},{8,9},{9,8},{10,11... | collective-permute-start | bytes 245768 | tf_op jit(solution)/shard_map/kernel/ppermute | solution.py:24
  87.1 2.0 %collective-permute-start.29 = (bf16[32,1280]{1,0:T(8,128)(2,1)S(1)}, bf16[32,1280]{1,0:T(8,128)(2,1)S(1)}, u32[]{:S(2)}, u32[]{:S(2)}) collective-permute-start(bf16[32,1280]{1,0:T(8,128)(2,1)S(1)} %collective-permute-done.28.refs_2_), channel_id=1, source_target_pairs={{0,1},{1,0},{2,3},{3,2},{4,5},{5,4},{6,7},{7,6},{8,9},{9,8},{10,11... | collective-permute-start | bytes 245768 | tf_op jit(solution)/shard_map/kernel/ppermute | solution.py:24
  95.6 2.8 %collective-permute-start.37 = (bf16[4,272,512]{2,1,0:T(8,128)(2,1)S(1)}, bf16[4,272,512]{2,1,0:T(8,128)(2,1)S(1)}, u32[]{:S(2)}, u32[]{:S(2)}) collective-permute-start(bf16[4,272,512]{2,1,0:T(8,128)(2,1)S(1)} %d_act_matmul.2), channel_id=1, source_target_pairs={{0,1},{1,0},{2,3},{3,2},{4,5},{5,4},{6,7},{7,6},{8,9},{9,8},{10,11... | collective-permute-start | bytes 3342344 | tf_op jit(solution)/shard_map/d_act/ppermute | solution.py:24
  100.3 9.6 %collective-permute-start.38 = (bf16[272,512]{1,0:T(8,128)(2,1)S(1)}, bf16[272,512]{1,0:T(8,128)(2,1)S(1)}, u32[]{:S(2)}, u32[]{:S(2)}) collective-permute-start(bf16[272,512]{1,0:T(8,128)(2,1)S(1)} %get-tuple-element.91), channel_id=1, source_target_pairs={{0,2},{1,3},{2,0},{3,1},{4,6},{5,7},{6,4},{7,5},{8,10},{9,11},{10,... | collective-permute-start | bytes 835592 | tf_op jit(solution)/shard_map/d_act/ppermute | solution.py:24
  101.8 14.4 %collective-permute-start.39 = (bf16[272,512]{1,0:T(8,128)(2,1)S(1)}, bf16[272,512]{1,0:T(8,128)(2,1)S(1)}, u32[]{:S(2)}, u32[]{:S(2)}) collective-permute-start(bf16[272,512]{1,0:T(8,128)(2,1)S(1)} %get-tuple-element.92), channel_id=1, source_target_pairs={{0,4},{1,5},{2,6},{3,7},{4,0},{5,1},{6,2},{7,3},{8,12},{9,13},{10,... | collective-permute-start | bytes 835592 | tf_op jit(solution)/shard_map/d_act/ppermute | solution.py:24
  102.4 13.9 %collective-permute-start.40 = (bf16[272,512]{1,0:T(8,128)(2,1)S(1)}, bf16[272,512]{1,0:T(8,128)(2,1)S(1)}, u32[]{:S(2)}, u32[]{:S(2)}) collective-permute-start(bf16[272,512]{1,0:T(8,128)(2,1)S(1)} %get-tuple-element.93), channel_id=1, source_target_pairs={{0,6},{1,7},{2,4},{3,5},{4,2},{5,3},{6,0},{7,1},{8,14},{9,15},{10,... | collective-permute-start | bytes 835592 | tf_op jit(solution)/shard_map/d_act/ppermute | solution.py:24
  103.9 15.6 %collective-permute-start.44 = (bf16[128,512]{1,0:T(8,128)(2,1)S(1)}, bf16[128,512]{1,0:T(8,128)(2,1)S(1)}, u32[]{:S(2)}, u32[]{:S(2)}) collective-permute-start(bf16[128,512]{1,0:T(8,128)(2,1)S(1)} %collective-permute-done.34.refs_8_), channel_id=1, source_target_pairs={{0,1},{1,0},{2,3},{3,2},{4,5},{5,4},{6,7},{7,6},{8,9},{9,8},{10,11... | collective-permute-start | bytes 393224 | tf_op jit(solution)/shard_map/grad_weight/ppermute | solution.py:24
  103.9 16.6 %collective-permute-start.45 = (bf16[128,512]{1,0:T(8,128)(2,1)S(1)}, bf16[128,512]{1,0:T(8,128)(2,1)S(1)}, u32[]{:S(2)}, u32[]{:S(2)}) collective-permute-start(bf16[128,512]{1,0:T(8,128)(2,1)S(1)} %collective-permute-done.35.refs_9_), channel_id=1, source_target_pairs={{0,1},{1,0},{2,3},{3,2},{4,5},{5,4},{6,7},{7,6},{8,9},{9,8},{10,11... | collective-permute-start | bytes 393224 | tf_op jit(solution)/shard_map/grad_weight/ppermute | solution.py:24
  109.9 10.6 %collective-permute-start.46 = (bf16[128,512]{1,0:T(8,128)(2,1)S(1)}, bf16[128,512]{1,0:T(8,128)(2,1)S(1)}, u32[]{:S(2)}, u32[]{:S(2)}) collective-permute-start(bf16[128,512]{1,0:T(8,128)(2,1)S(1)} %collective-permute-done.36.refs_10_), channel_id=1, source_target_pairs={{0,1},{1,0},{2,3},{3,2},{4,5},{5,4},{6,7},{7,6},{8,9},{9,8},{10,11... | collective-permute-start | bytes 393224 | tf_op jit(solution)/shard_map/grad_weight/ppermute | solution.py:24
  116.9 6.5 %collective-permute-start.42 = (f32[8,512]{1,0:T(8,128)S(1)}, f32[8,512]{1,0:T(8,128)S(1)}, u32[]{:S(2)}, u32[]{:S(2)}) collective-permute-start(f32[8,512]{1,0:T(8,128)S(1)} %pad_maximum_fusion), channel_id=1, source_target_pairs={{0,16},{8,24},{16,0},{24,8},{1,17},{9,25},{17,1},{25,9},{2,18},{10... | collective-permute-start | bytes 49160 | tf_op jit(solution)/shard_map/norm_backward/ppermute | solution.py:24
  117.3 6.1 %collective-permute-start.43 = (f32[8,512]{1,0:T(8,128)S(1)}, f32[8,512]{1,0:T(8,128)S(1)}, u32[]{:S(2)}, u32[]{:S(2)}) collective-permute-start(f32[8,512]{1,0:T(8,128)S(1)} %pad_maximum_fusion), channel_id=1, source_target_pairs={{0,24},{8,16},{16,8},{24,0},{1,25},{9,17},{17,9},{25,1},{2,26},{10... | collective-permute-start | bytes 49160 | tf_op jit(solution)/shard_map/norm_backward/ppermute | solution.py:24
  119.5 3.9 %collective-permute-start.41 = (f32[8,512]{1,0:T(8,128)S(1)}, f32[8,512]{1,0:T(8,128)S(1)}, u32[]{:S(2)}, u32[]{:S(2)}) collective-permute-start(f32[8,512]{1,0:T(8,128)S(1)} %pad_maximum_fusion), channel_id=1, source_target_pairs={{0,8},{8,0},{16,24},{24,16},{1,9},{9,1},{17,25},{25,17},{2,10},{10... | collective-permute-start | bytes 49160 | tf_op jit(solution)/shard_map/norm_backward/ppermute | solution.py:24
  (2 other events, 19.5 us)

commit v11 on v10

--- a/solution.py
+++ b/solution.py
@@ -159,7 +159,8 @@
     part = 2 * local_rows // n_col
     for k in range(n_col):
         start = pl.multiple_of((place_ref[1] ^ k) * part, part)
-        (odd_ref if k % 2 else even_ref)[k // 2] = strip[pl.ds(start, part), :]
+        ref = odd_ref if k % 2 else even_ref
+        ref[k // 2] = strip[pl.ds(start, part), :].astype(ref.dtype)
 
 
 def strip_call(place, z_slots, n_col):
@@ -167,11 +168,11 @@
     local_rows, columns = z_slots[0][0].shape
     tall = 2 * local_rows
     wide = len(upper_blocks(n_batch)) * local_rows
-    part = jax.ShapeDtypeStruct((n_col // 2, tall // n_col, wide), f32)
+    shape = (n_col // 2, tall // n_col, wide)
     operands = [place] + [z for slot in z_slots for z in slot]
     return pl.pallas_call(
         functools.partial(strip_kernel, n_batch, n_col),
-        out_shape=(part, part),
+        out_shape=(jax.ShapeDtypeStruct(shape, f32), jax.ShapeDtypeStruct(shape, bf16)),
         in_specs=[IN_SMEM] + [IN_VMEM] * (len(operands) - 1),
         out_specs=(IN_VMEM, IN_VMEM),
         scratch_shapes=[pltpu.VMEM((tall, wide), f32)],
@@ -463,6 +464,39 @@
     return pieces
 
 
+def finish_kernel(n_batch, rows, *refs):
+    sums, (d_pre, normalised, gain, deviation) = refs[:n_batch], refs[n_batch : n_batch + 4]
+    loss_ref, gain_ref, bias_ref, out_ref = refs[n_batch + 4 :]
+    both = exchange_sum(x[...] for x in sums)
+    bias_ref[...] = both[0:1] + both[1:2]
+    gain_ref[...] = both[2:3] + both[3:4]
+    loss_ref[...] = both[4:5, 0:128]
+    for v in range(2):
+        factor = gain[...] * deviation[v : v + 1]
+        mean_b, mean_g = both[v : v + 1] / rows, both[2 + v : 3 + v] / rows
+        out_ref[v] = factor * (d_pre[v] - mean_b - normalised[v] * mean_g)
+
+
+def finish_call(sums, d_pre, normalised, gain, deviation, rows):
+    _, local_rows, width = d_pre.shape
+    operands = list(sums) + [d_pre, normalised, gain[None], deviation[:, 0]]
+    out_shape = (
+        jax.ShapeDtypeStruct((1, 128), f32),
+        jax.ShapeDtypeStruct((1, width), f32),
+        jax.ShapeDtypeStruct((1, width), f32),
+        jax.ShapeDtypeStruct(d_pre.shape, f32),
+    )
+    return pl.pallas_call(
+        functools.partial(finish_kernel, len(sums), rows),
+        out_shape=out_shape,
+        in_specs=[IN_VMEM] * len(operands),
+        out_specs=(IN_VMEM,) * 4,
+        compiler_params=params(4),
+        cost_estimate=cost(0, 8 * d_pre.size),
+        name="views_gradient",
+    )(*operands)
+
+
 def shards(views, norm_scale_gain, norm_shift_bias, weight):
     n_batch = lax.axis_size("batch")
     n_col = lax.axis_size("col")
@@ -500,10 +534,13 @@
         preactivation = norm_scale_gain * normalised + norm_shift_bias
         act = jax.nn.gelu(preactivation, approximate=True).astype(bf16)
     with jax.named_scope("act_gather"):
-        pieces = link_pieces(act.reshape(tall, width), n_col)
-        pieces[1] = xor_send(pieces[0], "col", 1)
-        first, pieces[1] = lax.optimization_barrier((act[0], pieces[1]))
-        others = [ring_send(first, "batch", d) for d in range(1, n_batch)]
+        others = [ring_send(act[0], "batch", d) for d in range(1, n_batch)]
+        own = act.reshape(tall, width)
+        sibling = xor_send(own, "col", 1)
+        own, sibling = lax.optimization_barrier((own, sibling))
+        pieces = link_pieces(own, n_col)
+        pieces[1] = sibling
+        others, pieces[far[0]] = lax.optimization_barrier((others, pieces[far[0]]))
         pieces = sibling_pieces(pieces, n_col)
         far_pieces = link_pieces(jnp.concatenate(others), n_col)
     with jax.named_scope("z"):
@@ -540,17 +577,17 @@
         slots = list(zip([z_own0] + list(z_far), z_ring))
     with jax.named_scope("kernel"):
         even_part, odd_part = strip_call(place, slots, n_col)
-        even_part = even_part + xor_send(odd_part, "col", 1)
+        even_part = even_part + xor_send(odd_part, "col", 1).astype(f32)
         even_part, held_back = lax.optimization_barrier((even_part, [pieces[k] for k in evens]))
         strip = even_part[0]
         for k in far:
-            strip = strip + xor_send(even_part[k // 2], "col", k)
+            strip = strip + xor_send(even_part[k // 2].astype(bf16), "col", k).astype(f32)
         picked = pick_call(place, held_back, n_batch, n_col)
         blocks = [
             ring_send(x, "batch", 1 + i % (n_batch - 1)) for i, x in enumerate(picked)
         ]
         strips = gather_pieces(strip.astype(bf16), n_col)
-        strips, blocks = lax.optimization_barrier((strips, blocks))
+        strips, blocks[:-1] = lax.optimization_barrier((strips, blocks[:-1]))
     with jax.named_scope("dz"):
         constants = (
             4.0 * scale / denom,
@@ -562,6 +599,7 @@
             1.0 / denom / n_batch,
         )
         dz, share = dz_call(place, strip, [strips[k] for k in range(n_col)], slots, constants)
+        dz, blocks[-1] = lax.optimization_barrier((dz, blocks[-1]))
     with jax.named_scope("d_act"):
         (away,) = d_act_call(place, dz, share, held_weight, n_batch, n_col, None)
         got = xor_send(away, "col", 1)
@@ -595,17 +633,10 @@
                 jnp.broadcast_to(share, (2 * n_view, width)),
             ]
         )
-        both = exchange_sum(exchange(sums, "batch"))
-        sum_b, sum_g = both[:n_view], both[n_view : 2 * n_view]
-        loss = jnp.max(both[2 * n_view :])
-        grad_bias = jnp.sum(sum_b, axis=0)
-        grad_gain = jnp.sum(sum_g, axis=0)
-        views_gradient = (
-            norm_scale_gain
-            * (d_pre - sum_b[:, None, :] / rows - normalised * sum_g[:, None, :] / rows)
-            * inverse_deviation
-        )
-    return (loss, grad_weight, grad_gain, grad_bias, views_gradient)
+        loss, grad_gain, grad_bias, views_gradient = finish_call(
+            exchange(sums, "batch"), d_pre, normalised, norm_scale_gain, inverse_deviation, rows
+        )
+    return (loss[0, 0], grad_weight, grad_gain[0], grad_bias[0], views_gradient)
 
 
 def solution(mesh):

time: 126 us -> 125 us (level)
  starting transfers between devices: 40.9 us -> 47.5 us
  waiting for transfers between devices: 47.5 us -> 41.6 us
  other arithmetic: 5.35 us -> 3.21 us
    ppermute x38, waiting for transfers between devices: 38.3 us -> 29.6 us  [xor_send(): return lax.ppermute(x, axis, [(i, i ^ k) for i in range(n)])]
    ppermute x9, starting transfers between devices: 11.4 us -> 17.9 us  [ring_send(): lax.ppermute(x, axis, [(order[i], order[(i + d) % n]) for i in range(n)])]
    ppermute x9, waiting for transfers between devices: 9.23 us -> 12 us  [ring_send(): lax.ppermute(x, axis, [(order[i], order[(i + d) % n]) for i in range(n)])]
  transfers between devices with their start and end apart: 47 -> 47, of which waited for: 19 -> 20; matrix products, arithmetic and copies ran while one was open for 1% -> 1% of each run, Pallas kernels for 16% -> 19%
where the time goes in v11:
time: 125 us
  starting transfers between devices  47.5 us (38%)
  waiting for transfers between devices  41.6 us (33%)
  Pallas kernels  31.5 us (25%)
  other arithmetic  3.21 us (3%)
    ppermute x38, waiting for transfers between devices, xor_send(): return lax.ppermute(x, axis, [(i, i ^ k) for i in range(n)])  29.6 us
    ppermute x38, starting transfers between devices, xor_send(): return lax.ppermute(x, axis, [(i, i ^ k) for i in range(n)])  29.6 us
    ppermute x9, starting transfers between devices, ring_send(): lax.ppermute(x, axis, [(order[i], order[(i + d) % n]) for i in range(n)])  17.9 us
    ppermute x9, waiting for transfers between devices, ring_send(): lax.ppermute(x, axis, [(order[i], order[(i + d) % n]) for i in range(n)])  12 us
    pallas_call x6, Pallas kernels, z_call(): pl.pallas_call(functools.partial(z_kernel, tuple(ks), before is None, las...  9.68 us
    pallas_call x2, Pallas kernels, weight_grad_call(): pl.pallas_call(functools.partial(weight_grad_kernel, len(arrived), int(be...  5.79 us
    pallas_call x1, Pallas kernels, dz_call(): pl.pallas_call(functools.partial(dz_kernel, n_batch, n_col, tile, constan...  4.68 us
    pallas_call x2, Pallas kernels, d_act_call(): pl.pallas_call(functools.partial(d_act_kernel, count, (got is not None, n...  3.69 us
  transfers between devices with their start and end apart: 47, of which 20 were waited for; matrix products, arithmetic and copies ran while one was open for 1% of the time, Pallas kernels for 19%

profile of v11, /device:TPU:0, one launch (start us, length us, event | category | flops | bytes accessed | tf_op | source)
XLA Modules:
  0.0 124.9 jit_solution(14283202516430337052)
XLA Ops:
  1.7 1.0 fusion.8
  2.8 5.1 %collective-permute-start.2 = (f32[4,512]{1,0:T(4,128)S(1)}, f32[4,512]{1,0:T(4,128)S(1)}, u32[]{:S(2)}, u32[]{:S(2)}) collective-permute-start(f32[4,512]{1,0:T(4,128)S(1)} %pad_maximum_fusion.1), channel_id=1, source_target_pairs={{0,24},{8,16},{16,8},{24,0},{1,25},{9,17},{17,9},{25,1},{2,26},{10... | collective-permute-start | bytes 24584 | tf_op jit(solution)/shard_map/norm_stats/ppermute | solution.py:24
  8.6 3.5 %weight_load.1 = (bf16[4096,1024]{1,0:T(8,128)(2,1)S(1)}, f32[4,512]{1,0:T(4,128)S(1)}) custom-call(bf16[4096,1024]{1,0:T(8,128)(2,1)} %w_ref), custom_call_target="tpu_custom_call" | custom-call | bytes 16777216 | tf_op jit(solution)/shard_map/weight_load/weight_load/pallas_call | solution.py:78
  12.9 1.1 collective-permute-start.5
  14.4 1.5 %collective-permute-start.7 = (bf16[256,512]{1,0:T(8,128)(2,1)S(1)}, bf16[256,512]{1,0:T(8,128)(2,1)S(1)}, u32[]{:S(2)}, u32[]{:S(2)}) collective-permute-start(bf16[256,512]{1,0:T(8,128)(2,1)S(1)} %bitcast.27), channel_id=1, source_target_pairs={{0,2},{1,3},{2,0},{3,1},{4,6},{5,7},{6,4},{7,5},{8,10},{9,11},{10,... | collective-permute-start | bytes 786440 | tf_op jit(solution)/shard_map/act_gather/ppermute | solution.py:24
  15.9 1.5 %collective-permute-start.11 = (bf16[256,512]{1,0:T(8,128)(2,1)S(1)}, bf16[256,512]{1,0:T(8,128)(2,1)S(1)}, u32[]{:S(2)}, u32[]{:S(2)}) collective-permute-start(bf16[256,512]{1,0:T(8,128)(2,1)S(1)} %bitcast.28), channel_id=1, source_target_pairs={{0,6},{1,7},{2,4},{3,5},{4,2},{5,3},{6,0},{7,1},{8,14},{9,15},{10,... | collective-permute-start | bytes 786440 | tf_op jit(solution)/shard_map/act_gather/ppermute | solution.py:24
  17.9 3.4 %collective-permute-start.4 = (bf16[128,512]{1,0:T(8,128)(2,1)S(1)}, bf16[128,512]{1,0:T(8,128)(2,1)S(1)}, u32[]{:S(2)}, u32[]{:S(2)}) collective-permute-start(bf16[128,512]{1,0:T(8,128)(2,1)S(1)} %slice_bitcast_fusion), channel_id=1, source_target_pairs={{0,24},{16,8},{24,0},{8,16},{1,25},{17,9},{25,1},{9,17},{2,26},{18... | collective-permute-start | bytes 393224 | tf_op jit(solution)/shard_map/act_gather/ppermute | solution.py:34
  21.8 1.2 z_matmul.6.refs_4_
  23.1 2.7 %collective-permute-done.4 = bf16[128,512]{1,0:T(8,128)(2,1)S(1)} collective-permute-done((bf16[128,512]{1,0:T(8,128)(2,1)S(1)}, bf16[128,512]{1,0:T(8,128)(2,1)S(1)}, u32[]{:S(2)}, u32[]{:S(2)}) %collective-permute-start.4) | collective-permute-done | bytes 131104 | tf_op jit(solution)/shard_map/act_gather/ppermute | solution.py:34
  25.8 1.5 %collective-permute-done.3 = bf16[128,512]{1,0:T(8,128)(2,1)S(1)} collective-permute-done((bf16[128,512]{1,0:T(8,128)(2,1)S(1)}, bf16[128,512]{1,0:T(8,128)(2,1)S(1)}, u32[]{:S(2)}, u32[]{:S(2)}) %collective-permute-start.3) | collective-permute-done | bytes 131104 | tf_op jit(solution)/shard_map/act_gather/ppermute | solution.py:34
  27.3 2.1 %collective-permute-done.11.refs_2_.refs_3_ = bf16[256,512]{1,0:T(8,128)(2,1)S(1)} collective-permute-done((bf16[256,512]{1,0:T(8,128)(2,1)S(1)}, bf16[256,512]{1,0:T(8,128)(2,1)S(1)}, u32[]{:S(2)}, u32[]{:S(2)}) %collective-permute-start.11) | collective-permute-done | bytes 262176 | tf_op jit(solution)/shard_map/act_gather/ppermute | solution.py:24
  29.5 1.3 %collective-permute-done.9.refs_1_.refs_2_ = bf16[256,512]{1,0:T(8,128)(2,1)S(1)} collective-permute-done((bf16[256,512]{1,0:T(8,128)(2,1)S(1)}, bf16[256,512]{1,0:T(8,128)(2,1)S(1)}, u32[]{:S(2)}, u32[]{:S(2)}) %collective-permute-start.9) | collective-permute-done | bytes 262176 | tf_op jit(solution)/shard_map/act_gather/ppermute | solution.py:24
  30.8 1.5 %collective-permute-start.15 = (bf16[384,512]{1,0:T(8,128)(2,1)S(1)}, bf16[384,512]{1,0:T(8,128)(2,1)S(1)}, u32[]{:S(2)}, u32[]{:S(2)}) collective-permute-start(bf16[384,512]{1,0:T(8,128)(2,1)S(1)} %constant_dynamic-update-slice_fusion.refs_0_.refs_4_), channel_id=1, source_target_pairs={{0,6},{1,7},{2,4},{3,5},{4,2},{5,3},{6,0},{7,1},{8,14},{9,15},{10,... | collective-permute-start | bytes 1179656 | tf_op jit(solution)/shard_map/act_gather/ppermute | solution.py:24
  32.3 1.5 %z_matmul.7.refs_4_ = f32[256,1024]{1,0:T(8,128)S(1)} custom-call(s32[2]{0:T(128)S(1)} %pad_add_fusion.place_ref, bf16[256,512]{1,0:T(8,128)(2,1)S(1)} %collective-permute-done.7.refs_0_.refs_1_, bf16[256,512]{1,0:T(8,128)(2,1)S(1)} %collective-permute-done.9.refs_1_.refs_2_, bf16[256,512]{1,0:T(8,128)(2,1)S(1)} %collective-permute-done.11.refs_2_.refs_3_, ...), custom_call_target="tpu_custom_call" | custom-call | flops 805306368 | bytes 524288 | tf_op jit(solution)/shard_map/z/z_matmul/pallas_call | solution.py:126
  33.9 1.5 %z_matmul.8 = (bf16[128,1024]{1,0:T(8,128)(2,1)S(1)}, bf16[128,1024]{1,0:T(8,128)(2,1)S(1)}) custom-call(s32[2]{0:T(128)S(1)} %pad_add_fusion.place_ref, bf16[256,512]{1,0:T(8,128)(2,1)S(1)} %collective-permute-done.8.refs_0_.refs_1_, bf16[256,512]{1,0:T(8,128)(2,1)S(1)} %collective-permute-done.10.refs_1_.refs_2_, ...), custom_call_target="tpu_custom_call" | custom-call | flops 805306368 | bytes 524288 | tf_op jit(solution)/shard_map/z/z_matmul/pallas_call | solution.py:126
  35.4 2.1 %collective-permute-start.14 = (bf16[128,1024]{1,0:T(8,128)(2,1)S(1)}, bf16[128,1024]{1,0:T(8,128)(2,1)S(1)}, u32[]{:S(2)}, u32[]{:S(2)}) collective-permute-start(bf16[128,1024]{1,0:T(8,128)(2,1)S(1)} %get-tuple-element.71.refs_1_.refs_9_), channel_id=1, source_target_pairs={{0,16},{16,24},{24,8},{8,0},{1,17},{17,25},{25,9},{9,1},{2,18},{18... | collective-permute-start | bytes 786440 | tf_op jit(solution)/shard_map/z_ring/ppermute | solution.py:34
  37.5 1.5 %collective-permute-start.19 = (bf16[384,512]{1,0:T(8,128)(2,1)S(1)}, bf16[384,512]{1,0:T(8,128)(2,1)S(1)}, u32[]{:S(2)}, u32[]{:S(2)}) collective-permute-start(bf16[384,512]{1,0:T(8,128)(2,1)S(1)} %constant_dynamic-update-slice_fusion.refs_0_.refs_4_), channel_id=1, source_target_pairs={{0,4},{1,5},{2,6},{3,7},{4,0},{5,1},{6,2},{7,3},{8,12},{9,13},{10,... | collective-permute-start | bytes 1179656 | tf_op jit(solution)/shard_map/act_gather/ppermute | solution.py:24
  39.6 4.2 %collective-permute-done.15.refs_1_.refs_7_ = bf16[384,512]{1,0:T(8,128)(2,1)S(1)} collective-permute-done((bf16[384,512]{1,0:T(8,128)(2,1)S(1)}, bf16[384,512]{1,0:T(8,128)(2,1)S(1)}, u32[]{:S(2)}, u32[]{:S(2)}) %collective-permute-start.15) | collective-permute-done | bytes 393248 | tf_op jit(solution)/shard_map/act_gather/ppermute | solution.py:24
  44.7 2.1 %collective-permute-start.17 = (bf16[128,1024]{1,0:T(8,128)(2,1)S(1)}, bf16[128,1024]{1,0:T(8,128)(2,1)S(1)}, u32[]{:S(2)}, u32[]{:S(2)}) collective-permute-start(bf16[128,1024]{1,0:T(8,128)(2,1)S(1)} %collective-permute-done.14.refs_3_.refs_11_), channel_id=1, source_target_pairs={{0,16},{16,24},{24,8},{8,0},{1,17},{17,25},{25,9},{9,1},{2,18},{18... | collective-permute-start | bytes 786440 | tf_op jit(solution)/shard_map/z_ring/ppermute | solution.py:34
  46.9 4.9 %collective-permute-done.19.refs_1_.refs_6_ = bf16[384,512]{1,0:T(8,128)(2,1)S(1)} collective-permute-done((bf16[384,512]{1,0:T(8,128)(2,1)S(1)}, bf16[384,512]{1,0:T(8,128)(2,1)S(1)}, u32[]{:S(2)}, u32[]{:S(2)}) %collective-permute-start.19) | collective-permute-done | bytes 393248 | tf_op jit(solution)/shard_map/act_gather/ppermute | solution.py:24
  52.3 1.5 %z_matmul.9.refs_3_ = f32[384,1024]{1,0:T(8,128)S(1)} custom-call(s32[2]{0:T(128)S(1)} %pad_add_fusion.place_ref, bf16[384,512]{1,0:T(8,128)(2,1)S(1)} %constant_dynamic-update-slice_fusion.refs_0_.refs_4_, bf16[384,512]{1,0:T(8,128)(2,1)S(1)} %collective-permute-done.15.refs_1_.refs_7_, bf16[4096,1024]{1,0:T(8,128)(2,1)S(1)} %get-tuple-element.68.refs_2_.refs_3_.refs_4_.w_ref), custom_call_target="tpu_custom_call" | custom-call | flops 805306368 | bytes 786432 | tf_op jit(solution)/shard_map/z_far/z_matmul/pallas_call | solution.py:126
  53.9 2.1 %collective-permute-start.22 = (bf16[128,1024]{1,0:T(8,128)(2,1)S(1)}, bf16[128,1024]{1,0:T(8,128)(2,1)S(1)}, u32[]{:S(2)}, u32[]{:S(2)}) collective-permute-start(bf16[128,1024]{1,0:T(8,128)(2,1)S(1)} %collective-permute-done.17.refs_5_.refs_13_), channel_id=1, source_target_pairs={{0,16},{16,24},{24,8},{8,0},{1,17},{17,25},{25,9},{9,1},{2,18},{18... | collective-permute-start | bytes 786440 | tf_op jit(solution)/shard_map/z_far/ppermute | solution.py:34
  56.0 1.5 %z_matmul.10.refs_5_ = f32[384,1024]{1,0:T(8,128)S(1)} custom-call(s32[2]{0:T(128)S(1)} %pad_add_fusion.place_ref, bf16[384,512]{1,0:T(8,128)(2,1)S(1)} %collective-permute-done.16.refs_0_.refs_5_, bf16[384,512]{1,0:T(8,128)(2,1)S(1)} %collective-permute-done.19.refs_1_.refs_6_, bf16[4096,1024]{1,0:T(8,128)(2,1)S(1)} %get-tuple-element.68.refs_2_.refs_3_.refs_4_.w_ref, ...), custom_call_target="tpu_custom_call" | custom-call | flops 805306368 | bytes 786432 | tf_op jit(solution)/shard_map/z_far/z_matmul/pallas_call | solution.py:126
  57.5 2.3 %z_matmul.11 = (bf16[128,1024]{1,0:T(8,128)(2,1)S(1)}, bf16[128,1024]{1,0:T(8,128)(2,1)S(1)}, bf16[128,1024]{1,0:T(8,128)(2,1)S(1)}) custom-call(s32[2]{0:T(128)S(1)} %pad_add_fusion.place_ref, bf16[384,512]{1,0:T(8,128)(2,1)S(1)} %collective-permute-done.13.refs_0_.refs_4_, bf16[384,512]{1,0:T(8,128)(2,1)S(1)} %collective-permute-done.18.refs_1_.refs_5_, ...), custom_call_target="tpu_custom_call" | custom-call | flops 1610612736 | bytes 786432 | tf_op jit(solution)/shard_map/z_far/z_matmul/pallas_call | solution.py:126
  59.9 3.5 %collective-permute-done.22.refs_7_.refs_15_ = bf16[128,1024]{1,0:T(8,128)(2,1)S(1)} collective-permute-done((bf16[128,1024]{1,0:T(8,128)(2,1)S(1)}, bf16[128,1024]{1,0:T(8,128)(2,1)S(1)}, u32[]{:S(2)}, u32[]{:S(2)}) %collective-permute-start.22) | collective-permute-done | bytes 262176 | tf_op jit(solution)/shard_map/z_far/ppermute | solution.py:34
  63.4 2.6 %kernel_strip.1 = (f32[4,32,1280]{2,1,0:T(8,128)S(1)}, bf16[4,32,1280]{2,1,0:T(8,128)(2,1)S(1)}) custom-call(s32[2]{0:T(128)S(1)} %pad_add_fusion.place_ref, bf16[128,1024]{1,0:T(8,128)(2,1)S(1)} %get-tuple-element.70.refs_0_.refs_8_, bf16[128,1024]{1,0:T(8,128)(2,1)S(1)} %get-tuple-element.71.refs_1_.refs_9_, ...), custom_call_target="tpu_custom_call" | custom-call | flops 671088640 | bytes 2097152 | tf_op jit(solution)/shard_map/kernel/kernel_strip/pallas_call | solution.py:173
  66.1 1.6 %collective-permute-done.23 = bf16[4,32,1280]{2,1,0:T(8,128)(2,1)S(1)} collective-permute-done((bf16[4,32,1280]{2,1,0:T(8,128)(2,1)S(1)}, bf16[4,32,1280]{2,1,0:T(8,128)(2,1)S(1)}, u32[]{:S(2)}, u32[]{:S(2)}) %collective-permute-start.23) | collective-permute-done | bytes 327712 | tf_op jit(solution)/shard_map/kernel/ppermute | solution.py:24
  67.9 1.6 %collective-permute-start.24 = (bf16[32,1280]{1,0:T(8,128)(2,1)S(1)}, bf16[32,1280]{1,0:T(8,128)(2,1)S(1)}, u32[]{:S(2)}, u32[]{:S(2)}) collective-permute-start(bf16[32,1280]{1,0:T(8,128)(2,1)S(1)} %get-tuple-element.122), channel_id=1, source_target_pairs={{0,2},{1,3},{2,0},{3,1},{4,6},{5,7},{6,4},{7,5},{8,10},{9,11},{10,... | collective-permute-start | bytes 245768 | tf_op jit(solution)/shard_map/kernel/ppermute | solution.py:24
  70.4 1.0 collective-permute-start.25
  72.1 2.2 %collective-permute-start.34 = (bf16[128,512]{1,0:T(8,128)(2,1)S(1)}, bf16[128,512]{1,0:T(8,128)(2,1)S(1)}, u32[]{:S(2)}, u32[]{:S(2)}) collective-permute-start(bf16[128,512]{1,0:T(8,128)(2,1)S(1)} %get-tuple-element.90), channel_id=1, source_target_pairs={{0,16},{16,24},{24,8},{8,0},{1,17},{17,25},{25,9},{9,1},{2,18},{18... | collective-permute-start | bytes 393224 | tf_op jit(solution)/shard_map/kernel/ppermute | solution.py:34
  74.9 1.2 collective-permute-done.25
  76.2 1.8 %collective-permute-start.32 = (bf16[32,1280]{1,0:T(8,128)(2,1)S(1)}, bf16[32,1280]{1,0:T(8,128)(2,1)S(1)}, u32[]{:S(2)}, u32[]{:S(2)}) collective-permute-start(bf16[32,1280]{1,0:T(8,128)(2,1)S(1)} %get-tuple-element.92.refs_0_), channel_id=1, source_target_pairs={{0,6},{1,7},{2,4},{3,5},{4,2},{5,3},{6,0},{7,1},{8,14},{9,15},{10,... | collective-permute-start | bytes 245768 | tf_op jit(solution)/shard_map/kernel/ppermute | solution.py:24
  78.6 1.1 collective-permute-start.28
  79.7 2.1 %collective-permute-start.35 = (bf16[128,512]{1,0:T(8,128)(2,1)S(1)}, bf16[128,512]{1,0:T(8,128)(2,1)S(1)}, u32[]{:S(2)}, u32[]{:S(2)}) collective-permute-start(bf16[128,512]{1,0:T(8,128)(2,1)S(1)} %get-tuple-element.91), channel_id=1, source_target_pairs={{0,24},{16,8},{24,0},{8,16},{1,25},{17,9},{25,1},{9,17},{2,26},{18... | collective-permute-start | bytes 393224 | tf_op jit(solution)/shard_map/kernel/ppermute | solution.py:34
  83.3 3.2 %collective-permute-done.35.refs_9_ = bf16[128,512]{1,0:T(8,128)(2,1)S(1)} collective-permute-done((bf16[128,512]{1,0:T(8,128)(2,1)S(1)}, bf16[128,512]{1,0:T(8,128)(2,1)S(1)}, u32[]{:S(2)}, u32[]{:S(2)}) %collective-permute-start.35) | collective-permute-done | bytes 131104 | tf_op jit(solution)/shard_map/kernel/ppermute | solution.py:34
  86.6 2.5 %collective-permute-start.36 = (bf16[128,512]{1,0:T(8,128)(2,1)S(1)}, bf16[128,512]{1,0:T(8,128)(2,1)S(1)}, u32[]{:S(2)}, u32[]{:S(2)}) collective-permute-start(bf16[128,512]{1,0:T(8,128)(2,1)S(1)} %get-tuple-element.101), channel_id=1, source_target_pairs={{0,8},{16,0},{24,16},{8,24},{1,9},{17,1},{25,17},{9,25},{2,10},{18... | collective-permute-start | bytes 393224 | tf_op jit(solution)/shard_map/kernel/ppermute | solution.py:34
  89.1 4.7 %embedding_gradient.1 = (bf16[2,512,1024]{2,1,0:T(8,128)(2,1)S(1)}, f32[8,128]{1,0:T(8,128)S(1)}) custom-call(s32[2]{0:T(128)S(1)} %pad_add_fusion.place_ref, f32[32,1280]{1,0:T(8,128)S(1)} %get-tuple-element.119.own_ref, bf16[32,1280]{1,0:T(8,128)(2,1)S(1)} %get-tuple-element.92.refs_0_, bf16[32,1280]{1,0:T(8,128)(2,1)S(1)} %collective-permute-done.27.refs_1_, ...), custom_call_target="tpu_custom_call" | custom-call | flops 1073741824 | bytes 4194304 | tf_op jit(solution)/shard_map/dz/embedding_gradient/pallas_call | solution.py:251
  93.8 1.8 %d_act_matmul.2 = bf16[4,272,512]{2,1,0:T(8,128)(2,1)S(1)} custom-call(s32[2]{0:T(128)S(1)} %pad_add_fusion.place_ref, bf16[2,512,1024]{2,1,0:T(8,128)(2,1)S(1)} %get-tuple-element.102.dz_ref.refs_11_, f32[8,128]{1,0:T(8,128)S(1)} %get-tuple-element.103.share_ref, bf16[4096,1024]{1,0:T(8,128)(2,1)S(1)} %get-tuple-element.68.refs_2_.refs_3_.refs_4_.w_ref), custom_call_target="tpu_custom_call" | custom-call | flops 1073741824 | bytes 1048576 | tf_op jit(solution)/shard_map/d_act/d_act_matmul/pallas_call | solution.py:323
  95.7 2.7 %collective-permute-done.37.refs_0_ = bf16[4,272,512]{2,1,0:T(8,128)(2,1)S(1)} collective-permute-done((bf16[4,272,512]{2,1,0:T(8,128)(2,1)S(1)}, bf16[4,272,512]{2,1,0:T(8,128)(2,1)S(1)}, u32[]{:S(2)}, u32[]{:S(2)}) %collective-permute-start.37) | collective-permute-done | bytes 1114144 | tf_op jit(solution)/shard_map/d_act/ppermute | solution.py:24
  98.4 1.9 %d_act_matmul.3 = (bf16[272,512]{1,0:T(8,128)(2,1)S(1)}, bf16[272,512]{1,0:T(8,128)(2,1)S(1)}, bf16[272,512]{1,0:T(8,128)(2,1)S(1)}, f32[272,512]{1,0:T(8,128)S(1)}) custom-call(s32[2]{0:T(128)S(1)} %pad_add_fusion.place_ref, bf16[2,512,1024]{2,1,0:T(8,128)(2,1)S(1)} %get-tuple-element.102.dz_ref.refs_11_, f32[8,128]{1,0:T(8,128)S(1)} %get-tuple-element.103.share_ref, ...), custom_call_target="tpu_custom_call" | custom-call | flops 1073741824 | bytes 1048576 | tf_op jit(solution)/shard_map/d_act/d_act_matmul/pallas_call | solution.py:323
  100.3 1.3 %collective-permute-start.38 = (bf16[272,512]{1,0:T(8,128)(2,1)S(1)}, bf16[272,512]{1,0:T(8,128)(2,1)S(1)}, u32[]{:S(2)}, u32[]{:S(2)}) collective-permute-start(bf16[272,512]{1,0:T(8,128)(2,1)S(1)} %get-tuple-element.105), channel_id=1, source_target_pairs={{0,2},{1,3},{2,0},{3,1},{4,6},{5,7},{6,4},{7,5},{8,10},{9,11},{10,... | collective-permute-start | bytes 835592 | tf_op jit(solution)/shard_map/d_act/ppermute | solution.py:24
  101.6 1.5 %collective-permute-start.39 = (bf16[272,512]{1,0:T(8,128)(2,1)S(1)}, bf16[272,512]{1,0:T(8,128)(2,1)S(1)}, u32[]{:S(2)}, u32[]{:S(2)}) collective-permute-start(bf16[272,512]{1,0:T(8,128)(2,1)S(1)} %get-tuple-element.106), channel_id=1, source_target_pairs={{0,4},{1,5},{2,6},{3,7},{4,0},{5,1},{6,2},{7,3},{8,12},{9,13},{10,... | collective-permute-start | bytes 835592 | tf_op jit(solution)/shard_map/d_act/ppermute | solution.py:24
  104.3 2.9 %weight_gradient.2.refs_12_ = f32[1024,1024]{1,0:T(8,128)} custom-call(s32[2]{0:T(128)S(1)} %pad_add_fusion.place_ref, bf16[256,512]{1,0:T(8,128)(2,1)S(1)} %bitcast.32, bf16[256,512]{1,0:T(8,128)(2,1)S(1)} %collective-permute-done.7.refs_0_.refs_1_, bf16[256,512]{1,0:T(8,128)(2,1)S(1)} %collective-permute-done.9.refs_1_.refs_2_, ...), custom_call_target="tpu_custom_call" | custom-call | flops 1073741824 | bytes 2097152 | tf_op jit(solution)/shard_map/grad_weight/weight_gradient/pallas_call | solution.py:430
  107.2 2.6 %collective-permute-done.38 = bf16[272,512]{1,0:T(8,128)(2,1)S(1)} collective-permute-done((bf16[272,512]{1,0:T(8,128)(2,1)S(1)}, bf16[272,512]{1,0:T(8,128)(2,1)S(1)}, u32[]{:S(2)}, u32[]{:S(2)}) %collective-permute-start.38) | collective-permute-done | bytes 278560 | tf_op jit(solution)/shard_map/d_act/ppermute | solution.py:24
  109.8 6.2 %collective-permute-done.39 = bf16[272,512]{1,0:T(8,128)(2,1)S(1)} collective-permute-done((bf16[272,512]{1,0:T(8,128)(2,1)S(1)}, bf16[272,512]{1,0:T(8,128)(2,1)S(1)}, u32[]{:S(2)}, u32[]{:S(2)}) %collective-permute-start.39) | collective-permute-done | bytes 278560 | tf_op jit(solution)/shard_map/d_act/ppermute | solution.py:24
  116.7 1.1 collective-permute-start.43
  118.5 2.7 %collective-permute-start.41 = (f32[8,512]{1,0:T(8,128)S(1)}, f32[8,512]{1,0:T(8,128)S(1)}, u32[]{:S(2)}, u32[]{:S(2)}) collective-permute-start(f32[8,512]{1,0:T(8,128)S(1)} %pad_maximum_fusion.refs_0_), channel_id=1, source_target_pairs={{0,8},{8,0},{16,24},{24,16},{1,9},{9,1},{17,25},{25,17},{2,10},{10... | collective-permute-start | bytes 49160 | tf_op jit(solution)/shard_map/norm_backward/ppermute | solution.py:24
  121.1 2.9 %weight_gradient.3 = f32[1024,1024]{1,0:T(8,128)} custom-call(s32[2]{0:T(128)S(1)} %pad_add_fusion.place_ref, bf16[256,512]{1,0:T(8,128)(2,1)S(1)} %collective-permute-done.6.refs_1_.refs_0_, bf16[256,512]{1,0:T(8,128)(2,1)S(1)} %collective-permute-done.8.refs_0_.refs_1_, ...), custom_call_target="tpu_custom_call", output_to_operand_aliasing={{}: (13, {})} | custom-call | flops 1073741824 | bytes 2097152 | tf_op jit(solution)/shard_map/grad_weight/weight_gradient/pallas_call | solution.py:430
  (87 shorter events, 14.4 us)
Async XLA Ops:
  2.8 9.7 %copy-start = (f32[512]{0:T(512)S(1)}, f32[512]{0:T(512)}, u32[]{:S(2)}) copy-start(f32[512]{0:T(512)} %param.5) | copy-start | bytes 6148
  2.8 9.2 %collective-permute-start.2 = (f32[4,512]{1,0:T(4,128)S(1)}, f32[4,512]{1,0:T(4,128)S(1)}, u32[]{:S(2)}, u32[]{:S(2)}) collective-permute-start(f32[4,512]{1,0:T(4,128)S(1)} %pad_maximum_fusion.1), channel_id=1, source_target_pairs={{0,24},{8,16},{16,8},{24,0},{1,25},{9,17},{17,9},{25,1},{2,26},{10... | collective-permute-start | bytes 24584 | tf_op jit(solution)/shard_map/norm_stats/ppermute | solution.py:24
  7.9 4.5 %collective-permute-start.1 = (f32[4,512]{1,0:T(4,128)S(1)}, f32[4,512]{1,0:T(4,128)S(1)}, u32[]{:S(2)}, u32[]{:S(2)}) collective-permute-start(f32[4,512]{1,0:T(4,128)S(1)} %pad_maximum_fusion.1), channel_id=1, source_target_pairs={{0,16},{8,24},{16,0},{24,8},{1,17},{9,25},{17,1},{25,9},{2,18},{10... | collective-permute-start | bytes 24584 | tf_op jit(solution)/shard_map/norm_stats/ppermute | solution.py:24
  7.9 4.5 %collective-permute-start = (f32[4,512]{1,0:T(4,128)S(1)}, f32[4,512]{1,0:T(4,128)S(1)}, u32[]{:S(2)}, u32[]{:S(2)}) collective-permute-start(f32[4,512]{1,0:T(4,128)S(1)} %pad_maximum_fusion.1), channel_id=1, source_target_pairs={{0,8},{8,0},{16,24},{24,16},{1,9},{9,1},{17,25},{25,17},{2,10},{10... | collective-permute-start | bytes 24584 | tf_op jit(solution)/shard_map/norm_stats/ppermute | solution.py:24
  12.8 1.6 %collective-permute-start.6 = (bf16[256,512]{1,0:T(8,128)(2,1)S(1)}, bf16[256,512]{1,0:T(8,128)(2,1)S(1)}, u32[]{:S(2)}, u32[]{:S(2)}) collective-permute-start(bf16[256,512]{1,0:T(8,128)(2,1)S(1)} %bitcast.26), channel_id=1, source_target_pairs={{0,1},{1,0},{2,3},{3,2},{4,5},{5,4},{6,7},{7,6},{8,9},{9,8},{10,11... | collective-permute-start | bytes 786440 | tf_op jit(solution)/shard_map/act_gather/ppermute | solution.py:24
  12.9 8.4 %collective-permute-start.5 = (bf16[128,512]{1,0:T(8,128)(2,1)S(1)}, bf16[128,512]{1,0:T(8,128)(2,1)S(1)}, u32[]{:S(2)}, u32[]{:S(2)}) collective-permute-start(bf16[128,512]{1,0:T(8,128)(2,1)S(1)} %slice_bitcast_fusion), channel_id=1, source_target_pairs={{0,8},{16,0},{24,16},{8,24},{1,9},{17,1},{25,17},{9,25},{2,10},{18... | collective-permute-start | bytes 393224 | tf_op jit(solution)/shard_map/act_gather/ppermute | solution.py:34
  14.4 12.9 %collective-permute-start.7 = (bf16[256,512]{1,0:T(8,128)(2,1)S(1)}, bf16[256,512]{1,0:T(8,128)(2,1)S(1)}, u32[]{:S(2)}, u32[]{:S(2)}) collective-permute-start(bf16[256,512]{1,0:T(8,128)(2,1)S(1)} %bitcast.27), channel_id=1, source_target_pairs={{0,2},{1,3},{2,0},{3,1},{4,6},{5,7},{6,4},{7,5},{8,10},{9,11},{10,... | collective-permute-start | bytes 786440 | tf_op jit(solution)/shard_map/act_gather/ppermute | solution.py:24
  15.9 13.5 %collective-permute-start.11 = (bf16[256,512]{1,0:T(8,128)(2,1)S(1)}, bf16[256,512]{1,0:T(8,128)(2,1)S(1)}, u32[]{:S(2)}, u32[]{:S(2)}) collective-permute-start(bf16[256,512]{1,0:T(8,128)(2,1)S(1)} %bitcast.28), channel_id=1, source_target_pairs={{0,6},{1,7},{2,4},{3,5},{4,2},{5,3},{6,0},{7,1},{8,14},{9,15},{10,... | collective-permute-start | bytes 786440 | tf_op jit(solution)/shard_map/act_gather/ppermute | solution.py:24
  17.4 13.4 %collective-permute-start.9 = (bf16[256,512]{1,0:T(8,128)(2,1)S(1)}, bf16[256,512]{1,0:T(8,128)(2,1)S(1)}, u32[]{:S(2)}, u32[]{:S(2)}) collective-permute-start(bf16[256,512]{1,0:T(8,128)(2,1)S(1)} %bitcast.29), channel_id=1, source_target_pairs={{0,4},{1,5},{2,6},{3,7},{4,0},{5,1},{6,2},{7,3},{8,12},{9,13},{10,... | collective-permute-start | bytes 786440 | tf_op jit(solution)/shard_map/act_gather/ppermute | solution.py:24
  17.9 7.9 %collective-permute-start.4 = (bf16[128,512]{1,0:T(8,128)(2,1)S(1)}, bf16[128,512]{1,0:T(8,128)(2,1)S(1)}, u32[]{:S(2)}, u32[]{:S(2)}) collective-permute-start(bf16[128,512]{1,0:T(8,128)(2,1)S(1)} %slice_bitcast_fusion), channel_id=1, source_target_pairs={{0,24},{16,8},{24,0},{8,16},{1,25},{17,9},{25,1},{9,17},{2,26},{18... | collective-permute-start | bytes 393224 | tf_op jit(solution)/shard_map/act_gather/ppermute | solution.py:34
  21.3 6.0 %collective-permute-start.3 = (bf16[128,512]{1,0:T(8,128)(2,1)S(1)}, bf16[128,512]{1,0:T(8,128)(2,1)S(1)}, u32[]{:S(2)}, u32[]{:S(2)}) collective-permute-start(bf16[128,512]{1,0:T(8,128)(2,1)S(1)} %slice_bitcast_fusion), channel_id=1, source_target_pairs={{0,16},{16,24},{24,8},{8,0},{1,17},{17,25},{25,9},{9,1},{2,18},{18... | collective-permute-start | bytes 393224 | tf_op jit(solution)/shard_map/act_gather/ppermute | solution.py:34
  27.3 6.6 %collective-permute-start.8 = (bf16[256,512]{1,0:T(8,128)(2,1)S(1)}, bf16[256,512]{1,0:T(8,128)(2,1)S(1)}, u32[]{:S(2)}, u32[]{:S(2)}) collective-permute-start(bf16[256,512]{1,0:T(8,128)(2,1)S(1)} %collective-permute-done.7.refs_0_.refs_1_), channel_id=1, source_target_pairs={{0,1},{1,0},{2,3},{3,2},{4,5},{5,4},{6,7},{7,6},{8,9},{9,8},{10,11... | collective-permute-start | bytes 786440 | tf_op jit(solution)/shard_map/act_gather/ppermute | solution.py:24
  29.4 4.4 %collective-permute-start.12 = (bf16[256,512]{1,0:T(8,128)(2,1)S(1)}, bf16[256,512]{1,0:T(8,128)(2,1)S(1)}, u32[]{:S(2)}, u32[]{:S(2)}) collective-permute-start(bf16[256,512]{1,0:T(8,128)(2,1)S(1)} %collective-permute-done.11.refs_2_.refs_3_), channel_id=1, source_target_pairs={{0,1},{1,0},{2,3},{3,2},{4,5},{5,4},{6,7},{7,6},{8,9},{9,8},{10,11... | collective-permute-start | bytes 786440 | tf_op jit(solution)/shard_map/act_gather/ppermute | solution.py:24
  30.8 3.1 %collective-permute-start.10 = (bf16[256,512]{1,0:T(8,128)(2,1)S(1)}, bf16[256,512]{1,0:T(8,128)(2,1)S(1)}, u32[]{:S(2)}, u32[]{:S(2)}) collective-permute-start(bf16[256,512]{1,0:T(8,128)(2,1)S(1)} %collective-permute-done.9.refs_1_.refs_2_), channel_id=1, source_target_pairs={{0,1},{1,0},{2,3},{3,2},{4,5},{5,4},{6,7},{7,6},{8,9},{9,8},{10,11... | collective-permute-start | bytes 786440 | tf_op jit(solution)/shard_map/act_gather/ppermute | solution.py:24
  30.8 12.9 %collective-permute-start.15 = (bf16[384,512]{1,0:T(8,128)(2,1)S(1)}, bf16[384,512]{1,0:T(8,128)(2,1)S(1)}, u32[]{:S(2)}, u32[]{:S(2)}) collective-permute-start(bf16[384,512]{1,0:T(8,128)(2,1)S(1)} %constant_dynamic-update-slice_fusion.refs_0_.refs_4_), channel_id=1, source_target_pairs={{0,6},{1,7},{2,4},{3,5},{4,2},{5,3},{6,0},{7,1},{8,14},{9,15},{10,... | collective-permute-start | bytes 1179656 | tf_op jit(solution)/shard_map/act_gather/ppermute | solution.py:24
  35.4 9.3 %collective-permute-start.14 = (bf16[128,1024]{1,0:T(8,128)(2,1)S(1)}, bf16[128,1024]{1,0:T(8,128)(2,1)S(1)}, u32[]{:S(2)}, u32[]{:S(2)}) collective-permute-start(bf16[128,1024]{1,0:T(8,128)(2,1)S(1)} %get-tuple-element.71.refs_1_.refs_9_), channel_id=1, source_target_pairs={{0,16},{16,24},{24,8},{8,0},{1,17},{17,25},{25,9},{9,1},{2,18},{18... | collective-permute-start | bytes 786440 | tf_op jit(solution)/shard_map/z_ring/ppermute | solution.py:34
  37.5 14.2 %collective-permute-start.19 = (bf16[384,512]{1,0:T(8,128)(2,1)S(1)}, bf16[384,512]{1,0:T(8,128)(2,1)S(1)}, u32[]{:S(2)}, u32[]{:S(2)}) collective-permute-start(bf16[384,512]{1,0:T(8,128)(2,1)S(1)} %constant_dynamic-update-slice_fusion.refs_0_.refs_4_), channel_id=1, source_target_pairs={{0,4},{1,5},{2,6},{3,7},{4,0},{5,1},{6,2},{7,3},{8,12},{9,13},{10,... | collective-permute-start | bytes 1179656 | tf_op jit(solution)/shard_map/act_gather/ppermute | solution.py:24
  39.0 14.8 %collective-permute-start.16 = (bf16[384,512]{1,0:T(8,128)(2,1)S(1)}, bf16[384,512]{1,0:T(8,128)(2,1)S(1)}, u32[]{:S(2)}, u32[]{:S(2)}) collective-permute-start(bf16[384,512]{1,0:T(8,128)(2,1)S(1)} %constant_dynamic-update-slice_fusion.refs_0_.refs_4_), channel_id=1, source_target_pairs={{0,2},{1,3},{2,0},{3,1},{4,6},{5,7},{6,4},{7,5},{8,10},{9,11},{10,... | collective-permute-start | bytes 1179656 | tf_op jit(solution)/shard_map/act_gather/ppermute | solution.py:24
  44.7 9.1 %collective-permute-start.17 = (bf16[128,1024]{1,0:T(8,128)(2,1)S(1)}, bf16[128,1024]{1,0:T(8,128)(2,1)S(1)}, u32[]{:S(2)}, u32[]{:S(2)}) collective-permute-start(bf16[128,1024]{1,0:T(8,128)(2,1)S(1)} %collective-permute-done.14.refs_3_.refs_11_), channel_id=1, source_target_pairs={{0,16},{16,24},{24,8},{8,0},{1,17},{17,25},{25,9},{9,1},{2,18},{18... | collective-permute-start | bytes 786440 | tf_op jit(solution)/shard_map/z_ring/ppermute | solution.py:34
  46.8 10.6 %collective-permute-start.13 = (bf16[384,512]{1,0:T(8,128)(2,1)S(1)}, bf16[384,512]{1,0:T(8,128)(2,1)S(1)}, u32[]{:S(2)}, u32[]{:S(2)}) collective-permute-start(bf16[384,512]{1,0:T(8,128)(2,1)S(1)} %constant_dynamic-update-slice_fusion.refs_0_.refs_4_), channel_id=1, source_target_pairs={{0,1},{1,0},{2,3},{3,2},{4,5},{5,4},{6,7},{7,6},{8,9},{9,8},{10,11... | collective-permute-start | bytes 1179656 | tf_op jit(solution)/shard_map/z_far/ppermute | solution.py:24
  51.8 5.8 %collective-permute-start.20 = (bf16[384,512]{1,0:T(8,128)(2,1)S(1)}, bf16[384,512]{1,0:T(8,128)(2,1)S(1)}, u32[]{:S(2)}, u32[]{:S(2)}) collective-permute-start(bf16[384,512]{1,0:T(8,128)(2,1)S(1)} %collective-permute-done.19.refs_1_.refs_6_), channel_id=1, source_target_pairs={{0,1},{1,0},{2,3},{3,2},{4,5},{5,4},{6,7},{7,6},{8,9},{9,8},{10,11... | collective-permute-start | bytes 1179656 | tf_op jit(solution)/shard_map/z_far/ppermute | solution.py:24
  51.8 5.7 %collective-permute-start.21 = (bf16[384,512]{1,0:T(8,128)(2,1)S(1)}, bf16[384,512]{1,0:T(8,128)(2,1)S(1)}, u32[]{:S(2)}, u32[]{:S(2)}) collective-permute-start(bf16[384,512]{1,0:T(8,128)(2,1)S(1)} %collective-permute-done.15.refs_1_.refs_7_), channel_id=1, source_target_pairs={{0,1},{1,0},{2,3},{3,2},{4,5},{5,4},{6,7},{7,6},{8,9},{9,8},{10,11... | collective-permute-start | bytes 1179656 | tf_op jit(solution)/shard_map/z_far/ppermute | solution.py:24
  53.8 3.7 %collective-permute-start.18 = (bf16[384,512]{1,0:T(8,128)(2,1)S(1)}, bf16[384,512]{1,0:T(8,128)(2,1)S(1)}, u32[]{:S(2)}, u32[]{:S(2)}) collective-permute-start(bf16[384,512]{1,0:T(8,128)(2,1)S(1)} %collective-permute-done.16.refs_0_.refs_5_), channel_id=1, source_target_pairs={{0,1},{1,0},{2,3},{3,2},{4,5},{5,4},{6,7},{7,6},{8,9},{9,8},{10,11... | collective-permute-start | bytes 1179656 | tf_op jit(solution)/shard_map/z_far/ppermute | solution.py:24
  53.9 9.5 %collective-permute-start.22 = (bf16[128,1024]{1,0:T(8,128)(2,1)S(1)}, bf16[128,1024]{1,0:T(8,128)(2,1)S(1)}, u32[]{:S(2)}, u32[]{:S(2)}) collective-permute-start(bf16[128,1024]{1,0:T(8,128)(2,1)S(1)} %collective-permute-done.17.refs_5_.refs_13_), channel_id=1, source_target_pairs={{0,16},{16,24},{24,8},{8,0},{1,17},{17,25},{25,9},{9,1},{2,18},{18... | collective-permute-start | bytes 786440 | tf_op jit(solution)/shard_map/z_far/ppermute | solution.py:34
  66.1 1.7 %collective-permute-start.23 = (bf16[4,32,1280]{2,1,0:T(8,128)(2,1)S(1)}, bf16[4,32,1280]{2,1,0:T(8,128)(2,1)S(1)}, u32[]{:S(2)}, u32[]{:S(2)}) collective-permute-start(bf16[4,32,1280]{2,1,0:T(8,128)(2,1)S(1)} %get-tuple-element.84), channel_id=1, source_target_pairs={{0,1},{1,0},{2,3},{3,2},{4,5},{5,4},{6,7},{7,6},{8,9},{9,8},{10,11... | collective-permute-start | bytes 983048 | tf_op jit(solution)/shard_map/kernel/ppermute | solution.py:24
  67.9 6.4 %collective-permute-start.24 = (bf16[32,1280]{1,0:T(8,128)(2,1)S(1)}, bf16[32,1280]{1,0:T(8,128)(2,1)S(1)}, u32[]{:S(2)}, u32[]{:S(2)}) collective-permute-start(bf16[32,1280]{1,0:T(8,128)(2,1)S(1)} %get-tuple-element.122), channel_id=1, source_target_pairs={{0,2},{1,3},{2,0},{3,1},{4,6},{5,7},{6,4},{7,5},{8,10},{9,11},{10,... | collective-permute-start | bytes 245768 | tf_op jit(solution)/shard_map/kernel/ppermute | solution.py:24
  69.5 5.4 %collective-permute-start.26 = (bf16[32,1280]{1,0:T(8,128)(2,1)S(1)}, bf16[32,1280]{1,0:T(8,128)(2,1)S(1)}, u32[]{:S(2)}, u32[]{:S(2)}) collective-permute-start(bf16[32,1280]{1,0:T(8,128)(2,1)S(1)} %get-tuple-element.123), channel_id=1, source_target_pairs={{0,6},{1,7},{2,4},{3,5},{4,2},{5,3},{6,0},{7,1},{8,14},{9,15},{10,... | collective-permute-start | bytes 245768 | tf_op jit(solution)/shard_map/kernel/ppermute | solution.py:24
  70.4 5.7 %collective-permute-start.25 = (bf16[32,1280]{1,0:T(8,128)(2,1)S(1)}, bf16[32,1280]{1,0:T(8,128)(2,1)S(1)}, u32[]{:S(2)}, u32[]{:S(2)}) collective-permute-start(bf16[32,1280]{1,0:T(8,128)(2,1)S(1)} %get-tuple-element.124), channel_id=1, source_target_pairs={{0,4},{1,5},{2,6},{3,7},{4,0},{5,1},{6,2},{7,3},{8,12},{9,13},{10,... | collective-permute-start | bytes 245768 | tf_op jit(solution)/shard_map/kernel/ppermute | solution.py:24
  72.1 9.7 %collective-permute-start.34 = (bf16[128,512]{1,0:T(8,128)(2,1)S(1)}, bf16[128,512]{1,0:T(8,128)(2,1)S(1)}, u32[]{:S(2)}, u32[]{:S(2)}) collective-permute-start(bf16[128,512]{1,0:T(8,128)(2,1)S(1)} %get-tuple-element.90), channel_id=1, source_target_pairs={{0,16},{16,24},{24,8},{8,0},{1,17},{17,25},{25,9},{9,1},{2,18},{18... | collective-permute-start | bytes 393224 | tf_op jit(solution)/shard_map/kernel/ppermute | solution.py:34
  76.2 6.1 %collective-permute-start.32 = (bf16[32,1280]{1,0:T(8,128)(2,1)S(1)}, bf16[32,1280]{1,0:T(8,128)(2,1)S(1)}, u32[]{:S(2)}, u32[]{:S(2)}) collective-permute-start(bf16[32,1280]{1,0:T(8,128)(2,1)S(1)} %get-tuple-element.92.refs_0_), channel_id=1, source_target_pairs={{0,6},{1,7},{2,4},{3,5},{4,2},{5,3},{6,0},{7,1},{8,14},{9,15},{10,... | collective-permute-start | bytes 245768 | tf_op jit(solution)/shard_map/kernel/ppermute | solution.py:24
  77.9 4.9 %collective-permute-start.30 = (bf16[32,1280]{1,0:T(8,128)(2,1)S(1)}, bf16[32,1280]{1,0:T(8,128)(2,1)S(1)}, u32[]{:S(2)}, u32[]{:S(2)}) collective-permute-start(bf16[32,1280]{1,0:T(8,128)(2,1)S(1)} %get-tuple-element.92.refs_0_), channel_id=1, source_target_pairs={{0,4},{1,5},{2,6},{3,7},{4,0},{5,1},{6,2},{7,3},{8,12},{9,13},{10,... | collective-permute-start | bytes 245768 | tf_op jit(solution)/shard_map/kernel/ppermute | solution.py:24
  78.6 4.4 %collective-permute-start.28 = (bf16[32,1280]{1,0:T(8,128)(2,1)S(1)}, bf16[32,1280]{1,0:T(8,128)(2,1)S(1)}, u32[]{:S(2)}, u32[]{:S(2)}) collective-permute-start(bf16[32,1280]{1,0:T(8,128)(2,1)S(1)} %get-tuple-element.92.refs_0_), channel_id=1, source_target_pairs={{0,2},{1,3},{2,0},{3,1},{4,6},{5,7},{6,4},{7,5},{8,10},{9,11},{10,... | collective-permute-start | bytes 245768 | tf_op jit(solution)/shard_map/kernel/ppermute | solution.py:24
  79.7 6.9 %collective-permute-start.35 = (bf16[128,512]{1,0:T(8,128)(2,1)S(1)}, bf16[128,512]{1,0:T(8,128)(2,1)S(1)}, u32[]{:S(2)}, u32[]{:S(2)}) collective-permute-start(bf16[128,512]{1,0:T(8,128)(2,1)S(1)} %get-tuple-element.91), channel_id=1, source_target_pairs={{0,24},{16,8},{24,0},{8,16},{1,25},{17,9},{25,1},{9,17},{2,26},{18... | collective-permute-start | bytes 393224 | tf_op jit(solution)/shard_map/kernel/ppermute | solution.py:34
  81.8 7.3 %collective-permute-start.27 = (bf16[32,1280]{1,0:T(8,128)(2,1)S(1)}, bf16[32,1280]{1,0:T(8,128)(2,1)S(1)}, u32[]{:S(2)}, u32[]{:S(2)}) collective-permute-start(bf16[32,1280]{1,0:T(8,128)(2,1)S(1)} %get-tuple-element.92.refs_0_), channel_id=1, source_target_pairs={{0,1},{1,0},{2,3},{3,2},{4,5},{5,4},{6,7},{7,6},{8,9},{9,8},{10,11... | collective-permute-start | bytes 245768 | tf_op jit(solution)/shard_map/kernel/ppermute | solution.py:24
  82.3 6.8 %collective-permute-start.33 = (bf16[32,1280]{1,0:T(8,128)(2,1)S(1)}, bf16[32,1280]{1,0:T(8,128)(2,1)S(1)}, u32[]{:S(2)}, u32[]{:S(2)}) collective-permute-start(bf16[32,1280]{1,0:T(8,128)(2,1)S(1)} %collective-permute-done.32.refs_6_), channel_id=1, source_target_pairs={{0,1},{1,0},{2,3},{3,2},{4,5},{5,4},{6,7},{7,6},{8,9},{9,8},{10,11... | collective-permute-start | bytes 245768 | tf_op jit(solution)/shard_map/kernel/ppermute | solution.py:24
  82.8 6.2 %collective-permute-start.31 = (bf16[32,1280]{1,0:T(8,128)(2,1)S(1)}, bf16[32,1280]{1,0:T(8,128)(2,1)S(1)}, u32[]{:S(2)}, u32[]{:S(2)}) collective-permute-start(bf16[32,1280]{1,0:T(8,128)(2,1)S(1)} %collective-permute-done.30.refs_4_), channel_id=1, source_target_pairs={{0,1},{1,0},{2,3},{3,2},{4,5},{5,4},{6,7},{7,6},{8,9},{9,8},{10,11... | collective-permute-start | bytes 245768 | tf_op jit(solution)/shard_map/kernel/ppermute | solution.py:24
  83.0 6.1 %collective-permute-start.29 = (bf16[32,1280]{1,0:T(8,128)(2,1)S(1)}, bf16[32,1280]{1,0:T(8,128)(2,1)S(1)}, u32[]{:S(2)}, u32[]{:S(2)}) collective-permute-start(bf16[32,1280]{1,0:T(8,128)(2,1)S(1)} %collective-permute-done.28.refs_2_), channel_id=1, source_target_pairs={{0,1},{1,0},{2,3},{3,2},{4,5},{5,4},{6,7},{7,6},{8,9},{9,8},{10,11... | collective-permute-start | bytes 245768 | tf_op jit(solution)/shard_map/kernel/ppermute | solution.py:24
  86.6 7.2 %collective-permute-start.36 = (bf16[128,512]{1,0:T(8,128)(2,1)S(1)}, bf16[128,512]{1,0:T(8,128)(2,1)S(1)}, u32[]{:S(2)}, u32[]{:S(2)}) collective-permute-start(bf16[128,512]{1,0:T(8,128)(2,1)S(1)} %get-tuple-element.101), channel_id=1, source_target_pairs={{0,8},{16,0},{24,16},{8,24},{1,9},{17,1},{25,17},{9,25},{2,10},{18... | collective-permute-start | bytes 393224 | tf_op jit(solution)/shard_map/kernel/ppermute | solution.py:34
  95.6 2.8 %collective-permute-start.37 = (bf16[4,272,512]{2,1,0:T(8,128)(2,1)S(1)}, bf16[4,272,512]{2,1,0:T(8,128)(2,1)S(1)}, u32[]{:S(2)}, u32[]{:S(2)}) collective-permute-start(bf16[4,272,512]{2,1,0:T(8,128)(2,1)S(1)} %d_act_matmul.2), channel_id=1, source_target_pairs={{0,1},{1,0},{2,3},{3,2},{4,5},{5,4},{6,7},{7,6},{8,9},{9,8},{10,11... | collective-permute-start | bytes 3342344 | tf_op jit(solution)/shard_map/d_act/ppermute | solution.py:24
  100.3 9.6 %collective-permute-start.38 = (bf16[272,512]{1,0:T(8,128)(2,1)S(1)}, bf16[272,512]{1,0:T(8,128)(2,1)S(1)}, u32[]{:S(2)}, u32[]{:S(2)}) collective-permute-start(bf16[272,512]{1,0:T(8,128)(2,1)S(1)} %get-tuple-element.105), channel_id=1, source_target_pairs={{0,2},{1,3},{2,0},{3,1},{4,6},{5,7},{6,4},{7,5},{8,10},{9,11},{10,... | collective-permute-start | bytes 835592 | tf_op jit(solution)/shard_map/d_act/ppermute | solution.py:24
  101.6 14.4 %collective-permute-start.39 = (bf16[272,512]{1,0:T(8,128)(2,1)S(1)}, bf16[272,512]{1,0:T(8,128)(2,1)S(1)}, u32[]{:S(2)}, u32[]{:S(2)}) collective-permute-start(bf16[272,512]{1,0:T(8,128)(2,1)S(1)} %get-tuple-element.106), channel_id=1, source_target_pairs={{0,4},{1,5},{2,6},{3,7},{4,0},{5,1},{6,2},{7,3},{8,12},{9,13},{10,... | collective-permute-start | bytes 835592 | tf_op jit(solution)/shard_map/d_act/ppermute | solution.py:24
  103.2 12.9 %collective-permute-start.40 = (bf16[272,512]{1,0:T(8,128)(2,1)S(1)}, bf16[272,512]{1,0:T(8,128)(2,1)S(1)}, u32[]{:S(2)}, u32[]{:S(2)}) collective-permute-start(bf16[272,512]{1,0:T(8,128)(2,1)S(1)} %get-tuple-element.107), channel_id=1, source_target_pairs={{0,6},{1,7},{2,4},{3,5},{4,2},{5,3},{6,0},{7,1},{8,14},{9,15},{10,... | collective-permute-start | bytes 835592 | tf_op jit(solution)/shard_map/d_act/ppermute | solution.py:24
  103.8 14.6 %collective-permute-start.44 = (bf16[128,512]{1,0:T(8,128)(2,1)S(1)}, bf16[128,512]{1,0:T(8,128)(2,1)S(1)}, u32[]{:S(2)}, u32[]{:S(2)}) collective-permute-start(bf16[128,512]{1,0:T(8,128)(2,1)S(1)} %collective-permute-done.34.refs_8_), channel_id=1, source_target_pairs={{0,1},{1,0},{2,3},{3,2},{4,5},{5,4},{6,7},{7,6},{8,9},{9,8},{10,11... | collective-permute-start | bytes 393224 | tf_op jit(solution)/shard_map/grad_weight/ppermute | solution.py:24
  103.8 17.3 %collective-permute-start.45 = (bf16[128,512]{1,0:T(8,128)(2,1)S(1)}, bf16[128,512]{1,0:T(8,128)(2,1)S(1)}, u32[]{:S(2)}, u32[]{:S(2)}) collective-permute-start(bf16[128,512]{1,0:T(8,128)(2,1)S(1)} %collective-permute-done.35.refs_9_), channel_id=1, source_target_pairs={{0,1},{1,0},{2,3},{3,2},{4,5},{5,4},{6,7},{7,6},{8,9},{9,8},{10,11... | collective-permute-start | bytes 393224 | tf_op jit(solution)/shard_map/grad_weight/ppermute | solution.py:24
  109.8 11.3 %collective-permute-start.46 = (bf16[128,512]{1,0:T(8,128)(2,1)S(1)}, bf16[128,512]{1,0:T(8,128)(2,1)S(1)}, u32[]{:S(2)}, u32[]{:S(2)}) collective-permute-start(bf16[128,512]{1,0:T(8,128)(2,1)S(1)} %collective-permute-done.36.refs_10_), channel_id=1, source_target_pairs={{0,1},{1,0},{2,3},{3,2},{4,5},{5,4},{6,7},{7,6},{8,9},{9,8},{10,11... | collective-permute-start | bytes 393224 | tf_op jit(solution)/shard_map/grad_weight/ppermute | solution.py:24
  116.7 7.4 %collective-permute-start.43 = (f32[8,512]{1,0:T(8,128)S(1)}, f32[8,512]{1,0:T(8,128)S(1)}, u32[]{:S(2)}, u32[]{:S(2)}) collective-permute-start(f32[8,512]{1,0:T(8,128)S(1)} %pad_maximum_fusion.refs_0_), channel_id=1, source_target_pairs={{0,24},{8,16},{16,8},{24,0},{1,25},{9,17},{17,9},{25,1},{2,26},{10... | collective-permute-start | bytes 49160 | tf_op jit(solution)/shard_map/norm_backward/ppermute | solution.py:24
  117.7 6.3 %collective-permute-start.42 = (f32[8,512]{1,0:T(8,128)S(1)}, f32[8,512]{1,0:T(8,128)S(1)}, u32[]{:S(2)}, u32[]{:S(2)}) collective-permute-start(f32[8,512]{1,0:T(8,128)S(1)} %pad_maximum_fusion.refs_0_), channel_id=1, source_target_pairs={{0,16},{8,24},{16,0},{24,8},{1,17},{9,25},{17,1},{25,9},{2,18},{10... | collective-permute-start | bytes 49160 | tf_op jit(solution)/shard_map/norm_backward/ppermute | solution.py:24
  118.5 5.6 %collective-permute-start.41 = (f32[8,512]{1,0:T(8,128)S(1)}, f32[8,512]{1,0:T(8,128)S(1)}, u32[]{:S(2)}, u32[]{:S(2)}) collective-permute-start(f32[8,512]{1,0:T(8,128)S(1)} %pad_maximum_fusion.refs_0_), channel_id=1, source_target_pairs={{0,8},{8,0},{16,24},{24,16},{1,9},{9,1},{17,25},{25,17},{2,10},{10... | collective-permute-start | bytes 49160 | tf_op jit(solution)/shard_map/norm_backward/ppermute | solution.py:24
  (2 other events, 19.5 us)

commit v12 on v11

--- a/solution.py
+++ b/solution.py
@@ -371,56 +371,90 @@
     )(place, *pieces)
 
 
-def weight_grad_kernel(n_far, aliased, half, tile, which, place_ref, *refs):
-    near = [refs[:half], refs[half : 2 * half]]
-    arrived = refs[2 * half : 2 * half + n_far]
-    dz_ref = refs[2 * half + n_far]
-    out_ref, act, product, sems = refs[2 * half + n_far + 1 + aliased :]
-    block, parity = which
-    chosen = held_place(place_ref[0], place_ref[1], block, 2 * half, n_far + 1)
-    out_row = 2 * block + ((place_ref[1] & 1) ^ parity)
-    local_rows = near[0][0].shape[0] // 2
-    rows = dz_ref.shape[1]
+def rows_product(act, dz, width, tile, write):
+    for i in range(width // tile):
+        write(
+            i,
+            lax.dot_general(
+                act[:, pl.ds(i * tile, tile)],
+                dz[...],
+                (((0,), (0,)), ((), ())),
+                preferred_element_type=f32,
+            ),
+        )
+
+
+def weight_grad_kernel(n_batch, half, tile, block, place_ref, *refs):
+    own, far = refs[:half], refs[half : 2 * half]
+    dz_ref, out_ref, act = refs[2 * half :]
+    local_rows = own[0].shape[0] // 2
+    chosen = held_place(place_ref[0], place_ref[1], block, 2 * half, n_batch)
     for e in range(half):
 
         @pl.when(chosen == e)
         def _():
-            act[pl.ds(0, local_rows)] = near[0][e][:local_rows]
-            act[pl.ds(rows, local_rows)] = near[0][e][local_rows:]
-            act[pl.ds(local_rows, rows - local_rows)] = near[1][e][...]
-
-    for s in range(n_far):
-        act[pl.ds(rows + (s + 1) * local_rows, local_rows)] = arrived[s][...]
+            act[:local_rows] = own[e][:local_rows]
+            act[local_rows:] = far[e][...]
+
+    def write(i, product):
+        out_ref[pl.ds(i * tile, tile)] = product
+
+    rows_product(act, dz_ref.at[0], act.shape[1], tile, write)
+
+
+def weight_grad_call(place, n_batch, block, own, far, dz):
+    width = own[0].shape[1]
+    _, rows, columns = dz.shape
+    tile = min(256, width)
+    operands = [place] + list(own) + list(far) + [dz]
+    return pl.pallas_call(
+        functools.partial(weight_grad_kernel, n_batch, len(own), tile, block),
+        out_shape=jax.ShapeDtypeStruct((width, columns), f32),
+        in_specs=[IN_SMEM] + [IN_VMEM] * (len(operands) - 1),
+        out_specs=IN_VMEM,
+        scratch_shapes=[pltpu.VMEM((rows, width), bf16)],
+        compiler_params=params(8),
+        cost_estimate=cost(2 * rows * width * columns, 2 * rows * columns),
+        name="weight_gradient_0",
+    )(*operands)
+
+
+def weight_grad_last_kernel(n_batch, half, tile, aliased, which, place_ref, *refs):
+    own, (blocks_ref, dz_ref, before_ref) = refs[:half], refs[half : half + 3]
+    out_ref, act, product, sems = refs[half + 3 + aliased :]
+    local_rows = own[0].shape[0] // 2
+    block, parity = which
+    chosen = held_place(place_ref[0], place_ref[1], block, 2 * half, n_batch)
+    out_row = 2 * block + ((place_ref[1] & 1) ^ parity)
+    for e in range(half):
+
+        @pl.when(chosen == e)
+        def _():
+            act[:local_rows] = own[e][local_rows:]
+
+    act[local_rows:] = blocks_ref[...]
     width = act.shape[1]
     copies = []
-    for i in range(width // tile):
-        total = None
-        for v in range(2):
-            part = lax.dot_general(
-                act[pl.ds(v * rows, rows), pl.ds(i * tile, tile)],
-                dz_ref[v],
-                (((0,), (0,)), ((), ())),
-                preferred_element_type=f32,
-            )
-            total = part if total is None else total + part
-        product[pl.ds(i * tile, tile)] = total
+
+    def write(i, part):
+        here = pl.ds(i * tile, tile)
+        product[here] = before_ref[here] + part
         start = pl.multiple_of(out_row * width + i * tile, tile)
         copies.append(
-            pltpu.make_async_copy(
-                product.at[pl.ds(i * tile, tile)], out_ref.at[pl.ds(start, tile)], sems.at[i]
-            )
+            pltpu.make_async_copy(product.at[here], out_ref.at[pl.ds(start, tile)], sems.at[i])
         )
         copies[-1].start()
+
+    rows_product(act, dz_ref.at[1], width, tile, write)
     for copy in copies:
         copy.wait()
 
 
-def weight_grad_call(place, which, near, arrived, dz, features, before):
-    half = len(near[0])
-    width = near[0][0].shape[1]
+def weight_grad_last_call(place, which, own, blocks, dz, product, features, before):
+    width = own[0].shape[1]
     _, rows, columns = dz.shape
     tile = min(256, width)
-    operands = [place] + [x for group in near for x in group] + list(arrived) + [dz]
+    operands = [place] + list(own) + [blocks, dz, product]
     specs = [IN_SMEM] + [IN_VMEM] * (len(operands) - 1)
     aliases = {}
     if before is not None:
@@ -429,31 +463,39 @@
         specs.append(ANYWHERE)
     return pl.pallas_call(
         functools.partial(
-            weight_grad_kernel, len(arrived), int(before is not None), half, tile, which
+            weight_grad_last_kernel,
+            rows // (own[0].shape[0] // 2),
+            len(own),
+            tile,
+            int(before is not None),
+            which,
         ),
         out_shape=jax.ShapeDtypeStruct((features, columns), f32),
         in_specs=specs,
         out_specs=ANYWHERE,
         scratch_shapes=[
-            pltpu.VMEM((2 * rows, width), bf16),
+            pltpu.VMEM((rows, width), bf16),
             pltpu.VMEM((width, columns), f32),
             pltpu.SemaphoreType.DMA((width // tile,)),
         ],
         input_output_aliases=aliases,
-        compiler_params=params(12),
-        cost_estimate=cost(4 * rows * width * columns, 4 * width * columns),
-        name="weight_gradient",
+        compiler_params=params(10),
+        cost_estimate=cost(2 * rows * width * columns, 4 * width * columns),
+        name="weight_gradient_1",
     )(*operands)
-
-
-def gather_pieces(x, n_col):
-    return sibling_pieces(link_pieces(x, n_col), n_col)
 
 
 def link_pieces(x, n_col):
     pieces = {0: x}
-    for k in range(2, n_col, 2):
-        pieces[k] = xor_send(x, "col", k)
+    half = x.shape[0] // 2
+    for k in sorted(range(2, n_col, 2), key=lambda k: (bin(k).count("1"), k)):
+        low, high = k & -k, 1 << (k.bit_length() - 1)
+        if low == high:
+            pieces[k] = xor_send(x, "col", k)
+        else:
+            first = xor_send(pieces[k ^ low][:half], "col", low)
+            second = xor_send(pieces[k ^ high][half:], "col", high)
+            pieces[k] = jnp.concatenate([first, second])
     return pieces
 
 
@@ -561,33 +603,40 @@
         z_own0, z_own1 = z_of(pieces, [[0, 1], far, [k + 1 for k in far]])
     with jax.named_scope("z_ring"):
         z_ring = [z_own1, ring_send(z_own1, "batch", 1)]
-        z_ring[1], far_pieces[far[-1]] = lax.optimization_barrier((z_ring[1], far_pieces[far[-1]]))
+        z_ring[1], far_pieces[far[0]] = lax.optimization_barrier((z_ring[1], far_pieces[far[0]]))
         z_ring.append(ring_send(z_ring[1], "batch", 1))
     with jax.named_scope("z_far"):
         start = z_call(
-            place, [0, far[-1]], [far_pieces[0], far_pieces[far[-1]]], held_weight, None, False, local_rows
-        )
-        start, far_pieces[far[0]], z_ring[2] = lax.optimization_barrier(
-            (start, far_pieces[far[0]], z_ring[2])
+            place, [0] + far[:-1], [far_pieces[k] for k in [0] + far[:-1]], held_weight, None, False, local_rows
+        )
+        picked = list(pick_call(place, [pieces[k] for k in evens], n_batch, n_col))
+        start, far_pieces[far[-1]], z_ring[2], picked = lax.optimization_barrier(
+            (start, far_pieces[far[-1]], z_ring[2], picked)
         )
         far_pieces = sibling_pieces(far_pieces, n_col)
         for _ in range(3, n_batch):
             z_ring.append(ring_send(z_ring[-1], "batch", 1))
-        z_far = z_of(far_pieces, [far[:-1], odds], start)
+        z_far = z_of(far_pieces, [odds[:-1] + far[-1:] + odds[-1:]], start)
         slots = list(zip([z_own0] + list(z_far), z_ring))
     with jax.named_scope("kernel"):
         even_part, odd_part = strip_call(place, slots, n_col)
         even_part = even_part + xor_send(odd_part, "col", 1).astype(f32)
-        even_part, held_back = lax.optimization_barrier((even_part, [pieces[k] for k in evens]))
+        early = len(picked) // 3
+        even_part, picked[:early] = lax.optimization_barrier((even_part, picked[:early]))
+
+        def sent(i):
+            return ring_send(picked[i], "batch", 1 + i % (n_batch - 1))
+
         strip = even_part[0]
         for k in far:
             strip = strip + xor_send(even_part[k // 2].astype(bf16), "col", k).astype(f32)
-        picked = pick_call(place, held_back, n_batch, n_col)
-        blocks = [
-            ring_send(x, "batch", 1 + i % (n_batch - 1)) for i, x in enumerate(picked)
-        ]
-        strips = gather_pieces(strip.astype(bf16), n_col)
-        strips, blocks[:-1] = lax.optimization_barrier((strips, blocks[:-1]))
+        strip_b = strip.astype(bf16)
+        strips = {0: strip_b}
+        for k in far:
+            strips[k] = xor_send(strip_b, "col", k)
+        strips = sibling_pieces(strips, n_col)
+        blocks = [sent(i) for i in range(early)]
+        strips, blocks = lax.optimization_barrier((strips, blocks))
     with jax.named_scope("dz"):
         constants = (
             4.0 * scale / denom,
@@ -599,27 +648,41 @@
             1.0 / denom / n_batch,
         )
         dz, share = dz_call(place, strip, [strips[k] for k in range(n_col)], slots, constants)
-        dz, blocks[-1] = lax.optimization_barrier((dz, blocks[-1]))
+        blocks += [sent(i) for i in range(early, 2 * early)]
+        dz, blocks[early:] = lax.optimization_barrier((dz, blocks[early:]))
     with jax.named_scope("d_act"):
         (away,) = d_act_call(place, dz, share, held_weight, n_batch, n_col, None)
         got = xor_send(away, "col", 1)
         *sends, d_act = d_act_call(place, dz, share, held_weight, n_batch, n_col, got)
         arrived = [xor_send(part, "col", k) for k, part in zip(far, sends)]
     with jax.named_scope("grad_weight"):
+        late = picked[2 * early :]
+        d_act, picked[2 * early :] = lax.optimization_barrier((d_act, late))
+        blocks += [sent(i) for i in range(2 * early, len(picked))]
+        sides = ((0, evens), (1, odds))
+        products = {}
+        for block in range(n_col // n_batch // 2):
+            for parity, ks in sides:
+                products[block, parity] = weight_grad_call(
+                    place, n_batch, block, [pieces[k] for k in ks], [far_pieces[k] for k in ks], dz
+                )
         grad_weight = None
         for block in range(n_col // n_batch // 2):
-            mine = blocks[block * (n_batch - 1) : (block + 1) * (n_batch - 1)]
-            other = [xor_send(x, "col", 1) for x in mine]
-            for parity, ks, far_rows in ((0, evens, mine), (1, odds, other)):
-                grad_weight = weight_grad_call(
+            mine = jnp.concatenate(blocks[block * (n_batch - 1) : (block + 1) * (n_batch - 1)])
+            other = xor_send(mine, "col", 1)
+            for (parity, ks), far_rows in zip(sides, (mine, other)):
+                grad_weight = weight_grad_last_call(
                     place,
                     (block, parity),
-                    [[group[k] for k in ks] for group in (pieces, far_pieces)],
+                    [pieces[k] for k in ks],
                     far_rows,
                     dz,
+                    products[block, parity],
                     features // n_batch,
                     grad_weight,
                 )
+                if block == 0 and parity == 0:
+                    arrived, grad_weight = lax.optimization_barrier((arrived, grad_weight))
     with jax.named_scope("norm_backward"):
         share = exchange_sum(share_of(part[tall:]) for part in [d_act] + arrived)
         d_act = d_act[:tall]

time: 125 us -> 135 us (1.080)
  waiting for transfers between devices: 41.6 us -> 52.1 us
  starting transfers between devices: 47.5 us -> 46 us
    ppermute x9, waiting for transfers between devices: 12 us -> 17.9 us  [ring_send(): lax.ppermute(x, axis, [(order[i], order[(i + d) % n]) for i in range(n)])]
    ppermute x38, waiting for transfers between devices: 29.6 us -> 34.2 us  [xor_send(): return lax.ppermute(x, axis, [(i, i ^ k) for i in range(n)])]
    ppermute x9, starting transfers between devices: 17.9 us -> 15.7 us  [ring_send(): lax.ppermute(x, axis, [(order[i], order[(i + d) % n]) for i in range(n)])]
    pallas_call x2 -> x4, Pallas kernels: 5.79 us -> 7.43 us  [the longest x2 4.77 us: weight_grad_last_call(): pl.pallas_call(functools.partial(weight_grad_last_kernel, rows // (own[0]...]
    pallas_call x6 -> x5, Pallas kernels: 9.68 us -> 8.95 us  [z_call(): pl.pallas_call(functools.partial(z_kernel, tuple(ks), before is None, las...]
  transfers between devices with their start and end apart: 47 -> 47, of which waited for: 20 -> 25; matrix products, arithmetic and copies ran while one was open for 1% -> 1% of each run, Pallas kernels for 19% -> 17%
where the time goes in v12:
time: 135 us
  waiting for transfers between devices  52.1 us (39%)
  starting transfers between devices  46 us (34%)
  Pallas kernels  32.4 us (24%)
  other arithmetic  3.23 us (2%)
    ppermute x38, waiting for transfers between devices, xor_send(): return lax.ppermute(x, axis, [(i, i ^ k) for i in range(n)])  34.2 us
    ppermute x38, starting transfers between devices, xor_send(): return lax.ppermute(x, axis, [(i, i ^ k) for i in range(n)])  30.3 us
    ppermute x9, waiting for transfers between devices, ring_send(): lax.ppermute(x, axis, [(order[i], order[(i + d) % n]) for i in range(n)])  17.9 us
    ppermute x9, starting transfers between devices, ring_send(): lax.ppermute(x, axis, [(order[i], order[(i + d) % n]) for i in range(n)])  15.7 us
    pallas_call x5, Pallas kernels, z_call(): pl.pallas_call(functools.partial(z_kernel, tuple(ks), before is None, las...  8.95 us
    pallas_call x2, Pallas kernels, weight_grad_last_call(): pl.pallas_call(functools.partial(weight_grad_last_kernel, rows // (own[0]...  4.77 us
    pallas_call x1, Pallas kernels, dz_call(): pl.pallas_call(functools.partial(dz_kernel, n_batch, n_col, tile, constan...  4.68 us
    pallas_call x2, Pallas kernels, d_act_call(): pl.pallas_call(functools.partial(d_act_kernel, count, (got is not None, n...  3.68 us
  transfers between devices with their start and end apart: 47, of which 25 were waited for; matrix products, arithmetic and copies ran while one was open for 1% of the time, Pallas kernels for 17%

profile of v12, /device:TPU:0, one launch (start us, length us, event | category | flops | bytes accessed | tf_op | source)
XLA Modules:
  0.0 135.2 jit_solution(2565994991844835595)
XLA Ops:
  2.8 5.1 %collective-permute-start.2 = (f32[4,512]{1,0:T(4,128)S(1)}, f32[4,512]{1,0:T(4,128)S(1)}, u32[]{:S(2)}, u32[]{:S(2)}) collective-permute-start(f32[4,512]{1,0:T(4,128)S(1)} %pad_maximum_fusion.2), channel_id=1, source_target_pairs={{0,24},{8,16},{16,8},{24,0},{1,25},{9,17},{17,9},{25,1},{2,26},{10... | collective-permute-start | bytes 24584 | tf_op jit(solution)/shard_map/norm_stats/ppermute | solution.py:24
  8.6 3.5 %weight_load.1 = (bf16[4096,1024]{1,0:T(8,128)(2,1)S(1)}, f32[4,512]{1,0:T(4,128)S(1)}) custom-call(bf16[4096,1024]{1,0:T(8,128)(2,1)} %w_ref), custom_call_target="tpu_custom_call" | custom-call | bytes 16777216 | tf_op jit(solution)/shard_map/weight_load/weight_load/pallas_call | solution.py:78
  12.9 1.5 %collective-permute-done.6.refs_1_.refs_0_ = bf16[256,512]{1,0:T(8,128)(2,1)S(1)} collective-permute-done((bf16[256,512]{1,0:T(8,128)(2,1)S(1)}, bf16[256,512]{1,0:T(8,128)(2,1)S(1)}, u32[]{:S(2)}, u32[]{:S(2)}) %collective-permute-start.6) | collective-permute-done | bytes 262176 | tf_op jit(solution)/shard_map/act_gather/ppermute | solution.py:24
  14.4 1.5 %collective-permute-start.7 = (bf16[256,512]{1,0:T(8,128)(2,1)S(1)}, bf16[256,512]{1,0:T(8,128)(2,1)S(1)}, u32[]{:S(2)}, u32[]{:S(2)}) collective-permute-start(bf16[256,512]{1,0:T(8,128)(2,1)S(1)} %bitcast.27), channel_id=1, source_target_pairs={{0,2},{1,3},{2,0},{3,1},{4,6},{5,7},{6,4},{7,5},{8,10},{9,11},{10,... | collective-permute-start | bytes 786440 | tf_op jit(solution)/shard_map/act_gather/ppermute | solution.py:24
  15.9 1.5 %collective-permute-start.9 = (bf16[256,512]{1,0:T(8,128)(2,1)S(1)}, bf16[256,512]{1,0:T(8,128)(2,1)S(1)}, u32[]{:S(2)}, u32[]{:S(2)}) collective-permute-start(bf16[256,512]{1,0:T(8,128)(2,1)S(1)} %bitcast.28), channel_id=1, source_target_pairs={{0,4},{1,5},{2,6},{3,7},{4,0},{5,1},{6,2},{7,3},{8,12},{9,13},{10,... | collective-permute-start | bytes 786440 | tf_op jit(solution)/shard_map/act_gather/ppermute | solution.py:24
  17.4 2.1 %collective-permute-start.3 = (bf16[128,512]{1,0:T(8,128)(2,1)S(1)}, bf16[128,512]{1,0:T(8,128)(2,1)S(1)}, u32[]{:S(2)}, u32[]{:S(2)}) collective-permute-start(bf16[128,512]{1,0:T(8,128)(2,1)S(1)} %slice_bitcast_fusion), channel_id=1, source_target_pairs={{0,16},{16,24},{24,8},{8,0},{1,17},{17,25},{25,9},{9,1},{2,18},{18... | collective-permute-start | bytes 393224 | tf_op jit(solution)/shard_map/act_gather/ppermute | solution.py:34
  19.5 1.4 %collective-permute-start.4 = (bf16[128,512]{1,0:T(8,128)(2,1)S(1)}, bf16[128,512]{1,0:T(8,128)(2,1)S(1)}, u32[]{:S(2)}, u32[]{:S(2)}) collective-permute-start(bf16[128,512]{1,0:T(8,128)(2,1)S(1)} %slice_bitcast_fusion), channel_id=1, source_target_pairs={{0,24},{16,8},{24,0},{8,16},{1,25},{17,9},{25,1},{9,17},{2,26},{18... | collective-permute-start | bytes 393224 | tf_op jit(solution)/shard_map/act_gather/ppermute | solution.py:34
  22.0 1.5 %collective-permute-done.3 = bf16[128,512]{1,0:T(8,128)(2,1)S(1)} collective-permute-done((bf16[128,512]{1,0:T(8,128)(2,1)S(1)}, bf16[128,512]{1,0:T(8,128)(2,1)S(1)}, u32[]{:S(2)}, u32[]{:S(2)}) %collective-permute-start.3) | collective-permute-done | bytes 131104 | tf_op jit(solution)/shard_map/act_gather/ppermute | solution.py:34
  23.4 4.4 %collective-permute-done.4 = bf16[128,512]{1,0:T(8,128)(2,1)S(1)} collective-permute-done((bf16[128,512]{1,0:T(8,128)(2,1)S(1)}, bf16[128,512]{1,0:T(8,128)(2,1)S(1)}, u32[]{:S(2)}, u32[]{:S(2)}) %collective-permute-start.4) | collective-permute-done | bytes 131104 | tf_op jit(solution)/shard_map/act_gather/ppermute | solution.py:34
  27.9 4.6 %collective-permute-done.5 = bf16[128,512]{1,0:T(8,128)(2,1)S(1)} collective-permute-done((bf16[128,512]{1,0:T(8,128)(2,1)S(1)}, bf16[128,512]{1,0:T(8,128)(2,1)S(1)}, u32[]{:S(2)}, u32[]{:S(2)}) %collective-permute-start.5) | collective-permute-done | bytes 131104 | tf_op jit(solution)/shard_map/act_gather/ppermute | solution.py:34
  33.8 4.7 %collective-permute-done.11 = bf16[128,512]{1,0:T(8,128)(2,1)S(1)} collective-permute-done((bf16[128,512]{1,0:T(8,128)(2,1)S(1)}, bf16[128,512]{1,0:T(8,128)(2,1)S(1)}, u32[]{:S(2)}, u32[]{:S(2)}) %collective-permute-start.11) | collective-permute-done | bytes 131104 | tf_op jit(solution)/shard_map/act_gather/ppermute | solution.py:24
  39.0 1.6 %collective-permute-start.16 = (bf16[384,512]{1,0:T(8,128)(2,1)S(1)}, bf16[384,512]{1,0:T(8,128)(2,1)S(1)}, u32[]{:S(2)}, u32[]{:S(2)}) collective-permute-start(bf16[384,512]{1,0:T(8,128)(2,1)S(1)} %constant_dynamic-update-slice_fusion.2.refs_0_.refs_4_), channel_id=1, source_target_pairs={{0,2},{1,3},{2,0},{3,1},{4,6},{5,7},{6,4},{7,5},{8,10},{9,11},{10,... | collective-permute-start | bytes 1179656 | tf_op jit(solution)/shard_map/act_gather/ppermute | solution.py:24
  41.0 1.2 z_matmul.5.refs_4_
  42.3 1.5 %z_matmul.6.refs_4_ = f32[256,1024]{1,0:T(8,128)S(1)} custom-call(s32[2]{0:T(128)S(1)} %pad_add_fusion.place_ref, bf16[256,512]{1,0:T(8,128)(2,1)S(1)} %collective-permute-done.7.refs_0_.refs_1_, bf16[256,512]{1,0:T(8,128)(2,1)S(1)} %collective-permute-done.9.refs_1_.refs_2_, bf16[256,512]{1,0:T(8,128)(2,1)S(1)} %constant_dynamic-update-slice_fusion.refs_2_.refs_3_, ...), custom_call_target="tpu_custom_call" | custom-call | flops 805306368 | bytes 524288 | tf_op jit(solution)/shard_map/z/z_matmul/pallas_call | solution.py:126
  43.8 1.5 %z_matmul.7 = (bf16[128,1024]{1,0:T(8,128)(2,1)S(1)}, bf16[128,1024]{1,0:T(8,128)(2,1)S(1)}) custom-call(s32[2]{0:T(128)S(1)} %pad_add_fusion.place_ref, bf16[256,512]{1,0:T(8,128)(2,1)S(1)} %collective-permute-done.8.refs_0_.refs_1_, bf16[256,512]{1,0:T(8,128)(2,1)S(1)} %collective-permute-done.10.refs_1_.refs_2_, ...), custom_call_target="tpu_custom_call" | custom-call | flops 805306368 | bytes 524288 | tf_op jit(solution)/shard_map/z/z_matmul/pallas_call | solution.py:126
  45.4 5.1 %collective-permute-done.16.refs_1_.refs_5_ = bf16[384,512]{1,0:T(8,128)(2,1)S(1)} collective-permute-done((bf16[384,512]{1,0:T(8,128)(2,1)S(1)}, bf16[384,512]{1,0:T(8,128)(2,1)S(1)}, u32[]{:S(2)}, u32[]{:S(2)}) %collective-permute-start.16) | collective-permute-done | bytes 393248 | tf_op jit(solution)/shard_map/act_gather/ppermute | solution.py:24
  53.6 1.2 collective-permute-start.22
  58.1 1.9 %z_matmul.8.refs_6_ = f32[384,1024]{1,0:T(8,128)S(1)} custom-call(s32[2]{0:T(128)S(1)} %pad_add_fusion.place_ref, bf16[384,512]{1,0:T(8,128)(2,1)S(1)} %constant_dynamic-update-slice_fusion.2.refs_0_.refs_4_, bf16[384,512]{1,0:T(8,128)(2,1)S(1)} %collective-permute-done.16.refs_1_.refs_5_, bf16[384,512]{1,0:T(8,128)(2,1)S(1)} %collective-permute-done.18.refs_2_.refs_6_, ...), custom_call_target="tpu_custom_call" | custom-call | flops 1207959552 | bytes 786432 | tf_op jit(solution)/shard_map/z_far/z_matmul/pallas_call | solution.py:126
  60.8 2.4 %collective-permute-start.24 = (bf16[128,1024]{1,0:T(8,128)(2,1)S(1)}, bf16[128,1024]{1,0:T(8,128)(2,1)S(1)}, u32[]{:S(2)}, u32[]{:S(2)}) collective-permute-start(bf16[128,1024]{1,0:T(8,128)(2,1)S(1)} %collective-permute-done.22.refs_5_.refs_13_), channel_id=1, source_target_pairs={{0,16},{16,24},{24,8},{8,0},{1,17},{17,25},{25,9},{9,1},{2,18},{18... | collective-permute-start | bytes 786440 | tf_op jit(solution)/shard_map/z_far/ppermute | solution.py:34
  63.3 2.7 %z_matmul.9 = (bf16[128,1024]{1,0:T(8,128)(2,1)S(1)}, bf16[128,1024]{1,0:T(8,128)(2,1)S(1)}, bf16[128,1024]{1,0:T(8,128)(2,1)S(1)}) custom-call(s32[2]{0:T(128)S(1)} %pad_add_fusion.place_ref, bf16[384,512]{1,0:T(8,128)(2,1)S(1)} %collective-permute-done.14.refs_0_.refs_4_, bf16[384,512]{1,0:T(8,128)(2,1)S(1)} %collective-permute-done.17.refs_1_.refs_5_, ...), custom_call_target="tpu_custom_call" | custom-call | flops 2013265920 | bytes 786432 | tf_op jit(solution)/shard_map/z_far/z_matmul/pallas_call | solution.py:126
  66.0 4.0 %collective-permute-done.24.refs_7_.refs_15_ = bf16[128,1024]{1,0:T(8,128)(2,1)S(1)} collective-permute-done((bf16[128,1024]{1,0:T(8,128)(2,1)S(1)}, bf16[128,1024]{1,0:T(8,128)(2,1)S(1)}, u32[]{:S(2)}, u32[]{:S(2)}) %collective-permute-start.24) | collective-permute-done | bytes 262176 | tf_op jit(solution)/shard_map/z_far/ppermute | solution.py:34
  70.1 2.6 %kernel_strip.1 = (f32[4,32,1280]{2,1,0:T(8,128)S(1)}, bf16[4,32,1280]{2,1,0:T(8,128)(2,1)S(1)}) custom-call(s32[2]{0:T(128)S(1)} %pad_add_fusion.place_ref, bf16[128,1024]{1,0:T(8,128)(2,1)S(1)} %get-tuple-element.75.refs_0_.refs_8_, bf16[128,1024]{1,0:T(8,128)(2,1)S(1)} %get-tuple-element.76.refs_1_.refs_9_, ...), custom_call_target="tpu_custom_call" | custom-call | flops 671088640 | bytes 2097152 | tf_op jit(solution)/shard_map/kernel/kernel_strip/pallas_call | solution.py:173
  72.8 1.6 %collective-permute-done.25 = bf16[4,32,1280]{2,1,0:T(8,128)(2,1)S(1)} collective-permute-done((bf16[4,32,1280]{2,1,0:T(8,128)(2,1)S(1)}, bf16[4,32,1280]{2,1,0:T(8,128)(2,1)S(1)}, u32[]{:S(2)}, u32[]{:S(2)}) %collective-permute-start.25) | collective-permute-done | bytes 327712 | tf_op jit(solution)/shard_map/kernel/ppermute | solution.py:24
  74.6 1.6 %collective-permute-start.28 = (bf16[32,1280]{1,0:T(8,128)(2,1)S(1)}, bf16[32,1280]{1,0:T(8,128)(2,1)S(1)}, u32[]{:S(2)}, u32[]{:S(2)}) collective-permute-start(bf16[32,1280]{1,0:T(8,128)(2,1)S(1)} %get-tuple-element.133), channel_id=1, source_target_pairs={{0,6},{1,7},{2,4},{3,5},{4,2},{5,3},{6,0},{7,1},{8,14},{9,15},{10,... | collective-permute-start | bytes 245768 | tf_op jit(solution)/shard_map/kernel/ppermute | solution.py:24
  76.6 1.5 %collective-permute-start.26 = (bf16[32,1280]{1,0:T(8,128)(2,1)S(1)}, bf16[32,1280]{1,0:T(8,128)(2,1)S(1)}, u32[]{:S(2)}, u32[]{:S(2)}) collective-permute-start(bf16[32,1280]{1,0:T(8,128)(2,1)S(1)} %get-tuple-element.132), channel_id=1, source_target_pairs={{0,2},{1,3},{2,0},{3,1},{4,6},{5,7},{6,4},{7,5},{8,10},{9,11},{10,... | collective-permute-start | bytes 245768 | tf_op jit(solution)/shard_map/kernel/ppermute | solution.py:24
  78.1 2.2 %collective-permute-done.28 = bf16[32,1280]{1,0:T(8,128)(2,1)S(1)} collective-permute-done((bf16[32,1280]{1,0:T(8,128)(2,1)S(1)}, bf16[32,1280]{1,0:T(8,128)(2,1)S(1)}, u32[]{:S(2)}, u32[]{:S(2)}) %collective-permute-start.28) | collective-permute-done | bytes 81952 | tf_op jit(solution)/shard_map/kernel/ppermute | solution.py:24
  80.3 1.4 %collective-permute-done.27 = bf16[32,1280]{1,0:T(8,128)(2,1)S(1)} collective-permute-done((bf16[32,1280]{1,0:T(8,128)(2,1)S(1)}, bf16[32,1280]{1,0:T(8,128)(2,1)S(1)}, u32[]{:S(2)}, u32[]{:S(2)}) %collective-permute-start.27) | collective-permute-done | bytes 81952 | tf_op jit(solution)/shard_map/kernel/ppermute | solution.py:24
  82.7 1.5 %collective-permute-start.32 = (bf16[32,1280]{1,0:T(8,128)(2,1)S(1)}, bf16[32,1280]{1,0:T(8,128)(2,1)S(1)}, u32[]{:S(2)}, u32[]{:S(2)}) collective-permute-start(bf16[32,1280]{1,0:T(8,128)(2,1)S(1)} %get-tuple-element.96.refs_0_), channel_id=1, source_target_pairs={{0,4},{1,5},{2,6},{3,7},{4,0},{5,1},{6,2},{7,3},{8,12},{9,13},{10,... | collective-permute-start | bytes 245768 | tf_op jit(solution)/shard_map/kernel/ppermute | solution.py:24
  84.2 1.3 collective-permute-start.34
  85.5 2.8 %collective-permute-start.36 = (bf16[128,512]{1,0:T(8,128)(2,1)S(1)}, bf16[128,512]{1,0:T(8,128)(2,1)S(1)}, u32[]{:S(2)}, u32[]{:S(2)}) collective-permute-start(bf16[128,512]{1,0:T(8,128)(2,1)S(1)} %get-tuple-element.95), channel_id=1, source_target_pairs={{0,16},{16,24},{24,8},{8,0},{1,17},{17,25},{25,9},{9,1},{2,18},{18... | collective-permute-start | bytes 393224 | tf_op jit(solution)/shard_map/kernel/ppermute | solution.py:34
  89.5 1.5 %collective-permute-done.36 = bf16[128,512]{1,0:T(8,128)(2,1)S(1)} collective-permute-done((bf16[128,512]{1,0:T(8,128)(2,1)S(1)}, bf16[128,512]{1,0:T(8,128)(2,1)S(1)}, u32[]{:S(2)}, u32[]{:S(2)}) %collective-permute-start.36) | collective-permute-done | bytes 131104 | tf_op jit(solution)/shard_map/kernel/ppermute | solution.py:34
  91.0 1.9 %collective-permute-start.37 = (bf16[128,512]{1,0:T(8,128)(2,1)S(1)}, bf16[128,512]{1,0:T(8,128)(2,1)S(1)}, u32[]{:S(2)}, u32[]{:S(2)}) collective-permute-start(bf16[128,512]{1,0:T(8,128)(2,1)S(1)} %get-tuple-element.105), channel_id=1, source_target_pairs={{0,24},{16,8},{24,0},{8,16},{1,25},{17,9},{25,1},{9,17},{2,26},{18... | collective-permute-start | bytes 393224 | tf_op jit(solution)/shard_map/dz/ppermute | solution.py:34
  93.0 4.7 %embedding_gradient.1 = (bf16[2,512,1024]{2,1,0:T(8,128)(2,1)S(1)}, f32[8,128]{1,0:T(8,128)S(1)}) custom-call(s32[2]{0:T(128)S(1)} %pad_add_fusion.place_ref, f32[32,1280]{1,0:T(8,128)S(1)} %get-tuple-element.129.own_ref, bf16[32,1280]{1,0:T(8,128)(2,1)S(1)} %get-tuple-element.96.refs_0_, bf16[32,1280]{1,0:T(8,128)(2,1)S(1)} %collective-permute-done.29.refs_1_, ...), custom_call_target="tpu_custom_call" | custom-call | flops 1073741824 | bytes 4194304 | tf_op jit(solution)/shard_map/dz/embedding_gradient/pallas_call | solution.py:251
  97.9 1.8 %d_act_matmul.2 = bf16[4,272,512]{2,1,0:T(8,128)(2,1)S(1)} custom-call(s32[2]{0:T(128)S(1)} %pad_add_fusion.place_ref, bf16[2,512,1024]{2,1,0:T(8,128)(2,1)S(1)} %get-tuple-element.106.dz_ref.refs_8_.refs_5_, f32[8,128]{1,0:T(8,128)S(1)} %get-tuple-element.107.share_ref, bf16[4096,1024]{1,0:T(8,128)(2,1)S(1)} %get-tuple-element.73.refs_2_.refs_3_.refs_5_.w_ref), custom_call_target="tpu_custom_call" | custom-call | flops 1073741824 | bytes 1048576 | tf_op jit(solution)/shard_map/d_act/d_act_matmul/pallas_call | solution.py:323
  99.8 2.7 %collective-permute-done.38.refs_0_ = bf16[4,272,512]{2,1,0:T(8,128)(2,1)S(1)} collective-permute-done((bf16[4,272,512]{2,1,0:T(8,128)(2,1)S(1)}, bf16[4,272,512]{2,1,0:T(8,128)(2,1)S(1)}, u32[]{:S(2)}, u32[]{:S(2)}) %collective-permute-start.38) | collective-permute-done | bytes 1114144 | tf_op jit(solution)/shard_map/d_act/ppermute | solution.py:24
  102.6 1.8 %d_act_matmul.3 = (bf16[272,512]{1,0:T(8,128)(2,1)S(1)}, bf16[272,512]{1,0:T(8,128)(2,1)S(1)}, bf16[272,512]{1,0:T(8,128)(2,1)S(1)}, f32[272,512]{1,0:T(8,128)S(1)}) custom-call(s32[2]{0:T(128)S(1)} %pad_add_fusion.place_ref, bf16[2,512,1024]{2,1,0:T(8,128)(2,1)S(1)} %get-tuple-element.106.dz_ref.refs_8_.refs_5_, f32[8,128]{1,0:T(8,128)S(1)} %get-tuple-element.107.share_ref, ...), custom_call_target="tpu_custom_call" | custom-call | flops 1073741824 | bytes 1048576 | tf_op jit(solution)/shard_map/d_act/d_act_matmul/pallas_call | solution.py:323
  104.4 2.8 %collective-permute-start.42 = (bf16[128,512]{1,0:T(8,128)(2,1)S(1)}, bf16[128,512]{1,0:T(8,128)(2,1)S(1)}, u32[]{:S(2)}, u32[]{:S(2)}) collective-permute-start(bf16[128,512]{1,0:T(8,128)(2,1)S(1)} %get-tuple-element.116), channel_id=1, source_target_pairs={{0,8},{16,0},{24,16},{8,24},{1,9},{17,1},{25,17},{9,25},{2,10},{18... | collective-permute-start | bytes 393224 | tf_op jit(solution)/shard_map/grad_weight/ppermute | solution.py:34
  107.2 1.3 weight_gradient_0.2.refs_6_
  109.1 1.3 collective-permute-start.40
  110.4 1.7 %collective-permute-start.41 = (bf16[272,512]{1,0:T(8,128)(2,1)S(1)}, bf16[272,512]{1,0:T(8,128)(2,1)S(1)}, u32[]{:S(2)}, u32[]{:S(2)}) collective-permute-start(bf16[272,512]{1,0:T(8,128)(2,1)S(1)} %get-tuple-element.113), channel_id=1, source_target_pairs={{0,6},{1,7},{2,4},{3,5},{4,2},{5,3},{6,0},{7,1},{8,14},{9,15},{10,... | collective-permute-start | bytes 835592 | tf_op jit(solution)/shard_map/d_act/ppermute | solution.py:24
  112.2 2.4 %weight_gradient_1.2.refs_7_ = f32[1024,1024]{1,0:T(8,128)} custom-call(s32[2]{0:T(128)S(1)} %pad_add_fusion.place_ref, bf16[256,512]{1,0:T(8,128)(2,1)S(1)} %bitcast.32, bf16[256,512]{1,0:T(8,128)(2,1)S(1)} %collective-permute-done.7.refs_0_.refs_1_, bf16[256,512]{1,0:T(8,128)(2,1)S(1)} %collective-permute-done.9.refs_1_.refs_2_, ...), custom_call_target="tpu_custom_call" | custom-call | flops 536870912 | bytes 2097152 | tf_op jit(solution)/shard_map/grad_weight/weight_gradient_1/pallas_call | solution.py:464
  114.6 3.5 %collective-permute-done.39 = bf16[272,512]{1,0:T(8,128)(2,1)S(1)} collective-permute-done((bf16[272,512]{1,0:T(8,128)(2,1)S(1)}, bf16[272,512]{1,0:T(8,128)(2,1)S(1)}, u32[]{:S(2)}, u32[]{:S(2)}) %collective-permute-start.39) | collective-permute-done | bytes 278560 | tf_op jit(solution)/shard_map/d_act/ppermute | solution.py:24
  118.1 5.1 %collective-permute-done.40 = bf16[272,512]{1,0:T(8,128)(2,1)S(1)} collective-permute-done((bf16[272,512]{1,0:T(8,128)(2,1)S(1)}, bf16[272,512]{1,0:T(8,128)(2,1)S(1)}, u32[]{:S(2)}, u32[]{:S(2)}) %collective-permute-start.40) | collective-permute-done | bytes 278560 | tf_op jit(solution)/shard_map/d_act/ppermute | solution.py:24
  124.3 2.0 %collective-permute-start.44 = (f32[8,512]{1,0:T(8,128)S(1)}, f32[8,512]{1,0:T(8,128)S(1)}, u32[]{:S(2)}, u32[]{:S(2)}) collective-permute-start(f32[8,512]{1,0:T(8,128)S(1)} %pad_maximum_fusion.1.refs_0_), channel_id=1, source_target_pairs={{0,16},{8,24},{16,0},{24,8},{1,17},{9,25},{17,1},{25,9},{2,18},{10... | collective-permute-start | bytes 49160 | tf_op jit(solution)/shard_map/norm_backward/ppermute | solution.py:24
  126.2 2.1 %collective-permute-start.45 = (f32[8,512]{1,0:T(8,128)S(1)}, f32[8,512]{1,0:T(8,128)S(1)}, u32[]{:S(2)}, u32[]{:S(2)}) collective-permute-start(f32[8,512]{1,0:T(8,128)S(1)} %pad_maximum_fusion.1.refs_0_), channel_id=1, source_target_pairs={{0,24},{8,16},{16,8},{24,0},{1,25},{9,17},{17,9},{25,1},{2,26},{10... | collective-permute-start | bytes 49160 | tf_op jit(solution)/shard_map/norm_backward/ppermute | solution.py:24
  128.3 1.3 weight_gradient_0.3.refs_6_
  129.7 2.0 %collective-permute-done.45.refs_3_ = f32[8,512]{1,0:T(8,128)S(1)} collective-permute-done((f32[8,512]{1,0:T(8,128)S(1)}, f32[8,512]{1,0:T(8,128)S(1)}, u32[]{:S(2)}, u32[]{:S(2)}) %collective-permute-start.45) | collective-permute-done | bytes 16416 | tf_op jit(solution)/shard_map/norm_backward/ppermute | solution.py:24
  132.6 2.4 %weight_gradient_1.3 = f32[1024,1024]{1,0:T(8,128)} custom-call(s32[2]{0:T(128)S(1)} %pad_add_fusion.place_ref, bf16[256,512]{1,0:T(8,128)(2,1)S(1)} %collective-permute-done.6.refs_1_.refs_0_, bf16[256,512]{1,0:T(8,128)(2,1)S(1)} %collective-permute-done.8.refs_0_.refs_1_, ...), custom_call_target="tpu_custom_call", output_to_operand_aliasing={{}: (8, {})} | custom-call | flops 536870912 | bytes 2097152 | tf_op jit(solution)/shard_map/grad_weight/weight_gradient_1/pallas_call | solution.py:464
  (98 shorter events, 19.9 us)
Async XLA Ops:
  2.8 9.7 %copy-start = (f32[512]{0:T(512)S(1)}, f32[512]{0:T(512)}, u32[]{:S(2)}) copy-start(f32[512]{0:T(512)} %param.5) | copy-start | bytes 6148
  2.8 9.2 %collective-permute-start.2 = (f32[4,512]{1,0:T(4,128)S(1)}, f32[4,512]{1,0:T(4,128)S(1)}, u32[]{:S(2)}, u32[]{:S(2)}) collective-permute-start(f32[4,512]{1,0:T(4,128)S(1)} %pad_maximum_fusion.2), channel_id=1, source_target_pairs={{0,24},{8,16},{16,8},{24,0},{1,25},{9,17},{17,9},{25,1},{2,26},{10... | collective-permute-start | bytes 24584 | tf_op jit(solution)/shard_map/norm_stats/ppermute | solution.py:24
  7.9 4.5 %collective-permute-start.1 = (f32[4,512]{1,0:T(4,128)S(1)}, f32[4,512]{1,0:T(4,128)S(1)}, u32[]{:S(2)}, u32[]{:S(2)}) collective-permute-start(f32[4,512]{1,0:T(4,128)S(1)} %pad_maximum_fusion.2), channel_id=1, source_target_pairs={{0,16},{8,24},{16,0},{24,8},{1,17},{9,25},{17,1},{25,9},{2,18},{10... | collective-permute-start | bytes 24584 | tf_op jit(solution)/shard_map/norm_stats/ppermute | solution.py:24
  7.9 4.5 %collective-permute-start = (f32[4,512]{1,0:T(4,128)S(1)}, f32[4,512]{1,0:T(4,128)S(1)}, u32[]{:S(2)}, u32[]{:S(2)}) collective-permute-start(f32[4,512]{1,0:T(4,128)S(1)} %pad_maximum_fusion.2), channel_id=1, source_target_pairs={{0,8},{8,0},{16,24},{24,16},{1,9},{9,1},{17,25},{25,17},{2,10},{10... | collective-permute-start | bytes 24584 | tf_op jit(solution)/shard_map/norm_stats/ppermute | solution.py:24
  12.8 1.6 %collective-permute-start.6 = (bf16[256,512]{1,0:T(8,128)(2,1)S(1)}, bf16[256,512]{1,0:T(8,128)(2,1)S(1)}, u32[]{:S(2)}, u32[]{:S(2)}) collective-permute-start(bf16[256,512]{1,0:T(8,128)(2,1)S(1)} %bitcast.26), channel_id=1, source_target_pairs={{0,1},{1,0},{2,3},{3,2},{4,5},{5,4},{6,7},{7,6},{8,9},{9,8},{10,11... | collective-permute-start | bytes 786440 | tf_op jit(solution)/shard_map/act_gather/ppermute | solution.py:24
  14.4 18.1 %collective-permute-start.7 = (bf16[256,512]{1,0:T(8,128)(2,1)S(1)}, bf16[256,512]{1,0:T(8,128)(2,1)S(1)}, u32[]{:S(2)}, u32[]{:S(2)}) collective-permute-start(bf16[256,512]{1,0:T(8,128)(2,1)S(1)} %bitcast.27), channel_id=1, source_target_pairs={{0,2},{1,3},{2,0},{3,1},{4,6},{5,7},{6,4},{7,5},{8,10},{9,11},{10,... | collective-permute-start | bytes 786440 | tf_op jit(solution)/shard_map/act_gather/ppermute | solution.py:24
  15.9 16.6 %collective-permute-start.9 = (bf16[256,512]{1,0:T(8,128)(2,1)S(1)}, bf16[256,512]{1,0:T(8,128)(2,1)S(1)}, u32[]{:S(2)}, u32[]{:S(2)}) collective-permute-start(bf16[256,512]{1,0:T(8,128)(2,1)S(1)} %bitcast.28), channel_id=1, source_target_pairs={{0,4},{1,5},{2,6},{3,7},{4,0},{5,1},{6,2},{7,3},{8,12},{9,13},{10,... | collective-permute-start | bytes 786440 | tf_op jit(solution)/shard_map/act_gather/ppermute | solution.py:24
  17.4 6.0 %collective-permute-start.3 = (bf16[128,512]{1,0:T(8,128)(2,1)S(1)}, bf16[128,512]{1,0:T(8,128)(2,1)S(1)}, u32[]{:S(2)}, u32[]{:S(2)}) collective-permute-start(bf16[128,512]{1,0:T(8,128)(2,1)S(1)} %slice_bitcast_fusion), channel_id=1, source_target_pairs={{0,16},{16,24},{24,8},{8,0},{1,17},{17,25},{25,9},{9,1},{2,18},{18... | collective-permute-start | bytes 393224 | tf_op jit(solution)/shard_map/act_gather/ppermute | solution.py:34
  19.5 8.4 %collective-permute-start.4 = (bf16[128,512]{1,0:T(8,128)(2,1)S(1)}, bf16[128,512]{1,0:T(8,128)(2,1)S(1)}, u32[]{:S(2)}, u32[]{:S(2)}) collective-permute-start(bf16[128,512]{1,0:T(8,128)(2,1)S(1)} %slice_bitcast_fusion), channel_id=1, source_target_pairs={{0,24},{16,8},{24,0},{8,16},{1,25},{17,9},{25,1},{9,17},{2,26},{18... | collective-permute-start | bytes 393224 | tf_op jit(solution)/shard_map/act_gather/ppermute | solution.py:34
  20.9 11.6 %collective-permute-start.5 = (bf16[128,512]{1,0:T(8,128)(2,1)S(1)}, bf16[128,512]{1,0:T(8,128)(2,1)S(1)}, u32[]{:S(2)}, u32[]{:S(2)}) collective-permute-start(bf16[128,512]{1,0:T(8,128)(2,1)S(1)} %slice_bitcast_fusion), channel_id=1, source_target_pairs={{0,8},{16,0},{24,16},{8,24},{1,9},{17,1},{25,17},{9,25},{2,10},{18... | collective-permute-start | bytes 393224 | tf_op jit(solution)/shard_map/act_gather/ppermute | solution.py:34
  32.5 11.3 %collective-permute-start.8 = (bf16[256,512]{1,0:T(8,128)(2,1)S(1)}, bf16[256,512]{1,0:T(8,128)(2,1)S(1)}, u32[]{:S(2)}, u32[]{:S(2)}) collective-permute-start(bf16[256,512]{1,0:T(8,128)(2,1)S(1)} %collective-permute-done.7.refs_0_.refs_1_), channel_id=1, source_target_pairs={{0,1},{1,0},{2,3},{3,2},{4,5},{5,4},{6,7},{7,6},{8,9},{9,8},{10,11... | collective-permute-start | bytes 786440 | tf_op jit(solution)/shard_map/act_gather/ppermute | solution.py:24
  32.6 6.0 %collective-permute-start.11 = (bf16[128,512]{1,0:T(8,128)(2,1)S(1)}, bf16[128,512]{1,0:T(8,128)(2,1)S(1)}, u32[]{:S(2)}, u32[]{:S(2)}) collective-permute-start(bf16[128,512]{1,0:T(8,128)(2,1)S(1)} %slice.159), channel_id=1, source_target_pairs={{0,2},{1,3},{2,0},{3,1},{4,6},{5,7},{6,4},{7,5},{8,10},{9,11},{10,... | collective-permute-start | bytes 393224 | tf_op jit(solution)/shard_map/act_gather/ppermute | solution.py:24
  33.2 5.7 %collective-permute-start.12 = (bf16[128,512]{1,0:T(8,128)(2,1)S(1)}, bf16[128,512]{1,0:T(8,128)(2,1)S(1)}, u32[]{:S(2)}, u32[]{:S(2)}) collective-permute-start(bf16[128,512]{1,0:T(8,128)(2,1)S(1)} %slice.160), channel_id=1, source_target_pairs={{0,4},{1,5},{2,6},{3,7},{4,0},{5,1},{6,2},{7,3},{8,12},{9,13},{10,... | collective-permute-start | bytes 393224 | tf_op jit(solution)/shard_map/act_gather/ppermute | solution.py:24
  33.8 10.0 %collective-permute-start.10 = (bf16[256,512]{1,0:T(8,128)(2,1)S(1)}, bf16[256,512]{1,0:T(8,128)(2,1)S(1)}, u32[]{:S(2)}, u32[]{:S(2)}) collective-permute-start(bf16[256,512]{1,0:T(8,128)(2,1)S(1)} %collective-permute-done.9.refs_1_.refs_2_), channel_id=1, source_target_pairs={{0,1},{1,0},{2,3},{3,2},{4,5},{5,4},{6,7},{7,6},{8,9},{9,8},{10,11... | collective-permute-start | bytes 786440 | tf_op jit(solution)/shard_map/act_gather/ppermute | solution.py:24
  38.9 5.0 %collective-permute-start.13 = (bf16[256,512]{1,0:T(8,128)(2,1)S(1)}, bf16[256,512]{1,0:T(8,128)(2,1)S(1)}, u32[]{:S(2)}, u32[]{:S(2)}) collective-permute-start(bf16[256,512]{1,0:T(8,128)(2,1)S(1)} %constant_dynamic-update-slice_fusion.refs_2_.refs_3_), channel_id=1, source_target_pairs={{0,1},{1,0},{2,3},{3,2},{4,5},{5,4},{6,7},{7,6},{8,9},{9,8},{10,11... | collective-permute-start | bytes 786440 | tf_op jit(solution)/shard_map/act_gather/ppermute | solution.py:24
  39.0 11.6 %collective-permute-start.16 = (bf16[384,512]{1,0:T(8,128)(2,1)S(1)}, bf16[384,512]{1,0:T(8,128)(2,1)S(1)}, u32[]{:S(2)}, u32[]{:S(2)}) collective-permute-start(bf16[384,512]{1,0:T(8,128)(2,1)S(1)} %constant_dynamic-update-slice_fusion.2.refs_0_.refs_4_), channel_id=1, source_target_pairs={{0,2},{1,3},{2,0},{3,1},{4,6},{5,7},{6,4},{7,5},{8,10},{9,11},{10,... | collective-permute-start | bytes 1179656 | tf_op jit(solution)/shard_map/act_gather/ppermute | solution.py:24
  40.5 11.2 %collective-permute-start.18 = (bf16[384,512]{1,0:T(8,128)(2,1)S(1)}, bf16[384,512]{1,0:T(8,128)(2,1)S(1)}, u32[]{:S(2)}, u32[]{:S(2)}) collective-permute-start(bf16[384,512]{1,0:T(8,128)(2,1)S(1)} %constant_dynamic-update-slice_fusion.2.refs_0_.refs_4_), channel_id=1, source_target_pairs={{0,4},{1,5},{2,6},{3,7},{4,0},{5,1},{6,2},{7,3},{8,12},{9,13},{10,... | collective-permute-start | bytes 1179656 | tf_op jit(solution)/shard_map/act_gather/ppermute | solution.py:24
  45.4 8.2 %collective-permute-start.15 = (bf16[128,1024]{1,0:T(8,128)(2,1)S(1)}, bf16[128,1024]{1,0:T(8,128)(2,1)S(1)}, u32[]{:S(2)}, u32[]{:S(2)}) collective-permute-start(bf16[128,1024]{1,0:T(8,128)(2,1)S(1)} %get-tuple-element.76.refs_1_.refs_9_), channel_id=1, source_target_pairs={{0,16},{16,24},{24,8},{8,0},{1,17},{17,25},{25,9},{9,1},{2,18},{18... | collective-permute-start | bytes 786440 | tf_op jit(solution)/shard_map/z_ring/ppermute | solution.py:34
  50.6 6.6 %collective-permute-start.21 = (bf16[192,512]{1,0:T(8,128)(2,1)S(1)}, bf16[192,512]{1,0:T(8,128)(2,1)S(1)}, u32[]{:S(2)}, u32[]{:S(2)}) collective-permute-start(bf16[192,512]{1,0:T(8,128)(2,1)S(1)} %slice.162), channel_id=1, source_target_pairs={{0,4},{1,5},{2,6},{3,7},{4,0},{5,1},{6,2},{7,3},{8,12},{9,13},{10,... | collective-permute-start | bytes 589832 | tf_op jit(solution)/shard_map/act_gather/ppermute | solution.py:24
  51.8 6.3 %collective-permute-start.20 = (bf16[192,512]{1,0:T(8,128)(2,1)S(1)}, bf16[192,512]{1,0:T(8,128)(2,1)S(1)}, u32[]{:S(2)}, u32[]{:S(2)}) collective-permute-start(bf16[192,512]{1,0:T(8,128)(2,1)S(1)} %slice.161), channel_id=1, source_target_pairs={{0,2},{1,3},{2,0},{3,1},{4,6},{5,7},{6,4},{7,5},{8,10},{9,11},{10,... | collective-permute-start | bytes 589832 | tf_op jit(solution)/shard_map/act_gather/ppermute | solution.py:24
  53.6 7.3 %collective-permute-start.22 = (bf16[128,1024]{1,0:T(8,128)(2,1)S(1)}, bf16[128,1024]{1,0:T(8,128)(2,1)S(1)}, u32[]{:S(2)}, u32[]{:S(2)}) collective-permute-start(bf16[128,1024]{1,0:T(8,128)(2,1)S(1)} %collective-permute-done.15.refs_3_.refs_11_), channel_id=1, source_target_pairs={{0,16},{16,24},{24,8},{8,0},{1,17},{17,25},{25,9},{9,1},{2,18},{18... | collective-permute-start | bytes 786440 | tf_op jit(solution)/shard_map/z_ring/ppermute | solution.py:34
  54.7 8.5 %collective-permute-start.14 = (bf16[384,512]{1,0:T(8,128)(2,1)S(1)}, bf16[384,512]{1,0:T(8,128)(2,1)S(1)}, u32[]{:S(2)}, u32[]{:S(2)}) collective-permute-start(bf16[384,512]{1,0:T(8,128)(2,1)S(1)} %constant_dynamic-update-slice_fusion.2.refs_0_.refs_4_), channel_id=1, source_target_pairs={{0,1},{1,0},{2,3},{3,2},{4,5},{5,4},{6,7},{7,6},{8,9},{9,8},{10,11... | collective-permute-start | bytes 1179656 | tf_op jit(solution)/shard_map/z_far/ppermute | solution.py:24
  55.4 7.9 %collective-permute-start.19 = (bf16[384,512]{1,0:T(8,128)(2,1)S(1)}, bf16[384,512]{1,0:T(8,128)(2,1)S(1)}, u32[]{:S(2)}, u32[]{:S(2)}) collective-permute-start(bf16[384,512]{1,0:T(8,128)(2,1)S(1)} %collective-permute-done.18.refs_2_.refs_6_), channel_id=1, source_target_pairs={{0,1},{1,0},{2,3},{3,2},{4,5},{5,4},{6,7},{7,6},{8,9},{9,8},{10,11... | collective-permute-start | bytes 1179656 | tf_op jit(solution)/shard_map/z_far/ppermute | solution.py:24
  58.1 5.2 %collective-permute-start.17 = (bf16[384,512]{1,0:T(8,128)(2,1)S(1)}, bf16[384,512]{1,0:T(8,128)(2,1)S(1)}, u32[]{:S(2)}, u32[]{:S(2)}) collective-permute-start(bf16[384,512]{1,0:T(8,128)(2,1)S(1)} %collective-permute-done.16.refs_1_.refs_5_), channel_id=1, source_target_pairs={{0,1},{1,0},{2,3},{3,2},{4,5},{5,4},{6,7},{7,6},{8,9},{9,8},{10,11... | collective-permute-start | bytes 1179656 | tf_op jit(solution)/shard_map/z_far/ppermute | solution.py:24
  60.8 2.4 %collective-permute-start.23 = (bf16[384,512]{1,0:T(8,128)(2,1)S(1)}, bf16[384,512]{1,0:T(8,128)(2,1)S(1)}, u32[]{:S(2)}, u32[]{:S(2)}) collective-permute-start(bf16[384,512]{1,0:T(8,128)(2,1)S(1)} %pad_maximum_fusion.refs_3_.refs_7_), channel_id=1, source_target_pairs={{0,1},{1,0},{2,3},{3,2},{4,5},{5,4},{6,7},{7,6},{8,9},{9,8},{10,11... | collective-permute-start | bytes 1179656 | tf_op jit(solution)/shard_map/z_far/ppermute | solution.py:24
  60.8 9.2 %collective-permute-start.24 = (bf16[128,1024]{1,0:T(8,128)(2,1)S(1)}, bf16[128,1024]{1,0:T(8,128)(2,1)S(1)}, u32[]{:S(2)}, u32[]{:S(2)}) collective-permute-start(bf16[128,1024]{1,0:T(8,128)(2,1)S(1)} %collective-permute-done.22.refs_5_.refs_13_), channel_id=1, source_target_pairs={{0,16},{16,24},{24,8},{8,0},{1,17},{17,25},{25,9},{9,1},{2,18},{18... | collective-permute-start | bytes 786440 | tf_op jit(solution)/shard_map/z_far/ppermute | solution.py:34
  72.7 1.7 %collective-permute-start.25 = (bf16[4,32,1280]{2,1,0:T(8,128)(2,1)S(1)}, bf16[4,32,1280]{2,1,0:T(8,128)(2,1)S(1)}, u32[]{:S(2)}, u32[]{:S(2)}) collective-permute-start(bf16[4,32,1280]{2,1,0:T(8,128)(2,1)S(1)} %get-tuple-element.92), channel_id=1, source_target_pairs={{0,1},{1,0},{2,3},{3,2},{4,5},{5,4},{6,7},{7,6},{8,9},{9,8},{10,11... | collective-permute-start | bytes 983048 | tf_op jit(solution)/shard_map/kernel/ppermute | solution.py:24
  74.6 5.8 %collective-permute-start.28 = (bf16[32,1280]{1,0:T(8,128)(2,1)S(1)}, bf16[32,1280]{1,0:T(8,128)(2,1)S(1)}, u32[]{:S(2)}, u32[]{:S(2)}) collective-permute-start(bf16[32,1280]{1,0:T(8,128)(2,1)S(1)} %get-tuple-element.133), channel_id=1, source_target_pairs={{0,6},{1,7},{2,4},{3,5},{4,2},{5,3},{6,0},{7,1},{8,14},{9,15},{10,... | collective-permute-start | bytes 245768 | tf_op jit(solution)/shard_map/kernel/ppermute | solution.py:24
  76.1 5.6 %collective-permute-start.27 = (bf16[32,1280]{1,0:T(8,128)(2,1)S(1)}, bf16[32,1280]{1,0:T(8,128)(2,1)S(1)}, u32[]{:S(2)}, u32[]{:S(2)}) collective-permute-start(bf16[32,1280]{1,0:T(8,128)(2,1)S(1)} %get-tuple-element.134), channel_id=1, source_target_pairs={{0,4},{1,5},{2,6},{3,7},{4,0},{5,1},{6,2},{7,3},{8,12},{9,13},{10,... | collective-permute-start | bytes 245768 | tf_op jit(solution)/shard_map/kernel/ppermute | solution.py:24
  76.6 5.2 %collective-permute-start.26 = (bf16[32,1280]{1,0:T(8,128)(2,1)S(1)}, bf16[32,1280]{1,0:T(8,128)(2,1)S(1)}, u32[]{:S(2)}, u32[]{:S(2)}) collective-permute-start(bf16[32,1280]{1,0:T(8,128)(2,1)S(1)} %get-tuple-element.132), channel_id=1, source_target_pairs={{0,2},{1,3},{2,0},{3,1},{4,6},{5,7},{6,4},{7,5},{8,10},{9,11},{10,... | collective-permute-start | bytes 245768 | tf_op jit(solution)/shard_map/kernel/ppermute | solution.py:24
  81.9 6.4 %collective-permute-start.30 = (bf16[32,1280]{1,0:T(8,128)(2,1)S(1)}, bf16[32,1280]{1,0:T(8,128)(2,1)S(1)}, u32[]{:S(2)}, u32[]{:S(2)}) collective-permute-start(bf16[32,1280]{1,0:T(8,128)(2,1)S(1)} %get-tuple-element.96.refs_0_), channel_id=1, source_target_pairs={{0,2},{1,3},{2,0},{3,1},{4,6},{5,7},{6,4},{7,5},{8,10},{9,11},{10,... | collective-permute-start | bytes 245768 | tf_op jit(solution)/shard_map/kernel/ppermute | solution.py:24
  82.7 6.1 %collective-permute-start.32 = (bf16[32,1280]{1,0:T(8,128)(2,1)S(1)}, bf16[32,1280]{1,0:T(8,128)(2,1)S(1)}, u32[]{:S(2)}, u32[]{:S(2)}) collective-permute-start(bf16[32,1280]{1,0:T(8,128)(2,1)S(1)} %get-tuple-element.96.refs_0_), channel_id=1, source_target_pairs={{0,4},{1,5},{2,6},{3,7},{4,0},{5,1},{6,2},{7,3},{8,12},{9,13},{10,... | collective-permute-start | bytes 245768 | tf_op jit(solution)/shard_map/kernel/ppermute | solution.py:24
  84.2 5.3 %collective-permute-start.34 = (bf16[32,1280]{1,0:T(8,128)(2,1)S(1)}, bf16[32,1280]{1,0:T(8,128)(2,1)S(1)}, u32[]{:S(2)}, u32[]{:S(2)}) collective-permute-start(bf16[32,1280]{1,0:T(8,128)(2,1)S(1)} %get-tuple-element.96.refs_0_), channel_id=1, source_target_pairs={{0,6},{1,7},{2,4},{3,5},{4,2},{5,3},{6,0},{7,1},{8,14},{9,15},{10,... | collective-permute-start | bytes 245768 | tf_op jit(solution)/shard_map/kernel/ppermute | solution.py:24
  85.5 5.6 %collective-permute-start.36 = (bf16[128,512]{1,0:T(8,128)(2,1)S(1)}, bf16[128,512]{1,0:T(8,128)(2,1)S(1)}, u32[]{:S(2)}, u32[]{:S(2)}) collective-permute-start(bf16[128,512]{1,0:T(8,128)(2,1)S(1)} %get-tuple-element.95), channel_id=1, source_target_pairs={{0,16},{16,24},{24,8},{8,0},{1,17},{17,25},{25,9},{9,1},{2,18},{18... | collective-permute-start | bytes 393224 | tf_op jit(solution)/shard_map/kernel/ppermute | solution.py:34
  88.3 4.7 %collective-permute-start.29 = (bf16[32,1280]{1,0:T(8,128)(2,1)S(1)}, bf16[32,1280]{1,0:T(8,128)(2,1)S(1)}, u32[]{:S(2)}, u32[]{:S(2)}) collective-permute-start(bf16[32,1280]{1,0:T(8,128)(2,1)S(1)} %get-tuple-element.96.refs_0_), channel_id=1, source_target_pairs={{0,1},{1,0},{2,3},{3,2},{4,5},{5,4},{6,7},{7,6},{8,9},{9,8},{10,11... | collective-permute-start | bytes 245768 | tf_op jit(solution)/shard_map/kernel/ppermute | solution.py:24
  88.3 4.7 %collective-permute-start.31 = (bf16[32,1280]{1,0:T(8,128)(2,1)S(1)}, bf16[32,1280]{1,0:T(8,128)(2,1)S(1)}, u32[]{:S(2)}, u32[]{:S(2)}) collective-permute-start(bf16[32,1280]{1,0:T(8,128)(2,1)S(1)} %collective-permute-done.30.refs_2_), channel_id=1, source_target_pairs={{0,1},{1,0},{2,3},{3,2},{4,5},{5,4},{6,7},{7,6},{8,9},{9,8},{10,11... | collective-permute-start | bytes 245768 | tf_op jit(solution)/shard_map/kernel/ppermute | solution.py:24
  88.8 4.2 %collective-permute-start.33 = (bf16[32,1280]{1,0:T(8,128)(2,1)S(1)}, bf16[32,1280]{1,0:T(8,128)(2,1)S(1)}, u32[]{:S(2)}, u32[]{:S(2)}) collective-permute-start(bf16[32,1280]{1,0:T(8,128)(2,1)S(1)} %collective-permute-done.32.refs_4_), channel_id=1, source_target_pairs={{0,1},{1,0},{2,3},{3,2},{4,5},{5,4},{6,7},{7,6},{8,9},{9,8},{10,11... | collective-permute-start | bytes 245768 | tf_op jit(solution)/shard_map/kernel/ppermute | solution.py:24
  89.5 3.5 %collective-permute-start.35 = (bf16[32,1280]{1,0:T(8,128)(2,1)S(1)}, bf16[32,1280]{1,0:T(8,128)(2,1)S(1)}, u32[]{:S(2)}, u32[]{:S(2)}) collective-permute-start(bf16[32,1280]{1,0:T(8,128)(2,1)S(1)} %collective-permute-done.34.refs_6_), channel_id=1, source_target_pairs={{0,1},{1,0},{2,3},{3,2},{4,5},{5,4},{6,7},{7,6},{8,9},{9,8},{10,11... | collective-permute-start | bytes 245768 | tf_op jit(solution)/shard_map/kernel/ppermute | solution.py:24
  91.0 6.9 %collective-permute-start.37 = (bf16[128,512]{1,0:T(8,128)(2,1)S(1)}, bf16[128,512]{1,0:T(8,128)(2,1)S(1)}, u32[]{:S(2)}, u32[]{:S(2)}) collective-permute-start(bf16[128,512]{1,0:T(8,128)(2,1)S(1)} %get-tuple-element.105), channel_id=1, source_target_pairs={{0,24},{16,8},{24,0},{8,16},{1,25},{17,9},{25,1},{9,17},{2,26},{18... | collective-permute-start | bytes 393224 | tf_op jit(solution)/shard_map/dz/ppermute | solution.py:34
  99.7 2.8 %collective-permute-start.38 = (bf16[4,272,512]{2,1,0:T(8,128)(2,1)S(1)}, bf16[4,272,512]{2,1,0:T(8,128)(2,1)S(1)}, u32[]{:S(2)}, u32[]{:S(2)}) collective-permute-start(bf16[4,272,512]{2,1,0:T(8,128)(2,1)S(1)} %d_act_matmul.2), channel_id=1, source_target_pairs={{0,1},{1,0},{2,3},{3,2},{4,5},{5,4},{6,7},{7,6},{8,9},{9,8},{10,11... | collective-permute-start | bytes 3342344 | tf_op jit(solution)/shard_map/d_act/ppermute | solution.py:24
  104.4 7.7 %collective-permute-start.42 = (bf16[128,512]{1,0:T(8,128)(2,1)S(1)}, bf16[128,512]{1,0:T(8,128)(2,1)S(1)}, u32[]{:S(2)}, u32[]{:S(2)}) collective-permute-start(bf16[128,512]{1,0:T(8,128)(2,1)S(1)} %get-tuple-element.116), channel_id=1, source_target_pairs={{0,8},{16,0},{24,16},{8,24},{1,9},{17,1},{25,17},{9,25},{2,10},{18... | collective-permute-start | bytes 393224 | tf_op jit(solution)/shard_map/grad_weight/ppermute | solution.py:34
  108.5 9.6 %collective-permute-start.39 = (bf16[272,512]{1,0:T(8,128)(2,1)S(1)}, bf16[272,512]{1,0:T(8,128)(2,1)S(1)}, u32[]{:S(2)}, u32[]{:S(2)}) collective-permute-start(bf16[272,512]{1,0:T(8,128)(2,1)S(1)} %get-tuple-element.111), channel_id=1, source_target_pairs={{0,2},{1,3},{2,0},{3,1},{4,6},{5,7},{6,4},{7,5},{8,10},{9,11},{10,... | collective-permute-start | bytes 835592 | tf_op jit(solution)/shard_map/d_act/ppermute | solution.py:24
  109.1 14.1 %collective-permute-start.40 = (bf16[272,512]{1,0:T(8,128)(2,1)S(1)}, bf16[272,512]{1,0:T(8,128)(2,1)S(1)}, u32[]{:S(2)}, u32[]{:S(2)}) collective-permute-start(bf16[272,512]{1,0:T(8,128)(2,1)S(1)} %get-tuple-element.112), channel_id=1, source_target_pairs={{0,4},{1,5},{2,6},{3,7},{4,0},{5,1},{6,2},{7,3},{8,12},{9,13},{10,... | collective-permute-start | bytes 835592 | tf_op jit(solution)/shard_map/d_act/ppermute | solution.py:24
  110.4 12.8 %collective-permute-start.41 = (bf16[272,512]{1,0:T(8,128)(2,1)S(1)}, bf16[272,512]{1,0:T(8,128)(2,1)S(1)}, u32[]{:S(2)}, u32[]{:S(2)}) collective-permute-start(bf16[272,512]{1,0:T(8,128)(2,1)S(1)} %get-tuple-element.113), channel_id=1, source_target_pairs={{0,6},{1,7},{2,4},{3,5},{4,2},{5,3},{6,0},{7,1},{8,14},{9,15},{10,... | collective-permute-start | bytes 835592 | tf_op jit(solution)/shard_map/d_act/ppermute | solution.py:24
  112.1 20.5 %collective-permute-start.46 = (bf16[384,512]{1,0:T(8,128)(2,1)S(1)}, bf16[384,512]{1,0:T(8,128)(2,1)S(1)}, u32[]{:S(2)}, u32[]{:S(2)}) collective-permute-start(bf16[384,512]{1,0:T(8,128)(2,1)S(1)} %constant_dynamic-update-slice_fusion.5.refs_4_), channel_id=1, source_target_pairs={{0,1},{1,0},{2,3},{3,2},{4,5},{5,4},{6,7},{7,6},{8,9},{9,8},{10,11... | collective-permute-start | bytes 1179656 | tf_op jit(solution)/shard_map/grad_weight/ppermute | solution.py:24
  123.9 5.8 %collective-permute-start.43 = (f32[8,512]{1,0:T(8,128)S(1)}, f32[8,512]{1,0:T(8,128)S(1)}, u32[]{:S(2)}, u32[]{:S(2)}) collective-permute-start(f32[8,512]{1,0:T(8,128)S(1)} %pad_maximum_fusion.1.refs_0_), channel_id=1, source_target_pairs={{0,8},{8,0},{16,24},{24,16},{1,9},{9,1},{17,25},{25,17},{2,10},{10... | collective-permute-start | bytes 49160 | tf_op jit(solution)/shard_map/norm_backward/ppermute | solution.py:24
  124.3 5.4 %collective-permute-start.44 = (f32[8,512]{1,0:T(8,128)S(1)}, f32[8,512]{1,0:T(8,128)S(1)}, u32[]{:S(2)}, u32[]{:S(2)}) collective-permute-start(f32[8,512]{1,0:T(8,128)S(1)} %pad_maximum_fusion.1.refs_0_), channel_id=1, source_target_pairs={{0,16},{8,24},{16,0},{24,8},{1,17},{9,25},{17,1},{25,9},{2,18},{10... | collective-permute-start | bytes 49160 | tf_op jit(solution)/shard_map/norm_backward/ppermute | solution.py:24
  126.2 5.5 %collective-permute-start.45 = (f32[8,512]{1,0:T(8,128)S(1)}, f32[8,512]{1,0:T(8,128)S(1)}, u32[]{:S(2)}, u32[]{:S(2)}) collective-permute-start(f32[8,512]{1,0:T(8,128)S(1)} %pad_maximum_fusion.1.refs_0_), channel_id=1, source_target_pairs={{0,24},{8,16},{16,8},{24,0},{1,25},{9,17},{17,9},{25,1},{2,26},{10... | collective-permute-start | bytes 49160 | tf_op jit(solution)/shard_map/norm_backward/ppermute | solution.py:24
  (2 other events, 19.5 us)

commit v13 on v12

--- a/solution.py
+++ b/solution.py
@@ -576,39 +576,30 @@
         preactivation = norm_scale_gain * normalised + norm_shift_bias
         act = jax.nn.gelu(preactivation, approximate=True).astype(bf16)
     with jax.named_scope("act_gather"):
-        others = [ring_send(act[0], "batch", d) for d in range(1, n_batch)]
         own = act.reshape(tall, width)
-        sibling = xor_send(own, "col", 1)
-        own, sibling = lax.optimization_barrier((own, sibling))
-        pieces = link_pieces(own, n_col)
-        pieces[1] = sibling
-        others, pieces[far[0]] = lax.optimization_barrier((others, pieces[far[0]]))
+        pieces = {0: own, 1: xor_send(own, "col", 1)}
+        for k in far:
+            pieces[k] = xor_send(own, "col", k)
+        first, pieces[1] = lax.optimization_barrier((act[0], pieces[1]))
+        others = [ring_send(first, "batch", d) for d in range(1, n_batch)]
         pieces = sibling_pieces(pieces, n_col)
+    with jax.named_scope("z"):
+
+        def z_part(source, ks, before, last=False):
+            return z_call(
+                place, ks, [source[k] for k in ks], held_weight, before, last, local_rows
+            )
+
+        z_own = z_part(pieces, far, z_part(pieces, [0, 1], None))
+        z_own, others[-1] = lax.optimization_barrier((z_own, others[-1]))
+        z_own0, z_own1 = z_part(pieces, [k + 1 for k in far], z_own, True)
         far_pieces = link_pieces(jnp.concatenate(others), n_col)
-    with jax.named_scope("z"):
-
-        def z_of(source, groups, total=None):
-            for i, ks in enumerate(groups):
-                total = z_call(
-                    place,
-                    ks,
-                    [source[k] for k in ks],
-                    held_weight,
-                    total,
-                    i == len(groups) - 1,
-                    local_rows,
-                )
-            return total
-
-        z_own0, z_own1 = z_of(pieces, [[0, 1], far, [k + 1 for k in far]])
     with jax.named_scope("z_ring"):
         z_ring = [z_own1, ring_send(z_own1, "batch", 1)]
         z_ring[1], far_pieces[far[0]] = lax.optimization_barrier((z_ring[1], far_pieces[far[0]]))
         z_ring.append(ring_send(z_ring[1], "batch", 1))
     with jax.named_scope("z_far"):
-        start = z_call(
-            place, [0] + far[:-1], [far_pieces[k] for k in [0] + far[:-1]], held_weight, None, False, local_rows
-        )
+        start = z_part(far_pieces, [0] + far[:-1], None)
         picked = list(pick_call(place, [pieces[k] for k in evens], n_batch, n_col))
         start, far_pieces[far[-1]], z_ring[2], picked = lax.optimization_barrier(
             (start, far_pieces[far[-1]], z_ring[2], picked)
@@ -616,17 +607,11 @@
         far_pieces = sibling_pieces(far_pieces, n_col)
         for _ in range(3, n_batch):
             z_ring.append(ring_send(z_ring[-1], "batch", 1))
-        z_far = z_of(far_pieces, [odds[:-1] + far[-1:] + odds[-1:]], start)
+        z_far = z_part(far_pieces, odds[:-1] + far[-1:] + odds[-1:], start, True)
         slots = list(zip([z_own0] + list(z_far), z_ring))
     with jax.named_scope("kernel"):
         even_part, odd_part = strip_call(place, slots, n_col)
         even_part = even_part + xor_send(odd_part, "col", 1).astype(f32)
-        early = len(picked) // 3
-        even_part, picked[:early] = lax.optimization_barrier((even_part, picked[:early]))
-
-        def sent(i):
-            return ring_send(picked[i], "batch", 1 + i % (n_batch - 1))
-
         strip = even_part[0]
         for k in far:
             strip = strip + xor_send(even_part[k // 2].astype(bf16), "col", k).astype(f32)
@@ -635,8 +620,6 @@
         for k in far:
             strips[k] = xor_send(strip_b, "col", k)
         strips = sibling_pieces(strips, n_col)
-        blocks = [sent(i) for i in range(early)]
-        strips, blocks = lax.optimization_barrier((strips, blocks))
     with jax.named_scope("dz"):
         constants = (
             4.0 * scale / denom,
@@ -648,17 +631,16 @@
             1.0 / denom / n_batch,
         )
         dz, share = dz_call(place, strip, [strips[k] for k in range(n_col)], slots, constants)
-        blocks += [sent(i) for i in range(early, 2 * early)]
-        dz, blocks[early:] = lax.optimization_barrier((dz, blocks[early:]))
     with jax.named_scope("d_act"):
         (away,) = d_act_call(place, dz, share, held_weight, n_batch, n_col, None)
         got = xor_send(away, "col", 1)
         *sends, d_act = d_act_call(place, dz, share, held_weight, n_batch, n_col, got)
         arrived = [xor_send(part, "col", k) for k, part in zip(far, sends)]
     with jax.named_scope("grad_weight"):
-        late = picked[2 * early :]
-        d_act, picked[2 * early :] = lax.optimization_barrier((d_act, late))
-        blocks += [sent(i) for i in range(2 * early, len(picked))]
+        d_act, picked = lax.optimization_barrier((d_act, picked))
+        blocks = [
+            ring_send(x, "batch", 1 + i % (n_batch - 1)) for i, x in enumerate(picked)
+        ]
         sides = ((0, evens), (1, odds))
         products = {}
         for block in range(n_col // n_batch // 2):
@@ -666,6 +648,7 @@
                 products[block, parity] = weight_grad_call(
                     place, n_batch, block, [pieces[k] for k in ks], [far_pieces[k] for k in ks], dz
                 )
+        arrived, blocks, products = lax.optimization_barrier((arrived, blocks, products))
         grad_weight = None
         for block in range(n_col // n_batch // 2):
             mine = jnp.concatenate(blocks[block * (n_batch - 1) : (block + 1) * (n_batch - 1)])
@@ -681,8 +664,6 @@
                     features // n_batch,
                     grad_weight,
                 )
-                if block == 0 and parity == 0:
-                    arrived, grad_weight = lax.optimization_barrier((arrived, grad_weight))
     with jax.named_scope("norm_backward"):
         share = exchange_sum(share_of(part[tall:]) for part in [d_act] + arrived)
         d_act = d_act[:tall]

time: 135 us -> 125 us (0.926)
  waiting for transfers between devices: 52.1 us -> 34.7 us
  starting transfers between devices: 46 us -> 52.7 us
    ppermute x38 -> x37, waiting for transfers between devices: 34.2 us -> 24.4 us  [xor_send(): return lax.ppermute(x, axis, [(i, i ^ k) for i in range(n)])]
    ppermute x9, waiting for transfers between devices: 17.9 us -> 10.3 us  [ring_send(): lax.ppermute(x, axis, [(order[i], order[(i + d) % n]) for i in range(n)])]
    ppermute x9, starting transfers between devices: 15.7 us -> 21.6 us  [ring_send(): lax.ppermute(x, axis, [(order[i], order[(i + d) % n]) for i in range(n)])]
    ppermute x38 -> x37, starting transfers between devices: 30.3 us -> 31.2 us  [xor_send(): return lax.ppermute(x, axis, [(i, i ^ k) for i in range(n)])]
  transfers between devices with their start and end apart: 47 -> 46, of which waited for: 25 -> 18; matrix products, arithmetic and copies ran while one was open for 1% -> 1% of each run, Pallas kernels for 17% -> 15%
where the time goes in v13:
time: 125 us; the launch traced here: 124 us
  starting transfers between devices  52.7 us (42%)
  waiting for transfers between devices  34.7 us (28%)
  Pallas kernels  32.4 us (26%)
  other arithmetic  3.21 us (3%)
  between operations  1.25 us (1%)
    ppermute x37, starting transfers between devices, xor_send(): return lax.ppermute(x, axis, [(i, i ^ k) for i in range(n)])  31.2 us
    ppermute x37, waiting for transfers between devices, xor_send(): return lax.ppermute(x, axis, [(i, i ^ k) for i in range(n)])  24.4 us
    ppermute x9, starting transfers between devices, ring_send(): lax.ppermute(x, axis, [(order[i], order[(i + d) % n]) for i in range(n)])  21.6 us
    ppermute x9, waiting for transfers between devices, ring_send(): lax.ppermute(x, axis, [(order[i], order[(i + d) % n]) for i in range(n)])  10.3 us
    pallas_call x5, Pallas kernels, z_call(): pl.pallas_call(functools.partial(z_kernel, tuple(ks), before is None, las...  8.96 us
    pallas_call x2, Pallas kernels, weight_grad_last_call(): pl.pallas_call(functools.partial(weight_grad_last_kernel, rows // (own[0]...  4.76 us
    pallas_call x1, Pallas kernels, dz_call(): pl.pallas_call(functools.partial(dz_kernel, n_batch, n_col, tile, constan...  4.66 us
    pallas_call x2, Pallas kernels, d_act_call(): pl.pallas_call(functools.partial(d_act_kernel, count, (got is not None, n...  3.69 us
  transfers between devices with their start and end apart: 46, of which 18 were waited for; matrix products, arithmetic and copies ran while one was open for 1% of the time, Pallas kernels for 15%

profile of v13, /device:TPU:0, one launch (start us, length us, event | category | flops | bytes accessed | tf_op | source)
XLA Modules:
  0.0 124.4 jit_solution(15550821200824503296)
XLA Ops:
  2.8 5.1 %collective-permute-start.2 = (f32[4,512]{1,0:T(4,128)S(1)}, f32[4,512]{1,0:T(4,128)S(1)}, u32[]{:S(2)}, u32[]{:S(2)}) collective-permute-start(f32[4,512]{1,0:T(4,128)S(1)} %pad_maximum_fusion.2), channel_id=1, source_target_pairs={{0,24},{8,16},{16,8},{24,0},{1,25},{9,17},{17,9},{25,1},{2,26},{10... | collective-permute-start | bytes 24584 | tf_op jit(solution)/shard_map/norm_stats/ppermute | solution.py:24
  8.6 3.5 %weight_load.1 = (bf16[4096,1024]{1,0:T(8,128)(2,1)S(1)}, f32[4,512]{1,0:T(4,128)S(1)}) custom-call(bf16[4096,1024]{1,0:T(8,128)(2,1)} %w_ref), custom_call_target="tpu_custom_call" | custom-call | bytes 16777216 | tf_op jit(solution)/shard_map/weight_load/weight_load/pallas_call | solution.py:78
  12.9 1.6 %collective-permute-start.3 = (bf16[256,512]{1,0:T(8,128)(2,1)S(1)}, bf16[256,512]{1,0:T(8,128)(2,1)S(1)}, u32[]{:S(2)}, u32[]{:S(2)}) collective-permute-start(bf16[256,512]{1,0:T(8,128)(2,1)S(1)} %bitcast.29), channel_id=1, source_target_pairs={{0,2},{1,3},{2,0},{3,1},{4,6},{5,7},{6,4},{7,5},{8,10},{9,11},{10,... | collective-permute-start | bytes 786440 | tf_op jit(solution)/shard_map/act_gather/ppermute | solution.py:24
  14.4 1.5 %collective-permute-start.5 = (bf16[256,512]{1,0:T(8,128)(2,1)S(1)}, bf16[256,512]{1,0:T(8,128)(2,1)S(1)}, u32[]{:S(2)}, u32[]{:S(2)}) collective-permute-start(bf16[256,512]{1,0:T(8,128)(2,1)S(1)} %bitcast.30), channel_id=1, source_target_pairs={{0,4},{1,5},{2,6},{3,7},{4,0},{5,1},{6,2},{7,3},{8,12},{9,13},{10,... | collective-permute-start | bytes 786440 | tf_op jit(solution)/shard_map/act_gather/ppermute | solution.py:24
  16.5 2.1 %collective-permute-start.11 = (bf16[128,512]{1,0:T(8,128)(2,1)S(1)}, bf16[128,512]{1,0:T(8,128)(2,1)S(1)}, u32[]{:S(2)}, u32[]{:S(2)}) collective-permute-start(bf16[128,512]{1,0:T(8,128)(2,1)S(1)} %slice_bitcast_fusion.1), channel_id=1, source_target_pairs={{0,16},{16,24},{24,8},{8,0},{1,17},{17,25},{25,9},{9,1},{2,18},{18... | collective-permute-start | bytes 393224 | tf_op jit(solution)/shard_map/act_gather/ppermute | solution.py:34
  18.5 1.2 %z_matmul.5.refs_4_ = f32[256,1024]{1,0:T(8,128)S(1)} custom-call(s32[2]{0:T(128)S(1)} %pad_add_fusion.place_ref, bf16[256,512]{1,0:T(8,128)(2,1)S(1)} %bitcast.32, bf16[256,512]{1,0:T(8,128)(2,1)S(1)} %collective-permute-done.9.refs_1_.refs_0_, bf16[4096,1024]{1,0:T(8,128)(2,1)S(1)} %get-tuple-element.62.refs_2_.refs_3_.refs_5_.w_ref), custom_call_target="tpu_custom_call" | custom-call | flops 536870912 | bytes 524288 | tf_op jit(solution)/shard_map/z/z_matmul/pallas_call | solution.py:126
  19.8 2.3 %collective-permute-done.3.refs_0_.refs_1_ = bf16[256,512]{1,0:T(8,128)(2,1)S(1)} collective-permute-done((bf16[256,512]{1,0:T(8,128)(2,1)S(1)}, bf16[256,512]{1,0:T(8,128)(2,1)S(1)}, u32[]{:S(2)}, u32[]{:S(2)}) %collective-permute-start.3) | collective-permute-done | bytes 262176 | tf_op jit(solution)/shard_map/act_gather/ppermute | solution.py:24
  22.1 3.4 %collective-permute-start.12 = (bf16[128,512]{1,0:T(8,128)(2,1)S(1)}, bf16[128,512]{1,0:T(8,128)(2,1)S(1)}, u32[]{:S(2)}, u32[]{:S(2)}) collective-permute-start(bf16[128,512]{1,0:T(8,128)(2,1)S(1)} %slice_bitcast_fusion.1), channel_id=1, source_target_pairs={{0,24},{16,8},{24,0},{8,16},{1,25},{17,9},{25,1},{9,17},{2,26},{18... | collective-permute-start | bytes 393224 | tf_op jit(solution)/shard_map/act_gather/ppermute | solution.py:34
  25.4 3.0 %collective-permute-done.5.refs_1_.refs_2_ = bf16[256,512]{1,0:T(8,128)(2,1)S(1)} collective-permute-done((bf16[256,512]{1,0:T(8,128)(2,1)S(1)}, bf16[256,512]{1,0:T(8,128)(2,1)S(1)}, u32[]{:S(2)}, u32[]{:S(2)}) %collective-permute-start.5) | collective-permute-done | bytes 262176 | tf_op jit(solution)/shard_map/act_gather/ppermute | solution.py:24
  29.0 1.5 %z_matmul.6.refs_4_ = f32[256,1024]{1,0:T(8,128)S(1)} custom-call(s32[2]{0:T(128)S(1)} %pad_add_fusion.place_ref, bf16[256,512]{1,0:T(8,128)(2,1)S(1)} %collective-permute-done.3.refs_0_.refs_1_, bf16[256,512]{1,0:T(8,128)(2,1)S(1)} %collective-permute-done.5.refs_1_.refs_2_, bf16[256,512]{1,0:T(8,128)(2,1)S(1)} %collective-permute-done.7.refs_2_.refs_3_, ...), custom_call_target="tpu_custom_call" | custom-call | flops 805306368 | bytes 524288 | tf_op jit(solution)/shard_map/z/z_matmul/pallas_call | solution.py:126
  30.6 1.3 %collective-permute-start.15 = (bf16[384,512]{1,0:T(8,128)(2,1)S(1)}, bf16[384,512]{1,0:T(8,128)(2,1)S(1)}, u32[]{:S(2)}, u32[]{:S(2)}) collective-permute-start(bf16[384,512]{1,0:T(8,128)(2,1)S(1)} %constant_dynamic-update-slice_fusion.refs_0_.refs_4_), channel_id=1, source_target_pairs={{0,2},{1,3},{2,0},{3,1},{4,6},{5,7},{6,4},{7,5},{8,10},{9,11},{10,... | collective-permute-start | bytes 1179656 | tf_op jit(solution)/shard_map/z/ppermute | solution.py:24
  32.8 1.5 %z_matmul.7 = (bf16[128,1024]{1,0:T(8,128)(2,1)S(1)}, bf16[128,1024]{1,0:T(8,128)(2,1)S(1)}) custom-call(s32[2]{0:T(128)S(1)} %pad_add_fusion.place_ref, bf16[256,512]{1,0:T(8,128)(2,1)S(1)} %collective-permute-done.4.refs_0_.refs_1_, bf16[256,512]{1,0:T(8,128)(2,1)S(1)} %collective-permute-done.6.refs_1_.refs_2_, ...), custom_call_target="tpu_custom_call" | custom-call | flops 805306368 | bytes 524288 | tf_op jit(solution)/shard_map/z/z_matmul/pallas_call | solution.py:126
  34.3 3.3 %collective-permute-start.14 = (bf16[128,1024]{1,0:T(8,128)(2,1)S(1)}, bf16[128,1024]{1,0:T(8,128)(2,1)S(1)}, u32[]{:S(2)}, u32[]{:S(2)}) collective-permute-start(bf16[128,1024]{1,0:T(8,128)(2,1)S(1)} %get-tuple-element.67.refs_1_.refs_9_), channel_id=1, source_target_pairs={{0,16},{16,24},{24,8},{8,0},{1,17},{17,25},{25,9},{9,1},{2,18},{18... | collective-permute-start | bytes 786440 | tf_op jit(solution)/shard_map/z_ring/ppermute | solution.py:34
  37.6 4.6 %collective-permute-done.15.refs_1_.refs_5_ = bf16[384,512]{1,0:T(8,128)(2,1)S(1)} collective-permute-done((bf16[384,512]{1,0:T(8,128)(2,1)S(1)}, bf16[384,512]{1,0:T(8,128)(2,1)S(1)}, u32[]{:S(2)}, u32[]{:S(2)}) %collective-permute-start.15) | collective-permute-done | bytes 393248 | tf_op jit(solution)/shard_map/z/ppermute | solution.py:24
  42.2 1.6 %collective-permute-start.20 = (bf16[192,512]{1,0:T(8,128)(2,1)S(1)}, bf16[192,512]{1,0:T(8,128)(2,1)S(1)}, u32[]{:S(2)}, u32[]{:S(2)}) collective-permute-start(bf16[192,512]{1,0:T(8,128)(2,1)S(1)} %slice.150), channel_id=1, source_target_pairs={{0,4},{1,5},{2,6},{3,7},{4,0},{5,1},{6,2},{7,3},{8,12},{9,13},{10,... | collective-permute-start | bytes 589832 | tf_op jit(solution)/shard_map/z/ppermute | solution.py:24
  44.5 2.4 %collective-permute-start.21 = (bf16[128,1024]{1,0:T(8,128)(2,1)S(1)}, bf16[128,1024]{1,0:T(8,128)(2,1)S(1)}, u32[]{:S(2)}, u32[]{:S(2)}) collective-permute-start(bf16[128,1024]{1,0:T(8,128)(2,1)S(1)} %collective-permute-done.14.refs_3_.refs_11_), channel_id=1, source_target_pairs={{0,16},{16,24},{24,8},{8,0},{1,17},{17,25},{25,9},{9,1},{2,18},{18... | collective-permute-start | bytes 786440 | tf_op jit(solution)/shard_map/z_ring/ppermute | solution.py:34
  48.1 1.9 %z_matmul.8.refs_6_ = f32[384,1024]{1,0:T(8,128)S(1)} custom-call(s32[2]{0:T(128)S(1)} %pad_add_fusion.place_ref, bf16[384,512]{1,0:T(8,128)(2,1)S(1)} %constant_dynamic-update-slice_fusion.refs_0_.refs_4_, bf16[384,512]{1,0:T(8,128)(2,1)S(1)} %collective-permute-done.15.refs_1_.refs_5_, bf16[384,512]{1,0:T(8,128)(2,1)S(1)} %collective-permute-done.17.refs_2_.refs_6_, ...), custom_call_target="tpu_custom_call" | custom-call | flops 1207959552 | bytes 786432 | tf_op jit(solution)/shard_map/z_far/z_matmul/pallas_call | solution.py:126
  50.2 1.6 %collective-permute-done.21.refs_5_.refs_13_ = bf16[128,1024]{1,0:T(8,128)(2,1)S(1)} collective-permute-done((bf16[128,1024]{1,0:T(8,128)(2,1)S(1)}, bf16[128,1024]{1,0:T(8,128)(2,1)S(1)}, u32[]{:S(2)}, u32[]{:S(2)}) %collective-permute-start.21) | collective-permute-done | bytes 262176 | tf_op jit(solution)/shard_map/z_ring/ppermute | solution.py:34
  51.8 2.5 %collective-permute-start.23 = (bf16[128,1024]{1,0:T(8,128)(2,1)S(1)}, bf16[128,1024]{1,0:T(8,128)(2,1)S(1)}, u32[]{:S(2)}, u32[]{:S(2)}) collective-permute-start(bf16[128,1024]{1,0:T(8,128)(2,1)S(1)} %collective-permute-done.21.refs_5_.refs_13_), channel_id=1, source_target_pairs={{0,16},{16,24},{24,8},{8,0},{1,17},{17,25},{25,9},{9,1},{2,18},{18... | collective-permute-start | bytes 786440 | tf_op jit(solution)/shard_map/z_far/ppermute | solution.py:34
  54.3 2.7 %z_matmul.9 = (bf16[128,1024]{1,0:T(8,128)(2,1)S(1)}, bf16[128,1024]{1,0:T(8,128)(2,1)S(1)}, bf16[128,1024]{1,0:T(8,128)(2,1)S(1)}) custom-call(s32[2]{0:T(128)S(1)} %pad_add_fusion.place_ref, bf16[384,512]{1,0:T(8,128)(2,1)S(1)} %collective-permute-done.13.refs_0_.refs_4_, bf16[384,512]{1,0:T(8,128)(2,1)S(1)} %collective-permute-done.16.refs_1_.refs_5_, ...), custom_call_target="tpu_custom_call" | custom-call | flops 2013265920 | bytes 786432 | tf_op jit(solution)/shard_map/z_far/z_matmul/pallas_call | solution.py:126
  57.0 3.9 %collective-permute-done.23.refs_7_.refs_15_ = bf16[128,1024]{1,0:T(8,128)(2,1)S(1)} collective-permute-done((bf16[128,1024]{1,0:T(8,128)(2,1)S(1)}, bf16[128,1024]{1,0:T(8,128)(2,1)S(1)}, u32[]{:S(2)}, u32[]{:S(2)}) %collective-permute-start.23) | collective-permute-done | bytes 262176 | tf_op jit(solution)/shard_map/z_far/ppermute | solution.py:34
  61.0 2.6 %kernel_strip.1 = (f32[4,32,1280]{2,1,0:T(8,128)S(1)}, bf16[4,32,1280]{2,1,0:T(8,128)(2,1)S(1)}) custom-call(s32[2]{0:T(128)S(1)} %pad_add_fusion.place_ref, bf16[128,1024]{1,0:T(8,128)(2,1)S(1)} %get-tuple-element.66.refs_0_.refs_8_, bf16[128,1024]{1,0:T(8,128)(2,1)S(1)} %get-tuple-element.67.refs_1_.refs_9_, ...), custom_call_target="tpu_custom_call" | custom-call | flops 671088640 | bytes 2097152 | tf_op jit(solution)/shard_map/kernel/kernel_strip/pallas_call | solution.py:173
  63.7 1.6 %collective-permute-done.24 = bf16[4,32,1280]{2,1,0:T(8,128)(2,1)S(1)} collective-permute-done((bf16[4,32,1280]{2,1,0:T(8,128)(2,1)S(1)}, bf16[4,32,1280]{2,1,0:T(8,128)(2,1)S(1)}, u32[]{:S(2)}, u32[]{:S(2)}) %collective-permute-start.24) | collective-permute-done | bytes 327712 | tf_op jit(solution)/shard_map/kernel/ppermute | solution.py:24
  65.4 1.5 %collective-permute-start.27 = (bf16[32,1280]{1,0:T(8,128)(2,1)S(1)}, bf16[32,1280]{1,0:T(8,128)(2,1)S(1)}, u32[]{:S(2)}, u32[]{:S(2)}) collective-permute-start(bf16[32,1280]{1,0:T(8,128)(2,1)S(1)} %get-tuple-element.117), channel_id=1, source_target_pairs={{0,6},{1,7},{2,4},{3,5},{4,2},{5,3},{6,0},{7,1},{8,14},{9,15},{10,... | collective-permute-start | bytes 245768 | tf_op jit(solution)/shard_map/kernel/ppermute | solution.py:24
  66.9 1.5 %collective-permute-start.26 = (bf16[32,1280]{1,0:T(8,128)(2,1)S(1)}, bf16[32,1280]{1,0:T(8,128)(2,1)S(1)}, u32[]{:S(2)}, u32[]{:S(2)}) collective-permute-start(bf16[32,1280]{1,0:T(8,128)(2,1)S(1)} %get-tuple-element.118), channel_id=1, source_target_pairs={{0,4},{1,5},{2,6},{3,7},{4,0},{5,1},{6,2},{7,3},{8,12},{9,13},{10,... | collective-permute-start | bytes 245768 | tf_op jit(solution)/shard_map/kernel/ppermute | solution.py:24
  69.0 2.3 %collective-permute-done.27 = bf16[32,1280]{1,0:T(8,128)(2,1)S(1)} collective-permute-done((bf16[32,1280]{1,0:T(8,128)(2,1)S(1)}, bf16[32,1280]{1,0:T(8,128)(2,1)S(1)}, u32[]{:S(2)}, u32[]{:S(2)}) %collective-permute-start.27) | collective-permute-done | bytes 81952 | tf_op jit(solution)/shard_map/kernel/ppermute | solution.py:24
  71.3 1.4 %collective-permute-done.26 = bf16[32,1280]{1,0:T(8,128)(2,1)S(1)} collective-permute-done((bf16[32,1280]{1,0:T(8,128)(2,1)S(1)}, bf16[32,1280]{1,0:T(8,128)(2,1)S(1)}, u32[]{:S(2)}, u32[]{:S(2)}) %collective-permute-start.26) | collective-permute-done | bytes 81952 | tf_op jit(solution)/shard_map/kernel/ppermute | solution.py:24
  72.9 1.2 collective-permute-start.29
  74.9 1.6 %collective-permute-start.33 = (bf16[32,1280]{1,0:T(8,128)(2,1)S(1)}, bf16[32,1280]{1,0:T(8,128)(2,1)S(1)}, u32[]{:S(2)}, u32[]{:S(2)}) collective-permute-start(bf16[32,1280]{1,0:T(8,128)(2,1)S(1)} %get-tuple-element.110.refs_0_), channel_id=1, source_target_pairs={{0,6},{1,7},{2,4},{3,5},{4,2},{5,3},{6,0},{7,1},{8,14},{9,15},{10,... | collective-permute-start | bytes 245768 | tf_op jit(solution)/shard_map/kernel/ppermute | solution.py:24
  77.5 2.9 %collective-permute-done.31.refs_4_ = bf16[32,1280]{1,0:T(8,128)(2,1)S(1)} collective-permute-done((bf16[32,1280]{1,0:T(8,128)(2,1)S(1)}, bf16[32,1280]{1,0:T(8,128)(2,1)S(1)}, u32[]{:S(2)}, u32[]{:S(2)}) %collective-permute-start.31) | collective-permute-done | bytes 81952 | tf_op jit(solution)/shard_map/kernel/ppermute | solution.py:24
  81.8 4.7 %embedding_gradient.1 = (bf16[2,512,1024]{2,1,0:T(8,128)(2,1)S(1)}, f32[8,128]{1,0:T(8,128)S(1)}) custom-call(s32[2]{0:T(128)S(1)} %pad_add_fusion.place_ref, f32[32,1280]{1,0:T(8,128)S(1)} %get-tuple-element.111.own_ref, bf16[32,1280]{1,0:T(8,128)(2,1)S(1)} %get-tuple-element.110.refs_0_, bf16[32,1280]{1,0:T(8,128)(2,1)S(1)} %collective-permute-done.28.refs_1_, ...), custom_call_target="tpu_custom_call" | custom-call | flops 1073741824 | bytes 4194304 | tf_op jit(solution)/shard_map/dz/embedding_gradient/pallas_call | solution.py:251
  86.4 1.8 %d_act_matmul.2 = bf16[4,272,512]{2,1,0:T(8,128)(2,1)S(1)} custom-call(s32[2]{0:T(128)S(1)} %pad_add_fusion.place_ref, bf16[2,512,1024]{2,1,0:T(8,128)(2,1)S(1)} %get-tuple-element.82.dz_ref.refs_8_.refs_5_, f32[8,128]{1,0:T(8,128)S(1)} %get-tuple-element.83.share_ref, bf16[4096,1024]{1,0:T(8,128)(2,1)S(1)} %get-tuple-element.62.refs_2_.refs_3_.refs_5_.w_ref), custom_call_target="tpu_custom_call" | custom-call | flops 1073741824 | bytes 1048576 | tf_op jit(solution)/shard_map/d_act/d_act_matmul/pallas_call | solution.py:323
  88.7 2.4 %collective-permute-done.35.refs_0_ = bf16[4,272,512]{2,1,0:T(8,128)(2,1)S(1)} collective-permute-done((bf16[4,272,512]{2,1,0:T(8,128)(2,1)S(1)}, bf16[4,272,512]{2,1,0:T(8,128)(2,1)S(1)}, u32[]{:S(2)}, u32[]{:S(2)}) %collective-permute-start.35) | collective-permute-done | bytes 1114144 | tf_op jit(solution)/shard_map/d_act/ppermute | solution.py:24
  91.1 1.8 %d_act_matmul.3 = (bf16[272,512]{1,0:T(8,128)(2,1)S(1)}, bf16[272,512]{1,0:T(8,128)(2,1)S(1)}, bf16[272,512]{1,0:T(8,128)(2,1)S(1)}, f32[272,512]{1,0:T(8,128)S(1)}) custom-call(s32[2]{0:T(128)S(1)} %pad_add_fusion.place_ref, bf16[2,512,1024]{2,1,0:T(8,128)(2,1)S(1)} %get-tuple-element.82.dz_ref.refs_8_.refs_5_, f32[8,128]{1,0:T(8,128)S(1)} %get-tuple-element.83.share_ref, ...), custom_call_target="tpu_custom_call" | custom-call | flops 1073741824 | bytes 1048576 | tf_op jit(solution)/shard_map/d_act/d_act_matmul/pallas_call | solution.py:323
  93.8 1.2 collective-permute-start.37
  94.9 1.6 %collective-permute-start.38 = (bf16[272,512]{1,0:T(8,128)(2,1)S(1)}, bf16[272,512]{1,0:T(8,128)(2,1)S(1)}, u32[]{:S(2)}, u32[]{:S(2)}) collective-permute-start(bf16[272,512]{1,0:T(8,128)(2,1)S(1)} %get-tuple-element.91), channel_id=1, source_target_pairs={{0,6},{1,7},{2,4},{3,5},{4,2},{5,3},{6,0},{7,1},{8,14},{9,15},{10,... | collective-permute-start | bytes 835592 | tf_op jit(solution)/shard_map/d_act/ppermute | solution.py:24
  96.5 3.1 %collective-permute-start.39 = (bf16[128,512]{1,0:T(8,128)(2,1)S(1)}, bf16[128,512]{1,0:T(8,128)(2,1)S(1)}, u32[]{:S(2)}, u32[]{:S(2)}) collective-permute-start(bf16[128,512]{1,0:T(8,128)(2,1)S(1)} %get-tuple-element.92), channel_id=1, source_target_pairs={{0,16},{16,24},{24,8},{8,0},{1,17},{17,25},{25,9},{9,1},{2,18},{18... | collective-permute-start | bytes 393224 | tf_op jit(solution)/shard_map/grad_weight/ppermute | solution.py:34
  99.6 1.9 %collective-permute-start.40 = (bf16[128,512]{1,0:T(8,128)(2,1)S(1)}, bf16[128,512]{1,0:T(8,128)(2,1)S(1)}, u32[]{:S(2)}, u32[]{:S(2)}) collective-permute-start(bf16[128,512]{1,0:T(8,128)(2,1)S(1)} %get-tuple-element.93), channel_id=1, source_target_pairs={{0,24},{16,8},{24,0},{8,16},{1,25},{17,9},{25,1},{9,17},{2,26},{18... | collective-permute-start | bytes 393224 | tf_op jit(solution)/shard_map/grad_weight/ppermute | solution.py:34
  101.5 1.8 %collective-permute-done.39 = bf16[128,512]{1,0:T(8,128)(2,1)S(1)} collective-permute-done((bf16[128,512]{1,0:T(8,128)(2,1)S(1)}, bf16[128,512]{1,0:T(8,128)(2,1)S(1)}, u32[]{:S(2)}, u32[]{:S(2)}) %collective-permute-start.39) | collective-permute-done | bytes 131104 | tf_op jit(solution)/shard_map/grad_weight/ppermute | solution.py:34
  103.3 3.0 %collective-permute-start.41 = (bf16[128,512]{1,0:T(8,128)(2,1)S(1)}, bf16[128,512]{1,0:T(8,128)(2,1)S(1)}, u32[]{:S(2)}, u32[]{:S(2)}) collective-permute-start(bf16[128,512]{1,0:T(8,128)(2,1)S(1)} %get-tuple-element.94), channel_id=1, source_target_pairs={{0,8},{16,0},{24,16},{8,24},{1,9},{17,1},{25,17},{9,25},{2,10},{18... | collective-permute-start | bytes 393224 | tf_op jit(solution)/shard_map/grad_weight/ppermute | solution.py:34
  106.3 1.3 %weight_gradient_0.2.refs_6_ = f32[512,1024]{1,0:T(8,128)S(1)} custom-call(s32[2]{0:T(128)S(1)} %pad_add_fusion.place_ref, bf16[256,512]{1,0:T(8,128)(2,1)S(1)} %bitcast.34, bf16[256,512]{1,0:T(8,128)(2,1)S(1)} %collective-permute-done.3.refs_0_.refs_1_, bf16[256,512]{1,0:T(8,128)(2,1)S(1)} %collective-permute-done.5.refs_1_.refs_2_, ...), custom_call_target="tpu_custom_call" | custom-call | flops 536870912 | bytes 1048576 | tf_op jit(solution)/shard_map/grad_weight/weight_gradient_0/pallas_call | solution.py:410
  107.7 1.3 %weight_gradient_0.3.refs_6_ = f32[512,1024]{1,0:T(8,128)S(1)} custom-call(s32[2]{0:T(128)S(1)} %pad_add_fusion.place_ref, bf16[256,512]{1,0:T(8,128)(2,1)S(1)} %collective-permute-done.9.refs_1_.refs_0_, bf16[256,512]{1,0:T(8,128)(2,1)S(1)} %collective-permute-done.4.refs_0_.refs_1_, bf16[256,512]{1,0:T(8,128)(2,1)S(1)} %collective-permute-done.6.refs_1_.refs_2_, ...), custom_call_target="tpu_custom_call" | custom-call | flops 536870912 | bytes 1048576 | tf_op jit(solution)/shard_map/grad_weight/weight_gradient_0/pallas_call | solution.py:410
  109.0 2.9 %collective-permute-done.41 = bf16[128,512]{1,0:T(8,128)(2,1)S(1)} collective-permute-done((bf16[128,512]{1,0:T(8,128)(2,1)S(1)}, bf16[128,512]{1,0:T(8,128)(2,1)S(1)}, u32[]{:S(2)}, u32[]{:S(2)}) %collective-permute-start.41) | collective-permute-done | bytes 131104 | tf_op jit(solution)/shard_map/grad_weight/ppermute | solution.py:34
  112.8 2.6 %collective-permute-start.43 = (f32[8,512]{1,0:T(8,128)S(1)}, f32[8,512]{1,0:T(8,128)S(1)}, u32[]{:S(2)}, u32[]{:S(2)}) collective-permute-start(f32[8,512]{1,0:T(8,128)S(1)} %pad_maximum_fusion.1.refs_0_), channel_id=1, source_target_pairs={{0,16},{8,24},{16,0},{24,8},{1,17},{9,25},{17,1},{25,9},{2,18},{10... | collective-permute-start | bytes 49160 | tf_op jit(solution)/shard_map/norm_backward/ppermute | solution.py:24
  115.4 1.8 %collective-permute-start.44 = (f32[8,512]{1,0:T(8,128)S(1)}, f32[8,512]{1,0:T(8,128)S(1)}, u32[]{:S(2)}, u32[]{:S(2)}) collective-permute-start(f32[8,512]{1,0:T(8,128)S(1)} %pad_maximum_fusion.1.refs_0_), channel_id=1, source_target_pairs={{0,24},{8,16},{16,8},{24,0},{1,25},{9,17},{17,9},{25,1},{2,26},{10... | collective-permute-start | bytes 49160 | tf_op jit(solution)/shard_map/norm_backward/ppermute | solution.py:24
  117.2 2.4 %weight_gradient_1.2.refs_7_ = f32[1024,1024]{1,0:T(8,128)} custom-call(s32[2]{0:T(128)S(1)} %pad_add_fusion.place_ref, bf16[256,512]{1,0:T(8,128)(2,1)S(1)} %bitcast.35, bf16[256,512]{1,0:T(8,128)(2,1)S(1)} %collective-permute-done.3.refs_0_.refs_1_, bf16[256,512]{1,0:T(8,128)(2,1)S(1)} %collective-permute-done.5.refs_1_.refs_2_, ...), custom_call_target="tpu_custom_call" | custom-call | flops 536870912 | bytes 2097152 | tf_op jit(solution)/shard_map/grad_weight/weight_gradient_1/pallas_call | solution.py:464
  119.6 1.3 %collective-permute-done.44.refs_3_ = f32[8,512]{1,0:T(8,128)S(1)} collective-permute-done((f32[8,512]{1,0:T(8,128)S(1)}, f32[8,512]{1,0:T(8,128)S(1)}, u32[]{:S(2)}, u32[]{:S(2)}) %collective-permute-start.44) | collective-permute-done | bytes 16416 | tf_op jit(solution)/shard_map/norm_backward/ppermute | solution.py:24
  121.8 2.4 %weight_gradient_1.3 = f32[1024,1024]{1,0:T(8,128)} custom-call(s32[2]{0:T(128)S(1)} %pad_add_fusion.place_ref, bf16[256,512]{1,0:T(8,128)(2,1)S(1)} %collective-permute-done.9.refs_1_.refs_0_, bf16[256,512]{1,0:T(8,128)(2,1)S(1)} %collective-permute-done.4.refs_0_.refs_1_, ...), custom_call_target="tpu_custom_call", output_to_operand_aliasing={{}: (8, {})} | custom-call | flops 536870912 | bytes 2097152 | tf_op jit(solution)/shard_map/grad_weight/weight_gradient_1/pallas_call | solution.py:464
  (91 shorter events, 14.6 us)
Async XLA Ops:
  2.8 9.7 %copy-start = (f32[512]{0:T(512)S(1)}, f32[512]{0:T(512)}, u32[]{:S(2)}) copy-start(f32[512]{0:T(512)} %param.5) | copy-start | bytes 6148
  2.8 9.7 %copy-start.1 = (bf16[2,128,512]{2,1,0:T(8,128)(2,1)S(1)}, bf16[2,128,512]{2,1,0:T(8,128)(2,1)}, u32[]{:S(2)}) copy-start(bf16[2,128,512]{2,1,0:T(8,128)(2,1)} %param.4) | copy-start | bytes 786436
  2.8 9.2 %collective-permute-start.2 = (f32[4,512]{1,0:T(4,128)S(1)}, f32[4,512]{1,0:T(4,128)S(1)}, u32[]{:S(2)}, u32[]{:S(2)}) collective-permute-start(f32[4,512]{1,0:T(4,128)S(1)} %pad_maximum_fusion.2), channel_id=1, source_target_pairs={{0,24},{8,16},{16,8},{24,0},{1,25},{9,17},{17,9},{25,1},{2,26},{10... | collective-permute-start | bytes 24584 | tf_op jit(solution)/shard_map/norm_stats/ppermute | solution.py:24
  7.9 4.5 %collective-permute-start.1 = (f32[4,512]{1,0:T(4,128)S(1)}, f32[4,512]{1,0:T(4,128)S(1)}, u32[]{:S(2)}, u32[]{:S(2)}) collective-permute-start(f32[4,512]{1,0:T(4,128)S(1)} %pad_maximum_fusion.2), channel_id=1, source_target_pairs={{0,16},{8,24},{16,0},{24,8},{1,17},{9,25},{17,1},{25,9},{2,18},{10... | collective-permute-start | bytes 24584 | tf_op jit(solution)/shard_map/norm_stats/ppermute | solution.py:24
  7.9 4.5 %collective-permute-start = (f32[4,512]{1,0:T(4,128)S(1)}, f32[4,512]{1,0:T(4,128)S(1)}, u32[]{:S(2)}, u32[]{:S(2)}) collective-permute-start(f32[4,512]{1,0:T(4,128)S(1)} %pad_maximum_fusion.2), channel_id=1, source_target_pairs={{0,8},{8,0},{16,24},{24,16},{1,9},{9,1},{17,25},{25,17},{2,10},{10... | collective-permute-start | bytes 24584 | tf_op jit(solution)/shard_map/norm_stats/ppermute | solution.py:24
  12.8 3.6 %collective-permute-start.9 = (bf16[256,512]{1,0:T(8,128)(2,1)S(1)}, bf16[256,512]{1,0:T(8,128)(2,1)S(1)}, u32[]{:S(2)}, u32[]{:S(2)}) collective-permute-start(bf16[256,512]{1,0:T(8,128)(2,1)S(1)} %bitcast.28), channel_id=1, source_target_pairs={{0,1},{1,0},{2,3},{3,2},{4,5},{5,4},{6,7},{7,6},{8,9},{9,8},{10,11... | collective-permute-start | bytes 786440 | tf_op jit(solution)/shard_map/act_gather/ppermute | solution.py:24
  12.9 9.2 %collective-permute-start.3 = (bf16[256,512]{1,0:T(8,128)(2,1)S(1)}, bf16[256,512]{1,0:T(8,128)(2,1)S(1)}, u32[]{:S(2)}, u32[]{:S(2)}) collective-permute-start(bf16[256,512]{1,0:T(8,128)(2,1)S(1)} %bitcast.29), channel_id=1, source_target_pairs={{0,2},{1,3},{2,0},{3,1},{4,6},{5,7},{6,4},{7,5},{8,10},{9,11},{10,... | collective-permute-start | bytes 786440 | tf_op jit(solution)/shard_map/act_gather/ppermute | solution.py:24
  14.4 14.0 %collective-permute-start.5 = (bf16[256,512]{1,0:T(8,128)(2,1)S(1)}, bf16[256,512]{1,0:T(8,128)(2,1)S(1)}, u32[]{:S(2)}, u32[]{:S(2)}) collective-permute-start(bf16[256,512]{1,0:T(8,128)(2,1)S(1)} %bitcast.30), channel_id=1, source_target_pairs={{0,4},{1,5},{2,6},{3,7},{4,0},{5,1},{6,2},{7,3},{8,12},{9,13},{10,... | collective-permute-start | bytes 786440 | tf_op jit(solution)/shard_map/act_gather/ppermute | solution.py:24
  16.0 12.5 %collective-permute-start.7 = (bf16[256,512]{1,0:T(8,128)(2,1)S(1)}, bf16[256,512]{1,0:T(8,128)(2,1)S(1)}, u32[]{:S(2)}, u32[]{:S(2)}) collective-permute-start(bf16[256,512]{1,0:T(8,128)(2,1)S(1)} %bitcast.31), channel_id=1, source_target_pairs={{0,6},{1,7},{2,4},{3,5},{4,2},{5,3},{6,0},{7,1},{8,14},{9,15},{10,... | collective-permute-start | bytes 786440 | tf_op jit(solution)/shard_map/act_gather/ppermute | solution.py:24
  16.5 14.0 %collective-permute-start.11 = (bf16[128,512]{1,0:T(8,128)(2,1)S(1)}, bf16[128,512]{1,0:T(8,128)(2,1)S(1)}, u32[]{:S(2)}, u32[]{:S(2)}) collective-permute-start(bf16[128,512]{1,0:T(8,128)(2,1)S(1)} %slice_bitcast_fusion.1), channel_id=1, source_target_pairs={{0,16},{16,24},{24,8},{8,0},{1,17},{17,25},{25,9},{9,1},{2,18},{18... | collective-permute-start | bytes 393224 | tf_op jit(solution)/shard_map/act_gather/ppermute | solution.py:34
  18.5 12.1 %collective-permute-start.10 = (bf16[128,512]{1,0:T(8,128)(2,1)S(1)}, bf16[128,512]{1,0:T(8,128)(2,1)S(1)}, u32[]{:S(2)}, u32[]{:S(2)}) collective-permute-start(bf16[128,512]{1,0:T(8,128)(2,1)S(1)} %slice_bitcast_fusion.1), channel_id=1, source_target_pairs={{0,8},{16,0},{24,16},{8,24},{1,9},{17,1},{25,17},{9,25},{2,10},{18... | collective-permute-start | bytes 393224 | tf_op jit(solution)/shard_map/act_gather/ppermute | solution.py:34
  22.1 8.5 %collective-permute-start.12 = (bf16[128,512]{1,0:T(8,128)(2,1)S(1)}, bf16[128,512]{1,0:T(8,128)(2,1)S(1)}, u32[]{:S(2)}, u32[]{:S(2)}) collective-permute-start(bf16[128,512]{1,0:T(8,128)(2,1)S(1)} %slice_bitcast_fusion.1), channel_id=1, source_target_pairs={{0,24},{16,8},{24,0},{8,16},{1,25},{17,9},{25,1},{9,17},{2,26},{18... | collective-permute-start | bytes 393224 | tf_op jit(solution)/shard_map/act_gather/ppermute | solution.py:34
  28.4 4.3 %collective-permute-start.4 = (bf16[256,512]{1,0:T(8,128)(2,1)S(1)}, bf16[256,512]{1,0:T(8,128)(2,1)S(1)}, u32[]{:S(2)}, u32[]{:S(2)}) collective-permute-start(bf16[256,512]{1,0:T(8,128)(2,1)S(1)} %collective-permute-done.3.refs_0_.refs_1_), channel_id=1, source_target_pairs={{0,1},{1,0},{2,3},{3,2},{4,5},{5,4},{6,7},{7,6},{8,9},{9,8},{10,11... | collective-permute-start | bytes 786440 | tf_op jit(solution)/shard_map/act_gather/ppermute | solution.py:24
  28.4 4.3 %collective-permute-start.6 = (bf16[256,512]{1,0:T(8,128)(2,1)S(1)}, bf16[256,512]{1,0:T(8,128)(2,1)S(1)}, u32[]{:S(2)}, u32[]{:S(2)}) collective-permute-start(bf16[256,512]{1,0:T(8,128)(2,1)S(1)} %collective-permute-done.5.refs_1_.refs_2_), channel_id=1, source_target_pairs={{0,1},{1,0},{2,3},{3,2},{4,5},{5,4},{6,7},{7,6},{8,9},{9,8},{10,11... | collective-permute-start | bytes 786440 | tf_op jit(solution)/shard_map/act_gather/ppermute | solution.py:24
  30.5 2.3 %collective-permute-start.8 = (bf16[256,512]{1,0:T(8,128)(2,1)S(1)}, bf16[256,512]{1,0:T(8,128)(2,1)S(1)}, u32[]{:S(2)}, u32[]{:S(2)}) collective-permute-start(bf16[256,512]{1,0:T(8,128)(2,1)S(1)} %collective-permute-done.7.refs_2_.refs_3_), channel_id=1, source_target_pairs={{0,1},{1,0},{2,3},{3,2},{4,5},{5,4},{6,7},{7,6},{8,9},{9,8},{10,11... | collective-permute-start | bytes 786440 | tf_op jit(solution)/shard_map/act_gather/ppermute | solution.py:24
  30.6 11.6 %collective-permute-start.15 = (bf16[384,512]{1,0:T(8,128)(2,1)S(1)}, bf16[384,512]{1,0:T(8,128)(2,1)S(1)}, u32[]{:S(2)}, u32[]{:S(2)}) collective-permute-start(bf16[384,512]{1,0:T(8,128)(2,1)S(1)} %constant_dynamic-update-slice_fusion.refs_0_.refs_4_), channel_id=1, source_target_pairs={{0,2},{1,3},{2,0},{3,1},{4,6},{5,7},{6,4},{7,5},{8,10},{9,11},{10,... | collective-permute-start | bytes 1179656 | tf_op jit(solution)/shard_map/z/ppermute | solution.py:24
  31.9 11.9 %collective-permute-start.17 = (bf16[384,512]{1,0:T(8,128)(2,1)S(1)}, bf16[384,512]{1,0:T(8,128)(2,1)S(1)}, u32[]{:S(2)}, u32[]{:S(2)}) collective-permute-start(bf16[384,512]{1,0:T(8,128)(2,1)S(1)} %constant_dynamic-update-slice_fusion.refs_0_.refs_4_), channel_id=1, source_target_pairs={{0,4},{1,5},{2,6},{3,7},{4,0},{5,1},{6,2},{7,3},{8,12},{9,13},{10,... | collective-permute-start | bytes 1179656 | tf_op jit(solution)/shard_map/z/ppermute | solution.py:24
  34.3 10.1 %collective-permute-start.14 = (bf16[128,1024]{1,0:T(8,128)(2,1)S(1)}, bf16[128,1024]{1,0:T(8,128)(2,1)S(1)}, u32[]{:S(2)}, u32[]{:S(2)}) collective-permute-start(bf16[128,1024]{1,0:T(8,128)(2,1)S(1)} %get-tuple-element.67.refs_1_.refs_9_), channel_id=1, source_target_pairs={{0,16},{16,24},{24,8},{8,0},{1,17},{17,25},{25,9},{9,1},{2,18},{18... | collective-permute-start | bytes 786440 | tf_op jit(solution)/shard_map/z_ring/ppermute | solution.py:34
  42.2 7.8 %collective-permute-start.20 = (bf16[192,512]{1,0:T(8,128)(2,1)S(1)}, bf16[192,512]{1,0:T(8,128)(2,1)S(1)}, u32[]{:S(2)}, u32[]{:S(2)}) collective-permute-start(bf16[192,512]{1,0:T(8,128)(2,1)S(1)} %slice.150), channel_id=1, source_target_pairs={{0,4},{1,5},{2,6},{3,7},{4,0},{5,1},{6,2},{7,3},{8,12},{9,13},{10,... | collective-permute-start | bytes 589832 | tf_op jit(solution)/shard_map/z/ppermute | solution.py:24
  43.8 6.3 %collective-permute-start.19 = (bf16[192,512]{1,0:T(8,128)(2,1)S(1)}, bf16[192,512]{1,0:T(8,128)(2,1)S(1)}, u32[]{:S(2)}, u32[]{:S(2)}) collective-permute-start(bf16[192,512]{1,0:T(8,128)(2,1)S(1)} %slice.149), channel_id=1, source_target_pairs={{0,2},{1,3},{2,0},{3,1},{4,6},{5,7},{6,4},{7,5},{8,10},{9,11},{10,... | collective-permute-start | bytes 589832 | tf_op jit(solution)/shard_map/z/ppermute | solution.py:24
  44.5 7.4 %collective-permute-start.21 = (bf16[128,1024]{1,0:T(8,128)(2,1)S(1)}, bf16[128,1024]{1,0:T(8,128)(2,1)S(1)}, u32[]{:S(2)}, u32[]{:S(2)}) collective-permute-start(bf16[128,1024]{1,0:T(8,128)(2,1)S(1)} %collective-permute-done.14.refs_3_.refs_11_), channel_id=1, source_target_pairs={{0,16},{16,24},{24,8},{8,0},{1,17},{17,25},{25,9},{9,1},{2,18},{18... | collective-permute-start | bytes 786440 | tf_op jit(solution)/shard_map/z_ring/ppermute | solution.py:34
  47.5 6.8 %collective-permute-start.13 = (bf16[384,512]{1,0:T(8,128)(2,1)S(1)}, bf16[384,512]{1,0:T(8,128)(2,1)S(1)}, u32[]{:S(2)}, u32[]{:S(2)}) collective-permute-start(bf16[384,512]{1,0:T(8,128)(2,1)S(1)} %constant_dynamic-update-slice_fusion.refs_0_.refs_4_), channel_id=1, source_target_pairs={{0,1},{1,0},{2,3},{3,2},{4,5},{5,4},{6,7},{7,6},{8,9},{9,8},{10,11... | collective-permute-start | bytes 1179656 | tf_op jit(solution)/shard_map/z_far/ppermute | solution.py:24
  47.6 6.7 %collective-permute-start.16 = (bf16[384,512]{1,0:T(8,128)(2,1)S(1)}, bf16[384,512]{1,0:T(8,128)(2,1)S(1)}, u32[]{:S(2)}, u32[]{:S(2)}) collective-permute-start(bf16[384,512]{1,0:T(8,128)(2,1)S(1)} %collective-permute-done.15.refs_1_.refs_5_), channel_id=1, source_target_pairs={{0,1},{1,0},{2,3},{3,2},{4,5},{5,4},{6,7},{7,6},{8,9},{9,8},{10,11... | collective-permute-start | bytes 1179656 | tf_op jit(solution)/shard_map/z_far/ppermute | solution.py:24
  50.0 4.3 %collective-permute-start.18 = (bf16[384,512]{1,0:T(8,128)(2,1)S(1)}, bf16[384,512]{1,0:T(8,128)(2,1)S(1)}, u32[]{:S(2)}, u32[]{:S(2)}) collective-permute-start(bf16[384,512]{1,0:T(8,128)(2,1)S(1)} %collective-permute-done.17.refs_2_.refs_6_), channel_id=1, source_target_pairs={{0,1},{1,0},{2,3},{3,2},{4,5},{5,4},{6,7},{7,6},{8,9},{9,8},{10,11... | collective-permute-start | bytes 1179656 | tf_op jit(solution)/shard_map/z_far/ppermute | solution.py:24
  51.8 2.5 %collective-permute-start.22 = (bf16[384,512]{1,0:T(8,128)(2,1)S(1)}, bf16[384,512]{1,0:T(8,128)(2,1)S(1)}, u32[]{:S(2)}, u32[]{:S(2)}) collective-permute-start(bf16[384,512]{1,0:T(8,128)(2,1)S(1)} %pad_maximum_fusion.refs_3_.refs_7_), channel_id=1, source_target_pairs={{0,1},{1,0},{2,3},{3,2},{4,5},{5,4},{6,7},{7,6},{8,9},{9,8},{10,11... | collective-permute-start | bytes 1179656 | tf_op jit(solution)/shard_map/z_far/ppermute | solution.py:24
  51.8 9.2 %collective-permute-start.23 = (bf16[128,1024]{1,0:T(8,128)(2,1)S(1)}, bf16[128,1024]{1,0:T(8,128)(2,1)S(1)}, u32[]{:S(2)}, u32[]{:S(2)}) collective-permute-start(bf16[128,1024]{1,0:T(8,128)(2,1)S(1)} %collective-permute-done.21.refs_5_.refs_13_), channel_id=1, source_target_pairs={{0,16},{16,24},{24,8},{8,0},{1,17},{17,25},{25,9},{9,1},{2,18},{18... | collective-permute-start | bytes 786440 | tf_op jit(solution)/shard_map/z_far/ppermute | solution.py:34
  63.6 1.7 %collective-permute-start.24 = (bf16[4,32,1280]{2,1,0:T(8,128)(2,1)S(1)}, bf16[4,32,1280]{2,1,0:T(8,128)(2,1)S(1)}, u32[]{:S(2)}, u32[]{:S(2)}) collective-permute-start(bf16[4,32,1280]{2,1,0:T(8,128)(2,1)S(1)} %get-tuple-element.81), channel_id=1, source_target_pairs={{0,1},{1,0},{2,3},{3,2},{4,5},{5,4},{6,7},{7,6},{8,9},{9,8},{10,11... | collective-permute-start | bytes 983048 | tf_op jit(solution)/shard_map/kernel/ppermute | solution.py:24
  65.4 5.8 %collective-permute-start.27 = (bf16[32,1280]{1,0:T(8,128)(2,1)S(1)}, bf16[32,1280]{1,0:T(8,128)(2,1)S(1)}, u32[]{:S(2)}, u32[]{:S(2)}) collective-permute-start(bf16[32,1280]{1,0:T(8,128)(2,1)S(1)} %get-tuple-element.117), channel_id=1, source_target_pairs={{0,6},{1,7},{2,4},{3,5},{4,2},{5,3},{6,0},{7,1},{8,14},{9,15},{10,... | collective-permute-start | bytes 245768 | tf_op jit(solution)/shard_map/kernel/ppermute | solution.py:24
  66.9 5.7 %collective-permute-start.26 = (bf16[32,1280]{1,0:T(8,128)(2,1)S(1)}, bf16[32,1280]{1,0:T(8,128)(2,1)S(1)}, u32[]{:S(2)}, u32[]{:S(2)}) collective-permute-start(bf16[32,1280]{1,0:T(8,128)(2,1)S(1)} %get-tuple-element.118), channel_id=1, source_target_pairs={{0,4},{1,5},{2,6},{3,7},{4,0},{5,1},{6,2},{7,3},{8,12},{9,13},{10,... | collective-permute-start | bytes 245768 | tf_op jit(solution)/shard_map/kernel/ppermute | solution.py:24
  68.5 4.4 %collective-permute-start.25 = (bf16[32,1280]{1,0:T(8,128)(2,1)S(1)}, bf16[32,1280]{1,0:T(8,128)(2,1)S(1)}, u32[]{:S(2)}, u32[]{:S(2)}) collective-permute-start(bf16[32,1280]{1,0:T(8,128)(2,1)S(1)} %get-tuple-element.116), channel_id=1, source_target_pairs={{0,2},{1,3},{2,0},{3,1},{4,6},{5,7},{6,4},{7,5},{8,10},{9,11},{10,... | collective-permute-start | bytes 245768 | tf_op jit(solution)/shard_map/kernel/ppermute | solution.py:24
  72.9 4.5 %collective-permute-start.29 = (bf16[32,1280]{1,0:T(8,128)(2,1)S(1)}, bf16[32,1280]{1,0:T(8,128)(2,1)S(1)}, u32[]{:S(2)}, u32[]{:S(2)}) collective-permute-start(bf16[32,1280]{1,0:T(8,128)(2,1)S(1)} %get-tuple-element.110.refs_0_), channel_id=1, source_target_pairs={{0,2},{1,3},{2,0},{3,1},{4,6},{5,7},{6,4},{7,5},{8,10},{9,11},{10,... | collective-permute-start | bytes 245768 | tf_op jit(solution)/shard_map/kernel/ppermute | solution.py:24
  74.1 6.2 %collective-permute-start.31 = (bf16[32,1280]{1,0:T(8,128)(2,1)S(1)}, bf16[32,1280]{1,0:T(8,128)(2,1)S(1)}, u32[]{:S(2)}, u32[]{:S(2)}) collective-permute-start(bf16[32,1280]{1,0:T(8,128)(2,1)S(1)} %get-tuple-element.110.refs_0_), channel_id=1, source_target_pairs={{0,4},{1,5},{2,6},{3,7},{4,0},{5,1},{6,2},{7,3},{8,12},{9,13},{10,... | collective-permute-start | bytes 245768 | tf_op jit(solution)/shard_map/kernel/ppermute | solution.py:24
  74.9 5.5 %collective-permute-start.33 = (bf16[32,1280]{1,0:T(8,128)(2,1)S(1)}, bf16[32,1280]{1,0:T(8,128)(2,1)S(1)}, u32[]{:S(2)}, u32[]{:S(2)}) collective-permute-start(bf16[32,1280]{1,0:T(8,128)(2,1)S(1)} %get-tuple-element.110.refs_0_), channel_id=1, source_target_pairs={{0,6},{1,7},{2,4},{3,5},{4,2},{5,3},{6,0},{7,1},{8,14},{9,15},{10,... | collective-permute-start | bytes 245768 | tf_op jit(solution)/shard_map/kernel/ppermute | solution.py:24
  76.5 4.4 %collective-permute-start.28 = (bf16[32,1280]{1,0:T(8,128)(2,1)S(1)}, bf16[32,1280]{1,0:T(8,128)(2,1)S(1)}, u32[]{:S(2)}, u32[]{:S(2)}) collective-permute-start(bf16[32,1280]{1,0:T(8,128)(2,1)S(1)} %get-tuple-element.110.refs_0_), channel_id=1, source_target_pairs={{0,1},{1,0},{2,3},{3,2},{4,5},{5,4},{6,7},{7,6},{8,9},{9,8},{10,11... | collective-permute-start | bytes 245768 | tf_op jit(solution)/shard_map/kernel/ppermute | solution.py:24
  77.5 3.4 %collective-permute-start.30 = (bf16[32,1280]{1,0:T(8,128)(2,1)S(1)}, bf16[32,1280]{1,0:T(8,128)(2,1)S(1)}, u32[]{:S(2)}, u32[]{:S(2)}) collective-permute-start(bf16[32,1280]{1,0:T(8,128)(2,1)S(1)} %collective-permute-done.29.refs_2_), channel_id=1, source_target_pairs={{0,1},{1,0},{2,3},{3,2},{4,5},{5,4},{6,7},{7,6},{8,9},{9,8},{10,11... | collective-permute-start | bytes 245768 | tf_op jit(solution)/shard_map/kernel/ppermute | solution.py:24
  80.3 1.3 %collective-permute-start.32 = (bf16[32,1280]{1,0:T(8,128)(2,1)S(1)}, bf16[32,1280]{1,0:T(8,128)(2,1)S(1)}, u32[]{:S(2)}, u32[]{:S(2)}) collective-permute-start(bf16[32,1280]{1,0:T(8,128)(2,1)S(1)} %collective-permute-done.31.refs_4_), channel_id=1, source_target_pairs={{0,1},{1,0},{2,3},{3,2},{4,5},{5,4},{6,7},{7,6},{8,9},{9,8},{10,11... | collective-permute-start | bytes 245768 | tf_op jit(solution)/shard_map/kernel/ppermute | solution.py:24
  80.3 1.4 %collective-permute-start.34 = (bf16[32,1280]{1,0:T(8,128)(2,1)S(1)}, bf16[32,1280]{1,0:T(8,128)(2,1)S(1)}, u32[]{:S(2)}, u32[]{:S(2)}) collective-permute-start(bf16[32,1280]{1,0:T(8,128)(2,1)S(1)} %collective-permute-done.33.refs_6_), channel_id=1, source_target_pairs={{0,1},{1,0},{2,3},{3,2},{4,5},{5,4},{6,7},{7,6},{8,9},{9,8},{10,11... | collective-permute-start | bytes 245768 | tf_op jit(solution)/shard_map/kernel/ppermute | solution.py:24
  88.3 2.8 %collective-permute-start.35 = (bf16[4,272,512]{2,1,0:T(8,128)(2,1)S(1)}, bf16[4,272,512]{2,1,0:T(8,128)(2,1)S(1)}, u32[]{:S(2)}, u32[]{:S(2)}) collective-permute-start(bf16[4,272,512]{2,1,0:T(8,128)(2,1)S(1)} %d_act_matmul.2), channel_id=1, source_target_pairs={{0,1},{1,0},{2,3},{3,2},{4,5},{5,4},{6,7},{7,6},{8,9},{9,8},{10,11... | collective-permute-start | bytes 3342344 | tf_op jit(solution)/shard_map/d_act/ppermute | solution.py:24
  93.0 19.0 %collective-permute-start.36 = (bf16[272,512]{1,0:T(8,128)(2,1)S(1)}, bf16[272,512]{1,0:T(8,128)(2,1)S(1)}, u32[]{:S(2)}, u32[]{:S(2)}) collective-permute-start(bf16[272,512]{1,0:T(8,128)(2,1)S(1)} %get-tuple-element.89), channel_id=1, source_target_pairs={{0,2},{1,3},{2,0},{3,1},{4,6},{5,7},{6,4},{7,5},{8,10},{9,11},{10,... | collective-permute-start | bytes 835592 | tf_op jit(solution)/shard_map/d_act/ppermute | solution.py:24
  93.8 18.2 %collective-permute-start.37 = (bf16[272,512]{1,0:T(8,128)(2,1)S(1)}, bf16[272,512]{1,0:T(8,128)(2,1)S(1)}, u32[]{:S(2)}, u32[]{:S(2)}) collective-permute-start(bf16[272,512]{1,0:T(8,128)(2,1)S(1)} %get-tuple-element.90), channel_id=1, source_target_pairs={{0,4},{1,5},{2,6},{3,7},{4,0},{5,1},{6,2},{7,3},{8,12},{9,13},{10,... | collective-permute-start | bytes 835592 | tf_op jit(solution)/shard_map/d_act/ppermute | solution.py:24
  94.9 17.0 %collective-permute-start.38 = (bf16[272,512]{1,0:T(8,128)(2,1)S(1)}, bf16[272,512]{1,0:T(8,128)(2,1)S(1)}, u32[]{:S(2)}, u32[]{:S(2)}) collective-permute-start(bf16[272,512]{1,0:T(8,128)(2,1)S(1)} %get-tuple-element.91), channel_id=1, source_target_pairs={{0,6},{1,7},{2,4},{3,5},{4,2},{5,3},{6,0},{7,1},{8,14},{9,15},{10,... | collective-permute-start | bytes 835592 | tf_op jit(solution)/shard_map/d_act/ppermute | solution.py:24
  96.5 6.8 %collective-permute-start.39 = (bf16[128,512]{1,0:T(8,128)(2,1)S(1)}, bf16[128,512]{1,0:T(8,128)(2,1)S(1)}, u32[]{:S(2)}, u32[]{:S(2)}) collective-permute-start(bf16[128,512]{1,0:T(8,128)(2,1)S(1)} %get-tuple-element.92), channel_id=1, source_target_pairs={{0,16},{16,24},{24,8},{8,0},{1,17},{17,25},{25,9},{9,1},{2,18},{18... | collective-permute-start | bytes 393224 | tf_op jit(solution)/shard_map/grad_weight/ppermute | solution.py:34
  99.6 9.4 %collective-permute-start.40 = (bf16[128,512]{1,0:T(8,128)(2,1)S(1)}, bf16[128,512]{1,0:T(8,128)(2,1)S(1)}, u32[]{:S(2)}, u32[]{:S(2)}) collective-permute-start(bf16[128,512]{1,0:T(8,128)(2,1)S(1)} %get-tuple-element.93), channel_id=1, source_target_pairs={{0,24},{16,8},{24,0},{8,16},{1,25},{17,9},{25,1},{9,17},{2,26},{18... | collective-permute-start | bytes 393224 | tf_op jit(solution)/shard_map/grad_weight/ppermute | solution.py:34
  103.3 8.6 %collective-permute-start.41 = (bf16[128,512]{1,0:T(8,128)(2,1)S(1)}, bf16[128,512]{1,0:T(8,128)(2,1)S(1)}, u32[]{:S(2)}, u32[]{:S(2)}) collective-permute-start(bf16[128,512]{1,0:T(8,128)(2,1)S(1)} %get-tuple-element.94), channel_id=1, source_target_pairs={{0,8},{16,0},{24,16},{8,24},{1,9},{17,1},{25,17},{9,25},{2,10},{18... | collective-permute-start | bytes 393224 | tf_op jit(solution)/shard_map/grad_weight/ppermute | solution.py:34
  112.0 9.8 %collective-permute-start.45 = (bf16[384,512]{1,0:T(8,128)(2,1)S(1)}, bf16[384,512]{1,0:T(8,128)(2,1)S(1)}, u32[]{:S(2)}, u32[]{:S(2)}) collective-permute-start(bf16[384,512]{1,0:T(8,128)(2,1)S(1)} %constant_dynamic-update-slice_fusion.3.refs_4_), channel_id=1, source_target_pairs={{0,1},{1,0},{2,3},{3,2},{4,5},{5,4},{6,7},{7,6},{8,9},{9,8},{10,11... | collective-permute-start | bytes 1179656 | tf_op jit(solution)/shard_map/grad_weight/ppermute | solution.py:24
  112.8 6.8 %collective-permute-start.42 = (f32[8,512]{1,0:T(8,128)S(1)}, f32[8,512]{1,0:T(8,128)S(1)}, u32[]{:S(2)}, u32[]{:S(2)}) collective-permute-start(f32[8,512]{1,0:T(8,128)S(1)} %pad_maximum_fusion.1.refs_0_), channel_id=1, source_target_pairs={{0,8},{8,0},{16,24},{24,16},{1,9},{9,1},{17,25},{25,17},{2,10},{10... | collective-permute-start | bytes 49160 | tf_op jit(solution)/shard_map/norm_backward/ppermute | solution.py:24
  112.8 6.8 %collective-permute-start.43 = (f32[8,512]{1,0:T(8,128)S(1)}, f32[8,512]{1,0:T(8,128)S(1)}, u32[]{:S(2)}, u32[]{:S(2)}) collective-permute-start(f32[8,512]{1,0:T(8,128)S(1)} %pad_maximum_fusion.1.refs_0_), channel_id=1, source_target_pairs={{0,16},{8,24},{16,0},{24,8},{1,17},{9,25},{17,1},{25,9},{2,18},{10... | collective-permute-start | bytes 49160 | tf_op jit(solution)/shard_map/norm_backward/ppermute | solution.py:24
  115.4 5.5 %collective-permute-start.44 = (f32[8,512]{1,0:T(8,128)S(1)}, f32[8,512]{1,0:T(8,128)S(1)}, u32[]{:S(2)}, u32[]{:S(2)}) collective-permute-start(f32[8,512]{1,0:T(8,128)S(1)} %pad_maximum_fusion.1.refs_0_), channel_id=1, source_target_pairs={{0,24},{8,16},{16,8},{24,0},{1,25},{9,17},{17,9},{25,1},{2,26},{10... | collective-permute-start | bytes 49160 | tf_op jit(solution)/shard_map/norm_backward/ppermute | solution.py:24
  (1 other events, 9.7 us)

commit v14 on v11

--- a/solution.py
+++ b/solution.py
@@ -371,13 +371,12 @@
     )(place, *pieces)
 
 
-def weight_grad_kernel(n_far, aliased, half, tile, which, place_ref, *refs):
+def weight_grad_kernel(n_batch, aliased, half, tile, which, place_ref, *refs):
     near = [refs[:half], refs[half : 2 * half]]
-    arrived = refs[2 * half : 2 * half + n_far]
-    dz_ref = refs[2 * half + n_far]
-    out_ref, act, product, sems = refs[2 * half + n_far + 1 + aliased :]
+    blocks_ref, dz_ref = refs[2 * half : 2 * half + 2]
+    out_ref, act, product, sems = refs[2 * half + 2 + aliased :]
     block, parity = which
-    chosen = held_place(place_ref[0], place_ref[1], block, 2 * half, n_far + 1)
+    chosen = held_place(place_ref[0], place_ref[1], block, 2 * half, n_batch)
     out_row = 2 * block + ((place_ref[1] & 1) ^ parity)
     local_rows = near[0][0].shape[0] // 2
     rows = dz_ref.shape[1]
@@ -389,8 +388,7 @@
             act[pl.ds(rows, local_rows)] = near[0][e][local_rows:]
             act[pl.ds(local_rows, rows - local_rows)] = near[1][e][...]
 
-    for s in range(n_far):
-        act[pl.ds(rows + (s + 1) * local_rows, local_rows)] = arrived[s][...]
+    act[rows + local_rows :] = blocks_ref[...]
     width = act.shape[1]
     copies = []
     for i in range(width // tile):
@@ -415,12 +413,12 @@
         copy.wait()
 
 
-def weight_grad_call(place, which, near, arrived, dz, features, before):
+def weight_grad_call(place, which, near, blocks, dz, features, before):
     half = len(near[0])
     width = near[0][0].shape[1]
     _, rows, columns = dz.shape
     tile = min(256, width)
-    operands = [place] + [x for group in near for x in group] + list(arrived) + [dz]
+    operands = [place] + [x for group in near for x in group] + [blocks, dz]
     specs = [IN_SMEM] + [IN_VMEM] * (len(operands) - 1)
     aliases = {}
     if before is not None:
@@ -429,7 +427,12 @@
         specs.append(ANYWHERE)
     return pl.pallas_call(
         functools.partial(
-            weight_grad_kernel, len(arrived), int(before is not None), half, tile, which
+            weight_grad_kernel,
+            rows // (near[0][0].shape[0] // 2),
+            int(before is not None),
+            half,
+            tile,
+            which,
         ),
         out_shape=jax.ShapeDtypeStruct((features, columns), f32),
         in_specs=specs,
@@ -446,14 +449,17 @@
     )(*operands)
 
 
-def gather_pieces(x, n_col):
-    return sibling_pieces(link_pieces(x, n_col), n_col)
-
-
 def link_pieces(x, n_col):
     pieces = {0: x}
-    for k in range(2, n_col, 2):
-        pieces[k] = xor_send(x, "col", k)
+    half = x.shape[0] // 2
+    for k in sorted(range(2, n_col, 2), key=lambda k: (bin(k).count("1"), k)):
+        low, high = k & -k, 1 << (k.bit_length() - 1)
+        if low == high:
+            pieces[k] = xor_send(x, "col", k)
+        else:
+            first = xor_send(pieces[k ^ low][:half], "col", low)
+            second = xor_send(pieces[k ^ high][half:], "col", high)
+            pieces[k] = jnp.concatenate([first, second])
     return pieces
 
 
@@ -534,60 +540,58 @@
         preactivation = norm_scale_gain * normalised + norm_shift_bias
         act = jax.nn.gelu(preactivation, approximate=True).astype(bf16)
     with jax.named_scope("act_gather"):
-        others = [ring_send(act[0], "batch", d) for d in range(1, n_batch)]
         own = act.reshape(tall, width)
-        sibling = xor_send(own, "col", 1)
-        own, sibling = lax.optimization_barrier((own, sibling))
-        pieces = link_pieces(own, n_col)
-        pieces[1] = sibling
-        others, pieces[far[0]] = lax.optimization_barrier((others, pieces[far[0]]))
+        pieces = {0: own, 1: xor_send(own, "col", 1)}
+        for k in far:
+            pieces[k] = xor_send(own, "col", k)
+        first, pieces[1] = lax.optimization_barrier((act[0], pieces[1]))
+        others = [ring_send(first, "batch", d) for d in range(1, n_batch)]
         pieces = sibling_pieces(pieces, n_col)
+    with jax.named_scope("z"):
+
+        def z_part(source, ks, before, last=False):
+            return z_call(
+                place, ks, [source[k] for k in ks], held_weight, before, last, local_rows
+            )
+
+        z_own = z_part(pieces, far, z_part(pieces, [0, 1], None))
+        z_own, others[-1] = lax.optimization_barrier((z_own, others[-1]))
+        z_own0, z_own1 = z_part(pieces, [k + 1 for k in far], z_own, True)
         far_pieces = link_pieces(jnp.concatenate(others), n_col)
-    with jax.named_scope("z"):
-
-        def z_of(source, groups, total=None):
-            for i, ks in enumerate(groups):
-                total = z_call(
-                    place,
-                    ks,
-                    [source[k] for k in ks],
-                    held_weight,
-                    total,
-                    i == len(groups) - 1,
-                    local_rows,
-                )
-            return total
-
-        z_own0, z_own1 = z_of(pieces, [[0, 1], far, [k + 1 for k in far]])
     with jax.named_scope("z_ring"):
         z_ring = [z_own1, ring_send(z_own1, "batch", 1)]
-        z_ring[1], far_pieces[far[-1]] = lax.optimization_barrier((z_ring[1], far_pieces[far[-1]]))
+        z_ring[1], far_pieces[far[0]] = lax.optimization_barrier((z_ring[1], far_pieces[far[0]]))
         z_ring.append(ring_send(z_ring[1], "batch", 1))
     with jax.named_scope("z_far"):
-        start = z_call(
-            place, [0, far[-1]], [far_pieces[0], far_pieces[far[-1]]], held_weight, None, False, local_rows
-        )
-        start, far_pieces[far[0]], z_ring[2] = lax.optimization_barrier(
-            (start, far_pieces[far[0]], z_ring[2])
+        start = z_part(far_pieces, [0] + far[:-1], None)
+        picked = list(pick_call(place, [pieces[k] for k in evens], n_batch, n_col))
+        start, far_pieces[far[-1]], z_ring[2], picked = lax.optimization_barrier(
+            (start, far_pieces[far[-1]], z_ring[2], picked)
         )
         far_pieces = sibling_pieces(far_pieces, n_col)
         for _ in range(3, n_batch):
             z_ring.append(ring_send(z_ring[-1], "batch", 1))
-        z_far = z_of(far_pieces, [far[:-1], odds], start)
+        z_far = z_part(far_pieces, odds[:-1] + far[-1:] + odds[-1:], start, True)
         slots = list(zip([z_own0] + list(z_far), z_ring))
     with jax.named_scope("kernel"):
         even_part, odd_part = strip_call(place, slots, n_col)
+        blocks = [
+            ring_send(x, "batch", 1 + i % (n_batch - 1)) for i, x in enumerate(picked)
+        ]
+        third = len(blocks) // 3
+        odd_part, blocks[:third] = lax.optimization_barrier((odd_part, blocks[:third]))
         even_part = even_part + xor_send(odd_part, "col", 1).astype(f32)
-        even_part, held_back = lax.optimization_barrier((even_part, [pieces[k] for k in evens]))
         strip = even_part[0]
         for k in far:
             strip = strip + xor_send(even_part[k // 2].astype(bf16), "col", k).astype(f32)
-        picked = pick_call(place, held_back, n_batch, n_col)
-        blocks = [
-            ring_send(x, "batch", 1 + i % (n_batch - 1)) for i, x in enumerate(picked)
-        ]
-        strips = gather_pieces(strip.astype(bf16), n_col)
-        strips, blocks[:-1] = lax.optimization_barrier((strips, blocks[:-1]))
+        strip_b = strip.astype(bf16)
+        strips = {0: strip_b}
+        for k in far:
+            strips[k] = xor_send(strip_b, "col", k)
+        strips[far[0]], blocks[third : 2 * third] = lax.optimization_barrier(
+            (strips[far[0]], blocks[third : 2 * third])
+        )
+        strips = sibling_pieces(strips, n_col)
     with jax.named_scope("dz"):
         constants = (
             4.0 * scale / denom,
@@ -599,7 +603,7 @@
             1.0 / denom / n_batch,
         )
         dz, share = dz_call(place, strip, [strips[k] for k in range(n_col)], slots, constants)
-        dz, blocks[-1] = lax.optimization_barrier((dz, blocks[-1]))
+        dz, blocks[2 * third :] = lax.optimization_barrier((dz, blocks[2 * third :]))
     with jax.named_scope("d_act"):
         (away,) = d_act_call(place, dz, share, held_weight, n_batch, n_col, None)
         got = xor_send(away, "col", 1)
@@ -608,8 +612,8 @@
     with jax.named_scope("grad_weight"):
         grad_weight = None
         for block in range(n_col // n_batch // 2):
-            mine = blocks[block * (n_batch - 1) : (block + 1) * (n_batch - 1)]
-            other = [xor_send(x, "col", 1) for x in mine]
+            mine = jnp.concatenate(blocks[block * (n_batch - 1) : (block + 1) * (n_batch - 1)])
+            other = xor_send(mine, "col", 1)
             for parity, ks, far_rows in ((0, evens, mine), (1, odds, other)):
                 grad_weight = weight_grad_call(
                     place,
@@ -621,6 +625,7 @@
                     grad_weight,
                 )
     with jax.named_scope("norm_backward"):
+        arrived, grad_weight = lax.optimization_barrier((arrived, grad_weight))
         share = exchange_sum(share_of(part[tall:]) for part in [d_act] + arrived)
         d_act = d_act[:tall]
         for part in arrived:

time: 125 us -> 120 us (0.960)
  waiting for transfers between devices: 41.6 us -> 39.2 us
  starting transfers between devices: 47.5 us -> 45.3 us
    ppermute x9, starting transfers between devices: 17.9 us -> 12.1 us  [ring_send(): lax.ppermute(x, axis, [(order[i], order[(i + d) % n]) for i in range(n)])]
    ppermute x9, waiting for transfers between devices: 12 us -> 7.43 us  [ring_send(): lax.ppermute(x, axis, [(order[i], order[(i + d) % n]) for i in range(n)])]
    ppermute x38 -> x37, starting transfers between devices: 29.6 us -> 33.3 us  [xor_send(): return lax.ppermute(x, axis, [(i, i ^ k) for i in range(n)])]
    ppermute x38 -> x37, waiting for transfers between devices: 29.6 us -> 31.8 us  [xor_send(): return lax.ppermute(x, axis, [(i, i ^ k) for i in range(n)])]
    pallas_call x6 -> x5, Pallas kernels: 9.68 us -> 8.96 us  [z_call(): pl.pallas_call(functools.partial(z_kernel, tuple(ks), before is None, las...]
  transfers between devices with their start and end apart: 47 -> 46, of which waited for: 20 -> 20; matrix products, arithmetic and copies ran while one was open for 1% -> 0% of each run, Pallas kernels for 19% -> 23%
where the time goes in v14:
time: 120 us
  starting transfers between devices  45.3 us (38%)
  waiting for transfers between devices  39.2 us (33%)
  Pallas kernels  30.7 us (26%)
  other arithmetic  3.22 us (3%)
    ppermute x37, starting transfers between devices, xor_send(): return lax.ppermute(x, axis, [(i, i ^ k) for i in range(n)])  33.3 us
    ppermute x37, waiting for transfers between devices, xor_send(): return lax.ppermute(x, axis, [(i, i ^ k) for i in range(n)])  31.8 us
    ppermute x9, starting transfers between devices, ring_send(): lax.ppermute(x, axis, [(order[i], order[(i + d) % n]) for i in range(n)])  12.1 us
    pallas_call x5, Pallas kernels, z_call(): pl.pallas_call(functools.partial(z_kernel, tuple(ks), before is None, las...  8.96 us
    ppermute x9, waiting for transfers between devices, ring_send(): lax.ppermute(x, axis, [(order[i], order[(i + d) % n]) for i in range(n)])  7.43 us
    pallas_call x2, Pallas kernels, weight_grad_call(): pl.pallas_call(functools.partial(weight_grad_kernel, rows // (near[0][0]....  5.79 us
    pallas_call x1, Pallas kernels, dz_call(): pl.pallas_call(functools.partial(dz_kernel, n_batch, n_col, tile, constan...  4.68 us
    pallas_call x2, Pallas kernels, d_act_call(): pl.pallas_call(functools.partial(d_act_kernel, count, (got is not None, n...  3.68 us
  transfers between devices with their start and end apart: 46, of which 20 were waited for; matrix products, arithmetic and copies ran while one was open for 0% of the time, Pallas kernels for 23%

profile of v14, /device:TPU:0, one launch (start us, length us, event | category | flops | bytes accessed | tf_op | source)
XLA Modules:
  0.0 119.7 jit_solution(11278683689696201232)
XLA Ops:
  0.7 1.0 convert_reduce_fusion
  1.7 1.0 fusion.8
  2.8 5.1 %collective-permute-start.2 = (f32[4,512]{1,0:T(4,128)S(1)}, f32[4,512]{1,0:T(4,128)S(1)}, u32[]{:S(2)}, u32[]{:S(2)}) collective-permute-start(f32[4,512]{1,0:T(4,128)S(1)} %pad_maximum_fusion.2), channel_id=1, source_target_pairs={{0,24},{8,16},{16,8},{24,0},{1,25},{9,17},{17,9},{25,1},{2,26},{10... | collective-permute-start | bytes 24584 | tf_op jit(solution)/shard_map/norm_stats/ppermute | solution.py:24
  8.6 3.5 %weight_load.1 = (bf16[4096,1024]{1,0:T(8,128)(2,1)S(1)}, f32[4,512]{1,0:T(4,128)S(1)}) custom-call(bf16[4096,1024]{1,0:T(8,128)(2,1)} %w_ref), custom_call_target="tpu_custom_call" | custom-call | bytes 16777216 | tf_op jit(solution)/shard_map/weight_load/weight_load/pallas_call | solution.py:78
  12.9 2.5 %collective-permute-start.7 = (bf16[256,512]{1,0:T(8,128)(2,1)S(1)}, bf16[256,512]{1,0:T(8,128)(2,1)S(1)}, u32[]{:S(2)}, u32[]{:S(2)}) collective-permute-start(bf16[256,512]{1,0:T(8,128)(2,1)S(1)} %bitcast.29), channel_id=1, source_target_pairs={{0,6},{1,7},{2,4},{3,5},{4,2},{5,3},{6,0},{7,1},{8,14},{9,15},{10,... | collective-permute-start | bytes 786440 | tf_op jit(solution)/shard_map/act_gather/ppermute | solution.py:24
  16.5 2.1 %collective-permute-start.11 = (bf16[128,512]{1,0:T(8,128)(2,1)S(1)}, bf16[128,512]{1,0:T(8,128)(2,1)S(1)}, u32[]{:S(2)}, u32[]{:S(2)}) collective-permute-start(bf16[128,512]{1,0:T(8,128)(2,1)S(1)} %slice_bitcast_fusion.1), channel_id=1, source_target_pairs={{0,16},{16,24},{24,8},{8,0},{1,17},{17,25},{25,9},{9,1},{2,18},{18... | collective-permute-start | bytes 393224 | tf_op jit(solution)/shard_map/act_gather/ppermute | solution.py:34
  18.5 1.4 %collective-permute-start.12 = (bf16[128,512]{1,0:T(8,128)(2,1)S(1)}, bf16[128,512]{1,0:T(8,128)(2,1)S(1)}, u32[]{:S(2)}, u32[]{:S(2)}) collective-permute-start(bf16[128,512]{1,0:T(8,128)(2,1)S(1)} %slice_bitcast_fusion.1), channel_id=1, source_target_pairs={{0,24},{16,8},{24,0},{8,16},{1,25},{17,9},{25,1},{9,17},{2,26},{18... | collective-permute-start | bytes 393224 | tf_op jit(solution)/shard_map/act_gather/ppermute | solution.py:34
  20.0 1.2 %z_matmul.5.refs_4_ = f32[256,1024]{1,0:T(8,128)S(1)} custom-call(s32[2]{0:T(128)S(1)} %pad_add_fusion.place_ref, bf16[256,512]{1,0:T(8,128)(2,1)S(1)} %bitcast.32, bf16[256,512]{1,0:T(8,128)(2,1)S(1)} %collective-permute-done.9.refs_1_.refs_0_, bf16[4096,1024]{1,0:T(8,128)(2,1)S(1)} %get-tuple-element.60.refs_2_.refs_3_.refs_5_.w_ref), custom_call_target="tpu_custom_call" | custom-call | flops 536870912 | bytes 524288 | tf_op jit(solution)/shard_map/z/z_matmul/pallas_call | solution.py:126
  21.2 1.8 %collective-permute-done.7.refs_2_.refs_3_ = bf16[256,512]{1,0:T(8,128)(2,1)S(1)} collective-permute-done((bf16[256,512]{1,0:T(8,128)(2,1)S(1)}, bf16[256,512]{1,0:T(8,128)(2,1)S(1)}, u32[]{:S(2)}, u32[]{:S(2)}) %collective-permute-start.7) | collective-permute-done | bytes 262176 | tf_op jit(solution)/shard_map/act_gather/ppermute | solution.py:24
  23.0 1.0 collective-permute-start.10
  24.0 4.1 %collective-permute-done.5.refs_1_.refs_2_ = bf16[256,512]{1,0:T(8,128)(2,1)S(1)} collective-permute-done((bf16[256,512]{1,0:T(8,128)(2,1)S(1)}, bf16[256,512]{1,0:T(8,128)(2,1)S(1)}, u32[]{:S(2)}, u32[]{:S(2)}) %collective-permute-start.5) | collective-permute-done | bytes 262176 | tf_op jit(solution)/shard_map/act_gather/ppermute | solution.py:24
  28.6 1.5 %z_matmul.6.refs_4_ = f32[256,1024]{1,0:T(8,128)S(1)} custom-call(s32[2]{0:T(128)S(1)} %pad_add_fusion.place_ref, bf16[256,512]{1,0:T(8,128)(2,1)S(1)} %collective-permute-done.3.refs_0_.refs_1_, bf16[256,512]{1,0:T(8,128)(2,1)S(1)} %collective-permute-done.5.refs_1_.refs_2_, bf16[256,512]{1,0:T(8,128)(2,1)S(1)} %collective-permute-done.7.refs_2_.refs_3_, ...), custom_call_target="tpu_custom_call" | custom-call | flops 805306368 | bytes 524288 | tf_op jit(solution)/shard_map/z/z_matmul/pallas_call | solution.py:126
  30.4 1.2 collective-permute-done.10
  31.6 1.6 %collective-permute-start.17 = (bf16[384,512]{1,0:T(8,128)(2,1)S(1)}, bf16[384,512]{1,0:T(8,128)(2,1)S(1)}, u32[]{:S(2)}, u32[]{:S(2)}) collective-permute-start(bf16[384,512]{1,0:T(8,128)(2,1)S(1)} %constant_dynamic-update-slice_fusion.refs_0_.refs_4_), channel_id=1, source_target_pairs={{0,4},{1,5},{2,6},{3,7},{4,0},{5,1},{6,2},{7,3},{8,12},{9,13},{10,... | collective-permute-start | bytes 1179656 | tf_op jit(solution)/shard_map/z/ppermute | solution.py:24
  33.2 1.5 %collective-permute-start.15 = (bf16[384,512]{1,0:T(8,128)(2,1)S(1)}, bf16[384,512]{1,0:T(8,128)(2,1)S(1)}, u32[]{:S(2)}, u32[]{:S(2)}) collective-permute-start(bf16[384,512]{1,0:T(8,128)(2,1)S(1)} %constant_dynamic-update-slice_fusion.refs_0_.refs_4_), channel_id=1, source_target_pairs={{0,2},{1,3},{2,0},{3,1},{4,6},{5,7},{6,4},{7,5},{8,10},{9,11},{10,... | collective-permute-start | bytes 1179656 | tf_op jit(solution)/shard_map/z/ppermute | solution.py:24
  34.7 1.5 %z_matmul.7 = (bf16[128,1024]{1,0:T(8,128)(2,1)S(1)}, bf16[128,1024]{1,0:T(8,128)(2,1)S(1)}) custom-call(s32[2]{0:T(128)S(1)} %pad_add_fusion.place_ref, bf16[256,512]{1,0:T(8,128)(2,1)S(1)} %collective-permute-done.4.refs_0_.refs_1_, bf16[256,512]{1,0:T(8,128)(2,1)S(1)} %collective-permute-done.6.refs_1_.refs_2_, ...), custom_call_target="tpu_custom_call" | custom-call | flops 805306368 | bytes 524288 | tf_op jit(solution)/shard_map/z/z_matmul/pallas_call | solution.py:126
  36.3 6.4 %collective-permute-done.17.refs_2_.refs_6_ = bf16[384,512]{1,0:T(8,128)(2,1)S(1)} collective-permute-done((bf16[384,512]{1,0:T(8,128)(2,1)S(1)}, bf16[384,512]{1,0:T(8,128)(2,1)S(1)}, u32[]{:S(2)}, u32[]{:S(2)}) %collective-permute-start.17) | collective-permute-done | bytes 393248 | tf_op jit(solution)/shard_map/z/ppermute | solution.py:24
  42.7 1.6 %collective-permute-start.19 = (bf16[192,512]{1,0:T(8,128)(2,1)S(1)}, bf16[192,512]{1,0:T(8,128)(2,1)S(1)}, u32[]{:S(2)}, u32[]{:S(2)}) collective-permute-start(bf16[192,512]{1,0:T(8,128)(2,1)S(1)} %slice.149), channel_id=1, source_target_pairs={{0,2},{1,3},{2,0},{3,1},{4,6},{5,7},{6,4},{7,5},{8,10},{9,11},{10,... | collective-permute-start | bytes 589832 | tf_op jit(solution)/shard_map/z/ppermute | solution.py:24
  44.3 1.6 %collective-permute-start.20 = (bf16[192,512]{1,0:T(8,128)(2,1)S(1)}, bf16[192,512]{1,0:T(8,128)(2,1)S(1)}, u32[]{:S(2)}, u32[]{:S(2)}) collective-permute-start(bf16[192,512]{1,0:T(8,128)(2,1)S(1)} %slice.150), channel_id=1, source_target_pairs={{0,4},{1,5},{2,6},{3,7},{4,0},{5,1},{6,2},{7,3},{8,12},{9,13},{10,... | collective-permute-start | bytes 589832 | tf_op jit(solution)/shard_map/z/ppermute | solution.py:24
  47.6 1.9 %z_matmul.8.refs_6_ = f32[384,1024]{1,0:T(8,128)S(1)} custom-call(s32[2]{0:T(128)S(1)} %pad_add_fusion.place_ref, bf16[384,512]{1,0:T(8,128)(2,1)S(1)} %constant_dynamic-update-slice_fusion.refs_0_.refs_4_, bf16[384,512]{1,0:T(8,128)(2,1)S(1)} %collective-permute-done.15.refs_1_.refs_5_, bf16[384,512]{1,0:T(8,128)(2,1)S(1)} %collective-permute-done.17.refs_2_.refs_6_, ...), custom_call_target="tpu_custom_call" | custom-call | flops 1207959552 | bytes 786432 | tf_op jit(solution)/shard_map/z_far/z_matmul/pallas_call | solution.py:126
  50.1 2.6 %collective-permute-done.21.refs_5_.refs_13_ = bf16[128,1024]{1,0:T(8,128)(2,1)S(1)} collective-permute-done((bf16[128,1024]{1,0:T(8,128)(2,1)S(1)}, bf16[128,1024]{1,0:T(8,128)(2,1)S(1)}, u32[]{:S(2)}, u32[]{:S(2)}) %collective-permute-start.21) | collective-permute-done | bytes 262176 | tf_op jit(solution)/shard_map/z_ring/ppermute | solution.py:34
  52.7 2.0 %collective-permute-start.23 = (bf16[128,1024]{1,0:T(8,128)(2,1)S(1)}, bf16[128,1024]{1,0:T(8,128)(2,1)S(1)}, u32[]{:S(2)}, u32[]{:S(2)}) collective-permute-start(bf16[128,1024]{1,0:T(8,128)(2,1)S(1)} %collective-permute-done.21.refs_5_.refs_13_), channel_id=1, source_target_pairs={{0,16},{16,24},{24,8},{8,0},{1,17},{17,25},{25,9},{9,1},{2,18},{18... | collective-permute-start | bytes 786440 | tf_op jit(solution)/shard_map/z_far/ppermute | solution.py:34
  55.5 2.7 %z_matmul.9 = (bf16[128,1024]{1,0:T(8,128)(2,1)S(1)}, bf16[128,1024]{1,0:T(8,128)(2,1)S(1)}, bf16[128,1024]{1,0:T(8,128)(2,1)S(1)}) custom-call(s32[2]{0:T(128)S(1)} %pad_add_fusion.place_ref, bf16[384,512]{1,0:T(8,128)(2,1)S(1)} %collective-permute-done.13.refs_0_.refs_4_, bf16[384,512]{1,0:T(8,128)(2,1)S(1)} %collective-permute-done.16.refs_1_.refs_5_, ...), custom_call_target="tpu_custom_call" | custom-call | flops 2013265920 | bytes 786432 | tf_op jit(solution)/shard_map/z_far/z_matmul/pallas_call | solution.py:126
  58.2 3.6 %collective-permute-done.23.refs_7_.refs_15_ = bf16[128,1024]{1,0:T(8,128)(2,1)S(1)} collective-permute-done((bf16[128,1024]{1,0:T(8,128)(2,1)S(1)}, bf16[128,1024]{1,0:T(8,128)(2,1)S(1)}, u32[]{:S(2)}, u32[]{:S(2)}) %collective-permute-start.23) | collective-permute-done | bytes 262176 | tf_op jit(solution)/shard_map/z_far/ppermute | solution.py:34
  61.8 2.6 %kernel_strip.1 = (f32[4,32,1280]{2,1,0:T(8,128)S(1)}, bf16[4,32,1280]{2,1,0:T(8,128)(2,1)S(1)}) custom-call(s32[2]{0:T(128)S(1)} %pad_add_fusion.place_ref, bf16[128,1024]{1,0:T(8,128)(2,1)S(1)} %get-tuple-element.64.refs_0_.refs_8_, bf16[128,1024]{1,0:T(8,128)(2,1)S(1)} %get-tuple-element.65.refs_1_.refs_9_, ...), custom_call_target="tpu_custom_call" | custom-call | flops 671088640 | bytes 2097152 | tf_op jit(solution)/shard_map/kernel/kernel_strip/pallas_call | solution.py:173
  64.5 1.6 %collective-permute-done.25 = bf16[4,32,1280]{2,1,0:T(8,128)(2,1)S(1)} collective-permute-done((bf16[4,32,1280]{2,1,0:T(8,128)(2,1)S(1)}, bf16[4,32,1280]{2,1,0:T(8,128)(2,1)S(1)}, u32[]{:S(2)}, u32[]{:S(2)}) %collective-permute-start.25) | collective-permute-done | bytes 327712 | tf_op jit(solution)/shard_map/kernel/ppermute | solution.py:24
  67.1 1.4 %collective-permute-start.28 = (bf16[32,1280]{1,0:T(8,128)(2,1)S(1)}, bf16[32,1280]{1,0:T(8,128)(2,1)S(1)}, u32[]{:S(2)}, u32[]{:S(2)}) collective-permute-start(bf16[32,1280]{1,0:T(8,128)(2,1)S(1)} %get-tuple-element.113), channel_id=1, source_target_pairs={{0,6},{1,7},{2,4},{3,5},{4,2},{5,3},{6,0},{7,1},{8,14},{9,15},{10,... | collective-permute-start | bytes 245768 | tf_op jit(solution)/shard_map/kernel/ppermute | solution.py:24
  68.5 1.4 %collective-permute-start.27 = (bf16[32,1280]{1,0:T(8,128)(2,1)S(1)}, bf16[32,1280]{1,0:T(8,128)(2,1)S(1)}, u32[]{:S(2)}, u32[]{:S(2)}) collective-permute-start(bf16[32,1280]{1,0:T(8,128)(2,1)S(1)} %get-tuple-element.114), channel_id=1, source_target_pairs={{0,4},{1,5},{2,6},{3,7},{4,0},{5,1},{6,2},{7,3},{8,12},{9,13},{10,... | collective-permute-start | bytes 245768 | tf_op jit(solution)/shard_map/kernel/ppermute | solution.py:24
  69.8 2.2 %collective-permute-start.31 = (bf16[128,512]{1,0:T(8,128)(2,1)S(1)}, bf16[128,512]{1,0:T(8,128)(2,1)S(1)}, u32[]{:S(2)}, u32[]{:S(2)}) collective-permute-start(bf16[128,512]{1,0:T(8,128)(2,1)S(1)} %get-tuple-element.82), channel_id=1, source_target_pairs={{0,24},{16,8},{24,0},{8,16},{1,25},{17,9},{25,1},{9,17},{2,26},{18... | collective-permute-start | bytes 393224 | tf_op jit(solution)/shard_map/kernel/ppermute | solution.py:34
  72.8 1.2 %collective-permute-done.27 = bf16[32,1280]{1,0:T(8,128)(2,1)S(1)} collective-permute-done((bf16[32,1280]{1,0:T(8,128)(2,1)S(1)}, bf16[32,1280]{1,0:T(8,128)(2,1)S(1)}, u32[]{:S(2)}, u32[]{:S(2)}) %collective-permute-start.27) | collective-permute-done | bytes 81952 | tf_op jit(solution)/shard_map/kernel/ppermute | solution.py:24
  74.0 1.2 collective-permute-start.30
  75.2 1.6 %collective-permute-start.35 = (bf16[32,1280]{1,0:T(8,128)(2,1)S(1)}, bf16[32,1280]{1,0:T(8,128)(2,1)S(1)}, u32[]{:S(2)}, u32[]{:S(2)}) collective-permute-start(bf16[32,1280]{1,0:T(8,128)(2,1)S(1)} %get-tuple-element.106.refs_0_), channel_id=1, source_target_pairs={{0,6},{1,7},{2,4},{3,5},{4,2},{5,3},{6,0},{7,1},{8,14},{9,15},{10,... | collective-permute-start | bytes 245768 | tf_op jit(solution)/shard_map/kernel/ppermute | solution.py:24
  77.6 1.6 %collective-permute-done.30.refs_2_ = bf16[32,1280]{1,0:T(8,128)(2,1)S(1)} collective-permute-done((bf16[32,1280]{1,0:T(8,128)(2,1)S(1)}, bf16[32,1280]{1,0:T(8,128)(2,1)S(1)}, u32[]{:S(2)}, u32[]{:S(2)}) %collective-permute-start.30) | collective-permute-done | bytes 81952 | tf_op jit(solution)/shard_map/kernel/ppermute | solution.py:24
  79.2 1.6 %collective-permute-done.35.refs_6_ = bf16[32,1280]{1,0:T(8,128)(2,1)S(1)} collective-permute-done((bf16[32,1280]{1,0:T(8,128)(2,1)S(1)}, bf16[32,1280]{1,0:T(8,128)(2,1)S(1)}, u32[]{:S(2)}, u32[]{:S(2)}) %collective-permute-start.35) | collective-permute-done | bytes 81952 | tf_op jit(solution)/shard_map/kernel/ppermute | solution.py:24
  82.1 1.9 %collective-permute-start.37 = (bf16[128,512]{1,0:T(8,128)(2,1)S(1)}, bf16[128,512]{1,0:T(8,128)(2,1)S(1)}, u32[]{:S(2)}, u32[]{:S(2)}) collective-permute-start(bf16[128,512]{1,0:T(8,128)(2,1)S(1)} %get-tuple-element.85), channel_id=1, source_target_pairs={{0,8},{16,0},{24,16},{8,24},{1,9},{17,1},{25,17},{9,25},{2,10},{18... | collective-permute-start | bytes 393224 | tf_op jit(solution)/shard_map/kernel/ppermute | solution.py:34
  84.1 4.7 %embedding_gradient.1 = (bf16[2,512,1024]{2,1,0:T(8,128)(2,1)S(1)}, f32[8,128]{1,0:T(8,128)S(1)}) custom-call(s32[2]{0:T(128)S(1)} %pad_add_fusion.place_ref, f32[32,1280]{1,0:T(8,128)S(1)} %get-tuple-element.107.own_ref, bf16[32,1280]{1,0:T(8,128)(2,1)S(1)} %get-tuple-element.106.refs_0_, bf16[32,1280]{1,0:T(8,128)(2,1)S(1)} %collective-permute-done.29.refs_1_, ...), custom_call_target="tpu_custom_call" | custom-call | flops 1073741824 | bytes 4194304 | tf_op jit(solution)/shard_map/dz/embedding_gradient/pallas_call | solution.py:251
  88.8 1.8 %d_act_matmul.2 = bf16[4,272,512]{2,1,0:T(8,128)(2,1)S(1)} custom-call(s32[2]{0:T(128)S(1)} %pad_add_fusion.place_ref, bf16[2,512,1024]{2,1,0:T(8,128)(2,1)S(1)} %get-tuple-element.86.dz_ref.refs_9_, f32[8,128]{1,0:T(8,128)S(1)} %get-tuple-element.87.share_ref, bf16[4096,1024]{1,0:T(8,128)(2,1)S(1)} %get-tuple-element.60.refs_2_.refs_3_.refs_5_.w_ref), custom_call_target="tpu_custom_call" | custom-call | flops 1073741824 | bytes 1048576 | tf_op jit(solution)/shard_map/d_act/d_act_matmul/pallas_call | solution.py:323
  91.4 2.1 %collective-permute-done.38.refs_0_ = bf16[4,272,512]{2,1,0:T(8,128)(2,1)S(1)} collective-permute-done((bf16[4,272,512]{2,1,0:T(8,128)(2,1)S(1)}, bf16[4,272,512]{2,1,0:T(8,128)(2,1)S(1)}, u32[]{:S(2)}, u32[]{:S(2)}) %collective-permute-start.38) | collective-permute-done | bytes 1114144 | tf_op jit(solution)/shard_map/d_act/ppermute | solution.py:24
  93.5 1.8 %d_act_matmul.3 = (bf16[272,512]{1,0:T(8,128)(2,1)S(1)}, bf16[272,512]{1,0:T(8,128)(2,1)S(1)}, bf16[272,512]{1,0:T(8,128)(2,1)S(1)}, f32[272,512]{1,0:T(8,128)S(1)}) custom-call(s32[2]{0:T(128)S(1)} %pad_add_fusion.place_ref, bf16[2,512,1024]{2,1,0:T(8,128)(2,1)S(1)} %get-tuple-element.86.dz_ref.refs_9_, f32[8,128]{1,0:T(8,128)S(1)} %get-tuple-element.87.share_ref, ...), custom_call_target="tpu_custom_call" | custom-call | flops 1073741824 | bytes 1048576 | tf_op jit(solution)/shard_map/d_act/d_act_matmul/pallas_call | solution.py:323
  95.3 1.5 %collective-permute-start.39 = (bf16[272,512]{1,0:T(8,128)(2,1)S(1)}, bf16[272,512]{1,0:T(8,128)(2,1)S(1)}, u32[]{:S(2)}, u32[]{:S(2)}) collective-permute-start(bf16[272,512]{1,0:T(8,128)(2,1)S(1)} %get-tuple-element.89), channel_id=1, source_target_pairs={{0,2},{1,3},{2,0},{3,1},{4,6},{5,7},{6,4},{7,5},{8,10},{9,11},{10,... | collective-permute-start | bytes 835592 | tf_op jit(solution)/shard_map/d_act/ppermute | solution.py:24
  97.4 1.5 %collective-permute-start.41 = (bf16[272,512]{1,0:T(8,128)(2,1)S(1)}, bf16[272,512]{1,0:T(8,128)(2,1)S(1)}, u32[]{:S(2)}, u32[]{:S(2)}) collective-permute-start(bf16[272,512]{1,0:T(8,128)(2,1)S(1)} %get-tuple-element.91), channel_id=1, source_target_pairs={{0,6},{1,7},{2,4},{3,5},{4,2},{5,3},{6,0},{7,1},{8,14},{9,15},{10,... | collective-permute-start | bytes 835592 | tf_op jit(solution)/shard_map/d_act/ppermute | solution.py:24
  98.9 2.9 %weight_gradient.2.refs_10_ = f32[1024,1024]{1,0:T(8,128)} custom-call(s32[2]{0:T(128)S(1)} %pad_add_fusion.place_ref, bf16[256,512]{1,0:T(8,128)(2,1)S(1)} %bitcast.34, bf16[256,512]{1,0:T(8,128)(2,1)S(1)} %collective-permute-done.3.refs_0_.refs_1_, bf16[256,512]{1,0:T(8,128)(2,1)S(1)} %collective-permute-done.5.refs_1_.refs_2_, ...), custom_call_target="tpu_custom_call" | custom-call | flops 1073741824 | bytes 2097152 | tf_op jit(solution)/shard_map/grad_weight/weight_gradient/pallas_call | solution.py:428
  101.8 2.9 %weight_gradient.3 = f32[1024,1024]{1,0:T(8,128)} custom-call(s32[2]{0:T(128)S(1)} %pad_add_fusion.place_ref, bf16[256,512]{1,0:T(8,128)(2,1)S(1)} %collective-permute-done.9.refs_1_.refs_0_, bf16[256,512]{1,0:T(8,128)(2,1)S(1)} %collective-permute-done.4.refs_0_.refs_1_, ...), custom_call_target="tpu_custom_call", output_to_operand_aliasing={{}: (11, {})} | custom-call | flops 1073741824 | bytes 2097152 | tf_op jit(solution)/shard_map/grad_weight/weight_gradient/pallas_call | solution.py:428
  104.9 6.4 %collective-permute-done.40 = bf16[272,512]{1,0:T(8,128)(2,1)S(1)} collective-permute-done((bf16[272,512]{1,0:T(8,128)(2,1)S(1)}, bf16[272,512]{1,0:T(8,128)(2,1)S(1)}, u32[]{:S(2)}, u32[]{:S(2)}) %collective-permute-start.40) | collective-permute-done | bytes 278560 | tf_op jit(solution)/shard_map/d_act/ppermute | solution.py:24
  111.9 2.2 %collective-permute-start.45 = (f32[8,512]{1,0:T(8,128)S(1)}, f32[8,512]{1,0:T(8,128)S(1)}, u32[]{:S(2)}, u32[]{:S(2)}) collective-permute-start(f32[8,512]{1,0:T(8,128)S(1)} %pad_maximum_fusion.1.refs_0_), channel_id=1, source_target_pairs={{0,24},{8,16},{16,8},{24,0},{1,25},{9,17},{17,9},{25,1},{2,26},{10... | collective-permute-start | bytes 49160 | tf_op jit(solution)/shard_map/norm_backward/ppermute | solution.py:24
  114.6 1.8 %collective-permute-start.43 = (f32[8,512]{1,0:T(8,128)S(1)}, f32[8,512]{1,0:T(8,128)S(1)}, u32[]{:S(2)}, u32[]{:S(2)}) collective-permute-start(f32[8,512]{1,0:T(8,128)S(1)} %pad_maximum_fusion.1.refs_0_), channel_id=1, source_target_pairs={{0,8},{8,0},{16,24},{24,16},{1,9},{9,1},{17,25},{25,17},{2,10},{10... | collective-permute-start | bytes 49160 | tf_op jit(solution)/shard_map/norm_backward/ppermute | solution.py:24
  116.4 1.1 collective-permute-done.45.refs_3_
  117.5 1.2 %collective-permute-done.44.refs_2_ = f32[8,512]{1,0:T(8,128)S(1)} collective-permute-done((f32[8,512]{1,0:T(8,128)S(1)}, f32[8,512]{1,0:T(8,128)S(1)}, u32[]{:S(2)}, u32[]{:S(2)}) %collective-permute-start.44) | collective-permute-done | bytes 16416 | tf_op jit(solution)/shard_map/norm_backward/ppermute | solution.py:24
  (89 shorter events, 13.7 us)
Async XLA Ops:
  2.8 9.7 %copy-start = (f32[512]{0:T(512)S(1)}, f32[512]{0:T(512)}, u32[]{:S(2)}) copy-start(f32[512]{0:T(512)} %param.5) | copy-start | bytes 6148
  2.8 9.7 %copy-start.1 = (bf16[2,128,512]{2,1,0:T(8,128)(2,1)S(1)}, bf16[2,128,512]{2,1,0:T(8,128)(2,1)}, u32[]{:S(2)}) copy-start(bf16[2,128,512]{2,1,0:T(8,128)(2,1)} %param.4) | copy-start | bytes 786436
  2.8 9.2 %collective-permute-start.2 = (f32[4,512]{1,0:T(4,128)S(1)}, f32[4,512]{1,0:T(4,128)S(1)}, u32[]{:S(2)}, u32[]{:S(2)}) collective-permute-start(f32[4,512]{1,0:T(4,128)S(1)} %pad_maximum_fusion.2), channel_id=1, source_target_pairs={{0,24},{8,16},{16,8},{24,0},{1,25},{9,17},{17,9},{25,1},{2,26},{10... | collective-permute-start | bytes 24584 | tf_op jit(solution)/shard_map/norm_stats/ppermute | solution.py:24
  7.9 4.5 %collective-permute-start.1 = (f32[4,512]{1,0:T(4,128)S(1)}, f32[4,512]{1,0:T(4,128)S(1)}, u32[]{:S(2)}, u32[]{:S(2)}) collective-permute-start(f32[4,512]{1,0:T(4,128)S(1)} %pad_maximum_fusion.2), channel_id=1, source_target_pairs={{0,16},{8,24},{16,0},{24,8},{1,17},{9,25},{17,1},{25,9},{2,18},{10... | collective-permute-start | bytes 24584 | tf_op jit(solution)/shard_map/norm_stats/ppermute | solution.py:24
  7.9 4.5 %collective-permute-start = (f32[4,512]{1,0:T(4,128)S(1)}, f32[4,512]{1,0:T(4,128)S(1)}, u32[]{:S(2)}, u32[]{:S(2)}) collective-permute-start(f32[4,512]{1,0:T(4,128)S(1)} %pad_maximum_fusion.2), channel_id=1, source_target_pairs={{0,8},{8,0},{16,24},{24,16},{1,9},{9,1},{17,25},{25,17},{2,10},{10... | collective-permute-start | bytes 24584 | tf_op jit(solution)/shard_map/norm_stats/ppermute | solution.py:24
  12.8 3.6 %collective-permute-start.9 = (bf16[256,512]{1,0:T(8,128)(2,1)S(1)}, bf16[256,512]{1,0:T(8,128)(2,1)S(1)}, u32[]{:S(2)}, u32[]{:S(2)}) collective-permute-start(bf16[256,512]{1,0:T(8,128)(2,1)S(1)} %bitcast.28), channel_id=1, source_target_pairs={{0,1},{1,0},{2,3},{3,2},{4,5},{5,4},{6,7},{7,6},{8,9},{9,8},{10,11... | collective-permute-start | bytes 786440 | tf_op jit(solution)/shard_map/act_gather/ppermute | solution.py:24
  12.9 10.1 %collective-permute-start.7 = (bf16[256,512]{1,0:T(8,128)(2,1)S(1)}, bf16[256,512]{1,0:T(8,128)(2,1)S(1)}, u32[]{:S(2)}, u32[]{:S(2)}) collective-permute-start(bf16[256,512]{1,0:T(8,128)(2,1)S(1)} %bitcast.29), channel_id=1, source_target_pairs={{0,6},{1,7},{2,4},{3,5},{4,2},{5,3},{6,0},{7,1},{8,14},{9,15},{10,... | collective-permute-start | bytes 786440 | tf_op jit(solution)/shard_map/act_gather/ppermute | solution.py:24
  15.4 12.7 %collective-permute-start.5 = (bf16[256,512]{1,0:T(8,128)(2,1)S(1)}, bf16[256,512]{1,0:T(8,128)(2,1)S(1)}, u32[]{:S(2)}, u32[]{:S(2)}) collective-permute-start(bf16[256,512]{1,0:T(8,128)(2,1)S(1)} %bitcast.30), channel_id=1, source_target_pairs={{0,4},{1,5},{2,6},{3,7},{4,0},{5,1},{6,2},{7,3},{8,12},{9,13},{10,... | collective-permute-start | bytes 786440 | tf_op jit(solution)/shard_map/act_gather/ppermute | solution.py:24
  15.9 12.3 %collective-permute-start.3 = (bf16[256,512]{1,0:T(8,128)(2,1)S(1)}, bf16[256,512]{1,0:T(8,128)(2,1)S(1)}, u32[]{:S(2)}, u32[]{:S(2)}) collective-permute-start(bf16[256,512]{1,0:T(8,128)(2,1)S(1)} %bitcast.31), channel_id=1, source_target_pairs={{0,2},{1,3},{2,0},{3,1},{4,6},{5,7},{6,4},{7,5},{8,10},{9,11},{10,... | collective-permute-start | bytes 786440 | tf_op jit(solution)/shard_map/act_gather/ppermute | solution.py:24
  16.5 13.7 %collective-permute-start.11 = (bf16[128,512]{1,0:T(8,128)(2,1)S(1)}, bf16[128,512]{1,0:T(8,128)(2,1)S(1)}, u32[]{:S(2)}, u32[]{:S(2)}) collective-permute-start(bf16[128,512]{1,0:T(8,128)(2,1)S(1)} %slice_bitcast_fusion.1), channel_id=1, source_target_pairs={{0,16},{16,24},{24,8},{8,0},{1,17},{17,25},{25,9},{9,1},{2,18},{18... | collective-permute-start | bytes 393224 | tf_op jit(solution)/shard_map/act_gather/ppermute | solution.py:34
  18.5 11.8 %collective-permute-start.12 = (bf16[128,512]{1,0:T(8,128)(2,1)S(1)}, bf16[128,512]{1,0:T(8,128)(2,1)S(1)}, u32[]{:S(2)}, u32[]{:S(2)}) collective-permute-start(bf16[128,512]{1,0:T(8,128)(2,1)S(1)} %slice_bitcast_fusion.1), channel_id=1, source_target_pairs={{0,24},{16,8},{24,0},{8,16},{1,25},{17,9},{25,1},{9,17},{2,26},{18... | collective-permute-start | bytes 393224 | tf_op jit(solution)/shard_map/act_gather/ppermute | solution.py:34
  23.0 8.6 %collective-permute-start.10 = (bf16[128,512]{1,0:T(8,128)(2,1)S(1)}, bf16[128,512]{1,0:T(8,128)(2,1)S(1)}, u32[]{:S(2)}, u32[]{:S(2)}) collective-permute-start(bf16[128,512]{1,0:T(8,128)(2,1)S(1)} %slice_bitcast_fusion.1), channel_id=1, source_target_pairs={{0,8},{16,0},{24,16},{8,24},{1,9},{17,1},{25,17},{9,25},{2,10},{18... | collective-permute-start | bytes 393224 | tf_op jit(solution)/shard_map/act_gather/ppermute | solution.py:34
  28.1 6.5 %collective-permute-start.8 = (bf16[256,512]{1,0:T(8,128)(2,1)S(1)}, bf16[256,512]{1,0:T(8,128)(2,1)S(1)}, u32[]{:S(2)}, u32[]{:S(2)}) collective-permute-start(bf16[256,512]{1,0:T(8,128)(2,1)S(1)} %collective-permute-done.7.refs_2_.refs_3_), channel_id=1, source_target_pairs={{0,1},{1,0},{2,3},{3,2},{4,5},{5,4},{6,7},{7,6},{8,9},{9,8},{10,11... | collective-permute-start | bytes 786440 | tf_op jit(solution)/shard_map/act_gather/ppermute | solution.py:24
  28.2 6.4 %collective-permute-start.6 = (bf16[256,512]{1,0:T(8,128)(2,1)S(1)}, bf16[256,512]{1,0:T(8,128)(2,1)S(1)}, u32[]{:S(2)}, u32[]{:S(2)}) collective-permute-start(bf16[256,512]{1,0:T(8,128)(2,1)S(1)} %collective-permute-done.5.refs_1_.refs_2_), channel_id=1, source_target_pairs={{0,1},{1,0},{2,3},{3,2},{4,5},{5,4},{6,7},{7,6},{8,9},{9,8},{10,11... | collective-permute-start | bytes 786440 | tf_op jit(solution)/shard_map/act_gather/ppermute | solution.py:24
  30.2 4.5 %collective-permute-start.4 = (bf16[256,512]{1,0:T(8,128)(2,1)S(1)}, bf16[256,512]{1,0:T(8,128)(2,1)S(1)}, u32[]{:S(2)}, u32[]{:S(2)}) collective-permute-start(bf16[256,512]{1,0:T(8,128)(2,1)S(1)} %collective-permute-done.3.refs_0_.refs_1_), channel_id=1, source_target_pairs={{0,1},{1,0},{2,3},{3,2},{4,5},{5,4},{6,7},{7,6},{8,9},{9,8},{10,11... | collective-permute-start | bytes 786440 | tf_op jit(solution)/shard_map/act_gather/ppermute | solution.py:24
  31.6 11.1 %collective-permute-start.17 = (bf16[384,512]{1,0:T(8,128)(2,1)S(1)}, bf16[384,512]{1,0:T(8,128)(2,1)S(1)}, u32[]{:S(2)}, u32[]{:S(2)}) collective-permute-start(bf16[384,512]{1,0:T(8,128)(2,1)S(1)} %constant_dynamic-update-slice_fusion.refs_0_.refs_4_), channel_id=1, source_target_pairs={{0,4},{1,5},{2,6},{3,7},{4,0},{5,1},{6,2},{7,3},{8,12},{9,13},{10,... | collective-permute-start | bytes 1179656 | tf_op jit(solution)/shard_map/z/ppermute | solution.py:24
  33.2 11.1 %collective-permute-start.15 = (bf16[384,512]{1,0:T(8,128)(2,1)S(1)}, bf16[384,512]{1,0:T(8,128)(2,1)S(1)}, u32[]{:S(2)}, u32[]{:S(2)}) collective-permute-start(bf16[384,512]{1,0:T(8,128)(2,1)S(1)} %constant_dynamic-update-slice_fusion.refs_0_.refs_4_), channel_id=1, source_target_pairs={{0,2},{1,3},{2,0},{3,1},{4,6},{5,7},{6,4},{7,5},{8,10},{9,11},{10,... | collective-permute-start | bytes 1179656 | tf_op jit(solution)/shard_map/z/ppermute | solution.py:24
  36.2 9.7 %collective-permute-start.14 = (bf16[128,1024]{1,0:T(8,128)(2,1)S(1)}, bf16[128,1024]{1,0:T(8,128)(2,1)S(1)}, u32[]{:S(2)}, u32[]{:S(2)}) collective-permute-start(bf16[128,1024]{1,0:T(8,128)(2,1)S(1)} %get-tuple-element.65.refs_1_.refs_9_), channel_id=1, source_target_pairs={{0,16},{16,24},{24,8},{8,0},{1,17},{17,25},{25,9},{9,1},{2,18},{18... | collective-permute-start | bytes 786440 | tf_op jit(solution)/shard_map/z_ring/ppermute | solution.py:34
  42.7 6.9 %collective-permute-start.19 = (bf16[192,512]{1,0:T(8,128)(2,1)S(1)}, bf16[192,512]{1,0:T(8,128)(2,1)S(1)}, u32[]{:S(2)}, u32[]{:S(2)}) collective-permute-start(bf16[192,512]{1,0:T(8,128)(2,1)S(1)} %slice.149), channel_id=1, source_target_pairs={{0,2},{1,3},{2,0},{3,1},{4,6},{5,7},{6,4},{7,5},{8,10},{9,11},{10,... | collective-permute-start | bytes 589832 | tf_op jit(solution)/shard_map/z/ppermute | solution.py:24
  44.3 5.8 %collective-permute-start.20 = (bf16[192,512]{1,0:T(8,128)(2,1)S(1)}, bf16[192,512]{1,0:T(8,128)(2,1)S(1)}, u32[]{:S(2)}, u32[]{:S(2)}) collective-permute-start(bf16[192,512]{1,0:T(8,128)(2,1)S(1)} %slice.150), channel_id=1, source_target_pairs={{0,4},{1,5},{2,6},{3,7},{4,0},{5,1},{6,2},{7,3},{8,12},{9,13},{10,... | collective-permute-start | bytes 589832 | tf_op jit(solution)/shard_map/z/ppermute | solution.py:24
  45.9 6.8 %collective-permute-start.21 = (bf16[128,1024]{1,0:T(8,128)(2,1)S(1)}, bf16[128,1024]{1,0:T(8,128)(2,1)S(1)}, u32[]{:S(2)}, u32[]{:S(2)}) collective-permute-start(bf16[128,1024]{1,0:T(8,128)(2,1)S(1)} %collective-permute-done.14.refs_3_.refs_11_), channel_id=1, source_target_pairs={{0,16},{16,24},{24,8},{8,0},{1,17},{17,25},{25,9},{9,1},{2,18},{18... | collective-permute-start | bytes 786440 | tf_op jit(solution)/shard_map/z_ring/ppermute | solution.py:34
  47.1 7.6 %collective-permute-start.13 = (bf16[384,512]{1,0:T(8,128)(2,1)S(1)}, bf16[384,512]{1,0:T(8,128)(2,1)S(1)}, u32[]{:S(2)}, u32[]{:S(2)}) collective-permute-start(bf16[384,512]{1,0:T(8,128)(2,1)S(1)} %constant_dynamic-update-slice_fusion.refs_0_.refs_4_), channel_id=1, source_target_pairs={{0,1},{1,0},{2,3},{3,2},{4,5},{5,4},{6,7},{7,6},{8,9},{9,8},{10,11... | collective-permute-start | bytes 1179656 | tf_op jit(solution)/shard_map/z_far/ppermute | solution.py:24
  47.1 8.3 %collective-permute-start.16 = (bf16[384,512]{1,0:T(8,128)(2,1)S(1)}, bf16[384,512]{1,0:T(8,128)(2,1)S(1)}, u32[]{:S(2)}, u32[]{:S(2)}) collective-permute-start(bf16[384,512]{1,0:T(8,128)(2,1)S(1)} %collective-permute-done.15.refs_1_.refs_5_), channel_id=1, source_target_pairs={{0,1},{1,0},{2,3},{3,2},{4,5},{5,4},{6,7},{7,6},{8,9},{9,8},{10,11... | collective-permute-start | bytes 1179656 | tf_op jit(solution)/shard_map/z_far/ppermute | solution.py:24
  49.6 5.9 %collective-permute-start.18 = (bf16[384,512]{1,0:T(8,128)(2,1)S(1)}, bf16[384,512]{1,0:T(8,128)(2,1)S(1)}, u32[]{:S(2)}, u32[]{:S(2)}) collective-permute-start(bf16[384,512]{1,0:T(8,128)(2,1)S(1)} %collective-permute-done.17.refs_2_.refs_6_), channel_id=1, source_target_pairs={{0,1},{1,0},{2,3},{3,2},{4,5},{5,4},{6,7},{7,6},{8,9},{9,8},{10,11... | collective-permute-start | bytes 1179656 | tf_op jit(solution)/shard_map/z_far/ppermute | solution.py:24
  52.7 2.8 %collective-permute-start.22 = (bf16[384,512]{1,0:T(8,128)(2,1)S(1)}, bf16[384,512]{1,0:T(8,128)(2,1)S(1)}, u32[]{:S(2)}, u32[]{:S(2)}) collective-permute-start(bf16[384,512]{1,0:T(8,128)(2,1)S(1)} %pad_maximum_fusion.refs_3_.refs_7_), channel_id=1, source_target_pairs={{0,1},{1,0},{2,3},{3,2},{4,5},{5,4},{6,7},{7,6},{8,9},{9,8},{10,11... | collective-permute-start | bytes 1179656 | tf_op jit(solution)/shard_map/z_far/ppermute | solution.py:24
  52.7 9.1 %collective-permute-start.23 = (bf16[128,1024]{1,0:T(8,128)(2,1)S(1)}, bf16[128,1024]{1,0:T(8,128)(2,1)S(1)}, u32[]{:S(2)}, u32[]{:S(2)}) collective-permute-start(bf16[128,1024]{1,0:T(8,128)(2,1)S(1)} %collective-permute-done.21.refs_5_.refs_13_), channel_id=1, source_target_pairs={{0,16},{16,24},{24,8},{8,0},{1,17},{17,25},{25,9},{9,1},{2,18},{18... | collective-permute-start | bytes 786440 | tf_op jit(solution)/shard_map/z_far/ppermute | solution.py:34
  54.7 9.8 %collective-permute-start.24 = (bf16[128,512]{1,0:T(8,128)(2,1)S(1)}, bf16[128,512]{1,0:T(8,128)(2,1)S(1)}, u32[]{:S(2)}, u32[]{:S(2)}) collective-permute-start(bf16[128,512]{1,0:T(8,128)(2,1)S(1)} %get-tuple-element.80), channel_id=1, source_target_pairs={{0,16},{16,24},{24,8},{8,0},{1,17},{17,25},{25,9},{9,1},{2,18},{18... | collective-permute-start | bytes 393224 | tf_op jit(solution)/shard_map/kernel/ppermute | solution.py:34
  64.5 1.7 %collective-permute-start.25 = (bf16[4,32,1280]{2,1,0:T(8,128)(2,1)S(1)}, bf16[4,32,1280]{2,1,0:T(8,128)(2,1)S(1)}, u32[]{:S(2)}, u32[]{:S(2)}) collective-permute-start(bf16[4,32,1280]{2,1,0:T(8,128)(2,1)S(1)} %get-tuple-element.81), channel_id=1, source_target_pairs={{0,1},{1,0},{2,3},{3,2},{4,5},{5,4},{6,7},{7,6},{8,9},{9,8},{10,11... | collective-permute-start | bytes 983048 | tf_op jit(solution)/shard_map/kernel/ppermute | solution.py:24
  66.3 5.8 %collective-permute-start.26 = (bf16[32,1280]{1,0:T(8,128)(2,1)S(1)}, bf16[32,1280]{1,0:T(8,128)(2,1)S(1)}, u32[]{:S(2)}, u32[]{:S(2)}) collective-permute-start(bf16[32,1280]{1,0:T(8,128)(2,1)S(1)} %get-tuple-element.112), channel_id=1, source_target_pairs={{0,2},{1,3},{2,0},{3,1},{4,6},{5,7},{6,4},{7,5},{8,10},{9,11},{10,... | collective-permute-start | bytes 245768 | tf_op jit(solution)/shard_map/kernel/ppermute | solution.py:24
  67.1 5.7 %collective-permute-start.28 = (bf16[32,1280]{1,0:T(8,128)(2,1)S(1)}, bf16[32,1280]{1,0:T(8,128)(2,1)S(1)}, u32[]{:S(2)}, u32[]{:S(2)}) collective-permute-start(bf16[32,1280]{1,0:T(8,128)(2,1)S(1)} %get-tuple-element.113), channel_id=1, source_target_pairs={{0,6},{1,7},{2,4},{3,5},{4,2},{5,3},{6,0},{7,1},{8,14},{9,15},{10,... | collective-permute-start | bytes 245768 | tf_op jit(solution)/shard_map/kernel/ppermute | solution.py:24
  68.5 5.5 %collective-permute-start.27 = (bf16[32,1280]{1,0:T(8,128)(2,1)S(1)}, bf16[32,1280]{1,0:T(8,128)(2,1)S(1)}, u32[]{:S(2)}, u32[]{:S(2)}) collective-permute-start(bf16[32,1280]{1,0:T(8,128)(2,1)S(1)} %get-tuple-element.114), channel_id=1, source_target_pairs={{0,4},{1,5},{2,6},{3,7},{4,0},{5,1},{6,2},{7,3},{8,12},{9,13},{10,... | collective-permute-start | bytes 245768 | tf_op jit(solution)/shard_map/kernel/ppermute | solution.py:24
  69.8 7.8 %collective-permute-start.31 = (bf16[128,512]{1,0:T(8,128)(2,1)S(1)}, bf16[128,512]{1,0:T(8,128)(2,1)S(1)}, u32[]{:S(2)}, u32[]{:S(2)}) collective-permute-start(bf16[128,512]{1,0:T(8,128)(2,1)S(1)} %get-tuple-element.82), channel_id=1, source_target_pairs={{0,24},{16,8},{24,0},{8,16},{1,25},{17,9},{25,1},{9,17},{2,26},{18... | collective-permute-start | bytes 393224 | tf_op jit(solution)/shard_map/kernel/ppermute | solution.py:34
  74.0 5.1 %collective-permute-start.30 = (bf16[32,1280]{1,0:T(8,128)(2,1)S(1)}, bf16[32,1280]{1,0:T(8,128)(2,1)S(1)}, u32[]{:S(2)}, u32[]{:S(2)}) collective-permute-start(bf16[32,1280]{1,0:T(8,128)(2,1)S(1)} %get-tuple-element.106.refs_0_), channel_id=1, source_target_pairs={{0,2},{1,3},{2,0},{3,1},{4,6},{5,7},{6,4},{7,5},{8,10},{9,11},{10,... | collective-permute-start | bytes 245768 | tf_op jit(solution)/shard_map/kernel/ppermute | solution.py:24
  75.2 5.6 %collective-permute-start.35 = (bf16[32,1280]{1,0:T(8,128)(2,1)S(1)}, bf16[32,1280]{1,0:T(8,128)(2,1)S(1)}, u32[]{:S(2)}, u32[]{:S(2)}) collective-permute-start(bf16[32,1280]{1,0:T(8,128)(2,1)S(1)} %get-tuple-element.106.refs_0_), channel_id=1, source_target_pairs={{0,6},{1,7},{2,4},{3,5},{4,2},{5,3},{6,0},{7,1},{8,14},{9,15},{10,... | collective-permute-start | bytes 245768 | tf_op jit(solution)/shard_map/kernel/ppermute | solution.py:24
  76.8 4.8 %collective-permute-start.33 = (bf16[32,1280]{1,0:T(8,128)(2,1)S(1)}, bf16[32,1280]{1,0:T(8,128)(2,1)S(1)}, u32[]{:S(2)}, u32[]{:S(2)}) collective-permute-start(bf16[32,1280]{1,0:T(8,128)(2,1)S(1)} %get-tuple-element.106.refs_0_), channel_id=1, source_target_pairs={{0,4},{1,5},{2,6},{3,7},{4,0},{5,1},{6,2},{7,3},{8,12},{9,13},{10,... | collective-permute-start | bytes 245768 | tf_op jit(solution)/shard_map/kernel/ppermute | solution.py:24
  77.6 6.5 %collective-permute-start.29 = (bf16[32,1280]{1,0:T(8,128)(2,1)S(1)}, bf16[32,1280]{1,0:T(8,128)(2,1)S(1)}, u32[]{:S(2)}, u32[]{:S(2)}) collective-permute-start(bf16[32,1280]{1,0:T(8,128)(2,1)S(1)} %get-tuple-element.106.refs_0_), channel_id=1, source_target_pairs={{0,1},{1,0},{2,3},{3,2},{4,5},{5,4},{6,7},{7,6},{8,9},{9,8},{10,11... | collective-permute-start | bytes 245768 | tf_op jit(solution)/shard_map/kernel/ppermute | solution.py:24
  80.8 3.3 %collective-permute-start.36 = (bf16[32,1280]{1,0:T(8,128)(2,1)S(1)}, bf16[32,1280]{1,0:T(8,128)(2,1)S(1)}, u32[]{:S(2)}, u32[]{:S(2)}) collective-permute-start(bf16[32,1280]{1,0:T(8,128)(2,1)S(1)} %collective-permute-done.35.refs_6_), channel_id=1, source_target_pairs={{0,1},{1,0},{2,3},{3,2},{4,5},{5,4},{6,7},{7,6},{8,9},{9,8},{10,11... | collective-permute-start | bytes 245768 | tf_op jit(solution)/shard_map/kernel/ppermute | solution.py:24
  81.6 2.5 %collective-permute-start.34 = (bf16[32,1280]{1,0:T(8,128)(2,1)S(1)}, bf16[32,1280]{1,0:T(8,128)(2,1)S(1)}, u32[]{:S(2)}, u32[]{:S(2)}) collective-permute-start(bf16[32,1280]{1,0:T(8,128)(2,1)S(1)} %collective-permute-done.33.refs_4_), channel_id=1, source_target_pairs={{0,1},{1,0},{2,3},{3,2},{4,5},{5,4},{6,7},{7,6},{8,9},{9,8},{10,11... | collective-permute-start | bytes 245768 | tf_op jit(solution)/shard_map/kernel/ppermute | solution.py:24
  81.6 2.5 %collective-permute-start.32 = (bf16[32,1280]{1,0:T(8,128)(2,1)S(1)}, bf16[32,1280]{1,0:T(8,128)(2,1)S(1)}, u32[]{:S(2)}, u32[]{:S(2)}) collective-permute-start(bf16[32,1280]{1,0:T(8,128)(2,1)S(1)} %collective-permute-done.30.refs_2_), channel_id=1, source_target_pairs={{0,1},{1,0},{2,3},{3,2},{4,5},{5,4},{6,7},{7,6},{8,9},{9,8},{10,11... | collective-permute-start | bytes 245768 | tf_op jit(solution)/shard_map/kernel/ppermute | solution.py:24
  82.1 6.7 %collective-permute-start.37 = (bf16[128,512]{1,0:T(8,128)(2,1)S(1)}, bf16[128,512]{1,0:T(8,128)(2,1)S(1)}, u32[]{:S(2)}, u32[]{:S(2)}) collective-permute-start(bf16[128,512]{1,0:T(8,128)(2,1)S(1)} %get-tuple-element.85), channel_id=1, source_target_pairs={{0,8},{16,0},{24,16},{8,24},{1,9},{17,1},{25,17},{9,25},{2,10},{18... | collective-permute-start | bytes 393224 | tf_op jit(solution)/shard_map/kernel/ppermute | solution.py:34
  90.7 2.8 %collective-permute-start.38 = (bf16[4,272,512]{2,1,0:T(8,128)(2,1)S(1)}, bf16[4,272,512]{2,1,0:T(8,128)(2,1)S(1)}, u32[]{:S(2)}, u32[]{:S(2)}) collective-permute-start(bf16[4,272,512]{2,1,0:T(8,128)(2,1)S(1)} %d_act_matmul.2), channel_id=1, source_target_pairs={{0,1},{1,0},{2,3},{3,2},{4,5},{5,4},{6,7},{7,6},{8,9},{9,8},{10,11... | collective-permute-start | bytes 3342344 | tf_op jit(solution)/shard_map/d_act/ppermute | solution.py:24
  90.8 11.0 %collective-permute-start.42 = (bf16[384,512]{1,0:T(8,128)(2,1)S(1)}, bf16[384,512]{1,0:T(8,128)(2,1)S(1)}, u32[]{:S(2)}, u32[]{:S(2)}) collective-permute-start(bf16[384,512]{1,0:T(8,128)(2,1)S(1)} %constant_dynamic-update-slice_fusion.3.refs_8_), channel_id=1, source_target_pairs={{0,1},{1,0},{2,3},{3,2},{4,5},{5,4},{6,7},{7,6},{8,9},{9,8},{10,11... | collective-permute-start | bytes 1179656 | tf_op jit(solution)/shard_map/grad_weight/ppermute | solution.py:24
  95.3 9.6 %collective-permute-start.39 = (bf16[272,512]{1,0:T(8,128)(2,1)S(1)}, bf16[272,512]{1,0:T(8,128)(2,1)S(1)}, u32[]{:S(2)}, u32[]{:S(2)}) collective-permute-start(bf16[272,512]{1,0:T(8,128)(2,1)S(1)} %get-tuple-element.89), channel_id=1, source_target_pairs={{0,2},{1,3},{2,0},{3,1},{4,6},{5,7},{6,4},{7,5},{8,10},{9,11},{10,... | collective-permute-start | bytes 835592 | tf_op jit(solution)/shard_map/d_act/ppermute | solution.py:24
  96.9 14.4 %collective-permute-start.40 = (bf16[272,512]{1,0:T(8,128)(2,1)S(1)}, bf16[272,512]{1,0:T(8,128)(2,1)S(1)}, u32[]{:S(2)}, u32[]{:S(2)}) collective-permute-start(bf16[272,512]{1,0:T(8,128)(2,1)S(1)} %get-tuple-element.90), channel_id=1, source_target_pairs={{0,4},{1,5},{2,6},{3,7},{4,0},{5,1},{6,2},{7,3},{8,12},{9,13},{10,... | collective-permute-start | bytes 835592 | tf_op jit(solution)/shard_map/d_act/ppermute | solution.py:24
  97.4 13.9 %collective-permute-start.41 = (bf16[272,512]{1,0:T(8,128)(2,1)S(1)}, bf16[272,512]{1,0:T(8,128)(2,1)S(1)}, u32[]{:S(2)}, u32[]{:S(2)}) collective-permute-start(bf16[272,512]{1,0:T(8,128)(2,1)S(1)} %get-tuple-element.91), channel_id=1, source_target_pairs={{0,6},{1,7},{2,4},{3,5},{4,2},{5,3},{6,0},{7,1},{8,14},{9,15},{10,... | collective-permute-start | bytes 835592 | tf_op jit(solution)/shard_map/d_act/ppermute | solution.py:24
  111.9 5.6 %collective-permute-start.45 = (f32[8,512]{1,0:T(8,128)S(1)}, f32[8,512]{1,0:T(8,128)S(1)}, u32[]{:S(2)}, u32[]{:S(2)}) collective-permute-start(f32[8,512]{1,0:T(8,128)S(1)} %pad_maximum_fusion.1.refs_0_), channel_id=1, source_target_pairs={{0,24},{8,16},{16,8},{24,0},{1,25},{9,17},{17,9},{25,1},{2,26},{10... | collective-permute-start | bytes 49160 | tf_op jit(solution)/shard_map/norm_backward/ppermute | solution.py:24
  114.1 4.6 %collective-permute-start.44 = (f32[8,512]{1,0:T(8,128)S(1)}, f32[8,512]{1,0:T(8,128)S(1)}, u32[]{:S(2)}, u32[]{:S(2)}) collective-permute-start(f32[8,512]{1,0:T(8,128)S(1)} %pad_maximum_fusion.1.refs_0_), channel_id=1, source_target_pairs={{0,16},{8,24},{16,0},{24,8},{1,17},{9,25},{17,1},{25,9},{2,18},{10... | collective-permute-start | bytes 49160 | tf_op jit(solution)/shard_map/norm_backward/ppermute | solution.py:24
  114.6 4.2 %collective-permute-start.43 = (f32[8,512]{1,0:T(8,128)S(1)}, f32[8,512]{1,0:T(8,128)S(1)}, u32[]{:S(2)}, u32[]{:S(2)}) collective-permute-start(f32[8,512]{1,0:T(8,128)S(1)} %pad_maximum_fusion.1.refs_0_), channel_id=1, source_target_pairs={{0,8},{8,0},{16,24},{24,16},{1,9},{9,1},{17,25},{25,17},{2,10},{10... | collective-permute-start | bytes 49160 | tf_op jit(solution)/shard_map/norm_backward/ppermute | solution.py:24
  (1 other events, 9.7 us)

commit v15 on v14

--- a/solution.py
+++ b/solution.py
@@ -138,24 +138,51 @@
     return [(s, t) for s in range(n) for t in range(s, n)]
 
 
+def view_strip(z_refs):
+    local_rows = z_refs[0].shape[0]
+    rows = local_rows * len(z_refs)
+    zf = [z[...].astype(f32) for z in z_refs]
+    mean = sum(jnp.sum(z, axis=0, keepdims=True) for z in zf) / rows
+    rounded = jnp.concatenate([(z - mean).astype(bf16) for z in zf], axis=0)
+    for s in range(len(z_refs)):
+        yield lax.dot_general(
+            rounded[s * local_rows : (s + 1) * local_rows],
+            rounded[s * local_rows :],
+            (((1,), (1,)), ((), ())),
+            preferred_element_type=f32,
+        )
+
+
+def strip_first_kernel(*refs):
+    out_ref = refs[-1]
+    at = 0
+    for product in view_strip(refs[:-1]):
+        out_ref[:, pl.ds(at, product.shape[1])] = product
+        at += product.shape[1]
+
+
+def strip_first_call(z):
+    local_rows, columns = z[0].shape
+    wide = len(upper_blocks(len(z))) * local_rows
+    return pl.pallas_call(
+        strip_first_kernel,
+        out_shape=jax.ShapeDtypeStruct((local_rows, wide), f32),
+        in_specs=[IN_VMEM] * len(z),
+        out_specs=IN_VMEM,
+        compiler_params=params(12),
+        cost_estimate=cost(2 * local_rows * wide * columns, 2 * local_rows * columns * len(z)),
+        name="kernel_strip_0",
+    )(*z)
+
+
 def strip_kernel(n_batch, n_col, place_ref, *refs):
-    z_refs, (even_ref, odd_ref, strip) = refs[: 2 * n_batch], refs[2 * n_batch :]
+    z_refs, (first_ref, even_ref, odd_ref, strip) = refs[:n_batch], refs[n_batch:]
     local_rows = z_refs[0].shape[0]
-    rows = local_rows * n_batch
-    for v in range(2):
-        zf = [z[...].astype(f32) for z in z_refs[v::2]]
-        mean = sum(jnp.sum(z, axis=0, keepdims=True) for z in zf) / rows
-        rounded = jnp.concatenate([(z - mean).astype(bf16) for z in zf], axis=0)
-        at = 0
-        for s in range(n_batch):
-            product = lax.dot_general(
-                rounded[s * local_rows : (s + 1) * local_rows],
-                rounded[s * local_rows :],
-                (((1,), (1,)), ((), ())),
-                preferred_element_type=f32,
-            )
-            strip[pl.ds(v * local_rows, local_rows), pl.ds(at, product.shape[1])] = product
-            at += product.shape[1]
+    strip[:local_rows] = first_ref[...]
+    at = 0
+    for product in view_strip(z_refs):
+        strip[pl.ds(local_rows, local_rows), pl.ds(at, product.shape[1])] = product
+        at += product.shape[1]
     part = 2 * local_rows // n_col
     for k in range(n_col):
         start = pl.multiple_of((place_ref[1] ^ k) * part, part)
@@ -163,106 +190,106 @@
         ref[k // 2] = strip[pl.ds(start, part), :].astype(ref.dtype)
 
 
-def strip_call(place, z_slots, n_col):
-    n_batch = len(z_slots)
-    local_rows, columns = z_slots[0][0].shape
-    tall = 2 * local_rows
-    wide = len(upper_blocks(n_batch)) * local_rows
+def strip_call(place, z, first, n_col):
+    n_batch = len(z)
+    local_rows, columns = z[0].shape
+    tall, wide = 2 * local_rows, first.shape[1]
     shape = (n_col // 2, tall // n_col, wide)
-    operands = [place] + [z for slot in z_slots for z in slot]
+    operands = [place] + list(z) + [first]
     return pl.pallas_call(
         functools.partial(strip_kernel, n_batch, n_col),
         out_shape=(jax.ShapeDtypeStruct(shape, f32), jax.ShapeDtypeStruct(shape, bf16)),
         in_specs=[IN_SMEM] + [IN_VMEM] * (len(operands) - 1),
         out_specs=(IN_VMEM, IN_VMEM),
         scratch_shapes=[pltpu.VMEM((tall, wide), f32)],
-        compiler_params=params(18),
-        cost_estimate=cost(2 * tall * wide * columns, 2 * tall * columns * n_batch),
-        name="kernel_strip",
+        compiler_params=params(14),
+        cost_estimate=cost(2 * local_rows * wide * columns, 2 * local_rows * columns * n_batch),
+        name="kernel_strip_1",
     )(*operands)
 
 
-def dz_kernel(n_batch, n_col, tile, constants, place_ref, own_ref, *refs):
+def dz_kernel(v, n_batch, n_col, tile, constants, place_ref, own_ref, before_ref, *refs):
     coef, hinge_coef, inv_coef, inv_share, hinge_share, diag_share, block_share = constants
     strip_refs = refs[:n_col]
-    z_refs = refs[n_col : n_col + 2 * n_batch]
+    z_refs = refs[n_col : n_col + n_batch]
+    other_refs = refs[n_col + n_batch : n_col + 2 * n_batch]
     dz_ref, share_ref, strips, full, centred = refs[n_col + 2 * n_batch :]
     local_rows, columns = z_refs[0].shape
     rows = local_rows * n_batch
-    own = own_ref[...]
-    block = lax.broadcasted_iota(jnp.int32, own.shape, 1) // local_rows
-    on_diagonal = functools.reduce(
-        jnp.logical_or, [block == i for i, (s, t) in enumerate(upper_blocks(n_batch)) if s == t]
-    )
-    own = own * own * jnp.where(on_diagonal, 1.0, 2.0)
-    own = jnp.sum(jnp.sum(own, axis=0, keepdims=True), axis=1, keepdims=True)
-    share_ref[...] = jnp.broadcast_to(block_share * own, share_ref.shape)
+    share_ref[...] = before_ref[...]
+    if v == 0:
+        own = own_ref[...]
+        block = lax.broadcasted_iota(jnp.int32, own.shape, 1) // local_rows
+        on_diagonal = functools.reduce(
+            jnp.logical_or, [block == i for i, (s, t) in enumerate(upper_blocks(n_batch)) if s == t]
+        )
+        own = own * own * jnp.where(on_diagonal, 1.0, 2.0)
+        own = jnp.sum(jnp.sum(own, axis=0, keepdims=True), axis=1, keepdims=True)
+        share_ref[...] += jnp.broadcast_to(block_share * own, share_ref.shape)
     part = 2 * local_rows // n_col
     for k in range(n_col):
-        start = pl.multiple_of((place_ref[1] ^ k) * part, part)
-        strips[pl.ds(start, part), :] = strip_refs[k][...].astype(f32)
-    for v in range(2):
-        for i, (s, t) in enumerate(upper_blocks(n_batch)):
-            here, there = pl.ds(s * local_rows, local_rows), pl.ds(t * local_rows, local_rows)
-            block = strips[pl.ds(v * local_rows, local_rows), pl.ds(i * local_rows, local_rows)]
-            full[v, here, there] = block.astype(bf16)
-            if s < t:
-                full[v, there, here] = jnp.transpose(block).astype(bf16)
+        start = (place_ref[1] ^ k) * part - v * local_rows
+
+        @pl.when(jnp.logical_and(start >= 0, start < local_rows))
+        def _():
+            strips[pl.ds(pl.multiple_of(start, part), part), :] = strip_refs[k][...].astype(f32)
+
+    for i, (s, t) in enumerate(upper_blocks(n_batch)):
+        here, there = pl.ds(s * local_rows, local_rows), pl.ds(t * local_rows, local_rows)
+        block = strips[:, pl.ds(i * local_rows, local_rows)]
+        full[here, there] = block.astype(bf16)
+        if s < t:
+            full[there, here] = jnp.transpose(block).astype(bf16)
 
     def one_tile(j, carry):
         here = pl.ds(pl.multiple_of(j * tile, tile), tile)
-        share = jnp.zeros((1, 1), f32)
-        grads = []
-        z_views = []
-        for v in range(2):
-            zf = jnp.concatenate([z[:, here].astype(f32) for z in z_refs[v::2]], axis=0)
-            z_views.append(zf)
-            zc = zf - jnp.sum(zf, axis=0, keepdims=True) / rows
-            std = jnp.sqrt(jnp.sum(zc * zc, axis=0, keepdims=True) / (rows - 1) + eps_std)
-            zcb = zc.astype(bf16)
-            centred[...] = zcb
-            rounded = zcb.astype(f32)
-            diag = jnp.sum(rounded * rounded, axis=0, keepdims=True)
-            moved = jnp.dot(full[v], centred[...], preferred_element_type=f32)
-            pull = jnp.where(std < 1.0, hinge_coef, 0.0) / std
-            summed = coef * (moved - rounded * diag) - zc * pull
-            grads.append(summed - jnp.sum(summed, axis=0, keepdims=True) / rows)
-            share += hinge_share * jnp.sum(jnp.maximum(1.0 - std, 0.0), axis=1, keepdims=True)
-            share -= diag_share * jnp.sum(diag * diag, axis=1, keepdims=True)
-        diff = z_views[0] - z_views[1]
-        share += inv_share * jnp.sum(
-            jnp.sum(diff * diff, axis=0, keepdims=True), axis=1, keepdims=True
-        )
+        zf = jnp.concatenate([z[:, here].astype(f32) for z in z_refs], axis=0)
+        zc = zf - jnp.sum(zf, axis=0, keepdims=True) / rows
+        std = jnp.sqrt(jnp.sum(zc * zc, axis=0, keepdims=True) / (rows - 1) + eps_std)
+        zcb = zc.astype(bf16)
+        centred[...] = zcb
+        rounded = zcb.astype(f32)
+        diag = jnp.sum(rounded * rounded, axis=0, keepdims=True)
+        moved = jnp.dot(full[...], centred[...], preferred_element_type=f32)
+        pull = jnp.where(std < 1.0, hinge_coef, 0.0) / std
+        summed = coef * (moved - rounded * diag) - zc * pull
+        grad = summed - jnp.sum(summed, axis=0, keepdims=True) / rows
+        share = hinge_share * jnp.sum(jnp.maximum(1.0 - std, 0.0), axis=1, keepdims=True)
+        share -= diag_share * jnp.sum(diag * diag, axis=1, keepdims=True)
+        diff = zf - jnp.concatenate([z[:, here].astype(f32) for z in other_refs], axis=0)
+        if v == 0:
+            share += inv_share * jnp.sum(
+                jnp.sum(diff * diff, axis=0, keepdims=True), axis=1, keepdims=True
+            )
         share_ref[...] += jnp.broadcast_to(share, share_ref.shape)
-        dz_ref[0, :, here] = (grads[0] + inv_coef * diff).astype(bf16)
-        dz_ref[1, :, here] = (grads[1] - inv_coef * diff).astype(bf16)
+        dz_ref[:, here] = (grad + inv_coef * diff).astype(bf16)
         return carry
 
     lax.fori_loop(0, columns // tile, one_tile, 0)
 
 
-def dz_call(place, own, strips, z_slots, constants):
+def dz_call(place, v, own, before, strips, z_slots, constants):
     n_col, n_batch = len(strips), len(z_slots)
     local_rows, columns = z_slots[0][0].shape
-    tall = 2 * local_rows
     rows = local_rows * n_batch
     tile = min(256, columns)
-    operands = [place, own] + list(strips) + [z for slot in z_slots for z in slot]
-    return pl.pallas_call(
-        functools.partial(dz_kernel, n_batch, n_col, tile, constants),
+    operands = [place, own, before] + list(strips)
+    operands += [z[v] for z in z_slots] + [z[1 - v] for z in z_slots]
+    return pl.pallas_call(
+        functools.partial(dz_kernel, v, n_batch, n_col, tile, constants),
         out_shape=(
-            jax.ShapeDtypeStruct((2, rows, columns), bf16),
+            jax.ShapeDtypeStruct((rows, columns), bf16),
             jax.ShapeDtypeStruct((8, 128), f32),
         ),
         in_specs=[IN_SMEM] + [IN_VMEM] * (len(operands) - 1),
         out_specs=(IN_VMEM, IN_VMEM),
         scratch_shapes=[
-            pltpu.VMEM((tall, strips[0].shape[1]), f32),
-            pltpu.VMEM((2, rows, rows), bf16),
+            pltpu.VMEM((local_rows, strips[0].shape[1]), f32),
+            pltpu.VMEM((rows, rows), bf16),
             pltpu.VMEM((rows, tile), bf16),
         ],
-        compiler_params=params(24),
-        cost_estimate=cost(4 * rows * rows * columns, 8 * rows * columns),
+        compiler_params=params(16),
+        cost_estimate=cost(2 * rows * rows * columns, 6 * rows * columns),
         name="embedding_gradient",
     )(*operands)
 
@@ -283,45 +310,46 @@
     return rows[0:1].astype(f32) + rows[1:2].astype(f32) + rows[2:3].astype(f32)
 
 
-def d_act_kernel(count, adds, place_ref, dz_ref, share_ref, w_ref, *refs):
-    local_rows, columns = dz_ref.shape[1] // adds[1], dz_ref.shape[2]
-    tall = 2 * local_rows
-    dz = jnp.concatenate([dz_ref[0, :local_rows], dz_ref[1, :local_rows]], axis=0)
-    width = w_ref.shape[0] // adds[2]
-    share = share_ref[0:1, 0:1]
+def d_act_kernel(adds, tall, width, count, shares, place_ref, dz_ref, *refs):
+    refs = list(refs)
+    share = refs.pop(0)[0:1, 0:1] if shares else None
+    w_ref = refs.pop(0)
+    got = refs.pop(0) if adds else None
+    dz = dz_ref[:tall]
     for j in range(count):
-        k = 2 * ((j + 1) % count) if adds[0] else 2 * j + 1
+        k = 2 * ((j + 1) % count) if adds else 2 * j + 1
         part = lax.dot_general(
             dz,
             weight_rows(place_ref, w_ref, k, width),
             (((1,), (1,)), ((), ())),
             preferred_element_type=f32,
         )
-        if not adds[0]:
-            refs[0][j, :tall] = part.astype(refs[0].dtype)
-            refs[0][j, tall:] = share_rows(share, width, refs[0].dtype)
-        else:
-            got = refs[0]
-            out_ref = refs[j + 1]
-            slot = (j + 1) % count
-            out_ref[:tall] = (part + got[slot, :tall].astype(f32)).astype(out_ref.dtype)
-            whole_share = share + share_of(got[slot, tall:])[:, 0:1]
-            out_ref[tall:] = share_rows(whole_share, width, out_ref.dtype)
+        out = refs[j] if adds else refs[0].at[j]
+        whole_share = share
+        if adds:
+            part = part + got[k // 2, :tall].astype(f32)
+            if shares:
+                whole_share = share + share_of(got[k // 2, tall:])[:, 0:1]
+        out[:tall] = part.astype(out.dtype)
+        if shares:
+            out[tall:] = share_rows(whole_share, width, out.dtype)
 
 
 def d_act_call(place, dz, share, weight, n_batch, n_col, got):
+    width = weight.shape[0] // n_col
+    tall = dz.shape[0] // n_batch
     columns = weight.shape[1]
-    width = weight.shape[0] // n_col
-    tall = 2 * dz.shape[1] // n_batch
     count = n_col // 2
-    operands = [place, dz, share, weight] + ([] if got is None else [got])
+    long = tall if share is None else tall + EXTRA
+    operands = [place, dz] + ([] if share is None else [share]) + [weight]
     if got is None:
-        out_shape = (jax.ShapeDtypeStruct((count, tall + EXTRA, width), bf16),)
+        out_shape = (jax.ShapeDtypeStruct((count, long, width), bf16),)
     else:
-        out_shape = (jax.ShapeDtypeStruct((tall + EXTRA, width), bf16),) * (count - 1)
-        out_shape += (jax.ShapeDtypeStruct((tall + EXTRA, width), f32),)
-    return pl.pallas_call(
-        functools.partial(d_act_kernel, count, (got is not None, n_batch, n_col)),
+        operands.append(got)
+        out_shape = (jax.ShapeDtypeStruct((long, width), bf16),) * (count - 1)
+        out_shape += (jax.ShapeDtypeStruct((long, width), f32),)
+    return pl.pallas_call(
+        functools.partial(d_act_kernel, got is not None, tall, width, count, share is not None),
         out_shape=out_shape,
         in_specs=[IN_SMEM] + [IN_VMEM] * (len(operands) - 1),
         out_specs=(IN_VMEM,) * len(out_shape),
@@ -373,13 +401,13 @@
 
 def weight_grad_kernel(n_batch, aliased, half, tile, which, place_ref, *refs):
     near = [refs[:half], refs[half : 2 * half]]
-    blocks_ref, dz_ref = refs[2 * half : 2 * half + 2]
-    out_ref, act, product, sems = refs[2 * half + 2 + aliased :]
+    blocks_ref, *dz_refs = refs[2 * half : 2 * half + 3]
+    out_ref, act, product, sems = refs[2 * half + 3 + aliased :]
     block, parity = which
     chosen = held_place(place_ref[0], place_ref[1], block, 2 * half, n_batch)
     out_row = 2 * block + ((place_ref[1] & 1) ^ parity)
     local_rows = near[0][0].shape[0] // 2
-    rows = dz_ref.shape[1]
+    rows = dz_refs[0].shape[0]
     for e in range(half):
 
         @pl.when(chosen == e)
@@ -396,7 +424,7 @@
         for v in range(2):
             part = lax.dot_general(
                 act[pl.ds(v * rows, rows), pl.ds(i * tile, tile)],
-                dz_ref[v],
+                dz_refs[v][...],
                 (((0,), (0,)), ((), ())),
                 preferred_element_type=f32,
             )
@@ -416,9 +444,9 @@
 def weight_grad_call(place, which, near, blocks, dz, features, before):
     half = len(near[0])
     width = near[0][0].shape[1]
-    _, rows, columns = dz.shape
+    rows, columns = dz[0].shape
     tile = min(256, width)
-    operands = [place] + [x for group in near for x in group] + [blocks, dz]
+    operands = [place] + [x for group in near for x in group] + [blocks] + list(dz)
     specs = [IN_SMEM] + [IN_VMEM] * (len(operands) - 1)
     aliases = {}
     if before is not None:
@@ -574,7 +602,8 @@
         z_far = z_part(far_pieces, odds[:-1] + far[-1:] + odds[-1:], start, True)
         slots = list(zip([z_own0] + list(z_far), z_ring))
     with jax.named_scope("kernel"):
-        even_part, odd_part = strip_call(place, slots, n_col)
+        first_strip = strip_first_call([z0 for z0, _ in slots])
+        even_part, odd_part = strip_call(place, [z1 for _, z1 in slots], first_strip, n_col)
         blocks = [
             ring_send(x, "batch", 1 + i % (n_batch - 1)) for i, x in enumerate(picked)
         ]
@@ -602,13 +631,23 @@
             1.0 / denom / n_batch,
             1.0 / denom / n_batch,
         )
-        dz, share = dz_call(place, strip, [strips[k] for k in range(n_col)], slots, constants)
-        dz, blocks[2 * third :] = lax.optimization_barrier((dz, blocks[2 * third :]))
+        strips = [strips[k] for k in range(n_col)]
+        share = jnp.zeros((8, 128), f32)
+        dz0, share = dz_call(place, 0, strip, share, strips, slots, constants)
     with jax.named_scope("d_act"):
-        (away,) = d_act_call(place, dz, share, held_weight, n_batch, n_col, None)
-        got = xor_send(away, "col", 1)
-        *sends, d_act = d_act_call(place, dz, share, held_weight, n_batch, n_col, got)
-        arrived = [xor_send(part, "col", k) for k, part in zip(far, sends)]
+        (away0,) = d_act_call(place, dz0, None, held_weight, n_batch, n_col, None)
+        away0, share = lax.optimization_barrier((away0, share))
+        got0 = xor_send(away0, "col", 1)
+        dz1, share = dz_call(place, 1, strip, share, strips, slots, constants)
+        dz1, blocks[2 * third :] = lax.optimization_barrier((dz1, blocks[2 * third :]))
+        dz = [dz0, dz1]
+        (away1,) = d_act_call(place, dz1, share, held_weight, n_batch, n_col, None)
+        got1 = xor_send(away1, "col", 1)
+        views_d_act, arrived = [], []
+        for v, carried, got in ((0, None, got0), (1, share, got1)):
+            *sends, own = d_act_call(place, dz[v], carried, held_weight, n_batch, n_col, got)
+            arrived.append([xor_send(part, "col", k) for k, part in zip(far, sends)])
+            views_d_act.append(own)
     with jax.named_scope("grad_weight"):
         grad_weight = None
         for block in range(n_col // n_batch // 2):
@@ -626,11 +665,16 @@
                 )
     with jax.named_scope("norm_backward"):
         arrived, grad_weight = lax.optimization_barrier((arrived, grad_weight))
-        share = exchange_sum(share_of(part[tall:]) for part in [d_act] + arrived)
-        d_act = d_act[:tall]
-        for part in arrived:
-            d_act = d_act + part[:tall].astype(f32)
-        d_pre = d_act.reshape(n_view, local_rows, width) * gelu_slope(preactivation)
+        last = [views_d_act[1]] + arrived[1]
+        share = exchange_sum(share_of(part[local_rows:]) for part in last)
+        d_act = []
+        for own, parts in zip(views_d_act, arrived):
+            total = own[:local_rows]
+            for part in parts:
+                total = total + part[:local_rows].astype(f32)
+            d_act.append(total)
+        d_act = jnp.stack(d_act)
+        d_pre = d_act * gelu_slope(preactivation)
         sums = jnp.concatenate(
             [
                 jnp.sum(d_pre, axis=1),

time: 120 us -> 122 us (1.017)
  waiting for transfers between devices: 39.2 us -> 31.3 us
  Pallas kernels: 30.7 us -> 37.3 us
  starting transfers between devices: 45.3 us -> 48.9 us
    pallas_call x3 -> x7, Pallas kernels: 8.36 us -> 15.8 us  [the longest x4 8.18 us: d_act_call(): pl.pallas_call(functools.partial(d_act_kernel, got is not None, tall, wid...]
    ppermute x37 -> x41, waiting for transfers between devices: 31.8 us -> 24.4 us  [xor_send(): return lax.ppermute(x, axis, [(i, i ^ k) for i in range(n)])]
    ppermute x37 -> x41, starting transfers between devices: 33.3 us -> 36.8 us  [xor_send(): return lax.ppermute(x, axis, [(i, i ^ k) for i in range(n)])]
  transfers between devices with their start and end apart: 46 -> 50, of which waited for: 20 -> 19; matrix products, arithmetic and copies ran while one was open for 0% -> 0% of each run, Pallas kernels for 23% -> 30%
where the time goes in v15:
time: 122 us
  starting transfers between devices  48.9 us (40%)
  Pallas kernels  37.3 us (31%)
  waiting for transfers between devices  31.3 us (26%)
  other arithmetic  3.24 us (3%)
    ppermute x41, starting transfers between devices, xor_send(): return lax.ppermute(x, axis, [(i, i ^ k) for i in range(n)])  36.8 us
    ppermute x41, waiting for transfers between devices, xor_send(): return lax.ppermute(x, axis, [(i, i ^ k) for i in range(n)])  24.4 us
    ppermute x9, starting transfers between devices, ring_send(): lax.ppermute(x, axis, [(order[i], order[(i + d) % n]) for i in range(n)])  12.1 us
    pallas_call x5, Pallas kernels, z_call(): pl.pallas_call(functools.partial(z_kernel, tuple(ks), before is None, las...  8.95 us
    pallas_call x4, Pallas kernels, d_act_call(): pl.pallas_call(functools.partial(d_act_kernel, got is not None, tall, wid...  8.18 us
    ppermute x9, waiting for transfers between devices, ring_send(): lax.ppermute(x, axis, [(order[i], order[(i + d) % n]) for i in range(n)])  6.92 us
    pallas_call x2, Pallas kernels, dz_call(): pl.pallas_call(functools.partial(dz_kernel, v, n_batch, n_col, tile, cons...  6.54 us
    pallas_call x2, Pallas kernels, weight_grad_call(): pl.pallas_call(functools.partial(weight_grad_kernel, rows // (near[0][0]....  5.77 us
  transfers between devices with their start and end apart: 50, of which 19 were waited for; matrix products, arithmetic and copies ran while one was open for 0% of the time, Pallas kernels for 30%

profile of v15, /device:TPU:0, one launch (start us, length us, event | category | flops | bytes accessed | tf_op | source)
XLA Modules:
  0.0 122.0 jit_solution(16197765842476286980)
XLA Ops:
  2.8 5.1 %collective-permute-start.2 = (f32[4,512]{1,0:T(4,128)S(1)}, f32[4,512]{1,0:T(4,128)S(1)}, u32[]{:S(2)}, u32[]{:S(2)}) collective-permute-start(f32[4,512]{1,0:T(4,128)S(1)} %pad_maximum_fusion.2), channel_id=1, source_target_pairs={{0,24},{8,16},{16,8},{24,0},{1,25},{9,17},{17,9},{25,1},{2,26},{10... | collective-permute-start | bytes 24584 | tf_op jit(solution)/shard_map/norm_stats/ppermute | solution.py:24
  8.6 3.5 %weight_load.1 = (bf16[4096,1024]{1,0:T(8,128)(2,1)S(1)}, f32[4,512]{1,0:T(4,128)S(1)}) custom-call(bf16[4096,1024]{1,0:T(8,128)(2,1)} %w_ref), custom_call_target="tpu_custom_call" | custom-call | bytes 16777216 | tf_op jit(solution)/shard_map/weight_load/weight_load/pallas_call | solution.py:78
  12.9 2.5 %collective-permute-start.7 = (bf16[256,512]{1,0:T(8,128)(2,1)S(1)}, bf16[256,512]{1,0:T(8,128)(2,1)S(1)}, u32[]{:S(2)}, u32[]{:S(2)}) collective-permute-start(bf16[256,512]{1,0:T(8,128)(2,1)S(1)} %bitcast.31), channel_id=1, source_target_pairs={{0,6},{1,7},{2,4},{3,5},{4,2},{5,3},{6,0},{7,1},{8,14},{9,15},{10,... | collective-permute-start | bytes 786440 | tf_op jit(solution)/shard_map/act_gather/ppermute | solution.py:24
  16.5 2.1 %collective-permute-start.12 = (bf16[128,512]{1,0:T(8,128)(2,1)S(1)}, bf16[128,512]{1,0:T(8,128)(2,1)S(1)}, u32[]{:S(2)}, u32[]{:S(2)}) collective-permute-start(bf16[128,512]{1,0:T(8,128)(2,1)S(1)} %slice_bitcast_fusion.1), channel_id=1, source_target_pairs={{0,16},{16,24},{24,8},{8,0},{1,17},{17,25},{25,9},{9,1},{2,18},{18... | collective-permute-start | bytes 393224 | tf_op jit(solution)/shard_map/act_gather/ppermute | solution.py:34
  18.5 1.4 %collective-permute-start.13 = (bf16[128,512]{1,0:T(8,128)(2,1)S(1)}, bf16[128,512]{1,0:T(8,128)(2,1)S(1)}, u32[]{:S(2)}, u32[]{:S(2)}) collective-permute-start(bf16[128,512]{1,0:T(8,128)(2,1)S(1)} %slice_bitcast_fusion.1), channel_id=1, source_target_pairs={{0,24},{16,8},{24,0},{8,16},{1,25},{17,9},{25,1},{9,17},{2,26},{18... | collective-permute-start | bytes 393224 | tf_op jit(solution)/shard_map/act_gather/ppermute | solution.py:34
  20.0 1.2 %z_matmul.5.refs_4_ = f32[256,1024]{1,0:T(8,128)S(1)} custom-call(s32[2]{0:T(128)S(1)} %pad_add_fusion.place_ref, bf16[256,512]{1,0:T(8,128)(2,1)S(1)} %bitcast.34, bf16[256,512]{1,0:T(8,128)(2,1)S(1)} %collective-permute-done.9.refs_1_.refs_0_, bf16[4096,1024]{1,0:T(8,128)(2,1)S(1)} %get-tuple-element.71.refs_2_.refs_3_.refs_5_.refs_0_.refs_1_), custom_call_target="tpu_custom_call" | custom-call | flops 536870912 | bytes 524288 | tf_op jit(solution)/shard_map/z/z_matmul/pallas_call | solution.py:126
  21.2 1.8 %collective-permute-done.7.refs_2_.refs_3_ = bf16[256,512]{1,0:T(8,128)(2,1)S(1)} collective-permute-done((bf16[256,512]{1,0:T(8,128)(2,1)S(1)}, bf16[256,512]{1,0:T(8,128)(2,1)S(1)}, u32[]{:S(2)}, u32[]{:S(2)}) %collective-permute-start.7) | collective-permute-done | bytes 262176 | tf_op jit(solution)/shard_map/act_gather/ppermute | solution.py:24
  24.0 4.1 %collective-permute-done.5.refs_1_.refs_2_ = bf16[256,512]{1,0:T(8,128)(2,1)S(1)} collective-permute-done((bf16[256,512]{1,0:T(8,128)(2,1)S(1)}, bf16[256,512]{1,0:T(8,128)(2,1)S(1)}, u32[]{:S(2)}, u32[]{:S(2)}) %collective-permute-start.5) | collective-permute-done | bytes 262176 | tf_op jit(solution)/shard_map/act_gather/ppermute | solution.py:24
  28.6 1.5 %z_matmul.6.refs_4_ = f32[256,1024]{1,0:T(8,128)S(1)} custom-call(s32[2]{0:T(128)S(1)} %pad_add_fusion.place_ref, bf16[256,512]{1,0:T(8,128)(2,1)S(1)} %collective-permute-done.3.refs_0_.refs_1_, bf16[256,512]{1,0:T(8,128)(2,1)S(1)} %collective-permute-done.5.refs_1_.refs_2_, bf16[256,512]{1,0:T(8,128)(2,1)S(1)} %collective-permute-done.7.refs_2_.refs_3_, ...), custom_call_target="tpu_custom_call" | custom-call | flops 805306368 | bytes 524288 | tf_op jit(solution)/shard_map/z/z_matmul/pallas_call | solution.py:126
  30.4 1.2 collective-permute-done.10
  31.6 1.6 %collective-permute-start.15 = (bf16[384,512]{1,0:T(8,128)(2,1)S(1)}, bf16[384,512]{1,0:T(8,128)(2,1)S(1)}, u32[]{:S(2)}, u32[]{:S(2)}) collective-permute-start(bf16[384,512]{1,0:T(8,128)(2,1)S(1)} %constant_dynamic-update-slice_fusion.refs_0_.refs_4_), channel_id=1, source_target_pairs={{0,4},{1,5},{2,6},{3,7},{4,0},{5,1},{6,2},{7,3},{8,12},{9,13},{10,... | collective-permute-start | bytes 1179656 | tf_op jit(solution)/shard_map/z/ppermute | solution.py:24
  33.2 1.5 %collective-permute-start.14 = (bf16[384,512]{1,0:T(8,128)(2,1)S(1)}, bf16[384,512]{1,0:T(8,128)(2,1)S(1)}, u32[]{:S(2)}, u32[]{:S(2)}) collective-permute-start(bf16[384,512]{1,0:T(8,128)(2,1)S(1)} %constant_dynamic-update-slice_fusion.refs_0_.refs_4_), channel_id=1, source_target_pairs={{0,2},{1,3},{2,0},{3,1},{4,6},{5,7},{6,4},{7,5},{8,10},{9,11},{10,... | collective-permute-start | bytes 1179656 | tf_op jit(solution)/shard_map/z/ppermute | solution.py:24
  34.7 1.5 %z_matmul.7 = (bf16[128,1024]{1,0:T(8,128)(2,1)S(1)}, bf16[128,1024]{1,0:T(8,128)(2,1)S(1)}) custom-call(s32[2]{0:T(128)S(1)} %pad_add_fusion.place_ref, bf16[256,512]{1,0:T(8,128)(2,1)S(1)} %collective-permute-done.4.refs_0_.refs_1_, bf16[256,512]{1,0:T(8,128)(2,1)S(1)} %collective-permute-done.6.refs_1_.refs_2_, ...), custom_call_target="tpu_custom_call" | custom-call | flops 805306368 | bytes 524288 | tf_op jit(solution)/shard_map/z/z_matmul/pallas_call | solution.py:126
  36.3 6.4 %collective-permute-done.15.refs_2_.refs_6_ = bf16[384,512]{1,0:T(8,128)(2,1)S(1)} collective-permute-done((bf16[384,512]{1,0:T(8,128)(2,1)S(1)}, bf16[384,512]{1,0:T(8,128)(2,1)S(1)}, u32[]{:S(2)}, u32[]{:S(2)}) %collective-permute-start.15) | collective-permute-done | bytes 393248 | tf_op jit(solution)/shard_map/z/ppermute | solution.py:24
  42.7 1.6 %collective-permute-start.16 = (bf16[192,512]{1,0:T(8,128)(2,1)S(1)}, bf16[192,512]{1,0:T(8,128)(2,1)S(1)}, u32[]{:S(2)}, u32[]{:S(2)}) collective-permute-start(bf16[192,512]{1,0:T(8,128)(2,1)S(1)} %slice.149), channel_id=1, source_target_pairs={{0,2},{1,3},{2,0},{3,1},{4,6},{5,7},{6,4},{7,5},{8,10},{9,11},{10,... | collective-permute-start | bytes 589832 | tf_op jit(solution)/shard_map/z/ppermute | solution.py:24
  44.3 1.6 %collective-permute-start.17 = (bf16[192,512]{1,0:T(8,128)(2,1)S(1)}, bf16[192,512]{1,0:T(8,128)(2,1)S(1)}, u32[]{:S(2)}, u32[]{:S(2)}) collective-permute-start(bf16[192,512]{1,0:T(8,128)(2,1)S(1)} %slice.150), channel_id=1, source_target_pairs={{0,4},{1,5},{2,6},{3,7},{4,0},{5,1},{6,2},{7,3},{8,12},{9,13},{10,... | collective-permute-start | bytes 589832 | tf_op jit(solution)/shard_map/z/ppermute | solution.py:24
  47.6 1.9 %z_matmul.8.refs_6_ = f32[384,1024]{1,0:T(8,128)S(1)} custom-call(s32[2]{0:T(128)S(1)} %pad_add_fusion.place_ref, bf16[384,512]{1,0:T(8,128)(2,1)S(1)} %constant_dynamic-update-slice_fusion.refs_0_.refs_4_, bf16[384,512]{1,0:T(8,128)(2,1)S(1)} %collective-permute-done.14.refs_1_.refs_5_, bf16[384,512]{1,0:T(8,128)(2,1)S(1)} %collective-permute-done.15.refs_2_.refs_6_, ...), custom_call_target="tpu_custom_call" | custom-call | flops 1207959552 | bytes 786432 | tf_op jit(solution)/shard_map/z_far/z_matmul/pallas_call | solution.py:126
  50.1 2.6 %collective-permute-done.18.refs_2_.refs_14_.refs_10_ = bf16[128,1024]{1,0:T(8,128)(2,1)S(1)} collective-permute-done((bf16[128,1024]{1,0:T(8,128)(2,1)S(1)}, bf16[128,1024]{1,0:T(8,128)(2,1)S(1)}, u32[]{:S(2)}, u32[]{:S(2)}) %collective-permute-start.18) | collective-permute-done | bytes 262176 | tf_op jit(solution)/shard_map/z_ring/ppermute | solution.py:34
  52.7 2.0 %collective-permute-start.19 = (bf16[128,1024]{1,0:T(8,128)(2,1)S(1)}, bf16[128,1024]{1,0:T(8,128)(2,1)S(1)}, u32[]{:S(2)}, u32[]{:S(2)}) collective-permute-start(bf16[128,1024]{1,0:T(8,128)(2,1)S(1)} %collective-permute-done.18.refs_2_.refs_14_.refs_10_), channel_id=1, source_target_pairs={{0,16},{16,24},{24,8},{8,0},{1,17},{17,25},{25,9},{9,1},{2,18},{18... | collective-permute-start | bytes 786440 | tf_op jit(solution)/shard_map/z_far/ppermute | solution.py:34
  55.5 2.7 %z_matmul.9 = (bf16[128,1024]{1,0:T(8,128)(2,1)S(1)}, bf16[128,1024]{1,0:T(8,128)(2,1)S(1)}, bf16[128,1024]{1,0:T(8,128)(2,1)S(1)}) custom-call(s32[2]{0:T(128)S(1)} %pad_add_fusion.place_ref, bf16[384,512]{1,0:T(8,128)(2,1)S(1)} %collective-permute-done.20.refs_0_.refs_4_, bf16[384,512]{1,0:T(8,128)(2,1)S(1)} %collective-permute-done.21.refs_1_.refs_5_, ...), custom_call_target="tpu_custom_call" | custom-call | flops 2013265920 | bytes 786432 | tf_op jit(solution)/shard_map/z_far/z_matmul/pallas_call | solution.py:126
  59.3 2.5 %collective-permute-done.19.refs_3_.refs_15_.refs_11_ = bf16[128,1024]{1,0:T(8,128)(2,1)S(1)} collective-permute-done((bf16[128,1024]{1,0:T(8,128)(2,1)S(1)}, bf16[128,1024]{1,0:T(8,128)(2,1)S(1)}, u32[]{:S(2)}, u32[]{:S(2)}) %collective-permute-start.19) | collective-permute-done | bytes 262176 | tf_op jit(solution)/shard_map/z_far/ppermute | solution.py:34
  61.8 1.8 %kernel_strip_1.1 = (f32[4,32,1280]{2,1,0:T(8,128)S(1)}, bf16[4,32,1280]{2,1,0:T(8,128)(2,1)S(1)}) custom-call(s32[2]{0:T(128)S(1)} %pad_add_fusion.place_ref, bf16[128,1024]{1,0:T(8,128)(2,1)S(1)} %get-tuple-element.75.refs_0_.refs_12_.refs_8_, bf16[128,1024]{1,0:T(8,128)(2,1)S(1)} %collective-permute-done.11.refs_1_.refs_13_.refs_9_, ...), custom_call_target="tpu_custom_call" | custom-call | flops 335544320 | bytes 1048576 | tf_op jit(solution)/shard_map/kernel/kernel_strip_1/pallas_call | solution.py:199
  64.2 1.6 %collective-permute-done.25 = bf16[4,32,1280]{2,1,0:T(8,128)(2,1)S(1)} collective-permute-done((bf16[4,32,1280]{2,1,0:T(8,128)(2,1)S(1)}, bf16[4,32,1280]{2,1,0:T(8,128)(2,1)S(1)}, u32[]{:S(2)}, u32[]{:S(2)}) %collective-permute-start.25) | collective-permute-done | bytes 327712 | tf_op jit(solution)/shard_map/kernel/ppermute | solution.py:24
  66.7 1.4 %collective-permute-start.28 = (bf16[32,1280]{1,0:T(8,128)(2,1)S(1)}, bf16[32,1280]{1,0:T(8,128)(2,1)S(1)}, u32[]{:S(2)}, u32[]{:S(2)}) collective-permute-start(bf16[32,1280]{1,0:T(8,128)(2,1)S(1)} %get-tuple-element.135), channel_id=1, source_target_pairs={{0,6},{1,7},{2,4},{3,5},{4,2},{5,3},{6,0},{7,1},{8,14},{9,15},{10,... | collective-permute-start | bytes 245768 | tf_op jit(solution)/shard_map/kernel/ppermute | solution.py:24
  68.2 1.4 %collective-permute-start.27 = (bf16[32,1280]{1,0:T(8,128)(2,1)S(1)}, bf16[32,1280]{1,0:T(8,128)(2,1)S(1)}, u32[]{:S(2)}, u32[]{:S(2)}) collective-permute-start(bf16[32,1280]{1,0:T(8,128)(2,1)S(1)} %get-tuple-element.136), channel_id=1, source_target_pairs={{0,4},{1,5},{2,6},{3,7},{4,0},{5,1},{6,2},{7,3},{8,12},{9,13},{10,... | collective-permute-start | bytes 245768 | tf_op jit(solution)/shard_map/kernel/ppermute | solution.py:24
  69.5 2.2 %collective-permute-start.31 = (bf16[128,512]{1,0:T(8,128)(2,1)S(1)}, bf16[128,512]{1,0:T(8,128)(2,1)S(1)}, u32[]{:S(2)}, u32[]{:S(2)}) collective-permute-start(bf16[128,512]{1,0:T(8,128)(2,1)S(1)} %get-tuple-element.93), channel_id=1, source_target_pairs={{0,24},{16,8},{24,0},{8,16},{1,25},{17,9},{25,1},{9,17},{2,26},{18... | collective-permute-start | bytes 393224 | tf_op jit(solution)/shard_map/kernel/ppermute | solution.py:34
  72.5 1.2 collective-permute-done.27
  73.7 1.2 collective-permute-start.30
  74.9 1.6 %collective-permute-start.35 = (bf16[32,1280]{1,0:T(8,128)(2,1)S(1)}, bf16[32,1280]{1,0:T(8,128)(2,1)S(1)}, u32[]{:S(2)}, u32[]{:S(2)}) collective-permute-start(bf16[32,1280]{1,0:T(8,128)(2,1)S(1)} %get-tuple-element.128.refs_0_), channel_id=1, source_target_pairs={{0,6},{1,7},{2,4},{3,5},{4,2},{5,3},{6,0},{7,1},{8,14},{9,15},{10,... | collective-permute-start | bytes 245768 | tf_op jit(solution)/shard_map/kernel/ppermute | solution.py:24
  77.3 1.6 %collective-permute-done.30.refs_2_ = bf16[32,1280]{1,0:T(8,128)(2,1)S(1)} collective-permute-done((bf16[32,1280]{1,0:T(8,128)(2,1)S(1)}, bf16[32,1280]{1,0:T(8,128)(2,1)S(1)}, u32[]{:S(2)}, u32[]{:S(2)}) %collective-permute-start.30) | collective-permute-done | bytes 81952 | tf_op jit(solution)/shard_map/kernel/ppermute | solution.py:24
  78.9 1.6 %collective-permute-done.35.refs_6_ = bf16[32,1280]{1,0:T(8,128)(2,1)S(1)} collective-permute-done((bf16[32,1280]{1,0:T(8,128)(2,1)S(1)}, bf16[32,1280]{1,0:T(8,128)(2,1)S(1)}, u32[]{:S(2)}, u32[]{:S(2)}) %collective-permute-start.35) | collective-permute-done | bytes 81952 | tf_op jit(solution)/shard_map/kernel/ppermute | solution.py:24
  81.8 1.9 %collective-permute-start.41 = (bf16[128,512]{1,0:T(8,128)(2,1)S(1)}, bf16[128,512]{1,0:T(8,128)(2,1)S(1)}, u32[]{:S(2)}, u32[]{:S(2)}) collective-permute-start(bf16[128,512]{1,0:T(8,128)(2,1)S(1)} %get-tuple-element.104), channel_id=1, source_target_pairs={{0,8},{16,0},{24,16},{8,24},{1,9},{17,1},{25,17},{9,25},{2,10},{18... | collective-permute-start | bytes 393224 | tf_op jit(solution)/shard_map/kernel/ppermute | solution.py:34
  83.8 3.2 %embedding_gradient.2 = (bf16[512,1024]{1,0:T(8,128)(2,1)S(1)}, f32[8,128]{1,0:T(8,128)S(1)}) custom-call(s32[2]{0:T(128)S(1)} %pad_add_fusion.place_ref, f32[32,1280]{1,0:T(8,128)S(1)} %get-tuple-element.129.own_ref, f32[8,128]{1,0:T(8,128)S(1)} %broadcast_in_dim.8.before_ref, bf16[32,1280]{1,0:T(8,128)(2,1)S(1)} %get-tuple-element.128.refs_0_, ...), custom_call_target="tpu_custom_call" | custom-call | flops 536870912 | bytes 3145728 | tf_op jit(solution)/shard_map/dz/embedding_gradient/pallas_call | solution.py:278
  87.1 2.0 %d_act_matmul.4 = bf16[4,128,512]{2,1,0:T(8,128)(2,1)S(1)} custom-call(s32[2]{0:T(128)S(1)} %pad_add_fusion.place_ref, bf16[512,1024]{1,0:T(8,128)(2,1)S(1)} %get-tuple-element.95.dz_ref.refs_9_, bf16[4096,1024]{1,0:T(8,128)(2,1)S(1)} %get-tuple-element.71.refs_2_.refs_3_.refs_5_.refs_0_.refs_1_), custom_call_target="tpu_custom_call" | custom-call | flops 536870912 | bytes 524288 | tf_op jit(solution)/shard_map/d_act/d_act_matmul/pallas_call | solution.py:351
  89.1 3.3 %embedding_gradient.3 = (bf16[512,1024]{1,0:T(8,128)(2,1)S(1)}, f32[8,128]{1,0:T(8,128)S(1)}) custom-call(s32[2]{0:T(128)S(1)} %pad_add_fusion.place_ref, f32[32,1280]{1,0:T(8,128)S(1)} %get-tuple-element.129.own_ref, f32[8,128]{1,0:T(8,128)S(1)} %get-tuple-element.102.before_ref, bf16[32,1280]{1,0:T(8,128)(2,1)S(1)} %get-tuple-element.128.refs_0_, ...), custom_call_target="tpu_custom_call" | custom-call | flops 536870912 | bytes 3145728 | tf_op jit(solution)/shard_map/d_act/embedding_gradient/pallas_call | solution.py:278
  92.5 2.0 %d_act_matmul.6 = bf16[4,144,512]{2,1,0:T(8,128)(2,1)S(1)} custom-call(s32[2]{0:T(128)S(1)} %pad_add_fusion.place_ref, bf16[512,1024]{1,0:T(8,128)(2,1)S(1)} %get-tuple-element.105.dz_ref.refs_10_, f32[8,128]{1,0:T(8,128)S(1)} %get-tuple-element.106.refs_0_, bf16[4096,1024]{1,0:T(8,128)(2,1)S(1)} %get-tuple-element.71.refs_2_.refs_3_.refs_5_.refs_0_.refs_1_), custom_call_target="tpu_custom_call" | custom-call | flops 536870912 | bytes 524288 | tf_op jit(solution)/shard_map/d_act/d_act_matmul/pallas_call | solution.py:351
  95.3 2.0 %d_act_matmul.5 = (bf16[128,512]{1,0:T(8,128)(2,1)S(1)}, bf16[128,512]{1,0:T(8,128)(2,1)S(1)}, bf16[128,512]{1,0:T(8,128)(2,1)S(1)}, f32[128,512]{1,0:T(8,128)S(1)}) custom-call(s32[2]{0:T(128)S(1)} %pad_add_fusion.place_ref, bf16[512,1024]{1,0:T(8,128)(2,1)S(1)} %get-tuple-element.95.dz_ref.refs_9_, ...), custom_call_target="tpu_custom_call" | custom-call | flops 536870912 | bytes 524288 | tf_op jit(solution)/shard_map/d_act/d_act_matmul/pallas_call | solution.py:351
  97.3 1.6 %collective-permute-start.38 = (bf16[128,512]{1,0:T(8,128)(2,1)S(1)}, bf16[128,512]{1,0:T(8,128)(2,1)S(1)}, u32[]{:S(2)}, u32[]{:S(2)}) collective-permute-start(bf16[128,512]{1,0:T(8,128)(2,1)S(1)} %get-tuple-element.99), channel_id=1, source_target_pairs={{0,2},{1,3},{2,0},{3,1},{4,6},{5,7},{6,4},{7,5},{8,10},{9,11},{10,... | collective-permute-start | bytes 393224 | tf_op jit(solution)/shard_map/d_act/ppermute | solution.py:24
  99.4 1.5 %collective-permute-start.40 = (bf16[128,512]{1,0:T(8,128)(2,1)S(1)}, bf16[128,512]{1,0:T(8,128)(2,1)S(1)}, u32[]{:S(2)}, u32[]{:S(2)}) collective-permute-start(bf16[128,512]{1,0:T(8,128)(2,1)S(1)} %get-tuple-element.101), channel_id=1, source_target_pairs={{0,6},{1,7},{2,4},{3,5},{4,2},{5,3},{6,0},{7,1},{8,14},{9,15},{10,... | collective-permute-start | bytes 393224 | tf_op jit(solution)/shard_map/d_act/ppermute | solution.py:24
  100.9 2.0 %d_act_matmul.7 = (bf16[144,512]{1,0:T(8,128)(2,1)S(1)}, bf16[144,512]{1,0:T(8,128)(2,1)S(1)}, bf16[144,512]{1,0:T(8,128)(2,1)S(1)}, f32[144,512]{1,0:T(8,128)S(1)}) custom-call(s32[2]{0:T(128)S(1)} %pad_add_fusion.place_ref, bf16[512,1024]{1,0:T(8,128)(2,1)S(1)} %get-tuple-element.105.dz_ref.refs_10_, f32[8,128]{1,0:T(8,128)S(1)} %get-tuple-element.106.refs_0_, ...), custom_call_target="tpu_custom_call" | custom-call | flops 536870912 | bytes 524288 | tf_op jit(solution)/shard_map/d_act/d_act_matmul/pallas_call | solution.py:351
  102.9 1.6 %collective-permute-start.43 = (bf16[144,512]{1,0:T(8,128)(2,1)S(1)}, bf16[144,512]{1,0:T(8,128)(2,1)S(1)}, u32[]{:S(2)}, u32[]{:S(2)}) collective-permute-start(bf16[144,512]{1,0:T(8,128)(2,1)S(1)} %get-tuple-element.107), channel_id=1, source_target_pairs={{0,2},{1,3},{2,0},{3,1},{4,6},{5,7},{6,4},{7,5},{8,10},{9,11},{10,... | collective-permute-start | bytes 442376 | tf_op jit(solution)/shard_map/d_act/ppermute | solution.py:24
  105.0 1.5 %collective-permute-start.45 = (bf16[144,512]{1,0:T(8,128)(2,1)S(1)}, bf16[144,512]{1,0:T(8,128)(2,1)S(1)}, u32[]{:S(2)}, u32[]{:S(2)}) collective-permute-start(bf16[144,512]{1,0:T(8,128)(2,1)S(1)} %get-tuple-element.109), channel_id=1, source_target_pairs={{0,6},{1,7},{2,4},{3,5},{4,2},{5,3},{6,0},{7,1},{8,14},{9,15},{10,... | collective-permute-start | bytes 442376 | tf_op jit(solution)/shard_map/d_act/ppermute | solution.py:24
  106.5 2.9 %weight_gradient.2.refs_11_ = f32[1024,1024]{1,0:T(8,128)} custom-call(s32[2]{0:T(128)S(1)} %pad_add_fusion.place_ref, bf16[256,512]{1,0:T(8,128)(2,1)S(1)} %bitcast.36, bf16[256,512]{1,0:T(8,128)(2,1)S(1)} %collective-permute-done.3.refs_0_.refs_1_, bf16[256,512]{1,0:T(8,128)(2,1)S(1)} %collective-permute-done.5.refs_1_.refs_2_, ...), custom_call_target="tpu_custom_call" | custom-call | flops 1073741824 | bytes 2097152 | tf_op jit(solution)/shard_map/grad_weight/weight_gradient/pallas_call | solution.py:456
  109.4 2.9 %weight_gradient.3 = f32[1024,1024]{1,0:T(8,128)} custom-call(s32[2]{0:T(128)S(1)} %pad_add_fusion.place_ref, bf16[256,512]{1,0:T(8,128)(2,1)S(1)} %collective-permute-done.9.refs_1_.refs_0_, bf16[256,512]{1,0:T(8,128)(2,1)S(1)} %collective-permute-done.4.refs_0_.refs_1_, ...), custom_call_target="tpu_custom_call", output_to_operand_aliasing={{}: (12, {})} | custom-call | flops 1073741824 | bytes 2097152 | tf_op jit(solution)/shard_map/grad_weight/weight_gradient/pallas_call | solution.py:456
  112.3 1.3 %collective-permute-done.44 = bf16[144,512]{1,0:T(8,128)(2,1)S(1)} collective-permute-done((bf16[144,512]{1,0:T(8,128)(2,1)S(1)}, bf16[144,512]{1,0:T(8,128)(2,1)S(1)}, u32[]{:S(2)}, u32[]{:S(2)}) %collective-permute-start.44) | collective-permute-done | bytes 147488 | tf_op jit(solution)/shard_map/d_act/ppermute | solution.py:24
  114.3 2.2 %collective-permute-start.49 = (f32[8,512]{1,0:T(8,128)S(1)}, f32[8,512]{1,0:T(8,128)S(1)}, u32[]{:S(2)}, u32[]{:S(2)}) collective-permute-start(f32[8,512]{1,0:T(8,128)S(1)} %pad_maximum_fusion.1.refs_0_), channel_id=1, source_target_pairs={{0,24},{8,16},{16,8},{24,0},{1,25},{9,17},{17,9},{25,1},{2,26},{10... | collective-permute-start | bytes 49160 | tf_op jit(solution)/shard_map/norm_backward/ppermute | solution.py:24
  116.7 2.0 %collective-permute-start.47 = (f32[8,512]{1,0:T(8,128)S(1)}, f32[8,512]{1,0:T(8,128)S(1)}, u32[]{:S(2)}, u32[]{:S(2)}) collective-permute-start(f32[8,512]{1,0:T(8,128)S(1)} %pad_maximum_fusion.1.refs_0_), channel_id=1, source_target_pairs={{0,8},{8,0},{16,24},{24,16},{1,9},{9,1},{17,25},{25,17},{2,10},{10... | collective-permute-start | bytes 49160 | tf_op jit(solution)/shard_map/norm_backward/ppermute | solution.py:24
  119.9 1.2 %collective-permute-done.48.refs_2_ = f32[8,512]{1,0:T(8,128)S(1)} collective-permute-done((f32[8,512]{1,0:T(8,128)S(1)}, f32[8,512]{1,0:T(8,128)S(1)}, u32[]{:S(2)}, u32[]{:S(2)}) %collective-permute-start.48) | collective-permute-done | bytes 16416 | tf_op jit(solution)/shard_map/norm_backward/ppermute | solution.py:24
  (103 shorter events, 19.8 us)
Async XLA Ops:
  2.8 9.2 %collective-permute-start.2 = (f32[4,512]{1,0:T(4,128)S(1)}, f32[4,512]{1,0:T(4,128)S(1)}, u32[]{:S(2)}, u32[]{:S(2)}) collective-permute-start(f32[4,512]{1,0:T(4,128)S(1)} %pad_maximum_fusion.2), channel_id=1, source_target_pairs={{0,24},{8,16},{16,8},{24,0},{1,25},{9,17},{17,9},{25,1},{2,26},{10... | collective-permute-start | bytes 24584 | tf_op jit(solution)/shard_map/norm_stats/ppermute | solution.py:24
  7.9 4.5 %collective-permute-start.1 = (f32[4,512]{1,0:T(4,128)S(1)}, f32[4,512]{1,0:T(4,128)S(1)}, u32[]{:S(2)}, u32[]{:S(2)}) collective-permute-start(f32[4,512]{1,0:T(4,128)S(1)} %pad_maximum_fusion.2), channel_id=1, source_target_pairs={{0,16},{8,24},{16,0},{24,8},{1,17},{9,25},{17,1},{25,9},{2,18},{10... | collective-permute-start | bytes 24584 | tf_op jit(solution)/shard_map/norm_stats/ppermute | solution.py:24
  7.9 4.5 %collective-permute-start = (f32[4,512]{1,0:T(4,128)S(1)}, f32[4,512]{1,0:T(4,128)S(1)}, u32[]{:S(2)}, u32[]{:S(2)}) collective-permute-start(f32[4,512]{1,0:T(4,128)S(1)} %pad_maximum_fusion.2), channel_id=1, source_target_pairs={{0,8},{8,0},{16,24},{24,16},{1,9},{9,1},{17,25},{25,17},{2,10},{10... | collective-permute-start | bytes 24584 | tf_op jit(solution)/shard_map/norm_stats/ppermute | solution.py:24
  12.8 3.6 %collective-permute-start.9 = (bf16[256,512]{1,0:T(8,128)(2,1)S(1)}, bf16[256,512]{1,0:T(8,128)(2,1)S(1)}, u32[]{:S(2)}, u32[]{:S(2)}) collective-permute-start(bf16[256,512]{1,0:T(8,128)(2,1)S(1)} %bitcast.30), channel_id=1, source_target_pairs={{0,1},{1,0},{2,3},{3,2},{4,5},{5,4},{6,7},{7,6},{8,9},{9,8},{10,11... | collective-permute-start | bytes 786440 | tf_op jit(solution)/shard_map/act_gather/ppermute | solution.py:24
  12.9 10.1 %collective-permute-start.7 = (bf16[256,512]{1,0:T(8,128)(2,1)S(1)}, bf16[256,512]{1,0:T(8,128)(2,1)S(1)}, u32[]{:S(2)}, u32[]{:S(2)}) collective-permute-start(bf16[256,512]{1,0:T(8,128)(2,1)S(1)} %bitcast.31), channel_id=1, source_target_pairs={{0,6},{1,7},{2,4},{3,5},{4,2},{5,3},{6,0},{7,1},{8,14},{9,15},{10,... | collective-permute-start | bytes 786440 | tf_op jit(solution)/shard_map/act_gather/ppermute | solution.py:24
  15.4 12.7 %collective-permute-start.5 = (bf16[256,512]{1,0:T(8,128)(2,1)S(1)}, bf16[256,512]{1,0:T(8,128)(2,1)S(1)}, u32[]{:S(2)}, u32[]{:S(2)}) collective-permute-start(bf16[256,512]{1,0:T(8,128)(2,1)S(1)} %bitcast.32), channel_id=1, source_target_pairs={{0,4},{1,5},{2,6},{3,7},{4,0},{5,1},{6,2},{7,3},{8,12},{9,13},{10,... | collective-permute-start | bytes 786440 | tf_op jit(solution)/shard_map/act_gather/ppermute | solution.py:24
  15.9 12.3 %collective-permute-start.3 = (bf16[256,512]{1,0:T(8,128)(2,1)S(1)}, bf16[256,512]{1,0:T(8,128)(2,1)S(1)}, u32[]{:S(2)}, u32[]{:S(2)}) collective-permute-start(bf16[256,512]{1,0:T(8,128)(2,1)S(1)} %bitcast.33), channel_id=1, source_target_pairs={{0,2},{1,3},{2,0},{3,1},{4,6},{5,7},{6,4},{7,5},{8,10},{9,11},{10,... | collective-permute-start | bytes 786440 | tf_op jit(solution)/shard_map/act_gather/ppermute | solution.py:24
  16.5 13.7 %collective-permute-start.12 = (bf16[128,512]{1,0:T(8,128)(2,1)S(1)}, bf16[128,512]{1,0:T(8,128)(2,1)S(1)}, u32[]{:S(2)}, u32[]{:S(2)}) collective-permute-start(bf16[128,512]{1,0:T(8,128)(2,1)S(1)} %slice_bitcast_fusion.1), channel_id=1, source_target_pairs={{0,16},{16,24},{24,8},{8,0},{1,17},{17,25},{25,9},{9,1},{2,18},{18... | collective-permute-start | bytes 393224 | tf_op jit(solution)/shard_map/act_gather/ppermute | solution.py:34
  18.5 11.8 %collective-permute-start.13 = (bf16[128,512]{1,0:T(8,128)(2,1)S(1)}, bf16[128,512]{1,0:T(8,128)(2,1)S(1)}, u32[]{:S(2)}, u32[]{:S(2)}) collective-permute-start(bf16[128,512]{1,0:T(8,128)(2,1)S(1)} %slice_bitcast_fusion.1), channel_id=1, source_target_pairs={{0,24},{16,8},{24,0},{8,16},{1,25},{17,9},{25,1},{9,17},{2,26},{18... | collective-permute-start | bytes 393224 | tf_op jit(solution)/shard_map/act_gather/ppermute | solution.py:34
  23.0 8.6 %collective-permute-start.10 = (bf16[128,512]{1,0:T(8,128)(2,1)S(1)}, bf16[128,512]{1,0:T(8,128)(2,1)S(1)}, u32[]{:S(2)}, u32[]{:S(2)}) collective-permute-start(bf16[128,512]{1,0:T(8,128)(2,1)S(1)} %slice_bitcast_fusion.1), channel_id=1, source_target_pairs={{0,8},{16,0},{24,16},{8,24},{1,9},{17,1},{25,17},{9,25},{2,10},{18... | collective-permute-start | bytes 393224 | tf_op jit(solution)/shard_map/act_gather/ppermute | solution.py:34
  28.1 6.5 %collective-permute-start.8 = (bf16[256,512]{1,0:T(8,128)(2,1)S(1)}, bf16[256,512]{1,0:T(8,128)(2,1)S(1)}, u32[]{:S(2)}, u32[]{:S(2)}) collective-permute-start(bf16[256,512]{1,0:T(8,128)(2,1)S(1)} %collective-permute-done.7.refs_2_.refs_3_), channel_id=1, source_target_pairs={{0,1},{1,0},{2,3},{3,2},{4,5},{5,4},{6,7},{7,6},{8,9},{9,8},{10,11... | collective-permute-start | bytes 786440 | tf_op jit(solution)/shard_map/act_gather/ppermute | solution.py:24
  28.2 6.4 %collective-permute-start.6 = (bf16[256,512]{1,0:T(8,128)(2,1)S(1)}, bf16[256,512]{1,0:T(8,128)(2,1)S(1)}, u32[]{:S(2)}, u32[]{:S(2)}) collective-permute-start(bf16[256,512]{1,0:T(8,128)(2,1)S(1)} %collective-permute-done.5.refs_1_.refs_2_), channel_id=1, source_target_pairs={{0,1},{1,0},{2,3},{3,2},{4,5},{5,4},{6,7},{7,6},{8,9},{9,8},{10,11... | collective-permute-start | bytes 786440 | tf_op jit(solution)/shard_map/act_gather/ppermute | solution.py:24
  30.2 4.5 %collective-permute-start.4 = (bf16[256,512]{1,0:T(8,128)(2,1)S(1)}, bf16[256,512]{1,0:T(8,128)(2,1)S(1)}, u32[]{:S(2)}, u32[]{:S(2)}) collective-permute-start(bf16[256,512]{1,0:T(8,128)(2,1)S(1)} %collective-permute-done.3.refs_0_.refs_1_), channel_id=1, source_target_pairs={{0,1},{1,0},{2,3},{3,2},{4,5},{5,4},{6,7},{7,6},{8,9},{9,8},{10,11... | collective-permute-start | bytes 786440 | tf_op jit(solution)/shard_map/act_gather/ppermute | solution.py:24
  31.6 11.1 %collective-permute-start.15 = (bf16[384,512]{1,0:T(8,128)(2,1)S(1)}, bf16[384,512]{1,0:T(8,128)(2,1)S(1)}, u32[]{:S(2)}, u32[]{:S(2)}) collective-permute-start(bf16[384,512]{1,0:T(8,128)(2,1)S(1)} %constant_dynamic-update-slice_fusion.refs_0_.refs_4_), channel_id=1, source_target_pairs={{0,4},{1,5},{2,6},{3,7},{4,0},{5,1},{6,2},{7,3},{8,12},{9,13},{10,... | collective-permute-start | bytes 1179656 | tf_op jit(solution)/shard_map/z/ppermute | solution.py:24
  33.2 11.1 %collective-permute-start.14 = (bf16[384,512]{1,0:T(8,128)(2,1)S(1)}, bf16[384,512]{1,0:T(8,128)(2,1)S(1)}, u32[]{:S(2)}, u32[]{:S(2)}) collective-permute-start(bf16[384,512]{1,0:T(8,128)(2,1)S(1)} %constant_dynamic-update-slice_fusion.refs_0_.refs_4_), channel_id=1, source_target_pairs={{0,2},{1,3},{2,0},{3,1},{4,6},{5,7},{6,4},{7,5},{8,10},{9,11},{10,... | collective-permute-start | bytes 1179656 | tf_op jit(solution)/shard_map/z/ppermute | solution.py:24
  36.2 9.7 %collective-permute-start.11 = (bf16[128,1024]{1,0:T(8,128)(2,1)S(1)}, bf16[128,1024]{1,0:T(8,128)(2,1)S(1)}, u32[]{:S(2)}, u32[]{:S(2)}) collective-permute-start(bf16[128,1024]{1,0:T(8,128)(2,1)S(1)} %get-tuple-element.75.refs_0_.refs_12_.refs_8_), channel_id=1, source_target_pairs={{0,16},{16,24},{24,8},{8,0},{1,17},{17,25},{25,9},{9,1},{2,18},{18... | collective-permute-start | bytes 786440 | tf_op jit(solution)/shard_map/z_ring/ppermute | solution.py:34
  42.7 6.9 %collective-permute-start.16 = (bf16[192,512]{1,0:T(8,128)(2,1)S(1)}, bf16[192,512]{1,0:T(8,128)(2,1)S(1)}, u32[]{:S(2)}, u32[]{:S(2)}) collective-permute-start(bf16[192,512]{1,0:T(8,128)(2,1)S(1)} %slice.149), channel_id=1, source_target_pairs={{0,2},{1,3},{2,0},{3,1},{4,6},{5,7},{6,4},{7,5},{8,10},{9,11},{10,... | collective-permute-start | bytes 589832 | tf_op jit(solution)/shard_map/z/ppermute | solution.py:24
  44.3 5.8 %collective-permute-start.17 = (bf16[192,512]{1,0:T(8,128)(2,1)S(1)}, bf16[192,512]{1,0:T(8,128)(2,1)S(1)}, u32[]{:S(2)}, u32[]{:S(2)}) collective-permute-start(bf16[192,512]{1,0:T(8,128)(2,1)S(1)} %slice.150), channel_id=1, source_target_pairs={{0,4},{1,5},{2,6},{3,7},{4,0},{5,1},{6,2},{7,3},{8,12},{9,13},{10,... | collective-permute-start | bytes 589832 | tf_op jit(solution)/shard_map/z/ppermute | solution.py:24
  45.9 6.8 %collective-permute-start.18 = (bf16[128,1024]{1,0:T(8,128)(2,1)S(1)}, bf16[128,1024]{1,0:T(8,128)(2,1)S(1)}, u32[]{:S(2)}, u32[]{:S(2)}) collective-permute-start(bf16[128,1024]{1,0:T(8,128)(2,1)S(1)} %collective-permute-done.11.refs_1_.refs_13_.refs_9_), channel_id=1, source_target_pairs={{0,16},{16,24},{24,8},{8,0},{1,17},{17,25},{25,9},{9,1},{2,18},{18... | collective-permute-start | bytes 786440 | tf_op jit(solution)/shard_map/z_ring/ppermute | solution.py:34
  47.1 7.6 %collective-permute-start.20 = (bf16[384,512]{1,0:T(8,128)(2,1)S(1)}, bf16[384,512]{1,0:T(8,128)(2,1)S(1)}, u32[]{:S(2)}, u32[]{:S(2)}) collective-permute-start(bf16[384,512]{1,0:T(8,128)(2,1)S(1)} %constant_dynamic-update-slice_fusion.refs_0_.refs_4_), channel_id=1, source_target_pairs={{0,1},{1,0},{2,3},{3,2},{4,5},{5,4},{6,7},{7,6},{8,9},{9,8},{10,11... | collective-permute-start | bytes 1179656 | tf_op jit(solution)/shard_map/z_far/ppermute | solution.py:24
  47.1 8.3 %collective-permute-start.21 = (bf16[384,512]{1,0:T(8,128)(2,1)S(1)}, bf16[384,512]{1,0:T(8,128)(2,1)S(1)}, u32[]{:S(2)}, u32[]{:S(2)}) collective-permute-start(bf16[384,512]{1,0:T(8,128)(2,1)S(1)} %collective-permute-done.14.refs_1_.refs_5_), channel_id=1, source_target_pairs={{0,1},{1,0},{2,3},{3,2},{4,5},{5,4},{6,7},{7,6},{8,9},{9,8},{10,11... | collective-permute-start | bytes 1179656 | tf_op jit(solution)/shard_map/z_far/ppermute | solution.py:24
  49.6 5.9 %collective-permute-start.22 = (bf16[384,512]{1,0:T(8,128)(2,1)S(1)}, bf16[384,512]{1,0:T(8,128)(2,1)S(1)}, u32[]{:S(2)}, u32[]{:S(2)}) collective-permute-start(bf16[384,512]{1,0:T(8,128)(2,1)S(1)} %collective-permute-done.15.refs_2_.refs_6_), channel_id=1, source_target_pairs={{0,1},{1,0},{2,3},{3,2},{4,5},{5,4},{6,7},{7,6},{8,9},{9,8},{10,11... | collective-permute-start | bytes 1179656 | tf_op jit(solution)/shard_map/z_far/ppermute | solution.py:24
  52.7 2.8 %collective-permute-start.23 = (bf16[384,512]{1,0:T(8,128)(2,1)S(1)}, bf16[384,512]{1,0:T(8,128)(2,1)S(1)}, u32[]{:S(2)}, u32[]{:S(2)}) collective-permute-start(bf16[384,512]{1,0:T(8,128)(2,1)S(1)} %pad_maximum_fusion.refs_3_.refs_7_), channel_id=1, source_target_pairs={{0,1},{1,0},{2,3},{3,2},{4,5},{5,4},{6,7},{7,6},{8,9},{9,8},{10,11... | collective-permute-start | bytes 1179656 | tf_op jit(solution)/shard_map/z_far/ppermute | solution.py:24
  52.7 9.1 %collective-permute-start.19 = (bf16[128,1024]{1,0:T(8,128)(2,1)S(1)}, bf16[128,1024]{1,0:T(8,128)(2,1)S(1)}, u32[]{:S(2)}, u32[]{:S(2)}) collective-permute-start(bf16[128,1024]{1,0:T(8,128)(2,1)S(1)} %collective-permute-done.18.refs_2_.refs_14_.refs_10_), channel_id=1, source_target_pairs={{0,16},{16,24},{24,8},{8,0},{1,17},{17,25},{25,9},{9,1},{2,18},{18... | collective-permute-start | bytes 786440 | tf_op jit(solution)/shard_map/z_far/ppermute | solution.py:34
  54.7 9.5 %collective-permute-start.24 = (bf16[128,512]{1,0:T(8,128)(2,1)S(1)}, bf16[128,512]{1,0:T(8,128)(2,1)S(1)}, u32[]{:S(2)}, u32[]{:S(2)}) collective-permute-start(bf16[128,512]{1,0:T(8,128)(2,1)S(1)} %get-tuple-element.91), channel_id=1, source_target_pairs={{0,16},{16,24},{24,8},{8,0},{1,17},{17,25},{25,9},{9,1},{2,18},{18... | collective-permute-start | bytes 393224 | tf_op jit(solution)/shard_map/kernel/ppermute | solution.py:34
  66.0 5.8 %collective-permute-start.26 = (bf16[32,1280]{1,0:T(8,128)(2,1)S(1)}, bf16[32,1280]{1,0:T(8,128)(2,1)S(1)}, u32[]{:S(2)}, u32[]{:S(2)}) collective-permute-start(bf16[32,1280]{1,0:T(8,128)(2,1)S(1)} %get-tuple-element.134), channel_id=1, source_target_pairs={{0,2},{1,3},{2,0},{3,1},{4,6},{5,7},{6,4},{7,5},{8,10},{9,11},{10,... | collective-permute-start | bytes 245768 | tf_op jit(solution)/shard_map/kernel/ppermute | solution.py:24
  66.7 5.7 %collective-permute-start.28 = (bf16[32,1280]{1,0:T(8,128)(2,1)S(1)}, bf16[32,1280]{1,0:T(8,128)(2,1)S(1)}, u32[]{:S(2)}, u32[]{:S(2)}) collective-permute-start(bf16[32,1280]{1,0:T(8,128)(2,1)S(1)} %get-tuple-element.135), channel_id=1, source_target_pairs={{0,6},{1,7},{2,4},{3,5},{4,2},{5,3},{6,0},{7,1},{8,14},{9,15},{10,... | collective-permute-start | bytes 245768 | tf_op jit(solution)/shard_map/kernel/ppermute | solution.py:24
  68.2 5.5 %collective-permute-start.27 = (bf16[32,1280]{1,0:T(8,128)(2,1)S(1)}, bf16[32,1280]{1,0:T(8,128)(2,1)S(1)}, u32[]{:S(2)}, u32[]{:S(2)}) collective-permute-start(bf16[32,1280]{1,0:T(8,128)(2,1)S(1)} %get-tuple-element.136), channel_id=1, source_target_pairs={{0,4},{1,5},{2,6},{3,7},{4,0},{5,1},{6,2},{7,3},{8,12},{9,13},{10,... | collective-permute-start | bytes 245768 | tf_op jit(solution)/shard_map/kernel/ppermute | solution.py:24
  69.5 7.8 %collective-permute-start.31 = (bf16[128,512]{1,0:T(8,128)(2,1)S(1)}, bf16[128,512]{1,0:T(8,128)(2,1)S(1)}, u32[]{:S(2)}, u32[]{:S(2)}) collective-permute-start(bf16[128,512]{1,0:T(8,128)(2,1)S(1)} %get-tuple-element.93), channel_id=1, source_target_pairs={{0,24},{16,8},{24,0},{8,16},{1,25},{17,9},{25,1},{9,17},{2,26},{18... | collective-permute-start | bytes 393224 | tf_op jit(solution)/shard_map/kernel/ppermute | solution.py:34
  73.7 5.1 %collective-permute-start.30 = (bf16[32,1280]{1,0:T(8,128)(2,1)S(1)}, bf16[32,1280]{1,0:T(8,128)(2,1)S(1)}, u32[]{:S(2)}, u32[]{:S(2)}) collective-permute-start(bf16[32,1280]{1,0:T(8,128)(2,1)S(1)} %get-tuple-element.128.refs_0_), channel_id=1, source_target_pairs={{0,2},{1,3},{2,0},{3,1},{4,6},{5,7},{6,4},{7,5},{8,10},{9,11},{10,... | collective-permute-start | bytes 245768 | tf_op jit(solution)/shard_map/kernel/ppermute | solution.py:24
  74.9 5.6 %collective-permute-start.35 = (bf16[32,1280]{1,0:T(8,128)(2,1)S(1)}, bf16[32,1280]{1,0:T(8,128)(2,1)S(1)}, u32[]{:S(2)}, u32[]{:S(2)}) collective-permute-start(bf16[32,1280]{1,0:T(8,128)(2,1)S(1)} %get-tuple-element.128.refs_0_), channel_id=1, source_target_pairs={{0,6},{1,7},{2,4},{3,5},{4,2},{5,3},{6,0},{7,1},{8,14},{9,15},{10,... | collective-permute-start | bytes 245768 | tf_op jit(solution)/shard_map/kernel/ppermute | solution.py:24
  76.5 4.8 %collective-permute-start.33 = (bf16[32,1280]{1,0:T(8,128)(2,1)S(1)}, bf16[32,1280]{1,0:T(8,128)(2,1)S(1)}, u32[]{:S(2)}, u32[]{:S(2)}) collective-permute-start(bf16[32,1280]{1,0:T(8,128)(2,1)S(1)} %get-tuple-element.128.refs_0_), channel_id=1, source_target_pairs={{0,4},{1,5},{2,6},{3,7},{4,0},{5,1},{6,2},{7,3},{8,12},{9,13},{10,... | collective-permute-start | bytes 245768 | tf_op jit(solution)/shard_map/kernel/ppermute | solution.py:24
  77.3 6.5 %collective-permute-start.29 = (bf16[32,1280]{1,0:T(8,128)(2,1)S(1)}, bf16[32,1280]{1,0:T(8,128)(2,1)S(1)}, u32[]{:S(2)}, u32[]{:S(2)}) collective-permute-start(bf16[32,1280]{1,0:T(8,128)(2,1)S(1)} %get-tuple-element.128.refs_0_), channel_id=1, source_target_pairs={{0,1},{1,0},{2,3},{3,2},{4,5},{5,4},{6,7},{7,6},{8,9},{9,8},{10,11... | collective-permute-start | bytes 245768 | tf_op jit(solution)/shard_map/kernel/ppermute | solution.py:24
  80.5 3.3 %collective-permute-start.36 = (bf16[32,1280]{1,0:T(8,128)(2,1)S(1)}, bf16[32,1280]{1,0:T(8,128)(2,1)S(1)}, u32[]{:S(2)}, u32[]{:S(2)}) collective-permute-start(bf16[32,1280]{1,0:T(8,128)(2,1)S(1)} %collective-permute-done.35.refs_6_), channel_id=1, source_target_pairs={{0,1},{1,0},{2,3},{3,2},{4,5},{5,4},{6,7},{7,6},{8,9},{9,8},{10,11... | collective-permute-start | bytes 245768 | tf_op jit(solution)/shard_map/kernel/ppermute | solution.py:24
  81.3 2.5 %collective-permute-start.32 = (bf16[32,1280]{1,0:T(8,128)(2,1)S(1)}, bf16[32,1280]{1,0:T(8,128)(2,1)S(1)}, u32[]{:S(2)}, u32[]{:S(2)}) collective-permute-start(bf16[32,1280]{1,0:T(8,128)(2,1)S(1)} %collective-permute-done.30.refs_2_), channel_id=1, source_target_pairs={{0,1},{1,0},{2,3},{3,2},{4,5},{5,4},{6,7},{7,6},{8,9},{9,8},{10,11... | collective-permute-start | bytes 245768 | tf_op jit(solution)/shard_map/kernel/ppermute | solution.py:24
  81.8 10.6 %collective-permute-start.41 = (bf16[128,512]{1,0:T(8,128)(2,1)S(1)}, bf16[128,512]{1,0:T(8,128)(2,1)S(1)}, u32[]{:S(2)}, u32[]{:S(2)}) collective-permute-start(bf16[128,512]{1,0:T(8,128)(2,1)S(1)} %get-tuple-element.104), channel_id=1, source_target_pairs={{0,8},{16,0},{24,16},{8,24},{1,9},{17,1},{25,17},{9,25},{2,10},{18... | collective-permute-start | bytes 393224 | tf_op jit(solution)/shard_map/kernel/ppermute | solution.py:34
  92.4 2.8 %collective-permute-start.37 = (bf16[4,128,512]{2,1,0:T(8,128)(2,1)S(1)}, bf16[4,128,512]{2,1,0:T(8,128)(2,1)S(1)}, u32[]{:S(2)}, u32[]{:S(2)}) collective-permute-start(bf16[4,128,512]{2,1,0:T(8,128)(2,1)S(1)} %d_act_matmul.4), channel_id=1, source_target_pairs={{0,1},{1,0},{2,3},{3,2},{4,5},{5,4},{6,7},{7,6},{8,9},{9,8},{10,11... | collective-permute-start | bytes 1572872 | tf_op jit(solution)/shard_map/d_act/ppermute | solution.py:24
  94.5 6.3 %collective-permute-start.42 = (bf16[4,144,512]{2,1,0:T(8,128)(2,1)S(1)}, bf16[4,144,512]{2,1,0:T(8,128)(2,1)S(1)}, u32[]{:S(2)}, u32[]{:S(2)}) collective-permute-start(bf16[4,144,512]{2,1,0:T(8,128)(2,1)S(1)} %d_act_matmul.6), channel_id=1, source_target_pairs={{0,1},{1,0},{2,3},{3,2},{4,5},{5,4},{6,7},{7,6},{8,9},{9,8},{10,11... | collective-permute-start | bytes 1769480 | tf_op jit(solution)/shard_map/d_act/ppermute | solution.py:24
  95.2 9.3 %collective-permute-start.46 = (bf16[384,512]{1,0:T(8,128)(2,1)S(1)}, bf16[384,512]{1,0:T(8,128)(2,1)S(1)}, u32[]{:S(2)}, u32[]{:S(2)}) collective-permute-start(bf16[384,512]{1,0:T(8,128)(2,1)S(1)} %constant_dynamic-update-slice_fusion.3.refs_8_), channel_id=1, source_target_pairs={{0,1},{1,0},{2,3},{3,2},{4,5},{5,4},{6,7},{7,6},{8,9},{9,8},{10,11... | collective-permute-start | bytes 1179656 | tf_op jit(solution)/shard_map/grad_weight/ppermute | solution.py:24
  97.3 7.7 %collective-permute-start.38 = (bf16[128,512]{1,0:T(8,128)(2,1)S(1)}, bf16[128,512]{1,0:T(8,128)(2,1)S(1)}, u32[]{:S(2)}, u32[]{:S(2)}) collective-permute-start(bf16[128,512]{1,0:T(8,128)(2,1)S(1)} %get-tuple-element.99), channel_id=1, source_target_pairs={{0,2},{1,3},{2,0},{3,1},{4,6},{5,7},{6,4},{7,5},{8,10},{9,11},{10,... | collective-permute-start | bytes 393224 | tf_op jit(solution)/shard_map/d_act/ppermute | solution.py:24
  98.9 13.4 %collective-permute-start.39 = (bf16[128,512]{1,0:T(8,128)(2,1)S(1)}, bf16[128,512]{1,0:T(8,128)(2,1)S(1)}, u32[]{:S(2)}, u32[]{:S(2)}) collective-permute-start(bf16[128,512]{1,0:T(8,128)(2,1)S(1)} %get-tuple-element.100), channel_id=1, source_target_pairs={{0,4},{1,5},{2,6},{3,7},{4,0},{5,1},{6,2},{7,3},{8,12},{9,13},{10,... | collective-permute-start | bytes 393224 | tf_op jit(solution)/shard_map/d_act/ppermute | solution.py:24
  99.4 12.9 %collective-permute-start.40 = (bf16[128,512]{1,0:T(8,128)(2,1)S(1)}, bf16[128,512]{1,0:T(8,128)(2,1)S(1)}, u32[]{:S(2)}, u32[]{:S(2)}) collective-permute-start(bf16[128,512]{1,0:T(8,128)(2,1)S(1)} %get-tuple-element.101), channel_id=1, source_target_pairs={{0,6},{1,7},{2,4},{3,5},{4,2},{5,3},{6,0},{7,1},{8,14},{9,15},{10,... | collective-permute-start | bytes 393224 | tf_op jit(solution)/shard_map/d_act/ppermute | solution.py:24
  102.9 9.4 %collective-permute-start.43 = (bf16[144,512]{1,0:T(8,128)(2,1)S(1)}, bf16[144,512]{1,0:T(8,128)(2,1)S(1)}, u32[]{:S(2)}, u32[]{:S(2)}) collective-permute-start(bf16[144,512]{1,0:T(8,128)(2,1)S(1)} %get-tuple-element.107), channel_id=1, source_target_pairs={{0,2},{1,3},{2,0},{3,1},{4,6},{5,7},{6,4},{7,5},{8,10},{9,11},{10,... | collective-permute-start | bytes 442376 | tf_op jit(solution)/shard_map/d_act/ppermute | solution.py:24
  104.5 9.1 %collective-permute-start.44 = (bf16[144,512]{1,0:T(8,128)(2,1)S(1)}, bf16[144,512]{1,0:T(8,128)(2,1)S(1)}, u32[]{:S(2)}, u32[]{:S(2)}) collective-permute-start(bf16[144,512]{1,0:T(8,128)(2,1)S(1)} %get-tuple-element.108), channel_id=1, source_target_pairs={{0,4},{1,5},{2,6},{3,7},{4,0},{5,1},{6,2},{7,3},{8,12},{9,13},{10,... | collective-permute-start | bytes 442376 | tf_op jit(solution)/shard_map/d_act/ppermute | solution.py:24
  105.0 8.6 %collective-permute-start.45 = (bf16[144,512]{1,0:T(8,128)(2,1)S(1)}, bf16[144,512]{1,0:T(8,128)(2,1)S(1)}, u32[]{:S(2)}, u32[]{:S(2)}) collective-permute-start(bf16[144,512]{1,0:T(8,128)(2,1)S(1)} %get-tuple-element.109), channel_id=1, source_target_pairs={{0,6},{1,7},{2,4},{3,5},{4,2},{5,3},{6,0},{7,1},{8,14},{9,15},{10,... | collective-permute-start | bytes 442376 | tf_op jit(solution)/shard_map/d_act/ppermute | solution.py:24
  114.3 5.6 %collective-permute-start.49 = (f32[8,512]{1,0:T(8,128)S(1)}, f32[8,512]{1,0:T(8,128)S(1)}, u32[]{:S(2)}, u32[]{:S(2)}) collective-permute-start(f32[8,512]{1,0:T(8,128)S(1)} %pad_maximum_fusion.1.refs_0_), channel_id=1, source_target_pairs={{0,24},{8,16},{16,8},{24,0},{1,25},{9,17},{17,9},{25,1},{2,26},{10... | collective-permute-start | bytes 49160 | tf_op jit(solution)/shard_map/norm_backward/ppermute | solution.py:24
  116.5 4.6 %collective-permute-start.48 = (f32[8,512]{1,0:T(8,128)S(1)}, f32[8,512]{1,0:T(8,128)S(1)}, u32[]{:S(2)}, u32[]{:S(2)}) collective-permute-start(f32[8,512]{1,0:T(8,128)S(1)} %pad_maximum_fusion.1.refs_0_), channel_id=1, source_target_pairs={{0,16},{8,24},{16,0},{24,8},{1,17},{9,25},{17,1},{25,9},{2,18},{10... | collective-permute-start | bytes 49160 | tf_op jit(solution)/shard_map/norm_backward/ppermute | solution.py:24
  116.7 4.4 %collective-permute-start.47 = (f32[8,512]{1,0:T(8,128)S(1)}, f32[8,512]{1,0:T(8,128)S(1)}, u32[]{:S(2)}, u32[]{:S(2)}) collective-permute-start(f32[8,512]{1,0:T(8,128)S(1)} %pad_maximum_fusion.1.refs_0_), channel_id=1, source_target_pairs={{0,8},{8,0},{16,24},{24,16},{1,9},{9,1},{17,25},{25,17},{2,10},{10... | collective-permute-start | bytes 49160 | tf_op jit(solution)/shard_map/norm_backward/ppermute | solution.py:24
  (5 other events, 33.3 us)

commit v16 on v14

--- a/solution.py
+++ b/solution.py
@@ -283,50 +283,44 @@
     return rows[0:1].astype(f32) + rows[1:2].astype(f32) + rows[2:3].astype(f32)
 
 
-def d_act_kernel(count, adds, place_ref, dz_ref, share_ref, w_ref, *refs):
-    local_rows, columns = dz_ref.shape[1] // adds[1], dz_ref.shape[2]
-    tall = 2 * local_rows
+def d_act_kernel(ks, adds, tall, width, place_ref, dz_ref, share_ref, w_ref, *refs):
+    local_rows = tall // 2
     dz = jnp.concatenate([dz_ref[0, :local_rows], dz_ref[1, :local_rows]], axis=0)
-    width = w_ref.shape[0] // adds[2]
     share = share_ref[0:1, 0:1]
-    for j in range(count):
-        k = 2 * ((j + 1) % count) if adds[0] else 2 * j + 1
+    for j, k in enumerate(ks):
         part = lax.dot_general(
             dz,
             weight_rows(place_ref, w_ref, k, width),
             (((1,), (1,)), ((), ())),
             preferred_element_type=f32,
         )
-        if not adds[0]:
-            refs[0][j, :tall] = part.astype(refs[0].dtype)
-            refs[0][j, tall:] = share_rows(share, width, refs[0].dtype)
-        else:
-            got = refs[0]
-            out_ref = refs[j + 1]
-            slot = (j + 1) % count
-            out_ref[:tall] = (part + got[slot, :tall].astype(f32)).astype(out_ref.dtype)
-            whole_share = share + share_of(got[slot, tall:])[:, 0:1]
-            out_ref[tall:] = share_rows(whole_share, width, out_ref.dtype)
-
-
-def d_act_call(place, dz, share, weight, n_batch, n_col, got):
-    columns = weight.shape[1]
+        whole_share = share
+        out = refs[j + 1] if adds else refs[0].at[j]
+        if adds:
+            part = part + refs[0][j, :tall].astype(f32)
+            whole_share = share + share_of(refs[0][j, tall:])[:, 0:1]
+        out[:tall] = part.astype(out.dtype)
+        out[tall:] = share_rows(whole_share, width, out.dtype)
+
+
+def d_act_call(place, dz, share, weight, n_batch, n_col, ks, got):
     width = weight.shape[0] // n_col
     tall = 2 * dz.shape[1] // n_batch
-    count = n_col // 2
-    operands = [place, dz, share, weight] + ([] if got is None else [got])
+    columns = weight.shape[1]
+    long = tall + EXTRA
+    operands = [place, dz, share, weight]
     if got is None:
-        out_shape = (jax.ShapeDtypeStruct((count, tall + EXTRA, width), bf16),)
+        out_shape = (jax.ShapeDtypeStruct((len(ks), long, width), bf16),)
     else:
-        out_shape = (jax.ShapeDtypeStruct((tall + EXTRA, width), bf16),) * (count - 1)
-        out_shape += (jax.ShapeDtypeStruct((tall + EXTRA, width), f32),)
-    return pl.pallas_call(
-        functools.partial(d_act_kernel, count, (got is not None, n_batch, n_col)),
+        operands.append(got)
+        out_shape = tuple(jax.ShapeDtypeStruct((long, width), bf16 if k else f32) for k in ks)
+    return pl.pallas_call(
+        functools.partial(d_act_kernel, tuple(ks), got is not None, tall, width),
         out_shape=out_shape,
         in_specs=[IN_SMEM] + [IN_VMEM] * (len(operands) - 1),
         out_specs=(IN_VMEM,) * len(out_shape),
         compiler_params=params(8),
-        cost_estimate=cost(2 * tall * width * columns * count, 2 * count * width * tall),
+        cost_estimate=cost(2 * tall * width * columns * len(ks), 2 * len(ks) * width * tall),
         name="d_act_matmul",
     )(*operands)
 
@@ -605,10 +599,22 @@
         dz, share = dz_call(place, strip, [strips[k] for k in range(n_col)], slots, constants)
         dz, blocks[2 * third :] = lax.optimization_barrier((dz, blocks[2 * third :]))
     with jax.named_scope("d_act"):
-        (away,) = d_act_call(place, dz, share, held_weight, n_batch, n_col, None)
-        got = xor_send(away, "col", 1)
-        *sends, d_act = d_act_call(place, dz, share, held_weight, n_batch, n_col, got)
-        arrived = [xor_send(part, "col", k) for k, part in zip(far, sends)]
+        crossing = [k for k in far if k & (k - 1)]
+        groups = [crossing, [k for k in far if k not in crossing] + [0]]
+        got = []
+        for ks in groups:
+            (away,) = d_act_call(
+                place, dz, share, held_weight, n_batch, n_col, [k + 1 for k in ks], None
+            )
+            away, share = lax.optimization_barrier((away, share))
+            got.append(xor_send(away, "col", 1))
+        arrived = {}
+        for ks, part in zip(groups, got):
+            summed = d_act_call(place, dz, share, held_weight, n_batch, n_col, ks, part)
+            for k, piece in zip(ks, summed):
+                arrived[k] = xor_send(piece, "col", k) if k else piece
+        d_act = arrived.pop(0)
+        arrived = [arrived[k] for k in far]
     with jax.named_scope("grad_weight"):
         grad_weight = None
         for block in range(n_col // n_batch // 2):

time: 120 us -> 120 us (level)
  waiting for transfers between devices: 39.2 us -> 37.6 us
  Pallas kernels: 30.7 us -> 32.2 us
    ppermute x37 -> x38, waiting for transfers between devices: 31.8 us -> 30.1 us  [xor_send(): return lax.ppermute(x, axis, [(i, i ^ k) for i in range(n)])]
    pallas_call x2 -> x4, Pallas kernels: 3.68 us -> 5.17 us  [d_act_call(): pl.pallas_call(functools.partial(d_act_kernel, tuple(ks), got is not None...]
    ppermute x37 -> x38, starting transfers between devices: 33.3 us -> 33.4 us  [xor_send(): return lax.ppermute(x, axis, [(i, i ^ k) for i in range(n)])]
  transfers between devices with their start and end apart: 46 -> 47, of which waited for: 20 -> 19; matrix products, arithmetic and copies ran while one was open for 0% -> 0% of each run, Pallas kernels for 23% -> 24%
where the time goes in v16:
time: 120 us
  starting transfers between devices  45.5 us (38%)
  waiting for transfers between devices  37.6 us (31%)
  Pallas kernels  32.2 us (27%)
  other arithmetic  3.21 us (3%)
    ppermute x38, starting transfers between devices, xor_send(): return lax.ppermute(x, axis, [(i, i ^ k) for i in range(n)])  33.4 us
    ppermute x38, waiting for transfers between devices, xor_send(): return lax.ppermute(x, axis, [(i, i ^ k) for i in range(n)])  30.1 us
    ppermute x9, starting transfers between devices, ring_send(): lax.ppermute(x, axis, [(order[i], order[(i + d) % n]) for i in range(n)])  12.1 us
    pallas_call x5, Pallas kernels, z_call(): pl.pallas_call(functools.partial(z_kernel, tuple(ks), before is None, las...  8.96 us
    ppermute x9, waiting for transfers between devices, ring_send(): lax.ppermute(x, axis, [(order[i], order[(i + d) % n]) for i in range(n)])  7.43 us
    pallas_call x2, Pallas kernels, weight_grad_call(): pl.pallas_call(functools.partial(weight_grad_kernel, rows // (near[0][0]....  5.78 us
    pallas_call x4, Pallas kernels, d_act_call(): pl.pallas_call(functools.partial(d_act_kernel, tuple(ks), got is not None...  5.17 us
    pallas_call x1, Pallas kernels, dz_call(): pl.pallas_call(functools.partial(dz_kernel, n_batch, n_col, tile, constan...  4.67 us
  transfers between devices with their start and end apart: 47, of which 19 were waited for; matrix products, arithmetic and copies ran while one was open for 0% of the time, Pallas kernels for 24%

profile of v16, /device:TPU:0, one launch (start us, length us, event | category | flops | bytes accessed | tf_op | source)
XLA Modules:
  0.0 119.7 jit_solution(11514728209051422259)
XLA Ops:
  1.7 1.0 fusion.8
  2.8 5.1 %collective-permute-start.2 = (f32[4,512]{1,0:T(4,128)S(1)}, f32[4,512]{1,0:T(4,128)S(1)}, u32[]{:S(2)}, u32[]{:S(2)}) collective-permute-start(f32[4,512]{1,0:T(4,128)S(1)} %pad_maximum_fusion.2), channel_id=1, source_target_pairs={{0,24},{8,16},{16,8},{24,0},{1,25},{9,17},{17,9},{25,1},{2,26},{10... | collective-permute-start | bytes 24584 | tf_op jit(solution)/shard_map/norm_stats/ppermute | solution.py:24
  8.6 3.5 %weight_load.1 = (bf16[4096,1024]{1,0:T(8,128)(2,1)S(1)}, f32[4,512]{1,0:T(4,128)S(1)}) custom-call(bf16[4096,1024]{1,0:T(8,128)(2,1)} %w_ref), custom_call_target="tpu_custom_call" | custom-call | bytes 16777216 | tf_op jit(solution)/shard_map/weight_load/weight_load/pallas_call | solution.py:78
  12.9 2.5 %collective-permute-start.7 = (bf16[256,512]{1,0:T(8,128)(2,1)S(1)}, bf16[256,512]{1,0:T(8,128)(2,1)S(1)}, u32[]{:S(2)}, u32[]{:S(2)}) collective-permute-start(bf16[256,512]{1,0:T(8,128)(2,1)S(1)} %bitcast.29), channel_id=1, source_target_pairs={{0,6},{1,7},{2,4},{3,5},{4,2},{5,3},{6,0},{7,1},{8,14},{9,15},{10,... | collective-permute-start | bytes 786440 | tf_op jit(solution)/shard_map/act_gather/ppermute | solution.py:24
  16.5 2.1 %collective-permute-start.11 = (bf16[128,512]{1,0:T(8,128)(2,1)S(1)}, bf16[128,512]{1,0:T(8,128)(2,1)S(1)}, u32[]{:S(2)}, u32[]{:S(2)}) collective-permute-start(bf16[128,512]{1,0:T(8,128)(2,1)S(1)} %slice_bitcast_fusion.1), channel_id=1, source_target_pairs={{0,16},{16,24},{24,8},{8,0},{1,17},{17,25},{25,9},{9,1},{2,18},{18... | collective-permute-start | bytes 393224 | tf_op jit(solution)/shard_map/act_gather/ppermute | solution.py:34
  18.5 1.4 %collective-permute-start.12 = (bf16[128,512]{1,0:T(8,128)(2,1)S(1)}, bf16[128,512]{1,0:T(8,128)(2,1)S(1)}, u32[]{:S(2)}, u32[]{:S(2)}) collective-permute-start(bf16[128,512]{1,0:T(8,128)(2,1)S(1)} %slice_bitcast_fusion.1), channel_id=1, source_target_pairs={{0,24},{16,8},{24,0},{8,16},{1,25},{17,9},{25,1},{9,17},{2,26},{18... | collective-permute-start | bytes 393224 | tf_op jit(solution)/shard_map/act_gather/ppermute | solution.py:34
  20.0 1.2 %z_matmul.5.refs_4_ = f32[256,1024]{1,0:T(8,128)S(1)} custom-call(s32[2]{0:T(128)S(1)} %pad_add_fusion.place_ref, bf16[256,512]{1,0:T(8,128)(2,1)S(1)} %bitcast.32, bf16[256,512]{1,0:T(8,128)(2,1)S(1)} %collective-permute-done.9.refs_1_.refs_0_, bf16[4096,1024]{1,0:T(8,128)(2,1)S(1)} %get-tuple-element.63.refs_2_.refs_3_.refs_5_.w_ref), custom_call_target="tpu_custom_call" | custom-call | flops 536870912 | bytes 524288 | tf_op jit(solution)/shard_map/z/z_matmul/pallas_call | solution.py:126
  21.2 1.8 %collective-permute-done.7.refs_2_.refs_3_ = bf16[256,512]{1,0:T(8,128)(2,1)S(1)} collective-permute-done((bf16[256,512]{1,0:T(8,128)(2,1)S(1)}, bf16[256,512]{1,0:T(8,128)(2,1)S(1)}, u32[]{:S(2)}, u32[]{:S(2)}) %collective-permute-start.7) | collective-permute-done | bytes 262176 | tf_op jit(solution)/shard_map/act_gather/ppermute | solution.py:24
  24.0 4.1 %collective-permute-done.5.refs_1_.refs_2_ = bf16[256,512]{1,0:T(8,128)(2,1)S(1)} collective-permute-done((bf16[256,512]{1,0:T(8,128)(2,1)S(1)}, bf16[256,512]{1,0:T(8,128)(2,1)S(1)}, u32[]{:S(2)}, u32[]{:S(2)}) %collective-permute-start.5) | collective-permute-done | bytes 262176 | tf_op jit(solution)/shard_map/act_gather/ppermute | solution.py:24
  28.6 1.5 %z_matmul.6.refs_4_ = f32[256,1024]{1,0:T(8,128)S(1)} custom-call(s32[2]{0:T(128)S(1)} %pad_add_fusion.place_ref, bf16[256,512]{1,0:T(8,128)(2,1)S(1)} %collective-permute-done.3.refs_0_.refs_1_, bf16[256,512]{1,0:T(8,128)(2,1)S(1)} %collective-permute-done.5.refs_1_.refs_2_, bf16[256,512]{1,0:T(8,128)(2,1)S(1)} %collective-permute-done.7.refs_2_.refs_3_, ...), custom_call_target="tpu_custom_call" | custom-call | flops 805306368 | bytes 524288 | tf_op jit(solution)/shard_map/z/z_matmul/pallas_call | solution.py:126
  30.4 1.2 collective-permute-done.10
  31.6 1.6 %collective-permute-start.17 = (bf16[384,512]{1,0:T(8,128)(2,1)S(1)}, bf16[384,512]{1,0:T(8,128)(2,1)S(1)}, u32[]{:S(2)}, u32[]{:S(2)}) collective-permute-start(bf16[384,512]{1,0:T(8,128)(2,1)S(1)} %constant_dynamic-update-slice_fusion.refs_0_.refs_4_), channel_id=1, source_target_pairs={{0,4},{1,5},{2,6},{3,7},{4,0},{5,1},{6,2},{7,3},{8,12},{9,13},{10,... | collective-permute-start | bytes 1179656 | tf_op jit(solution)/shard_map/z/ppermute | solution.py:24
  33.2 1.5 %collective-permute-start.15 = (bf16[384,512]{1,0:T(8,128)(2,1)S(1)}, bf16[384,512]{1,0:T(8,128)(2,1)S(1)}, u32[]{:S(2)}, u32[]{:S(2)}) collective-permute-start(bf16[384,512]{1,0:T(8,128)(2,1)S(1)} %constant_dynamic-update-slice_fusion.refs_0_.refs_4_), channel_id=1, source_target_pairs={{0,2},{1,3},{2,0},{3,1},{4,6},{5,7},{6,4},{7,5},{8,10},{9,11},{10,... | collective-permute-start | bytes 1179656 | tf_op jit(solution)/shard_map/z/ppermute | solution.py:24
  34.7 1.5 %z_matmul.7 = (bf16[128,1024]{1,0:T(8,128)(2,1)S(1)}, bf16[128,1024]{1,0:T(8,128)(2,1)S(1)}) custom-call(s32[2]{0:T(128)S(1)} %pad_add_fusion.place_ref, bf16[256,512]{1,0:T(8,128)(2,1)S(1)} %collective-permute-done.4.refs_0_.refs_1_, bf16[256,512]{1,0:T(8,128)(2,1)S(1)} %collective-permute-done.6.refs_1_.refs_2_, ...), custom_call_target="tpu_custom_call" | custom-call | flops 805306368 | bytes 524288 | tf_op jit(solution)/shard_map/z/z_matmul/pallas_call | solution.py:126
  36.3 6.4 %collective-permute-done.17.refs_2_.refs_6_ = bf16[384,512]{1,0:T(8,128)(2,1)S(1)} collective-permute-done((bf16[384,512]{1,0:T(8,128)(2,1)S(1)}, bf16[384,512]{1,0:T(8,128)(2,1)S(1)}, u32[]{:S(2)}, u32[]{:S(2)}) %collective-permute-start.17) | collective-permute-done | bytes 393248 | tf_op jit(solution)/shard_map/z/ppermute | solution.py:24
  42.7 1.6 %collective-permute-start.19 = (bf16[192,512]{1,0:T(8,128)(2,1)S(1)}, bf16[192,512]{1,0:T(8,128)(2,1)S(1)}, u32[]{:S(2)}, u32[]{:S(2)}) collective-permute-start(bf16[192,512]{1,0:T(8,128)(2,1)S(1)} %slice.149), channel_id=1, source_target_pairs={{0,2},{1,3},{2,0},{3,1},{4,6},{5,7},{6,4},{7,5},{8,10},{9,11},{10,... | collective-permute-start | bytes 589832 | tf_op jit(solution)/shard_map/z/ppermute | solution.py:24
  44.3 1.6 %collective-permute-start.20 = (bf16[192,512]{1,0:T(8,128)(2,1)S(1)}, bf16[192,512]{1,0:T(8,128)(2,1)S(1)}, u32[]{:S(2)}, u32[]{:S(2)}) collective-permute-start(bf16[192,512]{1,0:T(8,128)(2,1)S(1)} %slice.150), channel_id=1, source_target_pairs={{0,4},{1,5},{2,6},{3,7},{4,0},{5,1},{6,2},{7,3},{8,12},{9,13},{10,... | collective-permute-start | bytes 589832 | tf_op jit(solution)/shard_map/z/ppermute | solution.py:24
  47.6 1.9 %z_matmul.8.refs_6_ = f32[384,1024]{1,0:T(8,128)S(1)} custom-call(s32[2]{0:T(128)S(1)} %pad_add_fusion.place_ref, bf16[384,512]{1,0:T(8,128)(2,1)S(1)} %constant_dynamic-update-slice_fusion.refs_0_.refs_4_, bf16[384,512]{1,0:T(8,128)(2,1)S(1)} %collective-permute-done.15.refs_1_.refs_5_, bf16[384,512]{1,0:T(8,128)(2,1)S(1)} %collective-permute-done.17.refs_2_.refs_6_, ...), custom_call_target="tpu_custom_call" | custom-call | flops 1207959552 | bytes 786432 | tf_op jit(solution)/shard_map/z_far/z_matmul/pallas_call | solution.py:126
  50.1 2.6 %collective-permute-done.21.refs_5_.refs_13_ = bf16[128,1024]{1,0:T(8,128)(2,1)S(1)} collective-permute-done((bf16[128,1024]{1,0:T(8,128)(2,1)S(1)}, bf16[128,1024]{1,0:T(8,128)(2,1)S(1)}, u32[]{:S(2)}, u32[]{:S(2)}) %collective-permute-start.21) | collective-permute-done | bytes 262176 | tf_op jit(solution)/shard_map/z_ring/ppermute | solution.py:34
  52.7 2.0 %collective-permute-start.23 = (bf16[128,1024]{1,0:T(8,128)(2,1)S(1)}, bf16[128,1024]{1,0:T(8,128)(2,1)S(1)}, u32[]{:S(2)}, u32[]{:S(2)}) collective-permute-start(bf16[128,1024]{1,0:T(8,128)(2,1)S(1)} %collective-permute-done.21.refs_5_.refs_13_), channel_id=1, source_target_pairs={{0,16},{16,24},{24,8},{8,0},{1,17},{17,25},{25,9},{9,1},{2,18},{18... | collective-permute-start | bytes 786440 | tf_op jit(solution)/shard_map/z_far/ppermute | solution.py:34
  55.5 2.7 %z_matmul.9 = (bf16[128,1024]{1,0:T(8,128)(2,1)S(1)}, bf16[128,1024]{1,0:T(8,128)(2,1)S(1)}, bf16[128,1024]{1,0:T(8,128)(2,1)S(1)}) custom-call(s32[2]{0:T(128)S(1)} %pad_add_fusion.place_ref, bf16[384,512]{1,0:T(8,128)(2,1)S(1)} %collective-permute-done.13.refs_0_.refs_4_, bf16[384,512]{1,0:T(8,128)(2,1)S(1)} %collective-permute-done.16.refs_1_.refs_5_, ...), custom_call_target="tpu_custom_call" | custom-call | flops 2013265920 | bytes 786432 | tf_op jit(solution)/shard_map/z_far/z_matmul/pallas_call | solution.py:126
  58.2 3.6 %collective-permute-done.23.refs_7_.refs_15_ = bf16[128,1024]{1,0:T(8,128)(2,1)S(1)} collective-permute-done((bf16[128,1024]{1,0:T(8,128)(2,1)S(1)}, bf16[128,1024]{1,0:T(8,128)(2,1)S(1)}, u32[]{:S(2)}, u32[]{:S(2)}) %collective-permute-start.23) | collective-permute-done | bytes 262176 | tf_op jit(solution)/shard_map/z_far/ppermute | solution.py:34
  61.8 2.6 %kernel_strip.1 = (f32[4,32,1280]{2,1,0:T(8,128)S(1)}, bf16[4,32,1280]{2,1,0:T(8,128)(2,1)S(1)}) custom-call(s32[2]{0:T(128)S(1)} %pad_add_fusion.place_ref, bf16[128,1024]{1,0:T(8,128)(2,1)S(1)} %get-tuple-element.67.refs_0_.refs_8_, bf16[128,1024]{1,0:T(8,128)(2,1)S(1)} %get-tuple-element.68.refs_1_.refs_9_, ...), custom_call_target="tpu_custom_call" | custom-call | flops 671088640 | bytes 2097152 | tf_op jit(solution)/shard_map/kernel/kernel_strip/pallas_call | solution.py:173
  64.5 1.6 %collective-permute-done.25 = bf16[4,32,1280]{2,1,0:T(8,128)(2,1)S(1)} collective-permute-done((bf16[4,32,1280]{2,1,0:T(8,128)(2,1)S(1)}, bf16[4,32,1280]{2,1,0:T(8,128)(2,1)S(1)}, u32[]{:S(2)}, u32[]{:S(2)}) %collective-permute-start.25) | collective-permute-done | bytes 327712 | tf_op jit(solution)/shard_map/kernel/ppermute | solution.py:24
  67.0 1.4 %collective-permute-start.28 = (bf16[32,1280]{1,0:T(8,128)(2,1)S(1)}, bf16[32,1280]{1,0:T(8,128)(2,1)S(1)}, u32[]{:S(2)}, u32[]{:S(2)}) collective-permute-start(bf16[32,1280]{1,0:T(8,128)(2,1)S(1)} %get-tuple-element.119), channel_id=1, source_target_pairs={{0,6},{1,7},{2,4},{3,5},{4,2},{5,3},{6,0},{7,1},{8,14},{9,15},{10,... | collective-permute-start | bytes 245768 | tf_op jit(solution)/shard_map/kernel/ppermute | solution.py:24
  68.4 1.4 %collective-permute-start.27 = (bf16[32,1280]{1,0:T(8,128)(2,1)S(1)}, bf16[32,1280]{1,0:T(8,128)(2,1)S(1)}, u32[]{:S(2)}, u32[]{:S(2)}) collective-permute-start(bf16[32,1280]{1,0:T(8,128)(2,1)S(1)} %get-tuple-element.120), channel_id=1, source_target_pairs={{0,4},{1,5},{2,6},{3,7},{4,0},{5,1},{6,2},{7,3},{8,12},{9,13},{10,... | collective-permute-start | bytes 245768 | tf_op jit(solution)/shard_map/kernel/ppermute | solution.py:24
  69.8 2.2 %collective-permute-start.31 = (bf16[128,512]{1,0:T(8,128)(2,1)S(1)}, bf16[128,512]{1,0:T(8,128)(2,1)S(1)}, u32[]{:S(2)}, u32[]{:S(2)}) collective-permute-start(bf16[128,512]{1,0:T(8,128)(2,1)S(1)} %get-tuple-element.85), channel_id=1, source_target_pairs={{0,24},{16,8},{24,0},{8,16},{1,25},{17,9},{25,1},{9,17},{2,26},{18... | collective-permute-start | bytes 393224 | tf_op jit(solution)/shard_map/kernel/ppermute | solution.py:34
  72.8 1.2 %collective-permute-done.27 = bf16[32,1280]{1,0:T(8,128)(2,1)S(1)} collective-permute-done((bf16[32,1280]{1,0:T(8,128)(2,1)S(1)}, bf16[32,1280]{1,0:T(8,128)(2,1)S(1)}, u32[]{:S(2)}, u32[]{:S(2)}) %collective-permute-start.27) | collective-permute-done | bytes 81952 | tf_op jit(solution)/shard_map/kernel/ppermute | solution.py:24
  74.0 1.2 collective-permute-start.30
  75.2 1.6 %collective-permute-start.35 = (bf16[32,1280]{1,0:T(8,128)(2,1)S(1)}, bf16[32,1280]{1,0:T(8,128)(2,1)S(1)}, u32[]{:S(2)}, u32[]{:S(2)}) collective-permute-start(bf16[32,1280]{1,0:T(8,128)(2,1)S(1)} %get-tuple-element.112.refs_0_), channel_id=1, source_target_pairs={{0,6},{1,7},{2,4},{3,5},{4,2},{5,3},{6,0},{7,1},{8,14},{9,15},{10,... | collective-permute-start | bytes 245768 | tf_op jit(solution)/shard_map/kernel/ppermute | solution.py:24
  77.6 1.6 %collective-permute-done.30.refs_2_ = bf16[32,1280]{1,0:T(8,128)(2,1)S(1)} collective-permute-done((bf16[32,1280]{1,0:T(8,128)(2,1)S(1)}, bf16[32,1280]{1,0:T(8,128)(2,1)S(1)}, u32[]{:S(2)}, u32[]{:S(2)}) %collective-permute-start.30) | collective-permute-done | bytes 81952 | tf_op jit(solution)/shard_map/kernel/ppermute | solution.py:24
  79.2 1.6 %collective-permute-done.35.refs_6_ = bf16[32,1280]{1,0:T(8,128)(2,1)S(1)} collective-permute-done((bf16[32,1280]{1,0:T(8,128)(2,1)S(1)}, bf16[32,1280]{1,0:T(8,128)(2,1)S(1)}, u32[]{:S(2)}, u32[]{:S(2)}) %collective-permute-start.35) | collective-permute-done | bytes 81952 | tf_op jit(solution)/shard_map/kernel/ppermute | solution.py:24
  82.1 2.0 %collective-permute-start.37 = (bf16[128,512]{1,0:T(8,128)(2,1)S(1)}, bf16[128,512]{1,0:T(8,128)(2,1)S(1)}, u32[]{:S(2)}, u32[]{:S(2)}) collective-permute-start(bf16[128,512]{1,0:T(8,128)(2,1)S(1)} %get-tuple-element.88), channel_id=1, source_target_pairs={{0,8},{16,0},{24,16},{8,24},{1,9},{17,1},{25,17},{9,25},{2,10},{18... | collective-permute-start | bytes 393224 | tf_op jit(solution)/shard_map/kernel/ppermute | solution.py:34
  84.1 4.7 %embedding_gradient.1 = (bf16[2,512,1024]{2,1,0:T(8,128)(2,1)S(1)}, f32[8,128]{1,0:T(8,128)S(1)}) custom-call(s32[2]{0:T(128)S(1)} %pad_add_fusion.place_ref, f32[32,1280]{1,0:T(8,128)S(1)} %get-tuple-element.113.own_ref, bf16[32,1280]{1,0:T(8,128)(2,1)S(1)} %get-tuple-element.112.refs_0_, bf16[32,1280]{1,0:T(8,128)(2,1)S(1)} %collective-permute-done.29.refs_1_, ...), custom_call_target="tpu_custom_call" | custom-call | flops 1073741824 | bytes 4194304 | tf_op jit(solution)/shard_map/dz/embedding_gradient/pallas_call | solution.py:251
  88.8 1.0 d_act_matmul.4
  89.8 1.6 %d_act_matmul.5 = bf16[3,272,512]{2,1,0:T(8,128)(2,1)S(1)} custom-call(s32[2]{0:T(128)S(1)} %pad_add_fusion.place_ref, bf16[2,512,1024]{2,1,0:T(8,128)(2,1)S(1)} %get-tuple-element.89.dz_ref.refs_9_, f32[8,128]{1,0:T(8,128)S(1)} %get-tuple-element.92.share_ref, bf16[4096,1024]{1,0:T(8,128)(2,1)S(1)} %get-tuple-element.63.refs_2_.refs_3_.refs_5_.w_ref), custom_call_target="tpu_custom_call" | custom-call | flops 805306368 | bytes 786432 | tf_op jit(solution)/shard_map/d_act/d_act_matmul/pallas_call | solution.py:317
  92.2 2.0 %collective-permute-done.41.refs_0_ = bf16[1,272,512]{2,1,0:T(8,128)(2,1)S(1)} collective-permute-done((bf16[1,272,512]{2,1,0:T(8,128)(2,1)S(1)}, bf16[1,272,512]{2,1,0:T(8,128)(2,1)S(1)}, u32[]{:S(2)}, u32[]{:S(2)}) %collective-permute-start.41) | collective-permute-done | bytes 278560 | tf_op jit(solution)/shard_map/d_act/ppermute | solution.py:24
  94.2 1.0 d_act_matmul.7
  95.3 1.5 %collective-permute-start.42 = (bf16[272,512]{1,0:T(8,128)(2,1)S(1)}, bf16[272,512]{1,0:T(8,128)(2,1)S(1)}, u32[]{:S(2)}, u32[]{:S(2)}) collective-permute-start(bf16[272,512]{1,0:T(8,128)(2,1)S(1)} %d_act_matmul.7), channel_id=1, source_target_pairs={{0,6},{1,7},{2,4},{3,5},{4,2},{5,3},{6,0},{7,1},{8,14},{9,15},{10,... | collective-permute-start | bytes 835592 | tf_op jit(solution)/shard_map/d_act/ppermute | solution.py:24
  96.8 1.6 %d_act_matmul.6 = (bf16[272,512]{1,0:T(8,128)(2,1)S(1)}, bf16[272,512]{1,0:T(8,128)(2,1)S(1)}, f32[272,512]{1,0:T(8,128)S(1)}) custom-call(s32[2]{0:T(128)S(1)} %pad_add_fusion.place_ref, bf16[2,512,1024]{2,1,0:T(8,128)(2,1)S(1)} %get-tuple-element.89.dz_ref.refs_9_, f32[8,128]{1,0:T(8,128)S(1)} %get-tuple-element.92.share_ref, ...), custom_call_target="tpu_custom_call" | custom-call | flops 805306368 | bytes 786432 | tf_op jit(solution)/shard_map/d_act/d_act_matmul/pallas_call | solution.py:317
  98.3 1.6 %collective-permute-start.39 = (bf16[272,512]{1,0:T(8,128)(2,1)S(1)}, bf16[272,512]{1,0:T(8,128)(2,1)S(1)}, u32[]{:S(2)}, u32[]{:S(2)}) collective-permute-start(bf16[272,512]{1,0:T(8,128)(2,1)S(1)} %get-tuple-element.95), channel_id=1, source_target_pairs={{0,2},{1,3},{2,0},{3,1},{4,6},{5,7},{6,4},{7,5},{8,10},{9,11},{10,... | collective-permute-start | bytes 835592 | tf_op jit(solution)/shard_map/d_act/ppermute | solution.py:24
  100.5 2.9 %weight_gradient.2.refs_10_ = f32[1024,1024]{1,0:T(8,128)} custom-call(s32[2]{0:T(128)S(1)} %pad_add_fusion.place_ref, bf16[256,512]{1,0:T(8,128)(2,1)S(1)} %bitcast.34, bf16[256,512]{1,0:T(8,128)(2,1)S(1)} %collective-permute-done.3.refs_0_.refs_1_, bf16[256,512]{1,0:T(8,128)(2,1)S(1)} %collective-permute-done.5.refs_1_.refs_2_, ...), custom_call_target="tpu_custom_call" | custom-call | flops 1073741824 | bytes 2097152 | tf_op jit(solution)/shard_map/grad_weight/weight_gradient/pallas_call | solution.py:422
  103.4 2.9 %weight_gradient.3 = f32[1024,1024]{1,0:T(8,128)} custom-call(s32[2]{0:T(128)S(1)} %pad_add_fusion.place_ref, bf16[256,512]{1,0:T(8,128)(2,1)S(1)} %collective-permute-done.9.refs_1_.refs_0_, bf16[256,512]{1,0:T(8,128)(2,1)S(1)} %collective-permute-done.4.refs_0_.refs_1_, ...), custom_call_target="tpu_custom_call", output_to_operand_aliasing={{}: (11, {})} | custom-call | flops 1073741824 | bytes 2097152 | tf_op jit(solution)/shard_map/grad_weight/weight_gradient/pallas_call | solution.py:422
  106.3 4.7 %collective-permute-done.39 = bf16[272,512]{1,0:T(8,128)(2,1)S(1)} collective-permute-done((bf16[272,512]{1,0:T(8,128)(2,1)S(1)}, bf16[272,512]{1,0:T(8,128)(2,1)S(1)}, u32[]{:S(2)}, u32[]{:S(2)}) %collective-permute-start.39) | collective-permute-done | bytes 278560 | tf_op jit(solution)/shard_map/d_act/ppermute | solution.py:24
  111.6 2.5 %collective-permute-start.46 = (f32[8,512]{1,0:T(8,128)S(1)}, f32[8,512]{1,0:T(8,128)S(1)}, u32[]{:S(2)}, u32[]{:S(2)}) collective-permute-start(f32[8,512]{1,0:T(8,128)S(1)} %pad_maximum_fusion.1.refs_0_), channel_id=1, source_target_pairs={{0,24},{8,16},{16,8},{24,0},{1,25},{9,17},{17,9},{25,1},{2,26},{10... | collective-permute-start | bytes 49160 | tf_op jit(solution)/shard_map/norm_backward/ppermute | solution.py:24
  114.3 1.8 %collective-permute-start.44 = (f32[8,512]{1,0:T(8,128)S(1)}, f32[8,512]{1,0:T(8,128)S(1)}, u32[]{:S(2)}, u32[]{:S(2)}) collective-permute-start(f32[8,512]{1,0:T(8,128)S(1)} %pad_maximum_fusion.1.refs_0_), channel_id=1, source_target_pairs={{0,8},{8,0},{16,24},{24,16},{1,9},{9,1},{17,25},{25,17},{2,10},{10... | collective-permute-start | bytes 49160 | tf_op jit(solution)/shard_map/norm_backward/ppermute | solution.py:24
  116.1 1.3 %collective-permute-done.46.refs_3_ = f32[8,512]{1,0:T(8,128)S(1)} collective-permute-done((f32[8,512]{1,0:T(8,128)S(1)}, f32[8,512]{1,0:T(8,128)S(1)}, u32[]{:S(2)}, u32[]{:S(2)}) %collective-permute-start.46) | collective-permute-done | bytes 16416 | tf_op jit(solution)/shard_map/norm_backward/ppermute | solution.py:24
  117.4 1.4 %collective-permute-done.45.refs_2_ = f32[8,512]{1,0:T(8,128)S(1)} collective-permute-done((f32[8,512]{1,0:T(8,128)S(1)}, f32[8,512]{1,0:T(8,128)S(1)}, u32[]{:S(2)}, u32[]{:S(2)}) %collective-permute-start.45) | collective-permute-done | bytes 16416 | tf_op jit(solution)/shard_map/norm_backward/ppermute | solution.py:24
  (93 shorter events, 15.3 us)
Async XLA Ops:
  2.8 9.7 %copy-start = (f32[512]{0:T(512)S(1)}, f32[512]{0:T(512)}, u32[]{:S(2)}) copy-start(f32[512]{0:T(512)} %param.5) | copy-start | bytes 6148
  2.8 9.2 %collective-permute-start.2 = (f32[4,512]{1,0:T(4,128)S(1)}, f32[4,512]{1,0:T(4,128)S(1)}, u32[]{:S(2)}, u32[]{:S(2)}) collective-permute-start(f32[4,512]{1,0:T(4,128)S(1)} %pad_maximum_fusion.2), channel_id=1, source_target_pairs={{0,24},{8,16},{16,8},{24,0},{1,25},{9,17},{17,9},{25,1},{2,26},{10... | collective-permute-start | bytes 24584 | tf_op jit(solution)/shard_map/norm_stats/ppermute | solution.py:24
  7.9 4.5 %collective-permute-start.1 = (f32[4,512]{1,0:T(4,128)S(1)}, f32[4,512]{1,0:T(4,128)S(1)}, u32[]{:S(2)}, u32[]{:S(2)}) collective-permute-start(f32[4,512]{1,0:T(4,128)S(1)} %pad_maximum_fusion.2), channel_id=1, source_target_pairs={{0,16},{8,24},{16,0},{24,8},{1,17},{9,25},{17,1},{25,9},{2,18},{10... | collective-permute-start | bytes 24584 | tf_op jit(solution)/shard_map/norm_stats/ppermute | solution.py:24
  7.9 4.5 %collective-permute-start = (f32[4,512]{1,0:T(4,128)S(1)}, f32[4,512]{1,0:T(4,128)S(1)}, u32[]{:S(2)}, u32[]{:S(2)}) collective-permute-start(f32[4,512]{1,0:T(4,128)S(1)} %pad_maximum_fusion.2), channel_id=1, source_target_pairs={{0,8},{8,0},{16,24},{24,16},{1,9},{9,1},{17,25},{25,17},{2,10},{10... | collective-permute-start | bytes 24584 | tf_op jit(solution)/shard_map/norm_stats/ppermute | solution.py:24
  12.8 3.6 %collective-permute-start.9 = (bf16[256,512]{1,0:T(8,128)(2,1)S(1)}, bf16[256,512]{1,0:T(8,128)(2,1)S(1)}, u32[]{:S(2)}, u32[]{:S(2)}) collective-permute-start(bf16[256,512]{1,0:T(8,128)(2,1)S(1)} %bitcast.28), channel_id=1, source_target_pairs={{0,1},{1,0},{2,3},{3,2},{4,5},{5,4},{6,7},{7,6},{8,9},{9,8},{10,11... | collective-permute-start | bytes 786440 | tf_op jit(solution)/shard_map/act_gather/ppermute | solution.py:24
  12.9 10.1 %collective-permute-start.7 = (bf16[256,512]{1,0:T(8,128)(2,1)S(1)}, bf16[256,512]{1,0:T(8,128)(2,1)S(1)}, u32[]{:S(2)}, u32[]{:S(2)}) collective-permute-start(bf16[256,512]{1,0:T(8,128)(2,1)S(1)} %bitcast.29), channel_id=1, source_target_pairs={{0,6},{1,7},{2,4},{3,5},{4,2},{5,3},{6,0},{7,1},{8,14},{9,15},{10,... | collective-permute-start | bytes 786440 | tf_op jit(solution)/shard_map/act_gather/ppermute | solution.py:24
  15.4 12.7 %collective-permute-start.5 = (bf16[256,512]{1,0:T(8,128)(2,1)S(1)}, bf16[256,512]{1,0:T(8,128)(2,1)S(1)}, u32[]{:S(2)}, u32[]{:S(2)}) collective-permute-start(bf16[256,512]{1,0:T(8,128)(2,1)S(1)} %bitcast.30), channel_id=1, source_target_pairs={{0,4},{1,5},{2,6},{3,7},{4,0},{5,1},{6,2},{7,3},{8,12},{9,13},{10,... | collective-permute-start | bytes 786440 | tf_op jit(solution)/shard_map/act_gather/ppermute | solution.py:24
  15.9 12.3 %collective-permute-start.3 = (bf16[256,512]{1,0:T(8,128)(2,1)S(1)}, bf16[256,512]{1,0:T(8,128)(2,1)S(1)}, u32[]{:S(2)}, u32[]{:S(2)}) collective-permute-start(bf16[256,512]{1,0:T(8,128)(2,1)S(1)} %bitcast.31), channel_id=1, source_target_pairs={{0,2},{1,3},{2,0},{3,1},{4,6},{5,7},{6,4},{7,5},{8,10},{9,11},{10,... | collective-permute-start | bytes 786440 | tf_op jit(solution)/shard_map/act_gather/ppermute | solution.py:24
  16.5 13.7 %collective-permute-start.11 = (bf16[128,512]{1,0:T(8,128)(2,1)S(1)}, bf16[128,512]{1,0:T(8,128)(2,1)S(1)}, u32[]{:S(2)}, u32[]{:S(2)}) collective-permute-start(bf16[128,512]{1,0:T(8,128)(2,1)S(1)} %slice_bitcast_fusion.1), channel_id=1, source_target_pairs={{0,16},{16,24},{24,8},{8,0},{1,17},{17,25},{25,9},{9,1},{2,18},{18... | collective-permute-start | bytes 393224 | tf_op jit(solution)/shard_map/act_gather/ppermute | solution.py:34
  18.5 11.8 %collective-permute-start.12 = (bf16[128,512]{1,0:T(8,128)(2,1)S(1)}, bf16[128,512]{1,0:T(8,128)(2,1)S(1)}, u32[]{:S(2)}, u32[]{:S(2)}) collective-permute-start(bf16[128,512]{1,0:T(8,128)(2,1)S(1)} %slice_bitcast_fusion.1), channel_id=1, source_target_pairs={{0,24},{16,8},{24,0},{8,16},{1,25},{17,9},{25,1},{9,17},{2,26},{18... | collective-permute-start | bytes 393224 | tf_op jit(solution)/shard_map/act_gather/ppermute | solution.py:34
  23.0 8.6 %collective-permute-start.10 = (bf16[128,512]{1,0:T(8,128)(2,1)S(1)}, bf16[128,512]{1,0:T(8,128)(2,1)S(1)}, u32[]{:S(2)}, u32[]{:S(2)}) collective-permute-start(bf16[128,512]{1,0:T(8,128)(2,1)S(1)} %slice_bitcast_fusion.1), channel_id=1, source_target_pairs={{0,8},{16,0},{24,16},{8,24},{1,9},{17,1},{25,17},{9,25},{2,10},{18... | collective-permute-start | bytes 393224 | tf_op jit(solution)/shard_map/act_gather/ppermute | solution.py:34
  28.1 6.5 %collective-permute-start.8 = (bf16[256,512]{1,0:T(8,128)(2,1)S(1)}, bf16[256,512]{1,0:T(8,128)(2,1)S(1)}, u32[]{:S(2)}, u32[]{:S(2)}) collective-permute-start(bf16[256,512]{1,0:T(8,128)(2,1)S(1)} %collective-permute-done.7.refs_2_.refs_3_), channel_id=1, source_target_pairs={{0,1},{1,0},{2,3},{3,2},{4,5},{5,4},{6,7},{7,6},{8,9},{9,8},{10,11... | collective-permute-start | bytes 786440 | tf_op jit(solution)/shard_map/act_gather/ppermute | solution.py:24
  28.2 6.4 %collective-permute-start.6 = (bf16[256,512]{1,0:T(8,128)(2,1)S(1)}, bf16[256,512]{1,0:T(8,128)(2,1)S(1)}, u32[]{:S(2)}, u32[]{:S(2)}) collective-permute-start(bf16[256,512]{1,0:T(8,128)(2,1)S(1)} %collective-permute-done.5.refs_1_.refs_2_), channel_id=1, source_target_pairs={{0,1},{1,0},{2,3},{3,2},{4,5},{5,4},{6,7},{7,6},{8,9},{9,8},{10,11... | collective-permute-start | bytes 786440 | tf_op jit(solution)/shard_map/act_gather/ppermute | solution.py:24
  30.2 4.5 %collective-permute-start.4 = (bf16[256,512]{1,0:T(8,128)(2,1)S(1)}, bf16[256,512]{1,0:T(8,128)(2,1)S(1)}, u32[]{:S(2)}, u32[]{:S(2)}) collective-permute-start(bf16[256,512]{1,0:T(8,128)(2,1)S(1)} %collective-permute-done.3.refs_0_.refs_1_), channel_id=1, source_target_pairs={{0,1},{1,0},{2,3},{3,2},{4,5},{5,4},{6,7},{7,6},{8,9},{9,8},{10,11... | collective-permute-start | bytes 786440 | tf_op jit(solution)/shard_map/act_gather/ppermute | solution.py:24
  31.6 11.1 %collective-permute-start.17 = (bf16[384,512]{1,0:T(8,128)(2,1)S(1)}, bf16[384,512]{1,0:T(8,128)(2,1)S(1)}, u32[]{:S(2)}, u32[]{:S(2)}) collective-permute-start(bf16[384,512]{1,0:T(8,128)(2,1)S(1)} %constant_dynamic-update-slice_fusion.refs_0_.refs_4_), channel_id=1, source_target_pairs={{0,4},{1,5},{2,6},{3,7},{4,0},{5,1},{6,2},{7,3},{8,12},{9,13},{10,... | collective-permute-start | bytes 1179656 | tf_op jit(solution)/shard_map/z/ppermute | solution.py:24
  33.2 11.1 %collective-permute-start.15 = (bf16[384,512]{1,0:T(8,128)(2,1)S(1)}, bf16[384,512]{1,0:T(8,128)(2,1)S(1)}, u32[]{:S(2)}, u32[]{:S(2)}) collective-permute-start(bf16[384,512]{1,0:T(8,128)(2,1)S(1)} %constant_dynamic-update-slice_fusion.refs_0_.refs_4_), channel_id=1, source_target_pairs={{0,2},{1,3},{2,0},{3,1},{4,6},{5,7},{6,4},{7,5},{8,10},{9,11},{10,... | collective-permute-start | bytes 1179656 | tf_op jit(solution)/shard_map/z/ppermute | solution.py:24
  36.2 9.7 %collective-permute-start.14 = (bf16[128,1024]{1,0:T(8,128)(2,1)S(1)}, bf16[128,1024]{1,0:T(8,128)(2,1)S(1)}, u32[]{:S(2)}, u32[]{:S(2)}) collective-permute-start(bf16[128,1024]{1,0:T(8,128)(2,1)S(1)} %get-tuple-element.68.refs_1_.refs_9_), channel_id=1, source_target_pairs={{0,16},{16,24},{24,8},{8,0},{1,17},{17,25},{25,9},{9,1},{2,18},{18... | collective-permute-start | bytes 786440 | tf_op jit(solution)/shard_map/z_ring/ppermute | solution.py:34
  42.7 6.9 %collective-permute-start.19 = (bf16[192,512]{1,0:T(8,128)(2,1)S(1)}, bf16[192,512]{1,0:T(8,128)(2,1)S(1)}, u32[]{:S(2)}, u32[]{:S(2)}) collective-permute-start(bf16[192,512]{1,0:T(8,128)(2,1)S(1)} %slice.149), channel_id=1, source_target_pairs={{0,2},{1,3},{2,0},{3,1},{4,6},{5,7},{6,4},{7,5},{8,10},{9,11},{10,... | collective-permute-start | bytes 589832 | tf_op jit(solution)/shard_map/z/ppermute | solution.py:24
  44.3 5.8 %collective-permute-start.20 = (bf16[192,512]{1,0:T(8,128)(2,1)S(1)}, bf16[192,512]{1,0:T(8,128)(2,1)S(1)}, u32[]{:S(2)}, u32[]{:S(2)}) collective-permute-start(bf16[192,512]{1,0:T(8,128)(2,1)S(1)} %slice.150), channel_id=1, source_target_pairs={{0,4},{1,5},{2,6},{3,7},{4,0},{5,1},{6,2},{7,3},{8,12},{9,13},{10,... | collective-permute-start | bytes 589832 | tf_op jit(solution)/shard_map/z/ppermute | solution.py:24
  45.9 6.8 %collective-permute-start.21 = (bf16[128,1024]{1,0:T(8,128)(2,1)S(1)}, bf16[128,1024]{1,0:T(8,128)(2,1)S(1)}, u32[]{:S(2)}, u32[]{:S(2)}) collective-permute-start(bf16[128,1024]{1,0:T(8,128)(2,1)S(1)} %collective-permute-done.14.refs_3_.refs_11_), channel_id=1, source_target_pairs={{0,16},{16,24},{24,8},{8,0},{1,17},{17,25},{25,9},{9,1},{2,18},{18... | collective-permute-start | bytes 786440 | tf_op jit(solution)/shard_map/z_ring/ppermute | solution.py:34
  47.1 7.6 %collective-permute-start.13 = (bf16[384,512]{1,0:T(8,128)(2,1)S(1)}, bf16[384,512]{1,0:T(8,128)(2,1)S(1)}, u32[]{:S(2)}, u32[]{:S(2)}) collective-permute-start(bf16[384,512]{1,0:T(8,128)(2,1)S(1)} %constant_dynamic-update-slice_fusion.refs_0_.refs_4_), channel_id=1, source_target_pairs={{0,1},{1,0},{2,3},{3,2},{4,5},{5,4},{6,7},{7,6},{8,9},{9,8},{10,11... | collective-permute-start | bytes 1179656 | tf_op jit(solution)/shard_map/z_far/ppermute | solution.py:24
  47.1 8.3 %collective-permute-start.16 = (bf16[384,512]{1,0:T(8,128)(2,1)S(1)}, bf16[384,512]{1,0:T(8,128)(2,1)S(1)}, u32[]{:S(2)}, u32[]{:S(2)}) collective-permute-start(bf16[384,512]{1,0:T(8,128)(2,1)S(1)} %collective-permute-done.15.refs_1_.refs_5_), channel_id=1, source_target_pairs={{0,1},{1,0},{2,3},{3,2},{4,5},{5,4},{6,7},{7,6},{8,9},{9,8},{10,11... | collective-permute-start | bytes 1179656 | tf_op jit(solution)/shard_map/z_far/ppermute | solution.py:24
  49.6 5.9 %collective-permute-start.18 = (bf16[384,512]{1,0:T(8,128)(2,1)S(1)}, bf16[384,512]{1,0:T(8,128)(2,1)S(1)}, u32[]{:S(2)}, u32[]{:S(2)}) collective-permute-start(bf16[384,512]{1,0:T(8,128)(2,1)S(1)} %collective-permute-done.17.refs_2_.refs_6_), channel_id=1, source_target_pairs={{0,1},{1,0},{2,3},{3,2},{4,5},{5,4},{6,7},{7,6},{8,9},{9,8},{10,11... | collective-permute-start | bytes 1179656 | tf_op jit(solution)/shard_map/z_far/ppermute | solution.py:24
  52.7 2.8 %collective-permute-start.22 = (bf16[384,512]{1,0:T(8,128)(2,1)S(1)}, bf16[384,512]{1,0:T(8,128)(2,1)S(1)}, u32[]{:S(2)}, u32[]{:S(2)}) collective-permute-start(bf16[384,512]{1,0:T(8,128)(2,1)S(1)} %pad_maximum_fusion.refs_3_.refs_7_), channel_id=1, source_target_pairs={{0,1},{1,0},{2,3},{3,2},{4,5},{5,4},{6,7},{7,6},{8,9},{9,8},{10,11... | collective-permute-start | bytes 1179656 | tf_op jit(solution)/shard_map/z_far/ppermute | solution.py:24
  52.7 9.1 %collective-permute-start.23 = (bf16[128,1024]{1,0:T(8,128)(2,1)S(1)}, bf16[128,1024]{1,0:T(8,128)(2,1)S(1)}, u32[]{:S(2)}, u32[]{:S(2)}) collective-permute-start(bf16[128,1024]{1,0:T(8,128)(2,1)S(1)} %collective-permute-done.21.refs_5_.refs_13_), channel_id=1, source_target_pairs={{0,16},{16,24},{24,8},{8,0},{1,17},{17,25},{25,9},{9,1},{2,18},{18... | collective-permute-start | bytes 786440 | tf_op jit(solution)/shard_map/z_far/ppermute | solution.py:34
  54.7 9.8 %collective-permute-start.24 = (bf16[128,512]{1,0:T(8,128)(2,1)S(1)}, bf16[128,512]{1,0:T(8,128)(2,1)S(1)}, u32[]{:S(2)}, u32[]{:S(2)}) collective-permute-start(bf16[128,512]{1,0:T(8,128)(2,1)S(1)} %get-tuple-element.83), channel_id=1, source_target_pairs={{0,16},{16,24},{24,8},{8,0},{1,17},{17,25},{25,9},{9,1},{2,18},{18... | collective-permute-start | bytes 393224 | tf_op jit(solution)/shard_map/kernel/ppermute | solution.py:34
  64.5 1.7 %collective-permute-start.25 = (bf16[4,32,1280]{2,1,0:T(8,128)(2,1)S(1)}, bf16[4,32,1280]{2,1,0:T(8,128)(2,1)S(1)}, u32[]{:S(2)}, u32[]{:S(2)}) collective-permute-start(bf16[4,32,1280]{2,1,0:T(8,128)(2,1)S(1)} %get-tuple-element.84), channel_id=1, source_target_pairs={{0,1},{1,0},{2,3},{3,2},{4,5},{5,4},{6,7},{7,6},{8,9},{9,8},{10,11... | collective-permute-start | bytes 983048 | tf_op jit(solution)/shard_map/kernel/ppermute | solution.py:24
  66.3 5.7 %collective-permute-start.26 = (bf16[32,1280]{1,0:T(8,128)(2,1)S(1)}, bf16[32,1280]{1,0:T(8,128)(2,1)S(1)}, u32[]{:S(2)}, u32[]{:S(2)}) collective-permute-start(bf16[32,1280]{1,0:T(8,128)(2,1)S(1)} %get-tuple-element.118), channel_id=1, source_target_pairs={{0,2},{1,3},{2,0},{3,1},{4,6},{5,7},{6,4},{7,5},{8,10},{9,11},{10,... | collective-permute-start | bytes 245768 | tf_op jit(solution)/shard_map/kernel/ppermute | solution.py:24
  67.0 5.7 %collective-permute-start.28 = (bf16[32,1280]{1,0:T(8,128)(2,1)S(1)}, bf16[32,1280]{1,0:T(8,128)(2,1)S(1)}, u32[]{:S(2)}, u32[]{:S(2)}) collective-permute-start(bf16[32,1280]{1,0:T(8,128)(2,1)S(1)} %get-tuple-element.119), channel_id=1, source_target_pairs={{0,6},{1,7},{2,4},{3,5},{4,2},{5,3},{6,0},{7,1},{8,14},{9,15},{10,... | collective-permute-start | bytes 245768 | tf_op jit(solution)/shard_map/kernel/ppermute | solution.py:24
  68.4 5.5 %collective-permute-start.27 = (bf16[32,1280]{1,0:T(8,128)(2,1)S(1)}, bf16[32,1280]{1,0:T(8,128)(2,1)S(1)}, u32[]{:S(2)}, u32[]{:S(2)}) collective-permute-start(bf16[32,1280]{1,0:T(8,128)(2,1)S(1)} %get-tuple-element.120), channel_id=1, source_target_pairs={{0,4},{1,5},{2,6},{3,7},{4,0},{5,1},{6,2},{7,3},{8,12},{9,13},{10,... | collective-permute-start | bytes 245768 | tf_op jit(solution)/shard_map/kernel/ppermute | solution.py:24
  69.8 7.8 %collective-permute-start.31 = (bf16[128,512]{1,0:T(8,128)(2,1)S(1)}, bf16[128,512]{1,0:T(8,128)(2,1)S(1)}, u32[]{:S(2)}, u32[]{:S(2)}) collective-permute-start(bf16[128,512]{1,0:T(8,128)(2,1)S(1)} %get-tuple-element.85), channel_id=1, source_target_pairs={{0,24},{16,8},{24,0},{8,16},{1,25},{17,9},{25,1},{9,17},{2,26},{18... | collective-permute-start | bytes 393224 | tf_op jit(solution)/shard_map/kernel/ppermute | solution.py:34
  74.0 5.1 %collective-permute-start.30 = (bf16[32,1280]{1,0:T(8,128)(2,1)S(1)}, bf16[32,1280]{1,0:T(8,128)(2,1)S(1)}, u32[]{:S(2)}, u32[]{:S(2)}) collective-permute-start(bf16[32,1280]{1,0:T(8,128)(2,1)S(1)} %get-tuple-element.112.refs_0_), channel_id=1, source_target_pairs={{0,2},{1,3},{2,0},{3,1},{4,6},{5,7},{6,4},{7,5},{8,10},{9,11},{10,... | collective-permute-start | bytes 245768 | tf_op jit(solution)/shard_map/kernel/ppermute | solution.py:24
  75.2 5.6 %collective-permute-start.35 = (bf16[32,1280]{1,0:T(8,128)(2,1)S(1)}, bf16[32,1280]{1,0:T(8,128)(2,1)S(1)}, u32[]{:S(2)}, u32[]{:S(2)}) collective-permute-start(bf16[32,1280]{1,0:T(8,128)(2,1)S(1)} %get-tuple-element.112.refs_0_), channel_id=1, source_target_pairs={{0,6},{1,7},{2,4},{3,5},{4,2},{5,3},{6,0},{7,1},{8,14},{9,15},{10,... | collective-permute-start | bytes 245768 | tf_op jit(solution)/shard_map/kernel/ppermute | solution.py:24
  76.8 4.8 %collective-permute-start.33 = (bf16[32,1280]{1,0:T(8,128)(2,1)S(1)}, bf16[32,1280]{1,0:T(8,128)(2,1)S(1)}, u32[]{:S(2)}, u32[]{:S(2)}) collective-permute-start(bf16[32,1280]{1,0:T(8,128)(2,1)S(1)} %get-tuple-element.112.refs_0_), channel_id=1, source_target_pairs={{0,4},{1,5},{2,6},{3,7},{4,0},{5,1},{6,2},{7,3},{8,12},{9,13},{10,... | collective-permute-start | bytes 245768 | tf_op jit(solution)/shard_map/kernel/ppermute | solution.py:24
  77.6 6.5 %collective-permute-start.29 = (bf16[32,1280]{1,0:T(8,128)(2,1)S(1)}, bf16[32,1280]{1,0:T(8,128)(2,1)S(1)}, u32[]{:S(2)}, u32[]{:S(2)}) collective-permute-start(bf16[32,1280]{1,0:T(8,128)(2,1)S(1)} %get-tuple-element.112.refs_0_), channel_id=1, source_target_pairs={{0,1},{1,0},{2,3},{3,2},{4,5},{5,4},{6,7},{7,6},{8,9},{9,8},{10,11... | collective-permute-start | bytes 245768 | tf_op jit(solution)/shard_map/kernel/ppermute | solution.py:24
  80.8 3.3 %collective-permute-start.36 = (bf16[32,1280]{1,0:T(8,128)(2,1)S(1)}, bf16[32,1280]{1,0:T(8,128)(2,1)S(1)}, u32[]{:S(2)}, u32[]{:S(2)}) collective-permute-start(bf16[32,1280]{1,0:T(8,128)(2,1)S(1)} %collective-permute-done.35.refs_6_), channel_id=1, source_target_pairs={{0,1},{1,0},{2,3},{3,2},{4,5},{5,4},{6,7},{7,6},{8,9},{9,8},{10,11... | collective-permute-start | bytes 245768 | tf_op jit(solution)/shard_map/kernel/ppermute | solution.py:24
  81.6 2.5 %collective-permute-start.34 = (bf16[32,1280]{1,0:T(8,128)(2,1)S(1)}, bf16[32,1280]{1,0:T(8,128)(2,1)S(1)}, u32[]{:S(2)}, u32[]{:S(2)}) collective-permute-start(bf16[32,1280]{1,0:T(8,128)(2,1)S(1)} %collective-permute-done.33.refs_4_), channel_id=1, source_target_pairs={{0,1},{1,0},{2,3},{3,2},{4,5},{5,4},{6,7},{7,6},{8,9},{9,8},{10,11... | collective-permute-start | bytes 245768 | tf_op jit(solution)/shard_map/kernel/ppermute | solution.py:24
  81.6 2.5 %collective-permute-start.32 = (bf16[32,1280]{1,0:T(8,128)(2,1)S(1)}, bf16[32,1280]{1,0:T(8,128)(2,1)S(1)}, u32[]{:S(2)}, u32[]{:S(2)}) collective-permute-start(bf16[32,1280]{1,0:T(8,128)(2,1)S(1)} %collective-permute-done.30.refs_2_), channel_id=1, source_target_pairs={{0,1},{1,0},{2,3},{3,2},{4,5},{5,4},{6,7},{7,6},{8,9},{9,8},{10,11... | collective-permute-start | bytes 245768 | tf_op jit(solution)/shard_map/kernel/ppermute | solution.py:24
  82.1 6.7 %collective-permute-start.37 = (bf16[128,512]{1,0:T(8,128)(2,1)S(1)}, bf16[128,512]{1,0:T(8,128)(2,1)S(1)}, u32[]{:S(2)}, u32[]{:S(2)}) collective-permute-start(bf16[128,512]{1,0:T(8,128)(2,1)S(1)} %get-tuple-element.88), channel_id=1, source_target_pairs={{0,8},{16,0},{24,16},{8,24},{1,9},{17,1},{25,17},{9,25},{2,10},{18... | collective-permute-start | bytes 393224 | tf_op jit(solution)/shard_map/kernel/ppermute | solution.py:34
  91.4 5.4 %collective-permute-start.38 = (bf16[3,272,512]{2,1,0:T(8,128)(2,1)S(1)}, bf16[3,272,512]{2,1,0:T(8,128)(2,1)S(1)}, u32[]{:S(2)}, u32[]{:S(2)}) collective-permute-start(bf16[3,272,512]{2,1,0:T(8,128)(2,1)S(1)} %d_act_matmul.5), channel_id=1, source_target_pairs={{0,1},{1,0},{2,3},{3,2},{4,5},{5,4},{6,7},{7,6},{8,9},{9,8},{10,11... | collective-permute-start | bytes 2506760 | tf_op jit(solution)/shard_map/d_act/ppermute | solution.py:24
  91.5 2.7 %collective-permute-start.41 = (bf16[1,272,512]{2,1,0:T(8,128)(2,1)S(1)}, bf16[1,272,512]{2,1,0:T(8,128)(2,1)S(1)}, u32[]{:S(2)}, u32[]{:S(2)}) collective-permute-start(bf16[1,272,512]{2,1,0:T(8,128)(2,1)S(1)} %d_act_matmul.4), channel_id=1, source_target_pairs={{0,1},{1,0},{2,3},{3,2},{4,5},{5,4},{6,7},{7,6},{8,9},{9,8},{10,11... | collective-permute-start | bytes 835592 | tf_op jit(solution)/shard_map/d_act/ppermute | solution.py:24
  92.1 11.3 %collective-permute-start.43 = (bf16[384,512]{1,0:T(8,128)(2,1)S(1)}, bf16[384,512]{1,0:T(8,128)(2,1)S(1)}, u32[]{:S(2)}, u32[]{:S(2)}) collective-permute-start(bf16[384,512]{1,0:T(8,128)(2,1)S(1)} %constant_dynamic-update-slice_fusion.3.refs_8_), channel_id=1, source_target_pairs={{0,1},{1,0},{2,3},{3,2},{4,5},{5,4},{6,7},{7,6},{8,9},{9,8},{10,11... | collective-permute-start | bytes 1179656 | tf_op jit(solution)/shard_map/grad_weight/ppermute | solution.py:24
  95.3 11.0 %collective-permute-start.42 = (bf16[272,512]{1,0:T(8,128)(2,1)S(1)}, bf16[272,512]{1,0:T(8,128)(2,1)S(1)}, u32[]{:S(2)}, u32[]{:S(2)}) collective-permute-start(bf16[272,512]{1,0:T(8,128)(2,1)S(1)} %d_act_matmul.7), channel_id=1, source_target_pairs={{0,6},{1,7},{2,4},{3,5},{4,2},{5,3},{6,0},{7,1},{8,14},{9,15},{10,... | collective-permute-start | bytes 835592 | tf_op jit(solution)/shard_map/d_act/ppermute | solution.py:24
  98.3 12.6 %collective-permute-start.39 = (bf16[272,512]{1,0:T(8,128)(2,1)S(1)}, bf16[272,512]{1,0:T(8,128)(2,1)S(1)}, u32[]{:S(2)}, u32[]{:S(2)}) collective-permute-start(bf16[272,512]{1,0:T(8,128)(2,1)S(1)} %get-tuple-element.95), channel_id=1, source_target_pairs={{0,2},{1,3},{2,0},{3,1},{4,6},{5,7},{6,4},{7,5},{8,10},{9,11},{10,... | collective-permute-start | bytes 835592 | tf_op jit(solution)/shard_map/d_act/ppermute | solution.py:24
  99.9 11.0 %collective-permute-start.40 = (bf16[272,512]{1,0:T(8,128)(2,1)S(1)}, bf16[272,512]{1,0:T(8,128)(2,1)S(1)}, u32[]{:S(2)}, u32[]{:S(2)}) collective-permute-start(bf16[272,512]{1,0:T(8,128)(2,1)S(1)} %get-tuple-element.96), channel_id=1, source_target_pairs={{0,4},{1,5},{2,6},{3,7},{4,0},{5,1},{6,2},{7,3},{8,12},{9,13},{10,... | collective-permute-start | bytes 835592 | tf_op jit(solution)/shard_map/d_act/ppermute | solution.py:24
  111.6 5.7 %collective-permute-start.46 = (f32[8,512]{1,0:T(8,128)S(1)}, f32[8,512]{1,0:T(8,128)S(1)}, u32[]{:S(2)}, u32[]{:S(2)}) collective-permute-start(f32[8,512]{1,0:T(8,128)S(1)} %pad_maximum_fusion.1.refs_0_), channel_id=1, source_target_pairs={{0,24},{8,16},{16,8},{24,0},{1,25},{9,17},{17,9},{25,1},{2,26},{10... | collective-permute-start | bytes 49160 | tf_op jit(solution)/shard_map/norm_backward/ppermute | solution.py:24
  114.1 4.6 %collective-permute-start.45 = (f32[8,512]{1,0:T(8,128)S(1)}, f32[8,512]{1,0:T(8,128)S(1)}, u32[]{:S(2)}, u32[]{:S(2)}) collective-permute-start(f32[8,512]{1,0:T(8,128)S(1)} %pad_maximum_fusion.1.refs_0_), channel_id=1, source_target_pairs={{0,16},{8,24},{16,0},{24,8},{1,17},{9,25},{17,1},{25,9},{2,18},{10... | collective-permute-start | bytes 49160 | tf_op jit(solution)/shard_map/norm_backward/ppermute | solution.py:24
  114.3 4.5 %collective-permute-start.44 = (f32[8,512]{1,0:T(8,128)S(1)}, f32[8,512]{1,0:T(8,128)S(1)}, u32[]{:S(2)}, u32[]{:S(2)}) collective-permute-start(f32[8,512]{1,0:T(8,128)S(1)} %pad_maximum_fusion.1.refs_0_), channel_id=1, source_target_pairs={{0,8},{8,0},{16,24},{24,16},{1,9},{9,1},{17,25},{25,17},{2,10},{10... | collective-permute-start | bytes 49160 | tf_op jit(solution)/shard_map/norm_backward/ppermute | solution.py:24
  (2 other events, 19.5 us)

commit v17 on v16

--- a/solution.py
+++ b/solution.py
@@ -283,44 +283,45 @@
     return rows[0:1].astype(f32) + rows[1:2].astype(f32) + rows[2:3].astype(f32)
 
 
-def d_act_kernel(ks, adds, tall, width, place_ref, dz_ref, share_ref, w_ref, *refs):
+def d_act_kernel(evens, odds, tall, width, place_ref, dz_ref, share_ref, w_ref, *refs):
     local_rows = tall // 2
     dz = jnp.concatenate([dz_ref[0, :local_rows], dz_ref[1, :local_rows]], axis=0)
     share = share_ref[0:1, 0:1]
-    for j, k in enumerate(ks):
-        part = lax.dot_general(
+    got, outs = (refs[0], refs[1:]) if evens else (None, refs)
+
+    def product(k):
+        return lax.dot_general(
             dz,
             weight_rows(place_ref, w_ref, k, width),
             (((1,), (1,)), ((), ())),
             preferred_element_type=f32,
         )
-        whole_share = share
-        out = refs[j + 1] if adds else refs[0].at[j]
-        if adds:
-            part = part + refs[0][j, :tall].astype(f32)
-            whole_share = share + share_of(refs[0][j, tall:])[:, 0:1]
-        out[:tall] = part.astype(out.dtype)
-        out[tall:] = share_rows(whole_share, width, out.dtype)
-
-
-def d_act_call(place, dz, share, weight, n_batch, n_col, ks, got):
+
+    for j, k in enumerate(evens):
+        out = outs[j]
+        out[:tall] = (product(k) + got[j, :tall].astype(f32)).astype(out.dtype)
+        out[tall:] = share_rows(share + share_of(got[j, tall:])[:, 0:1], width, out.dtype)
+    for j, k in enumerate(odds):
+        outs[-1][j, :tall] = product(k).astype(bf16)
+        outs[-1][j, tall:] = share_rows(share, width, bf16)
+
+
+def d_act_call(place, dz, share, weight, n_batch, n_col, evens, got, odds):
     width = weight.shape[0] // n_col
     tall = 2 * dz.shape[1] // n_batch
     columns = weight.shape[1]
-    long = tall + EXTRA
-    operands = [place, dz, share, weight]
-    if got is None:
-        out_shape = (jax.ShapeDtypeStruct((len(ks), long, width), bf16),)
-    else:
-        operands.append(got)
-        out_shape = tuple(jax.ShapeDtypeStruct((long, width), bf16 if k else f32) for k in ks)
-    return pl.pallas_call(
-        functools.partial(d_act_kernel, tuple(ks), got is not None, tall, width),
+    long, count = tall + EXTRA, len(evens) + len(odds)
+    operands = [place, dz, share, weight] + ([got] if evens else [])
+    out_shape = tuple(jax.ShapeDtypeStruct((long, width), bf16 if k else f32) for k in evens)
+    if odds:
+        out_shape += (jax.ShapeDtypeStruct((len(odds), long, width), bf16),)
+    return pl.pallas_call(
+        functools.partial(d_act_kernel, tuple(evens), tuple(odds), tall, width),
         out_shape=out_shape,
         in_specs=[IN_SMEM] + [IN_VMEM] * (len(operands) - 1),
         out_specs=(IN_VMEM,) * len(out_shape),
         compiler_params=params(8),
-        cost_estimate=cost(2 * tall * width * columns * len(ks), 2 * len(ks) * width * tall),
+        cost_estimate=cost(2 * tall * width * columns * count, 2 * count * width * tall),
         name="d_act_matmul",
     )(*operands)
 
@@ -600,19 +601,18 @@
         dz, blocks[2 * third :] = lax.optimization_barrier((dz, blocks[2 * third :]))
     with jax.named_scope("d_act"):
         crossing = [k for k in far if k & (k - 1)]
-        groups = [crossing, [k for k in far if k not in crossing] + [0]]
-        got = []
-        for ks in groups:
-            (away,) = d_act_call(
-                place, dz, share, held_weight, n_batch, n_col, [k + 1 for k in ks], None
-            )
-            away, share = lax.optimization_barrier((away, share))
-            got.append(xor_send(away, "col", 1))
-        arrived = {}
-        for ks, part in zip(groups, got):
-            summed = d_act_call(place, dz, share, held_weight, n_batch, n_col, ks, part)
-            for k, piece in zip(ks, summed):
-                arrived[k] = xor_send(piece, "col", k) if k else piece
+        others = [k for k in far if k not in crossing] + [0]
+
+        def products(evens, got, odds):
+            return d_act_call(place, dz, share, held_weight, n_batch, n_col, evens, got, odds)
+
+        (away,) = products([], None, [k + 1 for k in crossing])
+        *crossed, away = products(crossing, xor_send(away, "col", 1), [k + 1 for k in others])
+        summed = products(others, xor_send(away, "col", 1), [])
+        arrived = {
+            k: xor_send(piece, "col", k) if k else piece
+            for k, piece in zip(crossing + others, list(crossed) + list(summed))
+        }
         d_act = arrived.pop(0)
         arrived = [arrived[k] for k in far]
     with jax.named_scope("grad_weight"):
@@ -644,8 +644,13 @@
                 jnp.broadcast_to(share, (2 * n_view, width)),
             ]
         )
+        k = 1
+        while 2 * k < n_batch:
+            sums = sums + xor_send(sums, "batch", k)
+            k *= 2
+        sums = [sums, xor_send(sums, "batch", k)]
         loss, grad_gain, grad_bias, views_gradient = finish_call(
-            exchange(sums, "batch"), d_pre, normalised, norm_scale_gain, inverse_deviation, rows
+            sums, d_pre, normalised, norm_scale_gain, inverse_deviation, rows
         )
     return (loss[0, 0], grad_weight, grad_gain[0], grad_bias[0], views_gradient)
 

time: 120 us -> 120 us (level)
  waiting for transfers between devices: 37.6 us -> 39.5 us
  starting transfers between devices: 45.5 us -> 44.3 us
    ppermute x38 -> x37, waiting for transfers between devices: 30.1 us -> 32.1 us  [xor_send(): return lax.ppermute(x, axis, [(i, i ^ k) for i in range(n)])]
    ppermute x38 -> x37, starting transfers between devices: 33.4 us -> 32.2 us  [xor_send(): return lax.ppermute(x, axis, [(i, i ^ k) for i in range(n)])]
    pallas_call x4 -> x3, Pallas kernels: 5.17 us -> 4.43 us  [d_act_call(): pl.pallas_call(functools.partial(d_act_kernel, tuple(evens), tuple(odds),...]
  transfers between devices with their start and end apart: 47 -> 46, of which waited for: 19 -> 20; matrix products, arithmetic and copies ran while one was open for 0% -> 0% of each run, Pallas kernels for 24% -> 23%
where the time goes in v17:
time: 120 us
  starting transfers between devices  44.3 us (37%)
  waiting for transfers between devices  39.5 us (33%)
  Pallas kernels  31.5 us (26%)
  other arithmetic  3.23 us (3%)
    ppermute x37, starting transfers between devices, xor_send(): return lax.ppermute(x, axis, [(i, i ^ k) for i in range(n)])  32.2 us
    ppermute x37, waiting for transfers between devices, xor_send(): return lax.ppermute(x, axis, [(i, i ^ k) for i in range(n)])  32.1 us
    ppermute x9, starting transfers between devices, ring_send(): lax.ppermute(x, axis, [(order[i], order[(i + d) % n]) for i in range(n)])  12.1 us
    pallas_call x5, Pallas kernels, z_call(): pl.pallas_call(functools.partial(z_kernel, tuple(ks), before is None, las...  8.96 us
    ppermute x9, waiting for transfers between devices, ring_send(): lax.ppermute(x, axis, [(order[i], order[(i + d) % n]) for i in range(n)])  7.43 us
    pallas_call x2, Pallas kernels, weight_grad_call(): pl.pallas_call(functools.partial(weight_grad_kernel, rows // (near[0][0]....  5.79 us
    pallas_call x1, Pallas kernels, dz_call(): pl.pallas_call(functools.partial(dz_kernel, n_batch, n_col, tile, constan...  4.67 us
    pallas_call x3, Pallas kernels, d_act_call(): pl.pallas_call(functools.partial(d_act_kernel, tuple(evens), tuple(odds),...  4.43 us
  transfers between devices with their start and end apart: 46, of which 20 were waited for; matrix products, arithmetic and copies ran while one was open for 0% of the time, Pallas kernels for 23%

profile of v17, /device:TPU:0, one launch (start us, length us, event | category | flops | bytes accessed | tf_op | source)
XLA Modules:
  0.0 119.7 jit_solution(1453766541320020562)
XLA Ops:
  1.7 1.0 fusion.8
  2.8 5.1 %collective-permute-start.2 = (f32[4,512]{1,0:T(4,128)S(1)}, f32[4,512]{1,0:T(4,128)S(1)}, u32[]{:S(2)}, u32[]{:S(2)}) collective-permute-start(f32[4,512]{1,0:T(4,128)S(1)} %pad_maximum_fusion.2), channel_id=1, source_target_pairs={{0,24},{8,16},{16,8},{24,0},{1,25},{9,17},{17,9},{25,1},{2,26},{10... | collective-permute-start | bytes 24584 | tf_op jit(solution)/shard_map/norm_stats/ppermute | solution.py:24
  8.6 3.5 %weight_load.1 = (bf16[4096,1024]{1,0:T(8,128)(2,1)S(1)}, f32[4,512]{1,0:T(4,128)S(1)}) custom-call(bf16[4096,1024]{1,0:T(8,128)(2,1)} %w_ref), custom_call_target="tpu_custom_call" | custom-call | bytes 16777216 | tf_op jit(solution)/shard_map/weight_load/weight_load/pallas_call | solution.py:78
  12.9 2.5 %collective-permute-start.7 = (bf16[256,512]{1,0:T(8,128)(2,1)S(1)}, bf16[256,512]{1,0:T(8,128)(2,1)S(1)}, u32[]{:S(2)}, u32[]{:S(2)}) collective-permute-start(bf16[256,512]{1,0:T(8,128)(2,1)S(1)} %bitcast.29), channel_id=1, source_target_pairs={{0,6},{1,7},{2,4},{3,5},{4,2},{5,3},{6,0},{7,1},{8,14},{9,15},{10,... | collective-permute-start | bytes 786440 | tf_op jit(solution)/shard_map/act_gather/ppermute | solution.py:24
  16.5 2.1 %collective-permute-start.11 = (bf16[128,512]{1,0:T(8,128)(2,1)S(1)}, bf16[128,512]{1,0:T(8,128)(2,1)S(1)}, u32[]{:S(2)}, u32[]{:S(2)}) collective-permute-start(bf16[128,512]{1,0:T(8,128)(2,1)S(1)} %slice_bitcast_fusion.1), channel_id=1, source_target_pairs={{0,16},{16,24},{24,8},{8,0},{1,17},{17,25},{25,9},{9,1},{2,18},{18... | collective-permute-start | bytes 393224 | tf_op jit(solution)/shard_map/act_gather/ppermute | solution.py:34
  18.5 1.4 %collective-permute-start.12 = (bf16[128,512]{1,0:T(8,128)(2,1)S(1)}, bf16[128,512]{1,0:T(8,128)(2,1)S(1)}, u32[]{:S(2)}, u32[]{:S(2)}) collective-permute-start(bf16[128,512]{1,0:T(8,128)(2,1)S(1)} %slice_bitcast_fusion.1), channel_id=1, source_target_pairs={{0,24},{16,8},{24,0},{8,16},{1,25},{17,9},{25,1},{9,17},{2,26},{18... | collective-permute-start | bytes 393224 | tf_op jit(solution)/shard_map/act_gather/ppermute | solution.py:34
  20.0 1.2 %z_matmul.5.refs_4_ = f32[256,1024]{1,0:T(8,128)S(1)} custom-call(s32[2]{0:T(128)S(1)} %pad_add_fusion.place_ref, bf16[256,512]{1,0:T(8,128)(2,1)S(1)} %bitcast.32, bf16[256,512]{1,0:T(8,128)(2,1)S(1)} %collective-permute-done.9.refs_1_.refs_0_, bf16[4096,1024]{1,0:T(8,128)(2,1)S(1)} %get-tuple-element.61.refs_2_.refs_3_.refs_5_.w_ref), custom_call_target="tpu_custom_call" | custom-call | flops 536870912 | bytes 524288 | tf_op jit(solution)/shard_map/z/z_matmul/pallas_call | solution.py:126
  21.2 1.8 %collective-permute-done.7.refs_2_.refs_3_ = bf16[256,512]{1,0:T(8,128)(2,1)S(1)} collective-permute-done((bf16[256,512]{1,0:T(8,128)(2,1)S(1)}, bf16[256,512]{1,0:T(8,128)(2,1)S(1)}, u32[]{:S(2)}, u32[]{:S(2)}) %collective-permute-start.7) | collective-permute-done | bytes 262176 | tf_op jit(solution)/shard_map/act_gather/ppermute | solution.py:24
  23.0 1.0 collective-permute-start.10
  24.0 4.1 %collective-permute-done.5.refs_1_.refs_2_ = bf16[256,512]{1,0:T(8,128)(2,1)S(1)} collective-permute-done((bf16[256,512]{1,0:T(8,128)(2,1)S(1)}, bf16[256,512]{1,0:T(8,128)(2,1)S(1)}, u32[]{:S(2)}, u32[]{:S(2)}) %collective-permute-start.5) | collective-permute-done | bytes 262176 | tf_op jit(solution)/shard_map/act_gather/ppermute | solution.py:24
  28.6 1.5 %z_matmul.6.refs_4_ = f32[256,1024]{1,0:T(8,128)S(1)} custom-call(s32[2]{0:T(128)S(1)} %pad_add_fusion.place_ref, bf16[256,512]{1,0:T(8,128)(2,1)S(1)} %collective-permute-done.3.refs_0_.refs_1_, bf16[256,512]{1,0:T(8,128)(2,1)S(1)} %collective-permute-done.5.refs_1_.refs_2_, bf16[256,512]{1,0:T(8,128)(2,1)S(1)} %collective-permute-done.7.refs_2_.refs_3_, ...), custom_call_target="tpu_custom_call" | custom-call | flops 805306368 | bytes 524288 | tf_op jit(solution)/shard_map/z/z_matmul/pallas_call | solution.py:126
  30.4 1.2 collective-permute-done.10
  31.6 1.6 %collective-permute-start.17 = (bf16[384,512]{1,0:T(8,128)(2,1)S(1)}, bf16[384,512]{1,0:T(8,128)(2,1)S(1)}, u32[]{:S(2)}, u32[]{:S(2)}) collective-permute-start(bf16[384,512]{1,0:T(8,128)(2,1)S(1)} %constant_dynamic-update-slice_fusion.refs_0_.refs_4_), channel_id=1, source_target_pairs={{0,4},{1,5},{2,6},{3,7},{4,0},{5,1},{6,2},{7,3},{8,12},{9,13},{10,... | collective-permute-start | bytes 1179656 | tf_op jit(solution)/shard_map/z/ppermute | solution.py:24
  33.2 1.5 %collective-permute-start.15 = (bf16[384,512]{1,0:T(8,128)(2,1)S(1)}, bf16[384,512]{1,0:T(8,128)(2,1)S(1)}, u32[]{:S(2)}, u32[]{:S(2)}) collective-permute-start(bf16[384,512]{1,0:T(8,128)(2,1)S(1)} %constant_dynamic-update-slice_fusion.refs_0_.refs_4_), channel_id=1, source_target_pairs={{0,2},{1,3},{2,0},{3,1},{4,6},{5,7},{6,4},{7,5},{8,10},{9,11},{10,... | collective-permute-start | bytes 1179656 | tf_op jit(solution)/shard_map/z/ppermute | solution.py:24
  34.7 1.5 %z_matmul.7 = (bf16[128,1024]{1,0:T(8,128)(2,1)S(1)}, bf16[128,1024]{1,0:T(8,128)(2,1)S(1)}) custom-call(s32[2]{0:T(128)S(1)} %pad_add_fusion.place_ref, bf16[256,512]{1,0:T(8,128)(2,1)S(1)} %collective-permute-done.4.refs_0_.refs_1_, bf16[256,512]{1,0:T(8,128)(2,1)S(1)} %collective-permute-done.6.refs_1_.refs_2_, ...), custom_call_target="tpu_custom_call" | custom-call | flops 805306368 | bytes 524288 | tf_op jit(solution)/shard_map/z/z_matmul/pallas_call | solution.py:126
  36.3 6.4 %collective-permute-done.17.refs_2_.refs_6_ = bf16[384,512]{1,0:T(8,128)(2,1)S(1)} collective-permute-done((bf16[384,512]{1,0:T(8,128)(2,1)S(1)}, bf16[384,512]{1,0:T(8,128)(2,1)S(1)}, u32[]{:S(2)}, u32[]{:S(2)}) %collective-permute-start.17) | collective-permute-done | bytes 393248 | tf_op jit(solution)/shard_map/z/ppermute | solution.py:24
  42.7 1.6 %collective-permute-start.19 = (bf16[192,512]{1,0:T(8,128)(2,1)S(1)}, bf16[192,512]{1,0:T(8,128)(2,1)S(1)}, u32[]{:S(2)}, u32[]{:S(2)}) collective-permute-start(bf16[192,512]{1,0:T(8,128)(2,1)S(1)} %slice.149), channel_id=1, source_target_pairs={{0,2},{1,3},{2,0},{3,1},{4,6},{5,7},{6,4},{7,5},{8,10},{9,11},{10,... | collective-permute-start | bytes 589832 | tf_op jit(solution)/shard_map/z/ppermute | solution.py:24
  44.3 1.6 %collective-permute-start.20 = (bf16[192,512]{1,0:T(8,128)(2,1)S(1)}, bf16[192,512]{1,0:T(8,128)(2,1)S(1)}, u32[]{:S(2)}, u32[]{:S(2)}) collective-permute-start(bf16[192,512]{1,0:T(8,128)(2,1)S(1)} %slice.150), channel_id=1, source_target_pairs={{0,4},{1,5},{2,6},{3,7},{4,0},{5,1},{6,2},{7,3},{8,12},{9,13},{10,... | collective-permute-start | bytes 589832 | tf_op jit(solution)/shard_map/z/ppermute | solution.py:24
  47.6 1.9 %z_matmul.8.refs_6_ = f32[384,1024]{1,0:T(8,128)S(1)} custom-call(s32[2]{0:T(128)S(1)} %pad_add_fusion.place_ref, bf16[384,512]{1,0:T(8,128)(2,1)S(1)} %constant_dynamic-update-slice_fusion.refs_0_.refs_4_, bf16[384,512]{1,0:T(8,128)(2,1)S(1)} %collective-permute-done.15.refs_1_.refs_5_, bf16[384,512]{1,0:T(8,128)(2,1)S(1)} %collective-permute-done.17.refs_2_.refs_6_, ...), custom_call_target="tpu_custom_call" | custom-call | flops 1207959552 | bytes 786432 | tf_op jit(solution)/shard_map/z_far/z_matmul/pallas_call | solution.py:126
  50.1 2.6 %collective-permute-done.21.refs_5_.refs_13_ = bf16[128,1024]{1,0:T(8,128)(2,1)S(1)} collective-permute-done((bf16[128,1024]{1,0:T(8,128)(2,1)S(1)}, bf16[128,1024]{1,0:T(8,128)(2,1)S(1)}, u32[]{:S(2)}, u32[]{:S(2)}) %collective-permute-start.21) | collective-permute-done | bytes 262176 | tf_op jit(solution)/shard_map/z_ring/ppermute | solution.py:34
  52.7 2.0 %collective-permute-start.23 = (bf16[128,1024]{1,0:T(8,128)(2,1)S(1)}, bf16[128,1024]{1,0:T(8,128)(2,1)S(1)}, u32[]{:S(2)}, u32[]{:S(2)}) collective-permute-start(bf16[128,1024]{1,0:T(8,128)(2,1)S(1)} %collective-permute-done.21.refs_5_.refs_13_), channel_id=1, source_target_pairs={{0,16},{16,24},{24,8},{8,0},{1,17},{17,25},{25,9},{9,1},{2,18},{18... | collective-permute-start | bytes 786440 | tf_op jit(solution)/shard_map/z_far/ppermute | solution.py:34
  55.5 2.7 %z_matmul.9 = (bf16[128,1024]{1,0:T(8,128)(2,1)S(1)}, bf16[128,1024]{1,0:T(8,128)(2,1)S(1)}, bf16[128,1024]{1,0:T(8,128)(2,1)S(1)}) custom-call(s32[2]{0:T(128)S(1)} %pad_add_fusion.place_ref, bf16[384,512]{1,0:T(8,128)(2,1)S(1)} %collective-permute-done.13.refs_0_.refs_4_, bf16[384,512]{1,0:T(8,128)(2,1)S(1)} %collective-permute-done.16.refs_1_.refs_5_, ...), custom_call_target="tpu_custom_call" | custom-call | flops 2013265920 | bytes 786432 | tf_op jit(solution)/shard_map/z_far/z_matmul/pallas_call | solution.py:126
  58.2 3.6 %collective-permute-done.23.refs_7_.refs_15_ = bf16[128,1024]{1,0:T(8,128)(2,1)S(1)} collective-permute-done((bf16[128,1024]{1,0:T(8,128)(2,1)S(1)}, bf16[128,1024]{1,0:T(8,128)(2,1)S(1)}, u32[]{:S(2)}, u32[]{:S(2)}) %collective-permute-start.23) | collective-permute-done | bytes 262176 | tf_op jit(solution)/shard_map/z_far/ppermute | solution.py:34
  61.8 2.6 %kernel_strip.1 = (f32[4,32,1280]{2,1,0:T(8,128)S(1)}, bf16[4,32,1280]{2,1,0:T(8,128)(2,1)S(1)}) custom-call(s32[2]{0:T(128)S(1)} %pad_add_fusion.place_ref, bf16[128,1024]{1,0:T(8,128)(2,1)S(1)} %get-tuple-element.65.refs_0_.refs_8_, bf16[128,1024]{1,0:T(8,128)(2,1)S(1)} %get-tuple-element.66.refs_1_.refs_9_, ...), custom_call_target="tpu_custom_call" | custom-call | flops 671088640 | bytes 2097152 | tf_op jit(solution)/shard_map/kernel/kernel_strip/pallas_call | solution.py:173
  64.5 1.6 %collective-permute-done.25 = bf16[4,32,1280]{2,1,0:T(8,128)(2,1)S(1)} collective-permute-done((bf16[4,32,1280]{2,1,0:T(8,128)(2,1)S(1)}, bf16[4,32,1280]{2,1,0:T(8,128)(2,1)S(1)}, u32[]{:S(2)}, u32[]{:S(2)}) %collective-permute-start.25) | collective-permute-done | bytes 327712 | tf_op jit(solution)/shard_map/kernel/ppermute | solution.py:24
  67.0 1.4 %collective-permute-start.28 = (bf16[32,1280]{1,0:T(8,128)(2,1)S(1)}, bf16[32,1280]{1,0:T(8,128)(2,1)S(1)}, u32[]{:S(2)}, u32[]{:S(2)}) collective-permute-start(bf16[32,1280]{1,0:T(8,128)(2,1)S(1)} %get-tuple-element.115), channel_id=1, source_target_pairs={{0,6},{1,7},{2,4},{3,5},{4,2},{5,3},{6,0},{7,1},{8,14},{9,15},{10,... | collective-permute-start | bytes 245768 | tf_op jit(solution)/shard_map/kernel/ppermute | solution.py:24
  68.4 1.4 %collective-permute-start.27 = (bf16[32,1280]{1,0:T(8,128)(2,1)S(1)}, bf16[32,1280]{1,0:T(8,128)(2,1)S(1)}, u32[]{:S(2)}, u32[]{:S(2)}) collective-permute-start(bf16[32,1280]{1,0:T(8,128)(2,1)S(1)} %get-tuple-element.116), channel_id=1, source_target_pairs={{0,4},{1,5},{2,6},{3,7},{4,0},{5,1},{6,2},{7,3},{8,12},{9,13},{10,... | collective-permute-start | bytes 245768 | tf_op jit(solution)/shard_map/kernel/ppermute | solution.py:24
  69.8 2.2 %collective-permute-start.31 = (bf16[128,512]{1,0:T(8,128)(2,1)S(1)}, bf16[128,512]{1,0:T(8,128)(2,1)S(1)}, u32[]{:S(2)}, u32[]{:S(2)}) collective-permute-start(bf16[128,512]{1,0:T(8,128)(2,1)S(1)} %get-tuple-element.83), channel_id=1, source_target_pairs={{0,24},{16,8},{24,0},{8,16},{1,25},{17,9},{25,1},{9,17},{2,26},{18... | collective-permute-start | bytes 393224 | tf_op jit(solution)/shard_map/kernel/ppermute | solution.py:34
  72.8 1.2 %collective-permute-done.27 = bf16[32,1280]{1,0:T(8,128)(2,1)S(1)} collective-permute-done((bf16[32,1280]{1,0:T(8,128)(2,1)S(1)}, bf16[32,1280]{1,0:T(8,128)(2,1)S(1)}, u32[]{:S(2)}, u32[]{:S(2)}) %collective-permute-start.27) | collective-permute-done | bytes 81952 | tf_op jit(solution)/shard_map/kernel/ppermute | solution.py:24
  74.0 1.2 collective-permute-start.30
  75.2 1.6 %collective-permute-start.35 = (bf16[32,1280]{1,0:T(8,128)(2,1)S(1)}, bf16[32,1280]{1,0:T(8,128)(2,1)S(1)}, u32[]{:S(2)}, u32[]{:S(2)}) collective-permute-start(bf16[32,1280]{1,0:T(8,128)(2,1)S(1)} %get-tuple-element.108.refs_0_), channel_id=1, source_target_pairs={{0,6},{1,7},{2,4},{3,5},{4,2},{5,3},{6,0},{7,1},{8,14},{9,15},{10,... | collective-permute-start | bytes 245768 | tf_op jit(solution)/shard_map/kernel/ppermute | solution.py:24
  77.6 1.6 %collective-permute-done.30.refs_2_ = bf16[32,1280]{1,0:T(8,128)(2,1)S(1)} collective-permute-done((bf16[32,1280]{1,0:T(8,128)(2,1)S(1)}, bf16[32,1280]{1,0:T(8,128)(2,1)S(1)}, u32[]{:S(2)}, u32[]{:S(2)}) %collective-permute-start.30) | collective-permute-done | bytes 81952 | tf_op jit(solution)/shard_map/kernel/ppermute | solution.py:24
  79.2 1.6 %collective-permute-done.35.refs_6_ = bf16[32,1280]{1,0:T(8,128)(2,1)S(1)} collective-permute-done((bf16[32,1280]{1,0:T(8,128)(2,1)S(1)}, bf16[32,1280]{1,0:T(8,128)(2,1)S(1)}, u32[]{:S(2)}, u32[]{:S(2)}) %collective-permute-start.35) | collective-permute-done | bytes 81952 | tf_op jit(solution)/shard_map/kernel/ppermute | solution.py:24
  82.1 2.0 %collective-permute-start.37 = (bf16[128,512]{1,0:T(8,128)(2,1)S(1)}, bf16[128,512]{1,0:T(8,128)(2,1)S(1)}, u32[]{:S(2)}, u32[]{:S(2)}) collective-permute-start(bf16[128,512]{1,0:T(8,128)(2,1)S(1)} %get-tuple-element.86), channel_id=1, source_target_pairs={{0,8},{16,0},{24,16},{8,24},{1,9},{17,1},{25,17},{9,25},{2,10},{18... | collective-permute-start | bytes 393224 | tf_op jit(solution)/shard_map/kernel/ppermute | solution.py:34
  84.1 4.7 %embedding_gradient.1 = (bf16[2,512,1024]{2,1,0:T(8,128)(2,1)S(1)}, f32[8,128]{1,0:T(8,128)S(1)}) custom-call(s32[2]{0:T(128)S(1)} %pad_add_fusion.place_ref, f32[32,1280]{1,0:T(8,128)S(1)} %get-tuple-element.109.own_ref, bf16[32,1280]{1,0:T(8,128)(2,1)S(1)} %get-tuple-element.108.refs_0_, bf16[32,1280]{1,0:T(8,128)(2,1)S(1)} %collective-permute-done.29.refs_1_, ...), custom_call_target="tpu_custom_call" | custom-call | flops 1073741824 | bytes 4194304 | tf_op jit(solution)/shard_map/dz/embedding_gradient/pallas_call | solution.py:251
  88.8 1.0 d_act_matmul.3
  89.9 1.5 %collective-permute-done.38.refs_0_ = bf16[1,272,512]{2,1,0:T(8,128)(2,1)S(1)} collective-permute-done((bf16[1,272,512]{2,1,0:T(8,128)(2,1)S(1)}, bf16[1,272,512]{2,1,0:T(8,128)(2,1)S(1)}, u32[]{:S(2)}, u32[]{:S(2)}) %collective-permute-start.38) | collective-permute-done | bytes 278560 | tf_op jit(solution)/shard_map/d_act/ppermute | solution.py:24
  91.5 1.8 %d_act_matmul.4 = (bf16[272,512]{1,0:T(8,128)(2,1)S(1)}, bf16[3,272,512]{2,1,0:T(8,128)(2,1)S(1)}) custom-call(s32[2]{0:T(128)S(1)} %pad_add_fusion.place_ref, bf16[2,512,1024]{2,1,0:T(8,128)(2,1)S(1)} %get-tuple-element.87.dz_ref.refs_9_, f32[8,128]{1,0:T(8,128)S(1)} %get-tuple-element.88.share_ref, ...), custom_call_target="tpu_custom_call" | custom-call | flops 1073741824 | bytes 1048576 | tf_op jit(solution)/shard_map/d_act/d_act_matmul/pallas_call | solution.py:318
  94.0 1.4 %collective-permute-start.42 = (bf16[272,512]{1,0:T(8,128)(2,1)S(1)}, bf16[272,512]{1,0:T(8,128)(2,1)S(1)}, u32[]{:S(2)}, u32[]{:S(2)}) collective-permute-start(bf16[272,512]{1,0:T(8,128)(2,1)S(1)} %get-tuple-element.93), channel_id=1, source_target_pairs={{0,6},{1,7},{2,4},{3,5},{4,2},{5,3},{6,0},{7,1},{8,14},{9,15},{10,... | collective-permute-start | bytes 835592 | tf_op jit(solution)/shard_map/d_act/ppermute | solution.py:24
  95.7 1.6 %d_act_matmul.5 = (bf16[272,512]{1,0:T(8,128)(2,1)S(1)}, bf16[272,512]{1,0:T(8,128)(2,1)S(1)}, f32[272,512]{1,0:T(8,128)S(1)}) custom-call(s32[2]{0:T(128)S(1)} %pad_add_fusion.place_ref, bf16[2,512,1024]{2,1,0:T(8,128)(2,1)S(1)} %get-tuple-element.87.dz_ref.refs_9_, f32[8,128]{1,0:T(8,128)S(1)} %get-tuple-element.88.share_ref, ...), custom_call_target="tpu_custom_call" | custom-call | flops 805306368 | bytes 786432 | tf_op jit(solution)/shard_map/d_act/d_act_matmul/pallas_call | solution.py:318
  97.3 1.6 %collective-permute-start.40 = (bf16[272,512]{1,0:T(8,128)(2,1)S(1)}, bf16[272,512]{1,0:T(8,128)(2,1)S(1)}, u32[]{:S(2)}, u32[]{:S(2)}) collective-permute-start(bf16[272,512]{1,0:T(8,128)(2,1)S(1)} %get-tuple-element.91), channel_id=1, source_target_pairs={{0,2},{1,3},{2,0},{3,1},{4,6},{5,7},{6,4},{7,5},{8,10},{9,11},{10,... | collective-permute-start | bytes 835592 | tf_op jit(solution)/shard_map/d_act/ppermute | solution.py:24
  99.4 2.9 %weight_gradient.2.refs_10_ = f32[1024,1024]{1,0:T(8,128)} custom-call(s32[2]{0:T(128)S(1)} %pad_add_fusion.place_ref, bf16[256,512]{1,0:T(8,128)(2,1)S(1)} %bitcast.34, bf16[256,512]{1,0:T(8,128)(2,1)S(1)} %collective-permute-done.3.refs_0_.refs_1_, bf16[256,512]{1,0:T(8,128)(2,1)S(1)} %collective-permute-done.5.refs_1_.refs_2_, ...), custom_call_target="tpu_custom_call" | custom-call | flops 1073741824 | bytes 2097152 | tf_op jit(solution)/shard_map/grad_weight/weight_gradient/pallas_call | solution.py:423
  102.3 2.9 %weight_gradient.3 = f32[1024,1024]{1,0:T(8,128)} custom-call(s32[2]{0:T(128)S(1)} %pad_add_fusion.place_ref, bf16[256,512]{1,0:T(8,128)(2,1)S(1)} %collective-permute-done.9.refs_1_.refs_0_, bf16[256,512]{1,0:T(8,128)(2,1)S(1)} %collective-permute-done.4.refs_0_.refs_1_, ...), custom_call_target="tpu_custom_call", output_to_operand_aliasing={{}: (11, {})} | custom-call | flops 1073741824 | bytes 2097152 | tf_op jit(solution)/shard_map/grad_weight/weight_gradient/pallas_call | solution.py:423
  105.2 4.4 %collective-permute-done.40 = bf16[272,512]{1,0:T(8,128)(2,1)S(1)} collective-permute-done((bf16[272,512]{1,0:T(8,128)(2,1)S(1)}, bf16[272,512]{1,0:T(8,128)(2,1)S(1)}, u32[]{:S(2)}, u32[]{:S(2)}) %collective-permute-start.40) | collective-permute-done | bytes 278560 | tf_op jit(solution)/shard_map/d_act/ppermute | solution.py:24
  110.3 1.2 collective-permute-start.44
  111.5 2.6 %collective-permute-done.44 = f32[8,512]{1,0:T(8,128)S(1)} collective-permute-done((f32[8,512]{1,0:T(8,128)S(1)}, f32[8,512]{1,0:T(8,128)S(1)}, u32[]{:S(2)}, u32[]{:S(2)}) %collective-permute-start.44) | collective-permute-done | bytes 16416 | tf_op jit(solution)/shard_map/norm_backward/ppermute | solution.py:24
  114.1 2.2 %collective-permute-start.45 = (f32[8,512]{1,0:T(8,128)S(1)}, f32[8,512]{1,0:T(8,128)S(1)}, u32[]{:S(2)}, u32[]{:S(2)}) collective-permute-start(f32[8,512]{1,0:T(8,128)S(1)} %fusion.17.refs_0_), channel_id=1, source_target_pairs={{0,16},{8,24},{16,0},{24,8},{1,17},{9,25},{17,1},{25,9},{2,18},{10... | collective-permute-start | bytes 49160 | tf_op jit(solution)/shard_map/norm_backward/ppermute | solution.py:24
  116.3 2.5 %collective-permute-done.45.refs_1_ = f32[8,512]{1,0:T(8,128)S(1)} collective-permute-done((f32[8,512]{1,0:T(8,128)S(1)}, f32[8,512]{1,0:T(8,128)S(1)}, u32[]{:S(2)}, u32[]{:S(2)}) %collective-permute-start.45) | collective-permute-done | bytes 16416 | tf_op jit(solution)/shard_map/norm_backward/ppermute | solution.py:24
  (91 shorter events, 14.5 us)
Async XLA Ops:
  2.8 9.7 %copy-start = (f32[512]{0:T(512)S(1)}, f32[512]{0:T(512)}, u32[]{:S(2)}) copy-start(f32[512]{0:T(512)} %param.5) | copy-start | bytes 6148
  2.8 9.7 %copy-start.1 = (bf16[2,128,512]{2,1,0:T(8,128)(2,1)S(1)}, bf16[2,128,512]{2,1,0:T(8,128)(2,1)}, u32[]{:S(2)}) copy-start(bf16[2,128,512]{2,1,0:T(8,128)(2,1)} %param.4) | copy-start | bytes 786436
  2.8 9.2 %collective-permute-start.2 = (f32[4,512]{1,0:T(4,128)S(1)}, f32[4,512]{1,0:T(4,128)S(1)}, u32[]{:S(2)}, u32[]{:S(2)}) collective-permute-start(f32[4,512]{1,0:T(4,128)S(1)} %pad_maximum_fusion.2), channel_id=1, source_target_pairs={{0,24},{8,16},{16,8},{24,0},{1,25},{9,17},{17,9},{25,1},{2,26},{10... | collective-permute-start | bytes 24584 | tf_op jit(solution)/shard_map/norm_stats/ppermute | solution.py:24
  7.9 4.5 %collective-permute-start.1 = (f32[4,512]{1,0:T(4,128)S(1)}, f32[4,512]{1,0:T(4,128)S(1)}, u32[]{:S(2)}, u32[]{:S(2)}) collective-permute-start(f32[4,512]{1,0:T(4,128)S(1)} %pad_maximum_fusion.2), channel_id=1, source_target_pairs={{0,16},{8,24},{16,0},{24,8},{1,17},{9,25},{17,1},{25,9},{2,18},{10... | collective-permute-start | bytes 24584 | tf_op jit(solution)/shard_map/norm_stats/ppermute | solution.py:24
  7.9 4.5 %collective-permute-start = (f32[4,512]{1,0:T(4,128)S(1)}, f32[4,512]{1,0:T(4,128)S(1)}, u32[]{:S(2)}, u32[]{:S(2)}) collective-permute-start(f32[4,512]{1,0:T(4,128)S(1)} %pad_maximum_fusion.2), channel_id=1, source_target_pairs={{0,8},{8,0},{16,24},{24,16},{1,9},{9,1},{17,25},{25,17},{2,10},{10... | collective-permute-start | bytes 24584 | tf_op jit(solution)/shard_map/norm_stats/ppermute | solution.py:24
  12.8 3.6 %collective-permute-start.9 = (bf16[256,512]{1,0:T(8,128)(2,1)S(1)}, bf16[256,512]{1,0:T(8,128)(2,1)S(1)}, u32[]{:S(2)}, u32[]{:S(2)}) collective-permute-start(bf16[256,512]{1,0:T(8,128)(2,1)S(1)} %bitcast.28), channel_id=1, source_target_pairs={{0,1},{1,0},{2,3},{3,2},{4,5},{5,4},{6,7},{7,6},{8,9},{9,8},{10,11... | collective-permute-start | bytes 786440 | tf_op jit(solution)/shard_map/act_gather/ppermute | solution.py:24
  12.9 10.1 %collective-permute-start.7 = (bf16[256,512]{1,0:T(8,128)(2,1)S(1)}, bf16[256,512]{1,0:T(8,128)(2,1)S(1)}, u32[]{:S(2)}, u32[]{:S(2)}) collective-permute-start(bf16[256,512]{1,0:T(8,128)(2,1)S(1)} %bitcast.29), channel_id=1, source_target_pairs={{0,6},{1,7},{2,4},{3,5},{4,2},{5,3},{6,0},{7,1},{8,14},{9,15},{10,... | collective-permute-start | bytes 786440 | tf_op jit(solution)/shard_map/act_gather/ppermute | solution.py:24
  15.4 12.7 %collective-permute-start.5 = (bf16[256,512]{1,0:T(8,128)(2,1)S(1)}, bf16[256,512]{1,0:T(8,128)(2,1)S(1)}, u32[]{:S(2)}, u32[]{:S(2)}) collective-permute-start(bf16[256,512]{1,0:T(8,128)(2,1)S(1)} %bitcast.30), channel_id=1, source_target_pairs={{0,4},{1,5},{2,6},{3,7},{4,0},{5,1},{6,2},{7,3},{8,12},{9,13},{10,... | collective-permute-start | bytes 786440 | tf_op jit(solution)/shard_map/act_gather/ppermute | solution.py:24
  15.9 12.3 %collective-permute-start.3 = (bf16[256,512]{1,0:T(8,128)(2,1)S(1)}, bf16[256,512]{1,0:T(8,128)(2,1)S(1)}, u32[]{:S(2)}, u32[]{:S(2)}) collective-permute-start(bf16[256,512]{1,0:T(8,128)(2,1)S(1)} %bitcast.31), channel_id=1, source_target_pairs={{0,2},{1,3},{2,0},{3,1},{4,6},{5,7},{6,4},{7,5},{8,10},{9,11},{10,... | collective-permute-start | bytes 786440 | tf_op jit(solution)/shard_map/act_gather/ppermute | solution.py:24
  16.5 13.7 %collective-permute-start.11 = (bf16[128,512]{1,0:T(8,128)(2,1)S(1)}, bf16[128,512]{1,0:T(8,128)(2,1)S(1)}, u32[]{:S(2)}, u32[]{:S(2)}) collective-permute-start(bf16[128,512]{1,0:T(8,128)(2,1)S(1)} %slice_bitcast_fusion.1), channel_id=1, source_target_pairs={{0,16},{16,24},{24,8},{8,0},{1,17},{17,25},{25,9},{9,1},{2,18},{18... | collective-permute-start | bytes 393224 | tf_op jit(solution)/shard_map/act_gather/ppermute | solution.py:34
  18.5 11.8 %collective-permute-start.12 = (bf16[128,512]{1,0:T(8,128)(2,1)S(1)}, bf16[128,512]{1,0:T(8,128)(2,1)S(1)}, u32[]{:S(2)}, u32[]{:S(2)}) collective-permute-start(bf16[128,512]{1,0:T(8,128)(2,1)S(1)} %slice_bitcast_fusion.1), channel_id=1, source_target_pairs={{0,24},{16,8},{24,0},{8,16},{1,25},{17,9},{25,1},{9,17},{2,26},{18... | collective-permute-start | bytes 393224 | tf_op jit(solution)/shard_map/act_gather/ppermute | solution.py:34
  23.0 8.6 %collective-permute-start.10 = (bf16[128,512]{1,0:T(8,128)(2,1)S(1)}, bf16[128,512]{1,0:T(8,128)(2,1)S(1)}, u32[]{:S(2)}, u32[]{:S(2)}) collective-permute-start(bf16[128,512]{1,0:T(8,128)(2,1)S(1)} %slice_bitcast_fusion.1), channel_id=1, source_target_pairs={{0,8},{16,0},{24,16},{8,24},{1,9},{17,1},{25,17},{9,25},{2,10},{18... | collective-permute-start | bytes 393224 | tf_op jit(solution)/shard_map/act_gather/ppermute | solution.py:34
  28.1 6.5 %collective-permute-start.8 = (bf16[256,512]{1,0:T(8,128)(2,1)S(1)}, bf16[256,512]{1,0:T(8,128)(2,1)S(1)}, u32[]{:S(2)}, u32[]{:S(2)}) collective-permute-start(bf16[256,512]{1,0:T(8,128)(2,1)S(1)} %collective-permute-done.7.refs_2_.refs_3_), channel_id=1, source_target_pairs={{0,1},{1,0},{2,3},{3,2},{4,5},{5,4},{6,7},{7,6},{8,9},{9,8},{10,11... | collective-permute-start | bytes 786440 | tf_op jit(solution)/shard_map/act_gather/ppermute | solution.py:24
  28.2 6.4 %collective-permute-start.6 = (bf16[256,512]{1,0:T(8,128)(2,1)S(1)}, bf16[256,512]{1,0:T(8,128)(2,1)S(1)}, u32[]{:S(2)}, u32[]{:S(2)}) collective-permute-start(bf16[256,512]{1,0:T(8,128)(2,1)S(1)} %collective-permute-done.5.refs_1_.refs_2_), channel_id=1, source_target_pairs={{0,1},{1,0},{2,3},{3,2},{4,5},{5,4},{6,7},{7,6},{8,9},{9,8},{10,11... | collective-permute-start | bytes 786440 | tf_op jit(solution)/shard_map/act_gather/ppermute | solution.py:24
  30.2 4.5 %collective-permute-start.4 = (bf16[256,512]{1,0:T(8,128)(2,1)S(1)}, bf16[256,512]{1,0:T(8,128)(2,1)S(1)}, u32[]{:S(2)}, u32[]{:S(2)}) collective-permute-start(bf16[256,512]{1,0:T(8,128)(2,1)S(1)} %collective-permute-done.3.refs_0_.refs_1_), channel_id=1, source_target_pairs={{0,1},{1,0},{2,3},{3,2},{4,5},{5,4},{6,7},{7,6},{8,9},{9,8},{10,11... | collective-permute-start | bytes 786440 | tf_op jit(solution)/shard_map/act_gather/ppermute | solution.py:24
  31.6 11.1 %collective-permute-start.17 = (bf16[384,512]{1,0:T(8,128)(2,1)S(1)}, bf16[384,512]{1,0:T(8,128)(2,1)S(1)}, u32[]{:S(2)}, u32[]{:S(2)}) collective-permute-start(bf16[384,512]{1,0:T(8,128)(2,1)S(1)} %constant_dynamic-update-slice_fusion.refs_0_.refs_4_), channel_id=1, source_target_pairs={{0,4},{1,5},{2,6},{3,7},{4,0},{5,1},{6,2},{7,3},{8,12},{9,13},{10,... | collective-permute-start | bytes 1179656 | tf_op jit(solution)/shard_map/z/ppermute | solution.py:24
  33.2 11.1 %collective-permute-start.15 = (bf16[384,512]{1,0:T(8,128)(2,1)S(1)}, bf16[384,512]{1,0:T(8,128)(2,1)S(1)}, u32[]{:S(2)}, u32[]{:S(2)}) collective-permute-start(bf16[384,512]{1,0:T(8,128)(2,1)S(1)} %constant_dynamic-update-slice_fusion.refs_0_.refs_4_), channel_id=1, source_target_pairs={{0,2},{1,3},{2,0},{3,1},{4,6},{5,7},{6,4},{7,5},{8,10},{9,11},{10,... | collective-permute-start | bytes 1179656 | tf_op jit(solution)/shard_map/z/ppermute | solution.py:24
  36.2 9.7 %collective-permute-start.14 = (bf16[128,1024]{1,0:T(8,128)(2,1)S(1)}, bf16[128,1024]{1,0:T(8,128)(2,1)S(1)}, u32[]{:S(2)}, u32[]{:S(2)}) collective-permute-start(bf16[128,1024]{1,0:T(8,128)(2,1)S(1)} %get-tuple-element.66.refs_1_.refs_9_), channel_id=1, source_target_pairs={{0,16},{16,24},{24,8},{8,0},{1,17},{17,25},{25,9},{9,1},{2,18},{18... | collective-permute-start | bytes 786440 | tf_op jit(solution)/shard_map/z_ring/ppermute | solution.py:34
  42.7 6.9 %collective-permute-start.19 = (bf16[192,512]{1,0:T(8,128)(2,1)S(1)}, bf16[192,512]{1,0:T(8,128)(2,1)S(1)}, u32[]{:S(2)}, u32[]{:S(2)}) collective-permute-start(bf16[192,512]{1,0:T(8,128)(2,1)S(1)} %slice.149), channel_id=1, source_target_pairs={{0,2},{1,3},{2,0},{3,1},{4,6},{5,7},{6,4},{7,5},{8,10},{9,11},{10,... | collective-permute-start | bytes 589832 | tf_op jit(solution)/shard_map/z/ppermute | solution.py:24
  44.3 5.8 %collective-permute-start.20 = (bf16[192,512]{1,0:T(8,128)(2,1)S(1)}, bf16[192,512]{1,0:T(8,128)(2,1)S(1)}, u32[]{:S(2)}, u32[]{:S(2)}) collective-permute-start(bf16[192,512]{1,0:T(8,128)(2,1)S(1)} %slice.150), channel_id=1, source_target_pairs={{0,4},{1,5},{2,6},{3,7},{4,0},{5,1},{6,2},{7,3},{8,12},{9,13},{10,... | collective-permute-start | bytes 589832 | tf_op jit(solution)/shard_map/z/ppermute | solution.py:24
  45.9 6.8 %collective-permute-start.21 = (bf16[128,1024]{1,0:T(8,128)(2,1)S(1)}, bf16[128,1024]{1,0:T(8,128)(2,1)S(1)}, u32[]{:S(2)}, u32[]{:S(2)}) collective-permute-start(bf16[128,1024]{1,0:T(8,128)(2,1)S(1)} %collective-permute-done.14.refs_3_.refs_11_), channel_id=1, source_target_pairs={{0,16},{16,24},{24,8},{8,0},{1,17},{17,25},{25,9},{9,1},{2,18},{18... | collective-permute-start | bytes 786440 | tf_op jit(solution)/shard_map/z_ring/ppermute | solution.py:34
  47.1 7.6 %collective-permute-start.13 = (bf16[384,512]{1,0:T(8,128)(2,1)S(1)}, bf16[384,512]{1,0:T(8,128)(2,1)S(1)}, u32[]{:S(2)}, u32[]{:S(2)}) collective-permute-start(bf16[384,512]{1,0:T(8,128)(2,1)S(1)} %constant_dynamic-update-slice_fusion.refs_0_.refs_4_), channel_id=1, source_target_pairs={{0,1},{1,0},{2,3},{3,2},{4,5},{5,4},{6,7},{7,6},{8,9},{9,8},{10,11... | collective-permute-start | bytes 1179656 | tf_op jit(solution)/shard_map/z_far/ppermute | solution.py:24
  47.1 8.3 %collective-permute-start.16 = (bf16[384,512]{1,0:T(8,128)(2,1)S(1)}, bf16[384,512]{1,0:T(8,128)(2,1)S(1)}, u32[]{:S(2)}, u32[]{:S(2)}) collective-permute-start(bf16[384,512]{1,0:T(8,128)(2,1)S(1)} %collective-permute-done.15.refs_1_.refs_5_), channel_id=1, source_target_pairs={{0,1},{1,0},{2,3},{3,2},{4,5},{5,4},{6,7},{7,6},{8,9},{9,8},{10,11... | collective-permute-start | bytes 1179656 | tf_op jit(solution)/shard_map/z_far/ppermute | solution.py:24
  49.6 5.9 %collective-permute-start.18 = (bf16[384,512]{1,0:T(8,128)(2,1)S(1)}, bf16[384,512]{1,0:T(8,128)(2,1)S(1)}, u32[]{:S(2)}, u32[]{:S(2)}) collective-permute-start(bf16[384,512]{1,0:T(8,128)(2,1)S(1)} %collective-permute-done.17.refs_2_.refs_6_), channel_id=1, source_target_pairs={{0,1},{1,0},{2,3},{3,2},{4,5},{5,4},{6,7},{7,6},{8,9},{9,8},{10,11... | collective-permute-start | bytes 1179656 | tf_op jit(solution)/shard_map/z_far/ppermute | solution.py:24
  52.7 2.8 %collective-permute-start.22 = (bf16[384,512]{1,0:T(8,128)(2,1)S(1)}, bf16[384,512]{1,0:T(8,128)(2,1)S(1)}, u32[]{:S(2)}, u32[]{:S(2)}) collective-permute-start(bf16[384,512]{1,0:T(8,128)(2,1)S(1)} %pad_maximum_fusion.refs_3_.refs_7_), channel_id=1, source_target_pairs={{0,1},{1,0},{2,3},{3,2},{4,5},{5,4},{6,7},{7,6},{8,9},{9,8},{10,11... | collective-permute-start | bytes 1179656 | tf_op jit(solution)/shard_map/z_far/ppermute | solution.py:24
  52.7 9.1 %collective-permute-start.23 = (bf16[128,1024]{1,0:T(8,128)(2,1)S(1)}, bf16[128,1024]{1,0:T(8,128)(2,1)S(1)}, u32[]{:S(2)}, u32[]{:S(2)}) collective-permute-start(bf16[128,1024]{1,0:T(8,128)(2,1)S(1)} %collective-permute-done.21.refs_5_.refs_13_), channel_id=1, source_target_pairs={{0,16},{16,24},{24,8},{8,0},{1,17},{17,25},{25,9},{9,1},{2,18},{18... | collective-permute-start | bytes 786440 | tf_op jit(solution)/shard_map/z_far/ppermute | solution.py:34
  54.7 9.8 %collective-permute-start.24 = (bf16[128,512]{1,0:T(8,128)(2,1)S(1)}, bf16[128,512]{1,0:T(8,128)(2,1)S(1)}, u32[]{:S(2)}, u32[]{:S(2)}) collective-permute-start(bf16[128,512]{1,0:T(8,128)(2,1)S(1)} %get-tuple-element.81), channel_id=1, source_target_pairs={{0,16},{16,24},{24,8},{8,0},{1,17},{17,25},{25,9},{9,1},{2,18},{18... | collective-permute-start | bytes 393224 | tf_op jit(solution)/shard_map/kernel/ppermute | solution.py:34
  64.5 1.7 %collective-permute-start.25 = (bf16[4,32,1280]{2,1,0:T(8,128)(2,1)S(1)}, bf16[4,32,1280]{2,1,0:T(8,128)(2,1)S(1)}, u32[]{:S(2)}, u32[]{:S(2)}) collective-permute-start(bf16[4,32,1280]{2,1,0:T(8,128)(2,1)S(1)} %get-tuple-element.82), channel_id=1, source_target_pairs={{0,1},{1,0},{2,3},{3,2},{4,5},{5,4},{6,7},{7,6},{8,9},{9,8},{10,11... | collective-permute-start | bytes 983048 | tf_op jit(solution)/shard_map/kernel/ppermute | solution.py:24
  66.3 5.7 %collective-permute-start.26 = (bf16[32,1280]{1,0:T(8,128)(2,1)S(1)}, bf16[32,1280]{1,0:T(8,128)(2,1)S(1)}, u32[]{:S(2)}, u32[]{:S(2)}) collective-permute-start(bf16[32,1280]{1,0:T(8,128)(2,1)S(1)} %get-tuple-element.114), channel_id=1, source_target_pairs={{0,2},{1,3},{2,0},{3,1},{4,6},{5,7},{6,4},{7,5},{8,10},{9,11},{10,... | collective-permute-start | bytes 245768 | tf_op jit(solution)/shard_map/kernel/ppermute | solution.py:24
  67.0 5.7 %collective-permute-start.28 = (bf16[32,1280]{1,0:T(8,128)(2,1)S(1)}, bf16[32,1280]{1,0:T(8,128)(2,1)S(1)}, u32[]{:S(2)}, u32[]{:S(2)}) collective-permute-start(bf16[32,1280]{1,0:T(8,128)(2,1)S(1)} %get-tuple-element.115), channel_id=1, source_target_pairs={{0,6},{1,7},{2,4},{3,5},{4,2},{5,3},{6,0},{7,1},{8,14},{9,15},{10,... | collective-permute-start | bytes 245768 | tf_op jit(solution)/shard_map/kernel/ppermute | solution.py:24
  68.4 5.5 %collective-permute-start.27 = (bf16[32,1280]{1,0:T(8,128)(2,1)S(1)}, bf16[32,1280]{1,0:T(8,128)(2,1)S(1)}, u32[]{:S(2)}, u32[]{:S(2)}) collective-permute-start(bf16[32,1280]{1,0:T(8,128)(2,1)S(1)} %get-tuple-element.116), channel_id=1, source_target_pairs={{0,4},{1,5},{2,6},{3,7},{4,0},{5,1},{6,2},{7,3},{8,12},{9,13},{10,... | collective-permute-start | bytes 245768 | tf_op jit(solution)/shard_map/kernel/ppermute | solution.py:24
  69.8 7.8 %collective-permute-start.31 = (bf16[128,512]{1,0:T(8,128)(2,1)S(1)}, bf16[128,512]{1,0:T(8,128)(2,1)S(1)}, u32[]{:S(2)}, u32[]{:S(2)}) collective-permute-start(bf16[128,512]{1,0:T(8,128)(2,1)S(1)} %get-tuple-element.83), channel_id=1, source_target_pairs={{0,24},{16,8},{24,0},{8,16},{1,25},{17,9},{25,1},{9,17},{2,26},{18... | collective-permute-start | bytes 393224 | tf_op jit(solution)/shard_map/kernel/ppermute | solution.py:34
  74.0 5.1 %collective-permute-start.30 = (bf16[32,1280]{1,0:T(8,128)(2,1)S(1)}, bf16[32,1280]{1,0:T(8,128)(2,1)S(1)}, u32[]{:S(2)}, u32[]{:S(2)}) collective-permute-start(bf16[32,1280]{1,0:T(8,128)(2,1)S(1)} %get-tuple-element.108.refs_0_), channel_id=1, source_target_pairs={{0,2},{1,3},{2,0},{3,1},{4,6},{5,7},{6,4},{7,5},{8,10},{9,11},{10,... | collective-permute-start | bytes 245768 | tf_op jit(solution)/shard_map/kernel/ppermute | solution.py:24
  75.2 5.6 %collective-permute-start.35 = (bf16[32,1280]{1,0:T(8,128)(2,1)S(1)}, bf16[32,1280]{1,0:T(8,128)(2,1)S(1)}, u32[]{:S(2)}, u32[]{:S(2)}) collective-permute-start(bf16[32,1280]{1,0:T(8,128)(2,1)S(1)} %get-tuple-element.108.refs_0_), channel_id=1, source_target_pairs={{0,6},{1,7},{2,4},{3,5},{4,2},{5,3},{6,0},{7,1},{8,14},{9,15},{10,... | collective-permute-start | bytes 245768 | tf_op jit(solution)/shard_map/kernel/ppermute | solution.py:24
  76.8 4.8 %collective-permute-start.33 = (bf16[32,1280]{1,0:T(8,128)(2,1)S(1)}, bf16[32,1280]{1,0:T(8,128)(2,1)S(1)}, u32[]{:S(2)}, u32[]{:S(2)}) collective-permute-start(bf16[32,1280]{1,0:T(8,128)(2,1)S(1)} %get-tuple-element.108.refs_0_), channel_id=1, source_target_pairs={{0,4},{1,5},{2,6},{3,7},{4,0},{5,1},{6,2},{7,3},{8,12},{9,13},{10,... | collective-permute-start | bytes 245768 | tf_op jit(solution)/shard_map/kernel/ppermute | solution.py:24
  77.6 6.5 %collective-permute-start.29 = (bf16[32,1280]{1,0:T(8,128)(2,1)S(1)}, bf16[32,1280]{1,0:T(8,128)(2,1)S(1)}, u32[]{:S(2)}, u32[]{:S(2)}) collective-permute-start(bf16[32,1280]{1,0:T(8,128)(2,1)S(1)} %get-tuple-element.108.refs_0_), channel_id=1, source_target_pairs={{0,1},{1,0},{2,3},{3,2},{4,5},{5,4},{6,7},{7,6},{8,9},{9,8},{10,11... | collective-permute-start | bytes 245768 | tf_op jit(solution)/shard_map/kernel/ppermute | solution.py:24
  80.8 3.3 %collective-permute-start.36 = (bf16[32,1280]{1,0:T(8,128)(2,1)S(1)}, bf16[32,1280]{1,0:T(8,128)(2,1)S(1)}, u32[]{:S(2)}, u32[]{:S(2)}) collective-permute-start(bf16[32,1280]{1,0:T(8,128)(2,1)S(1)} %collective-permute-done.35.refs_6_), channel_id=1, source_target_pairs={{0,1},{1,0},{2,3},{3,2},{4,5},{5,4},{6,7},{7,6},{8,9},{9,8},{10,11... | collective-permute-start | bytes 245768 | tf_op jit(solution)/shard_map/kernel/ppermute | solution.py:24
  81.6 2.5 %collective-permute-start.34 = (bf16[32,1280]{1,0:T(8,128)(2,1)S(1)}, bf16[32,1280]{1,0:T(8,128)(2,1)S(1)}, u32[]{:S(2)}, u32[]{:S(2)}) collective-permute-start(bf16[32,1280]{1,0:T(8,128)(2,1)S(1)} %collective-permute-done.33.refs_4_), channel_id=1, source_target_pairs={{0,1},{1,0},{2,3},{3,2},{4,5},{5,4},{6,7},{7,6},{8,9},{9,8},{10,11... | collective-permute-start | bytes 245768 | tf_op jit(solution)/shard_map/kernel/ppermute | solution.py:24
  81.6 2.5 %collective-permute-start.32 = (bf16[32,1280]{1,0:T(8,128)(2,1)S(1)}, bf16[32,1280]{1,0:T(8,128)(2,1)S(1)}, u32[]{:S(2)}, u32[]{:S(2)}) collective-permute-start(bf16[32,1280]{1,0:T(8,128)(2,1)S(1)} %collective-permute-done.30.refs_2_), channel_id=1, source_target_pairs={{0,1},{1,0},{2,3},{3,2},{4,5},{5,4},{6,7},{7,6},{8,9},{9,8},{10,11... | collective-permute-start | bytes 245768 | tf_op jit(solution)/shard_map/kernel/ppermute | solution.py:24
  82.1 6.7 %collective-permute-start.37 = (bf16[128,512]{1,0:T(8,128)(2,1)S(1)}, bf16[128,512]{1,0:T(8,128)(2,1)S(1)}, u32[]{:S(2)}, u32[]{:S(2)}) collective-permute-start(bf16[128,512]{1,0:T(8,128)(2,1)S(1)} %get-tuple-element.86), channel_id=1, source_target_pairs={{0,8},{16,0},{24,16},{8,24},{1,9},{17,1},{25,17},{9,25},{2,10},{18... | collective-permute-start | bytes 393224 | tf_op jit(solution)/shard_map/kernel/ppermute | solution.py:34
  89.8 1.6 %collective-permute-start.38 = (bf16[1,272,512]{2,1,0:T(8,128)(2,1)S(1)}, bf16[1,272,512]{2,1,0:T(8,128)(2,1)S(1)}, u32[]{:S(2)}, u32[]{:S(2)}) collective-permute-start(bf16[1,272,512]{2,1,0:T(8,128)(2,1)S(1)} %d_act_matmul.3), channel_id=1, source_target_pairs={{0,1},{1,0},{2,3},{3,2},{4,5},{5,4},{6,7},{7,6},{8,9},{9,8},{10,11... | collective-permute-start | bytes 835592 | tf_op jit(solution)/shard_map/d_act/ppermute | solution.py:24
  93.3 2.4 %collective-permute-start.39 = (bf16[3,272,512]{2,1,0:T(8,128)(2,1)S(1)}, bf16[3,272,512]{2,1,0:T(8,128)(2,1)S(1)}, u32[]{:S(2)}, u32[]{:S(2)}) collective-permute-start(bf16[3,272,512]{2,1,0:T(8,128)(2,1)S(1)} %get-tuple-element.89), channel_id=1, source_target_pairs={{0,1},{1,0},{2,3},{3,2},{4,5},{5,4},{6,7},{7,6},{8,9},{9,8},{10,11... | collective-permute-start | bytes 2506760 | tf_op jit(solution)/shard_map/d_act/ppermute | solution.py:24
  93.6 8.7 %collective-permute-start.43 = (bf16[384,512]{1,0:T(8,128)(2,1)S(1)}, bf16[384,512]{1,0:T(8,128)(2,1)S(1)}, u32[]{:S(2)}, u32[]{:S(2)}) collective-permute-start(bf16[384,512]{1,0:T(8,128)(2,1)S(1)} %constant_dynamic-update-slice_fusion.3.refs_8_), channel_id=1, source_target_pairs={{0,1},{1,0},{2,3},{3,2},{4,5},{5,4},{6,7},{7,6},{8,9},{9,8},{10,11... | collective-permute-start | bytes 1179656 | tf_op jit(solution)/shard_map/grad_weight/ppermute | solution.py:24
  94.0 11.2 %collective-permute-start.42 = (bf16[272,512]{1,0:T(8,128)(2,1)S(1)}, bf16[272,512]{1,0:T(8,128)(2,1)S(1)}, u32[]{:S(2)}, u32[]{:S(2)}) collective-permute-start(bf16[272,512]{1,0:T(8,128)(2,1)S(1)} %get-tuple-element.93), channel_id=1, source_target_pairs={{0,6},{1,7},{2,4},{3,5},{4,2},{5,3},{6,0},{7,1},{8,14},{9,15},{10,... | collective-permute-start | bytes 835592 | tf_op jit(solution)/shard_map/d_act/ppermute | solution.py:24
  97.3 12.3 %collective-permute-start.40 = (bf16[272,512]{1,0:T(8,128)(2,1)S(1)}, bf16[272,512]{1,0:T(8,128)(2,1)S(1)}, u32[]{:S(2)}, u32[]{:S(2)}) collective-permute-start(bf16[272,512]{1,0:T(8,128)(2,1)S(1)} %get-tuple-element.91), channel_id=1, source_target_pairs={{0,2},{1,3},{2,0},{3,1},{4,6},{5,7},{6,4},{7,5},{8,10},{9,11},{10,... | collective-permute-start | bytes 835592 | tf_op jit(solution)/shard_map/d_act/ppermute | solution.py:24
  98.9 10.8 %collective-permute-start.41 = (bf16[272,512]{1,0:T(8,128)(2,1)S(1)}, bf16[272,512]{1,0:T(8,128)(2,1)S(1)}, u32[]{:S(2)}, u32[]{:S(2)}) collective-permute-start(bf16[272,512]{1,0:T(8,128)(2,1)S(1)} %get-tuple-element.92), channel_id=1, source_target_pairs={{0,4},{1,5},{2,6},{3,7},{4,0},{5,1},{6,2},{7,3},{8,12},{9,13},{10,... | collective-permute-start | bytes 835592 | tf_op jit(solution)/shard_map/d_act/ppermute | solution.py:24
  110.3 3.8 %collective-permute-start.44 = (f32[8,512]{1,0:T(8,128)S(1)}, f32[8,512]{1,0:T(8,128)S(1)}, u32[]{:S(2)}, u32[]{:S(2)}) collective-permute-start(f32[8,512]{1,0:T(8,128)S(1)} %pad_maximum_fusion.1), channel_id=1, source_target_pairs={{0,8},{8,0},{16,24},{24,16},{1,9},{9,1},{17,25},{25,17},{2,10},{10... | collective-permute-start | bytes 49160 | tf_op jit(solution)/shard_map/norm_backward/ppermute | solution.py:24
  114.1 4.7 %collective-permute-start.45 = (f32[8,512]{1,0:T(8,128)S(1)}, f32[8,512]{1,0:T(8,128)S(1)}, u32[]{:S(2)}, u32[]{:S(2)}) collective-permute-start(f32[8,512]{1,0:T(8,128)S(1)} %fusion.17.refs_0_), channel_id=1, source_target_pairs={{0,16},{8,24},{16,0},{24,8},{1,17},{9,25},{17,1},{25,9},{2,18},{10... | collective-permute-start | bytes 49160 | tf_op jit(solution)/shard_map/norm_backward/ppermute | solution.py:24
  (1 other events, 9.7 us)

commit v18 on v17

--- a/solution.py
+++ b/solution.py
@@ -88,6 +88,29 @@
         cost_estimate=cost(0, 4 * weight.size),
         name="weight_load",
     )(pltpu.with_memory_space_constraint(weight, pltpu.HBM))
+
+
+def stats_kernel(views_ref, out_ref):
+    n_view, local_rows, _ = views_ref.shape
+    for v in range(n_view):
+        x = views_ref[v].astype(f32)
+        mean = jnp.sum(x, axis=0, keepdims=True) / local_rows
+        centred = x - mean
+        out_ref[v : v + 1] = mean
+        out_ref[n_view + v : n_view + v + 1] = jnp.sum(centred * centred, axis=0, keepdims=True)
+
+
+def stats_call(views):
+    n_view, _, width = views.shape
+    return pl.pallas_call(
+        stats_kernel,
+        out_shape=jax.ShapeDtypeStruct((2 * n_view, width), f32),
+        in_specs=[IN_VMEM],
+        out_specs=IN_VMEM,
+        compiler_params=params(4),
+        cost_estimate=cost(0, 2 * views.size),
+        name="norm_statistics",
+    )(views)
 
 
 def weight_rows(place_ref, w_ref, k, width):
@@ -209,8 +232,8 @@
             if s < t:
                 full[v, there, here] = jnp.transpose(block).astype(bf16)
 
-    def one_tile(j, carry):
-        here = pl.ds(pl.multiple_of(j * tile, tile), tile)
+    for j in range(columns // tile):
+        here = pl.ds(j * tile, tile)
         share = jnp.zeros((1, 1), f32)
         grads = []
         z_views = []
@@ -220,10 +243,10 @@
             zc = zf - jnp.sum(zf, axis=0, keepdims=True) / rows
             std = jnp.sqrt(jnp.sum(zc * zc, axis=0, keepdims=True) / (rows - 1) + eps_std)
             zcb = zc.astype(bf16)
-            centred[...] = zcb
+            centred[2 * j + v] = zcb
             rounded = zcb.astype(f32)
             diag = jnp.sum(rounded * rounded, axis=0, keepdims=True)
-            moved = jnp.dot(full[v], centred[...], preferred_element_type=f32)
+            moved = jnp.dot(full[v], centred[2 * j + v], preferred_element_type=f32)
             pull = jnp.where(std < 1.0, hinge_coef, 0.0) / std
             summed = coef * (moved - rounded * diag) - zc * pull
             grads.append(summed - jnp.sum(summed, axis=0, keepdims=True) / rows)
@@ -236,9 +259,6 @@
         share_ref[...] += jnp.broadcast_to(share, share_ref.shape)
         dz_ref[0, :, here] = (grads[0] + inv_coef * diff).astype(bf16)
         dz_ref[1, :, here] = (grads[1] - inv_coef * diff).astype(bf16)
-        return carry
-
-    lax.fori_loop(0, columns // tile, one_tile, 0)
 
 
 def dz_call(place, own, strips, z_slots, constants):
@@ -259,9 +279,9 @@
         scratch_shapes=[
             pltpu.VMEM((tall, strips[0].shape[1]), f32),
             pltpu.VMEM((2, rows, rows), bf16),
-            pltpu.VMEM((rows, tile), bf16),
+            pltpu.VMEM((2 * columns // tile, rows, tile), bf16),
         ],
-        compiler_params=params(24),
+        compiler_params=params(28),
         cost_estimate=cost(4 * rows * rows * columns, 8 * rows * columns),
         name="embedding_gradient",
     )(*operands)
@@ -520,10 +540,7 @@
         held_weight, loaded = load_call(weight, (2 * n_view, width))
     with jax.named_scope("norm_stats"):
         hidden = views.astype(f32)
-        local_mean = jnp.mean(hidden, axis=1)
-        local_centred = hidden - local_mean[:, None, :]
-        local_spread = jnp.sum(local_centred * local_centred, axis=1)
-        stats = exchange(jnp.concatenate([local_mean, local_spread]), "batch")
+        stats = exchange(stats_call(views), "batch")
         stats[-1] = stats[-1] + loaded
         mean = exchange_sum(s[:n_view] for s in stats) / n_batch
         spread = exchange_sum(
@@ -644,13 +661,8 @@
                 jnp.broadcast_to(share, (2 * n_view, width)),
             ]
         )
-        k = 1
-        while 2 * k < n_batch:
-            sums = sums + xor_send(sums, "batch", k)
-            k *= 2
-        sums = [sums, xor_send(sums, "batch", k)]
         loss, grad_gain, grad_bias, views_gradient = finish_call(
-            sums, d_pre, normalised, norm_scale_gain, inverse_deviation, rows
+            exchange(sums, "batch"), d_pre, normalised, norm_scale_gain, inverse_deviation, rows
         )
     return (loss[0, 0], grad_weight, grad_gain[0], grad_bias[0], views_gradient)
 

time: 120 us -> 118 us (0.983)
  waiting for transfers between devices: 39.5 us -> 37.1 us
  other arithmetic: 3.23 us -> 1.16 us
    ppermute x37 -> x38, waiting for transfers between devices: 32.1 us -> 29.7 us  [xor_send(): return lax.ppermute(x, axis, [(i, i ^ k) for i in range(n)])]
    reduce_sum x2 -> x0, other arithmetic: 2.04 us -> none  [the longest x1 1.04 us: shards(): local_spread = jnp.sum(local_centred * local_centred, axis=1)]
    ppermute x37 -> x38, starting transfers between devices: 32.2 us -> 33.3 us  [xor_send(): return lax.ppermute(x, axis, [(i, i ^ k) for i in range(n)])]
  transfers between devices with their start and end apart: 46 -> 47, of which waited for: 20 -> 20; matrix products, arithmetic and copies ran while one was open for 0% -> 0% of each run, Pallas kernels for 23% -> 24%
where the time goes in v18:
time: 118 us; the launch traced here: 117 us
  starting transfers between devices  45.4 us (38%)
  waiting for transfers between devices  37.1 us (31%)
  Pallas kernels  31.7 us (27%)
    ppermute x38, starting transfers between devices, xor_send(): return lax.ppermute(x, axis, [(i, i ^ k) for i in range(n)])  33.3 us
    ppermute x38, waiting for transfers between devices, xor_send(): return lax.ppermute(x, axis, [(i, i ^ k) for i in range(n)])  29.7 us
    ppermute x9, starting transfers between devices, ring_send(): lax.ppermute(x, axis, [(order[i], order[(i + d) % n]) for i in range(n)])  12 us
    pallas_call x5, Pallas kernels, z_call(): pl.pallas_call(functools.partial(z_kernel, tuple(ks), before is None, las...  8.96 us
    ppermute x9, waiting for transfers between devices, ring_send(): lax.ppermute(x, axis, [(order[i], order[(i + d) % n]) for i in range(n)])  7.4 us
    pallas_call x2, Pallas kernels, weight_grad_call(): pl.pallas_call(functools.partial(weight_grad_kernel, rows // (near[0][0]....  5.8 us
    pallas_call x1, Pallas kernels, dz_call(): pl.pallas_call(functools.partial(dz_kernel, n_batch, n_col, tile, constan...  4.75 us
    pallas_call x3, Pallas kernels, d_act_call(): pl.pallas_call(functools.partial(d_act_kernel, tuple(evens), tuple(odds),...  4.43 us
  transfers between devices with their start and end apart: 47, of which 20 were waited for; matrix products, arithmetic and copies ran while one was open for 0% of the time, Pallas kernels for 24%

profile of v18, /device:TPU:0, one launch (start us, length us, event | category | flops | bytes accessed | tf_op | source)
XLA Modules:
  0.0 117.4 jit_solution(15250481875290573313)
XLA Ops:
  0.7 0.9 copy-done
  1.8 5.1 %collective-permute-start.2 = (f32[4,512]{1,0:T(4,128)S(1)}, f32[4,512]{1,0:T(4,128)S(1)}, u32[]{:S(2)}, u32[]{:S(2)}) collective-permute-start(f32[4,512]{1,0:T(4,128)S(1)} %norm_statistics.1), channel_id=1, source_target_pairs={{0,24},{8,16},{16,8},{24,0},{1,25},{9,17},{17,9},{25,1},{2,26},{10... | collective-permute-start | bytes 24584 | tf_op jit(solution)/shard_map/norm_stats/ppermute | solution.py:24
  7.6 3.5 %weight_load.1 = (bf16[4096,1024]{1,0:T(8,128)(2,1)S(1)}, f32[4,512]{1,0:T(4,128)S(1)}) custom-call(bf16[4096,1024]{1,0:T(8,128)(2,1)} %w_ref), custom_call_target="tpu_custom_call" | custom-call | bytes 16777216 | tf_op jit(solution)/shard_map/weight_load/weight_load/pallas_call | solution.py:78
  11.9 2.5 %collective-permute-start.7 = (bf16[256,512]{1,0:T(8,128)(2,1)S(1)}, bf16[256,512]{1,0:T(8,128)(2,1)S(1)}, u32[]{:S(2)}, u32[]{:S(2)}) collective-permute-start(bf16[256,512]{1,0:T(8,128)(2,1)S(1)} %bitcast.29), channel_id=1, source_target_pairs={{0,6},{1,7},{2,4},{3,5},{4,2},{5,3},{6,0},{7,1},{8,14},{9,15},{10,... | collective-permute-start | bytes 786440 | tf_op jit(solution)/shard_map/act_gather/ppermute | solution.py:24
  15.5 2.1 %collective-permute-start.11 = (bf16[128,512]{1,0:T(8,128)(2,1)S(1)}, bf16[128,512]{1,0:T(8,128)(2,1)S(1)}, u32[]{:S(2)}, u32[]{:S(2)}) collective-permute-start(bf16[128,512]{1,0:T(8,128)(2,1)S(1)} %slice_bitcast_fusion.1), channel_id=1, source_target_pairs={{0,16},{16,24},{24,8},{8,0},{1,17},{17,25},{25,9},{9,1},{2,18},{18... | collective-permute-start | bytes 393224 | tf_op jit(solution)/shard_map/act_gather/ppermute | solution.py:34
  17.6 1.4 %collective-permute-start.12 = (bf16[128,512]{1,0:T(8,128)(2,1)S(1)}, bf16[128,512]{1,0:T(8,128)(2,1)S(1)}, u32[]{:S(2)}, u32[]{:S(2)}) collective-permute-start(bf16[128,512]{1,0:T(8,128)(2,1)S(1)} %slice_bitcast_fusion.1), channel_id=1, source_target_pairs={{0,24},{16,8},{24,0},{8,16},{1,25},{17,9},{25,1},{9,17},{2,26},{18... | collective-permute-start | bytes 393224 | tf_op jit(solution)/shard_map/act_gather/ppermute | solution.py:34
  19.0 1.2 %z_matmul.5.refs_4_ = f32[256,1024]{1,0:T(8,128)S(1)} custom-call(s32[2]{0:T(128)S(1)} %pad_add_fusion.place_ref, bf16[256,512]{1,0:T(8,128)(2,1)S(1)} %bitcast.32, bf16[256,512]{1,0:T(8,128)(2,1)S(1)} %collective-permute-done.9.refs_1_.refs_0_, bf16[4096,1024]{1,0:T(8,128)(2,1)S(1)} %get-tuple-element.61.refs_2_.refs_3_.refs_5_.w_ref), custom_call_target="tpu_custom_call" | custom-call | flops 536870912 | bytes 524288 | tf_op jit(solution)/shard_map/z/z_matmul/pallas_call | solution.py:149
  20.2 1.8 %collective-permute-done.7.refs_2_.refs_3_ = bf16[256,512]{1,0:T(8,128)(2,1)S(1)} collective-permute-done((bf16[256,512]{1,0:T(8,128)(2,1)S(1)}, bf16[256,512]{1,0:T(8,128)(2,1)S(1)}, u32[]{:S(2)}, u32[]{:S(2)}) %collective-permute-start.7) | collective-permute-done | bytes 262176 | tf_op jit(solution)/shard_map/act_gather/ppermute | solution.py:24
  22.0 1.0 collective-permute-start.10
  23.0 4.1 %collective-permute-done.5.refs_1_.refs_2_ = bf16[256,512]{1,0:T(8,128)(2,1)S(1)} collective-permute-done((bf16[256,512]{1,0:T(8,128)(2,1)S(1)}, bf16[256,512]{1,0:T(8,128)(2,1)S(1)}, u32[]{:S(2)}, u32[]{:S(2)}) %collective-permute-start.5) | collective-permute-done | bytes 262176 | tf_op jit(solution)/shard_map/act_gather/ppermute | solution.py:24
  27.7 1.5 %z_matmul.6.refs_4_ = f32[256,1024]{1,0:T(8,128)S(1)} custom-call(s32[2]{0:T(128)S(1)} %pad_add_fusion.place_ref, bf16[256,512]{1,0:T(8,128)(2,1)S(1)} %collective-permute-done.3.refs_0_.refs_1_, bf16[256,512]{1,0:T(8,128)(2,1)S(1)} %collective-permute-done.5.refs_1_.refs_2_, bf16[256,512]{1,0:T(8,128)(2,1)S(1)} %collective-permute-done.7.refs_2_.refs_3_, ...), custom_call_target="tpu_custom_call" | custom-call | flops 805306368 | bytes 524288 | tf_op jit(solution)/shard_map/z/z_matmul/pallas_call | solution.py:149
  29.4 1.2 %collective-permute-done.10 = bf16[128,512]{1,0:T(8,128)(2,1)S(1)} collective-permute-done((bf16[128,512]{1,0:T(8,128)(2,1)S(1)}, bf16[128,512]{1,0:T(8,128)(2,1)S(1)}, u32[]{:S(2)}, u32[]{:S(2)}) %collective-permute-start.10) | collective-permute-done | bytes 131104 | tf_op jit(solution)/shard_map/act_gather/ppermute | solution.py:34
  30.6 1.6 %collective-permute-start.17 = (bf16[384,512]{1,0:T(8,128)(2,1)S(1)}, bf16[384,512]{1,0:T(8,128)(2,1)S(1)}, u32[]{:S(2)}, u32[]{:S(2)}) collective-permute-start(bf16[384,512]{1,0:T(8,128)(2,1)S(1)} %constant_dynamic-update-slice_fusion.refs_0_.refs_4_), channel_id=1, source_target_pairs={{0,4},{1,5},{2,6},{3,7},{4,0},{5,1},{6,2},{7,3},{8,12},{9,13},{10,... | collective-permute-start | bytes 1179656 | tf_op jit(solution)/shard_map/z/ppermute | solution.py:24
  32.2 1.5 %collective-permute-start.15 = (bf16[384,512]{1,0:T(8,128)(2,1)S(1)}, bf16[384,512]{1,0:T(8,128)(2,1)S(1)}, u32[]{:S(2)}, u32[]{:S(2)}) collective-permute-start(bf16[384,512]{1,0:T(8,128)(2,1)S(1)} %constant_dynamic-update-slice_fusion.refs_0_.refs_4_), channel_id=1, source_target_pairs={{0,2},{1,3},{2,0},{3,1},{4,6},{5,7},{6,4},{7,5},{8,10},{9,11},{10,... | collective-permute-start | bytes 1179656 | tf_op jit(solution)/shard_map/z/ppermute | solution.py:24
  33.7 1.5 %z_matmul.7 = (bf16[128,1024]{1,0:T(8,128)(2,1)S(1)}, bf16[128,1024]{1,0:T(8,128)(2,1)S(1)}) custom-call(s32[2]{0:T(128)S(1)} %pad_add_fusion.place_ref, bf16[256,512]{1,0:T(8,128)(2,1)S(1)} %collective-permute-done.4.refs_0_.refs_1_, bf16[256,512]{1,0:T(8,128)(2,1)S(1)} %collective-permute-done.6.refs_1_.refs_2_, ...), custom_call_target="tpu_custom_call" | custom-call | flops 805306368 | bytes 524288 | tf_op jit(solution)/shard_map/z/z_matmul/pallas_call | solution.py:149
  35.4 6.4 %collective-permute-done.17.refs_2_.refs_6_ = bf16[384,512]{1,0:T(8,128)(2,1)S(1)} collective-permute-done((bf16[384,512]{1,0:T(8,128)(2,1)S(1)}, bf16[384,512]{1,0:T(8,128)(2,1)S(1)}, u32[]{:S(2)}, u32[]{:S(2)}) %collective-permute-start.17) | collective-permute-done | bytes 393248 | tf_op jit(solution)/shard_map/z/ppermute | solution.py:24
  41.7 1.6 %collective-permute-start.19 = (bf16[192,512]{1,0:T(8,128)(2,1)S(1)}, bf16[192,512]{1,0:T(8,128)(2,1)S(1)}, u32[]{:S(2)}, u32[]{:S(2)}) collective-permute-start(bf16[192,512]{1,0:T(8,128)(2,1)S(1)} %slice.160), channel_id=1, source_target_pairs={{0,2},{1,3},{2,0},{3,1},{4,6},{5,7},{6,4},{7,5},{8,10},{9,11},{10,... | collective-permute-start | bytes 589832 | tf_op jit(solution)/shard_map/z/ppermute | solution.py:24
  43.3 1.6 %collective-permute-start.20 = (bf16[192,512]{1,0:T(8,128)(2,1)S(1)}, bf16[192,512]{1,0:T(8,128)(2,1)S(1)}, u32[]{:S(2)}, u32[]{:S(2)}) collective-permute-start(bf16[192,512]{1,0:T(8,128)(2,1)S(1)} %slice.161), channel_id=1, source_target_pairs={{0,4},{1,5},{2,6},{3,7},{4,0},{5,1},{6,2},{7,3},{8,12},{9,13},{10,... | collective-permute-start | bytes 589832 | tf_op jit(solution)/shard_map/z/ppermute | solution.py:24
  46.7 1.9 %z_matmul.8.refs_6_ = f32[384,1024]{1,0:T(8,128)S(1)} custom-call(s32[2]{0:T(128)S(1)} %pad_add_fusion.place_ref, bf16[384,512]{1,0:T(8,128)(2,1)S(1)} %constant_dynamic-update-slice_fusion.refs_0_.refs_4_, bf16[384,512]{1,0:T(8,128)(2,1)S(1)} %collective-permute-done.15.refs_1_.refs_5_, bf16[384,512]{1,0:T(8,128)(2,1)S(1)} %collective-permute-done.17.refs_2_.refs_6_, ...), custom_call_target="tpu_custom_call" | custom-call | flops 1207959552 | bytes 786432 | tf_op jit(solution)/shard_map/z_far/z_matmul/pallas_call | solution.py:149
  49.1 2.6 %collective-permute-done.21.refs_5_.refs_13_ = bf16[128,1024]{1,0:T(8,128)(2,1)S(1)} collective-permute-done((bf16[128,1024]{1,0:T(8,128)(2,1)S(1)}, bf16[128,1024]{1,0:T(8,128)(2,1)S(1)}, u32[]{:S(2)}, u32[]{:S(2)}) %collective-permute-start.21) | collective-permute-done | bytes 262176 | tf_op jit(solution)/shard_map/z_ring/ppermute | solution.py:34
  51.7 2.0 %collective-permute-start.23 = (bf16[128,1024]{1,0:T(8,128)(2,1)S(1)}, bf16[128,1024]{1,0:T(8,128)(2,1)S(1)}, u32[]{:S(2)}, u32[]{:S(2)}) collective-permute-start(bf16[128,1024]{1,0:T(8,128)(2,1)S(1)} %collective-permute-done.21.refs_5_.refs_13_), channel_id=1, source_target_pairs={{0,16},{16,24},{24,8},{8,0},{1,17},{17,25},{25,9},{9,1},{2,18},{18... | collective-permute-start | bytes 786440 | tf_op jit(solution)/shard_map/z_far/ppermute | solution.py:34
  54.5 2.7 %z_matmul.9 = (bf16[128,1024]{1,0:T(8,128)(2,1)S(1)}, bf16[128,1024]{1,0:T(8,128)(2,1)S(1)}, bf16[128,1024]{1,0:T(8,128)(2,1)S(1)}) custom-call(s32[2]{0:T(128)S(1)} %pad_add_fusion.place_ref, bf16[384,512]{1,0:T(8,128)(2,1)S(1)} %collective-permute-done.13.refs_0_.refs_4_, bf16[384,512]{1,0:T(8,128)(2,1)S(1)} %collective-permute-done.16.refs_1_.refs_5_, ...), custom_call_target="tpu_custom_call" | custom-call | flops 2013265920 | bytes 786432 | tf_op jit(solution)/shard_map/z_far/z_matmul/pallas_call | solution.py:149
  57.3 3.6 %collective-permute-done.23.refs_7_.refs_15_ = bf16[128,1024]{1,0:T(8,128)(2,1)S(1)} collective-permute-done((bf16[128,1024]{1,0:T(8,128)(2,1)S(1)}, bf16[128,1024]{1,0:T(8,128)(2,1)S(1)}, u32[]{:S(2)}, u32[]{:S(2)}) %collective-permute-start.23) | collective-permute-done | bytes 262176 | tf_op jit(solution)/shard_map/z_far/ppermute | solution.py:34
  60.8 2.7 %kernel_strip.1 = (f32[4,32,1280]{2,1,0:T(8,128)S(1)}, bf16[4,32,1280]{2,1,0:T(8,128)(2,1)S(1)}) custom-call(s32[2]{0:T(128)S(1)} %pad_add_fusion.place_ref, bf16[128,1024]{1,0:T(8,128)(2,1)S(1)} %get-tuple-element.65.refs_0_.refs_8_, bf16[128,1024]{1,0:T(8,128)(2,1)S(1)} %get-tuple-element.66.refs_1_.refs_9_, ...), custom_call_target="tpu_custom_call" | custom-call | flops 671088640 | bytes 2097152 | tf_op jit(solution)/shard_map/kernel/kernel_strip/pallas_call | solution.py:196
  63.6 1.6 %collective-permute-done.25 = bf16[4,32,1280]{2,1,0:T(8,128)(2,1)S(1)} collective-permute-done((bf16[4,32,1280]{2,1,0:T(8,128)(2,1)S(1)}, bf16[4,32,1280]{2,1,0:T(8,128)(2,1)S(1)}, u32[]{:S(2)}, u32[]{:S(2)}) %collective-permute-start.25) | collective-permute-done | bytes 327712 | tf_op jit(solution)/shard_map/kernel/ppermute | solution.py:24
  66.1 1.4 %collective-permute-start.28 = (bf16[32,1280]{1,0:T(8,128)(2,1)S(1)}, bf16[32,1280]{1,0:T(8,128)(2,1)S(1)}, u32[]{:S(2)}, u32[]{:S(2)}) collective-permute-start(bf16[32,1280]{1,0:T(8,128)(2,1)S(1)} %get-tuple-element.115), channel_id=1, source_target_pairs={{0,6},{1,7},{2,4},{3,5},{4,2},{5,3},{6,0},{7,1},{8,14},{9,15},{10,... | collective-permute-start | bytes 245768 | tf_op jit(solution)/shard_map/kernel/ppermute | solution.py:24
  67.5 1.4 %collective-permute-start.27 = (bf16[32,1280]{1,0:T(8,128)(2,1)S(1)}, bf16[32,1280]{1,0:T(8,128)(2,1)S(1)}, u32[]{:S(2)}, u32[]{:S(2)}) collective-permute-start(bf16[32,1280]{1,0:T(8,128)(2,1)S(1)} %get-tuple-element.116), channel_id=1, source_target_pairs={{0,4},{1,5},{2,6},{3,7},{4,0},{5,1},{6,2},{7,3},{8,12},{9,13},{10,... | collective-permute-start | bytes 245768 | tf_op jit(solution)/shard_map/kernel/ppermute | solution.py:24
  68.9 2.2 %collective-permute-start.31 = (bf16[128,512]{1,0:T(8,128)(2,1)S(1)}, bf16[128,512]{1,0:T(8,128)(2,1)S(1)}, u32[]{:S(2)}, u32[]{:S(2)}) collective-permute-start(bf16[128,512]{1,0:T(8,128)(2,1)S(1)} %get-tuple-element.83), channel_id=1, source_target_pairs={{0,24},{16,8},{24,0},{8,16},{1,25},{17,9},{25,1},{9,17},{2,26},{18... | collective-permute-start | bytes 393224 | tf_op jit(solution)/shard_map/kernel/ppermute | solution.py:34
  71.8 1.2 %collective-permute-done.27 = bf16[32,1280]{1,0:T(8,128)(2,1)S(1)} collective-permute-done((bf16[32,1280]{1,0:T(8,128)(2,1)S(1)}, bf16[32,1280]{1,0:T(8,128)(2,1)S(1)}, u32[]{:S(2)}, u32[]{:S(2)}) %collective-permute-start.27) | collective-permute-done | bytes 81952 | tf_op jit(solution)/shard_map/kernel/ppermute | solution.py:24
  73.0 1.2 %collective-permute-start.30 = (bf16[32,1280]{1,0:T(8,128)(2,1)S(1)}, bf16[32,1280]{1,0:T(8,128)(2,1)S(1)}, u32[]{:S(2)}, u32[]{:S(2)}) collective-permute-start(bf16[32,1280]{1,0:T(8,128)(2,1)S(1)} %get-tuple-element.108.refs_0_), channel_id=1, source_target_pairs={{0,2},{1,3},{2,0},{3,1},{4,6},{5,7},{6,4},{7,5},{8,10},{9,11},{10,... | collective-permute-start | bytes 245768 | tf_op jit(solution)/shard_map/kernel/ppermute | solution.py:24
  74.2 1.6 %collective-permute-start.35 = (bf16[32,1280]{1,0:T(8,128)(2,1)S(1)}, bf16[32,1280]{1,0:T(8,128)(2,1)S(1)}, u32[]{:S(2)}, u32[]{:S(2)}) collective-permute-start(bf16[32,1280]{1,0:T(8,128)(2,1)S(1)} %get-tuple-element.108.refs_0_), channel_id=1, source_target_pairs={{0,6},{1,7},{2,4},{3,5},{4,2},{5,3},{6,0},{7,1},{8,14},{9,15},{10,... | collective-permute-start | bytes 245768 | tf_op jit(solution)/shard_map/kernel/ppermute | solution.py:24
  76.6 1.6 %collective-permute-done.30.refs_2_ = bf16[32,1280]{1,0:T(8,128)(2,1)S(1)} collective-permute-done((bf16[32,1280]{1,0:T(8,128)(2,1)S(1)}, bf16[32,1280]{1,0:T(8,128)(2,1)S(1)}, u32[]{:S(2)}, u32[]{:S(2)}) %collective-permute-start.30) | collective-permute-done | bytes 81952 | tf_op jit(solution)/shard_map/kernel/ppermute | solution.py:24
  78.2 1.6 %collective-permute-done.35.refs_6_ = bf16[32,1280]{1,0:T(8,128)(2,1)S(1)} collective-permute-done((bf16[32,1280]{1,0:T(8,128)(2,1)S(1)}, bf16[32,1280]{1,0:T(8,128)(2,1)S(1)}, u32[]{:S(2)}, u32[]{:S(2)}) %collective-permute-start.35) | collective-permute-done | bytes 81952 | tf_op jit(solution)/shard_map/kernel/ppermute | solution.py:24
  81.2 1.9 %collective-permute-start.37 = (bf16[128,512]{1,0:T(8,128)(2,1)S(1)}, bf16[128,512]{1,0:T(8,128)(2,1)S(1)}, u32[]{:S(2)}, u32[]{:S(2)}) collective-permute-start(bf16[128,512]{1,0:T(8,128)(2,1)S(1)} %get-tuple-element.86), channel_id=1, source_target_pairs={{0,8},{16,0},{24,16},{8,24},{1,9},{17,1},{25,17},{9,25},{2,10},{18... | collective-permute-start | bytes 393224 | tf_op jit(solution)/shard_map/kernel/ppermute | solution.py:34
  83.1 4.7 %embedding_gradient.1 = (bf16[2,512,1024]{2,1,0:T(8,128)(2,1)S(1)}, f32[8,128]{1,0:T(8,128)S(1)}) custom-call(s32[2]{0:T(128)S(1)} %pad_add_fusion.place_ref, f32[32,1280]{1,0:T(8,128)S(1)} %get-tuple-element.109.own_ref, bf16[32,1280]{1,0:T(8,128)(2,1)S(1)} %get-tuple-element.108.refs_0_, bf16[32,1280]{1,0:T(8,128)(2,1)S(1)} %collective-permute-done.29.refs_1_, ...), custom_call_target="tpu_custom_call" | custom-call | flops 1073741824 | bytes 4194304 | tf_op jit(solution)/shard_map/dz/embedding_gradient/pallas_call | solution.py:271
  87.9 1.0 d_act_matmul.3
  89.0 1.5 %collective-permute-done.38.refs_0_ = bf16[1,272,512]{2,1,0:T(8,128)(2,1)S(1)} collective-permute-done((bf16[1,272,512]{2,1,0:T(8,128)(2,1)S(1)}, bf16[1,272,512]{2,1,0:T(8,128)(2,1)S(1)}, u32[]{:S(2)}, u32[]{:S(2)}) %collective-permute-start.38) | collective-permute-done | bytes 278560 | tf_op jit(solution)/shard_map/d_act/ppermute | solution.py:24
  90.5 1.8 %d_act_matmul.4 = (bf16[272,512]{1,0:T(8,128)(2,1)S(1)}, bf16[3,272,512]{2,1,0:T(8,128)(2,1)S(1)}) custom-call(s32[2]{0:T(128)S(1)} %pad_add_fusion.place_ref, bf16[2,512,1024]{2,1,0:T(8,128)(2,1)S(1)} %get-tuple-element.87.dz_ref.refs_9_, f32[8,128]{1,0:T(8,128)S(1)} %get-tuple-element.88.share_ref, ...), custom_call_target="tpu_custom_call" | custom-call | flops 1073741824 | bytes 1048576 | tf_op jit(solution)/shard_map/d_act/d_act_matmul/pallas_call | solution.py:338
  93.1 1.5 %collective-permute-start.42 = (bf16[272,512]{1,0:T(8,128)(2,1)S(1)}, bf16[272,512]{1,0:T(8,128)(2,1)S(1)}, u32[]{:S(2)}, u32[]{:S(2)}) collective-permute-start(bf16[272,512]{1,0:T(8,128)(2,1)S(1)} %get-tuple-element.93), channel_id=1, source_target_pairs={{0,6},{1,7},{2,4},{3,5},{4,2},{5,3},{6,0},{7,1},{8,14},{9,15},{10,... | collective-permute-start | bytes 835592 | tf_op jit(solution)/shard_map/d_act/ppermute | solution.py:24
  94.8 1.6 %d_act_matmul.5 = (bf16[272,512]{1,0:T(8,128)(2,1)S(1)}, bf16[272,512]{1,0:T(8,128)(2,1)S(1)}, f32[272,512]{1,0:T(8,128)S(1)}) custom-call(s32[2]{0:T(128)S(1)} %pad_add_fusion.place_ref, bf16[2,512,1024]{2,1,0:T(8,128)(2,1)S(1)} %get-tuple-element.87.dz_ref.refs_9_, f32[8,128]{1,0:T(8,128)S(1)} %get-tuple-element.88.share_ref, ...), custom_call_target="tpu_custom_call" | custom-call | flops 805306368 | bytes 786432 | tf_op jit(solution)/shard_map/d_act/d_act_matmul/pallas_call | solution.py:338
  96.4 1.6 %collective-permute-start.40 = (bf16[272,512]{1,0:T(8,128)(2,1)S(1)}, bf16[272,512]{1,0:T(8,128)(2,1)S(1)}, u32[]{:S(2)}, u32[]{:S(2)}) collective-permute-start(bf16[272,512]{1,0:T(8,128)(2,1)S(1)} %get-tuple-element.91), channel_id=1, source_target_pairs={{0,2},{1,3},{2,0},{3,1},{4,6},{5,7},{6,4},{7,5},{8,10},{9,11},{10,... | collective-permute-start | bytes 835592 | tf_op jit(solution)/shard_map/d_act/ppermute | solution.py:24
  98.5 2.9 %weight_gradient.2.refs_10_ = f32[1024,1024]{1,0:T(8,128)} custom-call(s32[2]{0:T(128)S(1)} %pad_add_fusion.place_ref, bf16[256,512]{1,0:T(8,128)(2,1)S(1)} %bitcast.34, bf16[256,512]{1,0:T(8,128)(2,1)S(1)} %collective-permute-done.3.refs_0_.refs_1_, bf16[256,512]{1,0:T(8,128)(2,1)S(1)} %collective-permute-done.5.refs_1_.refs_2_, ...), custom_call_target="tpu_custom_call" | custom-call | flops 1073741824 | bytes 2097152 | tf_op jit(solution)/shard_map/grad_weight/weight_gradient/pallas_call | solution.py:443
  101.4 2.9 %weight_gradient.3 = f32[1024,1024]{1,0:T(8,128)} custom-call(s32[2]{0:T(128)S(1)} %pad_add_fusion.place_ref, bf16[256,512]{1,0:T(8,128)(2,1)S(1)} %collective-permute-done.9.refs_1_.refs_0_, bf16[256,512]{1,0:T(8,128)(2,1)S(1)} %collective-permute-done.4.refs_0_.refs_1_, ...), custom_call_target="tpu_custom_call", output_to_operand_aliasing={{}: (11, {})} | custom-call | flops 1073741824 | bytes 2097152 | tf_op jit(solution)/shard_map/grad_weight/weight_gradient/pallas_call | solution.py:443
  104.3 4.4 %collective-permute-done.40 = bf16[272,512]{1,0:T(8,128)(2,1)S(1)} collective-permute-done((bf16[272,512]{1,0:T(8,128)(2,1)S(1)}, bf16[272,512]{1,0:T(8,128)(2,1)S(1)}, u32[]{:S(2)}, u32[]{:S(2)}) %collective-permute-start.40) | collective-permute-done | bytes 278560 | tf_op jit(solution)/shard_map/d_act/ppermute | solution.py:24
  109.4 2.5 %collective-permute-start.46 = (f32[8,512]{1,0:T(8,128)S(1)}, f32[8,512]{1,0:T(8,128)S(1)}, u32[]{:S(2)}, u32[]{:S(2)}) collective-permute-start(f32[8,512]{1,0:T(8,128)S(1)} %pad_maximum_fusion.1.refs_0_), channel_id=1, source_target_pairs={{0,24},{8,16},{16,8},{24,0},{1,25},{9,17},{17,9},{25,1},{2,26},{10... | collective-permute-start | bytes 49160 | tf_op jit(solution)/shard_map/norm_backward/ppermute | solution.py:24
  112.0 1.8 %collective-permute-start.44 = (f32[8,512]{1,0:T(8,128)S(1)}, f32[8,512]{1,0:T(8,128)S(1)}, u32[]{:S(2)}, u32[]{:S(2)}) collective-permute-start(f32[8,512]{1,0:T(8,128)S(1)} %pad_maximum_fusion.1.refs_0_), channel_id=1, source_target_pairs={{0,8},{8,0},{16,24},{24,16},{1,9},{9,1},{17,25},{25,17},{2,10},{10... | collective-permute-start | bytes 49160 | tf_op jit(solution)/shard_map/norm_backward/ppermute | solution.py:24
  113.8 1.3 %collective-permute-done.46.refs_3_ = f32[8,512]{1,0:T(8,128)S(1)} collective-permute-done((f32[8,512]{1,0:T(8,128)S(1)}, f32[8,512]{1,0:T(8,128)S(1)}, u32[]{:S(2)}, u32[]{:S(2)}) %collective-permute-start.46) | collective-permute-done | bytes 16416 | tf_op jit(solution)/shard_map/norm_backward/ppermute | solution.py:24
  115.1 1.4 %collective-permute-done.45.refs_2_ = f32[8,512]{1,0:T(8,128)S(1)} collective-permute-done((f32[8,512]{1,0:T(8,128)S(1)}, f32[8,512]{1,0:T(8,128)S(1)}, u32[]{:S(2)}, u32[]{:S(2)}) %collective-permute-start.45) | collective-permute-done | bytes 16416 | tf_op jit(solution)/shard_map/norm_backward/ppermute | solution.py:24
  (91 shorter events, 13.6 us)
Async XLA Ops:
  1.8 9.7 %copy-start.1 = (bf16[2,128,512]{2,1,0:T(8,128)(2,1)S(1)}, bf16[2,128,512]{2,1,0:T(8,128)(2,1)}, u32[]{:S(2)}) copy-start(bf16[2,128,512]{2,1,0:T(8,128)(2,1)} %views_ref) | copy-start | bytes 786436
  1.8 9.2 %collective-permute-start.2 = (f32[4,512]{1,0:T(4,128)S(1)}, f32[4,512]{1,0:T(4,128)S(1)}, u32[]{:S(2)}, u32[]{:S(2)}) collective-permute-start(f32[4,512]{1,0:T(4,128)S(1)} %norm_statistics.1), channel_id=1, source_target_pairs={{0,24},{8,16},{16,8},{24,0},{1,25},{9,17},{17,9},{25,1},{2,26},{10... | collective-permute-start | bytes 24584 | tf_op jit(solution)/shard_map/norm_stats/ppermute | solution.py:24
  6.9 4.5 %collective-permute-start.1 = (f32[4,512]{1,0:T(4,128)S(1)}, f32[4,512]{1,0:T(4,128)S(1)}, u32[]{:S(2)}, u32[]{:S(2)}) collective-permute-start(f32[4,512]{1,0:T(4,128)S(1)} %norm_statistics.1), channel_id=1, source_target_pairs={{0,16},{8,24},{16,0},{24,8},{1,17},{9,25},{17,1},{25,9},{2,18},{10... | collective-permute-start | bytes 24584 | tf_op jit(solution)/shard_map/norm_stats/ppermute | solution.py:24
  7.0 4.5 %collective-permute-start = (f32[4,512]{1,0:T(4,128)S(1)}, f32[4,512]{1,0:T(4,128)S(1)}, u32[]{:S(2)}, u32[]{:S(2)}) collective-permute-start(f32[4,512]{1,0:T(4,128)S(1)} %norm_statistics.1), channel_id=1, source_target_pairs={{0,8},{8,0},{16,24},{24,16},{1,9},{9,1},{17,25},{25,17},{2,10},{10... | collective-permute-start | bytes 24584 | tf_op jit(solution)/shard_map/norm_stats/ppermute | solution.py:24
  11.8 3.6 %collective-permute-start.9 = (bf16[256,512]{1,0:T(8,128)(2,1)S(1)}, bf16[256,512]{1,0:T(8,128)(2,1)S(1)}, u32[]{:S(2)}, u32[]{:S(2)}) collective-permute-start(bf16[256,512]{1,0:T(8,128)(2,1)S(1)} %bitcast.28), channel_id=1, source_target_pairs={{0,1},{1,0},{2,3},{3,2},{4,5},{5,4},{6,7},{7,6},{8,9},{9,8},{10,11... | collective-permute-start | bytes 786440 | tf_op jit(solution)/shard_map/act_gather/ppermute | solution.py:24
  11.9 10.1 %collective-permute-start.7 = (bf16[256,512]{1,0:T(8,128)(2,1)S(1)}, bf16[256,512]{1,0:T(8,128)(2,1)S(1)}, u32[]{:S(2)}, u32[]{:S(2)}) collective-permute-start(bf16[256,512]{1,0:T(8,128)(2,1)S(1)} %bitcast.29), channel_id=1, source_target_pairs={{0,6},{1,7},{2,4},{3,5},{4,2},{5,3},{6,0},{7,1},{8,14},{9,15},{10,... | collective-permute-start | bytes 786440 | tf_op jit(solution)/shard_map/act_gather/ppermute | solution.py:24
  14.4 12.7 %collective-permute-start.5 = (bf16[256,512]{1,0:T(8,128)(2,1)S(1)}, bf16[256,512]{1,0:T(8,128)(2,1)S(1)}, u32[]{:S(2)}, u32[]{:S(2)}) collective-permute-start(bf16[256,512]{1,0:T(8,128)(2,1)S(1)} %bitcast.30), channel_id=1, source_target_pairs={{0,4},{1,5},{2,6},{3,7},{4,0},{5,1},{6,2},{7,3},{8,12},{9,13},{10,... | collective-permute-start | bytes 786440 | tf_op jit(solution)/shard_map/act_gather/ppermute | solution.py:24
  14.9 12.3 %collective-permute-start.3 = (bf16[256,512]{1,0:T(8,128)(2,1)S(1)}, bf16[256,512]{1,0:T(8,128)(2,1)S(1)}, u32[]{:S(2)}, u32[]{:S(2)}) collective-permute-start(bf16[256,512]{1,0:T(8,128)(2,1)S(1)} %bitcast.31), channel_id=1, source_target_pairs={{0,2},{1,3},{2,0},{3,1},{4,6},{5,7},{6,4},{7,5},{8,10},{9,11},{10,... | collective-permute-start | bytes 786440 | tf_op jit(solution)/shard_map/act_gather/ppermute | solution.py:24
  15.5 13.7 %collective-permute-start.11 = (bf16[128,512]{1,0:T(8,128)(2,1)S(1)}, bf16[128,512]{1,0:T(8,128)(2,1)S(1)}, u32[]{:S(2)}, u32[]{:S(2)}) collective-permute-start(bf16[128,512]{1,0:T(8,128)(2,1)S(1)} %slice_bitcast_fusion.1), channel_id=1, source_target_pairs={{0,16},{16,24},{24,8},{8,0},{1,17},{17,25},{25,9},{9,1},{2,18},{18... | collective-permute-start | bytes 393224 | tf_op jit(solution)/shard_map/act_gather/ppermute | solution.py:34
  17.6 11.8 %collective-permute-start.12 = (bf16[128,512]{1,0:T(8,128)(2,1)S(1)}, bf16[128,512]{1,0:T(8,128)(2,1)S(1)}, u32[]{:S(2)}, u32[]{:S(2)}) collective-permute-start(bf16[128,512]{1,0:T(8,128)(2,1)S(1)} %slice_bitcast_fusion.1), channel_id=1, source_target_pairs={{0,24},{16,8},{24,0},{8,16},{1,25},{17,9},{25,1},{9,17},{2,26},{18... | collective-permute-start | bytes 393224 | tf_op jit(solution)/shard_map/act_gather/ppermute | solution.py:34
  22.0 8.6 %collective-permute-start.10 = (bf16[128,512]{1,0:T(8,128)(2,1)S(1)}, bf16[128,512]{1,0:T(8,128)(2,1)S(1)}, u32[]{:S(2)}, u32[]{:S(2)}) collective-permute-start(bf16[128,512]{1,0:T(8,128)(2,1)S(1)} %slice_bitcast_fusion.1), channel_id=1, source_target_pairs={{0,8},{16,0},{24,16},{8,24},{1,9},{17,1},{25,17},{9,25},{2,10},{18... | collective-permute-start | bytes 393224 | tf_op jit(solution)/shard_map/act_gather/ppermute | solution.py:34
  27.1 6.5 %collective-permute-start.8 = (bf16[256,512]{1,0:T(8,128)(2,1)S(1)}, bf16[256,512]{1,0:T(8,128)(2,1)S(1)}, u32[]{:S(2)}, u32[]{:S(2)}) collective-permute-start(bf16[256,512]{1,0:T(8,128)(2,1)S(1)} %collective-permute-done.7.refs_2_.refs_3_), channel_id=1, source_target_pairs={{0,1},{1,0},{2,3},{3,2},{4,5},{5,4},{6,7},{7,6},{8,9},{9,8},{10,11... | collective-permute-start | bytes 786440 | tf_op jit(solution)/shard_map/act_gather/ppermute | solution.py:24
  27.2 6.4 %collective-permute-start.6 = (bf16[256,512]{1,0:T(8,128)(2,1)S(1)}, bf16[256,512]{1,0:T(8,128)(2,1)S(1)}, u32[]{:S(2)}, u32[]{:S(2)}) collective-permute-start(bf16[256,512]{1,0:T(8,128)(2,1)S(1)} %collective-permute-done.5.refs_1_.refs_2_), channel_id=1, source_target_pairs={{0,1},{1,0},{2,3},{3,2},{4,5},{5,4},{6,7},{7,6},{8,9},{9,8},{10,11... | collective-permute-start | bytes 786440 | tf_op jit(solution)/shard_map/act_gather/ppermute | solution.py:24
  29.2 4.5 %collective-permute-start.4 = (bf16[256,512]{1,0:T(8,128)(2,1)S(1)}, bf16[256,512]{1,0:T(8,128)(2,1)S(1)}, u32[]{:S(2)}, u32[]{:S(2)}) collective-permute-start(bf16[256,512]{1,0:T(8,128)(2,1)S(1)} %collective-permute-done.3.refs_0_.refs_1_), channel_id=1, source_target_pairs={{0,1},{1,0},{2,3},{3,2},{4,5},{5,4},{6,7},{7,6},{8,9},{9,8},{10,11... | collective-permute-start | bytes 786440 | tf_op jit(solution)/shard_map/act_gather/ppermute | solution.py:24
  30.6 11.1 %collective-permute-start.17 = (bf16[384,512]{1,0:T(8,128)(2,1)S(1)}, bf16[384,512]{1,0:T(8,128)(2,1)S(1)}, u32[]{:S(2)}, u32[]{:S(2)}) collective-permute-start(bf16[384,512]{1,0:T(8,128)(2,1)S(1)} %constant_dynamic-update-slice_fusion.refs_0_.refs_4_), channel_id=1, source_target_pairs={{0,4},{1,5},{2,6},{3,7},{4,0},{5,1},{6,2},{7,3},{8,12},{9,13},{10,... | collective-permute-start | bytes 1179656 | tf_op jit(solution)/shard_map/z/ppermute | solution.py:24
  32.2 11.1 %collective-permute-start.15 = (bf16[384,512]{1,0:T(8,128)(2,1)S(1)}, bf16[384,512]{1,0:T(8,128)(2,1)S(1)}, u32[]{:S(2)}, u32[]{:S(2)}) collective-permute-start(bf16[384,512]{1,0:T(8,128)(2,1)S(1)} %constant_dynamic-update-slice_fusion.refs_0_.refs_4_), channel_id=1, source_target_pairs={{0,2},{1,3},{2,0},{3,1},{4,6},{5,7},{6,4},{7,5},{8,10},{9,11},{10,... | collective-permute-start | bytes 1179656 | tf_op jit(solution)/shard_map/z/ppermute | solution.py:24
  35.2 9.7 %collective-permute-start.14 = (bf16[128,1024]{1,0:T(8,128)(2,1)S(1)}, bf16[128,1024]{1,0:T(8,128)(2,1)S(1)}, u32[]{:S(2)}, u32[]{:S(2)}) collective-permute-start(bf16[128,1024]{1,0:T(8,128)(2,1)S(1)} %get-tuple-element.66.refs_1_.refs_9_), channel_id=1, source_target_pairs={{0,16},{16,24},{24,8},{8,0},{1,17},{17,25},{25,9},{9,1},{2,18},{18... | collective-permute-start | bytes 786440 | tf_op jit(solution)/shard_map/z_ring/ppermute | solution.py:34
  41.7 6.9 %collective-permute-start.19 = (bf16[192,512]{1,0:T(8,128)(2,1)S(1)}, bf16[192,512]{1,0:T(8,128)(2,1)S(1)}, u32[]{:S(2)}, u32[]{:S(2)}) collective-permute-start(bf16[192,512]{1,0:T(8,128)(2,1)S(1)} %slice.160), channel_id=1, source_target_pairs={{0,2},{1,3},{2,0},{3,1},{4,6},{5,7},{6,4},{7,5},{8,10},{9,11},{10,... | collective-permute-start | bytes 589832 | tf_op jit(solution)/shard_map/z/ppermute | solution.py:24
  43.3 5.8 %collective-permute-start.20 = (bf16[192,512]{1,0:T(8,128)(2,1)S(1)}, bf16[192,512]{1,0:T(8,128)(2,1)S(1)}, u32[]{:S(2)}, u32[]{:S(2)}) collective-permute-start(bf16[192,512]{1,0:T(8,128)(2,1)S(1)} %slice.161), channel_id=1, source_target_pairs={{0,4},{1,5},{2,6},{3,7},{4,0},{5,1},{6,2},{7,3},{8,12},{9,13},{10,... | collective-permute-start | bytes 589832 | tf_op jit(solution)/shard_map/z/ppermute | solution.py:24
  44.9 6.8 %collective-permute-start.21 = (bf16[128,1024]{1,0:T(8,128)(2,1)S(1)}, bf16[128,1024]{1,0:T(8,128)(2,1)S(1)}, u32[]{:S(2)}, u32[]{:S(2)}) collective-permute-start(bf16[128,1024]{1,0:T(8,128)(2,1)S(1)} %collective-permute-done.14.refs_3_.refs_11_), channel_id=1, source_target_pairs={{0,16},{16,24},{24,8},{8,0},{1,17},{17,25},{25,9},{9,1},{2,18},{18... | collective-permute-start | bytes 786440 | tf_op jit(solution)/shard_map/z_ring/ppermute | solution.py:34
  46.1 7.6 %collective-permute-start.13 = (bf16[384,512]{1,0:T(8,128)(2,1)S(1)}, bf16[384,512]{1,0:T(8,128)(2,1)S(1)}, u32[]{:S(2)}, u32[]{:S(2)}) collective-permute-start(bf16[384,512]{1,0:T(8,128)(2,1)S(1)} %constant_dynamic-update-slice_fusion.refs_0_.refs_4_), channel_id=1, source_target_pairs={{0,1},{1,0},{2,3},{3,2},{4,5},{5,4},{6,7},{7,6},{8,9},{9,8},{10,11... | collective-permute-start | bytes 1179656 | tf_op jit(solution)/shard_map/z_far/ppermute | solution.py:24
  46.2 8.3 %collective-permute-start.16 = (bf16[384,512]{1,0:T(8,128)(2,1)S(1)}, bf16[384,512]{1,0:T(8,128)(2,1)S(1)}, u32[]{:S(2)}, u32[]{:S(2)}) collective-permute-start(bf16[384,512]{1,0:T(8,128)(2,1)S(1)} %collective-permute-done.15.refs_1_.refs_5_), channel_id=1, source_target_pairs={{0,1},{1,0},{2,3},{3,2},{4,5},{5,4},{6,7},{7,6},{8,9},{9,8},{10,11... | collective-permute-start | bytes 1179656 | tf_op jit(solution)/shard_map/z_far/ppermute | solution.py:24
  48.6 5.9 %collective-permute-start.18 = (bf16[384,512]{1,0:T(8,128)(2,1)S(1)}, bf16[384,512]{1,0:T(8,128)(2,1)S(1)}, u32[]{:S(2)}, u32[]{:S(2)}) collective-permute-start(bf16[384,512]{1,0:T(8,128)(2,1)S(1)} %collective-permute-done.17.refs_2_.refs_6_), channel_id=1, source_target_pairs={{0,1},{1,0},{2,3},{3,2},{4,5},{5,4},{6,7},{7,6},{8,9},{9,8},{10,11... | collective-permute-start | bytes 1179656 | tf_op jit(solution)/shard_map/z_far/ppermute | solution.py:24
  51.7 2.8 %collective-permute-start.22 = (bf16[384,512]{1,0:T(8,128)(2,1)S(1)}, bf16[384,512]{1,0:T(8,128)(2,1)S(1)}, u32[]{:S(2)}, u32[]{:S(2)}) collective-permute-start(bf16[384,512]{1,0:T(8,128)(2,1)S(1)} %pad_maximum_fusion.refs_3_.refs_7_), channel_id=1, source_target_pairs={{0,1},{1,0},{2,3},{3,2},{4,5},{5,4},{6,7},{7,6},{8,9},{9,8},{10,11... | collective-permute-start | bytes 1179656 | tf_op jit(solution)/shard_map/z_far/ppermute | solution.py:24
  51.7 9.1 %collective-permute-start.23 = (bf16[128,1024]{1,0:T(8,128)(2,1)S(1)}, bf16[128,1024]{1,0:T(8,128)(2,1)S(1)}, u32[]{:S(2)}, u32[]{:S(2)}) collective-permute-start(bf16[128,1024]{1,0:T(8,128)(2,1)S(1)} %collective-permute-done.21.refs_5_.refs_13_), channel_id=1, source_target_pairs={{0,16},{16,24},{24,8},{8,0},{1,17},{17,25},{25,9},{9,1},{2,18},{18... | collective-permute-start | bytes 786440 | tf_op jit(solution)/shard_map/z_far/ppermute | solution.py:34
  53.7 9.8 %collective-permute-start.24 = (bf16[128,512]{1,0:T(8,128)(2,1)S(1)}, bf16[128,512]{1,0:T(8,128)(2,1)S(1)}, u32[]{:S(2)}, u32[]{:S(2)}) collective-permute-start(bf16[128,512]{1,0:T(8,128)(2,1)S(1)} %get-tuple-element.81), channel_id=1, source_target_pairs={{0,16},{16,24},{24,8},{8,0},{1,17},{17,25},{25,9},{9,1},{2,18},{18... | collective-permute-start | bytes 393224 | tf_op jit(solution)/shard_map/kernel/ppermute | solution.py:34
  63.5 1.7 %collective-permute-start.25 = (bf16[4,32,1280]{2,1,0:T(8,128)(2,1)S(1)}, bf16[4,32,1280]{2,1,0:T(8,128)(2,1)S(1)}, u32[]{:S(2)}, u32[]{:S(2)}) collective-permute-start(bf16[4,32,1280]{2,1,0:T(8,128)(2,1)S(1)} %get-tuple-element.82), channel_id=1, source_target_pairs={{0,1},{1,0},{2,3},{3,2},{4,5},{5,4},{6,7},{7,6},{8,9},{9,8},{10,11... | collective-permute-start | bytes 983048 | tf_op jit(solution)/shard_map/kernel/ppermute | solution.py:24
  65.3 5.7 %collective-permute-start.26 = (bf16[32,1280]{1,0:T(8,128)(2,1)S(1)}, bf16[32,1280]{1,0:T(8,128)(2,1)S(1)}, u32[]{:S(2)}, u32[]{:S(2)}) collective-permute-start(bf16[32,1280]{1,0:T(8,128)(2,1)S(1)} %get-tuple-element.114), channel_id=1, source_target_pairs={{0,2},{1,3},{2,0},{3,1},{4,6},{5,7},{6,4},{7,5},{8,10},{9,11},{10,... | collective-permute-start | bytes 245768 | tf_op jit(solution)/shard_map/kernel/ppermute | solution.py:24
  66.1 5.7 %collective-permute-start.28 = (bf16[32,1280]{1,0:T(8,128)(2,1)S(1)}, bf16[32,1280]{1,0:T(8,128)(2,1)S(1)}, u32[]{:S(2)}, u32[]{:S(2)}) collective-permute-start(bf16[32,1280]{1,0:T(8,128)(2,1)S(1)} %get-tuple-element.115), channel_id=1, source_target_pairs={{0,6},{1,7},{2,4},{3,5},{4,2},{5,3},{6,0},{7,1},{8,14},{9,15},{10,... | collective-permute-start | bytes 245768 | tf_op jit(solution)/shard_map/kernel/ppermute | solution.py:24
  67.5 5.5 %collective-permute-start.27 = (bf16[32,1280]{1,0:T(8,128)(2,1)S(1)}, bf16[32,1280]{1,0:T(8,128)(2,1)S(1)}, u32[]{:S(2)}, u32[]{:S(2)}) collective-permute-start(bf16[32,1280]{1,0:T(8,128)(2,1)S(1)} %get-tuple-element.116), channel_id=1, source_target_pairs={{0,4},{1,5},{2,6},{3,7},{4,0},{5,1},{6,2},{7,3},{8,12},{9,13},{10,... | collective-permute-start | bytes 245768 | tf_op jit(solution)/shard_map/kernel/ppermute | solution.py:24
  68.9 7.7 %collective-permute-start.31 = (bf16[128,512]{1,0:T(8,128)(2,1)S(1)}, bf16[128,512]{1,0:T(8,128)(2,1)S(1)}, u32[]{:S(2)}, u32[]{:S(2)}) collective-permute-start(bf16[128,512]{1,0:T(8,128)(2,1)S(1)} %get-tuple-element.83), channel_id=1, source_target_pairs={{0,24},{16,8},{24,0},{8,16},{1,25},{17,9},{25,1},{9,17},{2,26},{18... | collective-permute-start | bytes 393224 | tf_op jit(solution)/shard_map/kernel/ppermute | solution.py:34
  73.0 5.1 %collective-permute-start.30 = (bf16[32,1280]{1,0:T(8,128)(2,1)S(1)}, bf16[32,1280]{1,0:T(8,128)(2,1)S(1)}, u32[]{:S(2)}, u32[]{:S(2)}) collective-permute-start(bf16[32,1280]{1,0:T(8,128)(2,1)S(1)} %get-tuple-element.108.refs_0_), channel_id=1, source_target_pairs={{0,2},{1,3},{2,0},{3,1},{4,6},{5,7},{6,4},{7,5},{8,10},{9,11},{10,... | collective-permute-start | bytes 245768 | tf_op jit(solution)/shard_map/kernel/ppermute | solution.py:24
  74.2 5.6 %collective-permute-start.35 = (bf16[32,1280]{1,0:T(8,128)(2,1)S(1)}, bf16[32,1280]{1,0:T(8,128)(2,1)S(1)}, u32[]{:S(2)}, u32[]{:S(2)}) collective-permute-start(bf16[32,1280]{1,0:T(8,128)(2,1)S(1)} %get-tuple-element.108.refs_0_), channel_id=1, source_target_pairs={{0,6},{1,7},{2,4},{3,5},{4,2},{5,3},{6,0},{7,1},{8,14},{9,15},{10,... | collective-permute-start | bytes 245768 | tf_op jit(solution)/shard_map/kernel/ppermute | solution.py:24
  75.9 4.8 %collective-permute-start.33 = (bf16[32,1280]{1,0:T(8,128)(2,1)S(1)}, bf16[32,1280]{1,0:T(8,128)(2,1)S(1)}, u32[]{:S(2)}, u32[]{:S(2)}) collective-permute-start(bf16[32,1280]{1,0:T(8,128)(2,1)S(1)} %get-tuple-element.108.refs_0_), channel_id=1, source_target_pairs={{0,4},{1,5},{2,6},{3,7},{4,0},{5,1},{6,2},{7,3},{8,12},{9,13},{10,... | collective-permute-start | bytes 245768 | tf_op jit(solution)/shard_map/kernel/ppermute | solution.py:24
  76.6 6.5 %collective-permute-start.29 = (bf16[32,1280]{1,0:T(8,128)(2,1)S(1)}, bf16[32,1280]{1,0:T(8,128)(2,1)S(1)}, u32[]{:S(2)}, u32[]{:S(2)}) collective-permute-start(bf16[32,1280]{1,0:T(8,128)(2,1)S(1)} %get-tuple-element.108.refs_0_), channel_id=1, source_target_pairs={{0,1},{1,0},{2,3},{3,2},{4,5},{5,4},{6,7},{7,6},{8,9},{9,8},{10,11... | collective-permute-start | bytes 245768 | tf_op jit(solution)/shard_map/kernel/ppermute | solution.py:24
  79.8 3.3 %collective-permute-start.36 = (bf16[32,1280]{1,0:T(8,128)(2,1)S(1)}, bf16[32,1280]{1,0:T(8,128)(2,1)S(1)}, u32[]{:S(2)}, u32[]{:S(2)}) collective-permute-start(bf16[32,1280]{1,0:T(8,128)(2,1)S(1)} %collective-permute-done.35.refs_6_), channel_id=1, source_target_pairs={{0,1},{1,0},{2,3},{3,2},{4,5},{5,4},{6,7},{7,6},{8,9},{9,8},{10,11... | collective-permute-start | bytes 245768 | tf_op jit(solution)/shard_map/kernel/ppermute | solution.py:24
  80.7 2.5 %collective-permute-start.34 = (bf16[32,1280]{1,0:T(8,128)(2,1)S(1)}, bf16[32,1280]{1,0:T(8,128)(2,1)S(1)}, u32[]{:S(2)}, u32[]{:S(2)}) collective-permute-start(bf16[32,1280]{1,0:T(8,128)(2,1)S(1)} %collective-permute-done.33.refs_4_), channel_id=1, source_target_pairs={{0,1},{1,0},{2,3},{3,2},{4,5},{5,4},{6,7},{7,6},{8,9},{9,8},{10,11... | collective-permute-start | bytes 245768 | tf_op jit(solution)/shard_map/kernel/ppermute | solution.py:24
  80.7 2.5 %collective-permute-start.32 = (bf16[32,1280]{1,0:T(8,128)(2,1)S(1)}, bf16[32,1280]{1,0:T(8,128)(2,1)S(1)}, u32[]{:S(2)}, u32[]{:S(2)}) collective-permute-start(bf16[32,1280]{1,0:T(8,128)(2,1)S(1)} %collective-permute-done.30.refs_2_), channel_id=1, source_target_pairs={{0,1},{1,0},{2,3},{3,2},{4,5},{5,4},{6,7},{7,6},{8,9},{9,8},{10,11... | collective-permute-start | bytes 245768 | tf_op jit(solution)/shard_map/kernel/ppermute | solution.py:24
  81.2 6.7 %collective-permute-start.37 = (bf16[128,512]{1,0:T(8,128)(2,1)S(1)}, bf16[128,512]{1,0:T(8,128)(2,1)S(1)}, u32[]{:S(2)}, u32[]{:S(2)}) collective-permute-start(bf16[128,512]{1,0:T(8,128)(2,1)S(1)} %get-tuple-element.86), channel_id=1, source_target_pairs={{0,8},{16,0},{24,16},{8,24},{1,9},{17,1},{25,17},{9,25},{2,10},{18... | collective-permute-start | bytes 393224 | tf_op jit(solution)/shard_map/kernel/ppermute | solution.py:34
  88.9 1.6 %collective-permute-start.38 = (bf16[1,272,512]{2,1,0:T(8,128)(2,1)S(1)}, bf16[1,272,512]{2,1,0:T(8,128)(2,1)S(1)}, u32[]{:S(2)}, u32[]{:S(2)}) collective-permute-start(bf16[1,272,512]{2,1,0:T(8,128)(2,1)S(1)} %d_act_matmul.3), channel_id=1, source_target_pairs={{0,1},{1,0},{2,3},{3,2},{4,5},{5,4},{6,7},{7,6},{8,9},{9,8},{10,11... | collective-permute-start | bytes 835592 | tf_op jit(solution)/shard_map/d_act/ppermute | solution.py:24
  92.4 2.4 %collective-permute-start.39 = (bf16[3,272,512]{2,1,0:T(8,128)(2,1)S(1)}, bf16[3,272,512]{2,1,0:T(8,128)(2,1)S(1)}, u32[]{:S(2)}, u32[]{:S(2)}) collective-permute-start(bf16[3,272,512]{2,1,0:T(8,128)(2,1)S(1)} %get-tuple-element.89), channel_id=1, source_target_pairs={{0,1},{1,0},{2,3},{3,2},{4,5},{5,4},{6,7},{7,6},{8,9},{9,8},{10,11... | collective-permute-start | bytes 2506760 | tf_op jit(solution)/shard_map/d_act/ppermute | solution.py:24
  92.6 8.7 %collective-permute-start.43 = (bf16[384,512]{1,0:T(8,128)(2,1)S(1)}, bf16[384,512]{1,0:T(8,128)(2,1)S(1)}, u32[]{:S(2)}, u32[]{:S(2)}) collective-permute-start(bf16[384,512]{1,0:T(8,128)(2,1)S(1)} %constant_dynamic-update-slice_fusion.3.refs_8_), channel_id=1, source_target_pairs={{0,1},{1,0},{2,3},{3,2},{4,5},{5,4},{6,7},{7,6},{8,9},{9,8},{10,11... | collective-permute-start | bytes 1179656 | tf_op jit(solution)/shard_map/grad_weight/ppermute | solution.py:24
  93.1 11.2 %collective-permute-start.42 = (bf16[272,512]{1,0:T(8,128)(2,1)S(1)}, bf16[272,512]{1,0:T(8,128)(2,1)S(1)}, u32[]{:S(2)}, u32[]{:S(2)}) collective-permute-start(bf16[272,512]{1,0:T(8,128)(2,1)S(1)} %get-tuple-element.93), channel_id=1, source_target_pairs={{0,6},{1,7},{2,4},{3,5},{4,2},{5,3},{6,0},{7,1},{8,14},{9,15},{10,... | collective-permute-start | bytes 835592 | tf_op jit(solution)/shard_map/d_act/ppermute | solution.py:24
  96.4 12.3 %collective-permute-start.40 = (bf16[272,512]{1,0:T(8,128)(2,1)S(1)}, bf16[272,512]{1,0:T(8,128)(2,1)S(1)}, u32[]{:S(2)}, u32[]{:S(2)}) collective-permute-start(bf16[272,512]{1,0:T(8,128)(2,1)S(1)} %get-tuple-element.91), channel_id=1, source_target_pairs={{0,2},{1,3},{2,0},{3,1},{4,6},{5,7},{6,4},{7,5},{8,10},{9,11},{10,... | collective-permute-start | bytes 835592 | tf_op jit(solution)/shard_map/d_act/ppermute | solution.py:24
  97.9 10.8 %collective-permute-start.41 = (bf16[272,512]{1,0:T(8,128)(2,1)S(1)}, bf16[272,512]{1,0:T(8,128)(2,1)S(1)}, u32[]{:S(2)}, u32[]{:S(2)}) collective-permute-start(bf16[272,512]{1,0:T(8,128)(2,1)S(1)} %get-tuple-element.92), channel_id=1, source_target_pairs={{0,4},{1,5},{2,6},{3,7},{4,0},{5,1},{6,2},{7,3},{8,12},{9,13},{10,... | collective-permute-start | bytes 835592 | tf_op jit(solution)/shard_map/d_act/ppermute | solution.py:24
  109.4 5.8 %collective-permute-start.46 = (f32[8,512]{1,0:T(8,128)S(1)}, f32[8,512]{1,0:T(8,128)S(1)}, u32[]{:S(2)}, u32[]{:S(2)}) collective-permute-start(f32[8,512]{1,0:T(8,128)S(1)} %pad_maximum_fusion.1.refs_0_), channel_id=1, source_target_pairs={{0,24},{8,16},{16,8},{24,0},{1,25},{9,17},{17,9},{25,1},{2,26},{10... | collective-permute-start | bytes 49160 | tf_op jit(solution)/shard_map/norm_backward/ppermute | solution.py:24
  111.9 4.6 %collective-permute-start.45 = (f32[8,512]{1,0:T(8,128)S(1)}, f32[8,512]{1,0:T(8,128)S(1)}, u32[]{:S(2)}, u32[]{:S(2)}) collective-permute-start(f32[8,512]{1,0:T(8,128)S(1)} %pad_maximum_fusion.1.refs_0_), channel_id=1, source_target_pairs={{0,16},{8,24},{16,0},{24,8},{1,17},{9,25},{17,1},{25,9},{2,18},{10... | collective-permute-start | bytes 49160 | tf_op jit(solution)/shard_map/norm_backward/ppermute | solution.py:24
  112.0 4.6 %collective-permute-start.44 = (f32[8,512]{1,0:T(8,128)S(1)}, f32[8,512]{1,0:T(8,128)S(1)}, u32[]{:S(2)}, u32[]{:S(2)}) collective-permute-start(f32[8,512]{1,0:T(8,128)S(1)} %pad_maximum_fusion.1.refs_0_), channel_id=1, source_target_pairs={{0,8},{8,0},{16,24},{24,16},{1,9},{9,1},{17,25},{25,17},{2,10},{10... | collective-permute-start | bytes 49160 | tf_op jit(solution)/shard_map/norm_backward/ppermute | solution.py:24
  (3 other events, 20.4 us)

commit v19 on v18

--- a/solution.py
+++ b/solution.py
@@ -572,8 +572,14 @@
         far_pieces = link_pieces(jnp.concatenate(others), n_col)
     with jax.named_scope("z_ring"):
         z_ring = [z_own1, ring_send(z_own1, "batch", 1)]
-        z_ring[1], far_pieces[far[0]] = lax.optimization_barrier((z_ring[1], far_pieces[far[0]]))
+        reach = n_batch // 2
+        back = [ring_send(z_own1, "batch", n_batch - 1)]
+        z_ring[1], far_pieces[far[0]], back[0] = lax.optimization_barrier(
+            (z_ring[1], far_pieces[far[0]], back[0])
+        )
         z_ring.append(ring_send(z_ring[1], "batch", 1))
+        for _ in range(reach + 2, n_batch):
+            back.append(ring_send(back[-1], "batch", n_batch - 1))
     with jax.named_scope("z_far"):
         start = z_part(far_pieces, [0] + far[:-1], None)
         picked = list(pick_call(place, [pieces[k] for k in evens], n_batch, n_col))
@@ -581,8 +587,9 @@
             (start, far_pieces[far[-1]], z_ring[2], picked)
         )
         far_pieces = sibling_pieces(far_pieces, n_col)
-        for _ in range(3, n_batch):
+        for _ in range(3, reach + 1):
             z_ring.append(ring_send(z_ring[-1], "batch", 1))
+        z_ring += back[::-1]
         z_far = z_part(far_pieces, odds[:-1] + far[-1:] + odds[-1:], start, True)
         slots = list(zip([z_own0] + list(z_far), z_ring))
     with jax.named_scope("kernel"):

time: 118 us -> 117 us (level)
  starting transfers between devices: 45.4 us -> 44.1 us
    ppermute x9, waiting for transfers between devices: 7.4 us -> 10.3 us  [ring_send(): lax.ppermute(x, axis, [(order[i], order[(i + d) % n]) for i in range(n)])]
    ppermute x38, waiting for transfers between devices: 29.7 us -> 27.6 us  [xor_send(): return lax.ppermute(x, axis, [(i, i ^ k) for i in range(n)])]
  transfers between devices with their start and end apart: 47 -> 47, of which waited for: 20 -> 25; matrix products, arithmetic and copies ran while one was open for 0% -> 0% of each run, Pallas kernels for 24% -> 24%
where the time goes in v19:
time: 117 us
  starting transfers between devices  44.1 us (38%)
  waiting for transfers between devices  37.8 us (32%)
  Pallas kernels  31.7 us (27%)
    ppermute x38, starting transfers between devices, xor_send(): return lax.ppermute(x, axis, [(i, i ^ k) for i in range(n)])  33.2 us
    ppermute x38, waiting for transfers between devices, xor_send(): return lax.ppermute(x, axis, [(i, i ^ k) for i in range(n)])  27.6 us
    ppermute x9, starting transfers between devices, ring_send(): lax.ppermute(x, axis, [(order[i], order[(i + d) % n]) for i in range(n)])  10.9 us
    ppermute x9, waiting for transfers between devices, ring_send(): lax.ppermute(x, axis, [(order[i], order[(i + d) % n]) for i in range(n)])  10.3 us
    pallas_call x5, Pallas kernels, z_call(): pl.pallas_call(functools.partial(z_kernel, tuple(ks), before is None, las...  8.96 us
    pallas_call x2, Pallas kernels, weight_grad_call(): pl.pallas_call(functools.partial(weight_grad_kernel, rows // (near[0][0]....  5.8 us
    pallas_call x1, Pallas kernels, dz_call(): pl.pallas_call(functools.partial(dz_kernel, n_batch, n_col, tile, constan...  4.74 us
    pallas_call x3, Pallas kernels, d_act_call(): pl.pallas_call(functools.partial(d_act_kernel, tuple(evens), tuple(odds),...  4.43 us
  transfers between devices with their start and end apart: 47, of which 25 were waited for; matrix products, arithmetic and copies ran while one was open for 0% of the time, Pallas kernels for 24%

profile of v19, /device:TPU:0, one launch (start us, length us, event | category | flops | bytes accessed | tf_op | source)
XLA Modules:
  0.0 116.9 jit_solution(9000575159067113970)
XLA Ops:
  0.7 0.9 copy-done
  1.8 5.1 %collective-permute-start.2 = (f32[4,512]{1,0:T(4,128)S(1)}, f32[4,512]{1,0:T(4,128)S(1)}, u32[]{:S(2)}, u32[]{:S(2)}) collective-permute-start(f32[4,512]{1,0:T(4,128)S(1)} %norm_statistics.1), channel_id=1, source_target_pairs={{0,24},{8,16},{16,8},{24,0},{1,25},{9,17},{17,9},{25,1},{2,26},{10... | collective-permute-start | bytes 24584 | tf_op jit(solution)/shard_map/norm_stats/ppermute | solution.py:24
  7.6 3.5 %weight_load.1 = (bf16[4096,1024]{1,0:T(8,128)(2,1)S(1)}, f32[4,512]{1,0:T(4,128)S(1)}) custom-call(bf16[4096,1024]{1,0:T(8,128)(2,1)} %w_ref), custom_call_target="tpu_custom_call" | custom-call | bytes 16777216 | tf_op jit(solution)/shard_map/weight_load/weight_load/pallas_call | solution.py:78
  11.9 2.5 %collective-permute-start.7 = (bf16[256,512]{1,0:T(8,128)(2,1)S(1)}, bf16[256,512]{1,0:T(8,128)(2,1)S(1)}, u32[]{:S(2)}, u32[]{:S(2)}) collective-permute-start(bf16[256,512]{1,0:T(8,128)(2,1)S(1)} %bitcast.29), channel_id=1, source_target_pairs={{0,6},{1,7},{2,4},{3,5},{4,2},{5,3},{6,0},{7,1},{8,14},{9,15},{10,... | collective-permute-start | bytes 786440 | tf_op jit(solution)/shard_map/act_gather/ppermute | solution.py:24
  15.5 2.1 %collective-permute-start.11 = (bf16[128,512]{1,0:T(8,128)(2,1)S(1)}, bf16[128,512]{1,0:T(8,128)(2,1)S(1)}, u32[]{:S(2)}, u32[]{:S(2)}) collective-permute-start(bf16[128,512]{1,0:T(8,128)(2,1)S(1)} %slice_bitcast_fusion.1), channel_id=1, source_target_pairs={{0,16},{16,24},{24,8},{8,0},{1,17},{17,25},{25,9},{9,1},{2,18},{18... | collective-permute-start | bytes 393224 | tf_op jit(solution)/shard_map/act_gather/ppermute | solution.py:34
  17.6 1.4 %collective-permute-start.12 = (bf16[128,512]{1,0:T(8,128)(2,1)S(1)}, bf16[128,512]{1,0:T(8,128)(2,1)S(1)}, u32[]{:S(2)}, u32[]{:S(2)}) collective-permute-start(bf16[128,512]{1,0:T(8,128)(2,1)S(1)} %slice_bitcast_fusion.1), channel_id=1, source_target_pairs={{0,24},{16,8},{24,0},{8,16},{1,25},{17,9},{25,1},{9,17},{2,26},{18... | collective-permute-start | bytes 393224 | tf_op jit(solution)/shard_map/act_gather/ppermute | solution.py:34
  19.0 1.2 %z_matmul.5.refs_4_ = f32[256,1024]{1,0:T(8,128)S(1)} custom-call(s32[2]{0:T(128)S(1)} %pad_add_fusion.place_ref, bf16[256,512]{1,0:T(8,128)(2,1)S(1)} %bitcast.32, bf16[256,512]{1,0:T(8,128)(2,1)S(1)} %collective-permute-done.9.refs_1_.refs_0_, bf16[4096,1024]{1,0:T(8,128)(2,1)S(1)} %get-tuple-element.62.refs_2_.refs_3_.refs_5_.w_ref), custom_call_target="tpu_custom_call" | custom-call | flops 536870912 | bytes 524288 | tf_op jit(solution)/shard_map/z/z_matmul/pallas_call | solution.py:149
  20.2 1.8 %collective-permute-done.7.refs_2_.refs_3_ = bf16[256,512]{1,0:T(8,128)(2,1)S(1)} collective-permute-done((bf16[256,512]{1,0:T(8,128)(2,1)S(1)}, bf16[256,512]{1,0:T(8,128)(2,1)S(1)}, u32[]{:S(2)}, u32[]{:S(2)}) %collective-permute-start.7) | collective-permute-done | bytes 262176 | tf_op jit(solution)/shard_map/act_gather/ppermute | solution.py:24
  22.0 1.0 collective-permute-start.10
  23.0 4.1 %collective-permute-done.5.refs_1_.refs_2_ = bf16[256,512]{1,0:T(8,128)(2,1)S(1)} collective-permute-done((bf16[256,512]{1,0:T(8,128)(2,1)S(1)}, bf16[256,512]{1,0:T(8,128)(2,1)S(1)}, u32[]{:S(2)}, u32[]{:S(2)}) %collective-permute-start.5) | collective-permute-done | bytes 262176 | tf_op jit(solution)/shard_map/act_gather/ppermute | solution.py:24
  27.7 1.5 %z_matmul.6.refs_4_ = f32[256,1024]{1,0:T(8,128)S(1)} custom-call(s32[2]{0:T(128)S(1)} %pad_add_fusion.place_ref, bf16[256,512]{1,0:T(8,128)(2,1)S(1)} %collective-permute-done.3.refs_0_.refs_1_, bf16[256,512]{1,0:T(8,128)(2,1)S(1)} %collective-permute-done.5.refs_1_.refs_2_, bf16[256,512]{1,0:T(8,128)(2,1)S(1)} %collective-permute-done.7.refs_2_.refs_3_, ...), custom_call_target="tpu_custom_call" | custom-call | flops 805306368 | bytes 524288 | tf_op jit(solution)/shard_map/z/z_matmul/pallas_call | solution.py:149
  29.4 1.2 %collective-permute-done.10 = bf16[128,512]{1,0:T(8,128)(2,1)S(1)} collective-permute-done((bf16[128,512]{1,0:T(8,128)(2,1)S(1)}, bf16[128,512]{1,0:T(8,128)(2,1)S(1)}, u32[]{:S(2)}, u32[]{:S(2)}) %collective-permute-start.10) | collective-permute-done | bytes 131104 | tf_op jit(solution)/shard_map/act_gather/ppermute | solution.py:34
  30.6 1.6 %collective-permute-start.18 = (bf16[384,512]{1,0:T(8,128)(2,1)S(1)}, bf16[384,512]{1,0:T(8,128)(2,1)S(1)}, u32[]{:S(2)}, u32[]{:S(2)}) collective-permute-start(bf16[384,512]{1,0:T(8,128)(2,1)S(1)} %constant_dynamic-update-slice_fusion.refs_0_.refs_4_), channel_id=1, source_target_pairs={{0,4},{1,5},{2,6},{3,7},{4,0},{5,1},{6,2},{7,3},{8,12},{9,13},{10,... | collective-permute-start | bytes 1179656 | tf_op jit(solution)/shard_map/z/ppermute | solution.py:24
  32.2 1.5 %collective-permute-start.15 = (bf16[384,512]{1,0:T(8,128)(2,1)S(1)}, bf16[384,512]{1,0:T(8,128)(2,1)S(1)}, u32[]{:S(2)}, u32[]{:S(2)}) collective-permute-start(bf16[384,512]{1,0:T(8,128)(2,1)S(1)} %constant_dynamic-update-slice_fusion.refs_0_.refs_4_), channel_id=1, source_target_pairs={{0,2},{1,3},{2,0},{3,1},{4,6},{5,7},{6,4},{7,5},{8,10},{9,11},{10,... | collective-permute-start | bytes 1179656 | tf_op jit(solution)/shard_map/z/ppermute | solution.py:24
  33.7 1.5 %z_matmul.7 = (bf16[128,1024]{1,0:T(8,128)(2,1)S(1)}, bf16[128,1024]{1,0:T(8,128)(2,1)S(1)}) custom-call(s32[2]{0:T(128)S(1)} %pad_add_fusion.place_ref, bf16[256,512]{1,0:T(8,128)(2,1)S(1)} %collective-permute-done.4.refs_0_.refs_1_, bf16[256,512]{1,0:T(8,128)(2,1)S(1)} %collective-permute-done.6.refs_1_.refs_2_, ...), custom_call_target="tpu_custom_call" | custom-call | flops 805306368 | bytes 524288 | tf_op jit(solution)/shard_map/z/z_matmul/pallas_call | solution.py:149
  35.3 2.9 %collective-permute-start.14 = (bf16[128,1024]{1,0:T(8,128)(2,1)S(1)}, bf16[128,1024]{1,0:T(8,128)(2,1)S(1)}, u32[]{:S(2)}, u32[]{:S(2)}) collective-permute-start(bf16[128,1024]{1,0:T(8,128)(2,1)S(1)} %get-tuple-element.67.refs_1_.refs_9_), channel_id=1, source_target_pairs={{0,16},{16,24},{24,8},{8,0},{1,17},{17,25},{25,9},{9,1},{2,18},{18... | collective-permute-start | bytes 786440 | tf_op jit(solution)/shard_map/z_ring/ppermute | solution.py:34
  38.2 3.5 %collective-permute-done.18.refs_2_.refs_6_ = bf16[384,512]{1,0:T(8,128)(2,1)S(1)} collective-permute-done((bf16[384,512]{1,0:T(8,128)(2,1)S(1)}, bf16[384,512]{1,0:T(8,128)(2,1)S(1)}, u32[]{:S(2)}, u32[]{:S(2)}) %collective-permute-start.18) | collective-permute-done | bytes 393248 | tf_op jit(solution)/shard_map/z/ppermute | solution.py:24
  41.7 1.6 %collective-permute-start.20 = (bf16[192,512]{1,0:T(8,128)(2,1)S(1)}, bf16[192,512]{1,0:T(8,128)(2,1)S(1)}, u32[]{:S(2)}, u32[]{:S(2)}) collective-permute-start(bf16[192,512]{1,0:T(8,128)(2,1)S(1)} %slice.160), channel_id=1, source_target_pairs={{0,2},{1,3},{2,0},{3,1},{4,6},{5,7},{6,4},{7,5},{8,10},{9,11},{10,... | collective-permute-start | bytes 589832 | tf_op jit(solution)/shard_map/z/ppermute | solution.py:24
  43.3 1.6 %collective-permute-start.21 = (bf16[192,512]{1,0:T(8,128)(2,1)S(1)}, bf16[192,512]{1,0:T(8,128)(2,1)S(1)}, u32[]{:S(2)}, u32[]{:S(2)}) collective-permute-start(bf16[192,512]{1,0:T(8,128)(2,1)S(1)} %slice.161), channel_id=1, source_target_pairs={{0,4},{1,5},{2,6},{3,7},{4,0},{5,1},{6,2},{7,3},{8,12},{9,13},{10,... | collective-permute-start | bytes 589832 | tf_op jit(solution)/shard_map/z/ppermute | solution.py:24
  44.9 4.6 %collective-permute-done.16.refs_7_.refs_15_ = bf16[128,1024]{1,0:T(8,128)(2,1)S(1)} collective-permute-done((bf16[128,1024]{1,0:T(8,128)(2,1)S(1)}, bf16[128,1024]{1,0:T(8,128)(2,1)S(1)}, u32[]{:S(2)}, u32[]{:S(2)}) %collective-permute-start.16) | collective-permute-done | bytes 262176 | tf_op jit(solution)/shard_map/z_ring/ppermute | solution.py:34
  51.1 1.9 %z_matmul.8.refs_6_ = f32[384,1024]{1,0:T(8,128)S(1)} custom-call(s32[2]{0:T(128)S(1)} %pad_add_fusion.place_ref, bf16[384,512]{1,0:T(8,128)(2,1)S(1)} %constant_dynamic-update-slice_fusion.refs_0_.refs_4_, bf16[384,512]{1,0:T(8,128)(2,1)S(1)} %collective-permute-done.15.refs_1_.refs_5_, bf16[384,512]{1,0:T(8,128)(2,1)S(1)} %collective-permute-done.18.refs_2_.refs_6_, ...), custom_call_target="tpu_custom_call" | custom-call | flops 1207959552 | bytes 786432 | tf_op jit(solution)/shard_map/z_far/z_matmul/pallas_call | solution.py:149
  53.2 3.8 %collective-permute-done.22.refs_5_.refs_13_ = bf16[128,1024]{1,0:T(8,128)(2,1)S(1)} collective-permute-done((bf16[128,1024]{1,0:T(8,128)(2,1)S(1)}, bf16[128,1024]{1,0:T(8,128)(2,1)S(1)}, u32[]{:S(2)}, u32[]{:S(2)}) %collective-permute-start.22) | collective-permute-done | bytes 262176 | tf_op jit(solution)/shard_map/z_ring/ppermute | solution.py:34
  57.0 1.2 %collective-permute-start.24 = (bf16[128,512]{1,0:T(8,128)(2,1)S(1)}, bf16[128,512]{1,0:T(8,128)(2,1)S(1)}, u32[]{:S(2)}, u32[]{:S(2)}) collective-permute-start(bf16[128,512]{1,0:T(8,128)(2,1)S(1)} %get-tuple-element.83), channel_id=1, source_target_pairs={{0,16},{16,24},{24,8},{8,0},{1,17},{17,25},{25,9},{9,1},{2,18},{18... | collective-permute-start | bytes 393224 | tf_op jit(solution)/shard_map/kernel/ppermute | solution.py:34
  58.7 2.7 %z_matmul.9 = (bf16[128,1024]{1,0:T(8,128)(2,1)S(1)}, bf16[128,1024]{1,0:T(8,128)(2,1)S(1)}, bf16[128,1024]{1,0:T(8,128)(2,1)S(1)}) custom-call(s32[2]{0:T(128)S(1)} %pad_add_fusion.place_ref, bf16[384,512]{1,0:T(8,128)(2,1)S(1)} %collective-permute-done.13.refs_0_.refs_4_, bf16[384,512]{1,0:T(8,128)(2,1)S(1)} %collective-permute-done.17.refs_1_.refs_5_, ...), custom_call_target="tpu_custom_call" | custom-call | flops 2013265920 | bytes 786432 | tf_op jit(solution)/shard_map/z_far/z_matmul/pallas_call | solution.py:149
  61.5 2.6 %kernel_strip.1 = (f32[4,32,1280]{2,1,0:T(8,128)S(1)}, bf16[4,32,1280]{2,1,0:T(8,128)(2,1)S(1)}) custom-call(s32[2]{0:T(128)S(1)} %pad_add_fusion.place_ref, bf16[128,1024]{1,0:T(8,128)(2,1)S(1)} %get-tuple-element.66.refs_0_.refs_8_, bf16[128,1024]{1,0:T(8,128)(2,1)S(1)} %get-tuple-element.67.refs_1_.refs_9_, ...), custom_call_target="tpu_custom_call" | custom-call | flops 671088640 | bytes 2097152 | tf_op jit(solution)/shard_map/kernel/kernel_strip/pallas_call | solution.py:196
  64.3 1.5 %collective-permute-done.25 = bf16[4,32,1280]{2,1,0:T(8,128)(2,1)S(1)} collective-permute-done((bf16[4,32,1280]{2,1,0:T(8,128)(2,1)S(1)}, bf16[4,32,1280]{2,1,0:T(8,128)(2,1)S(1)}, u32[]{:S(2)}, u32[]{:S(2)}) %collective-permute-start.25) | collective-permute-done | bytes 327712 | tf_op jit(solution)/shard_map/kernel/ppermute | solution.py:24
  65.9 1.3 %collective-permute-start.26 = (bf16[32,1280]{1,0:T(8,128)(2,1)S(1)}, bf16[32,1280]{1,0:T(8,128)(2,1)S(1)}, u32[]{:S(2)}, u32[]{:S(2)}) collective-permute-start(bf16[32,1280]{1,0:T(8,128)(2,1)S(1)} %get-tuple-element.116), channel_id=1, source_target_pairs={{0,2},{1,3},{2,0},{3,1},{4,6},{5,7},{6,4},{7,5},{8,10},{9,11},{10,... | collective-permute-start | bytes 245768 | tf_op jit(solution)/shard_map/kernel/ppermute | solution.py:24
  67.2 1.4 %collective-permute-start.28 = (bf16[32,1280]{1,0:T(8,128)(2,1)S(1)}, bf16[32,1280]{1,0:T(8,128)(2,1)S(1)}, u32[]{:S(2)}, u32[]{:S(2)}) collective-permute-start(bf16[32,1280]{1,0:T(8,128)(2,1)S(1)} %get-tuple-element.117), channel_id=1, source_target_pairs={{0,6},{1,7},{2,4},{3,5},{4,2},{5,3},{6,0},{7,1},{8,14},{9,15},{10,... | collective-permute-start | bytes 245768 | tf_op jit(solution)/shard_map/kernel/ppermute | solution.py:24
  69.5 1.3 %collective-permute-start.31 = (bf16[128,512]{1,0:T(8,128)(2,1)S(1)}, bf16[128,512]{1,0:T(8,128)(2,1)S(1)}, u32[]{:S(2)}, u32[]{:S(2)}) collective-permute-start(bf16[128,512]{1,0:T(8,128)(2,1)S(1)} %get-tuple-element.85), channel_id=1, source_target_pairs={{0,24},{16,8},{24,0},{8,16},{1,25},{17,9},{25,1},{9,17},{2,26},{18... | collective-permute-start | bytes 393224 | tf_op jit(solution)/shard_map/kernel/ppermute | solution.py:34
  71.3 1.7 %collective-permute-done.28 = bf16[32,1280]{1,0:T(8,128)(2,1)S(1)} collective-permute-done((bf16[32,1280]{1,0:T(8,128)(2,1)S(1)}, bf16[32,1280]{1,0:T(8,128)(2,1)S(1)}, u32[]{:S(2)}, u32[]{:S(2)}) %collective-permute-start.28) | collective-permute-done | bytes 81952 | tf_op jit(solution)/shard_map/kernel/ppermute | solution.py:24
  73.0 1.2 %collective-permute-done.27 = bf16[32,1280]{1,0:T(8,128)(2,1)S(1)} collective-permute-done((bf16[32,1280]{1,0:T(8,128)(2,1)S(1)}, bf16[32,1280]{1,0:T(8,128)(2,1)S(1)}, u32[]{:S(2)}, u32[]{:S(2)}) %collective-permute-start.27) | collective-permute-done | bytes 81952 | tf_op jit(solution)/shard_map/kernel/ppermute | solution.py:24
  75.0 1.5 %collective-permute-start.35 = (bf16[32,1280]{1,0:T(8,128)(2,1)S(1)}, bf16[32,1280]{1,0:T(8,128)(2,1)S(1)}, u32[]{:S(2)}, u32[]{:S(2)}) collective-permute-start(bf16[32,1280]{1,0:T(8,128)(2,1)S(1)} %get-tuple-element.110.refs_0_), channel_id=1, source_target_pairs={{0,6},{1,7},{2,4},{3,5},{4,2},{5,3},{6,0},{7,1},{8,14},{9,15},{10,... | collective-permute-start | bytes 245768 | tf_op jit(solution)/shard_map/kernel/ppermute | solution.py:24
  76.5 1.4 %collective-permute-start.33 = (bf16[32,1280]{1,0:T(8,128)(2,1)S(1)}, bf16[32,1280]{1,0:T(8,128)(2,1)S(1)}, u32[]{:S(2)}, u32[]{:S(2)}) collective-permute-start(bf16[32,1280]{1,0:T(8,128)(2,1)S(1)} %get-tuple-element.110.refs_0_), channel_id=1, source_target_pairs={{0,4},{1,5},{2,6},{3,7},{4,0},{5,1},{6,2},{7,3},{8,12},{9,13},{10,... | collective-permute-start | bytes 245768 | tf_op jit(solution)/shard_map/kernel/ppermute | solution.py:24
  77.8 1.6 %collective-permute-done.30.refs_2_ = bf16[32,1280]{1,0:T(8,128)(2,1)S(1)} collective-permute-done((bf16[32,1280]{1,0:T(8,128)(2,1)S(1)}, bf16[32,1280]{1,0:T(8,128)(2,1)S(1)}, u32[]{:S(2)}, u32[]{:S(2)}) %collective-permute-start.30) | collective-permute-done | bytes 81952 | tf_op jit(solution)/shard_map/kernel/ppermute | solution.py:24
  79.4 1.2 %collective-permute-done.35.refs_6_ = bf16[32,1280]{1,0:T(8,128)(2,1)S(1)} collective-permute-done((bf16[32,1280]{1,0:T(8,128)(2,1)S(1)}, bf16[32,1280]{1,0:T(8,128)(2,1)S(1)}, u32[]{:S(2)}, u32[]{:S(2)}) %collective-permute-start.35) | collective-permute-done | bytes 81952 | tf_op jit(solution)/shard_map/kernel/ppermute | solution.py:24
  82.9 4.7 %embedding_gradient.1 = (bf16[2,512,1024]{2,1,0:T(8,128)(2,1)S(1)}, f32[8,128]{1,0:T(8,128)S(1)}) custom-call(s32[2]{0:T(128)S(1)} %pad_add_fusion.place_ref, f32[32,1280]{1,0:T(8,128)S(1)} %get-tuple-element.111.own_ref, bf16[32,1280]{1,0:T(8,128)(2,1)S(1)} %get-tuple-element.110.refs_0_, bf16[32,1280]{1,0:T(8,128)(2,1)S(1)} %collective-permute-done.29.refs_1_, ...), custom_call_target="tpu_custom_call" | custom-call | flops 1073741824 | bytes 4194304 | tf_op jit(solution)/shard_map/dz/embedding_gradient/pallas_call | solution.py:271
  88.2 1.0 d_act_matmul.3
  89.3 1.5 %collective-permute-done.38.refs_0_ = bf16[1,272,512]{2,1,0:T(8,128)(2,1)S(1)} collective-permute-done((bf16[1,272,512]{2,1,0:T(8,128)(2,1)S(1)}, bf16[1,272,512]{2,1,0:T(8,128)(2,1)S(1)}, u32[]{:S(2)}, u32[]{:S(2)}) %collective-permute-start.38) | collective-permute-done | bytes 278560 | tf_op jit(solution)/shard_map/d_act/ppermute | solution.py:24
  90.9 1.8 %d_act_matmul.4 = (bf16[272,512]{1,0:T(8,128)(2,1)S(1)}, bf16[3,272,512]{2,1,0:T(8,128)(2,1)S(1)}) custom-call(s32[2]{0:T(128)S(1)} %pad_add_fusion.place_ref, bf16[2,512,1024]{2,1,0:T(8,128)(2,1)S(1)} %get-tuple-element.89.dz_ref.refs_9_, f32[8,128]{1,0:T(8,128)S(1)} %get-tuple-element.90.share_ref, ...), custom_call_target="tpu_custom_call" | custom-call | flops 1073741824 | bytes 1048576 | tf_op jit(solution)/shard_map/d_act/d_act_matmul/pallas_call | solution.py:338
  93.4 1.3 %collective-permute-start.42 = (bf16[272,512]{1,0:T(8,128)(2,1)S(1)}, bf16[272,512]{1,0:T(8,128)(2,1)S(1)}, u32[]{:S(2)}, u32[]{:S(2)}) collective-permute-start(bf16[272,512]{1,0:T(8,128)(2,1)S(1)} %get-tuple-element.95), channel_id=1, source_target_pairs={{0,6},{1,7},{2,4},{3,5},{4,2},{5,3},{6,0},{7,1},{8,14},{9,15},{10,... | collective-permute-start | bytes 835592 | tf_op jit(solution)/shard_map/d_act/ppermute | solution.py:24
  95.2 1.6 %d_act_matmul.5 = (bf16[272,512]{1,0:T(8,128)(2,1)S(1)}, bf16[272,512]{1,0:T(8,128)(2,1)S(1)}, f32[272,512]{1,0:T(8,128)S(1)}) custom-call(s32[2]{0:T(128)S(1)} %pad_add_fusion.place_ref, bf16[2,512,1024]{2,1,0:T(8,128)(2,1)S(1)} %get-tuple-element.89.dz_ref.refs_9_, f32[8,128]{1,0:T(8,128)S(1)} %get-tuple-element.90.share_ref, ...), custom_call_target="tpu_custom_call" | custom-call | flops 805306368 | bytes 786432 | tf_op jit(solution)/shard_map/d_act/d_act_matmul/pallas_call | solution.py:338
  96.7 1.3 %collective-permute-start.40 = (bf16[272,512]{1,0:T(8,128)(2,1)S(1)}, bf16[272,512]{1,0:T(8,128)(2,1)S(1)}, u32[]{:S(2)}, u32[]{:S(2)}) collective-permute-start(bf16[272,512]{1,0:T(8,128)(2,1)S(1)} %get-tuple-element.93), channel_id=1, source_target_pairs={{0,2},{1,3},{2,0},{3,1},{4,6},{5,7},{6,4},{7,5},{8,10},{9,11},{10,... | collective-permute-start | bytes 835592 | tf_op jit(solution)/shard_map/d_act/ppermute | solution.py:24
  98.7 2.9 %weight_gradient.2.refs_10_ = f32[1024,1024]{1,0:T(8,128)} custom-call(s32[2]{0:T(128)S(1)} %pad_add_fusion.place_ref, bf16[256,512]{1,0:T(8,128)(2,1)S(1)} %bitcast.34, bf16[256,512]{1,0:T(8,128)(2,1)S(1)} %collective-permute-done.3.refs_0_.refs_1_, bf16[256,512]{1,0:T(8,128)(2,1)S(1)} %collective-permute-done.5.refs_1_.refs_2_, ...), custom_call_target="tpu_custom_call" | custom-call | flops 1073741824 | bytes 2097152 | tf_op jit(solution)/shard_map/grad_weight/weight_gradient/pallas_call | solution.py:443
  101.6 2.9 %weight_gradient.3 = f32[1024,1024]{1,0:T(8,128)} custom-call(s32[2]{0:T(128)S(1)} %pad_add_fusion.place_ref, bf16[256,512]{1,0:T(8,128)(2,1)S(1)} %collective-permute-done.9.refs_1_.refs_0_, bf16[256,512]{1,0:T(8,128)(2,1)S(1)} %collective-permute-done.4.refs_0_.refs_1_, ...), custom_call_target="tpu_custom_call", output_to_operand_aliasing={{}: (11, {})} | custom-call | flops 1073741824 | bytes 2097152 | tf_op jit(solution)/shard_map/grad_weight/weight_gradient/pallas_call | solution.py:443
  104.5 4.3 %collective-permute-done.40 = bf16[272,512]{1,0:T(8,128)(2,1)S(1)} collective-permute-done((bf16[272,512]{1,0:T(8,128)(2,1)S(1)}, bf16[272,512]{1,0:T(8,128)(2,1)S(1)}, u32[]{:S(2)}, u32[]{:S(2)}) %collective-permute-start.40) | collective-permute-done | bytes 278560 | tf_op jit(solution)/shard_map/d_act/ppermute | solution.py:24
  109.7 1.5 %collective-permute-start.46 = (f32[8,512]{1,0:T(8,128)S(1)}, f32[8,512]{1,0:T(8,128)S(1)}, u32[]{:S(2)}, u32[]{:S(2)}) collective-permute-start(f32[8,512]{1,0:T(8,128)S(1)} %pad_maximum_fusion.1.refs_0_), channel_id=1, source_target_pairs={{0,24},{8,16},{16,8},{24,0},{1,25},{9,17},{17,9},{25,1},{2,26},{10... | collective-permute-start | bytes 49160 | tf_op jit(solution)/shard_map/norm_backward/ppermute | solution.py:24
  111.7 2.4 %collective-permute-start.44 = (f32[8,512]{1,0:T(8,128)S(1)}, f32[8,512]{1,0:T(8,128)S(1)}, u32[]{:S(2)}, u32[]{:S(2)}) collective-permute-start(f32[8,512]{1,0:T(8,128)S(1)} %pad_maximum_fusion.1.refs_0_), channel_id=1, source_target_pairs={{0,8},{8,0},{16,24},{24,16},{1,9},{9,1},{17,25},{25,17},{2,10},{10... | collective-permute-start | bytes 49160 | tf_op jit(solution)/shard_map/norm_backward/ppermute | solution.py:24
  114.1 1.1 collective-permute-done.46.refs_3_
  (91 shorter events, 15.8 us)
Async XLA Ops:
  1.8 9.7 %copy-start.1 = (bf16[2,128,512]{2,1,0:T(8,128)(2,1)S(1)}, bf16[2,128,512]{2,1,0:T(8,128)(2,1)}, u32[]{:S(2)}) copy-start(bf16[2,128,512]{2,1,0:T(8,128)(2,1)} %views_ref) | copy-start | bytes 786436
  1.8 9.2 %collective-permute-start.2 = (f32[4,512]{1,0:T(4,128)S(1)}, f32[4,512]{1,0:T(4,128)S(1)}, u32[]{:S(2)}, u32[]{:S(2)}) collective-permute-start(f32[4,512]{1,0:T(4,128)S(1)} %norm_statistics.1), channel_id=1, source_target_pairs={{0,24},{8,16},{16,8},{24,0},{1,25},{9,17},{17,9},{25,1},{2,26},{10... | collective-permute-start | bytes 24584 | tf_op jit(solution)/shard_map/norm_stats/ppermute | solution.py:24
  6.9 4.5 %collective-permute-start.1 = (f32[4,512]{1,0:T(4,128)S(1)}, f32[4,512]{1,0:T(4,128)S(1)}, u32[]{:S(2)}, u32[]{:S(2)}) collective-permute-start(f32[4,512]{1,0:T(4,128)S(1)} %norm_statistics.1), channel_id=1, source_target_pairs={{0,16},{8,24},{16,0},{24,8},{1,17},{9,25},{17,1},{25,9},{2,18},{10... | collective-permute-start | bytes 24584 | tf_op jit(solution)/shard_map/norm_stats/ppermute | solution.py:24
  7.0 4.5 %collective-permute-start = (f32[4,512]{1,0:T(4,128)S(1)}, f32[4,512]{1,0:T(4,128)S(1)}, u32[]{:S(2)}, u32[]{:S(2)}) collective-permute-start(f32[4,512]{1,0:T(4,128)S(1)} %norm_statistics.1), channel_id=1, source_target_pairs={{0,8},{8,0},{16,24},{24,16},{1,9},{9,1},{17,25},{25,17},{2,10},{10... | collective-permute-start | bytes 24584 | tf_op jit(solution)/shard_map/norm_stats/ppermute | solution.py:24
  11.8 3.6 %collective-permute-start.9 = (bf16[256,512]{1,0:T(8,128)(2,1)S(1)}, bf16[256,512]{1,0:T(8,128)(2,1)S(1)}, u32[]{:S(2)}, u32[]{:S(2)}) collective-permute-start(bf16[256,512]{1,0:T(8,128)(2,1)S(1)} %bitcast.28), channel_id=1, source_target_pairs={{0,1},{1,0},{2,3},{3,2},{4,5},{5,4},{6,7},{7,6},{8,9},{9,8},{10,11... | collective-permute-start | bytes 786440 | tf_op jit(solution)/shard_map/act_gather/ppermute | solution.py:24
  11.9 10.1 %collective-permute-start.7 = (bf16[256,512]{1,0:T(8,128)(2,1)S(1)}, bf16[256,512]{1,0:T(8,128)(2,1)S(1)}, u32[]{:S(2)}, u32[]{:S(2)}) collective-permute-start(bf16[256,512]{1,0:T(8,128)(2,1)S(1)} %bitcast.29), channel_id=1, source_target_pairs={{0,6},{1,7},{2,4},{3,5},{4,2},{5,3},{6,0},{7,1},{8,14},{9,15},{10,... | collective-permute-start | bytes 786440 | tf_op jit(solution)/shard_map/act_gather/ppermute | solution.py:24
  14.4 12.7 %collective-permute-start.5 = (bf16[256,512]{1,0:T(8,128)(2,1)S(1)}, bf16[256,512]{1,0:T(8,128)(2,1)S(1)}, u32[]{:S(2)}, u32[]{:S(2)}) collective-permute-start(bf16[256,512]{1,0:T(8,128)(2,1)S(1)} %bitcast.30), channel_id=1, source_target_pairs={{0,4},{1,5},{2,6},{3,7},{4,0},{5,1},{6,2},{7,3},{8,12},{9,13},{10,... | collective-permute-start | bytes 786440 | tf_op jit(solution)/shard_map/act_gather/ppermute | solution.py:24
  14.9 12.3 %collective-permute-start.3 = (bf16[256,512]{1,0:T(8,128)(2,1)S(1)}, bf16[256,512]{1,0:T(8,128)(2,1)S(1)}, u32[]{:S(2)}, u32[]{:S(2)}) collective-permute-start(bf16[256,512]{1,0:T(8,128)(2,1)S(1)} %bitcast.31), channel_id=1, source_target_pairs={{0,2},{1,3},{2,0},{3,1},{4,6},{5,7},{6,4},{7,5},{8,10},{9,11},{10,... | collective-permute-start | bytes 786440 | tf_op jit(solution)/shard_map/act_gather/ppermute | solution.py:24
  15.5 13.7 %collective-permute-start.11 = (bf16[128,512]{1,0:T(8,128)(2,1)S(1)}, bf16[128,512]{1,0:T(8,128)(2,1)S(1)}, u32[]{:S(2)}, u32[]{:S(2)}) collective-permute-start(bf16[128,512]{1,0:T(8,128)(2,1)S(1)} %slice_bitcast_fusion.1), channel_id=1, source_target_pairs={{0,16},{16,24},{24,8},{8,0},{1,17},{17,25},{25,9},{9,1},{2,18},{18... | collective-permute-start | bytes 393224 | tf_op jit(solution)/shard_map/act_gather/ppermute | solution.py:34
  17.6 11.8 %collective-permute-start.12 = (bf16[128,512]{1,0:T(8,128)(2,1)S(1)}, bf16[128,512]{1,0:T(8,128)(2,1)S(1)}, u32[]{:S(2)}, u32[]{:S(2)}) collective-permute-start(bf16[128,512]{1,0:T(8,128)(2,1)S(1)} %slice_bitcast_fusion.1), channel_id=1, source_target_pairs={{0,24},{16,8},{24,0},{8,16},{1,25},{17,9},{25,1},{9,17},{2,26},{18... | collective-permute-start | bytes 393224 | tf_op jit(solution)/shard_map/act_gather/ppermute | solution.py:34
  22.0 8.6 %collective-permute-start.10 = (bf16[128,512]{1,0:T(8,128)(2,1)S(1)}, bf16[128,512]{1,0:T(8,128)(2,1)S(1)}, u32[]{:S(2)}, u32[]{:S(2)}) collective-permute-start(bf16[128,512]{1,0:T(8,128)(2,1)S(1)} %slice_bitcast_fusion.1), channel_id=1, source_target_pairs={{0,8},{16,0},{24,16},{8,24},{1,9},{17,1},{25,17},{9,25},{2,10},{18... | collective-permute-start | bytes 393224 | tf_op jit(solution)/shard_map/act_gather/ppermute | solution.py:34
  27.1 6.5 %collective-permute-start.8 = (bf16[256,512]{1,0:T(8,128)(2,1)S(1)}, bf16[256,512]{1,0:T(8,128)(2,1)S(1)}, u32[]{:S(2)}, u32[]{:S(2)}) collective-permute-start(bf16[256,512]{1,0:T(8,128)(2,1)S(1)} %collective-permute-done.7.refs_2_.refs_3_), channel_id=1, source_target_pairs={{0,1},{1,0},{2,3},{3,2},{4,5},{5,4},{6,7},{7,6},{8,9},{9,8},{10,11... | collective-permute-start | bytes 786440 | tf_op jit(solution)/shard_map/act_gather/ppermute | solution.py:24
  27.2 6.4 %collective-permute-start.6 = (bf16[256,512]{1,0:T(8,128)(2,1)S(1)}, bf16[256,512]{1,0:T(8,128)(2,1)S(1)}, u32[]{:S(2)}, u32[]{:S(2)}) collective-permute-start(bf16[256,512]{1,0:T(8,128)(2,1)S(1)} %collective-permute-done.5.refs_1_.refs_2_), channel_id=1, source_target_pairs={{0,1},{1,0},{2,3},{3,2},{4,5},{5,4},{6,7},{7,6},{8,9},{9,8},{10,11... | collective-permute-start | bytes 786440 | tf_op jit(solution)/shard_map/act_gather/ppermute | solution.py:24
  29.2 4.5 %collective-permute-start.4 = (bf16[256,512]{1,0:T(8,128)(2,1)S(1)}, bf16[256,512]{1,0:T(8,128)(2,1)S(1)}, u32[]{:S(2)}, u32[]{:S(2)}) collective-permute-start(bf16[256,512]{1,0:T(8,128)(2,1)S(1)} %collective-permute-done.3.refs_0_.refs_1_), channel_id=1, source_target_pairs={{0,1},{1,0},{2,3},{3,2},{4,5},{5,4},{6,7},{7,6},{8,9},{9,8},{10,11... | collective-permute-start | bytes 786440 | tf_op jit(solution)/shard_map/act_gather/ppermute | solution.py:24
  30.6 11.1 %collective-permute-start.18 = (bf16[384,512]{1,0:T(8,128)(2,1)S(1)}, bf16[384,512]{1,0:T(8,128)(2,1)S(1)}, u32[]{:S(2)}, u32[]{:S(2)}) collective-permute-start(bf16[384,512]{1,0:T(8,128)(2,1)S(1)} %constant_dynamic-update-slice_fusion.refs_0_.refs_4_), channel_id=1, source_target_pairs={{0,4},{1,5},{2,6},{3,7},{4,0},{5,1},{6,2},{7,3},{8,12},{9,13},{10,... | collective-permute-start | bytes 1179656 | tf_op jit(solution)/shard_map/z/ppermute | solution.py:24
  32.2 11.1 %collective-permute-start.15 = (bf16[384,512]{1,0:T(8,128)(2,1)S(1)}, bf16[384,512]{1,0:T(8,128)(2,1)S(1)}, u32[]{:S(2)}, u32[]{:S(2)}) collective-permute-start(bf16[384,512]{1,0:T(8,128)(2,1)S(1)} %constant_dynamic-update-slice_fusion.refs_0_.refs_4_), channel_id=1, source_target_pairs={{0,2},{1,3},{2,0},{3,1},{4,6},{5,7},{6,4},{7,5},{8,10},{9,11},{10,... | collective-permute-start | bytes 1179656 | tf_op jit(solution)/shard_map/z/ppermute | solution.py:24
  35.2 14.3 %collective-permute-start.16 = (bf16[128,1024]{1,0:T(8,128)(2,1)S(1)}, bf16[128,1024]{1,0:T(8,128)(2,1)S(1)}, u32[]{:S(2)}, u32[]{:S(2)}) collective-permute-start(bf16[128,1024]{1,0:T(8,128)(2,1)S(1)} %get-tuple-element.67.refs_1_.refs_9_), channel_id=1, source_target_pairs={{0,8},{16,0},{24,16},{8,24},{1,9},{17,1},{25,17},{9,25},{2,10},{18... | collective-permute-start | bytes 786440 | tf_op jit(solution)/shard_map/z_ring/ppermute | solution.py:34
  35.3 14.2 %collective-permute-start.14 = (bf16[128,1024]{1,0:T(8,128)(2,1)S(1)}, bf16[128,1024]{1,0:T(8,128)(2,1)S(1)}, u32[]{:S(2)}, u32[]{:S(2)}) collective-permute-start(bf16[128,1024]{1,0:T(8,128)(2,1)S(1)} %get-tuple-element.67.refs_1_.refs_9_), channel_id=1, source_target_pairs={{0,16},{16,24},{24,8},{8,0},{1,17},{17,25},{25,9},{9,1},{2,18},{18... | collective-permute-start | bytes 786440 | tf_op jit(solution)/shard_map/z_ring/ppermute | solution.py:34
  41.7 11.3 %collective-permute-start.20 = (bf16[192,512]{1,0:T(8,128)(2,1)S(1)}, bf16[192,512]{1,0:T(8,128)(2,1)S(1)}, u32[]{:S(2)}, u32[]{:S(2)}) collective-permute-start(bf16[192,512]{1,0:T(8,128)(2,1)S(1)} %slice.160), channel_id=1, source_target_pairs={{0,2},{1,3},{2,0},{3,1},{4,6},{5,7},{6,4},{7,5},{8,10},{9,11},{10,... | collective-permute-start | bytes 589832 | tf_op jit(solution)/shard_map/z/ppermute | solution.py:24
  43.3 9.9 %collective-permute-start.21 = (bf16[192,512]{1,0:T(8,128)(2,1)S(1)}, bf16[192,512]{1,0:T(8,128)(2,1)S(1)}, u32[]{:S(2)}, u32[]{:S(2)}) collective-permute-start(bf16[192,512]{1,0:T(8,128)(2,1)S(1)} %slice.161), channel_id=1, source_target_pairs={{0,4},{1,5},{2,6},{3,7},{4,0},{5,1},{6,2},{7,3},{8,12},{9,13},{10,... | collective-permute-start | bytes 589832 | tf_op jit(solution)/shard_map/z/ppermute | solution.py:24
  49.5 7.5 %collective-permute-start.22 = (bf16[128,1024]{1,0:T(8,128)(2,1)S(1)}, bf16[128,1024]{1,0:T(8,128)(2,1)S(1)}, u32[]{:S(2)}, u32[]{:S(2)}) collective-permute-start(bf16[128,1024]{1,0:T(8,128)(2,1)S(1)} %collective-permute-done.14.refs_3_.refs_11_), channel_id=1, source_target_pairs={{0,16},{16,24},{24,8},{8,0},{1,17},{17,25},{25,9},{9,1},{2,18},{18... | collective-permute-start | bytes 786440 | tf_op jit(solution)/shard_map/z_ring/ppermute | solution.py:34
  50.5 7.7 %collective-permute-start.13 = (bf16[384,512]{1,0:T(8,128)(2,1)S(1)}, bf16[384,512]{1,0:T(8,128)(2,1)S(1)}, u32[]{:S(2)}, u32[]{:S(2)}) collective-permute-start(bf16[384,512]{1,0:T(8,128)(2,1)S(1)} %constant_dynamic-update-slice_fusion.refs_0_.refs_4_), channel_id=1, source_target_pairs={{0,1},{1,0},{2,3},{3,2},{4,5},{5,4},{6,7},{7,6},{8,9},{9,8},{10,11... | collective-permute-start | bytes 1179656 | tf_op jit(solution)/shard_map/z_far/ppermute | solution.py:24
  50.6 7.6 %collective-permute-start.17 = (bf16[384,512]{1,0:T(8,128)(2,1)S(1)}, bf16[384,512]{1,0:T(8,128)(2,1)S(1)}, u32[]{:S(2)}, u32[]{:S(2)}) collective-permute-start(bf16[384,512]{1,0:T(8,128)(2,1)S(1)} %collective-permute-done.15.refs_1_.refs_5_), channel_id=1, source_target_pairs={{0,1},{1,0},{2,3},{3,2},{4,5},{5,4},{6,7},{7,6},{8,9},{9,8},{10,11... | collective-permute-start | bytes 1179656 | tf_op jit(solution)/shard_map/z_far/ppermute | solution.py:24
  53.0 5.2 %collective-permute-start.19 = (bf16[384,512]{1,0:T(8,128)(2,1)S(1)}, bf16[384,512]{1,0:T(8,128)(2,1)S(1)}, u32[]{:S(2)}, u32[]{:S(2)}) collective-permute-start(bf16[384,512]{1,0:T(8,128)(2,1)S(1)} %collective-permute-done.18.refs_2_.refs_6_), channel_id=1, source_target_pairs={{0,1},{1,0},{2,3},{3,2},{4,5},{5,4},{6,7},{7,6},{8,9},{9,8},{10,11... | collective-permute-start | bytes 1179656 | tf_op jit(solution)/shard_map/z_far/ppermute | solution.py:24
  57.0 1.7 %collective-permute-start.23 = (bf16[384,512]{1,0:T(8,128)(2,1)S(1)}, bf16[384,512]{1,0:T(8,128)(2,1)S(1)}, u32[]{:S(2)}, u32[]{:S(2)}) collective-permute-start(bf16[384,512]{1,0:T(8,128)(2,1)S(1)} %pad_maximum_fusion.refs_3_.refs_7_), channel_id=1, source_target_pairs={{0,1},{1,0},{2,3},{3,2},{4,5},{5,4},{6,7},{7,6},{8,9},{9,8},{10,11... | collective-permute-start | bytes 1179656 | tf_op jit(solution)/shard_map/z_far/ppermute | solution.py:24
  57.0 7.1 %collective-permute-start.24 = (bf16[128,512]{1,0:T(8,128)(2,1)S(1)}, bf16[128,512]{1,0:T(8,128)(2,1)S(1)}, u32[]{:S(2)}, u32[]{:S(2)}) collective-permute-start(bf16[128,512]{1,0:T(8,128)(2,1)S(1)} %get-tuple-element.83), channel_id=1, source_target_pairs={{0,16},{16,24},{24,8},{8,0},{1,17},{17,25},{25,9},{9,1},{2,18},{18... | collective-permute-start | bytes 393224 | tf_op jit(solution)/shard_map/kernel/ppermute | solution.py:34
  64.1 1.7 %collective-permute-start.25 = (bf16[4,32,1280]{2,1,0:T(8,128)(2,1)S(1)}, bf16[4,32,1280]{2,1,0:T(8,128)(2,1)S(1)}, u32[]{:S(2)}, u32[]{:S(2)}) collective-permute-start(bf16[4,32,1280]{2,1,0:T(8,128)(2,1)S(1)} %get-tuple-element.84), channel_id=1, source_target_pairs={{0,1},{1,0},{2,3},{3,2},{4,5},{5,4},{6,7},{7,6},{8,9},{9,8},{10,11... | collective-permute-start | bytes 983048 | tf_op jit(solution)/shard_map/kernel/ppermute | solution.py:24
  65.9 5.4 %collective-permute-start.26 = (bf16[32,1280]{1,0:T(8,128)(2,1)S(1)}, bf16[32,1280]{1,0:T(8,128)(2,1)S(1)}, u32[]{:S(2)}, u32[]{:S(2)}) collective-permute-start(bf16[32,1280]{1,0:T(8,128)(2,1)S(1)} %get-tuple-element.116), channel_id=1, source_target_pairs={{0,2},{1,3},{2,0},{3,1},{4,6},{5,7},{6,4},{7,5},{8,10},{9,11},{10,... | collective-permute-start | bytes 245768 | tf_op jit(solution)/shard_map/kernel/ppermute | solution.py:24
  67.2 5.8 %collective-permute-start.28 = (bf16[32,1280]{1,0:T(8,128)(2,1)S(1)}, bf16[32,1280]{1,0:T(8,128)(2,1)S(1)}, u32[]{:S(2)}, u32[]{:S(2)}) collective-permute-start(bf16[32,1280]{1,0:T(8,128)(2,1)S(1)} %get-tuple-element.117), channel_id=1, source_target_pairs={{0,6},{1,7},{2,4},{3,5},{4,2},{5,3},{6,0},{7,1},{8,14},{9,15},{10,... | collective-permute-start | bytes 245768 | tf_op jit(solution)/shard_map/kernel/ppermute | solution.py:24
  68.7 5.6 %collective-permute-start.27 = (bf16[32,1280]{1,0:T(8,128)(2,1)S(1)}, bf16[32,1280]{1,0:T(8,128)(2,1)S(1)}, u32[]{:S(2)}, u32[]{:S(2)}) collective-permute-start(bf16[32,1280]{1,0:T(8,128)(2,1)S(1)} %get-tuple-element.118), channel_id=1, source_target_pairs={{0,4},{1,5},{2,6},{3,7},{4,0},{5,1},{6,2},{7,3},{8,12},{9,13},{10,... | collective-permute-start | bytes 245768 | tf_op jit(solution)/shard_map/kernel/ppermute | solution.py:24
  69.5 8.4 %collective-permute-start.31 = (bf16[128,512]{1,0:T(8,128)(2,1)S(1)}, bf16[128,512]{1,0:T(8,128)(2,1)S(1)}, u32[]{:S(2)}, u32[]{:S(2)}) collective-permute-start(bf16[128,512]{1,0:T(8,128)(2,1)S(1)} %get-tuple-element.85), channel_id=1, source_target_pairs={{0,24},{16,8},{24,0},{8,16},{1,25},{17,9},{25,1},{9,17},{2,26},{18... | collective-permute-start | bytes 393224 | tf_op jit(solution)/shard_map/kernel/ppermute | solution.py:34
  74.3 5.1 %collective-permute-start.30 = (bf16[32,1280]{1,0:T(8,128)(2,1)S(1)}, bf16[32,1280]{1,0:T(8,128)(2,1)S(1)}, u32[]{:S(2)}, u32[]{:S(2)}) collective-permute-start(bf16[32,1280]{1,0:T(8,128)(2,1)S(1)} %get-tuple-element.110.refs_0_), channel_id=1, source_target_pairs={{0,2},{1,3},{2,0},{3,1},{4,6},{5,7},{6,4},{7,5},{8,10},{9,11},{10,... | collective-permute-start | bytes 245768 | tf_op jit(solution)/shard_map/kernel/ppermute | solution.py:24
  75.0 5.6 %collective-permute-start.35 = (bf16[32,1280]{1,0:T(8,128)(2,1)S(1)}, bf16[32,1280]{1,0:T(8,128)(2,1)S(1)}, u32[]{:S(2)}, u32[]{:S(2)}) collective-permute-start(bf16[32,1280]{1,0:T(8,128)(2,1)S(1)} %get-tuple-element.110.refs_0_), channel_id=1, source_target_pairs={{0,6},{1,7},{2,4},{3,5},{4,2},{5,3},{6,0},{7,1},{8,14},{9,15},{10,... | collective-permute-start | bytes 245768 | tf_op jit(solution)/shard_map/kernel/ppermute | solution.py:24
  76.5 4.9 %collective-permute-start.33 = (bf16[32,1280]{1,0:T(8,128)(2,1)S(1)}, bf16[32,1280]{1,0:T(8,128)(2,1)S(1)}, u32[]{:S(2)}, u32[]{:S(2)}) collective-permute-start(bf16[32,1280]{1,0:T(8,128)(2,1)S(1)} %get-tuple-element.110.refs_0_), channel_id=1, source_target_pairs={{0,4},{1,5},{2,6},{3,7},{4,0},{5,1},{6,2},{7,3},{8,12},{9,13},{10,... | collective-permute-start | bytes 245768 | tf_op jit(solution)/shard_map/kernel/ppermute | solution.py:24
  77.8 4.7 %collective-permute-start.29 = (bf16[32,1280]{1,0:T(8,128)(2,1)S(1)}, bf16[32,1280]{1,0:T(8,128)(2,1)S(1)}, u32[]{:S(2)}, u32[]{:S(2)}) collective-permute-start(bf16[32,1280]{1,0:T(8,128)(2,1)S(1)} %get-tuple-element.110.refs_0_), channel_id=1, source_target_pairs={{0,1},{1,0},{2,3},{3,2},{4,5},{5,4},{6,7},{7,6},{8,9},{9,8},{10,11... | collective-permute-start | bytes 245768 | tf_op jit(solution)/shard_map/kernel/ppermute | solution.py:24
  80.6 2.0 %collective-permute-start.36 = (bf16[32,1280]{1,0:T(8,128)(2,1)S(1)}, bf16[32,1280]{1,0:T(8,128)(2,1)S(1)}, u32[]{:S(2)}, u32[]{:S(2)}) collective-permute-start(bf16[32,1280]{1,0:T(8,128)(2,1)S(1)} %collective-permute-done.35.refs_6_), channel_id=1, source_target_pairs={{0,1},{1,0},{2,3},{3,2},{4,5},{5,4},{6,7},{7,6},{8,9},{9,8},{10,11... | collective-permute-start | bytes 245768 | tf_op jit(solution)/shard_map/kernel/ppermute | solution.py:24
  81.4 1.3 %collective-permute-start.34 = (bf16[32,1280]{1,0:T(8,128)(2,1)S(1)}, bf16[32,1280]{1,0:T(8,128)(2,1)S(1)}, u32[]{:S(2)}, u32[]{:S(2)}) collective-permute-start(bf16[32,1280]{1,0:T(8,128)(2,1)S(1)} %collective-permute-done.33.refs_4_), channel_id=1, source_target_pairs={{0,1},{1,0},{2,3},{3,2},{4,5},{5,4},{6,7},{7,6},{8,9},{9,8},{10,11... | collective-permute-start | bytes 245768 | tf_op jit(solution)/shard_map/kernel/ppermute | solution.py:24
  81.4 1.4 %collective-permute-start.32 = (bf16[32,1280]{1,0:T(8,128)(2,1)S(1)}, bf16[32,1280]{1,0:T(8,128)(2,1)S(1)}, u32[]{:S(2)}, u32[]{:S(2)}) collective-permute-start(bf16[32,1280]{1,0:T(8,128)(2,1)S(1)} %collective-permute-done.30.refs_2_), channel_id=1, source_target_pairs={{0,1},{1,0},{2,3},{3,2},{4,5},{5,4},{6,7},{7,6},{8,9},{9,8},{10,11... | collective-permute-start | bytes 245768 | tf_op jit(solution)/shard_map/kernel/ppermute | solution.py:24
  81.9 6.3 %collective-permute-start.37 = (bf16[128,512]{1,0:T(8,128)(2,1)S(1)}, bf16[128,512]{1,0:T(8,128)(2,1)S(1)}, u32[]{:S(2)}, u32[]{:S(2)}) collective-permute-start(bf16[128,512]{1,0:T(8,128)(2,1)S(1)} %get-tuple-element.88), channel_id=1, source_target_pairs={{0,8},{16,0},{24,16},{8,24},{1,9},{17,1},{25,17},{9,25},{2,10},{18... | collective-permute-start | bytes 393224 | tf_op jit(solution)/shard_map/kernel/ppermute | solution.py:34
  89.3 1.6 %collective-permute-start.38 = (bf16[1,272,512]{2,1,0:T(8,128)(2,1)S(1)}, bf16[1,272,512]{2,1,0:T(8,128)(2,1)S(1)}, u32[]{:S(2)}, u32[]{:S(2)}) collective-permute-start(bf16[1,272,512]{2,1,0:T(8,128)(2,1)S(1)} %d_act_matmul.3), channel_id=1, source_target_pairs={{0,1},{1,0},{2,3},{3,2},{4,5},{5,4},{6,7},{7,6},{8,9},{9,8},{10,11... | collective-permute-start | bytes 835592 | tf_op jit(solution)/shard_map/d_act/ppermute | solution.py:24
  92.7 2.4 %collective-permute-start.39 = (bf16[3,272,512]{2,1,0:T(8,128)(2,1)S(1)}, bf16[3,272,512]{2,1,0:T(8,128)(2,1)S(1)}, u32[]{:S(2)}, u32[]{:S(2)}) collective-permute-start(bf16[3,272,512]{2,1,0:T(8,128)(2,1)S(1)} %get-tuple-element.91), channel_id=1, source_target_pairs={{0,1},{1,0},{2,3},{3,2},{4,5},{5,4},{6,7},{7,6},{8,9},{9,8},{10,11... | collective-permute-start | bytes 2506760 | tf_op jit(solution)/shard_map/d_act/ppermute | solution.py:24
  93.0 8.6 %collective-permute-start.43 = (bf16[384,512]{1,0:T(8,128)(2,1)S(1)}, bf16[384,512]{1,0:T(8,128)(2,1)S(1)}, u32[]{:S(2)}, u32[]{:S(2)}) collective-permute-start(bf16[384,512]{1,0:T(8,128)(2,1)S(1)} %constant_dynamic-update-slice_fusion.3.refs_8_), channel_id=1, source_target_pairs={{0,1},{1,0},{2,3},{3,2},{4,5},{5,4},{6,7},{7,6},{8,9},{9,8},{10,11... | collective-permute-start | bytes 1179656 | tf_op jit(solution)/shard_map/grad_weight/ppermute | solution.py:24
  93.4 11.1 %collective-permute-start.42 = (bf16[272,512]{1,0:T(8,128)(2,1)S(1)}, bf16[272,512]{1,0:T(8,128)(2,1)S(1)}, u32[]{:S(2)}, u32[]{:S(2)}) collective-permute-start(bf16[272,512]{1,0:T(8,128)(2,1)S(1)} %get-tuple-element.95), channel_id=1, source_target_pairs={{0,6},{1,7},{2,4},{3,5},{4,2},{5,3},{6,0},{7,1},{8,14},{9,15},{10,... | collective-permute-start | bytes 835592 | tf_op jit(solution)/shard_map/d_act/ppermute | solution.py:24
  96.7 12.1 %collective-permute-start.40 = (bf16[272,512]{1,0:T(8,128)(2,1)S(1)}, bf16[272,512]{1,0:T(8,128)(2,1)S(1)}, u32[]{:S(2)}, u32[]{:S(2)}) collective-permute-start(bf16[272,512]{1,0:T(8,128)(2,1)S(1)} %get-tuple-element.93), channel_id=1, source_target_pairs={{0,2},{1,3},{2,0},{3,1},{4,6},{5,7},{6,4},{7,5},{8,10},{9,11},{10,... | collective-permute-start | bytes 835592 | tf_op jit(solution)/shard_map/d_act/ppermute | solution.py:24
  98.0 11.0 %collective-permute-start.41 = (bf16[272,512]{1,0:T(8,128)(2,1)S(1)}, bf16[272,512]{1,0:T(8,128)(2,1)S(1)}, u32[]{:S(2)}, u32[]{:S(2)}) collective-permute-start(bf16[272,512]{1,0:T(8,128)(2,1)S(1)} %get-tuple-element.94), channel_id=1, source_target_pairs={{0,4},{1,5},{2,6},{3,7},{4,0},{5,1},{6,2},{7,3},{8,12},{9,13},{10,... | collective-permute-start | bytes 835592 | tf_op jit(solution)/shard_map/d_act/ppermute | solution.py:24
  109.7 5.6 %collective-permute-start.46 = (f32[8,512]{1,0:T(8,128)S(1)}, f32[8,512]{1,0:T(8,128)S(1)}, u32[]{:S(2)}, u32[]{:S(2)}) collective-permute-start(f32[8,512]{1,0:T(8,128)S(1)} %pad_maximum_fusion.1.refs_0_), channel_id=1, source_target_pairs={{0,24},{8,16},{16,8},{24,0},{1,25},{9,17},{17,9},{25,1},{2,26},{10... | collective-permute-start | bytes 49160 | tf_op jit(solution)/shard_map/norm_backward/ppermute | solution.py:24
  111.2 4.8 %collective-permute-start.45 = (f32[8,512]{1,0:T(8,128)S(1)}, f32[8,512]{1,0:T(8,128)S(1)}, u32[]{:S(2)}, u32[]{:S(2)}) collective-permute-start(f32[8,512]{1,0:T(8,128)S(1)} %pad_maximum_fusion.1.refs_0_), channel_id=1, source_target_pairs={{0,16},{8,24},{16,0},{24,8},{1,17},{9,25},{17,1},{25,9},{2,18},{10... | collective-permute-start | bytes 49160 | tf_op jit(solution)/shard_map/norm_backward/ppermute | solution.py:24
  111.7 4.3 %collective-permute-start.44 = (f32[8,512]{1,0:T(8,128)S(1)}, f32[8,512]{1,0:T(8,128)S(1)}, u32[]{:S(2)}, u32[]{:S(2)}) collective-permute-start(f32[8,512]{1,0:T(8,128)S(1)} %pad_maximum_fusion.1.refs_0_), channel_id=1, source_target_pairs={{0,8},{8,0},{16,24},{24,16},{1,9},{9,1},{17,25},{25,17},{2,10},{10... | collective-permute-start | bytes 49160 | tf_op jit(solution)/shard_map/norm_backward/ppermute | solution.py:24
  (3 other events, 20.4 us)
